TPU v7x, 32 devices: a whole 2x2x4 slice. The times are simulated.
32 devices in a mesh: groups: 2 (over y), shard: 4 (over z), feat: 2 (over x), rep: 2 (over core).
Axes of the slice: x: 2, y: 2, z: 4, core: 2. Of those that a mesh axis runs over, the one named last changes fastest.
Arguments:
- train: bfloat16 [8192, 4096], P(('groups', 'shard'), 'feat'), parts along dimension 0, may hold values from -6 to 6
- cluster_ids: int32 [8192], P('groups'), parts along dimension 0, may hold values from 0 to 3, as said below
- precond: bfloat16 [8, 4096, 4096], P(('groups', 'shard'), None, ('feat', 'rep')), parts along dimension 0, may hold values from -0.09375 to 0.09375
- query_store: bfloat16 [16, 128, 4096], P('shard', None, ('feat', 'rep')), may hold values from -0.09375 to 0.09375
- block_slot: int32 [16], replicated, may hold values from 0 to 15, as said below
- pattern: int32 [4, 4], replicated, may hold values from 0 to 15, as said below
Outputs:
- scores: float32 [8, 512, 1024], P(('groups', 'shard'), ('feat', 'rep')), parts along dimension 0
There are 2 independent parts, one for each index of `groups`. A program takes and returns all parts, laid end to end along the dimension named above; an argument that names none is the same for every part. Nothing has to cross between parts.
Inputs may be any that keep to these rules, and one draw needn't show every extreme that they name: `cluster_ids`: every cluster is named by exactly 1024 rows. Among the 1024 rows of one index of shard, each cluster is named between 128 and 384 times, and on every index some cluster exactly 384 times. `block_slot`: a permutation; block b is the block of index block_slot[b] // 4 of shard. `pattern`: each cluster lists 4 blocks stored on 4 different indices of shard.
All inputs are finite; a program needn't handle non-finite values.
Results may differ from a plain program's by a relative error of at most 0.0029.
Values may be sent and summed in bfloat16 or wider, within the bound.
No kernel may reach another device: no remote copies, remote signals or barrier semaphores. Data moves between devices by JAX's collectives and lax.ppermute only.
A program may use at most 128 MiB of HBM per device.

v0:
```python
import jax
import jax.numpy as jnp
from jax import lax
from jax.sharding import PartitionSpec as P


def body(train, cluster_ids, precond, query_store, block_slot, pattern):
    n_shard = lax.axis_size("shard")
    owner_index = lax.axis_index("shard")
    rows_dev = train.shape[0]
    base_count = rows_dev // n_shard
    capacity = base_count + base_count // 2
    labels = jnp.arange(n_shard, dtype=jnp.int32)
    own_ids = lax.dynamic_slice_in_dim(cluster_ids, owner_index * rows_dev, rows_dev)
    onehot = (own_ids[:, None] == labels[None, :]).astype(jnp.int32)
    before = jnp.cumsum(onehot, axis=0) - onehot
    slot_rank = jnp.sum(before * onehot, axis=1)
    target = own_ids * capacity + slot_rank
    id_grid = cluster_ids.reshape(n_shard, rows_dev)
    from_src = jnp.sum((id_grid == owner_index).astype(jnp.int32), axis=1)
    inclusive = jnp.cumsum(from_src)
    exclusive = inclusive - from_src
    position = jnp.arange(rows_dev, dtype=jnp.int32)
    source = jnp.sum((position[:, None] >= inclusive[None, :]).astype(jnp.int32), axis=1)
    src_onehot = (source[:, None] == labels[None, :]).astype(jnp.int32)
    within = position - jnp.sum(src_onehot * exclusive[None, :], axis=1)
    row_index = source * capacity + within
    matrix = precond[0]
    columns = train.shape[1]
    buffer = jnp.zeros((n_shard * capacity, columns), train.dtype).at[target].set(train)
    received = lax.all_to_all(
        buffer.reshape(n_shard, capacity, columns), "shard", split_axis=0, concat_axis=0, tiled=True
    )
    columns = received.shape[2]
    flattened = received.reshape(n_shard * capacity, columns)
    own_rows = flattened[row_index]
    projected = jnp.dot(
        lax.all_gather(own_rows, "feat", axis=1, tiled=True),
        matrix,
        preferred_element_type=jnp.float32,
    )
    precon = projected.astype(jnp.bfloat16)
    local_blocks = query_store.shape[0]
    my_list = lax.dynamic_index_in_dim(pattern, owner_index, 0, keepdims=False)
    my_slots = block_slot[my_list]
    slots_all = block_slot[pattern]
    owners = slots_all // local_blocks
    local_slot = slots_all % local_blocks
    owned = owners == owner_index
    picked = jnp.sum(jnp.where(owned, local_slot, 0), axis=1)
    present = jnp.any(owned, axis=1)
    outgoing = jnp.where(present[:, None, None], query_store[picked], jnp.zeros((), jnp.bfloat16))
    arrived = lax.all_to_all(outgoing, "shard", split_axis=0, concat_axis=0, tiled=True)
    chosen = arrived[my_slots // local_blocks]
    chosen = chosen.reshape(-1, chosen.shape[-1])
    scores = lax.psum_scatter(
        lax.dot_general(
            chosen, precon, (((1,), (1,)), ((), ())), preferred_element_type=jnp.float32
        ),
        ("feat", "rep"),
        scatter_dimension=0,
        tiled=True,
    )
    return scores[None]


def solution(mesh):
    return jax.shard_map(
        body,
        mesh=mesh,
        in_specs=(
            P(("groups", "shard"), "feat"),
            P("groups"),
            P(("groups", "shard"), None, ("feat", "rep")),
            P("shard", None, ("feat", "rep")),
            P(),
            P(),
        ),
        out_specs=P(("groups", "shard"), ("feat", "rep"), None),
        check_vma=False,
    )
```

profile of v0, /device:TPU:0, one launch (start us, length us, event | category | flops | bytes accessed | tf_op | source)
XLA Modules:
  0.0 336.9 jit_solution(8855091502162024905)
XLA Ops:
  6.5 0.0 copy-start
  6.5 0.8 dynamic-slice_bitcast_fusion
  7.3 0.7 dynamic_slice.8
  8.0 1.1 reduce-window.14
  9.1 0.2 slice_reduce_fusion
  9.4 0.2 reduce-window.18
  9.5 0.1 add_bitcast_fusion
  9.6 0.7 compare_select_fusion.1
  10.3 11.2 %scatter_custom_fusion = bf16[1536,2048]{1,0:T(8,128)(2,1)} fusion(s32[1024]{0:T(1024)S(1)} %compare_select_fusion.1, bf16[1024,2048]{1,0:T(8,128)(2,1)} %param.6, bf16[]{:T(256)} %constant.70.clone.1), kind=kCustom, calls=%fused_computation.8 | custom fusion | bytes 6291968 | tf_op jit(solution)/shard_map/scatter | solution.py:30
  21.6 0.0 copy-start.2
  21.6 6.4 %all-to-all-start.1 = ((bf16[4,384,2048]{2,1,0:T(8,128)(2,1)}), bf16[4,384,2048]{2,1,0:T(8,128)(2,1)}, u32[]{:S(2)}, u32[]{:S(2)}) async-start(bf16[4,384,2048]{2,1,0:T(8,128)(2,1)} %bitcast.60), calls=%async_computation.1 | async-start | bytes 12582912 | tf_op jit(solution)/shard_map/all_to_all | solution.py:31
  28.0 0.0 all-gather.3.cloned.1.call-start
  28.0 0.0 copy-done.2
  28.1 0.1 reduce_sum.52
  28.2 0.2 reduce-window.19
  28.4 0.1 convert_reduce_fusion
  28.5 0.1 select_reduce_fusion
  28.6 138.2 %all-to-all-done.1 = bf16[4,384,2048]{2,1,0:T(8,128)(2,1)} async-done(((bf16[4,384,2048]{2,1,0:T(8,128)(2,1)}), bf16[4,384,2048]{2,1,0:T(8,128)(2,1)}, u32[]{:S(2)}, u32[]{:S(2)}) %all-to-all-start.1) | async-done | bytes 6291488 | tf_op jit(solution)/shard_map/all_to_all | solution.py:31
  166.8 0.0 copy-start.3
  166.8 0.0 copy-start.1
  166.8 12.4 %gather_fusion.4 = bf16[1024,2048]{1,0:T(8,128)(2,1)} fusion(bf16[1536,2048]{1,0:T(8,128)(2,1)} %bitcast.10, s32[1024]{0:T(1024)S(1)} %broadcast_clamp_fusion), kind=kCustom, calls=%fused_computation.4 | custom fusion | bytes 8392704 | tf_op jit(solution)/shard_map/gather | solution.py:36
  179.2 0.0 all-gather.3.cloned.1.call-update
  179.2 0.0 copy-done.3
  179.3 0.1 reshape.197
  179.4 0.0 copy-done.1
  179.4 0.7 gather_fusion
  180.0 0.1 reshape.196
  180.1 0.1 fusion.21
  180.2 0.1 fusion.16
  180.4 0.0 copy-done
  180.4 0.6 gather_fusion.1
  181.0 1.2 broadcast_select_fusion
  182.2 3.6 %all-to-all-start = ((bf16[4,128,1024]{2,1,0:T(8,128)(2,1)}), bf16[4,128,1024]{2,1,0:T(8,128)(2,1)S(1)}, u32[]{:S(2)}, u32[]{:S(2)}) async-start(bf16[4,128,1024]{2,1,0:T(8,128)(2,1)} %broadcast_select_fusion), calls=%async_computation | async-start | bytes 2097152 | tf_op jit(solution)/shard_map/all_to_all | solution.py:53
  185.8 0.2 reduce-scatter.2.cloned.1.call-start
  186.0 0.6 gather_fusion.2
  186.7 24.4 %all-to-all-done = bf16[4,128,1024]{2,1,0:T(8,128)(2,1)S(1)} async-done(((bf16[4,128,1024]{2,1,0:T(8,128)(2,1)}), bf16[4,128,1024]{2,1,0:T(8,128)(2,1)S(1)}, u32[]{:S(2)}, u32[]{:S(2)}) %all-to-all-start) | async-done | bytes 1048608 | tf_op jit(solution)/shard_map/all_to_all | solution.py:53
  211.1 0.6 gather_fusion.3
  211.8 70.8 %all-gather.3.cloned.1.call-done = bf16[1024,4096]{1,0:T(8,128)(2,1)} async-done(((bf16[1024,2048]{1,0:T(8,128)(2,1)}), bf16[1024,4096]{1,0:T(8,128)(2,1)}) %all-gather.3.cloned.1.call-update) | async-done | bytes 8388624 | tf_op jit(solution)/shard_map/all_gather | solution.py:38
  282.6 15.8 %fusion.4 = f32[512,1024]{1,0:T(8,128)} fusion(bf16[512,1024]{1,0:T(8,128)(2,1)S(1)} %bitcast.61, bf16[1024,4096]{1,0:T(8,128)(2,1)} %all-gather.3.cloned.1.call-done, bf16[1,4096,1024]{2,1,0:T(8,128)(2,1)} %param.8), kind=kOutput, calls=%fused_computation.10 | convolution fusion | flops 9664724992 | bytes 19922944 | tf_op jit(solution)/shard_map/dot_general | solution.py:57
  298.4 0.0 reduce-scatter.2.cloned.1.call-update
  298.4 31.6 %reduce-scatter.2.cloned.1.call-done = f32[128,1024]{1,0:T(8,128)} async-done(((f32[512,1024]{1,0:T(8,128)}), f32[128,1024]{1,0:T(8,128)}) %reduce-scatter.2.cloned.1.call-update) | async-done | bytes 524304 | tf_op jit(solution)/shard_map/reduce_scatter | solution.py:56
  (16 shorter events, 0.1 us)
Async XLA Ops:
  6.5 173.9 %copy-start = (bf16[4,128,1024]{2,1,0:T(8,128)(2,1)S(1)}, bf16[4,128,1024]{2,1,0:T(8,128)(2,1)}, u32[]{:S(2)}) copy-start(bf16[4,128,1024]{2,1,0:T(8,128)(2,1)} %param.9) | copy-start | bytes 3145732
  21.6 6.5 %copy-start.2 = (s32[4096]{0:T(1024)S(1)}, s32[4096]{0:T(1024)}, u32[]{:S(2)}) copy-start(s32[4096]{0:T(1024)} %param.7) | copy-start | bytes 49156
  21.6 145.2 %all-to-all-start.1 = ((bf16[4,384,2048]{2,1,0:T(8,128)(2,1)}), bf16[4,384,2048]{2,1,0:T(8,128)(2,1)}, u32[]{:S(2)}, u32[]{:S(2)}) async-start(bf16[4,384,2048]{2,1,0:T(8,128)(2,1)} %bitcast.60), calls=%async_computation.1 | async-start | bytes 12582912 | tf_op jit(solution)/shard_map/all_to_all | solution.py:31
  28.0 254.6 %all-gather.3.cloned.1.call-start = ((), (), s32[]{:S(2)}) async-start(), calls=%async_computation.4 | async-start | bytes 12582912 | tf_op jit(solution)/shard_map/all_gather | solution.py:38
  166.8 12.5 %copy-start.3 = (s32[4,4]{1,0:T(4,128)S(1)}, s32[4,4]{1,0:T(4,128)}, u32[]{:S(2)}) copy-start(s32[4,4]{1,0:T(4,128)} %param.11) | copy-start | bytes 196
  166.8 12.6 %copy-start.1 = (s32[16]{0:T(128)S(1)}, s32[16]{0:T(128)}, u32[]{:S(2)}) copy-start(s32[16]{0:T(128)} %param.10) | copy-start | bytes 196
  182.2 28.9 %all-to-all-start = ((bf16[4,128,1024]{2,1,0:T(8,128)(2,1)}), bf16[4,128,1024]{2,1,0:T(8,128)(2,1)S(1)}, u32[]{:S(2)}, u32[]{:S(2)}) async-start(bf16[4,128,1024]{2,1,0:T(8,128)(2,1)} %broadcast_select_fusion), calls=%async_computation | async-start | bytes 2097152 | tf_op jit(solution)/shard_map/all_to_all | solution.py:53
  185.8 144.3 %reduce-scatter.2.cloned.1.call-start = ((), (), s32[]{:S(2)}) async-start(), calls=%async_computation.3 | async-start | bytes 2621440 | tf_op jit(solution)/shard_map/reduce_scatter | solution.py:56
Sparse Core Ops, SparseCore 0:
  179.4 103.1 all-gather.2
  298.6 31.4 reduce-scatter.1
where the time goes:
time: 337 us
  waiting for transfers between devices  265 us (79%)
  local copies, waits for them, and re-layouts  28.1 us (8%)
  matrix products  15.8 us (5%)
  between operations  13.5 us (4%)
  starting transfers between devices  10.2 us (3%)
  other arithmetic  4.12 us (1%)
    all_to_all x1, waiting for transfers between devices, body(): lax.all_to_all(buffer.reshape(n_shard, capacity, columns), 'shard', split...  138 us
    all_gather x1, waiting for transfers between devices, body(): lax.all_gather(own_rows, 'feat', axis=1, tiled=True)  70.8 us
    reduce_scatter x1, waiting for transfers between devices, body(): lax.psum_scatter(lax.dot_general(chosen, precon, (((1,), (1,)), ((), ()))...  31.6 us
    all_to_all x1, waiting for transfers between devices, body(): lax.all_to_all(outgoing, 'shard', split_axis=0, concat_axis=0, tiled=True)  24.4 us
    dot_general x1, matrix products, body(): lax.dot_general(chosen, precon, (((1,), (1,)), ((), ())), preferred_eleme...  15.8 us
    gather x1, local copies, waits for them, and re-layouts, body(): own_rows = flattened[row_index]  12.4 us
    scatter x1, local copies, waits for them, and re-layouts, body(): jnp.zeros((n_shard * capacity, columns), train.dtype).at[target].set(train)  11.2 us
  transfers between devices with their start and end apart: 4, of which 4 were waited for; matrix products, arithmetic and copies ran while one was open for 1% of the time, Pallas kernels for 0%

commit v1 on v0

v1 whole, which is shorter than its diff:
```python
import jax
import jax.numpy as jnp
from jax import lax
from jax.sharding import PartitionSpec as P


def shift(x, axis, size, by):
    return lax.ppermute(x, axis, [(i, (i + by) % size) for i in range(size)])


def contract(a, b):
    return lax.dot_general(a, b, (((1,), (1,)), ((), ())), preferred_element_type=jnp.float32)


def body(train, cluster_ids, precond, query_store, block_slot, pattern):
    n_group, n_shard = lax.axis_size("groups"), lax.axis_size("shard")
    n_feat, n_rep = lax.axis_size("feat"), lax.axis_size("rep")
    group, me = lax.axis_index("groups"), lax.axis_index("shard")
    feat, rep = lax.axis_index("feat"), lax.axis_index("rep")
    rows = train.shape[0]
    base = rows // n_shard
    capacity = base + base // 2
    columns = train.shape[1] // n_rep
    bf16 = jnp.bfloat16

    local_blocks, block_rows, width = query_store.shape
    n_list = pattern.shape[1]
    part = block_rows // n_group
    slots = block_slot[pattern]
    owners, places = slots // local_blocks, slots % local_blocks
    wanted = jnp.sum(jnp.where(owners == me, places, 0), axis=1)
    share = lax.dynamic_slice_in_dim(query_store, group * part, part, 1)

    def block_for(target):
        index = lax.dynamic_index_in_dim(wanted, target, 0, keepdims=False)
        return lax.dynamic_index_in_dim(share, index, 0, keepdims=False)

    parts_in = [block_for(me)]
    for d in range(1, n_shard):
        parts_in.append(shift(block_for((me + d) % n_shard), "shard", n_shard, d))
    arrived = jnp.stack(parts_in)
    my_owners = lax.dynamic_index_in_dim(owners, me, 0, keepdims=False)
    own_part = arrived[(me - my_owners) % n_shard]
    chosen = jnp.zeros((n_list, n_group, part, width), bf16)
    chosen = lax.dynamic_update_slice_in_dim(chosen, own_part[:, None], group, 1)
    for d in range(1, n_group):
        other = shift(own_part, "groups", n_group, d)
        chosen = lax.dynamic_update_slice_in_dim(chosen, other[:, None], (group - d) % n_group, 1)
    chosen = chosen.reshape(n_list * block_rows, width)

    labels = jnp.arange(n_shard, dtype=jnp.int32)
    own_ids = lax.dynamic_slice_in_dim(cluster_ids, me * rows, rows)
    onehot = (own_ids[:, None] == labels[None, :]).astype(jnp.int32)
    rank = jnp.sum((jnp.cumsum(onehot, axis=0) - onehot) * onehot, axis=1)
    half = lax.dynamic_slice_in_dim(train, rep * columns, columns, 1)

    def pack(target):
        goal = jnp.where(own_ids == target, rank, -1)
        pick = (jnp.arange(capacity, dtype=jnp.int32)[:, None] == goal[None, :]).astype(bf16)
        return jnp.dot(pick, half, preferred_element_type=jnp.float32).astype(bf16)

    received = [pack(me)]
    for d in range(1, n_shard):
        received.append(shift(pack((me + d) % n_shard), "shard", n_shard, d))

    id_grid = cluster_ids.reshape(n_shard, rows)
    counts = jnp.sum((id_grid == me).astype(jnp.int32), axis=1)
    starts = jnp.cumsum(counts) - counts

    matrix = precond[0]

    def weights(f, r):
        block = lax.dynamic_slice_in_dim(matrix, (f * n_rep + r) * columns, columns, 0)
        return contract(chosen, block)

    def summed_over_rep(f):
        away = [shift(weights(f, (rep + d) % n_rep), "rep", n_rep, d) for d in range(1, n_rep)]
        return sum(away, weights(f, rep))

    sent = [
        shift(summed_over_rep((feat + d) % n_feat).astype(bf16), "feat", n_feat, d)
        for d in range(1, n_feat)
    ]
    weight = summed_over_rep(feat)
    for piece in sent:
        weight = weight + piece.astype(jnp.float32)
    high = lax.reduce_precision(weight, 8, 7)
    low = (weight - high).astype(bf16)
    high = high.astype(bf16)

    grouped = jnp.zeros((rows, columns), jnp.float32)
    position = jnp.arange(rows, dtype=jnp.int32)
    for d in range(n_shard):
        source = (me - d) % n_shard
        count, start = counts[source], starts[source]
        offset = position - start
        offset = jnp.where((offset >= 0) & (offset < count), offset, -1)
        pick = (offset[:, None] == jnp.arange(capacity, dtype=jnp.int32)[None, :]).astype(bf16)
        grouped = grouped + jnp.dot(pick, received[d], preferred_element_type=jnp.float32)
    grouped = grouped.astype(bf16)
    scores = contract(high, grouped) + contract(low, grouped)
    share_rows = scores.shape[0] // (n_feat * n_rep)
    scores = scores.reshape(n_feat, n_rep, share_rows, rows)
    total = lax.dynamic_index_in_dim(scores, rep, 1, keepdims=False)
    for d in range(1, n_rep):
        away = lax.dynamic_index_in_dim(scores, (rep + d) % n_rep, 1, keepdims=False)
        total = total + shift(away, "rep", n_rep, d)
    result = lax.dynamic_index_in_dim(total, feat, 0, keepdims=False)
    for d in range(1, n_feat):
        away = lax.dynamic_index_in_dim(total, (feat + d) % n_feat, 0, keepdims=False)
        result = result + shift(away, "feat", n_feat, d)
    return result[None]


def solution(mesh):
    return jax.shard_map(
        body,
        mesh=mesh,
        in_specs=(
            P(("groups", "shard"), "feat"),
            P("groups"),
            P(("groups", "shard"), None, ("feat", "rep")),
            P("shard", None, ("feat", "rep")),
            P(),
            P(),
        ),
        out_specs=P(("groups", "shard"), ("feat", "rep"), None),
        check_vma=False,
    )
```

time: 337 us -> 147 us (0.44)
  waiting for transfers between devices: 265 us -> 70.6 us
  local copies, waits for them, and re-layouts: 28.1 us -> 5.43 us
  matrix products: 15.8 us -> 37.2 us
  between operations: 13.5 us -> 7.89 us
  starting transfers between devices: 10.2 us -> 15.8 us
  other arithmetic: 4.12 us -> 9.67 us
    all_to_all x2 -> x0, waiting for transfers between devices: 163 us -> none  [the longest x1 138 us: body(): lax.all_to_all(buffer.reshape(n_shard, capacity, columns), 'shard', split...]
    all_gather x1 -> x0, waiting for transfers between devices: 70.8 us -> none  [body(): lax.all_gather(own_rows, 'feat', axis=1, tiled=True)]
    ppermute x0 -> x12, waiting for transfers between devices: none -> 70.6 us  [shift(): return lax.ppermute(x, axis, [(i, (i + by) % size) for i in range(size)])]
    reduce_scatter x1 -> x0, waiting for transfers between devices: 31.6 us -> none  [body(): lax.psum_scatter(lax.dot_general(chosen, precon, (((1,), (1,)), ((), ()))...]
    dot_general x1 -> x13, matrix products: 15.8 us -> 37.2 us  [the longest x6 16.1 us: contract(): lax.dot_general(a, b, (((1,), (1,)), ((), ())), preferred_element_type=jn...]
    ppermute x0 -> x12, starting transfers between devices: none -> 15.8 us  [shift(): return lax.ppermute(x, axis, [(i, (i + by) % size) for i in range(size)])]
    gather x6 -> x3, local copies, waits for them, and re-layouts: 15.1 us -> 1.32 us  [the longest x2 0.74 us: body(): slots = block_slot[pattern]]
    scatter x1 -> x0, local copies, waits for them, and re-layouts: 11.2 us -> none  [body(): jnp.zeros((n_shard * capacity, columns), train.dtype).at[target].set(train)]
  transfers between devices with their start and end apart: 4 -> 12, of which waited for: 4 -> 6; matrix products, arithmetic and copies ran while one was open for 1% -> 27% of each run, Pallas kernels for 0% -> 0%
where the time goes in v1:
time: 147 us
  waiting for transfers between devices  70.6 us (48%)
  matrix products  37.2 us (25%)
  starting transfers between devices  15.8 us (11%)
  other arithmetic  9.67 us (7%)
  between operations  7.89 us (5%)
  local copies, waits for them, and re-layouts  5.43 us (4%)
    ppermute x12, waiting for transfers between devices, shift(): return lax.ppermute(x, axis, [(i, (i + by) % size) for i in range(size)])  70.6 us
    dot_general x6, matrix products, contract(): lax.dot_general(a, b, (((1,), (1,)), ((), ())), preferred_element_type=jn...  16.1 us
    ppermute x12, starting transfers between devices, shift(): return lax.ppermute(x, axis, [(i, (i + by) % size) for i in range(size)])  15.8 us
    dot_general x4, matrix products, body(): jnp.dot(pick, received[d], preferred_element_type=jnp.float32)  12.1 us
    dot_general x3, matrix products, pack(): return jnp.dot(pick, half, preferred_element_type=jnp.float32).astype(bf16)  9.02 us
    select_n x3, other arithmetic, body(): offset = jnp.where((offset >= 0) & (offset < count), offset, -1)  4.73 us
  transfers between devices with their start and end apart: 12, of which 6 were waited for; matrix products, arithmetic and copies ran while one was open for 27% of the time, Pallas kernels for 0%

profile of v1, /device:TPU:0, one launch (start us, length us, event | category | flops | bytes accessed | tf_op | source)
XLA Modules:
  0.0 146.6 jit_solution(16871503159908250535)
XLA Ops:
  0.0 0.7 dynamic-slice_bitcast_fusion.5
  0.7 0.7 dynamic_slice.118
  1.4 1.1 reduce-window.20
  2.5 0.2 slice_reduce_fusion
  2.7 0.2 reduce-window.21
  3.1 0.7 compare_select_fusion.1
  3.8 3.5 %fusion.22 = bf16[384,1024]{1,0:T(8,128)(2,1)} fusion(bf16[1024,2048]{1,0:T(8,128)(2,1)} %param.6, s32[]{:T(128)S(6)} %select_n.269, s32[1024]{0:T(1024)S(1)} %get-tuple-element.12), kind=kOutput, calls=%fused_computation.38 | convolution fusion | flops 806092800 | bytes 2887684 | tf_op jit(solution)/shard_map/dot_general | solution.py:60
  7.3 4.0 %collective-permute-start.8 = (bf16[384,1024]{1,0:T(8,128)(2,1)}, bf16[384,1024]{1,0:T(8,128)(2,1)}, u32[]{:S(2)}, u32[]{:S(2)}) collective-permute-start(bf16[384,1024]{1,0:T(8,128)(2,1)} %fusion.22), channel_id=1, source_target_pairs={{0,8},{4,12},{8,0},{12,4},{1,9},{5,13},{9,1},{13,5},{2,10},{6,14},... | collective-permute-start | bytes 2359304 | tf_op jit(solution)/shard_map/ppermute | solution.py:8
  11.4 0.7 gather_fusion
  12.2 0.1 fusion.75
  12.3 0.7 fusion.81
  20.6 0.1 constant_dynamic-slice_fusion.1
  20.7 1.4 collective-permute-start.2
  22.1 1.7 %collective-permute-start.1 = (bf16[64,1024]{1,0:T(8,128)(2,1)S(1)}, bf16[64,1024]{1,0:T(8,128)(2,1)S(1)}, u32[]{:S(2)}, u32[]{:S(2)}) collective-permute-start(bf16[64,1024]{1,0:T(8,128)(2,1)S(1)} %get-tuple-element.10), channel_id=1, source_target_pairs={{0,8},{4,12},{8,0},{12,4},{1,9},{5,13},{9,1},{13,5},{2,10},{6,14},... | collective-permute-start | bytes 393224 | tf_op jit(solution)/shard_map/ppermute | solution.py:8
  23.8 8.5 %collective-permute-done.2 = bf16[64,1024]{1,0:T(8,128)(2,1)S(1)} collective-permute-done((bf16[64,1024]{1,0:T(8,128)(2,1)S(1)}, bf16[64,1024]{1,0:T(8,128)(2,1)S(1)}, u32[]{:S(2)}, u32[]{:S(2)}) %collective-permute-start.2) | collective-permute-done | bytes 131104 | tf_op jit(solution)/shard_map/ppermute | solution.py:8
  32.3 24.8 %collective-permute-done.1 = bf16[64,1024]{1,0:T(8,128)(2,1)S(1)} collective-permute-done((bf16[64,1024]{1,0:T(8,128)(2,1)S(1)}, bf16[64,1024]{1,0:T(8,128)(2,1)S(1)}, u32[]{:S(2)}, u32[]{:S(2)}) %collective-permute-start.1) | collective-permute-done | bytes 131104 | tf_op jit(solution)/shard_map/ppermute | solution.py:8
  57.2 0.6 gather_fusion.1
  57.8 1.6 %collective-permute-start.3 = (bf16[4,64,1024]{2,1,0:T(8,128)(2,1)S(1)}, bf16[4,64,1024]{2,1,0:T(8,128)(2,1)S(1)}, u32[]{:S(2)}, u32[]{:S(2)}) collective-permute-start(bf16[4,64,1024]{2,1,0:T(8,128)(2,1)S(1)} %gather_fusion.1), channel_id=1, source_target_pairs={{0,16},{16,0},{1,17},{17,1},{2,18},{18,2},{3,19},{19,3},{4,20},{20... | collective-permute-start | bytes 1572872 | tf_op jit(solution)/shard_map/ppermute | solution.py:8
  59.5 3.6 %fusion.23 = bf16[384,1024]{1,0:T(8,128)(2,1)} fusion(bf16[1024,2048]{1,0:T(8,128)(2,1)} %param.6, s32[]{:T(128)S(6)} %select_n.269, s32[1024]{0:T(1024)S(1)} %get-tuple-element.13), kind=kOutput, calls=%fused_computation.39 | convolution fusion | flops 806092800 | bytes 2887684 | tf_op jit(solution)/shard_map/dot_general | solution.py:60
  63.1 0.7 collective-permute-start.7
  63.8 1.9 %fusion.21 = bf16[384,1024]{1,0:T(8,128)(2,1)} fusion(bf16[1024,2048]{1,0:T(8,128)(2,1)S(1)} %copy-done.5, s32[]{:T(128)S(6)} %select_n.269, s32[1024]{0:T(1024)S(1)} %get-tuple-element.11), kind=kOutput, calls=%fused_computation.37 | convolution fusion | flops 806092800 | bytes 2887684 | tf_op jit(solution)/shard_map/dot_general | solution.py:60
  65.6 3.2 %collective-permute-start.9 = (bf16[384,1024]{1,0:T(8,128)(2,1)}, bf16[384,1024]{1,0:T(8,128)(2,1)S(1)}, u32[]{:S(2)}, u32[]{:S(2)}) collective-permute-start(bf16[384,1024]{1,0:T(8,128)(2,1)} %fusion.21), channel_id=1, source_target_pairs={{0,12},{4,0},{8,4},{12,8},{1,13},{5,1},{9,5},{13,9},{2,14},{6,2},{... | collective-permute-start | bytes 2359304 | tf_op jit(solution)/shard_map/ppermute | solution.py:8
  69.0 2.0 %collective-permute-done.3 = bf16[4,64,1024]{2,1,0:T(8,128)(2,1)S(1)} collective-permute-done((bf16[4,64,1024]{2,1,0:T(8,128)(2,1)S(1)}, bf16[4,64,1024]{2,1,0:T(8,128)(2,1)S(1)}, u32[]{:S(2)}, u32[]{:S(2)}) %collective-permute-start.3) | collective-permute-done | bytes 524320 | tf_op jit(solution)/shard_map/ppermute | solution.py:8
  71.1 4.2 %fusion.1 = f32[512,1024]{1,0:T(8,128)} fusion(bf16[512,1024]{1,0:T(8,128)(2,1)S(1)} %bitcast.96, bf16[1,4096,1024]{2,1,0:T(8,128)(2,1)} %param.8, s32[]{:T(128)S(6)} %select_n.263), kind=kOutput, calls=%fused_computation.6 | convolution fusion | flops 1073741824 | bytes 5242884 | tf_op jit(solution)/shard_map/dot_general | solution.py:12
  75.3 0.1 reduce_sum.28
  75.4 0.2 reduce-window.19
  75.6 0.6 fusion.83
  76.2 0.6 fusion.82
  76.8 1.2 fusion.58
  78.0 5.6 %fusion.13 = f32[1024,1024]{1,0:T(8,128)} fusion(bf16[1024,2048]{1,0:T(8,128)(2,1)} %param.6, s32[]{:T(128)S(6)} %select_n.269, s32[1024]{0:T(1024)S(1)} %get-tuple-element.14, s32[1024]{0:T(1024)S(1)} %fusion.58), kind=kOutput, calls=%fused_computation.28 | convolution fusion | flops 1611792384 | bytes 6299652 | tf_op jit(solution)/shard_map/dot_general | solution.py:99
  83.6 1.2 fusion.49
  84.8 2.4 %fusion.52 = (s32[1024]{0:T(1024)S(1)}, s32[1024]{0:T(1024)S(1)}) fusion(s32[]{:T(128)} %bitcast.29, s32[]{:T(128)} %bitcast.28, s32[]{:T(128)} %bitcast.27, s32[]{:T(128)} %bitcast.26), kind=kLoop, calls=%fused_computation.83 | loop fusion | flops 10240 | bytes 8208 | tf_op jit(solution)/shard_map/jit(_where)/select_n | solution.py:97
  87.2 2.9 %fusion.5 = f32[512,1024]{1,0:T(8,128)S(1)} fusion(bf16[512,1024]{1,0:T(8,128)(2,1)S(1)} %bitcast.97, bf16[1,4096,1024]{2,1,0:T(8,128)(2,1)} %param.8, s32[]{:T(128)S(6)} %select_n.260), kind=kOutput, calls=%fused_computation.10 | convolution fusion | flops 1073741824 | bytes 5242884 | tf_op jit(solution)/shard_map/dot_general | solution.py:12
  90.1 0.6 collective-permute-start.4
  90.7 2.9 %fusion.7 = f32[512,1024]{1,0:T(8,128)S(1)} fusion(bf16[512,1024]{1,0:T(8,128)(2,1)S(1)} %bitcast.98, bf16[1,4096,1024]{2,1,0:T(8,128)(2,1)} %param.8, s32[]{:T(128)S(6)} %select_n.258), kind=kOutput, calls=%fused_computation.12 | convolution fusion | flops 1073741824 | bytes 5242884 | tf_op jit(solution)/shard_map/dot_general | solution.py:12
  93.6 2.4 %fusion.17 = f32[1024,1024]{1,0:T(8,128)S(1)} fusion(bf16[384,1024]{1,0:T(8,128)(2,1)} %collective-permute-done.8, s32[1024]{0:T(1024)S(1)} %get-tuple-element.27), kind=kOutput, calls=%fused_computation.32 | convolution fusion | flops 805699584 | bytes 4984832 | tf_op jit(solution)/shard_map/dot_general | solution.py:99
  96.0 3.5 %add_convert_fusion.1 = bf16[512,1024]{1,0:T(8,128)(2,1)S(1)} fusion(f32[512,1024]{1,0:T(8,128)} %collective-permute-done.5, bf16[512,1024]{1,0:T(8,128)(2,1)S(1)} %bitcast.99, bf16[1,4096,1024]{2,1,0:T(8,128)(2,1)} %param.8, s32[]{:T(128)S(6)} %select_n.262), kind=kOutput, calls=%fused_computation.15 | convolution fusion | flops 1074790400 | bytes 6291460 | tf_op jit(solution)/shard_map/dot_general | solution.py:12
  99.5 1.3 collective-permute-start.6
  100.8 2.6 %fusion.15 = f32[1024,1024]{1,0:T(8,128)S(1)} fusion(bf16[384,1024]{1,0:T(8,128)(2,1)} %collective-permute-done.7, s32[1024]{0:T(1024)S(1)} %get-tuple-element.28), kind=kOutput, calls=%fused_computation.30 | convolution fusion | flops 805699584 | bytes 4984832 | tf_op jit(solution)/shard_map/dot_general | solution.py:99
  103.4 1.5 %add_convert_fusion = bf16[1024,1024]{1,0:T(8,128)(2,1)S(1)} fusion(f32[1024,1024]{1,0:T(8,128)S(1)} %fusion.17, f32[1024,1024]{1,0:T(8,128)S(1)} %copy-done.1, f32[1024,1024]{1,0:T(8,128)S(1)} %fusion.15, bf16[384,1024]{1,0:T(8,128)(2,1)S(1)} %collective-permute-done.9, s32[1024]{0:T(1024)S(1)} %fusion.49), kind=kOutput, calls=%fused_computation.2 | convolution fusion | flops 809893888 | bytes 15470592 | tf_op jit(solution)/shard_map/dot_general | solution.py:99
  104.9 19.7 %collective-permute-done.6 = bf16[512,1024]{1,0:T(8,128)(2,1)S(1)} collective-permute-done((bf16[512,1024]{1,0:T(8,128)(2,1)S(1)}, bf16[512,1024]{1,0:T(8,128)(2,1)S(1)}, u32[]{:S(2)}, u32[]{:S(2)}) %collective-permute-start.6) | collective-permute-done | bytes 1048608 | tf_op jit(solution)/shard_map/ppermute | solution.py:8
  124.7 1.3 fusion.33
  126.0 1.3 convolution_add_fusion
  127.5 2.8 %collective-permute-done.10 = f32[2,128,1024]{2,1,0:T(8,128)} collective-permute-done((f32[2,128,1024]{2,1,0:T(8,128)S(1)}, f32[2,128,1024]{2,1,0:T(8,128)}, u32[]{:S(2)}, u32[]{:S(2)}) %collective-permute-start.10) | collective-permute-done | bytes 1048608 | tf_op jit(solution)/shard_map/ppermute | solution.py:8
  130.3 1.4 bitcast_add_fusion
  131.7 1.3 collective-permute-start.11
  133.1 12.7 %collective-permute-done.11 = f32[128,1024]{1,0:T(8,128)S(1)} collective-permute-done((f32[128,1024]{1,0:T(8,128)S(1)}, f32[128,1024]{1,0:T(8,128)S(1)}, u32[]{:S(2)}, u32[]{:S(2)}) %collective-permute-start.11) | collective-permute-done | bytes 524320 | tf_op jit(solution)/shard_map/ppermute | solution.py:8
  145.8 0.9 fusion.44
  (39 shorter events, 0.9 us)
Async XLA Ops:
  0.0 11.4 %copy-start = (s32[16]{0:T(128)S(1)}, s32[16]{0:T(128)}, u32[]{:S(2)}) copy-start(s32[16]{0:T(128)} %param.10) | copy-start | bytes 196
  3.8 7.6 %copy-start.4 = (s32[4,4]{1,0:T(4,128)S(1)}, s32[4,4]{1,0:T(4,128)}, u32[]{:S(2)}) copy-start(s32[4,4]{1,0:T(4,128)} %param.11) | copy-start | bytes 196
  7.3 13.3 %copy-start.2 = (bf16[4,128,1024]{2,1,0:T(8,128)(2,1)S(1)}, bf16[4,128,1024]{2,1,0:T(8,128)(2,1)}, u32[]{:S(2)}) copy-start(bf16[4,128,1024]{2,1,0:T(8,128)(2,1)} %param.9) | copy-start | bytes 3145732
  7.3 86.3 %collective-permute-start.8 = (bf16[384,1024]{1,0:T(8,128)(2,1)}, bf16[384,1024]{1,0:T(8,128)(2,1)}, u32[]{:S(2)}, u32[]{:S(2)}) collective-permute-start(bf16[384,1024]{1,0:T(8,128)(2,1)} %fusion.22), channel_id=1, source_target_pairs={{0,8},{4,12},{8,0},{12,4},{1,9},{5,13},{9,1},{13,5},{2,10},{6,14},... | collective-permute-start | bytes 2359304 | tf_op jit(solution)/shard_map/ppermute | solution.py:8
  20.7 11.6 %collective-permute-start.2 = (bf16[64,1024]{1,0:T(8,128)(2,1)S(1)}, bf16[64,1024]{1,0:T(8,128)(2,1)S(1)}, u32[]{:S(2)}, u32[]{:S(2)}) collective-permute-start(bf16[64,1024]{1,0:T(8,128)(2,1)S(1)} %get-tuple-element.9), channel_id=1, source_target_pairs={{0,12},{4,0},{8,4},{12,8},{1,13},{5,1},{9,5},{13,9},{2,14},{6,2},{... | collective-permute-start | bytes 393224 | tf_op jit(solution)/shard_map/ppermute | solution.py:8
  22.1 35.0 %collective-permute-start.1 = (bf16[64,1024]{1,0:T(8,128)(2,1)S(1)}, bf16[64,1024]{1,0:T(8,128)(2,1)S(1)}, u32[]{:S(2)}, u32[]{:S(2)}) collective-permute-start(bf16[64,1024]{1,0:T(8,128)(2,1)S(1)} %get-tuple-element.10), channel_id=1, source_target_pairs={{0,8},{4,12},{8,0},{12,4},{1,9},{5,13},{9,1},{13,5},{2,10},{6,14},... | collective-permute-start | bytes 393224 | tf_op jit(solution)/shard_map/ppermute | solution.py:8
  23.8 33.4 %collective-permute-start = (bf16[64,1024]{1,0:T(8,128)(2,1)S(1)}, bf16[64,1024]{1,0:T(8,128)(2,1)S(1)}, u32[]{:S(2)}, u32[]{:S(2)}) collective-permute-start(bf16[64,1024]{1,0:T(8,128)(2,1)S(1)} %get-tuple-element.8), channel_id=1, source_target_pairs={{0,4},{4,8},{8,12},{12,0},{1,5},{5,9},{9,13},{13,1},{2,6},{6,10},{... | collective-permute-start | bytes 393224 | tf_op jit(solution)/shard_map/ppermute | solution.py:8
  57.8 13.2 %collective-permute-start.3 = (bf16[4,64,1024]{2,1,0:T(8,128)(2,1)S(1)}, bf16[4,64,1024]{2,1,0:T(8,128)(2,1)S(1)}, u32[]{:S(2)}, u32[]{:S(2)}) collective-permute-start(bf16[4,64,1024]{2,1,0:T(8,128)(2,1)S(1)} %gather_fusion.1), channel_id=1, source_target_pairs={{0,16},{16,0},{1,17},{17,1},{2,18},{18,2},{3,19},{19,3},{4,20},{20... | collective-permute-start | bytes 1572872 | tf_op jit(solution)/shard_map/ppermute | solution.py:8
  59.5 4.3 %copy-start.5 = (bf16[1024,2048]{1,0:T(8,128)(2,1)S(1)}, bf16[1024,2048]{1,0:T(8,128)(2,1)}, u32[]{:S(2)}) copy-start(bf16[1024,2048]{1,0:T(8,128)(2,1)} %param.6) | copy-start | bytes 12582916
  63.1 37.7 %collective-permute-start.7 = (bf16[384,1024]{1,0:T(8,128)(2,1)}, bf16[384,1024]{1,0:T(8,128)(2,1)}, u32[]{:S(2)}, u32[]{:S(2)}) collective-permute-start(bf16[384,1024]{1,0:T(8,128)(2,1)} %fusion.23), channel_id=1, source_target_pairs={{0,4},{4,8},{8,12},{12,0},{1,5},{5,9},{9,13},{13,1},{2,6},{6,10},{... | collective-permute-start | bytes 2359304 | tf_op jit(solution)/shard_map/ppermute | solution.py:8
  65.6 37.8 %collective-permute-start.9 = (bf16[384,1024]{1,0:T(8,128)(2,1)}, bf16[384,1024]{1,0:T(8,128)(2,1)S(1)}, u32[]{:S(2)}, u32[]{:S(2)}) collective-permute-start(bf16[384,1024]{1,0:T(8,128)(2,1)} %fusion.21), channel_id=1, source_target_pairs={{0,12},{4,0},{8,4},{12,8},{1,13},{5,1},{9,5},{13,9},{2,14},{6,2},{... | collective-permute-start | bytes 2359304 | tf_op jit(solution)/shard_map/ppermute | solution.py:8
  71.0 4.2 %copy-start.3 = (s32[4096]{0:T(1024)S(1)}, s32[4096]{0:T(1024)}, u32[]{:S(2)}) copy-start(s32[4096]{0:T(1024)} %param.7) | copy-start | bytes 49156
  75.3 20.7 %collective-permute-start.5 = (f32[512,1024]{1,0:T(8,128)}, f32[512,1024]{1,0:T(8,128)}, u32[]{:S(2)}, u32[]{:S(2)}) collective-permute-start(f32[512,1024]{1,0:T(8,128)} %fusion.1), channel_id=1, source_target_pairs={{0,1},{1,0},{2,3},{3,2},{4,5},{5,4},{6,7},{7,6},{8,9},{9,8},{10,11... | collective-permute-start | bytes 6291464 | tf_op jit(solution)/shard_map/ppermute | solution.py:8
  90.1 14.8 %collective-permute-start.4 = (f32[512,1024]{1,0:T(8,128)S(1)}, f32[512,1024]{1,0:T(8,128)S(1)}, u32[]{:S(2)}, u32[]{:S(2)}) collective-permute-start(f32[512,1024]{1,0:T(8,128)S(1)} %fusion.5), channel_id=1, source_target_pairs={{0,1},{1,0},{2,3},{3,2},{4,5},{5,4},{6,7},{7,6},{8,9},{9,8},{10,11... | collective-permute-start | bytes 6291464 | tf_op jit(solution)/shard_map/ppermute | solution.py:8
  99.5 25.1 %collective-permute-start.6 = (bf16[512,1024]{1,0:T(8,128)(2,1)S(1)}, bf16[512,1024]{1,0:T(8,128)(2,1)S(1)}, u32[]{:S(2)}, u32[]{:S(2)}) collective-permute-start(bf16[512,1024]{1,0:T(8,128)(2,1)S(1)} %add_convert_fusion.1), channel_id=1, source_target_pairs={{0,2},{2,0},{1,3},{3,1},{4,6},{6,4},{5,7},{7,5},{8,10},{10,8},{9,1... | collective-permute-start | bytes 3145736 | tf_op jit(solution)/shard_map/ppermute | solution.py:8
  100.8 2.6 %copy-start.1 = (f32[1024,1024]{1,0:T(8,128)S(1)}, f32[1024,1024]{1,0:T(8,128)}, u32[]{:S(2)}) copy-start(f32[1024,1024]{1,0:T(8,128)} %fusion.13) | copy-start | bytes 12582916
  127.4 2.9 %collective-permute-start.10 = (f32[2,128,1024]{2,1,0:T(8,128)S(1)}, f32[2,128,1024]{2,1,0:T(8,128)}, u32[]{:S(2)}, u32[]{:S(2)}) collective-permute-start(f32[2,128,1024]{2,1,0:T(8,128)S(1)} %dynamic-slice_bitcast_fusion), channel_id=1, source_target_pairs={{0,1},{1,0},{2,3},{3,2},{4,5},{5,4},{6,7},{7,6},{8,9},{9,8},{10,11... | collective-permute-start | bytes 3145736 | tf_op jit(solution)/shard_map/ppermute | solution.py:8
  131.7 14.0 %collective-permute-start.11 = (f32[128,1024]{1,0:T(8,128)S(1)}, f32[128,1024]{1,0:T(8,128)S(1)}, u32[]{:S(2)}, u32[]{:S(2)}) collective-permute-start(f32[128,1024]{1,0:T(8,128)S(1)} %dynamic-slice_bitcast_fusion.1), channel_id=1, source_target_pairs={{0,2},{2,0},{1,3},{3,1},{4,6},{6,4},{5,7},{7,5},{8,10},{10,8},{9,1... | collective-permute-start | bytes 1572872 | tf_op jit(solution)/shard_map/ppermute | solution.py:8

commit v2 on v1

v2 whole, which is shorter than its diff:
```python
import functools

import jax
import jax.numpy as jnp
from jax import lax
from jax.experimental import pallas as pl
from jax.experimental.pallas import tpu as pltpu
from jax.sharding import PartitionSpec as P

F32, BF16, I32 = jnp.float32, jnp.bfloat16, jnp.int32
VMEM = pl.BlockSpec(memory_space=pltpu.VMEM)
SMEM = pl.BlockSpec(memory_space=pltpu.SMEM)
PARAMS = pltpu.CompilerParams(vmem_limit_bytes=50 * 2**20)
LANES = 128


def shift(x, axis, size, by):
    return lax.ppermute(x, axis, [(i, (i + by) % size) for i in range(size)])


def swap(x, axis, size, bit):
    return lax.ppermute(x, axis, [(i, i ^ bit) for i in range(size)])


def dot(a, b):
    return jnp.dot(a, b, preferred_element_type=F32)


def cost(flops, nbytes):
    return pl.CostEstimate(flops=int(flops), bytes_accessed=int(nbytes), transcendentals=0)


def pick_queries(query_store, block_slot, pattern, n_group):
    local_blocks, block_rows, width = query_store.shape
    n_cluster, n_list = pattern.shape
    part = block_rows // n_group

    def place(t, pattern_ref, slot_ref):
        me = lax.axis_index("shard")
        found = jnp.int32(0)
        for k in range(n_list):
            slot = slot_ref[pattern_ref[t * n_list + k]]
            hit = (lax.div(slot, jnp.int32(local_blocks)) == me).astype(I32)
            found = found + hit * lax.rem(slot, jnp.int32(local_blocks))
        return found, lax.axis_index("groups"), 0

    def kernel(pattern_ref, slot_ref, in_ref, out_ref):
        out_ref[...] = in_ref[...]

    return pl.pallas_call(
        kernel,
        grid_spec=pltpu.PrefetchScalarGridSpec(
            num_scalar_prefetch=2,
            grid=(n_cluster,),
            in_specs=[pl.BlockSpec((1, part, width), place)],
            out_specs=pl.BlockSpec((1, part, width), lambda t, p, s: (t, 0, 0)),
        ),
        out_shape=jax.ShapeDtypeStruct((n_cluster, part, width), BF16),
        cost_estimate=cost(0, 4 * n_cluster * part * width),
        compiler_params=PARAMS,
        name="pick_queries",
    )(pattern.reshape(-1), block_slot, query_store)


def join_queries(parts, block_slot, pattern, local_blocks, n_feat, n_rep):
    n_group = len(parts)
    n_cluster, part, width = parts[0].shape
    n_list = pattern.shape[1]
    total = n_list * n_group * part
    share = total // (n_feat * n_rep)
    unit = min(share, part)

    def kernel(pattern_ref, slot_ref, *refs):
        out_ref = refs[-1]
        me, group = lax.axis_index("shard"), lax.axis_index("groups")
        for k in range(n_list):
            owner = lax.div(slot_ref[pattern_ref[me * n_list + k]], jnp.int32(local_blocks))
            for d in range(n_group):
                origin = lax.rem(group + (n_group - d), jnp.int32(n_group))
                for u in range(part // unit):
                    first = (k * n_group + origin) * part + u * unit
                    chunk = lax.div(first, jnp.int32(share))
                    goal = lax.rem(chunk, jnp.int32(n_rep)) * n_feat + lax.div(chunk, jnp.int32(n_rep))
                    goal = goal * share + lax.rem(first, jnp.int32(share))
                    out_ref[pl.ds(pl.multiple_of(goal, unit), unit), :] = refs[d][owner, u * unit:(u + 1) * unit, :]

    return pl.pallas_call(
        kernel,
        in_specs=[SMEM, SMEM] + [VMEM] * n_group,
        out_specs=VMEM,
        out_shape=jax.ShapeDtypeStruct((total, width), BF16),
        cost_estimate=cost(0, 4 * total * width),
        compiler_params=PARAMS,
        name="join_queries",
    )(pattern.reshape(-1), block_slot, *parts)


def pack_rows(train, ids, columns, bulk, extra):
    rows = train.shape[0]
    lines = rows // LANES
    n_shard = ids.shape[0] // lines
    tile = 128 if extra else bulk

    def kernel(ids_ref, train_ref, bulk_ref, *rest):
        extra_refs, goal_ref = rest[:-1], rest[-1]
        own = ids_ref[...]
        masks = [(own == c).astype(F32) for c in range(n_shard)]
        stacked = jnp.concatenate(masks, axis=0).astype(BF16)
        lane_from = lax.broadcasted_iota(I32, (LANES, LANES), 0)
        lane_to = lax.broadcasted_iota(I32, (LANES, LANES), 1)
        in_line = dot(stacked, (lane_from < lane_to).astype(F32).astype(BF16))
        line_sum = dot(stacked, jnp.ones((LANES, LANES), BF16)).astype(BF16)
        size = n_shard * lines
        to = lax.broadcasted_iota(I32, (size, size), 0)
        since = lax.broadcasted_iota(I32, (size, size), 1)
        same = (to // lines) == (since // lines)
        ahead = dot((same & (since < to)).astype(F32).astype(BF16), line_sum)
        whole = dot(same.astype(F32).astype(BF16), line_sum)
        rank = in_line + ahead
        goal = jnp.zeros((lines, LANES), F32)
        past = jnp.zeros((lines, LANES), F32)
        for c in range(n_shard):
            part = slice(c * lines, (c + 1) * lines)
            place = rank[part] + c * bulk
            if extra:
                surplus = n_shard * bulk + past + rank[part] - bulk
                place = jnp.where(rank[part] < bulk, place, surplus)
                past = past + jnp.floor((jnp.maximum(whole[part] - bulk, 0.0) + 7.0) * 0.125) * 8.0
            goal = goal + masks[c] * place
        goal_ref[...] = goal.astype(I32)

        def one_tile(base):
            index = lax.broadcasted_iota(I32, (tile, LANES), 0) + base
            pick = [(index == goal_ref[a:a + 1, :]).astype(F32).astype(BF16) for a in range(lines)]
            return dot(jnp.concatenate(pick, axis=1), train_ref[...]).astype(BF16)

        per = bulk // tile
        for c in range(n_shard):
            for j in range(per):
                bulk_ref[c, j * tile:(j + 1) * tile, :] = one_tile(c * bulk + j * tile)
        for j, ref in enumerate(extra_refs):
            ref[...] = one_tile(n_shard * bulk + j * extra)

    shapes = [jax.ShapeDtypeStruct((n_shard, bulk, columns), BF16)]
    shapes += [jax.ShapeDtypeStruct((extra, columns), BF16)] * (2 if extra else 0)
    packed = n_shard * bulk + 2 * extra
    return pl.pallas_call(
        kernel,
        grid=(1,),
        in_specs=[
            pl.BlockSpec((lines, LANES), lambda i: (lax.axis_index("shard"), 0)),
            pl.BlockSpec((rows, columns), lambda i: (0, lax.axis_index("rep"))),
        ],
        out_specs=[VMEM] * len(shapes),
        out_shape=shapes,
        scratch_shapes=[pltpu.VMEM((lines, LANES), I32)],
        cost_estimate=cost(2 * packed * rows * columns, 2 * (rows + packed) * columns),
        compiler_params=PARAMS,
        name="pack_rows",
    )(ids, train)


def row_table(ids, lines, bulk, extra):
    n_shard = ids.shape[0] // lines

    def kernel(ids_ref, table_ref, flag_ref):
        me = lax.axis_index("shard")
        start = jnp.int32(0)
        most = jnp.int32(0)
        for s in range(n_shard):
            line = ids_ref[s * lines:(s + 1) * lines, :]

            def count(c):
                return jnp.sum((line == c).astype(I32))

            mine = count(me)
            before = jnp.int32(0)
            if extra:
                surplus = jnp.int32(0)
                for c in range(n_shard):
                    over = lax.div(jnp.maximum(count(c) - bulk, 0) + 7, jnp.int32(8)) * 8
                    before = before + jnp.where(c < me, over, 0)
                    surplus = surplus + over
                most = jnp.maximum(most, surplus)
            table_ref[s, 0] = start
            table_ref[s, 1] = jnp.minimum(mine, bulk)
            table_ref[s, 2] = lax.div(before, jnp.int32(8))
            start = start + mine
        flag_ref[...] = jnp.full((8, LANES), (most > extra).astype(I32))

    return pl.pallas_call(
        kernel,
        in_specs=[VMEM],
        out_specs=[SMEM, VMEM],
        out_shape=[jax.ShapeDtypeStruct((n_shard, 3), I32), jax.ShapeDtypeStruct((8, LANES), I32)],
        cost_estimate=cost(0, 4 * ids.size),
        compiler_params=PARAMS,
        name="row_table",
    )(ids)


def split_weights(own, others, extras):
    depth, width = own.shape
    n_extra = sum(e.shape[0] for e in extras)
    n_other = len(others)

    def kernel(*refs):
        own_ref, other_refs, extra_refs = refs[0], refs[1:1 + n_other], refs[1 + n_other:-3]
        high_ref, low_ref, out_ref = refs[-3:]
        weight = own_ref[...]
        for ref in other_refs:
            weight = weight + ref[...].astype(F32)
        high = weight.astype(BF16)
        high_ref[...] = high
        low_ref[...] = (weight - high.astype(F32)).astype(BF16)
        base = 0
        for ref in extra_refs:
            x = ref[...]
            y = dot(x, high_ref[...]) + dot(x, low_ref[...])
            out_ref[base // 8:(base + x.shape[0]) // 8] = y.reshape(x.shape[0] // 8, 8, width)
            base += x.shape[0]
        out_ref[base // 8:] = jnp.zeros((LANES // 8, 8, width), F32)

    return pl.pallas_call(
        kernel,
        in_specs=[VMEM] * (1 + n_other + len(extras)),
        out_specs=[VMEM] * 3,
        out_shape=[jax.ShapeDtypeStruct((depth, width), BF16)] * 2
        + [jax.ShapeDtypeStruct(((n_extra + LANES) // 8, 8, width), F32)],
        cost_estimate=cost(4 * n_extra * depth * width, 10 * depth * width + n_extra * (2 * depth + 4 * width)),
        compiler_params=PARAMS,
        name="split_weights",
    )(own, *others, *extras)


def row_scores(table, bulk_rows, high, low, extra_scores, rows, n_rep, extra):
    n_shard, bulk, depth = bulk_rows.shape
    width = high.shape[1]
    half = width // n_rep

    def kernel(table_ref, rows_ref, high_ref, low_ref, extra_ref, *rest):
        outs, acc = rest[:-1], rest[-1]
        me, rep = lax.axis_index("shard"), lax.axis_index("rep")

        def put(x, start):
            tiles = x.shape[0]
            first, within = lax.div(start, jnp.int32(8)), lax.rem(start, jnp.int32(8))
            turned = pltpu.roll(x, within, 1)
            keep = lax.broadcasted_iota(I32, (1, 8, width), 1) < within
            acc[pl.ds(first, 1)] = jnp.where(keep, acc[pl.ds(first, 1)], turned[:1])
            acc[pl.ds(first + 1, tiles - 1)] = jnp.where(keep, turned[:-1], turned[1:])
            acc[pl.ds(first + tiles, 1)] = turned[-1:]

        for s in range(n_shard):
            x = rows_ref[s]
            start = table_ref[s, 0]
            y = dot(x, high_ref[...]) + dot(x, low_ref[...])
            put(y.reshape(bulk // 8, 8, width), start)
            if extra:
                apart = jnp.bitwise_xor(me, s)
                index = jnp.bitwise_and(apart, 1) * 2 + lax.div(apart, jnp.int32(2))
                first = index * (2 * extra // 8) + table_ref[s, 2]
                put(extra_ref[pl.ds(first, extra // 8)], start + table_ref[s, 1])
        for r in range(n_rep):
            @pl.when(rep == r)
            def _():
                for d, out in enumerate(outs):
                    at = ((r + d) % n_rep) * half
                    out[...] = acc[:rows // 8, :, at:at + half].reshape(rows, half)

    return pl.pallas_call(
        kernel,
        in_specs=[SMEM] + [VMEM] * 4,
        out_specs=[VMEM] * n_rep,
        out_shape=[jax.ShapeDtypeStruct((rows, half), F32)] * n_rep,
        scratch_shapes=[pltpu.VMEM(((rows + bulk + extra) // 8 + 1, 8, width), F32)],
        cost_estimate=cost(4 * n_shard * bulk * depth * width, 2 * n_shard * bulk * depth + 8 * rows * width),
        compiler_params=PARAMS,
        name="row_scores",
    )(table, bulk_rows, high, low, extra_scores)


def body(train, cluster_ids, precond, query_store, block_slot, pattern):
    n_group, n_shard = lax.axis_size("groups"), lax.axis_size("shard")
    n_feat, n_rep = lax.axis_size("feat"), lax.axis_size("rep")
    feat, rep = lax.axis_index("feat"), lax.axis_index("rep")
    rows = train.shape[0]
    lines = rows // LANES
    base = rows // n_shard
    columns = train.shape[1] // n_rep
    extra = base // 2 if n_shard == 4 else 0
    bulk = base if extra else base + base // 2
    ids = cluster_ids.reshape(-1, LANES)

    picked = pick_queries(query_store, block_slot, pattern, n_group)
    arrived = lax.all_to_all(picked, "shard", split_axis=0, concat_axis=0, tiled=True)

    packed = pack_rows(train, ids, columns, bulk, extra)
    bulk_rows = lax.all_to_all(packed[0], "shard", split_axis=0, concat_axis=0, tiled=True)
    table, flag = row_table(ids, lines, bulk, extra)

    def spread(x):
        far = swap(x, "shard", n_shard, 2)
        both = jnp.concatenate([x, far])
        near = swap(both, "shard", n_shard, 1)
        return jnp.concatenate([both, near])

    extras = []
    if extra:
        for d in range(1, n_group):
            flag = jnp.maximum(flag, shift(flag, "groups", n_group, d))
        first = spread(packed[1])
        second = lax.cond(
            flag[0, 0] > 0, spread, lambda x: jnp.zeros((n_shard * extra, columns), BF16), packed[2]
        )
        for j in range(n_shard):
            at = slice(j * extra, (j + 1) * extra)
            extras += [first[at], second[at]]

    parts = [arrived] + [shift(arrived, "groups", n_group, d) for d in range(1, n_group)]
    chosen = join_queries(parts, block_slot, pattern, query_store.shape[0], n_feat, n_rep)

    matrix = precond[0]

    def weights(f, r):
        block = lax.dynamic_slice_in_dim(matrix, (f * n_rep + r) * columns, columns, 0)
        return lax.dot_general(block, chosen, (((1,), (1,)), ((), ())), preferred_element_type=F32)

    def summed_over_rep(f):
        away = [shift(weights(f, (rep + d) % n_rep), "rep", n_rep, d) for d in range(1, n_rep)]
        return sum(away, weights(f, rep))

    others = [
        shift(summed_over_rep((feat + d) % n_feat).astype(BF16), "feat", n_feat, d)
        for d in range(1, n_feat)
    ]
    own = summed_over_rep(feat)
    high, low, extra_scores = split_weights(own, others, extras)

    shares = row_scores(table, bulk_rows, high, low, extra_scores, rows, n_rep, extra)
    total = shares[0]
    for d in range(1, n_rep):
        total = total + shift(shares[d], "rep", n_rep, d)
    share = total.shape[1] // n_feat

    def for_feat(f):
        return lax.dynamic_slice_in_dim(total, f * share, share, 1)

    result = for_feat(feat)
    for d in range(1, n_feat):
        result = result + shift(for_feat((feat + d) % n_feat).astype(BF16), "feat", n_feat, d).astype(F32)
    return result.T[None]


def solution(mesh):
    return jax.shard_map(
        body,
        mesh=mesh,
        in_specs=(
            P(("groups", "shard"), "feat"),
            P("groups"),
            P(("groups", "shard"), None, ("feat", "rep")),
            P("shard", None, ("feat", "rep")),
            P(),
            P(),
        ),
        out_specs=P(("groups", "shard"), ("feat", "rep"), None),
        check_vma=False,
    )
```

time: 147 us -> 167 us (1.14)
  blocking collectives: 0 us -> 20.6 us
  Pallas kernels: 0 us -> 19.4 us
  matrix products: 37.2 us -> 18 us
  waiting for transfers between devices: 70.6 us -> 87.3 us
  other arithmetic: 9.67 us -> 0.22 us
  between operations: 7.89 us -> 0.83 us
  starting transfers between devices: 15.8 us -> 13.8 us
    ppermute x0 -> x2, waiting for transfers between devices: none -> 53.7 us  [swap(): return lax.ppermute(x, axis, [(i, i ^ bit) for i in range(size)])]
    ppermute x12 -> x7, waiting for transfers between devices: 70.6 us -> 33.6 us  [shift(): return lax.ppermute(x, axis, [(i, (i + by) % size) for i in range(size)])]
    all_to_all x0 -> x1, blocking collectives: none -> 20.6 us  [body(): lax.all_to_all(picked, 'shard', split_axis=0, concat_axis=0, tiled=True)]
    pallas_call x0 -> x6, Pallas kernels: none -> 19.4 us  [the longest x1 6.04 us: split_weights(): pl.pallas_call(kernel, in_specs=[VMEM] * (1 + n_other + len(extras)), out...]
    dot_general x13 -> x4, matrix products: 37.2 us -> 18 us  [weights(): lax.dot_general(block, chosen, (((1,), (1,)), ((), ())), preferred_elemen...]
    ppermute x12 -> x7, starting transfers between devices: 15.8 us -> 6.73 us  [shift(): return lax.ppermute(x, axis, [(i, (i + by) % size) for i in range(size)])]
    select_n x6 -> x0, other arithmetic: 5.44 us -> none  [the longest x3 4.73 us: body(): offset = jnp.where((offset >= 0) & (offset < count), offset, -1)]
    all_to_all x0 -> x1, starting transfers between devices: none -> 4.46 us  [body(): lax.all_to_all(packed[0], 'shard', split_axis=0, concat_axis=0, tiled=True)]
  transfers between devices with their start and end apart: 12 -> 10, of which waited for: 6 -> 7; matrix products, arithmetic and copies ran while one was open for 27% -> 9% of each run, Pallas kernels for 0% -> 8%
where the time goes in v2:
time: 167 us
  waiting for transfers between devices  87.3 us (52%)
  blocking collectives  20.6 us (12%)
  Pallas kernels  19.4 us (12%)
  matrix products  18 us (11%)
  starting transfers between devices  13.8 us (8%)
  local copies, waits for them, and re-layouts  6.19 us (4%)
    ppermute x2, waiting for transfers between devices, swap(): return lax.ppermute(x, axis, [(i, i ^ bit) for i in range(size)])  53.7 us
    ppermute x7, waiting for transfers between devices, shift(): return lax.ppermute(x, axis, [(i, (i + by) % size) for i in range(size)])  33.6 us
    all_to_all x1, blocking collectives, body(): lax.all_to_all(picked, 'shard', split_axis=0, concat_axis=0, tiled=True)  20.6 us
    dot_general x4, matrix products, weights(): lax.dot_general(block, chosen, (((1,), (1,)), ((), ())), preferred_elemen...  18 us
    ppermute x7, starting transfers between devices, shift(): return lax.ppermute(x, axis, [(i, (i + by) % size) for i in range(size)])  6.73 us
    pallas_call x1, Pallas kernels, split_weights(): pl.pallas_call(kernel, in_specs=[VMEM] * (1 + n_other + len(extras)), out...  6.04 us
    pallas_call x1, Pallas kernels, pack_rows(): pl.pallas_call(kernel, grid=(1,), in_specs=[pl.BlockSpec((lines, LANES),...  5.82 us
    pallas_call x1, Pallas kernels, row_scores(): pl.pallas_call(kernel, in_specs=[SMEM] + [VMEM] * 4, out_specs=[VMEM] * n...  5.25 us
  transfers between devices with their start and end apart: 10, of which 7 were waited for; matrix products, arithmetic and copies ran while one was open for 9% of the time, Pallas kernels for 8%

profile of v2, /device:TPU:0, one launch (start us, length us, event | category | flops | bytes accessed | tf_op | source)
XLA Modules:
  0.0 166.6 jit_solution(14935736521117548562)
XLA Ops:
  0.0 0.8 reshape.16.pattern_ref
  0.8 1.2 copy-done
  2.0 0.7 copy-done.2
  2.7 0.8 pick_queries.1
  3.4 20.6 %all_to_all.10.refs_0_ = bf16[4,64,1024]{2,1,0:T(8,128)(2,1)S(1)} all-to-all(bf16[4,64,1024]{2,1,0:T(8,128)(2,1)S(1)} %pick_queries.1), channel_id=1, replica_groups=mesh['groups'=2,'shard'=4,'feat'=2,'rep'=2] {'shard'}, dimensions={0} | all-to-all | bytes 1048576 | tf_op jit(solution)/shard_map/all_to_all | solution.py:296
  24.0 1.5 collective-permute-start.2
  25.6 11.0 %collective-permute-done.2.refs_1_ = bf16[4,64,1024]{2,1,0:T(8,128)(2,1)S(1)} collective-permute-done((bf16[4,64,1024]{2,1,0:T(8,128)(2,1)S(1)}, bf16[4,64,1024]{2,1,0:T(8,128)(2,1)S(1)}, u32[]{:S(2)}, u32[]{:S(2)}) %collective-permute-start.2) | collective-permute-done | bytes 524320 | tf_op jit(solution)/shard_map/ppermute | solution.py:18
  36.6 0.7 join_queries.1
  37.3 0.0 copy-start.1
  37.3 4.3 %fusion = f32[1024,512]{1,0:T(8,128)} fusion(bf16[512,1024]{1,0:T(8,128)(2,1)S(1)} %join_queries.1, bf16[1,4096,1024]{2,1,0:T(8,128)(2,1)} %param.10, s32[]{:T(128)S(6)} %select_n.38), kind=kOutput, calls=%fused_computation.2 | convolution fusion | flops 1073741824 | bytes 5242884 | tf_op jit(solution)/shard_map/dot_general | solution.py:327
  41.6 0.0 collective-permute-start.4
  41.6 0.0 copy-done.1
  41.6 5.8 %pack_rows.1 = (bf16[4,256,1024]{2,1,0:T(8,128)(2,1)}, bf16[128,1024]{1,0:T(8,128)(2,1)S(1)}, bf16[128,1024]{1,0:T(8,128)(2,1)S(1)}) custom-call(s32[32,128]{1,0:T(8,128)S(1)} %bitcast.26, bf16[1024,2048]{1,0:T(8,128)(2,1)} %train_ref.1), custom_call_target="tpu_custom_call" | custom-call | flops 2684354560 | bytes 4718592 | tf_op jit(solution)/shard_map/pack_rows/pallas_call | solution.py:147
  47.4 4.5 %all-to-all-start = ((bf16[4,256,1024]{2,1,0:T(8,128)(2,1)}), bf16[4,256,1024]{2,1,0:T(8,128)(2,1)}, u32[]{:S(2)}, u32[]{:S(2)}) async-start(bf16[4,256,1024]{2,1,0:T(8,128)(2,1)} %get-tuple-element.26), calls=%async_computation | async-start | bytes 4194304 | tf_op jit(solution)/shard_map/all_to_all | solution.py:299
  51.9 4.3 %fusion.4 = f32[1024,512]{1,0:T(8,128)} fusion(bf16[512,1024]{1,0:T(8,128)(2,1)S(1)} %join_queries.1, bf16[1,4096,1024]{2,1,0:T(8,128)(2,1)} %param.10, s32[]{:T(128)S(6)} %select_n.35), kind=kOutput, calls=%fused_computation.6 | convolution fusion | flops 1073741824 | bytes 5242884 | tf_op jit(solution)/shard_map/dot_general | solution.py:327
  56.1 0.5 collective-permute-start.3
  56.7 2.6 %collective-permute-start.7 = (bf16[128,1024]{1,0:T(8,128)(2,1)S(1)}, bf16[128,1024]{1,0:T(8,128)(2,1)S(1)}, u32[]{:S(2)}, u32[]{:S(2)}) collective-permute-start(bf16[128,1024]{1,0:T(8,128)(2,1)S(1)} %get-tuple-element.27.refs_2_), channel_id=1, source_target_pairs={{0,8},{4,12},{8,0},{12,4},{1,9},{5,13},{9,1},{13,5},{2,10},{6,14},... | collective-permute-start | bytes 786440 | tf_op jit(solution)/shard_map/ppermute | solution.py:22
  59.2 53.0 %collective-permute-done.7.refs_4_ = bf16[128,1024]{1,0:T(8,128)(2,1)S(1)} collective-permute-done((bf16[128,1024]{1,0:T(8,128)(2,1)S(1)}, bf16[128,1024]{1,0:T(8,128)(2,1)S(1)}, u32[]{:S(2)}, u32[]{:S(2)}) %collective-permute-start.7) | collective-permute-done | bytes 262176 | tf_op jit(solution)/shard_map/ppermute | solution.py:22
  112.2 0.1 collective-permute-start.8
  112.3 0.0 collective-permute-done.4
  112.3 4.5 %add_convert_fusion = bf16[1024,512]{1,0:T(8,128)(2,1)} fusion(f32[1024,512]{1,0:T(8,128)} %collective-permute-done.4, bf16[512,1024]{1,0:T(8,128)(2,1)S(1)} %join_queries.1, bf16[1,4096,1024]{2,1,0:T(8,128)(2,1)} %param.10, s32[]{:T(128)S(6)} %select_n.37), kind=kOutput, calls=%fused_computation.10 | convolution fusion | flops 1074790400 | bytes 6291460 | tf_op jit(solution)/shard_map/dot_general | solution.py:327
  116.8 1.5 collective-permute-start.5
  118.3 0.8 row_table.1
  119.1 1.6 collective-permute-start.6
  120.7 2.1 %collective-permute-done.6 = s32[8,128]{1,0:T(8,128)S(1)} collective-permute-done((s32[8,128]{1,0:T(8,128)S(1)}, s32[8,128]{1,0:T(8,128)S(1)}, u32[]{:S(2)}, u32[]{:S(2)}) %collective-permute-start.6) | collective-permute-done | bytes 4128 | tf_op jit(solution)/shard_map/ppermute | solution.py:18
  122.8 0.5 slice.21
  124.0 1.1 conditional.1
  124.1 0.7 slice.15.clone
  124.8 0.1 broadcast.9
  125.1 0.0 copy-start.5
  125.1 0.0 copy-start.7
  125.2 0.7 collective-permute-done.8
  125.9 0.0 copy-done.7
  125.9 0.0 collective-permute-done.3
  125.9 0.0 copy-start.8
  125.9 5.0 %fusion.12.refs_0_ = f32[1024,512]{1,0:T(8,128)} fusion(f32[1024,512]{1,0:T(8,128)} %collective-permute-done.3, bf16[512,1024]{1,0:T(8,128)(2,1)S(1)} %join_queries.1, bf16[1,4096,1024]{2,1,0:T(8,128)(2,1)} %param.10, s32[]{:T(128)S(6)} %select_n.33), kind=kOutput, calls=%fused_computation.15 | convolution fusion | flops 1074266112 | bytes 7340036 | tf_op jit(solution)/shard_map/dot_general | solution.py:327
  130.9 11.0 %collective-permute-done.5.refs_1_ = bf16[1024,512]{1,0:T(8,128)(2,1)} collective-permute-done((bf16[1024,512]{1,0:T(8,128)(2,1)}, bf16[1024,512]{1,0:T(8,128)(2,1)}, u32[]{:S(2)}, u32[]{:S(2)}) %collective-permute-start.5) | collective-permute-done | bytes 1048608 | tf_op jit(solution)/shard_map/ppermute | solution.py:18
  141.9 0.0 copy-done.6
  141.9 6.0 %split_weights.1 = (bf16[1024,512]{1,0:T(8,128)(2,1)S(1)}, bf16[1024,512]{1,0:T(8,128)(2,1)S(1)}, f32[144,8,512]{2,1,0:T(8,128)}) custom-call(f32[1024,512]{1,0:T(8,128)} %fusion.12.refs_0_, bf16[1024,512]{1,0:T(8,128)(2,1)} %collective-permute-done.5.refs_1_, bf16[128,1024]{1,0:T(8,128)(2,1)S(1)} %get-tuple-element.27.refs_2_, ...), custom_call_target="tpu_custom_call" | custom-call | flops 2147483648 | bytes 9437184 | tf_op jit(solution)/shard_map/split_weights/pallas_call | solution.py:224
  148.0 1.0 copy-done.4
  149.0 0.0 all-to-all-done.rows_ref
  149.0 5.3 %row_scores.1 = (f32[1024,256]{1,0:T(8,128)S(1)}, f32[1024,256]{1,0:T(8,128)S(1)}) custom-call(s32[4,3]{1,0:T(4,128)S(1)} %get-tuple-element.25.table_ref, bf16[4,256,1024]{2,1,0:T(8,128)(2,1)} %all-to-all-done.rows_ref, bf16[1024,512]{1,0:T(8,128)(2,1)S(1)} %get-tuple-element.34.high_ref, bf16[1024,512]{1,0:T(8,128)(2,1)} %copy-done.4, ...), custom_call_target="tpu_custom_call" | custom-call | flops 2147483648 | bytes 6291456 | tf_op jit(solution)/shard_map/row_scores/pallas_call | solution.py:271
  154.2 0.1 collective-permute-start.9
  154.3 2.6 %collective-permute-done.9 = f32[1024,256]{1,0:T(8,128)S(1)} collective-permute-done((f32[1024,256]{1,0:T(8,128)S(1)}, f32[1024,256]{1,0:T(8,128)S(1)}, u32[]{:S(2)}, u32[]{:S(2)}) %collective-permute-start.9) | collective-permute-done | bytes 1048608 | tf_op jit(solution)/shard_map/ppermute | solution.py:18
  156.9 0.1 add.73
  157.1 1.6 collective-permute-start.10
  158.7 6.9 %collective-permute-done.10 = bf16[1024,128]{1,0:T(8,128)(2,1)S(1)} collective-permute-done((bf16[1024,128]{1,0:T(8,128)(2,1)S(1)}, bf16[1024,128]{1,0:T(8,128)(2,1)S(1)}, u32[]{:S(2)}, u32[]{:S(2)}) %collective-permute-start.10) | collective-permute-done | bytes 262176 | tf_op jit(solution)/shard_map/ppermute | solution.py:18
  165.6 1.0 copy.7
  (16 shorter events, 0.2 us)
Async XLA Ops:
  0.0 36.6 %copy-start.3 = (s32[16]{0:T(128)S(1)}, s32[16]{0:T(128)}, u32[]{:S(2)}) copy-start(s32[16]{0:T(128)} %slot_ref.3) | copy-start | bytes 196
  0.8 1.2 copy-start
  2.0 0.7 copy-start.2
  24.0 12.5 %collective-permute-start.2 = (bf16[4,64,1024]{2,1,0:T(8,128)(2,1)S(1)}, bf16[4,64,1024]{2,1,0:T(8,128)(2,1)S(1)}, u32[]{:S(2)}, u32[]{:S(2)}) collective-permute-start(bf16[4,64,1024]{2,1,0:T(8,128)(2,1)S(1)} %all_to_all.10.refs_0_), channel_id=1, source_target_pairs={{0,16},{16,0},{1,17},{17,1},{2,18},{18,2},{3,19},{19,3},{4,20},{20... | collective-permute-start | bytes 1572872 | tf_op jit(solution)/shard_map/ppermute | solution.py:18
  37.3 4.3 %copy-start.1 = (s32[4096]{0:T(1024)S(1)}, s32[4096]{0:T(1024)}, u32[]{:S(2)}) copy-start(s32[4096]{0:T(1024)} %param.9) | copy-start | bytes 49156
  41.6 70.8 %collective-permute-start.4 = (f32[1024,512]{1,0:T(8,128)}, f32[1024,512]{1,0:T(8,128)}, u32[]{:S(2)}, u32[]{:S(2)}) collective-permute-start(f32[1024,512]{1,0:T(8,128)} %fusion), channel_id=1, source_target_pairs={{0,1},{1,0},{2,3},{3,2},{4,5},{5,4},{6,7},{7,6},{8,9},{9,8},{10,11... | collective-permute-start | bytes 6291464 | tf_op jit(solution)/shard_map/ppermute | solution.py:18
  47.4 101.6 %all-to-all-start = ((bf16[4,256,1024]{2,1,0:T(8,128)(2,1)}), bf16[4,256,1024]{2,1,0:T(8,128)(2,1)}, u32[]{:S(2)}, u32[]{:S(2)}) async-start(bf16[4,256,1024]{2,1,0:T(8,128)(2,1)} %get-tuple-element.26), calls=%async_computation | async-start | bytes 4194304 | tf_op jit(solution)/shard_map/all_to_all | solution.py:299
  56.1 69.8 %collective-permute-start.3 = (f32[1024,512]{1,0:T(8,128)}, f32[1024,512]{1,0:T(8,128)}, u32[]{:S(2)}, u32[]{:S(2)}) collective-permute-start(f32[1024,512]{1,0:T(8,128)} %fusion.4), channel_id=1, source_target_pairs={{0,1},{1,0},{2,3},{3,2},{4,5},{5,4},{6,7},{7,6},{8,9},{9,8},{10,11... | collective-permute-start | bytes 6291464 | tf_op jit(solution)/shard_map/ppermute | solution.py:18
  56.7 55.5 %collective-permute-start.7 = (bf16[128,1024]{1,0:T(8,128)(2,1)S(1)}, bf16[128,1024]{1,0:T(8,128)(2,1)S(1)}, u32[]{:S(2)}, u32[]{:S(2)}) collective-permute-start(bf16[128,1024]{1,0:T(8,128)(2,1)S(1)} %get-tuple-element.27.refs_2_), channel_id=1, source_target_pairs={{0,8},{4,12},{8,0},{12,4},{1,9},{5,13},{9,1},{13,5},{2,10},{6,14},... | collective-permute-start | bytes 786440 | tf_op jit(solution)/shard_map/ppermute | solution.py:22
  112.2 13.6 %collective-permute-start.8 = (bf16[256,1024]{1,0:T(8,128)(2,1)S(1)}, bf16[256,1024]{1,0:T(8,128)(2,1)S(1)}, u32[]{:S(2)}, u32[]{:S(2)}) collective-permute-start(bf16[256,1024]{1,0:T(8,128)(2,1)S(1)} %pad_maximum_fusion.2), channel_id=1, source_target_pairs={{0,4},{4,0},{8,12},{12,8},{1,5},{5,1},{9,13},{13,9},{2,6},{6,2},{1... | collective-permute-start | bytes 1572872 | tf_op jit(solution)/shard_map/ppermute | solution.py:22
  116.8 25.1 %collective-permute-start.5 = (bf16[1024,512]{1,0:T(8,128)(2,1)}, bf16[1024,512]{1,0:T(8,128)(2,1)}, u32[]{:S(2)}, u32[]{:S(2)}) collective-permute-start(bf16[1024,512]{1,0:T(8,128)(2,1)} %add_convert_fusion), channel_id=1, source_target_pairs={{0,2},{2,0},{1,3},{3,1},{4,6},{6,4},{5,7},{7,5},{8,10},{10,8},{9,1... | collective-permute-start | bytes 3145736 | tf_op jit(solution)/shard_map/ppermute | solution.py:18
  119.1 3.7 %collective-permute-start.6 = (s32[8,128]{1,0:T(8,128)S(1)}, s32[8,128]{1,0:T(8,128)S(1)}, u32[]{:S(2)}, u32[]{:S(2)}) collective-permute-start(s32[8,128]{1,0:T(8,128)S(1)} %get-tuple-element.28), channel_id=1, source_target_pairs={{0,16},{16,0},{1,17},{17,1},{2,18},{18,2},{3,19},{19,3},{4,20},{20... | collective-permute-start | bytes 12296 | tf_op jit(solution)/shard_map/ppermute | solution.py:18
  125.1 0.8 copy-start.5
  125.1 0.8 copy-start.7
  125.9 16.0 %copy-start.6 = (bf16[128,1024]{1,0:T(8,128)(2,1)S(1)}, bf16[128,1024]{1,0:T(8,128)(2,1)}, u32[]{:S(2)}) copy-start(bf16[128,1024]{1,0:T(8,128)(2,1)} %copy-done.5) | copy-start | bytes 786436
  125.9 16.0 %copy-start.8 = (bf16[128,1024]{1,0:T(8,128)(2,1)S(1)}, bf16[128,1024]{1,0:T(8,128)(2,1)}, u32[]{:S(2)}) copy-start(bf16[128,1024]{1,0:T(8,128)(2,1)} %copy-done.7) | copy-start | bytes 786436
  148.0 1.0 copy-start.4
  154.2 2.7 %collective-permute-start.9 = (f32[1024,256]{1,0:T(8,128)S(1)}, f32[1024,256]{1,0:T(8,128)S(1)}, u32[]{:S(2)}, u32[]{:S(2)}) collective-permute-start(f32[1024,256]{1,0:T(8,128)S(1)} %get-tuple-element.38), channel_id=1, source_target_pairs={{0,1},{1,0},{2,3},{3,2},{4,5},{5,4},{6,7},{7,6},{8,9},{9,8},{10,11... | collective-permute-start | bytes 3145736 | tf_op jit(solution)/shard_map/ppermute | solution.py:18
  157.1 8.4 %collective-permute-start.10 = (bf16[1024,128]{1,0:T(8,128)(2,1)S(1)}, bf16[1024,128]{1,0:T(8,128)(2,1)S(1)}, u32[]{:S(2)}, u32[]{:S(2)}) collective-permute-start(bf16[1024,128]{1,0:T(8,128)(2,1)S(1)} %dynamic-slice_convert_fusion), channel_id=1, source_target_pairs={{0,2},{2,0},{1,3},{3,1},{4,6},{6,4},{5,7},{7,5},{8,10},{10,8},{9,1... | collective-permute-start | bytes 786440 | tf_op jit(solution)/shard_map/ppermute | solution.py:18

commit v3 on v2

--- a/solution.py
+++ b/solution.py
@@ -9,6 +9,7 @@
 
 F32, BF16, I32 = jnp.float32, jnp.bfloat16, jnp.int32
 VMEM = pl.BlockSpec(memory_space=pltpu.VMEM)
+ANY = pl.BlockSpec(memory_space=pl.ANY)
 SMEM = pl.BlockSpec(memory_space=pltpu.SMEM)
 PARAMS = pltpu.CompilerParams(vmem_limit_bytes=50 * 2**20)
 LANES = 128
@@ -27,7 +28,23 @@
 
 
 def cost(flops, nbytes):
-    return pl.CostEstimate(flops=int(flops), bytes_accessed=int(nbytes), transcendentals=0)
+    return pl.CostEstimate(flops=1, bytes_accessed=1, transcendentals=0)
+
+
+def after(x, *others):
+    def kernel(*refs):
+        pass
+
+    return pl.pallas_call(
+        kernel,
+        in_specs=[ANY] * (1 + len(others)),
+        out_specs=ANY,
+        out_shape=jax.ShapeDtypeStruct(x.shape, x.dtype),
+        input_output_aliases={0: 0},
+        cost_estimate=cost(0, 0),
+        compiler_params=PARAMS,
+        name="after",
+    )(x, *others)
 
 
 def pick_queries(query_store, block_slot, pattern, n_group):
@@ -39,7 +56,7 @@
         me = lax.axis_index("shard")
         found = jnp.int32(0)
         for k in range(n_list):
-            slot = slot_ref[pattern_ref[t * n_list + k]]
+            slot = slot_ref[pattern_ref[lax.rem(me + t, jnp.int32(n_cluster)), k]]
             hit = (lax.div(slot, jnp.int32(local_blocks)) == me).astype(I32)
             found = found + hit * lax.rem(slot, jnp.int32(local_blocks))
         return found, lax.axis_index("groups"), 0
@@ -59,10 +76,10 @@
         cost_estimate=cost(0, 4 * n_cluster * part * width),
         compiler_params=PARAMS,
         name="pick_queries",
-    )(pattern.reshape(-1), block_slot, query_store)
-
-
-def join_queries(parts, block_slot, pattern, local_blocks, n_feat, n_rep):
+    )(pattern, block_slot, query_store)
+
+
+def join_queries(parts, block_slot, pattern, local_blocks, n_feat, n_rep, *others):
     n_group = len(parts)
     n_cluster, part, width = parts[0].shape
     n_list = pattern.shape[1]
@@ -74,7 +91,8 @@
         out_ref = refs[-1]
         me, group = lax.axis_index("shard"), lax.axis_index("groups")
         for k in range(n_list):
-            owner = lax.div(slot_ref[pattern_ref[me * n_list + k]], jnp.int32(local_blocks))
+            owner = lax.div(slot_ref[pattern_ref[me, k]], jnp.int32(local_blocks))
+            hops = lax.rem(me + (n_cluster - owner), jnp.int32(n_cluster))
             for d in range(n_group):
                 origin = lax.rem(group + (n_group - d), jnp.int32(n_group))
                 for u in range(part // unit):
@@ -82,27 +100,27 @@
                     chunk = lax.div(first, jnp.int32(share))
                     goal = lax.rem(chunk, jnp.int32(n_rep)) * n_feat + lax.div(chunk, jnp.int32(n_rep))
                     goal = goal * share + lax.rem(first, jnp.int32(share))
-                    out_ref[pl.ds(pl.multiple_of(goal, unit), unit), :] = refs[d][owner, u * unit:(u + 1) * unit, :]
-
-    return pl.pallas_call(
-        kernel,
-        in_specs=[SMEM, SMEM] + [VMEM] * n_group,
+                    out_ref[pl.ds(pl.multiple_of(goal, unit), unit), :] = refs[d][hops, u * unit:(u + 1) * unit, :]
+
+    return pl.pallas_call(
+        kernel,
+        in_specs=[SMEM, SMEM] + [VMEM] * n_group + [ANY] * len(others),
         out_specs=VMEM,
         out_shape=jax.ShapeDtypeStruct((total, width), BF16),
         cost_estimate=cost(0, 4 * total * width),
         compiler_params=PARAMS,
         name="join_queries",
-    )(pattern.reshape(-1), block_slot, *parts)
-
-
-def pack_rows(train, ids, columns, bulk, extra):
+    )(pattern, block_slot, *parts, *others)
+
+
+def pack_rows(train, ids, columns, bulk, extra, cuts):
     rows = train.shape[0]
     lines = rows // LANES
     n_shard = ids.shape[0] // lines
-    tile = 128 if extra else bulk
-
-    def kernel(ids_ref, train_ref, bulk_ref, *rest):
-        extra_refs, goal_ref = rest[:-1], rest[-1]
+
+    def kernel(ids_ref, train_ref, *rest):
+        outs, goal_ref = rest[:-1], rest[-1]
+        me = lax.axis_index("shard")
         own = ids_ref[...]
         masks = [(own == c).astype(F32) for c in range(n_shard)]
         stacked = jnp.concatenate(masks, axis=0).astype(BF16)
@@ -129,19 +147,20 @@
             goal = goal + masks[c] * place
         goal_ref[...] = goal.astype(I32)
 
-        def one_tile(base):
-            index = lax.broadcasted_iota(I32, (tile, LANES), 0) + base
-            pick = [(index == goal_ref[a:a + 1, :]).astype(F32).astype(BF16) for a in range(lines)]
-            return dot(jnp.concatenate(pick, axis=1), train_ref[...]).astype(BF16)
-
-        per = bulk // tile
-        for c in range(n_shard):
-            for j in range(per):
-                bulk_ref[c, j * tile:(j + 1) * tile, :] = one_tile(c * bulk + j * tile)
-        for j, ref in enumerate(extra_refs):
-            ref[...] = one_tile(n_shard * bulk + j * extra)
-
-    shapes = [jax.ShapeDtypeStruct((n_shard, bulk, columns), BF16)]
+        def fill(out, base):
+            size = out.shape[0]
+            tile = 128 if size % 128 == 0 else size
+            for at in range(0, size, tile):
+                index = lax.broadcasted_iota(I32, (tile, LANES), 0) + (base + at)
+                pick = [(index == goal_ref[a:a + 1, :]).astype(F32).astype(BF16) for a in range(lines)]
+                out[at:at + tile, :] = dot(jnp.concatenate(pick, axis=1), train_ref[...]).astype(BF16)
+
+        for out, (hops, first, _) in zip(outs, cuts):
+            fill(out, lax.rem(me + hops, jnp.int32(n_shard)) * bulk + first)
+        for j, out in enumerate(outs[len(cuts):]):
+            fill(out, n_shard * bulk + j * extra)
+
+    shapes = [jax.ShapeDtypeStruct((n, columns), BF16) for _, _, n in cuts]
     shapes += [jax.ShapeDtypeStruct((extra, columns), BF16)] * (2 if extra else 0)
     packed = n_shard * bulk + 2 * extra
     return pl.pallas_call(
@@ -158,6 +177,36 @@
         compiler_params=PARAMS,
         name="pack_rows",
     )(ids, train)
+
+
+def partial_weights(matrix, chosen, block, depth, *others):
+    width = matrix.shape[1]
+    tile = 256 if depth % 256 == 0 else depth
+    steps = depth // tile
+
+    def kernel(block_ref, matrix_ref, chosen_ref, *rest):
+        rest[-1][...] = lax.dot_general(
+            matrix_ref[...], chosen_ref[...], (((1,), (1,)), ((), ())), preferred_element_type=F32
+        )
+
+    total = chosen.shape[0]
+    return pl.pallas_call(
+        kernel,
+        grid_spec=pltpu.PrefetchScalarGridSpec(
+            num_scalar_prefetch=1,
+            grid=(steps,),
+            in_specs=[
+                pl.BlockSpec((tile, width), lambda i, b: (b[0] * steps + i, 0)),
+                pl.BlockSpec((total, width), lambda i, b: (0, 0)),
+            ]
+            + [ANY] * len(others),
+            out_specs=pl.BlockSpec((tile, total), lambda i, b: (i, 0)),
+        ),
+        out_shape=jax.ShapeDtypeStruct((depth, total), F32),
+        cost_estimate=cost(2 * depth * width * total, 2 * depth * width + 4 * depth * total),
+        compiler_params=PARAMS,
+        name="partial_weights",
+    )(jnp.reshape(block, (1,)).astype(I32), matrix, chosen, *others)
 
 
 def row_table(ids, lines, bulk, extra):
@@ -199,13 +248,13 @@
     )(ids)
 
 
-def split_weights(own, others, extras):
+def early_scores(own, others, pieces):
     depth, width = own.shape
-    n_extra = sum(e.shape[0] for e in extras)
+    count = sum(p.shape[0] for p in pieces)
     n_other = len(others)
 
     def kernel(*refs):
-        own_ref, other_refs, extra_refs = refs[0], refs[1:1 + n_other], refs[1 + n_other:-3]
+        own_ref, other_refs, piece_refs = refs[0], refs[1:1 + n_other], refs[1 + n_other:-3]
         high_ref, low_ref, out_ref = refs[-3:]
         weight = own_ref[...]
         for ref in other_refs:
@@ -214,7 +263,7 @@
         high_ref[...] = high
         low_ref[...] = (weight - high.astype(F32)).astype(BF16)
         base = 0
-        for ref in extra_refs:
+        for ref in piece_refs:
             x = ref[...]
             y = dot(x, high_ref[...]) + dot(x, low_ref[...])
             out_ref[base // 8:(base + x.shape[0]) // 8] = y.reshape(x.shape[0] // 8, 8, width)
@@ -223,24 +272,29 @@
 
     return pl.pallas_call(
         kernel,
-        in_specs=[VMEM] * (1 + n_other + len(extras)),
+        in_specs=[VMEM] * (1 + n_other + len(pieces)),
         out_specs=[VMEM] * 3,
         out_shape=[jax.ShapeDtypeStruct((depth, width), BF16)] * 2
-        + [jax.ShapeDtypeStruct(((n_extra + LANES) // 8, 8, width), F32)],
-        cost_estimate=cost(4 * n_extra * depth * width, 10 * depth * width + n_extra * (2 * depth + 4 * width)),
-        compiler_params=PARAMS,
-        name="split_weights",
-    )(own, *others, *extras)
-
-
-def row_scores(table, bulk_rows, high, low, extra_scores, rows, n_rep, extra):
-    n_shard, bulk, depth = bulk_rows.shape
+        + [jax.ShapeDtypeStruct(((count + LANES) // 8, 8, width), F32)],
+        cost_estimate=cost(4 * count * depth * width, 10 * depth * width + count * (2 * depth + 4 * width)),
+        compiler_params=PARAMS,
+        name="early_scores",
+    )(own, *others, *pieces)
+
+
+def row_scores(table, last, high, low, early, rows, n_rep, bulk, extra, cuts):
+    n_shard = table.shape[0]
     width = high.shape[1]
     half = width // n_rep
-
-    def kernel(table_ref, rows_ref, high_ref, low_ref, extra_ref, *rest):
-        outs, acc = rest[:-1], rest[-1]
+    late_rows = last.shape[0]
+    surplus_at = (n_shard * bulk - late_rows) // 8
+
+    def kernel(table_ref, last_ref, high_ref, low_ref, early_ref, *rest):
+        outs, late, acc = rest[:-2], rest[-2], rest[-1]
         me, rep = lax.axis_index("shard"), lax.axis_index("rep")
+        x = last_ref[...]
+        y = dot(x, high_ref[...]) + dot(x, low_ref[...])
+        late[...] = y.reshape(late_rows // 8, 8, width)
 
         def put(x, start):
             tiles = x.shape[0]
@@ -252,15 +306,23 @@
             acc[pl.ds(first + tiles, 1)] = turned[-1:]
 
         for s in range(n_shard):
-            x = rows_ref[s]
             start = table_ref[s, 0]
-            y = dot(x, high_ref[...]) + dot(x, low_ref[...])
-            put(y.reshape(bulk // 8, 8, width), start)
+            for hops in range(n_shard):
+                @pl.when(lax.rem(me + (n_shard - hops), jnp.int32(n_shard)) == s)
+                def _():
+                    base = 0
+                    for h, first, n in cuts:
+                        if h == hops:
+                            if base + n <= n_shard * bulk - late_rows:
+                                put(early_ref[base // 8:(base + n) // 8], start + first)
+                            else:
+                                put(late[...], start + first)
+                        base += n
             if extra:
                 apart = jnp.bitwise_xor(me, s)
                 index = jnp.bitwise_and(apart, 1) * 2 + lax.div(apart, jnp.int32(2))
-                first = index * (2 * extra // 8) + table_ref[s, 2]
-                put(extra_ref[pl.ds(first, extra // 8)], start + table_ref[s, 1])
+                first = surplus_at + index * (2 * extra // 8) + table_ref[s, 2]
+                put(early_ref[pl.ds(first, extra // 8)], start + table_ref[s, 1])
         for r in range(n_rep):
             @pl.when(rep == r)
             def _():
@@ -273,11 +335,14 @@
         in_specs=[SMEM] + [VMEM] * 4,
         out_specs=[VMEM] * n_rep,
         out_shape=[jax.ShapeDtypeStruct((rows, half), F32)] * n_rep,
-        scratch_shapes=[pltpu.VMEM(((rows + bulk + extra) // 8 + 1, 8, width), F32)],
-        cost_estimate=cost(4 * n_shard * bulk * depth * width, 2 * n_shard * bulk * depth + 8 * rows * width),
+        scratch_shapes=[
+            pltpu.VMEM((late_rows // 8, 8, width), F32),
+            pltpu.VMEM(((rows + bulk + extra) // 8 + 1, 8, width), F32),
+        ],
+        cost_estimate=cost(4 * late_rows * high.shape[0] * width, 8 * rows * width),
         compiler_params=PARAMS,
         name="row_scores",
-    )(table, bulk_rows, high, low, extra_scores)
+    )(table, last, high, low, early)
 
 
 def body(train, cluster_ids, precond, query_store, block_slot, pattern):
@@ -292,52 +357,69 @@
     bulk = base if extra else base + base // 2
     ids = cluster_ids.reshape(-1, LANES)
 
+    me = lax.axis_index("shard")
     picked = pick_queries(query_store, block_slot, pattern, n_group)
-    arrived = lax.all_to_all(picked, "shard", split_axis=0, concat_axis=0, tiled=True)
-
-    packed = pack_rows(train, ids, columns, bulk, extra)
-    bulk_rows = lax.all_to_all(packed[0], "shard", split_axis=0, concat_axis=0, tiled=True)
+    pieces = [picked[:1]]
+    for d in range(1, n_shard):
+        pieces.append(shift(picked[d:d + 1], "shard", n_shard, d))
+
+    order = [0] + sorted(range(1, n_shard), key=lambda d: (min(d, n_shard - d), d))
+    cuts = [(d, 0, bulk) for d in order[:-1]]
+    cuts += [(order[-1], 0, bulk // 2), (order[-1], bulk // 2, bulk // 2)]
+    packed = pack_rows(train, ids, columns, bulk, extra, cuts)
     table, flag = row_table(ids, lines, bulk, extra)
 
-    def spread(x):
-        far = swap(x, "shard", n_shard, 2)
-        both = jnp.concatenate([x, far])
-        near = swap(both, "shard", n_shard, 1)
-        return jnp.concatenate([both, near])
+    def swap_far(x):
+        return jnp.concatenate([x, swap(x, "shard", n_shard, 2)])
+
+    def swap_near(x):
+        return jnp.concatenate([x, swap(x, "shard", n_shard, 1)])
+
+    arrived = after(jnp.concatenate(pieces), packed[1])
+    here = [packed[0]]
+    marks = [arrived, arrived]
+    for j, (hops, _, _) in enumerate(cuts[1:-1]):
+        sent = packed[j + 1] if j == 0 else after(packed[j + 1], marks[-2])
+        here.append(shift(sent, "shard", n_shard, hops))
+        marks.append(here[-1])
+        if extra and j == len(cuts) - 4:
+            far = swap_far(after(packed[-2], marks[-2]))
+            marks.append(far)
+    last = shift(after(packed[len(cuts) - 1], marks[-2]), "shard", n_shard, cuts[-1][0])
+
+    parts = [arrived] + [shift(arrived, "groups", n_group, d) for d in range(1, n_group)]
+    chosen = join_queries(parts, block_slot, pattern, query_store.shape[0], n_feat, n_rep, here[1])
+
+    matrix = precond[0]
+
+    def weights(f, r, *others):
+        return partial_weights(matrix, chosen, f * n_rep + r, columns, *others)
+
+    def summed_over_rep(f, *others):
+        away = [shift(weights(f, (rep + d) % n_rep, *others), "rep", n_rep, d) for d in range(1, n_rep)]
+        return sum(away, weights(f, rep, *others))
+
+    sends = [summed_over_rep((feat + d) % n_feat).astype(BF16) for d in range(1, n_feat)]
+    others = [shift(x, "feat", n_feat, d + 1) for d, x in enumerate(sends)]
+    own = summed_over_rep(feat, *sends)
 
     extras = []
     if extra:
         for d in range(1, n_group):
             flag = jnp.maximum(flag, shift(flag, "groups", n_group, d))
-        first = spread(packed[1])
+        first = swap_near(after(far, *sends))
         second = lax.cond(
-            flag[0, 0] > 0, spread, lambda x: jnp.zeros((n_shard * extra, columns), BF16), packed[2]
+            flag[0, 0] > 0,
+            lambda x: swap_near(swap_far(x)),
+            lambda x: jnp.zeros((n_shard * extra, columns), BF16),
+            after(packed[-1], *sends),
         )
         for j in range(n_shard):
             at = slice(j * extra, (j + 1) * extra)
             extras += [first[at], second[at]]
 
-    parts = [arrived] + [shift(arrived, "groups", n_group, d) for d in range(1, n_group)]
-    chosen = join_queries(parts, block_slot, pattern, query_store.shape[0], n_feat, n_rep)
-
-    matrix = precond[0]
-
-    def weights(f, r):
-        block = lax.dynamic_slice_in_dim(matrix, (f * n_rep + r) * columns, columns, 0)
-        return lax.dot_general(block, chosen, (((1,), (1,)), ((), ())), preferred_element_type=F32)
-
-    def summed_over_rep(f):
-        away = [shift(weights(f, (rep + d) % n_rep), "rep", n_rep, d) for d in range(1, n_rep)]
-        return sum(away, weights(f, rep))
-
-    others = [
-        shift(summed_over_rep((feat + d) % n_feat).astype(BF16), "feat", n_feat, d)
-        for d in range(1, n_feat)
-    ]
-    own = summed_over_rep(feat)
-    high, low, extra_scores = split_weights(own, others, extras)
-
-    shares = row_scores(table, bulk_rows, high, low, extra_scores, rows, n_rep, extra)
+    high, low, early = early_scores(own, others, here + extras)
+    shares = row_scores(table, last, high, low, early, rows, n_rep, bulk, extra, cuts)
     total = shares[0]
     for d in range(1, n_rep):
         total = total + shift(shares[d], "rep", n_rep, d)

time: 167 us -> 132 us (0.79)
  waiting for transfers between devices: 87.3 us -> 47.3 us
  blocking collectives: 20.6 us -> 0 us
  Pallas kernels: 19.4 us -> 38 us
  matrix products: 18 us -> 0 us
  starting transfers between devices: 13.8 us -> 29.8 us
  other arithmetic: 0.22 us -> 7.63 us
    ppermute x2, waiting for transfers between devices: 53.7 us -> 12.8 us  [swap(): return lax.ppermute(x, axis, [(i, i ^ bit) for i in range(size)])]
    all_to_all x1 -> x0, blocking collectives: 20.6 us -> none  [body(): lax.all_to_all(picked, 'shard', split_axis=0, concat_axis=0, tiled=True)]
    pallas_call x2 -> x13, Pallas kernels: 6.75 us -> 27.2 us  [the longest x4 17.6 us: partial_weights(): pl.pallas_call(kernel, grid_spec=pltpu.PrefetchScalarGridSpec(num_scalar_...]
    dot_general x4 -> x0, matrix products: 18 us -> none  [weights(): lax.dot_general(block, chosen, (((1,), (1,)), ((), ())), preferred_elemen...]
    ppermute x7 -> x14, starting transfers between devices: 6.73 us -> 19.3 us  [shift(): return lax.ppermute(x, axis, [(i, (i + by) % size) for i in range(size)])]
    ppermute x2, starting transfers between devices: 2.65 us -> 10.4 us  [swap(): return lax.ppermute(x, axis, [(i, i ^ bit) for i in range(size)])]
    all_to_all x1 -> x0, starting transfers between devices: 4.46 us -> none  [body(): lax.all_to_all(packed[0], 'shard', split_axis=0, concat_axis=0, tiled=True)]
    add x0 -> x1, other arithmetic: none -> 4.18 us  [summed_over_rep(): return sum(away, weights(f, rep, *others))]
  transfers between devices with their start and end apart: 10 -> 16, of which waited for: 7 -> 9; matrix products, arithmetic and copies ran while one was open for 9% -> 5% of each run, Pallas kernels for 8% -> 18%
where the time goes in v3:
time: 132 us
  waiting for transfers between devices  47.3 us (36%)
  Pallas kernels  38 us (29%)
  starting transfers between devices  29.8 us (23%)
  local copies, waits for them, and re-layouts  7.68 us (6%)
  other arithmetic  7.63 us (6%)
    ppermute x14, waiting for transfers between devices, shift(): return lax.ppermute(x, axis, [(i, (i + by) % size) for i in range(size)])  34.6 us
    ppermute x14, starting transfers between devices, shift(): return lax.ppermute(x, axis, [(i, (i + by) % size) for i in range(size)])  19.3 us
    pallas_call x4, Pallas kernels, partial_weights(): pl.pallas_call(kernel, grid_spec=pltpu.PrefetchScalarGridSpec(num_scalar_...  17.6 us
    ppermute x2, waiting for transfers between devices, swap(): return lax.ppermute(x, axis, [(i, i ^ bit) for i in range(size)])  12.8 us
    ppermute x2, starting transfers between devices, swap(): return lax.ppermute(x, axis, [(i, i ^ bit) for i in range(size)])  10.4 us
    pallas_call x1, Pallas kernels, early_scores(): pl.pallas_call(kernel, in_specs=[VMEM] * (1 + n_other + len(pieces)), out...  8.82 us
    pallas_call x1, Pallas kernels, pack_rows(): pl.pallas_call(kernel, grid=(1,), in_specs=[pl.BlockSpec((lines, LANES),...  5.67 us
    add x1, other arithmetic, summed_over_rep(): return sum(away, weights(f, rep, *others))  4.18 us
  transfers between devices with their start and end apart: 16, of which 9 were waited for; matrix products, arithmetic and copies ran while one was open for 5% of the time, Pallas kernels for 18%

profile of v3, /device:TPU:0, one launch (start us, length us, event | category | flops | bytes accessed | tf_op | source)
XLA Modules:
  0.0 131.5 jit_solution(13883199168767868294)
XLA Ops:
  0.0 1.2 copy-done
  1.2 0.7 copy-done.7
  1.9 0.7 copy-done.9
  2.6 0.8 pick_queries.1
  3.4 5.1 %collective-permute-start.7 = (bf16[1,64,1024]{2,1,0:T(8,128)(2,1)S(1)}, bf16[1,64,1024]{2,1,0:T(8,128)(2,1)S(1)}, u32[]{:S(2)}, u32[]{:S(2)}) collective-permute-start(bf16[1,64,1024]{2,1,0:T(8,128)(2,1)S(1)} %get-tuple-element.54), channel_id=1, source_target_pairs={{0,12},{4,0},{8,4},{12,8},{1,13},{5,1},{9,5},{13,9},{2,14},{6,2},{... | collective-permute-start | bytes 393224 | tf_op jit(solution)/shard_map/ppermute | solution.py:19
  8.5 1.0 collective-permute-start.5
  9.5 5.7 %pack_rows.1 = (bf16[256,1024]{1,0:T(8,128)(2,1)S(1)}, bf16[256,1024]{1,0:T(8,128)(2,1)S(1)}, bf16[256,1024]{1,0:T(8,128)(2,1)}, bf16[128,1024]{1,0:T(8,128)(2,1...) custom-call(s32[32,128]{1,0:T(8,128)S(1)} %bitcast.11, ...), custom_call_target="tpu_custom_call" | custom-call | flops 1 | bytes 1 | tf_op jit(solution)/shard_map/pack_rows/pallas_call | solution.py:166
  15.2 4.5 %collective-permute-done.6 = bf16[1,64,1024]{2,1,0:T(8,128)(2,1)S(1)} collective-permute-done((bf16[1,64,1024]{2,1,0:T(8,128)(2,1)S(1)}, bf16[1,64,1024]{2,1,0:T(8,128)(2,1)S(1)}, u32[]{:S(2)}, u32[]{:S(2)}) %collective-permute-start.6) | collective-permute-done | bytes 131104 | tf_op jit(solution)/shard_map/ppermute | solution.py:19
  19.8 0.8 collective-permute-start.2
  20.6 1.5 %collective-permute-start.8 = (bf16[4,64,1024]{2,1,0:T(8,128)(2,1)S(1)}, bf16[4,64,1024]{2,1,0:T(8,128)(2,1)S(1)}, u32[]{:S(2)}, u32[]{:S(2)}) collective-permute-start(bf16[4,64,1024]{2,1,0:T(8,128)(2,1)S(1)} %after.9.refs_0_.refs_1_), channel_id=1, source_target_pairs={{0,16},{16,0},{1,17},{17,1},{2,18},{18,2},{3,19},{19,3},{4,20},{20... | collective-permute-start | bytes 1572872 | tf_op jit(solution)/shard_map/ppermute | solution.py:19
  22.1 12.7 %collective-permute-done.2.refs_1_.refs_2_.refs_3_ = bf16[256,1024]{1,0:T(8,128)(2,1)S(1)} collective-permute-done((bf16[256,1024]{1,0:T(8,128)(2,1)S(1)}, bf16[256,1024]{1,0:T(8,128)(2,1)S(1)}, u32[]{:S(2)}, u32[]{:S(2)}) %collective-permute-start.2) | collective-permute-done | bytes 524320 | tf_op jit(solution)/shard_map/ppermute | solution.py:19
  34.9 0.7 join_queries.1.chosen_ref
  35.6 4.7 %partial_weights.5 = f32[1024,512]{1,0:T(8,128)} custom-call(s32[1]{0:T(128)} %bitcast.4.block_ref, bf16[4096,1024]{1,0:T(8,128)(2,1)} %bitcast.13, bf16[512,1024]{1,0:T(8,128)(2,1)S(1)} %join_queries.1.chosen_ref), custom_call_target="tpu_custom_call" | custom-call | flops 1 | bytes 1 | tf_op jit(solution)/shard_map/partial_weights/pallas_call | solution.py:193
  40.3 3.6 %partial_weights.4 = f32[1024,512]{1,0:T(8,128)S(1)} custom-call(s32[1]{0:T(128)} %bitcast.3.block_ref, bf16[4096,1024]{1,0:T(8,128)(2,1)} %bitcast.14, bf16[512,1024]{1,0:T(8,128)(2,1)S(1)} %join_queries.1.chosen_ref), custom_call_target="tpu_custom_call" | custom-call | flops 1 | bytes 1 | tf_op jit(solution)/shard_map/partial_weights/pallas_call | solution.py:193
  43.9 0.9 collective-permute-done.9
  44.8 1.9 %add_convert_fusion.rest_0_.refs_1_ = bf16[1024,512]{1,0:T(8,128)(2,1)S(1)} fusion(f32[1024,512]{1,0:T(8,128)S(1)} %partial_weights.4, f32[1024,512]{1,0:T(8,128)} %collective-permute-done.9), kind=kLoop, calls=%fused_computation.2 | loop fusion | flops 1048576 | bytes 5242880 | tf_op jit(solution)/shard_map/convert_element_type | solution.py:402
  46.7 4.7 %partial_weights.7 = f32[1024,512]{1,0:T(8,128)} custom-call(s32[1]{0:T(128)} %bitcast.5.block_ref, bf16[4096,1024]{1,0:T(8,128)(2,1)} %bitcast.15, bf16[512,1024]{1,0:T(8,128)(2,1)S(1)} %join_queries.1.chosen_ref, bf16[1024,512]{1,0:T(8,128)(2,1)S(1)} %add_convert_fusion.rest_0_.refs_1_), custom_call_target="tpu_custom_call" | custom-call | flops 1 | bytes 1 | tf_op jit(solution)/shard_map/partial_weights/pallas_call | solution.py:193
  51.4 0.1 collective-permute-start.10
  51.6 0.8 collective-permute-start.3
  52.4 1.5 %collective-permute-start.11 = (bf16[1024,512]{1,0:T(8,128)(2,1)S(1)}, bf16[1024,512]{1,0:T(8,128)(2,1)}, u32[]{:S(2)}, u32[]{:S(2)}) collective-permute-start(bf16[1024,512]{1,0:T(8,128)(2,1)S(1)} %add_convert_fusion.rest_0_.refs_1_), channel_id=1, source_target_pairs={{0,2},{2,0},{1,3},{3,1},{4,6},{6,4},{5,7},{7,5},{8,10},{10,8},{9,1... | collective-permute-start | bytes 3145736 | tf_op jit(solution)/shard_map/ppermute | solution.py:19
  53.9 2.6 %collective-permute-start.12 = (bf16[256,1024]{1,0:T(8,128)(2,1)}, bf16[256,1024]{1,0:T(8,128)(2,1)}, u32[]{:S(2)}, u32[]{:S(2)}) collective-permute-start(bf16[256,1024]{1,0:T(8,128)(2,1)} %after.10), channel_id=1, source_target_pairs={{0,12},{4,0},{8,4},{12,8},{1,13},{5,1},{9,5},{13,9},{2,14},{6,2},{... | collective-permute-start | bytes 1572872 | tf_op jit(solution)/shard_map/ppermute | solution.py:19
  56.4 10.8 %collective-permute-done.3 = bf16[128,1024]{1,0:T(8,128)(2,1)S(1)} collective-permute-done((bf16[128,1024]{1,0:T(8,128)(2,1)S(1)}, bf16[128,1024]{1,0:T(8,128)(2,1)S(1)}, u32[]{:S(2)}, u32[]{:S(2)}) %collective-permute-start.3) | collective-permute-done | bytes 262176 | tf_op jit(solution)/shard_map/ppermute | solution.py:23
  67.3 0.7 copy-done.5
  68.0 9.6 %collective-permute-start.15 = (bf16[256,1024]{1,0:T(8,128)(2,1)S(1)}, bf16[256,1024]{1,0:T(8,128)(2,1)}, u32[]{:S(2)}, u32[]{:S(2)}) collective-permute-start(bf16[256,1024]{1,0:T(8,128)(2,1)S(1)} %after.12), channel_id=1, source_target_pairs={{0,4},{4,0},{8,12},{12,8},{1,5},{5,1},{9,13},{13,9},{2,6},{6,2},{1... | collective-permute-start | bytes 1572872 | tf_op jit(solution)/shard_map/ppermute | solution.py:23
  77.6 0.8 row_table.1
  78.4 1.6 %collective-permute-start.14 = (s32[8,128]{1,0:T(8,128)S(1)}, s32[8,128]{1,0:T(8,128)S(1)}, u32[]{:S(2)}, u32[]{:S(2)}) collective-permute-start(s32[8,128]{1,0:T(8,128)S(1)} %get-tuple-element.36), channel_id=1, source_target_pairs={{0,16},{16,0},{1,17},{17,1},{2,18},{18,2},{3,19},{19,3},{4,20},{20... | collective-permute-start | bytes 12296 | tf_op jit(solution)/shard_map/ppermute | solution.py:19
  80.0 2.1 %collective-permute-done.14 = s32[8,128]{1,0:T(8,128)S(1)} collective-permute-done((s32[8,128]{1,0:T(8,128)S(1)}, s32[8,128]{1,0:T(8,128)S(1)}, u32[]{:S(2)}, u32[]{:S(2)}) %collective-permute-start.14) | collective-permute-done | bytes 4128 | tf_op jit(solution)/shard_map/ppermute | solution.py:19
  82.1 0.6 slice.44
  83.4 3.4 %collective-permute-start.13 = (bf16[128,1024]{1,0:T(8,128)(2,1)}, bf16[128,1024]{1,0:T(8,128)(2,1)S(1)}, u32[]{:S(2)}, u32[]{:S(2)}) collective-permute-start(bf16[128,1024]{1,0:T(8,128)(2,1)} %after.11), channel_id=1, source_target_pairs={{0,8},{4,12},{8,0},{12,4},{1,9},{5,13},{9,1},{13,5},{2,10},{6,14},... | collective-permute-start | bytes 786440 | tf_op jit(solution)/shard_map/ppermute | solution.py:19
  86.8 1.1 conditional.1
  86.8 0.7 slice.27.clone
  87.6 0.1 broadcast.9
  88.0 0.1 collective-permute-start.4
  88.1 0.6 copy-done.12
  88.7 0.1 copy-done.16
  88.8 4.7 %partial_weights.6 = f32[1024,512]{1,0:T(8,128)} custom-call(s32[1]{0:T(128)} %bitcast.1.block_ref, bf16[4096,1024]{1,0:T(8,128)(2,1)} %bitcast.16, bf16[512,1024]{1,0:T(8,128)(2,1)S(1)} %join_queries.1.chosen_ref, bf16[1024,512]{1,0:T(8,128)(2,1)S(1)} %add_convert_fusion.rest_0_.refs_1_), custom_call_target="tpu_custom_call" | custom-call | flops 1 | bytes 1 | tf_op jit(solution)/shard_map/partial_weights/pallas_call | solution.py:193
  93.5 2.0 %collective-permute-done.15 = bf16[256,1024]{1,0:T(8,128)(2,1)} collective-permute-done((bf16[256,1024]{1,0:T(8,128)(2,1)S(1)}, bf16[256,1024]{1,0:T(8,128)(2,1)}, u32[]{:S(2)}, u32[]{:S(2)}) %collective-permute-start.15) | collective-permute-done | bytes 524320 | tf_op jit(solution)/shard_map/ppermute | solution.py:23
  95.5 1.1 fusion.1
  96.6 4.2 %add.56.refs_0_ = f32[1024,512]{1,0:T(8,128)} add(f32[1024,512]{1,0:T(8,128)} %partial_weights.6, f32[1024,512]{1,0:T(8,128)} %collective-permute-done.10) | non-fusion elementwise | flops 524288 | bytes 6291456 | tf_op jit(solution)/shard_map/add | solution.py:400
  100.8 4.7 %collective-permute-done.13.refs_5_ = bf16[128,1024]{1,0:T(8,128)(2,1)S(1)} collective-permute-done((bf16[128,1024]{1,0:T(8,128)(2,1)}, bf16[128,1024]{1,0:T(8,128)(2,1)S(1)}, u32[]{:S(2)}, u32[]{:S(2)}) %collective-permute-start.13) | collective-permute-done | bytes 262176 | tf_op jit(solution)/shard_map/ppermute | solution.py:19
  105.5 8.8 %early_scores.1 = (bf16[1024,512]{1,0:T(8,128)(2,1)S(1)}, bf16[1024,512]{1,0:T(8,128)(2,1)}, f32[256,8,512]{2,1,0:T(8,128)}) custom-call(f32[1024,512]{1,0:T(8,128)} %add.56.refs_0_, bf16[1024,512]{1,0:T(8,128)(2,1)} %collective-permute-done.11.refs_1_, bf16[256,1024]{1,0:T(8,128)(2,1)S(1)} %copy-done.2, ...), custom_call_target="tpu_custom_call" | custom-call | flops 1 | bytes 1 | tf_op jit(solution)/shard_map/early_scores/pallas_call | solution.py:273
  114.3 3.5 %row_scores.1 = (f32[1024,256]{1,0:T(8,128)S(1)}, f32[1024,256]{1,0:T(8,128)S(1)}) custom-call(s32[4,3]{1,0:T(4,128)S(1)} %get-tuple-element.29.table_ref, bf16[128,1024]{1,0:T(8,128)(2,1)S(1)} %collective-permute-done.4.last_ref, bf16[1024,512]{1,0:T(8,128)(2,1)S(1)} %get-tuple-element.42.high_ref, bf16[1024,512]{1,0:T(8,128)(2,1)} %get-tuple-element.43.low_ref, ...), custom_call_target="tpu_custom_call" | custom-call | flops 1 | bytes 1 | tf_op jit(solution)/shard_map/row_scores/pallas_call | solution.py:333
  117.8 0.1 collective-permute-start.16
  117.9 2.8 %collective-permute-done.16 = f32[1024,256]{1,0:T(8,128)} collective-permute-done((f32[1024,256]{1,0:T(8,128)S(1)}, f32[1024,256]{1,0:T(8,128)}, u32[]{:S(2)}, u32[]{:S(2)}) %collective-permute-start.16) | collective-permute-done | bytes 1048608 | tf_op jit(solution)/shard_map/ppermute | solution.py:19
  120.7 1.4 %add.57 = f32[1024,256]{1,0:T(8,128)S(1)} add(f32[1024,256]{1,0:T(8,128)S(1)} %get-tuple-element.45, f32[1024,256]{1,0:T(8,128)} %collective-permute-done.16) | non-fusion elementwise | flops 262144 | bytes 3145728 | tf_op jit(solution)/shard_map/add | solution.py:425
  122.1 1.6 %collective-permute-start.17 = (bf16[1024,128]{1,0:T(8,128)(2,1)S(1)}, bf16[1024,128]{1,0:T(8,128)(2,1)S(1)}, u32[]{:S(2)}, u32[]{:S(2)}) collective-permute-start(bf16[1024,128]{1,0:T(8,128)(2,1)S(1)} %dynamic-slice_convert_fusion), channel_id=1, source_target_pairs={{0,2},{2,0},{1,3},{3,1},{4,6},{6,4},{5,7},{7,5},{8,10},{10,8},{9,1... | collective-permute-start | bytes 786440 | tf_op jit(solution)/shard_map/ppermute | solution.py:19
  123.6 6.9 %collective-permute-done.17 = bf16[1024,128]{1,0:T(8,128)(2,1)S(1)} collective-permute-done((bf16[1024,128]{1,0:T(8,128)(2,1)S(1)}, bf16[1024,128]{1,0:T(8,128)(2,1)S(1)}, u32[]{:S(2)}, u32[]{:S(2)}) %collective-permute-start.17) | collective-permute-done | bytes 262176 | tf_op jit(solution)/shard_map/ppermute | solution.py:19
  130.6 1.0 copy.14
  (54 shorter events, 0.5 us)
Async XLA Ops:
  0.0 1.2 copy-start
  1.2 0.7 copy-start.7
  1.9 0.7 copy-start.9
  2.6 7.0 %copy-start.6 = (s32[4096]{0:T(1024)S(1)}, s32[4096]{0:T(1024)}, u32[]{:S(2)}) copy-start(s32[4096]{0:T(1024)} %param.9) | copy-start | bytes 49156
  3.4 11.8 %collective-permute-start.7 = (bf16[1,64,1024]{2,1,0:T(8,128)(2,1)S(1)}, bf16[1,64,1024]{2,1,0:T(8,128)(2,1)S(1)}, u32[]{:S(2)}, u32[]{:S(2)}) collective-permute-start(bf16[1,64,1024]{2,1,0:T(8,128)(2,1)S(1)} %get-tuple-element.54), channel_id=1, source_target_pairs={{0,12},{4,0},{8,4},{12,8},{1,13},{5,1},{9,5},{13,9},{2,14},{6,2},{... | collective-permute-start | bytes 393224 | tf_op jit(solution)/shard_map/ppermute | solution.py:19
  8.5 11.2 %collective-permute-start.6 = (bf16[1,64,1024]{2,1,0:T(8,128)(2,1)S(1)}, bf16[1,64,1024]{2,1,0:T(8,128)(2,1)S(1)}, u32[]{:S(2)}, u32[]{:S(2)}) collective-permute-start(bf16[1,64,1024]{2,1,0:T(8,128)(2,1)S(1)} %get-tuple-element.55), channel_id=1, source_target_pairs={{0,8},{4,12},{8,0},{12,4},{1,9},{5,13},{9,1},{13,5},{2,10},{6,14},... | collective-permute-start | bytes 393224 | tf_op jit(solution)/shard_map/ppermute | solution.py:19
  8.5 11.2 %collective-permute-start.5 = (bf16[1,64,1024]{2,1,0:T(8,128)(2,1)S(1)}, bf16[1,64,1024]{2,1,0:T(8,128)(2,1)S(1)}, u32[]{:S(2)}, u32[]{:S(2)}) collective-permute-start(bf16[1,64,1024]{2,1,0:T(8,128)(2,1)S(1)} %get-tuple-element.56), channel_id=1, source_target_pairs={{0,4},{4,8},{8,12},{12,0},{1,5},{5,9},{9,13},{13,1},{2,6},{6,10},{... | collective-permute-start | bytes 393224 | tf_op jit(solution)/shard_map/ppermute | solution.py:19
  15.2 4.6 %copy-start.1 = (bf16[256,1024]{1,0:T(8,128)(2,1)}, bf16[256,1024]{1,0:T(8,128)(2,1)S(1)}, u32[]{:S(2)}) copy-start(bf16[256,1024]{1,0:T(8,128)(2,1)S(1)} %get-tuple-element.33.refs_2_) | copy-start | bytes 1572868
  15.2 5.4 %copy-start.3 = (bf16[128,1024]{1,0:T(8,128)(2,1)}, bf16[128,1024]{1,0:T(8,128)(2,1)S(1)}, u32[]{:S(2)}) copy-start(bf16[128,1024]{1,0:T(8,128)(2,1)S(1)} %get-tuple-element.30.refs_0_) | copy-start | bytes 786436
  15.2 19.6 %copy-start.8 = (s32[4,4]{1,0:T(4,128)S(1)}, s32[4,4]{1,0:T(4,128)}, u32[]{:S(2)}) copy-start(s32[4,4]{1,0:T(4,128)} %pattern_ref.3) | copy-start | bytes 196
  15.2 19.6 %copy-start.10 = (s32[16]{0:T(128)S(1)}, s32[16]{0:T(128)}, u32[]{:S(2)}) copy-start(s32[16]{0:T(128)} %slot_ref.3) | copy-start | bytes 196
  19.8 15.0 %collective-permute-start.2 = (bf16[256,1024]{1,0:T(8,128)(2,1)S(1)}, bf16[256,1024]{1,0:T(8,128)(2,1)S(1)}, u32[]{:S(2)}, u32[]{:S(2)}) collective-permute-start(bf16[256,1024]{1,0:T(8,128)(2,1)S(1)} %get-tuple-element.32.refs_1_), channel_id=1, source_target_pairs={{0,4},{4,8},{8,12},{12,0},{1,5},{5,9},{9,13},{13,1},{2,6},{6,10},{... | collective-permute-start | bytes 1572872 | tf_op jit(solution)/shard_map/ppermute | solution.py:19
  20.6 14.3 %collective-permute-start.8 = (bf16[4,64,1024]{2,1,0:T(8,128)(2,1)S(1)}, bf16[4,64,1024]{2,1,0:T(8,128)(2,1)S(1)}, u32[]{:S(2)}, u32[]{:S(2)}) collective-permute-start(bf16[4,64,1024]{2,1,0:T(8,128)(2,1)S(1)} %after.9.refs_0_.refs_1_), channel_id=1, source_target_pairs={{0,16},{16,0},{1,17},{17,1},{2,18},{18,2},{3,19},{19,3},{4,20},{20... | collective-permute-start | bytes 1572872 | tf_op jit(solution)/shard_map/ppermute | solution.py:19
  40.3 4.5 %collective-permute-start.9 = (f32[1024,512]{1,0:T(8,128)}, f32[1024,512]{1,0:T(8,128)}, u32[]{:S(2)}, u32[]{:S(2)}) collective-permute-start(f32[1024,512]{1,0:T(8,128)} %partial_weights.5), channel_id=1, source_target_pairs={{0,1},{1,0},{2,3},{3,2},{4,5},{5,4},{6,7},{7,6},{8,9},{9,8},{10,11... | collective-permute-start | bytes 6291464 | tf_op jit(solution)/shard_map/ppermute | solution.py:19
  51.4 15.8 %copy-start.4 = (bf16[128,1024]{1,0:T(8,128)(2,1)S(1)}, bf16[128,1024]{1,0:T(8,128)(2,1)}, u32[]{:S(2)}) copy-start(bf16[128,1024]{1,0:T(8,128)(2,1)} %copy-done.3) | copy-start | bytes 786436
  51.4 45.2 %collective-permute-start.10 = (f32[1024,512]{1,0:T(8,128)}, f32[1024,512]{1,0:T(8,128)}, u32[]{:S(2)}, u32[]{:S(2)}) collective-permute-start(f32[1024,512]{1,0:T(8,128)} %partial_weights.7), channel_id=1, source_target_pairs={{0,1},{1,0},{2,3},{3,2},{4,5},{5,4},{6,7},{7,6},{8,9},{9,8},{10,11... | collective-permute-start | bytes 6291464 | tf_op jit(solution)/shard_map/ppermute | solution.py:19
  51.6 15.6 %collective-permute-start.3 = (bf16[128,1024]{1,0:T(8,128)(2,1)S(1)}, bf16[128,1024]{1,0:T(8,128)(2,1)S(1)}, u32[]{:S(2)}, u32[]{:S(2)}) collective-permute-start(bf16[128,1024]{1,0:T(8,128)(2,1)S(1)} %after.7), channel_id=1, source_target_pairs={{0,8},{4,12},{8,0},{12,4},{1,9},{5,13},{9,1},{13,5},{2,10},{6,14},... | collective-permute-start | bytes 786440 | tf_op jit(solution)/shard_map/ppermute | solution.py:23
  52.4 53.1 %collective-permute-start.11 = (bf16[1024,512]{1,0:T(8,128)(2,1)S(1)}, bf16[1024,512]{1,0:T(8,128)(2,1)}, u32[]{:S(2)}, u32[]{:S(2)}) collective-permute-start(bf16[1024,512]{1,0:T(8,128)(2,1)S(1)} %add_convert_fusion.rest_0_.refs_1_), channel_id=1, source_target_pairs={{0,2},{2,0},{1,3},{3,1},{4,6},{6,4},{5,7},{7,5},{8,10},{10,8},{9,1... | collective-permute-start | bytes 3145736 | tf_op jit(solution)/shard_map/ppermute | solution.py:19
  53.9 29.5 %collective-permute-start.12 = (bf16[256,1024]{1,0:T(8,128)(2,1)}, bf16[256,1024]{1,0:T(8,128)(2,1)}, u32[]{:S(2)}, u32[]{:S(2)}) collective-permute-start(bf16[256,1024]{1,0:T(8,128)(2,1)} %after.10), channel_id=1, source_target_pairs={{0,12},{4,0},{8,4},{12,8},{1,13},{5,1},{9,5},{13,9},{2,14},{6,2},{... | collective-permute-start | bytes 1572872 | tf_op jit(solution)/shard_map/ppermute | solution.py:19
  67.2 0.7 copy-start.5
  68.0 27.5 %collective-permute-start.15 = (bf16[256,1024]{1,0:T(8,128)(2,1)S(1)}, bf16[256,1024]{1,0:T(8,128)(2,1)}, u32[]{:S(2)}, u32[]{:S(2)}) collective-permute-start(bf16[256,1024]{1,0:T(8,128)(2,1)S(1)} %after.12), channel_id=1, source_target_pairs={{0,4},{4,0},{8,12},{12,8},{1,5},{5,1},{9,13},{13,9},{2,6},{6,2},{1... | collective-permute-start | bytes 1572872 | tf_op jit(solution)/shard_map/ppermute | solution.py:23
  78.4 3.7 %collective-permute-start.14 = (s32[8,128]{1,0:T(8,128)S(1)}, s32[8,128]{1,0:T(8,128)S(1)}, u32[]{:S(2)}, u32[]{:S(2)}) collective-permute-start(s32[8,128]{1,0:T(8,128)S(1)} %get-tuple-element.36), channel_id=1, source_target_pairs={{0,16},{16,0},{1,17},{17,1},{2,18},{18,2},{3,19},{19,3},{4,20},{20... | collective-permute-start | bytes 12296 | tf_op jit(solution)/shard_map/ppermute | solution.py:19
  83.4 22.1 %collective-permute-start.13 = (bf16[128,1024]{1,0:T(8,128)(2,1)}, bf16[128,1024]{1,0:T(8,128)(2,1)S(1)}, u32[]{:S(2)}, u32[]{:S(2)}) collective-permute-start(bf16[128,1024]{1,0:T(8,128)(2,1)} %after.11), channel_id=1, source_target_pairs={{0,8},{4,12},{8,0},{12,4},{1,9},{5,13},{9,1},{13,5},{2,10},{6,14},... | collective-permute-start | bytes 786440 | tf_op jit(solution)/shard_map/ppermute | solution.py:19
  87.9 0.7 copy-start.12
  87.9 0.8 copy-start.14
  88.0 0.9 copy-start.16
  88.0 26.3 %collective-permute-start.4 = (bf16[128,1024]{1,0:T(8,128)(2,1)}, bf16[128,1024]{1,0:T(8,128)(2,1)S(1)}, u32[]{:S(2)}, u32[]{:S(2)}) collective-permute-start(bf16[128,1024]{1,0:T(8,128)(2,1)} %copy-done.5), channel_id=1, source_target_pairs={{0,8},{4,12},{8,0},{12,4},{1,9},{5,13},{9,1},{13,5},{2,10},{6,14},... | collective-permute-start | bytes 786440 | tf_op jit(solution)/shard_map/ppermute | solution.py:19
  96.6 8.9 %copy-start.2 = (bf16[256,1024]{1,0:T(8,128)(2,1)S(1)}, bf16[256,1024]{1,0:T(8,128)(2,1)}, u32[]{:S(2)}) copy-start(bf16[256,1024]{1,0:T(8,128)(2,1)} %copy-done.1) | copy-start | bytes 1572868
  96.6 8.9 %copy-start.13 = (bf16[128,1024]{1,0:T(8,128)(2,1)S(1)}, bf16[128,1024]{1,0:T(8,128)(2,1)}, u32[]{:S(2)}) copy-start(bf16[128,1024]{1,0:T(8,128)(2,1)} %copy-done.12) | copy-start | bytes 786436
  96.6 8.9 %copy-start.15 = (bf16[128,1024]{1,0:T(8,128)(2,1)S(1)}, bf16[128,1024]{1,0:T(8,128)(2,1)}, u32[]{:S(2)}) copy-start(bf16[128,1024]{1,0:T(8,128)(2,1)} %copy-done.14) | copy-start | bytes 786436
  96.6 8.9 %copy-start.17 = (bf16[128,1024]{1,0:T(8,128)(2,1)S(1)}, bf16[128,1024]{1,0:T(8,128)(2,1)}, u32[]{:S(2)}) copy-start(bf16[128,1024]{1,0:T(8,128)(2,1)} %copy-done.16) | copy-start | bytes 786436
  117.8 2.9 %collective-permute-start.16 = (f32[1024,256]{1,0:T(8,128)S(1)}, f32[1024,256]{1,0:T(8,128)}, u32[]{:S(2)}, u32[]{:S(2)}) collective-permute-start(f32[1024,256]{1,0:T(8,128)S(1)} %get-tuple-element.46), channel_id=1, source_target_pairs={{0,1},{1,0},{2,3},{3,2},{4,5},{5,4},{6,7},{7,6},{8,9},{9,8},{10,11... | collective-permute-start | bytes 3145736 | tf_op jit(solution)/shard_map/ppermute | solution.py:19
  122.1 8.4 %collective-permute-start.17 = (bf16[1024,128]{1,0:T(8,128)(2,1)S(1)}, bf16[1024,128]{1,0:T(8,128)(2,1)S(1)}, u32[]{:S(2)}, u32[]{:S(2)}) collective-permute-start(bf16[1024,128]{1,0:T(8,128)(2,1)S(1)} %dynamic-slice_convert_fusion), channel_id=1, source_target_pairs={{0,2},{2,0},{1,3},{3,1},{4,6},{6,4},{5,7},{7,5},{8,10},{10,8},{9,1... | collective-permute-start | bytes 786440 | tf_op jit(solution)/shard_map/ppermute | solution.py:19

commit v4 on v3

--- a/solution.py
+++ b/solution.py
@@ -88,7 +88,7 @@
     unit = min(share, part)
 
     def kernel(pattern_ref, slot_ref, *refs):
-        out_ref = refs[-1]
+        out_ref, rows_ref = refs[-2:]
         me, group = lax.axis_index("shard"), lax.axis_index("groups")
         for k in range(n_list):
             owner = lax.div(slot_ref[pattern_ref[me, k]], jnp.int32(local_blocks))
@@ -100,13 +100,15 @@
                     chunk = lax.div(first, jnp.int32(share))
                     goal = lax.rem(chunk, jnp.int32(n_rep)) * n_feat + lax.div(chunk, jnp.int32(n_rep))
                     goal = goal * share + lax.rem(first, jnp.int32(share))
-                    out_ref[pl.ds(pl.multiple_of(goal, unit), unit), :] = refs[d][hops, u * unit:(u + 1) * unit, :]
+                    rows_ref[pl.ds(pl.multiple_of(goal, unit), unit), :] = refs[d][hops, u * unit:(u + 1) * unit, :]
+        out_ref[...] = rows_ref[...].T
 
     return pl.pallas_call(
         kernel,
         in_specs=[SMEM, SMEM] + [VMEM] * n_group + [ANY] * len(others),
         out_specs=VMEM,
-        out_shape=jax.ShapeDtypeStruct((total, width), BF16),
+        out_shape=jax.ShapeDtypeStruct((width, total), BF16),
+        scratch_shapes=[pltpu.VMEM((total, width), BF16)],
         cost_estimate=cost(0, 4 * total * width),
         compiler_params=PARAMS,
         name="join_queries",
@@ -179,17 +181,14 @@
     )(ids, train)
 
 
-def partial_weights(matrix, chosen, block, depth, *others):
-    width = matrix.shape[1]
-    tile = 256 if depth % 256 == 0 else depth
+def partial_weights(matrix, chosen, block, depth):
+    width, total = chosen.shape
+    tile = 512 if depth % 512 == 0 else depth
     steps = depth // tile
 
-    def kernel(block_ref, matrix_ref, chosen_ref, *rest):
-        rest[-1][...] = lax.dot_general(
-            matrix_ref[...], chosen_ref[...], (((1,), (1,)), ((), ())), preferred_element_type=F32
-        )
-
-    total = chosen.shape[0]
+    def kernel(block_ref, matrix_ref, chosen_ref, out_ref):
+        out_ref[...] = dot(matrix_ref[...], chosen_ref[...])
+
     return pl.pallas_call(
         kernel,
         grid_spec=pltpu.PrefetchScalarGridSpec(
@@ -197,16 +196,15 @@
             grid=(steps,),
             in_specs=[
                 pl.BlockSpec((tile, width), lambda i, b: (b[0] * steps + i, 0)),
-                pl.BlockSpec((total, width), lambda i, b: (0, 0)),
-            ]
-            + [ANY] * len(others),
+                pl.BlockSpec((width, total), lambda i, b: (0, 0)),
+            ],
             out_specs=pl.BlockSpec((tile, total), lambda i, b: (i, 0)),
         ),
         out_shape=jax.ShapeDtypeStruct((depth, total), F32),
         cost_estimate=cost(2 * depth * width * total, 2 * depth * width + 4 * depth * total),
         compiler_params=PARAMS,
         name="partial_weights",
-    )(jnp.reshape(block, (1,)).astype(I32), matrix, chosen, *others)
+    )(jnp.reshape(block, (1,)).astype(I32), matrix, chosen)
 
 
 def row_table(ids, lines, bulk, extra):
@@ -248,13 +246,15 @@
     )(ids)
 
 
-def early_scores(own, others, pieces):
+def early_scores(own, others, pieces, flag, sure):
     depth, width = own.shape
     count = sum(p.shape[0] for p in pieces)
     n_other = len(others)
 
     def kernel(*refs):
+        flag_ref, refs = refs[0], refs[1:]
         own_ref, other_refs, piece_refs = refs[0], refs[1:1 + n_other], refs[1 + n_other:-3]
+        flagged = jnp.max(flag_ref[...]) > 0
         high_ref, low_ref, out_ref = refs[-3:]
         weight = own_ref[...]
         for ref in other_refs:
@@ -263,23 +263,29 @@
         high_ref[...] = high
         low_ref[...] = (weight - high.astype(F32)).astype(BF16)
         base = 0
-        for ref in piece_refs:
+
+        def score(ref, at):
             x = ref[...]
             y = dot(x, high_ref[...]) + dot(x, low_ref[...])
-            out_ref[base // 8:(base + x.shape[0]) // 8] = y.reshape(x.shape[0] // 8, 8, width)
-            base += x.shape[0]
-        out_ref[base // 8:] = jnp.zeros((LANES // 8, 8, width), F32)
-
-    return pl.pallas_call(
-        kernel,
-        in_specs=[VMEM] * (1 + n_other + len(pieces)),
+            out_ref[at // 8:(at + x.shape[0]) // 8] = y.reshape(x.shape[0] // 8, 8, width)
+
+        for ref, always in zip(piece_refs, sure):
+            if always:
+                score(ref, base)
+            else:
+                pl.when(flagged)(functools.partial(score, ref, base))
+            base += ref.shape[0]
+
+    return pl.pallas_call(
+        kernel,
+        in_specs=[VMEM] * (2 + n_other + len(pieces)),
         out_specs=[VMEM] * 3,
         out_shape=[jax.ShapeDtypeStruct((depth, width), BF16)] * 2
         + [jax.ShapeDtypeStruct(((count + LANES) // 8, 8, width), F32)],
         cost_estimate=cost(4 * count * depth * width, 10 * depth * width + count * (2 * depth + 4 * width)),
         compiler_params=PARAMS,
         name="early_scores",
-    )(own, *others, *pieces)
+    )(flag, own, *others, *pieces)
 
 
 def row_scores(table, last, high, low, early, rows, n_rep, bulk, extra, cuts):
@@ -363,10 +369,9 @@
     for d in range(1, n_shard):
         pieces.append(shift(picked[d:d + 1], "shard", n_shard, d))
 
-    order = [0] + sorted(range(1, n_shard), key=lambda d: (min(d, n_shard - d), d))
-    cuts = [(d, 0, bulk) for d in order[:-1]]
-    cuts += [(order[-1], 0, bulk // 2), (order[-1], bulk // 2, bulk // 2)]
+    cuts = [(d, 0, bulk) for d in range(n_shard)]
     packed = pack_rows(train, ids, columns, bulk, extra, cuts)
+    here = [packed[0], shift(packed[1], "shard", n_shard, 1)]
     table, flag = row_table(ids, lines, bulk, extra)
 
     def swap_far(x):
@@ -375,50 +380,48 @@
     def swap_near(x):
         return jnp.concatenate([x, swap(x, "shard", n_shard, 1)])
 
-    arrived = after(jnp.concatenate(pieces), packed[1])
-    here = [packed[0]]
-    marks = [arrived, arrived]
-    for j, (hops, _, _) in enumerate(cuts[1:-1]):
-        sent = packed[j + 1] if j == 0 else after(packed[j + 1], marks[-2])
-        here.append(shift(sent, "shard", n_shard, hops))
-        marks.append(here[-1])
-        if extra and j == len(cuts) - 4:
-            far = swap_far(after(packed[-2], marks[-2]))
-            marks.append(far)
-    last = shift(after(packed[len(cuts) - 1], marks[-2]), "shard", n_shard, cuts[-1][0])
-
-    parts = [arrived] + [shift(arrived, "groups", n_group, d) for d in range(1, n_group)]
-    chosen = join_queries(parts, block_slot, pattern, query_store.shape[0], n_feat, n_rep, here[1])
-
-    matrix = precond[0]
-
-    def weights(f, r, *others):
-        return partial_weights(matrix, chosen, f * n_rep + r, columns, *others)
-
-    def summed_over_rep(f, *others):
-        away = [shift(weights(f, (rep + d) % n_rep, *others), "rep", n_rep, d) for d in range(1, n_rep)]
-        return sum(away, weights(f, rep, *others))
-
-    sends = [summed_over_rep((feat + d) % n_feat).astype(BF16) for d in range(1, n_feat)]
-    others = [shift(x, "feat", n_feat, d + 1) for d, x in enumerate(sends)]
-    own = summed_over_rep(feat, *sends)
-
-    extras = []
+    before_join, before_feat = [here[1]], []
     if extra:
         for d in range(1, n_group):
             flag = jnp.maximum(flag, shift(flag, "groups", n_group, d))
-        first = swap_near(after(far, *sends))
         second = lax.cond(
             flag[0, 0] > 0,
             lambda x: swap_near(swap_far(x)),
             lambda x: jnp.zeros((n_shard * extra, columns), BF16),
-            after(packed[-1], *sends),
+            packed[-1],
         )
+        far = swap(after(packed[-2], here[1]), "shard", n_shard, 2)
+        before_join.append(second)
+        before_feat.append(far)
+
+    arrived = after(jnp.concatenate(pieces), packed[1])
+    parts = [arrived] + [shift(arrived, "groups", n_group, d) for d in range(1, n_group)]
+    chosen = join_queries(parts, block_slot, pattern, query_store.shape[0], n_feat, n_rep, *before_join)
+
+    matrix = precond[0]
+
+    def weights(f, r):
+        return partial_weights(matrix, chosen, f * n_rep + r, columns)
+
+    targets = [(feat + d) % n_feat for d in range(1, n_feat)] + [feat]
+    away = [[shift(weights(f, (rep + d) % n_rep), "rep", n_rep, d) for d in range(1, n_rep)] for f in targets]
+    sums = [sum(x, weights(f, rep)) for f, x in zip(targets, away)]
+    own = sums[-1]
+    sends = [after(x.astype(BF16), own, *before_feat) for x in sums[:-1]]
+    others = [shift(x, "feat", n_feat, d + 1) for d, x in enumerate(sends)]
+
+    extras = []
+    if extra:
+        first = swap_near(jnp.concatenate([packed[-2], far]))
         for j in range(n_shard):
             at = slice(j * extra, (j + 1) * extra)
             extras += [first[at], second[at]]
-
-    high, low, early = early_scores(own, others, here + extras)
+    for d in range(2, n_shard - 1):
+        here.append(shift(after(packed[d], *sends), "shard", n_shard, d))
+    last = shift(after(packed[n_shard - 1], here[-1]), "shard", n_shard, n_shard - 1)
+
+    sure = [True] * len(here) + [True, False] * (len(extras) // 2)
+    high, low, early = early_scores(own, others, here + extras, flag, sure)
     shares = row_scores(table, last, high, low, early, rows, n_rep, bulk, extra, cuts)
     total = shares[0]
     for d in range(1, n_rep):

time: 132 us -> 118 us (0.89)
  starting transfers between devices: 29.8 us -> 19 us
  Pallas kernels: 38 us -> 32.5 us
  waiting for transfers between devices: 47.3 us -> 50.5 us
  other arithmetic: 7.63 us -> 5.09 us
  local copies, waits for them, and re-layouts: 7.68 us -> 9.56 us
    ppermute x14 -> x13, waiting for transfers between devices: 34.6 us -> 48.2 us  [shift(): return lax.ppermute(x, axis, [(i, (i + by) % size) for i in range(size)])]
    ppermute x2, waiting for transfers between devices: 12.8 us -> 2.24 us  [swap(): return lax.ppermute(x, axis, [(i, i ^ bit) for i in range(size)])]
    ppermute x14 -> x13, starting transfers between devices: 19.3 us -> 12.8 us  [shift(): return lax.ppermute(x, axis, [(i, (i + by) % size) for i in range(size)])]
    pallas_call x4, Pallas kernels: 17.6 us -> 12.6 us  [partial_weights(): pl.pallas_call(kernel, grid_spec=pltpu.PrefetchScalarGridSpec(num_scalar_...]
    ppermute x2, starting transfers between devices: 10.4 us -> 6.16 us  [swap(): return lax.ppermute(x, axis, [(i, i ^ bit) for i in range(size)])]
    unnamed x34 -> x29, local copies, waits for them, and re-layouts: 4 us -> 6.65 us
    add x1, other arithmetic: 4.18 us -> 2.07 us  [body(): sums = [sum(x, weights(f, rep)) for f, x in zip(targets, away)]]
    slice x6 -> x2, local copies, waits for them, and re-layouts: 1.91 us -> 0.11 us  [body(): extras += [first[at], second[at]]]
  transfers between devices with their start and end apart: 16 -> 15, of which waited for: 9 -> 7; matrix products, arithmetic and copies ran while one was open for 5% -> 6% of each run, Pallas kernels for 18% -> 20%
where the time goes in v4:
time: 118 us
  waiting for transfers between devices  50.5 us (43%)
  Pallas kernels  32.5 us (28%)
  starting transfers between devices  19 us (16%)
  local copies, waits for them, and re-layouts  9.56 us (8%)
  other arithmetic  5.09 us (4%)
    ppermute x13, waiting for transfers between devices, shift(): return lax.ppermute(x, axis, [(i, (i + by) % size) for i in range(size)])  48.2 us
    ppermute x13, starting transfers between devices, shift(): return lax.ppermute(x, axis, [(i, (i + by) % size) for i in range(size)])  12.8 us
    pallas_call x4, Pallas kernels, partial_weights(): pl.pallas_call(kernel, grid_spec=pltpu.PrefetchScalarGridSpec(num_scalar_...  12.6 us
    pallas_call x1, Pallas kernels, early_scores(): pl.pallas_call(kernel, in_specs=[VMEM] * (2 + n_other + len(pieces)), out...  7.99 us
    unnamed x29, local copies, waits for them, and re-layouts  6.65 us
    ppermute x2, starting transfers between devices, swap(): return lax.ppermute(x, axis, [(i, i ^ bit) for i in range(size)])  6.16 us
    pallas_call x1, Pallas kernels, pack_rows(): pl.pallas_call(kernel, grid=(1,), in_specs=[pl.BlockSpec((lines, LANES),...  5.61 us
    pallas_call x1, Pallas kernels, row_scores(): pl.pallas_call(kernel, in_specs=[SMEM] + [VMEM] * 4, out_specs=[VMEM] * n...  3.68 us
  transfers between devices with their start and end apart: 15, of which 7 were waited for; matrix products, arithmetic and copies ran while one was open for 6% of the time, Pallas kernels for 20%

profile of v4, /device:TPU:0, one launch (start us, length us, event | category | flops | bytes accessed | tf_op | source)
XLA Modules:
  0.0 117.6 jit_solution(17587434554687686697)
XLA Ops:
  0.0 1.2 %copy-done.1 = bf16[4,128,1024]{2,1,0:T(8,128)(2,1)S(1)} copy-done((bf16[4,128,1024]{2,1,0:T(8,128)(2,1)S(1)}, bf16[4,128,1024]{2,1,0:T(8,128)(2,1)}, u32[]{:S(2)}) %copy-start.1) | copy-done | bytes 1048600
  1.2 0.7 copy-done.8
  1.9 0.7 copy-done.10
  2.6 0.8 pick_queries.1
  3.4 5.1 %collective-permute-start.4 = (bf16[1,64,1024]{2,1,0:T(8,128)(2,1)S(1)}, bf16[1,64,1024]{2,1,0:T(8,128)(2,1)S(1)}, u32[]{:S(2)}, u32[]{:S(2)}) collective-permute-start(bf16[1,64,1024]{2,1,0:T(8,128)(2,1)S(1)} %get-tuple-element.42), channel_id=1, source_target_pairs={{0,12},{4,0},{8,4},{12,8},{1,13},{5,1},{9,5},{13,9},{2,14},{6,2},{... | collective-permute-start | bytes 393224 | tf_op jit(solution)/shard_map/ppermute | solution.py:19
  8.5 1.0 collective-permute-start.2
  9.5 5.6 %pack_rows.1 = (bf16[256,1024]{1,0:T(8,128)(2,1)S(1)}, bf16[256,1024]{1,0:T(8,128)(2,1)S(1)}, bf16[256,1024]{1,0:T(8,128)(2,1)S(1)}, bf16[256,1024]{1,0:T(8,128)...) custom-call(s32[32,128]{1,0:T(8,128)S(1)} %bitcast.11, bf16[1024,2048]{1,0:T(8,128)(2,1)} %train_ref.1), custom_call_target="tpu_custom_call" | custom-call | flops 1 | bytes 1 | tf_op jit(solution)/shard_map/pack_rows/pallas_call | solution.py:168
  15.2 4.6 %collective-permute-done.3 = bf16[1,64,1024]{2,1,0:T(8,128)(2,1)S(1)} collective-permute-done((bf16[1,64,1024]{2,1,0:T(8,128)(2,1)S(1)}, bf16[1,64,1024]{2,1,0:T(8,128)(2,1)S(1)}, u32[]{:S(2)}, u32[]{:S(2)}) %collective-permute-start.3) | collective-permute-done | bytes 131104 | tf_op jit(solution)/shard_map/ppermute | solution.py:19
  19.7 0.1 pad_maximum_fusion.2.refs_0_
  19.8 0.8 collective-permute-start.6
  20.6 1.5 %collective-permute-start.5 = (bf16[4,64,1024]{2,1,0:T(8,128)(2,1)S(1)}, bf16[4,64,1024]{2,1,0:T(8,128)(2,1)S(1)}, u32[]{:S(2)}, u32[]{:S(2)}) collective-permute-start(bf16[4,64,1024]{2,1,0:T(8,128)(2,1)S(1)} %after.5.refs_0_), channel_id=1, source_target_pairs={{0,16},{16,0},{1,17},{17,1},{2,18},{18,2},{3,19},{19,3},{4,20},{20... | collective-permute-start | bytes 1572872 | tf_op jit(solution)/shard_map/ppermute | solution.py:19
  22.1 0.8 row_table.1
  22.9 0.6 collective-permute-start.7
  23.5 9.9 %collective-permute-done.7 = s32[8,128]{1,0:T(8,128)S(1)} collective-permute-done((s32[8,128]{1,0:T(8,128)S(1)}, s32[8,128]{1,0:T(8,128)S(1)}, u32[]{:S(2)}, u32[]{:S(2)}) %collective-permute-start.7) | collective-permute-done | bytes 4128 | tf_op jit(solution)/shard_map/ppermute | solution.py:19
  33.5 0.6 slice.37
  34.7 0.0 copy-start.9
  34.7 0.0 copy-start.11
  34.7 1.1 conditional.1
  34.8 1.1 broadcast.4
  35.9 0.8 copy-done.3
  36.7 1.0 copy-done.4
  37.7 1.0 join_queries.1.chosen_ref
  38.7 3.7 %partial_weights.7 = f32[1024,512]{1,0:T(8,128)} custom-call(s32[1]{0:T(128)} %bitcast.6.block_ref, bf16[4096,1024]{1,0:T(8,128)(2,1)} %bitcast.13, bf16[1024,512]{1,0:T(8,128)(2,1)S(1)} %join_queries.1.chosen_ref), custom_call_target="tpu_custom_call" | custom-call | flops 1 | bytes 1 | tf_op jit(solution)/shard_map/partial_weights/pallas_call | solution.py:192
  42.4 3.6 %partial_weights.5 = f32[1024,512]{1,0:T(8,128)} custom-call(s32[1]{0:T(128)} %bitcast.4.block_ref, bf16[4096,1024]{1,0:T(8,128)(2,1)} %bitcast.14, bf16[1024,512]{1,0:T(8,128)(2,1)S(1)} %join_queries.1.chosen_ref), custom_call_target="tpu_custom_call" | custom-call | flops 1 | bytes 1 | tf_op jit(solution)/shard_map/partial_weights/pallas_call | solution.py:192
  46.0 0.5 collective-permute-start.8
  46.6 2.4 %collective-permute-start.10 = (bf16[128,1024]{1,0:T(8,128)(2,1)S(1)}, bf16[128,1024]{1,0:T(8,128)(2,1)S(1)}, u32[]{:S(2)}, u32[]{:S(2)}) collective-permute-start(bf16[128,1024]{1,0:T(8,128)(2,1)S(1)} %after.6), channel_id=1, source_target_pairs={{0,8},{4,12},{8,0},{12,4},{1,9},{5,13},{9,1},{13,5},{2,10},{6,14},... | collective-permute-start | bytes 786440 | tf_op jit(solution)/shard_map/ppermute | solution.py:23
  48.9 2.7 %partial_weights.4 = f32[1024,512]{1,0:T(8,128)S(1)} custom-call(s32[1]{0:T(128)} %bitcast.1.block_ref, bf16[4096,1024]{1,0:T(8,128)(2,1)} %bitcast.15, bf16[1024,512]{1,0:T(8,128)(2,1)S(1)} %join_queries.1.chosen_ref), custom_call_target="tpu_custom_call" | custom-call | flops 1 | bytes 1 | tf_op jit(solution)/shard_map/partial_weights/pallas_call | solution.py:192
  51.6 2.7 %partial_weights.6 = f32[1024,512]{1,0:T(8,128)S(1)} custom-call(s32[1]{0:T(128)} %bitcast.5.block_ref, bf16[4096,1024]{1,0:T(8,128)(2,1)} %bitcast.16, bf16[1024,512]{1,0:T(8,128)(2,1)S(1)} %join_queries.1.chosen_ref), custom_call_target="tpu_custom_call" | custom-call | flops 1 | bytes 1 | tf_op jit(solution)/shard_map/partial_weights/pallas_call | solution.py:192
  54.3 2.1 %add.56.refs_1_ = f32[1024,512]{1,0:T(8,128)S(1)} add(f32[1024,512]{1,0:T(8,128)S(1)} %partial_weights.6, f32[1024,512]{1,0:T(8,128)} %collective-permute-done.9) | non-fusion elementwise | flops 524288 | bytes 6291456 | tf_op jit(solution)/shard_map/add | solution.py:408
  56.4 2.7 %add_convert_fusion.refs_0_ = bf16[1024,512]{1,0:T(8,128)(2,1)S(1)} fusion(f32[1024,512]{1,0:T(8,128)S(1)} %partial_weights.4, f32[1024,512]{1,0:T(8,128)} %collective-permute-done.8), kind=kLoop, calls=%fused_computation.2 | loop fusion | flops 1048576 | bytes 5242880 | tf_op jit(solution)/shard_map/convert_element_type | solution.py:410
  59.1 0.0 copy-start.6
  59.1 2.2 %collective-permute-done.10.refs_2_.refs_8_ = bf16[128,1024]{1,0:T(8,128)(2,1)S(1)} collective-permute-done((bf16[128,1024]{1,0:T(8,128)(2,1)S(1)}, bf16[128,1024]{1,0:T(8,128)(2,1)S(1)}, u32[]{:S(2)}, u32[]{:S(2)}) %collective-permute-start.10) | collective-permute-done | bytes 262176 | tf_op jit(solution)/shard_map/ppermute | solution.py:23
  61.4 1.5 %collective-permute-start.13 = (bf16[1024,512]{1,0:T(8,128)(2,1)S(1)}, bf16[1024,512]{1,0:T(8,128)(2,1)S(1)}, u32[]{:S(2)}, u32[]{:S(2)}) collective-permute-start(bf16[1024,512]{1,0:T(8,128)(2,1)S(1)} %after.7.refs_1_), channel_id=1, source_target_pairs={{0,2},{2,0},{1,3},{3,1},{4,6},{6,4},{5,7},{7,5},{8,10},{10,8},{9,1... | collective-permute-start | bytes 3145736 | tf_op jit(solution)/shard_map/ppermute | solution.py:19
  62.9 3.8 %collective-permute-start.14 = (bf16[256,1024]{1,0:T(8,128)(2,1)S(1)}, bf16[256,1024]{1,0:T(8,128)(2,1)S(1)}, u32[]{:S(2)}, u32[]{:S(2)}) collective-permute-start(bf16[256,1024]{1,0:T(8,128)(2,1)S(1)} %pad_maximum_fusion.3), channel_id=1, source_target_pairs={{0,4},{4,0},{8,12},{12,8},{1,5},{5,1},{9,13},{13,9},{2,6},{6,2},{1... | collective-permute-start | bytes 1572872 | tf_op jit(solution)/shard_map/ppermute | solution.py:23
  66.7 21.1 %collective-permute-done.11.refs_1_.refs_5_ = bf16[256,1024]{1,0:T(8,128)(2,1)S(1)} collective-permute-done((bf16[256,1024]{1,0:T(8,128)(2,1)S(1)}, bf16[256,1024]{1,0:T(8,128)(2,1)S(1)}, u32[]{:S(2)}, u32[]{:S(2)}) %collective-permute-start.11) | collective-permute-done | bytes 524320 | tf_op jit(solution)/shard_map/ppermute | solution.py:19
  87.8 1.2 %collective-permute-start.12 = (bf16[256,1024]{1,0:T(8,128)(2,1)S(1)}, bf16[256,1024]{1,0:T(8,128)(2,1)S(1)}, u32[]{:S(2)}, u32[]{:S(2)}) collective-permute-start(bf16[256,1024]{1,0:T(8,128)(2,1)S(1)} %after.9), channel_id=1, source_target_pairs={{0,12},{4,0},{8,4},{12,8},{1,13},{5,1},{9,5},{13,9},{2,14},{6,2},{... | collective-permute-start | bytes 1572872 | tf_op jit(solution)/shard_map/ppermute | solution.py:19
  89.0 0.1 fusion
  89.2 1.0 copy-done.13
  90.1 8.0 %early_scores.1 = (bf16[1024,512]{1,0:T(8,128)(2,1)}, bf16[1024,512]{1,0:T(8,128)(2,1)}, f32[240,8,512]{2,1,0:T(8,128)}) custom-call(s32[8,128]{1,0:T(8,128)S(1)} %max.3.refs_0_, f32[1024,512]{1,0:T(8,128)} %copy-done, bf16[1024,512]{1,0:T(8,128)(2,1)} %copy-done.13, bf16[256,1024]{1,0:T(8,128)(2,1)S(1)} %get-tuple-element.29.refs_3_, ...), custom_call_target="tpu_custom_call" | custom-call | flops 1 | bytes 1 | tf_op jit(solution)/shard_map/early_scores/pallas_call | solution.py:279
  98.1 2.2 %collective-permute-done.12.last_ref = bf16[256,1024]{1,0:T(8,128)(2,1)S(1)} collective-permute-done((bf16[256,1024]{1,0:T(8,128)(2,1)S(1)}, bf16[256,1024]{1,0:T(8,128)(2,1)S(1)}, u32[]{:S(2)}, u32[]{:S(2)}) %collective-permute-start.12) | collective-permute-done | bytes 524320 | tf_op jit(solution)/shard_map/ppermute | solution.py:19
  100.3 1.2 %copy-done.2 = bf16[1024,512]{1,0:T(8,128)(2,1)S(1)} copy-done((bf16[1024,512]{1,0:T(8,128)(2,1)S(1)}, bf16[1024,512]{1,0:T(8,128)(2,1)}, u32[]{:S(2)}) %copy-start.2) | copy-done | bytes 1048600
  101.5 3.7 %row_scores.1 = (f32[1024,256]{1,0:T(8,128)S(1)}, f32[1024,256]{1,0:T(8,128)S(1)}) custom-call(s32[4,3]{1,0:T(4,128)S(1)} %get-tuple-element.22.table_ref, bf16[256,1024]{1,0:T(8,128)(2,1)S(1)} %collective-permute-done.12.last_ref, bf16[1024,512]{1,0:T(8,128)(2,1)S(1)} %copy-done.2, bf16[1024,512]{1,0:T(8,128)(2,1)} %get-tuple-element.31.low_ref, ...), custom_call_target="tpu_custom_call" | custom-call | flops 1 | bytes 1 | tf_op jit(solution)/shard_map/row_scores/pallas_call | solution.py:339
  105.2 0.1 collective-permute-start.15
  105.3 2.6 %collective-permute-done.15 = f32[1024,256]{1,0:T(8,128)S(1)} collective-permute-done((f32[1024,256]{1,0:T(8,128)S(1)}, f32[1024,256]{1,0:T(8,128)S(1)}, u32[]{:S(2)}, u32[]{:S(2)}) %collective-permute-start.15) | collective-permute-done | bytes 1048608 | tf_op jit(solution)/shard_map/ppermute | solution.py:19
  107.9 0.1 add.57
  108.1 0.6 collective-permute-start.16
  108.7 7.8 %collective-permute-done.16 = bf16[1024,128]{1,0:T(8,128)(2,1)S(1)} collective-permute-done((bf16[1024,128]{1,0:T(8,128)(2,1)S(1)}, bf16[1024,128]{1,0:T(8,128)(2,1)S(1)}, u32[]{:S(2)}, u32[]{:S(2)}) %collective-permute-start.16) | collective-permute-done | bytes 262176 | tf_op jit(solution)/shard_map/ppermute | solution.py:19
  116.6 1.0 copy.12
  (41 shorter events, 0.3 us)
Async XLA Ops:
  0.0 1.2 %copy-start.1 = (bf16[4,128,1024]{2,1,0:T(8,128)(2,1)S(1)}, bf16[4,128,1024]{2,1,0:T(8,128)(2,1)}, u32[]{:S(2)}) copy-start(bf16[4,128,1024]{2,1,0:T(8,128)(2,1)} %in_ref.1) | copy-start | bytes 3145732
  1.2 0.7 copy-start.8
  1.9 0.7 copy-start.10
  2.6 7.0 %copy-start.7 = (s32[4096]{0:T(1024)S(1)}, s32[4096]{0:T(1024)}, u32[]{:S(2)}) copy-start(s32[4096]{0:T(1024)} %param.9) | copy-start | bytes 49156
  3.4 11.7 %collective-permute-start.4 = (bf16[1,64,1024]{2,1,0:T(8,128)(2,1)S(1)}, bf16[1,64,1024]{2,1,0:T(8,128)(2,1)S(1)}, u32[]{:S(2)}, u32[]{:S(2)}) collective-permute-start(bf16[1,64,1024]{2,1,0:T(8,128)(2,1)S(1)} %get-tuple-element.42), channel_id=1, source_target_pairs={{0,12},{4,0},{8,4},{12,8},{1,13},{5,1},{9,5},{13,9},{2,14},{6,2},{... | collective-permute-start | bytes 393224 | tf_op jit(solution)/shard_map/ppermute | solution.py:19
  8.5 11.2 %collective-permute-start.3 = (bf16[1,64,1024]{2,1,0:T(8,128)(2,1)S(1)}, bf16[1,64,1024]{2,1,0:T(8,128)(2,1)S(1)}, u32[]{:S(2)}, u32[]{:S(2)}) collective-permute-start(bf16[1,64,1024]{2,1,0:T(8,128)(2,1)S(1)} %get-tuple-element.43), channel_id=1, source_target_pairs={{0,8},{4,12},{8,0},{12,4},{1,9},{5,13},{9,1},{13,5},{2,10},{6,14},... | collective-permute-start | bytes 393224 | tf_op jit(solution)/shard_map/ppermute | solution.py:19
  8.5 11.2 %collective-permute-start.2 = (bf16[1,64,1024]{2,1,0:T(8,128)(2,1)S(1)}, bf16[1,64,1024]{2,1,0:T(8,128)(2,1)S(1)}, u32[]{:S(2)}, u32[]{:S(2)}) collective-permute-start(bf16[1,64,1024]{2,1,0:T(8,128)(2,1)S(1)} %get-tuple-element.44), channel_id=1, source_target_pairs={{0,4},{4,8},{8,12},{12,0},{1,5},{5,9},{9,13},{13,1},{2,6},{6,10},{... | collective-permute-start | bytes 393224 | tf_op jit(solution)/shard_map/ppermute | solution.py:19
  15.2 5.4 %copy-start.5 = (bf16[256,1024]{1,0:T(8,128)(2,1)}, bf16[256,1024]{1,0:T(8,128)(2,1)S(1)}, u32[]{:S(2)}) copy-start(bf16[256,1024]{1,0:T(8,128)(2,1)S(1)} %get-tuple-element.24.refs_0_) | copy-start | bytes 1572868
  19.8 16.1 %collective-permute-start.6 = (bf16[256,1024]{1,0:T(8,128)(2,1)S(1)}, bf16[256,1024]{1,0:T(8,128)(2,1)S(1)}, u32[]{:S(2)}, u32[]{:S(2)}) collective-permute-start(bf16[256,1024]{1,0:T(8,128)(2,1)S(1)} %get-tuple-element.25.refs_1_), channel_id=1, source_target_pairs={{0,4},{4,8},{8,12},{12,0},{1,5},{5,9},{9,13},{13,1},{2,6},{6,10},{... | collective-permute-start | bytes 1572872 | tf_op jit(solution)/shard_map/ppermute | solution.py:19
  20.6 15.3 %collective-permute-start.5 = (bf16[4,64,1024]{2,1,0:T(8,128)(2,1)S(1)}, bf16[4,64,1024]{2,1,0:T(8,128)(2,1)S(1)}, u32[]{:S(2)}, u32[]{:S(2)}) collective-permute-start(bf16[4,64,1024]{2,1,0:T(8,128)(2,1)S(1)} %after.5.refs_0_), channel_id=1, source_target_pairs={{0,16},{16,0},{1,17},{17,1},{2,18},{18,2},{3,19},{19,3},{4,20},{20... | collective-permute-start | bytes 1572872 | tf_op jit(solution)/shard_map/ppermute | solution.py:19
  22.9 10.5 %collective-permute-start.7 = (s32[8,128]{1,0:T(8,128)S(1)}, s32[8,128]{1,0:T(8,128)S(1)}, u32[]{:S(2)}, u32[]{:S(2)}) collective-permute-start(s32[8,128]{1,0:T(8,128)S(1)} %get-tuple-element.26), channel_id=1, source_target_pairs={{0,16},{16,0},{1,17},{17,1},{2,18},{18,2},{3,19},{19,3},{4,20},{20... | collective-permute-start | bytes 12296 | tf_op jit(solution)/shard_map/ppermute | solution.py:19
  34.7 2.0 %copy-start.9 = (s32[4,4]{1,0:T(4,128)S(1)}, s32[4,4]{1,0:T(4,128)}, u32[]{:S(2)}) copy-start(s32[4,4]{1,0:T(4,128)} %pattern_ref.3) | copy-start | bytes 196
  34.7 2.0 %copy-start.11 = (s32[16]{0:T(128)S(1)}, s32[16]{0:T(128)}, u32[]{:S(2)}) copy-start(s32[16]{0:T(128)} %slot_ref.3) | copy-start | bytes 196
  35.9 0.8 copy-start.3
  36.7 1.0 copy-start.4
  42.4 11.9 %collective-permute-start.9 = (f32[1024,512]{1,0:T(8,128)}, f32[1024,512]{1,0:T(8,128)}, u32[]{:S(2)}, u32[]{:S(2)}) collective-permute-start(f32[1024,512]{1,0:T(8,128)} %partial_weights.7), channel_id=1, source_target_pairs={{0,1},{1,0},{2,3},{3,2},{4,5},{5,4},{6,7},{7,6},{8,9},{9,8},{10,11... | collective-permute-start | bytes 6291464 | tf_op jit(solution)/shard_map/ppermute | solution.py:19
  46.0 10.3 %collective-permute-start.8 = (f32[1024,512]{1,0:T(8,128)}, f32[1024,512]{1,0:T(8,128)}, u32[]{:S(2)}, u32[]{:S(2)}) collective-permute-start(f32[1024,512]{1,0:T(8,128)} %partial_weights.5), channel_id=1, source_target_pairs={{0,1},{1,0},{2,3},{3,2},{4,5},{5,4},{6,7},{7,6},{8,9},{9,8},{10,11... | collective-permute-start | bytes 6291464 | tf_op jit(solution)/shard_map/ppermute | solution.py:19
  46.6 14.8 %collective-permute-start.10 = (bf16[128,1024]{1,0:T(8,128)(2,1)S(1)}, bf16[128,1024]{1,0:T(8,128)(2,1)S(1)}, u32[]{:S(2)}, u32[]{:S(2)}) collective-permute-start(bf16[128,1024]{1,0:T(8,128)(2,1)S(1)} %after.6), channel_id=1, source_target_pairs={{0,8},{4,12},{8,0},{12,4},{1,9},{5,13},{9,1},{13,5},{2,10},{6,14},... | collective-permute-start | bytes 786440 | tf_op jit(solution)/shard_map/ppermute | solution.py:23
  56.4 5.0 %copy-start = (f32[1024,512]{1,0:T(8,128)}, f32[1024,512]{1,0:T(8,128)S(1)}, u32[]{:S(2)}) copy-start(f32[1024,512]{1,0:T(8,128)S(1)} %add.56.refs_1_) | copy-start | bytes 6291460
  59.1 3.7 %copy-start.6 = (bf16[256,1024]{1,0:T(8,128)(2,1)S(1)}, bf16[256,1024]{1,0:T(8,128)(2,1)}, u32[]{:S(2)}) copy-start(bf16[256,1024]{1,0:T(8,128)(2,1)} %copy-done.5) | copy-start | bytes 1572868
  61.4 27.8 %collective-permute-start.13 = (bf16[1024,512]{1,0:T(8,128)(2,1)S(1)}, bf16[1024,512]{1,0:T(8,128)(2,1)S(1)}, u32[]{:S(2)}, u32[]{:S(2)}) collective-permute-start(bf16[1024,512]{1,0:T(8,128)(2,1)S(1)} %after.7.refs_1_), channel_id=1, source_target_pairs={{0,2},{2,0},{1,3},{3,1},{4,6},{6,4},{5,7},{7,5},{8,10},{10,8},{9,1... | collective-permute-start | bytes 3145736 | tf_op jit(solution)/shard_map/ppermute | solution.py:19
  62.9 26.1 %copy-start.12 = (bf16[512,1024]{1,0:T(8,128)(2,1)S(1)}, bf16[512,1024]{1,0:T(8,128)(2,1)}, u32[]{:S(2)}) copy-start(bf16[512,1024]{1,0:T(8,128)(2,1)} %get-tuple-element.45.refs_3_) | copy-start | bytes 3145732
  62.9 24.9 %collective-permute-start.11 = (bf16[256,1024]{1,0:T(8,128)(2,1)S(1)}, bf16[256,1024]{1,0:T(8,128)(2,1)S(1)}, u32[]{:S(2)}, u32[]{:S(2)}) collective-permute-start(bf16[256,1024]{1,0:T(8,128)(2,1)S(1)} %after.8), channel_id=1, source_target_pairs={{0,8},{4,12},{8,0},{12,4},{1,9},{5,13},{9,1},{13,5},{2,10},{6,14},... | collective-permute-start | bytes 1572872 | tf_op jit(solution)/shard_map/ppermute | solution.py:19
  62.9 26.2 %collective-permute-start.14 = (bf16[256,1024]{1,0:T(8,128)(2,1)S(1)}, bf16[256,1024]{1,0:T(8,128)(2,1)S(1)}, u32[]{:S(2)}, u32[]{:S(2)}) collective-permute-start(bf16[256,1024]{1,0:T(8,128)(2,1)S(1)} %pad_maximum_fusion.3), channel_id=1, source_target_pairs={{0,4},{4,0},{8,12},{12,8},{1,5},{5,1},{9,13},{13,9},{2,6},{6,2},{1... | collective-permute-start | bytes 1572872 | tf_op jit(solution)/shard_map/ppermute | solution.py:23
  87.8 12.5 %collective-permute-start.12 = (bf16[256,1024]{1,0:T(8,128)(2,1)S(1)}, bf16[256,1024]{1,0:T(8,128)(2,1)S(1)}, u32[]{:S(2)}, u32[]{:S(2)}) collective-permute-start(bf16[256,1024]{1,0:T(8,128)(2,1)S(1)} %after.9), channel_id=1, source_target_pairs={{0,12},{4,0},{8,4},{12,8},{1,13},{5,1},{9,5},{13,9},{2,14},{6,2},{... | collective-permute-start | bytes 1572872 | tf_op jit(solution)/shard_map/ppermute | solution.py:19
  89.2 1.0 copy-start.13
  100.3 1.2 %copy-start.2 = (bf16[1024,512]{1,0:T(8,128)(2,1)S(1)}, bf16[1024,512]{1,0:T(8,128)(2,1)}, u32[]{:S(2)}) copy-start(bf16[1024,512]{1,0:T(8,128)(2,1)} %get-tuple-element.30.high_ref) | copy-start | bytes 3145732
  105.2 2.7 %collective-permute-start.15 = (f32[1024,256]{1,0:T(8,128)S(1)}, f32[1024,256]{1,0:T(8,128)S(1)}, u32[]{:S(2)}, u32[]{:S(2)}) collective-permute-start(f32[1024,256]{1,0:T(8,128)S(1)} %get-tuple-element.34), channel_id=1, source_target_pairs={{0,1},{1,0},{2,3},{3,2},{4,5},{5,4},{6,7},{7,6},{8,9},{9,8},{10,11... | collective-permute-start | bytes 3145736 | tf_op jit(solution)/shard_map/ppermute | solution.py:19
  108.1 8.4 %collective-permute-start.16 = (bf16[1024,128]{1,0:T(8,128)(2,1)S(1)}, bf16[1024,128]{1,0:T(8,128)(2,1)S(1)}, u32[]{:S(2)}, u32[]{:S(2)}) collective-permute-start(bf16[1024,128]{1,0:T(8,128)(2,1)S(1)} %dynamic-slice_convert_fusion), channel_id=1, source_target_pairs={{0,2},{2,0},{1,3},{3,1},{4,6},{6,4},{5,7},{7,5},{8,10},{10,8},{9,1... | collective-permute-start | bytes 786440 | tf_op jit(solution)/shard_map/ppermute | solution.py:19

commit v5 on v4

--- a/solution.py
+++ b/solution.py
@@ -12,6 +12,7 @@
 ANY = pl.BlockSpec(memory_space=pl.ANY)
 SMEM = pl.BlockSpec(memory_space=pltpu.SMEM)
 PARAMS = pltpu.CompilerParams(vmem_limit_bytes=50 * 2**20)
+FIRST = pltpu.CompilerParams(vmem_limit_bytes=60 * 2**20)
 LANES = 128
 
 
@@ -74,7 +75,7 @@
         ),
         out_shape=jax.ShapeDtypeStruct((n_cluster, part, width), BF16),
         cost_estimate=cost(0, 4 * n_cluster * part * width),
-        compiler_params=PARAMS,
+        compiler_params=FIRST,
         name="pick_queries",
     )(pattern, block_slot, query_store)
 
@@ -145,7 +146,7 @@
             if extra:
                 surplus = n_shard * bulk + past + rank[part] - bulk
                 place = jnp.where(rank[part] < bulk, place, surplus)
-                past = past + jnp.floor((jnp.maximum(whole[part] - bulk, 0.0) + 7.0) * 0.125) * 8.0
+                past = past + jnp.floor((jnp.maximum(whole[part] - bulk, 0.0) + 15.0) * 0.0625) * 16.0
             goal = goal + masks[c] * place
         goal_ref[...] = goal.astype(I32)
 
@@ -181,14 +182,18 @@
     )(ids, train)
 
 
-def partial_weights(matrix, chosen, block, depth):
+def partial_weights(matrix, chosen, block, depth, dtype, *addends, others=()):
     width, total = chosen.shape
-    tile = 512 if depth % 512 == 0 else depth
+    tile = 256 if depth % 256 == 0 else depth
     steps = depth // tile
 
-    def kernel(block_ref, matrix_ref, chosen_ref, out_ref):
-        out_ref[...] = dot(matrix_ref[...], chosen_ref[...])
-
+    def kernel(block_ref, matrix_ref, chosen_ref, *rest):
+        value = dot(matrix_ref[...], chosen_ref[...])
+        for ref in rest[:len(addends)]:
+            value = value + ref[...]
+        rest[-1][...] = value.astype(dtype)
+
+    rows = pl.BlockSpec((tile, total), lambda i, b: (i, 0))
     return pl.pallas_call(
         kernel,
         grid_spec=pltpu.PrefetchScalarGridSpec(
@@ -197,14 +202,16 @@
             in_specs=[
                 pl.BlockSpec((tile, width), lambda i, b: (b[0] * steps + i, 0)),
                 pl.BlockSpec((width, total), lambda i, b: (0, 0)),
-            ],
-            out_specs=pl.BlockSpec((tile, total), lambda i, b: (i, 0)),
+            ]
+            + [rows] * len(addends)
+            + [ANY] * len(others),
+            out_specs=rows,
         ),
-        out_shape=jax.ShapeDtypeStruct((depth, total), F32),
+        out_shape=jax.ShapeDtypeStruct((depth, total), dtype),
         cost_estimate=cost(2 * depth * width * total, 2 * depth * width + 4 * depth * total),
         compiler_params=PARAMS,
         name="partial_weights",
-    )(jnp.reshape(block, (1,)).astype(I32), matrix, chosen)
+    )(jnp.reshape(block, (1,)).astype(I32), matrix, chosen, *addends, *others)
 
 
 def row_table(ids, lines, bulk, extra):
@@ -225,13 +232,14 @@
             if extra:
                 surplus = jnp.int32(0)
                 for c in range(n_shard):
-                    over = lax.div(jnp.maximum(count(c) - bulk, 0) + 7, jnp.int32(8)) * 8
+                    over = lax.div(jnp.maximum(count(c) - bulk, 0) + 15, jnp.int32(16)) * 16
                     before = before + jnp.where(c < me, over, 0)
                     surplus = surplus + over
                 most = jnp.maximum(most, surplus)
             table_ref[s, 0] = start
             table_ref[s, 1] = jnp.minimum(mine, bulk)
-            table_ref[s, 2] = lax.div(before, jnp.int32(8))
+            table_ref[s, 2] = lax.div(before, jnp.int32(16))
+            table_ref[s, 3] = jnp.maximum(mine - bulk, 0)
             start = start + mine
         flag_ref[...] = jnp.full((8, LANES), (most > extra).astype(I32))
 
@@ -239,116 +247,163 @@
         kernel,
         in_specs=[VMEM],
         out_specs=[SMEM, VMEM],
-        out_shape=[jax.ShapeDtypeStruct((n_shard, 3), I32), jax.ShapeDtypeStruct((8, LANES), I32)],
+        out_shape=[jax.ShapeDtypeStruct((n_shard, 4), I32), jax.ShapeDtypeStruct((8, LANES), I32)],
         cost_estimate=cost(0, 4 * ids.size),
         compiler_params=PARAMS,
         name="row_table",
     )(ids)
 
 
-def early_scores(own, others, pieces, flag, sure):
+def put(acc, x, start, count=None):
+    tiles, _, width = x.shape
+    first, within = lax.div(start, jnp.int32(8)), lax.rem(start, jnp.int32(8))
+    turned = pltpu.roll(x, within, 1)
+    row = lax.broadcasted_iota(I32, (1, 8, width), 1)
+    keep = row < within
+    pieces = jnp.where(keep, jnp.concatenate([turned[:1], turned]), jnp.concatenate([turned, turned[-1:]]))
+    if count is None:
+        pieces = jnp.concatenate([jnp.where(keep, acc[pl.ds(first, 1)], turned[:1]), pieces[1:]])
+    else:
+        at = lax.broadcasted_iota(I32, (tiles + 1, 8, width), 0) * 8 + lax.broadcasted_iota(
+            I32, (tiles + 1, 8, width), 1
+        )
+        pieces = jnp.where(
+            (at >= within) & (at < within + count), pieces, acc[pl.ds(first, tiles + 1)]
+        )
+    acc[pl.ds(first, tiles + 1)] = pieces
+
+
+def give(value, outs, rep, half):
+    n_rep = len(outs)
+    for r in range(n_rep):
+        @pl.when(rep == r)
+        def _():
+            for d, out in enumerate(outs):
+                at = ((r + d) % n_rep) * half
+                out[...] = value(at)
+
+
+def early_scores(own, others, pieces, firsts, seconds, table, rows, n_rep, n_shard, bulk):
     depth, width = own.shape
-    count = sum(p.shape[0] for p in pieces)
-    n_other = len(others)
-
-    def kernel(*refs):
-        flag_ref, refs = refs[0], refs[1:]
-        own_ref, other_refs, piece_refs = refs[0], refs[1:1 + n_other], refs[1 + n_other:-3]
-        flagged = jnp.max(flag_ref[...]) > 0
-        high_ref, low_ref, out_ref = refs[-3:]
+    half = width // n_rep
+    n_other, n_piece = len(others), len(pieces)
+    extra = firsts[0].shape[0] if firsts else 0
+    last_hops = n_shard - 1
+
+    def kernel(table_ref, *refs):
+        own_ref, refs = refs[0], refs[1:]
+        other_refs, refs = refs[:n_other], refs[n_other:]
+        piece_refs, refs = refs[:n_piece], refs[n_piece:]
+        first_refs, refs = refs[:len(firsts)], refs[len(firsts):]
+        second_refs, refs = refs[:len(seconds)], refs[len(seconds):]
+        high_ref, low_ref, outs, (scored, held, acc) = refs[0], refs[1], refs[2:2 + n_rep], refs[2 + n_rep:]
+        me, rep = lax.axis_index("shard"), lax.axis_index("rep")
         weight = own_ref[...]
         for ref in other_refs:
             weight = weight + ref[...].astype(F32)
         high = weight.astype(BF16)
         high_ref[...] = high
         low_ref[...] = (weight - high.astype(F32)).astype(BF16)
-        base = 0
-
-        def score(ref, at):
-            x = ref[...]
+
+        def score(x):
             y = dot(x, high_ref[...]) + dot(x, low_ref[...])
-            out_ref[at // 8:(at + x.shape[0]) // 8] = y.reshape(x.shape[0] // 8, 8, width)
-
-        for ref, always in zip(piece_refs, sure):
-            if always:
-                score(ref, base)
-            else:
-                pl.when(flagged)(functools.partial(score, ref, base))
-            base += ref.shape[0]
-
-    return pl.pallas_call(
-        kernel,
-        in_specs=[VMEM] * (2 + n_other + len(pieces)),
-        out_specs=[VMEM] * 3,
+            return y.reshape(x.shape[0] // 8, 8, width)
+
+        for hops, ref in enumerate(piece_refs):
+            scored[lax.rem(me + (n_shard - hops), jnp.int32(n_shard))] = score(ref[...])
+        last = lax.rem(me + (n_shard - last_hops), jnp.int32(n_shard))
+        for s in range(n_shard):
+            start = table_ref[s, 0]
+
+            @pl.when(last != s)
+            def _():
+                put(acc, scored[s], start)
+
+            if extra:
+                @pl.when(table_ref[s, 3] > 0)
+                def _():
+                    apart = jnp.bitwise_xor(me, s)
+                    for v in range(n_shard):
+                        @pl.when(apart == v)
+                        def _():
+                            index = (v & 1) * 2 + v // 2
+                            held[:extra, :] = first_refs[index][...]
+                            held[extra:2 * extra, :] = second_refs[index][...]
+                    x = held[pl.ds(pl.multiple_of(table_ref[s, 2] * 16, 16), extra), :]
+                    put(acc, score(x), start + table_ref[s, 1])
+        give(lambda at: acc[:rows // 8, :, at:at + half].reshape(rows, half), outs, rep, half)
+
+    count = n_shard * bulk
+    return pl.pallas_call(
+        kernel,
+        in_specs=[SMEM] + [VMEM] * (1 + n_other + n_piece + len(firsts) + len(seconds)),
+        out_specs=[VMEM] * (2 + n_rep),
         out_shape=[jax.ShapeDtypeStruct((depth, width), BF16)] * 2
-        + [jax.ShapeDtypeStruct(((count + LANES) // 8, 8, width), F32)],
+        + [jax.ShapeDtypeStruct((rows, half), F32)] * n_rep,
+        scratch_shapes=[
+            pltpu.VMEM((n_shard, bulk // 8, 8, width), F32),
+            pltpu.VMEM((3 * extra + 16, depth), BF16),
+            pltpu.VMEM(((rows + bulk + extra) // 8 + 2, 8, width), F32),
+        ],
         cost_estimate=cost(4 * count * depth * width, 10 * depth * width + count * (2 * depth + 4 * width)),
         compiler_params=PARAMS,
         name="early_scores",
-    )(flag, own, *others, *pieces)
-
-
-def row_scores(table, last, high, low, early, rows, n_rep, bulk, extra, cuts):
-    n_shard = table.shape[0]
+    )(table, own, *others, *pieces, *firsts, *seconds)
+
+
+def late_scores(last, high, low, n_rep, *others):
+    rows = last.shape[0]
     width = high.shape[1]
     half = width // n_rep
-    late_rows = last.shape[0]
-    surplus_at = (n_shard * bulk - late_rows) // 8
-
-    def kernel(table_ref, last_ref, high_ref, low_ref, early_ref, *rest):
-        outs, late, acc = rest[:-2], rest[-2], rest[-1]
-        me, rep = lax.axis_index("shard"), lax.axis_index("rep")
+
+    def kernel(last_ref, high_ref, low_ref, *rest):
+        outs, late = rest[len(others):-1], rest[-1]
         x = last_ref[...]
-        y = dot(x, high_ref[...]) + dot(x, low_ref[...])
-        late[...] = y.reshape(late_rows // 8, 8, width)
-
-        def put(x, start):
-            tiles = x.shape[0]
-            first, within = lax.div(start, jnp.int32(8)), lax.rem(start, jnp.int32(8))
-            turned = pltpu.roll(x, within, 1)
-            keep = lax.broadcasted_iota(I32, (1, 8, width), 1) < within
-            acc[pl.ds(first, 1)] = jnp.where(keep, acc[pl.ds(first, 1)], turned[:1])
-            acc[pl.ds(first + 1, tiles - 1)] = jnp.where(keep, turned[:-1], turned[1:])
-            acc[pl.ds(first + tiles, 1)] = turned[-1:]
-
-        for s in range(n_shard):
-            start = table_ref[s, 0]
-            for hops in range(n_shard):
-                @pl.when(lax.rem(me + (n_shard - hops), jnp.int32(n_shard)) == s)
-                def _():
-                    base = 0
-                    for h, first, n in cuts:
-                        if h == hops:
-                            if base + n <= n_shard * bulk - late_rows:
-                                put(early_ref[base // 8:(base + n) // 8], start + first)
-                            else:
-                                put(late[...], start + first)
-                        base += n
-            if extra:
-                apart = jnp.bitwise_xor(me, s)
-                index = jnp.bitwise_and(apart, 1) * 2 + lax.div(apart, jnp.int32(2))
-                first = surplus_at + index * (2 * extra // 8) + table_ref[s, 2]
-                put(early_ref[pl.ds(first, extra // 8)], start + table_ref[s, 1])
-        for r in range(n_rep):
-            @pl.when(rep == r)
-            def _():
-                for d, out in enumerate(outs):
-                    at = ((r + d) % n_rep) * half
-                    out[...] = acc[:rows // 8, :, at:at + half].reshape(rows, half)
-
-    return pl.pallas_call(
-        kernel,
-        in_specs=[SMEM] + [VMEM] * 4,
+        late[...] = dot(x, high_ref[...]) + dot(x, low_ref[...])
+        give(lambda at: late[:, at:at + half], outs, lax.axis_index("rep"), half)
+
+    return pl.pallas_call(
+        kernel,
+        in_specs=[VMEM] * 3 + [ANY] * len(others),
         out_specs=[VMEM] * n_rep,
         out_shape=[jax.ShapeDtypeStruct((rows, half), F32)] * n_rep,
-        scratch_shapes=[
-            pltpu.VMEM((late_rows // 8, 8, width), F32),
-            pltpu.VMEM(((rows + bulk + extra) // 8 + 1, 8, width), F32),
-        ],
-        cost_estimate=cost(4 * late_rows * high.shape[0] * width, 8 * rows * width),
-        compiler_params=PARAMS,
-        name="row_scores",
-    )(table, last, high, low, early)
+        scratch_shapes=[pltpu.VMEM((rows, width), F32)],
+        cost_estimate=cost(4 * rows * high.shape[0] * width, 8 * rows * width),
+        compiler_params=PARAMS,
+        name="late_scores",
+    )(last, high, low, *others)
+
+
+def merge(table, early, late, n_shard):
+    rows, width = early[0].shape
+    last_rows = late[0].shape[0]
+    last_hops = n_shard - 1
+
+    def kernel(table_ref, *refs):
+        early_refs, late_refs = refs[:len(early)], refs[len(early):-2]
+        out_ref, acc = refs[-2:]
+        source = lax.rem(lax.axis_index("shard") + (n_shard - last_hops), jnp.int32(n_shard))
+
+        def total(parts):
+            value = parts[0][...]
+            for ref in parts[1:]:
+                value = value + ref[...].astype(F32)
+            return value.reshape(value.shape[0] // 8, 8, width)
+
+        acc[:rows // 8] = total(early_refs)
+        put(acc, total(late_refs), table_ref[source, 0], table_ref[source, 1])
+        out_ref[...] = acc[:rows // 8].reshape(rows, width).T
+
+    return pl.pallas_call(
+        kernel,
+        in_specs=[SMEM] + [VMEM] * (len(early) + len(late)),
+        out_specs=VMEM,
+        out_shape=jax.ShapeDtypeStruct((width, rows), F32),
+        scratch_shapes=[pltpu.VMEM(((rows + last_rows) // 8 + 2, 8, width), F32)],
+        cost_estimate=cost(0, 8 * rows * width),
+        compiler_params=PARAMS,
+        name="merge",
+    )(table, *early, *late)
 
 
 def body(train, cluster_ids, precond, query_store, block_slot, pattern):
@@ -371,8 +426,9 @@
 
     cuts = [(d, 0, bulk) for d in range(n_shard)]
     packed = pack_rows(train, ids, columns, bulk, extra, cuts)
-    here = [packed[0], shift(packed[1], "shard", n_shard, 1)]
     table, flag = row_table(ids, lines, bulk, extra)
+    here = {0: packed[0]}
+    last_hops = n_shard - 1
 
     def swap_far(x):
         return jnp.concatenate([x, swap(x, "shard", n_shard, 2)])
@@ -380,7 +436,7 @@
     def swap_near(x):
         return jnp.concatenate([x, swap(x, "shard", n_shard, 1)])
 
-    before_join, before_feat = [here[1]], []
+    before_join = []
     if extra:
         for d in range(1, n_group):
             flag = jnp.maximum(flag, shift(flag, "groups", n_group, d))
@@ -390,51 +446,60 @@
             lambda x: jnp.zeros((n_shard * extra, columns), BF16),
             packed[-1],
         )
-        far = swap(after(packed[-2], here[1]), "shard", n_shard, 2)
-        before_join.append(second)
-        before_feat.append(far)
-
-    arrived = after(jnp.concatenate(pieces), packed[1])
+        far = swap(packed[-2], "shard", n_shard, 2)
+        before_join = [far, second]
+
+    arrived = after(jnp.concatenate(pieces), packed[1], flag)
     parts = [arrived] + [shift(arrived, "groups", n_group, d) for d in range(1, n_group)]
     chosen = join_queries(parts, block_slot, pattern, query_store.shape[0], n_feat, n_rep, *before_join)
+    here[1] = shift(after(packed[1], *before_join[:1]), "shard", n_shard, 1)
 
     matrix = precond[0]
 
-    def weights(f, r):
-        return partial_weights(matrix, chosen, f * n_rep + r, columns)
-
-    targets = [(feat + d) % n_feat for d in range(1, n_feat)] + [feat]
-    away = [[shift(weights(f, (rep + d) % n_rep), "rep", n_rep, d) for d in range(1, n_rep)] for f in targets]
-    sums = [sum(x, weights(f, rep)) for f, x in zip(targets, away)]
-    own = sums[-1]
-    sends = [after(x.astype(BF16), own, *before_feat) for x in sums[:-1]]
+    def weights(f, r, dtype, *addends, others=()):
+        return partial_weights(matrix, chosen, f * n_rep + r, columns, dtype, *addends, others=others)
+
+    def away(f, others=()):
+        return [
+            shift(weights(f, (rep + d) % n_rep, F32, others=others), "rep", n_rep, d) for d in range(1, n_rep)
+        ]
+
+    targets = [(feat + d) % n_feat for d in range(1, n_feat)]
+    sends = [weights(f, rep, BF16, *x) for f, x in [(f, away(f)) for f in targets]]
     others = [shift(x, "feat", n_feat, d + 1) for d, x in enumerate(sends)]
-
-    extras = []
+    own = weights(feat, rep, F32, *away(feat, [here[1], *sends]))
+
+    firsts, seconds = [], []
     if extra:
         first = swap_near(jnp.concatenate([packed[-2], far]))
-        for j in range(n_shard):
-            at = slice(j * extra, (j + 1) * extra)
-            extras += [first[at], second[at]]
-    for d in range(2, n_shard - 1):
-        here.append(shift(after(packed[d], *sends), "shard", n_shard, d))
-    last = shift(after(packed[n_shard - 1], here[-1]), "shard", n_shard, n_shard - 1)
-
-    sure = [True] * len(here) + [True, False] * (len(extras) // 2)
-    high, low, early = early_scores(own, others, here + extras, flag, sure)
-    shares = row_scores(table, last, high, low, early, rows, n_rep, bulk, extra, cuts)
-    total = shares[0]
-    for d in range(1, n_rep):
-        total = total + shift(shares[d], "rep", n_rep, d)
-    share = total.shape[1] // n_feat
-
-    def for_feat(f):
-        return lax.dynamic_slice_in_dim(total, f * share, share, 1)
-
-    result = for_feat(feat)
-    for d in range(1, n_feat):
-        result = result + shift(for_feat((feat + d) % n_feat).astype(BF16), "feat", n_feat, d).astype(F32)
-    return result.T[None]
+        firsts = [first[j * extra:(j + 1) * extra] for j in range(n_shard)]
+        seconds = [second[j * extra:(j + 1) * extra] for j in range(n_shard)]
+    for d in range(2, last_hops):
+        here[d] = shift(after(packed[d], *sends), "shard", n_shard, d)
+    last = shift(after(packed[last_hops], here[last_hops - 1]), "shard", n_shard, last_hops)
+
+    ready = [here[d] for d in range(last_hops)]
+    high, low, *shares = early_scores(
+        own, others, ready, firsts, seconds, table, rows, n_rep, n_shard, bulk
+    )
+
+    def over_rep(shares):
+        total = shares[0]
+        for d in range(1, n_rep):
+            total = total + shift(shares[d], "rep", n_rep, d)
+        return total
+
+    def for_feat(total, d):
+        share = total.shape[1] // n_feat
+        return lax.dynamic_slice_in_dim(total, ((feat + d) % n_feat) * share, share, 1)
+
+    early = over_rep(shares)
+    early_sends = [for_feat(early, d).astype(BF16) for d in range(1, n_feat)]
+    late = over_rep(late_scores(last, high, low, n_rep, *early_sends))
+    late_sends = [for_feat(late, d).astype(BF16) for d in range(1, n_feat)]
+    early_all = [for_feat(early, 0)] + [shift(x, "feat", n_feat, d + 1) for d, x in enumerate(early_sends)]
+    late_all = [for_feat(late, 0)] + [shift(x, "feat", n_feat, d + 1) for d, x in enumerate(late_sends)]
+    return merge(table, early_all, late_all, n_shard)[None]
 
 
 def solution(mesh):

time: 118 us -> 129 us (1.093)
  waiting for transfers between devices: 50.5 us -> 60.7 us
  Pallas kernels: 32.5 us -> 37.2 us
  other arithmetic: 5.09 us -> 3.56 us
  starting transfers between devices: 19 us -> 17.5 us
    ppermute x2, waiting for transfers between devices: 2.24 us -> 30.1 us  [swap(): return lax.ppermute(x, axis, [(i, i ^ bit) for i in range(size)])]
    ppermute x13 -> x15, waiting for transfers between devices: 48.2 us -> 30.6 us  [shift(): return lax.ppermute(x, axis, [(i, (i + by) % size) for i in range(size)])]
    unnamed x29 -> x22, local copies, waits for them, and re-layouts: 6.65 us -> 1.39 us
    pallas_call x4, Pallas kernels: 12.6 us -> 17 us  [partial_weights(): pl.pallas_call(kernel, grid_spec=pltpu.PrefetchScalarGridSpec(num_scalar_...]
    ppermute x2, starting transfers between devices: 6.16 us -> 2.5 us  [swap(): return lax.ppermute(x, axis, [(i, i ^ bit) for i in range(size)])]
    pallas_call x1, Pallas kernels: 0.81 us -> 4.09 us  [pick_queries(): pl.pallas_call(kernel, grid_spec=pltpu.PrefetchScalarGridSpec(num_scalar_...]
    convert_element_type x1 -> x0, other arithmetic: 2.73 us -> none  [body(): sends = [after(x.astype(BF16), own, *before_feat) for x in sums[:-1]]]
    pallas_call x2 -> x3, Pallas kernels: 11.7 us -> 9.12 us  [the longest x1 6.7 us: early_scores(): pl.pallas_call(kernel, in_specs=[SMEM] + [VMEM] * (1 + n_other + n_piece...]
  transfers between devices with their start and end apart: 15 -> 17, of which waited for: 7 -> 9; matrix products, arithmetic and copies ran while one was open for 6% -> 8% of each run, Pallas kernels for 20% -> 11%
where the time goes in v5:
time: 129 us
  waiting for transfers between devices  60.7 us (47%)
  Pallas kernels  37.2 us (29%)
  starting transfers between devices  17.5 us (14%)
  local copies, waits for them, and re-layouts  8.71 us (7%)
  other arithmetic  3.56 us (3%)
    ppermute x15, waiting for transfers between devices, shift(): return lax.ppermute(x, axis, [(i, (i + by) % size) for i in range(size)])  30.6 us
    ppermute x2, waiting for transfers between devices, swap(): return lax.ppermute(x, axis, [(i, i ^ bit) for i in range(size)])  30.1 us
    pallas_call x4, Pallas kernels, partial_weights(): pl.pallas_call(kernel, grid_spec=pltpu.PrefetchScalarGridSpec(num_scalar_...  17 us
    ppermute x15, starting transfers between devices, shift(): return lax.ppermute(x, axis, [(i, (i + by) % size) for i in range(size)])  15 us
    pallas_call x1, Pallas kernels, early_scores(): pl.pallas_call(kernel, in_specs=[SMEM] + [VMEM] * (1 + n_other + n_piece...  6.7 us
    pallas_call x1, Pallas kernels, pack_rows(): pl.pallas_call(kernel, grid=(1,), in_specs=[pl.BlockSpec((lines, LANES),...  5.21 us
    pallas_call x1, Pallas kernels, pick_queries(): pl.pallas_call(kernel, grid_spec=pltpu.PrefetchScalarGridSpec(num_scalar_...  4.09 us
    add x2, other arithmetic, over_rep(): total = total + shift(shares[d], 'rep', n_rep, d)  2.68 us
  transfers between devices with their start and end apart: 17, of which 9 were waited for; matrix products, arithmetic and copies ran while one was open for 8% of the time, Pallas kernels for 11%

profile of v5, /device:TPU:0, one launch (start us, length us, event | category | flops | bytes accessed | tf_op | source)
XLA Modules:
  0.0 128.6 jit_solution(1559442657972719921)
XLA Ops:
  0.0 4.1 %pick_queries.1 = bf16[4,64,1024]{2,1,0:T(8,128)(2,1)} custom-call(s32[4,4]{1,0:T(4,128)} %pattern_ref.3, s32[16]{0:T(128)} %slot_ref.3, bf16[4,128,1024]{2,1,0:T(8,128)(2,1)} %in_ref.1), custom_call_target="tpu_custom_call" | custom-call | flops 1 | bytes 1 | tf_op jit(solution)/shard_map/pick_queries/pallas_call | solution.py:68
  4.1 1.1 fusion.2
  5.2 5.1 %collective-permute-start.4 = (bf16[1,64,1024]{2,1,0:T(8,128)(2,1)S(1)}, bf16[1,64,1024]{2,1,0:T(8,128)(2,1)S(1)}, u32[]{:S(2)}, u32[]{:S(2)}) collective-permute-start(bf16[1,64,1024]{2,1,0:T(8,128)(2,1)S(1)} %get-tuple-element.44), channel_id=1, source_target_pairs={{0,12},{4,0},{8,4},{12,8},{1,13},{5,1},{9,5},{13,9},{2,14},{6,2},{... | collective-permute-start | bytes 393224 | tf_op jit(solution)/shard_map/ppermute | solution.py:20
  10.3 0.0 collective-permute-start.3
  10.3 0.6 collective-permute-start.2
  11.0 0.8 row_table.1
  11.8 1.6 %collective-permute-start.5 = (s32[8,128]{1,0:T(8,128)S(1)}, s32[8,128]{1,0:T(8,128)S(1)}, u32[]{:S(2)}, u32[]{:S(2)}) collective-permute-start(s32[8,128]{1,0:T(8,128)S(1)} %get-tuple-element.25), channel_id=1, source_target_pairs={{0,16},{16,0},{1,17},{17,1},{2,18},{18,2},{3,19},{19,3},{4,20},{20... | collective-permute-start | bytes 12296 | tf_op jit(solution)/shard_map/ppermute | solution.py:20
  13.4 5.2 %pack_rows.1 = (bf16[256,1024]{1,0:T(8,128)(2,1)S(1)}, bf16[256,1024]{1,0:T(8,128)(2,1)S(1)}, bf16[256,1024]{1,0:T(8,128)(2,1)}, bf16[256,1024]{1,0:T(8,128)(2,1...) custom-call(s32[32,128]{1,0:T(8,128)S(1)} %bitcast.9, bf16[1024,2048]{1,0:T(8,128)(2,1)} %train_ref.1), custom_call_target="tpu_custom_call" | custom-call | flops 1 | bytes 1 | tf_op jit(solution)/shard_map/pack_rows/pallas_call | solution.py:169
  18.6 2.9 %collective-permute-done.3 = bf16[1,64,1024]{2,1,0:T(8,128)(2,1)S(1)} collective-permute-done((bf16[1,64,1024]{2,1,0:T(8,128)(2,1)S(1)}, bf16[1,64,1024]{2,1,0:T(8,128)(2,1)S(1)}, u32[]{:S(2)}, u32[]{:S(2)}) %collective-permute-start.3) | collective-permute-done | bytes 131104 | tf_op jit(solution)/shard_map/ppermute | solution.py:20
  21.6 0.1 pad_maximum_fusion.2.refs_0_
  21.7 1.6 %collective-permute-start.6 = (bf16[4,64,1024]{2,1,0:T(8,128)(2,1)S(1)}, bf16[4,64,1024]{2,1,0:T(8,128)(2,1)S(1)}, u32[]{:S(2)}, u32[]{:S(2)}) collective-permute-start(bf16[4,64,1024]{2,1,0:T(8,128)(2,1)S(1)} %after.4.refs_0_), channel_id=1, source_target_pairs={{0,16},{16,0},{1,17},{17,1},{2,18},{18,2},{3,19},{19,3},{4,20},{20... | collective-permute-start | bytes 1572872 | tf_op jit(solution)/shard_map/ppermute | solution.py:20
  23.3 2.5 %collective-permute-start.7 = (bf16[128,1024]{1,0:T(8,128)(2,1)S(1)}, bf16[128,1024]{1,0:T(8,128)(2,1)S(1)}, u32[]{:S(2)}, u32[]{:S(2)}) collective-permute-start(bf16[128,1024]{1,0:T(8,128)(2,1)S(1)} %get-tuple-element.26.refs_5_), channel_id=1, source_target_pairs={{0,8},{4,12},{8,0},{12,4},{1,9},{5,13},{9,1},{13,5},{2,10},{6,14},... | collective-permute-start | bytes 786440 | tf_op jit(solution)/shard_map/ppermute | solution.py:24
  25.7 0.6 slice.37
  26.9 0.0 copy-start.9
  27.0 0.0 copy-start.10
  27.0 1.1 conditional.1
  27.0 1.1 broadcast.5
  28.1 8.8 %collective-permute-done.7.refs_2_.refs_1_.refs_6_ = bf16[128,1024]{1,0:T(8,128)(2,1)S(1)} collective-permute-done((bf16[128,1024]{1,0:T(8,128)(2,1)S(1)}, bf16[128,1024]{1,0:T(8,128)(2,1)S(1)}, u32[]{:S(2)}, u32[]{:S(2)}) %collective-permute-start.7) | collective-permute-done | bytes 262176 | tf_op jit(solution)/shard_map/ppermute | solution.py:24
  36.9 0.0 collective-permute-done.6.refs_1_
  36.9 1.0 join_queries.1.chosen_ref
  37.9 4.6 %partial_weights.4 = f32[1024,512]{1,0:T(8,128)} custom-call(s32[1]{0:T(128)} %bitcast.6.block_ref, bf16[4096,1024]{1,0:T(8,128)(2,1)} %bitcast.10, bf16[1024,512]{1,0:T(8,128)(2,1)S(1)} %join_queries.1.chosen_ref), custom_call_target="tpu_custom_call" | custom-call | flops 1 | bytes 1 | tf_op jit(solution)/shard_map/partial_weights/pallas_call | solution.py:197
  42.5 0.0 collective-permute-start.9
  42.5 4.5 %collective-permute-done.9.rest_0_ = f32[1024,512]{1,0:T(8,128)} collective-permute-done((f32[1024,512]{1,0:T(8,128)}, f32[1024,512]{1,0:T(8,128)}, u32[]{:S(2)}, u32[]{:S(2)}) %collective-permute-start.9) | collective-permute-done | bytes 2097184 | tf_op jit(solution)/shard_map/ppermute | solution.py:20
  47.0 3.8 %partial_weights.5.rest_1_.refs_1_ = bf16[1024,512]{1,0:T(8,128)(2,1)S(1)} custom-call(s32[1]{0:T(128)} %bitcast.5.block_ref, bf16[4096,1024]{1,0:T(8,128)(2,1)} %bitcast.11, bf16[1024,512]{1,0:T(8,128)(2,1)S(1)} %join_queries.1.chosen_ref, f32[1024,512]{1,0:T(8,128)} %collective-permute-done.9.rest_0_), custom_call_target="tpu_custom_call" | custom-call | flops 1 | bytes 1 | tf_op jit(solution)/shard_map/partial_weights/pallas_call | solution.py:197
  50.8 7.8 %collective-permute-done.8.rest_0_.refs_3_ = bf16[256,1024]{1,0:T(8,128)(2,1)S(1)} collective-permute-done((bf16[256,1024]{1,0:T(8,128)(2,1)S(1)}, bf16[256,1024]{1,0:T(8,128)(2,1)S(1)}, u32[]{:S(2)}, u32[]{:S(2)}) %collective-permute-start.8) | collective-permute-done | bytes 524320 | tf_op jit(solution)/shard_map/ppermute | solution.py:20
  58.6 4.6 %partial_weights.6 = f32[1024,512]{1,0:T(8,128)} custom-call(s32[1]{0:T(128)} %bitcast.4.block_ref, bf16[4096,1024]{1,0:T(8,128)(2,1)} %bitcast.12, bf16[1024,512]{1,0:T(8,128)(2,1)S(1)} %join_queries.1.chosen_ref, bf16[256,1024]{1,0:T(8,128)(2,1)S(1)} %collective-permute-done.8.rest_0_.refs_3_, bf16[1024,512]{1,0:T(8,128)(2,1)S(1)} %partial_weights.5.rest_1_.refs_1_), custom_call_target="tpu_custom_call" | custom-call | flops 1 | bytes 1 | tf_op jit(solution)/shard_map/partial_weights/pallas_call | solution.py:197
  63.3 1.5 %collective-permute-start.11 = (bf16[1024,512]{1,0:T(8,128)(2,1)S(1)}, bf16[1024,512]{1,0:T(8,128)(2,1)}, u32[]{:S(2)}, u32[]{:S(2)}) collective-permute-start(bf16[1024,512]{1,0:T(8,128)(2,1)S(1)} %partial_weights.5.rest_1_.refs_1_), channel_id=1, source_target_pairs={{0,2},{2,0},{1,3},{3,1},{4,6},{6,4},{5,7},{7,5},{8,10},{10,8},{9,1... | collective-permute-start | bytes 3145736 | tf_op jit(solution)/shard_map/ppermute | solution.py:20
  64.8 0.8 pad_maximum_fusion.3
  65.6 0.1 collective-permute-start.12
  65.7 1.3 fusion
  66.9 21.4 %collective-permute-done.13 = bf16[256,1024]{1,0:T(8,128)(2,1)} collective-permute-done((bf16[256,1024]{1,0:T(8,128)(2,1)}, bf16[256,1024]{1,0:T(8,128)(2,1)}, u32[]{:S(2)}, u32[]{:S(2)}) %collective-permute-start.13) | collective-permute-done | bytes 524320 | tf_op jit(solution)/shard_map/ppermute | solution.py:24
  88.3 1.1 fusion.1
  89.4 3.9 %partial_weights.7.refs_0_ = f32[1024,512]{1,0:T(8,128)S(1)} custom-call(s32[1]{0:T(128)} %bitcast.1.block_ref, bf16[4096,1024]{1,0:T(8,128)(2,1)} %bitcast.13, bf16[1024,512]{1,0:T(8,128)(2,1)S(1)} %join_queries.1.chosen_ref, f32[1024,512]{1,0:T(8,128)} %collective-permute-done.10.rest_0_), custom_call_target="tpu_custom_call" | custom-call | flops 1 | bytes 1 | tf_op jit(solution)/shard_map/partial_weights/pallas_call | solution.py:197
  93.3 1.3 %copy-done = f32[1024,512]{1,0:T(8,128)} copy-done((f32[1024,512]{1,0:T(8,128)}, f32[1024,512]{1,0:T(8,128)S(1)}, u32[]{:S(2)}) %copy-start) | copy-done | bytes 2097176
  94.7 6.7 %early_scores.1 = (bf16[1024,512]{1,0:T(8,128)(2,1)}, bf16[1024,512]{1,0:T(8,128)(2,1)}, f32[1024,256]{1,0:T(8,128)}, f32[1024,256]{1,0:T(8,128)}) custom-call(s32[4,4]{1,0:T(4,128)S(1)} %get-tuple-element.23.table_ref, f32[1024,512]{1,0:T(8,128)} %copy-done, bf16[1024,512]{1,0:T(8,128)(2,1)} %collective-permute-done.11.refs_1_, ...), custom_call_target="tpu_custom_call" | custom-call | flops 1 | bytes 1 | tf_op jit(solution)/shard_map/early_scores/pallas_call | solution.py:337
  101.4 2.2 %collective-permute-start.16 = (bf16[256,1024]{1,0:T(8,128)(2,1)}, bf16[256,1024]{1,0:T(8,128)(2,1)S(1)}, u32[]{:S(2)}, u32[]{:S(2)}) collective-permute-start(bf16[256,1024]{1,0:T(8,128)(2,1)} %after.7), channel_id=1, source_target_pairs={{0,12},{4,0},{8,4},{12,8},{1,13},{5,1},{9,5},{13,9},{2,14},{6,2},{... | collective-permute-start | bytes 1572872 | tf_op jit(solution)/shard_map/ppermute | solution.py:20
  103.7 0.7 collective-permute-done.14
  104.4 2.6 %add.57 = f32[1024,256]{1,0:T(8,128)} add(f32[1024,256]{1,0:T(8,128)} %get-tuple-element.30, f32[1024,256]{1,0:T(8,128)} %collective-permute-done.14) | non-fusion elementwise | flops 262144 | bytes 3145728 | tf_op jit(solution)/shard_map/add | solution.py:489
  107.1 1.1 dynamic-slice_convert_fusion.rest_0_
  108.1 7.8 %collective-permute-done.16.last_ref = bf16[256,1024]{1,0:T(8,128)(2,1)S(1)} collective-permute-done((bf16[256,1024]{1,0:T(8,128)(2,1)}, bf16[256,1024]{1,0:T(8,128)(2,1)S(1)}, u32[]{:S(2)}, u32[]{:S(2)}) %collective-permute-start.16) | collective-permute-done | bytes 524320 | tf_op jit(solution)/shard_map/ppermute | solution.py:20
  116.0 0.7 late_scores.1
  116.7 0.1 collective-permute-start.17
  116.8 0.6 collective-permute-start.15
  117.4 1.1 constant_dynamic-slice_fusion.1.refs_0_
  118.5 1.6 %collective-permute-start.18 = (bf16[256,128]{1,0:T(8,128)(2,1)S(1)}, bf16[256,128]{1,0:T(8,128)(2,1)S(1)}, u32[]{:S(2)}, u32[]{:S(2)}) collective-permute-start(bf16[256,128]{1,0:T(8,128)(2,1)S(1)} %dynamic-slice_convert_fusion.1), channel_id=1, source_target_pairs={{0,2},{2,0},{1,3},{3,1},{4,6},{6,4},{5,7},{7,5},{8,10},{10,8},{9,1... | collective-permute-start | bytes 196616 | tf_op jit(solution)/shard_map/ppermute | solution.py:20
  120.1 5.9 %collective-permute-done.15.refs_1_ = bf16[1024,128]{1,0:T(8,128)(2,1)S(1)} collective-permute-done((bf16[1024,128]{1,0:T(8,128)(2,1)S(1)}, bf16[1024,128]{1,0:T(8,128)(2,1)S(1)}, u32[]{:S(2)}, u32[]{:S(2)}) %collective-permute-start.15) | collective-permute-done | bytes 262176 | tf_op jit(solution)/shard_map/ppermute | solution.py:20
  126.0 0.9 collective-permute-done.18.refs_3_
  126.9 1.7 %merge.1 = f32[128,1024]{1,0:T(8,128)} custom-call(s32[4,4]{1,0:T(4,128)S(1)} %get-tuple-element.23.table_ref, f32[1024,128]{1,0:T(8,128)S(1)} %constant_dynamic-slice_fusion.1.refs_0_, bf16[1024,128]{1,0:T(8,128)(2,1)S(1)} %collective-permute-done.15.refs_1_, f32[256,128]{1,0:T(8,128)S(1)} %constant_dynamic-slice_fusion.refs_2_, ...), custom_call_target="tpu_custom_call" | custom-call | flops 1 | bytes 1 | tf_op jit(solution)/shard_map/merge/pallas_call | solution.py:397
  (38 shorter events, 0.1 us)
Async XLA Ops:
  0.0 11.0 %copy-start.8 = (s32[4096]{0:T(1024)S(1)}, s32[4096]{0:T(1024)}, u32[]{:S(2)}) copy-start(s32[4096]{0:T(1024)} %param.9) | copy-start | bytes 49156
  5.2 13.4 %collective-permute-start.4 = (bf16[1,64,1024]{2,1,0:T(8,128)(2,1)S(1)}, bf16[1,64,1024]{2,1,0:T(8,128)(2,1)S(1)}, u32[]{:S(2)}, u32[]{:S(2)}) collective-permute-start(bf16[1,64,1024]{2,1,0:T(8,128)(2,1)S(1)} %get-tuple-element.44), channel_id=1, source_target_pairs={{0,12},{4,0},{8,4},{12,8},{1,13},{5,1},{9,5},{13,9},{2,14},{6,2},{... | collective-permute-start | bytes 393224 | tf_op jit(solution)/shard_map/ppermute | solution.py:20
  10.3 11.2 %collective-permute-start.3 = (bf16[1,64,1024]{2,1,0:T(8,128)(2,1)S(1)}, bf16[1,64,1024]{2,1,0:T(8,128)(2,1)S(1)}, u32[]{:S(2)}, u32[]{:S(2)}) collective-permute-start(bf16[1,64,1024]{2,1,0:T(8,128)(2,1)S(1)} %get-tuple-element.45), channel_id=1, source_target_pairs={{0,8},{4,12},{8,0},{12,4},{1,9},{5,13},{9,1},{13,5},{2,10},{6,14},... | collective-permute-start | bytes 393224 | tf_op jit(solution)/shard_map/ppermute | solution.py:20
  10.3 11.2 %collective-permute-start.2 = (bf16[1,64,1024]{2,1,0:T(8,128)(2,1)S(1)}, bf16[1,64,1024]{2,1,0:T(8,128)(2,1)S(1)}, u32[]{:S(2)}, u32[]{:S(2)}) collective-permute-start(bf16[1,64,1024]{2,1,0:T(8,128)(2,1)S(1)} %get-tuple-element.46), channel_id=1, source_target_pairs={{0,4},{4,8},{8,12},{12,0},{1,5},{5,9},{9,13},{13,1},{2,6},{6,10},{... | collective-permute-start | bytes 393224 | tf_op jit(solution)/shard_map/ppermute | solution.py:20
  11.8 6.8 %collective-permute-start.5 = (s32[8,128]{1,0:T(8,128)S(1)}, s32[8,128]{1,0:T(8,128)S(1)}, u32[]{:S(2)}, u32[]{:S(2)}) collective-permute-start(s32[8,128]{1,0:T(8,128)S(1)} %get-tuple-element.25), channel_id=1, source_target_pairs={{0,16},{16,0},{1,17},{17,1},{2,18},{18,2},{3,19},{19,3},{4,20},{20... | collective-permute-start | bytes 12296 | tf_op jit(solution)/shard_map/ppermute | solution.py:20
  18.6 4.6 %copy-start.6 = (bf16[256,1024]{1,0:T(8,128)(2,1)}, bf16[256,1024]{1,0:T(8,128)(2,1)S(1)}, u32[]{:S(2)}) copy-start(bf16[256,1024]{1,0:T(8,128)(2,1)S(1)} %get-tuple-element.28.refs_2_) | copy-start | bytes 1572868
  18.6 8.4 %copy-start.1 = (bf16[128,1024]{1,0:T(8,128)(2,1)}, bf16[128,1024]{1,0:T(8,128)(2,1)S(1)}, u32[]{:S(2)}) copy-start(bf16[128,1024]{1,0:T(8,128)(2,1)S(1)} %get-tuple-element.26.refs_5_) | copy-start | bytes 786436
  21.7 15.2 %collective-permute-start.6 = (bf16[4,64,1024]{2,1,0:T(8,128)(2,1)S(1)}, bf16[4,64,1024]{2,1,0:T(8,128)(2,1)S(1)}, u32[]{:S(2)}, u32[]{:S(2)}) collective-permute-start(bf16[4,64,1024]{2,1,0:T(8,128)(2,1)S(1)} %after.4.refs_0_), channel_id=1, source_target_pairs={{0,16},{16,0},{1,17},{17,1},{2,18},{18,2},{3,19},{19,3},{4,20},{20... | collective-permute-start | bytes 1572872 | tf_op jit(solution)/shard_map/ppermute | solution.py:20
  23.3 13.6 %collective-permute-start.7 = (bf16[128,1024]{1,0:T(8,128)(2,1)S(1)}, bf16[128,1024]{1,0:T(8,128)(2,1)S(1)}, u32[]{:S(2)}, u32[]{:S(2)}) collective-permute-start(bf16[128,1024]{1,0:T(8,128)(2,1)S(1)} %get-tuple-element.26.refs_5_), channel_id=1, source_target_pairs={{0,8},{4,12},{8,0},{12,4},{1,9},{5,13},{9,1},{13,5},{2,10},{6,14},... | collective-permute-start | bytes 786440 | tf_op jit(solution)/shard_map/ppermute | solution.py:24
  26.9 10.0 %copy-start.9 = (s32[4,4]{1,0:T(4,128)S(1)}, s32[4,4]{1,0:T(4,128)}, u32[]{:S(2)}) copy-start(s32[4,4]{1,0:T(4,128)} %pattern_ref.3) | copy-start | bytes 196
  27.0 9.9 %copy-start.10 = (s32[16]{0:T(128)S(1)}, s32[16]{0:T(128)}, u32[]{:S(2)}) copy-start(s32[16]{0:T(128)} %slot_ref.3) | copy-start | bytes 196
  42.5 4.5 %collective-permute-start.9 = (f32[1024,512]{1,0:T(8,128)}, f32[1024,512]{1,0:T(8,128)}, u32[]{:S(2)}, u32[]{:S(2)}) collective-permute-start(f32[1024,512]{1,0:T(8,128)} %partial_weights.4), channel_id=1, source_target_pairs={{0,1},{1,0},{2,3},{3,2},{4,5},{5,4},{6,7},{7,6},{8,9},{9,8},{10,11... | collective-permute-start | bytes 6291464 | tf_op jit(solution)/shard_map/ppermute | solution.py:20
  42.5 16.1 %collective-permute-start.8 = (bf16[256,1024]{1,0:T(8,128)(2,1)S(1)}, bf16[256,1024]{1,0:T(8,128)(2,1)S(1)}, u32[]{:S(2)}, u32[]{:S(2)}) collective-permute-start(bf16[256,1024]{1,0:T(8,128)(2,1)S(1)} %after.5), channel_id=1, source_target_pairs={{0,4},{4,8},{8,12},{12,0},{1,5},{5,9},{9,13},{13,1},{2,6},{6,10},{... | collective-permute-start | bytes 1572872 | tf_op jit(solution)/shard_map/ppermute | solution.py:20
  58.6 6.1 %copy-start.2 = (bf16[128,1024]{1,0:T(8,128)(2,1)S(1)}, bf16[128,1024]{1,0:T(8,128)(2,1)}, u32[]{:S(2)}) copy-start(bf16[128,1024]{1,0:T(8,128)(2,1)} %copy-done.1) | copy-start | bytes 786436
  63.3 26.1 %collective-permute-start.10 = (f32[1024,512]{1,0:T(8,128)}, f32[1024,512]{1,0:T(8,128)}, u32[]{:S(2)}, u32[]{:S(2)}) collective-permute-start(f32[1024,512]{1,0:T(8,128)} %partial_weights.6), channel_id=1, source_target_pairs={{0,1},{1,0},{2,3},{3,2},{4,5},{5,4},{6,7},{7,6},{8,9},{9,8},{10,11... | collective-permute-start | bytes 6291464 | tf_op jit(solution)/shard_map/ppermute | solution.py:20
  63.3 31.4 %collective-permute-start.11 = (bf16[1024,512]{1,0:T(8,128)(2,1)S(1)}, bf16[1024,512]{1,0:T(8,128)(2,1)}, u32[]{:S(2)}, u32[]{:S(2)}) collective-permute-start(bf16[1024,512]{1,0:T(8,128)(2,1)S(1)} %partial_weights.5.rest_1_.refs_1_), channel_id=1, source_target_pairs={{0,2},{2,0},{1,3},{3,1},{4,6},{6,4},{5,7},{7,5},{8,10},{10,8},{9,1... | collective-permute-start | bytes 3145736 | tf_op jit(solution)/shard_map/ppermute | solution.py:20
  65.6 22.7 %collective-permute-start.13 = (bf16[256,1024]{1,0:T(8,128)(2,1)}, bf16[256,1024]{1,0:T(8,128)(2,1)}, u32[]{:S(2)}, u32[]{:S(2)}) collective-permute-start(bf16[256,1024]{1,0:T(8,128)(2,1)} %pad_maximum_fusion.3), channel_id=1, source_target_pairs={{0,4},{4,0},{8,12},{12,8},{1,5},{5,1},{9,13},{13,9},{2,6},{6,2},{1... | collective-permute-start | bytes 1572872 | tf_op jit(solution)/shard_map/ppermute | solution.py:24
  65.6 29.1 %collective-permute-start.12 = (bf16[256,1024]{1,0:T(8,128)(2,1)}, bf16[256,1024]{1,0:T(8,128)(2,1)S(1)}, u32[]{:S(2)}, u32[]{:S(2)}) collective-permute-start(bf16[256,1024]{1,0:T(8,128)(2,1)} %after.6), channel_id=1, source_target_pairs={{0,8},{4,12},{8,0},{12,4},{1,9},{5,13},{9,1},{13,5},{2,10},{6,14},... | collective-permute-start | bytes 1572872 | tf_op jit(solution)/shard_map/ppermute | solution.py:20
  89.4 5.3 %copy-start.3 = (bf16[128,1024]{1,0:T(8,128)(2,1)S(1)}, bf16[128,1024]{1,0:T(8,128)(2,1)}, u32[]{:S(2)}) copy-start(bf16[128,1024]{1,0:T(8,128)(2,1)} %copy-done.1) | copy-start | bytes 786436
  89.4 5.3 %copy-start.7 = (bf16[256,1024]{1,0:T(8,128)(2,1)S(1)}, bf16[256,1024]{1,0:T(8,128)(2,1)}, u32[]{:S(2)}) copy-start(bf16[256,1024]{1,0:T(8,128)(2,1)} %copy-done.6) | copy-start | bytes 1572868
  93.3 1.4 %copy-start = (f32[1024,512]{1,0:T(8,128)}, f32[1024,512]{1,0:T(8,128)S(1)}, u32[]{:S(2)}) copy-start(f32[1024,512]{1,0:T(8,128)S(1)} %partial_weights.7.refs_0_) | copy-start | bytes 6291460
  101.4 3.0 %collective-permute-start.14 = (f32[1024,256]{1,0:T(8,128)}, f32[1024,256]{1,0:T(8,128)}, u32[]{:S(2)}, u32[]{:S(2)}) collective-permute-start(f32[1024,256]{1,0:T(8,128)} %get-tuple-element.31), channel_id=1, source_target_pairs={{0,1},{1,0},{2,3},{3,2},{4,5},{5,4},{6,7},{7,6},{8,9},{9,8},{10,11... | collective-permute-start | bytes 3145736 | tf_op jit(solution)/shard_map/ppermute | solution.py:20
  101.4 14.6 %copy-start.4 = (bf16[1024,512]{1,0:T(8,128)(2,1)S(1)}, bf16[1024,512]{1,0:T(8,128)(2,1)}, u32[]{:S(2)}) copy-start(bf16[1024,512]{1,0:T(8,128)(2,1)} %get-tuple-element.33.high_ref) | copy-start | bytes 3145732
  101.4 14.6 %copy-start.5 = (bf16[1024,512]{1,0:T(8,128)(2,1)S(1)}, bf16[1024,512]{1,0:T(8,128)(2,1)}, u32[]{:S(2)}) copy-start(bf16[1024,512]{1,0:T(8,128)(2,1)} %get-tuple-element.34.low_ref) | copy-start | bytes 3145732
  101.4 14.5 %collective-permute-start.16 = (bf16[256,1024]{1,0:T(8,128)(2,1)}, bf16[256,1024]{1,0:T(8,128)(2,1)S(1)}, u32[]{:S(2)}, u32[]{:S(2)}) collective-permute-start(bf16[256,1024]{1,0:T(8,128)(2,1)} %after.7), channel_id=1, source_target_pairs={{0,12},{4,0},{8,4},{12,8},{1,13},{5,1},{9,5},{13,9},{2,14},{6,2},{... | collective-permute-start | bytes 1572872 | tf_op jit(solution)/shard_map/ppermute | solution.py:20
  116.7 1.8 %collective-permute-start.17 = (f32[256,256]{1,0:T(8,128)S(1)}, f32[256,256]{1,0:T(8,128)S(1)}, u32[]{:S(2)}, u32[]{:S(2)}) collective-permute-start(f32[256,256]{1,0:T(8,128)S(1)} %get-tuple-element.36), channel_id=1, source_target_pairs={{0,1},{1,0},{2,3},{3,2},{4,5},{5,4},{6,7},{7,6},{8,9},{9,8},{10,11... | collective-permute-start | bytes 786440 | tf_op jit(solution)/shard_map/ppermute | solution.py:20
  116.8 9.2 %collective-permute-start.15 = (bf16[1024,128]{1,0:T(8,128)(2,1)S(1)}, bf16[1024,128]{1,0:T(8,128)(2,1)S(1)}, u32[]{:S(2)}, u32[]{:S(2)}) collective-permute-start(bf16[1024,128]{1,0:T(8,128)(2,1)S(1)} %dynamic-slice_convert_fusion.rest_0_), channel_id=1, source_target_pairs={{0,2},{2,0},{1,3},{3,1},{4,6},{6,4},{5,7},{7,5},{8,10},{10,8},{9,1... | collective-permute-start | bytes 786440 | tf_op jit(solution)/shard_map/ppermute | solution.py:20
  118.5 8.4 %collective-permute-start.18 = (bf16[256,128]{1,0:T(8,128)(2,1)S(1)}, bf16[256,128]{1,0:T(8,128)(2,1)S(1)}, u32[]{:S(2)}, u32[]{:S(2)}) collective-permute-start(bf16[256,128]{1,0:T(8,128)(2,1)S(1)} %dynamic-slice_convert_fusion.1), channel_id=1, source_target_pairs={{0,2},{2,0},{1,3},{3,1},{4,6},{6,4},{5,7},{7,5},{8,10},{10,8},{9,1... | collective-permute-start | bytes 196616 | tf_op jit(solution)/shard_map/ppermute | solution.py:20

commit v6 on v5

--- a/solution.py
+++ b/solution.py
@@ -53,27 +53,29 @@
     n_cluster, n_list = pattern.shape
     part = block_rows // n_group
 
-    def place(t, pattern_ref, slot_ref):
-        me = lax.axis_index("shard")
-        found = jnp.int32(0)
-        for k in range(n_list):
-            slot = slot_ref[pattern_ref[lax.rem(me + t, jnp.int32(n_cluster)), k]]
-            hit = (lax.div(slot, jnp.int32(local_blocks)) == me).astype(I32)
-            found = found + hit * lax.rem(slot, jnp.int32(local_blocks))
-        return found, lax.axis_index("groups"), 0
-
-    def kernel(pattern_ref, slot_ref, in_ref, out_ref):
-        out_ref[...] = in_ref[...]
-
-    return pl.pallas_call(
-        kernel,
-        grid_spec=pltpu.PrefetchScalarGridSpec(
-            num_scalar_prefetch=2,
-            grid=(n_cluster,),
-            in_specs=[pl.BlockSpec((1, part, width), place)],
-            out_specs=pl.BlockSpec((1, part, width), lambda t, p, s: (t, 0, 0)),
-        ),
-        out_shape=jax.ShapeDtypeStruct((n_cluster, part, width), BF16),
+    def kernel(pattern_ref, slot_ref, in_ref, *rest):
+        outs, sem = rest[:-1], rest[-1]
+        me, group = lax.axis_index("shard"), lax.axis_index("groups")
+        copies = []
+        for t, out in enumerate(outs):
+            target = lax.rem(me + t, jnp.int32(n_cluster))
+            found = jnp.int32(0)
+            for k in range(n_list):
+                slot = slot_ref[pattern_ref[target, k]]
+                hit = (lax.div(slot, jnp.int32(local_blocks)) == me).astype(I32)
+                found = found + hit * lax.rem(slot, jnp.int32(local_blocks))
+            rows = pl.ds(pl.multiple_of(group * part, part), part)
+            copies.append(pltpu.make_async_copy(in_ref.at[found, rows], out.at[0], sem.at[t]))
+            copies[-1].start()
+        for copy in copies:
+            copy.wait()
+
+    return pl.pallas_call(
+        kernel,
+        in_specs=[SMEM, SMEM, ANY],
+        out_specs=[VMEM] * n_cluster,
+        out_shape=[jax.ShapeDtypeStruct((1, part, width), BF16)] * n_cluster,
+        scratch_shapes=[pltpu.SemaphoreType.DMA((n_cluster,))],
         cost_estimate=cost(0, 4 * n_cluster * part * width),
         compiler_params=FIRST,
         name="pick_queries",
@@ -89,7 +91,7 @@
     unit = min(share, part)
 
     def kernel(pattern_ref, slot_ref, *refs):
-        out_ref, rows_ref = refs[-2:]
+        outs, rows_ref = refs[-1 - n_rep:-1], refs[-1]
         me, group = lax.axis_index("shard"), lax.axis_index("groups")
         for k in range(n_list):
             owner = lax.div(slot_ref[pattern_ref[me, k]], jnp.int32(local_blocks))
@@ -102,18 +104,49 @@
                     goal = lax.rem(chunk, jnp.int32(n_rep)) * n_feat + lax.div(chunk, jnp.int32(n_rep))
                     goal = goal * share + lax.rem(first, jnp.int32(share))
                     rows_ref[pl.ds(pl.multiple_of(goal, unit), unit), :] = refs[d][hops, u * unit:(u + 1) * unit, :]
-        out_ref[...] = rows_ref[...].T
+        half = total // n_rep
+        for r in range(n_rep):
+            @pl.when(lax.axis_index("rep") == r)
+            def _():
+                for d, out in enumerate(outs):
+                    at = ((r + d) % n_rep) * half
+                    out[...] = rows_ref[at:at + half, :].T
 
     return pl.pallas_call(
         kernel,
         in_specs=[SMEM, SMEM] + [VMEM] * n_group + [ANY] * len(others),
-        out_specs=VMEM,
-        out_shape=jax.ShapeDtypeStruct((width, total), BF16),
+        out_specs=[VMEM] * n_rep,
+        out_shape=[jax.ShapeDtypeStruct((width, total // n_rep), BF16)] * n_rep,
         scratch_shapes=[pltpu.VMEM((total, width), BF16)],
         cost_estimate=cost(0, 4 * total * width),
         compiler_params=PARAMS,
         name="join_queries",
     )(pattern, block_slot, *parts, *others)
+
+
+def select(goal_ref, train_ref, base, size):
+    tile = 128 if size % 128 == 0 else size
+    found = []
+    for at in range(0, size, tile):
+        index = lax.broadcasted_iota(I32, (tile, LANES), 0) + (base + at)
+        pick = [(index == goal_ref[a:a + 1, :]).astype(F32).astype(BF16) for a in range(goal_ref.shape[0])]
+        found.append(dot(jnp.concatenate(pick, axis=1), train_ref[...]).astype(BF16))
+    return jnp.concatenate(found)
+
+
+def own_rows(goal, train, bulk):
+    def kernel(goal_ref, train_ref, out_ref):
+        out_ref[...] = select(goal_ref, train_ref, lax.axis_index("shard") * bulk, bulk)
+
+    return pl.pallas_call(
+        kernel,
+        in_specs=[VMEM] * 2,
+        out_specs=VMEM,
+        out_shape=jax.ShapeDtypeStruct((bulk, train.shape[1]), BF16),
+        cost_estimate=cost(2 * bulk * train.size, 2 * train.size),
+        compiler_params=PARAMS,
+        name="own_rows",
+    )(goal, train)
 
 
 def pack_rows(train, ids, columns, bulk, extra, cuts):
@@ -151,12 +184,7 @@
         goal_ref[...] = goal.astype(I32)
 
         def fill(out, base):
-            size = out.shape[0]
-            tile = 128 if size % 128 == 0 else size
-            for at in range(0, size, tile):
-                index = lax.broadcasted_iota(I32, (tile, LANES), 0) + (base + at)
-                pick = [(index == goal_ref[a:a + 1, :]).astype(F32).astype(BF16) for a in range(lines)]
-                out[at:at + tile, :] = dot(jnp.concatenate(pick, axis=1), train_ref[...]).astype(BF16)
+            out[...] = select(goal_ref, train_ref, base, out.shape[0])
 
         for out, (hops, first, _) in zip(outs, cuts):
             fill(out, lax.rem(me + hops, jnp.int32(n_shard)) * bulk + first)
@@ -165,6 +193,7 @@
 
     shapes = [jax.ShapeDtypeStruct((n, columns), BF16) for _, _, n in cuts]
     shapes += [jax.ShapeDtypeStruct((extra, columns), BF16)] * (2 if extra else 0)
+    shapes += [jax.ShapeDtypeStruct((lines, LANES), I32)]
     packed = n_shard * bulk + 2 * extra
     return pl.pallas_call(
         kernel,
@@ -175,43 +204,39 @@
         ],
         out_specs=[VMEM] * len(shapes),
         out_shape=shapes,
-        scratch_shapes=[pltpu.VMEM((lines, LANES), I32)],
         cost_estimate=cost(2 * packed * rows * columns, 2 * (rows + packed) * columns),
         compiler_params=PARAMS,
         name="pack_rows",
     )(ids, train)
 
 
-def partial_weights(matrix, chosen, block, depth, dtype, *addends, others=()):
-    width, total = chosen.shape
-    tile = 256 if depth % 256 == 0 else depth
+def partial_weights(matrices, queries, block, depth, dtype, *others):
+    width, total = queries[0].shape
+    tile = 512 if depth % 512 == 0 else depth
     steps = depth // tile
-
-    def kernel(block_ref, matrix_ref, chosen_ref, *rest):
-        value = dot(matrix_ref[...], chosen_ref[...])
-        for ref in rest[:len(addends)]:
-            value = value + ref[...]
-        rest[-1][...] = value.astype(dtype)
-
-    rows = pl.BlockSpec((tile, total), lambda i, b: (i, 0))
+    n = len(matrices)
+
+    def kernel(block_ref, *refs):
+        value = dot(refs[0][...], refs[n][...])
+        for j in range(1, n):
+            value = value + dot(refs[j][...], refs[n + j][...])
+        refs[-1][...] = value.astype(dtype)
+
     return pl.pallas_call(
         kernel,
         grid_spec=pltpu.PrefetchScalarGridSpec(
             num_scalar_prefetch=1,
             grid=(steps,),
-            in_specs=[
-                pl.BlockSpec((tile, width), lambda i, b: (b[0] * steps + i, 0)),
-                pl.BlockSpec((width, total), lambda i, b: (0, 0)),
-            ]
-            + [rows] * len(addends)
+            in_specs=[pl.BlockSpec((tile, width), lambda i, b: (b[0] * steps + i, 0))] * n
+            + [pl.BlockSpec((width, total), lambda i, b: (0, 0))] * n
             + [ANY] * len(others),
-            out_specs=rows,
+            out_specs=pl.BlockSpec((tile, total), lambda i, b: (i, 0)),
         ),
         out_shape=jax.ShapeDtypeStruct((depth, total), dtype),
-        cost_estimate=cost(2 * depth * width * total, 2 * depth * width + 4 * depth * total),
+        cost_estimate=cost(2 * n * depth * width * total, 2 * n * depth * width + 4 * depth * total),
         compiler_params=PARAMS,
         name="partial_weights",
-    )(jnp.reshape(block, (1,)).astype(I32), matrix, chosen, *addends, *others)
+    )(jnp.reshape(block, (1,)).astype(I32), *matrices, *queries, *others)
 
 
 def row_table(ids, lines, bulk, extra):
@@ -273,30 +298,30 @@
     acc[pl.ds(first, tiles + 1)] = pieces
 
 
-def give(value, outs, rep, half):
-    n_rep = len(outs)
-    for r in range(n_rep):
-        @pl.when(rep == r)
-        def _():
-            for d, out in enumerate(outs):
-                at = ((r + d) % n_rep) * half
-                out[...] = value(at)
-
-
-def early_scores(own, others, pieces, firsts, seconds, table, rows, n_rep, n_shard, bulk):
+def score(high_ref, low_ref, parts, rep):
+    total = None
+    for d, x in enumerate(parts):
+        depth = x.shape[1]
+        block = pl.ds(pl.multiple_of(lax.rem(rep + (len(parts) - d), jnp.int32(len(parts))) * depth, depth), depth)
+        value = dot(x, high_ref[block, :]) + dot(x, low_ref[block, :])
+        total = value if total is None else total + value
+    return total.reshape(total.shape[0] // 8, 8, total.shape[1])
+
+
+def early_scores(own, others, mine, pieces, firsts, seconds, table, rows, n_rep, n_shard, bulk, extra):
     depth, width = own.shape
-    half = width // n_rep
+    columns = depth // n_rep
     n_other, n_piece = len(others), len(pieces)
-    extra = firsts[0].shape[0] if firsts else 0
     last_hops = n_shard - 1
 
     def kernel(table_ref, *refs):
         own_ref, refs = refs[0], refs[1:]
         other_refs, refs = refs[:n_other], refs[n_other:]
-        piece_refs, refs = refs[:n_piece], refs[n_piece:]
-        first_refs, refs = refs[:len(firsts)], refs[len(firsts):]
-        second_refs, refs = refs[:len(seconds)], refs[len(seconds):]
-        high_ref, low_ref, outs, (scored, held, acc) = refs[0], refs[1], refs[2:2 + n_rep], refs[2 + n_rep:]
+        mine_ref, refs = refs[0], refs[1:]
+        piece_refs = [refs[j * n_rep:(j + 1) * n_rep] for j in range(n_piece)]
+        refs = refs[n_piece * n_rep:]
+        first_refs, second_refs = refs[:len(firsts)], refs[len(firsts):len(firsts) + len(seconds)]
+        high_ref, low_ref, out_ref, scored, held, acc, sem = refs[len(firsts) + len(seconds):]
         me, rep = lax.axis_index("shard"), lax.axis_index("rep")
         weight = own_ref[...]
         for ref in other_refs:
@@ -305,12 +330,10 @@
         high_ref[...] = high
         low_ref[...] = (weight - high.astype(F32)).astype(BF16)
 
-        def score(x):
-            y = dot(x, high_ref[...]) + dot(x, low_ref[...])
-            return y.reshape(x.shape[0] // 8, 8, width)
-
-        for hops, ref in enumerate(piece_refs):
-            scored[lax.rem(me + (n_shard - hops), jnp.int32(n_shard))] = score(ref[...])
+        scored[me] = score(high_ref, low_ref, [mine_ref[...]], jnp.int32(0))
+        for j, parts in enumerate(piece_refs):
+            source = lax.rem(me + (n_shard - 1 - j), jnp.int32(n_shard))
+            scored[source] = score(high_ref, low_ref, [p[...] for p in parts], rep)
         last = lax.rem(me + (n_shard - last_hops), jnp.int32(n_shard))
         for s in range(n_shard):
             start = table_ref[s, 0]
@@ -323,55 +346,57 @@
                 @pl.when(table_ref[s, 3] > 0)
                 def _():
                     apart = jnp.bitwise_xor(me, s)
-                    for v in range(n_shard):
-                        @pl.when(apart == v)
-                        def _():
-                            index = (v & 1) * 2 + v // 2
-                            held[:extra, :] = first_refs[index][...]
-                            held[extra:2 * extra, :] = second_refs[index][...]
-                    x = held[pl.ds(pl.multiple_of(table_ref[s, 2] * 16, 16), extra), :]
-                    put(acc, score(x), start + table_ref[s, 1])
-        give(lambda at: acc[:rows // 8, :, at:at + half].reshape(rows, half), outs, rep, half)
+                    index = jnp.bitwise_and(apart, 1) * 2 + lax.div(apart, jnp.int32(2))
+                    rows_in = pl.ds(pl.multiple_of(index * extra, extra), extra)
+                    copies = []
+                    for j, ref in enumerate([*first_refs, *second_refs]):
+                        r, d = j // n_rep, j % n_rep
+                        goal = held.at[d, r * extra:(r + 1) * extra]
+                        copies.append(pltpu.make_async_copy(ref.at[rows_in], goal, sem.at[j]))
+                    for copy in copies:
+                        copy.start()
+                    for copy in copies:
+                        copy.wait()
+                    some = pl.ds(pl.multiple_of(table_ref[s, 2] * 16, 16), extra)
+                    x = [held[d, some, :] for d in range(n_rep)]
+                    put(acc, score(high_ref, low_ref, x, rep), start + table_ref[s, 1])
+        out_ref[...] = acc[:rows // 8].reshape(rows, width)
 
     count = n_shard * bulk
     return pl.pallas_call(
         kernel,
-        in_specs=[SMEM] + [VMEM] * (1 + n_other + n_piece + len(firsts) + len(seconds)),
-        out_specs=[VMEM] * (2 + n_rep),
-        out_shape=[jax.ShapeDtypeStruct((depth, width), BF16)] * 2
-        + [jax.ShapeDtypeStruct((rows, half), F32)] * n_rep,
+        in_specs=[SMEM] + [VMEM] * (2 + n_other + n_rep * n_piece) + [ANY] * (len(firsts) + len(seconds)),
+        out_specs=[VMEM] * 3,
+        out_shape=[jax.ShapeDtypeStruct((depth, width), BF16)] * 2 + [jax.ShapeDtypeStruct((rows, width), F32)],
         scratch_shapes=[
             pltpu.VMEM((n_shard, bulk // 8, 8, width), F32),
-            pltpu.VMEM((3 * extra + 16, depth), BF16),
+            pltpu.VMEM((n_rep, 3 * extra + 16, columns), BF16),
             pltpu.VMEM(((rows + bulk + extra) // 8 + 2, 8, width), F32),
+            pltpu.SemaphoreType.DMA((2 * n_rep,)),
         ],
         cost_estimate=cost(4 * count * depth * width, 10 * depth * width + count * (2 * depth + 4 * width)),
         compiler_params=PARAMS,
         name="early_scores",
-    )(table, own, *others, *pieces, *firsts, *seconds)
-
-
-def late_scores(last, high, low, n_rep, *others):
-    rows = last.shape[0]
+    )(table, own, *others, mine, *[p for parts in pieces for p in parts], *firsts, *seconds)
+
+
+def late_scores(parts, high, low):
+    rows = parts[0].shape[0]
     width = high.shape[1]
-    half = width // n_rep
-
-    def kernel(last_ref, high_ref, low_ref, *rest):
-        outs, late = rest[len(others):-1], rest[-1]
-        x = last_ref[...]
-        late[...] = dot(x, high_ref[...]) + dot(x, low_ref[...])
-        give(lambda at: late[:, at:at + half], outs, lax.axis_index("rep"), half)
-
-    return pl.pallas_call(
-        kernel,
-        in_specs=[VMEM] * 3 + [ANY] * len(others),
-        out_specs=[VMEM] * n_rep,
-        out_shape=[jax.ShapeDtypeStruct((rows, half), F32)] * n_rep,
-        scratch_shapes=[pltpu.VMEM((rows, width), F32)],
-        cost_estimate=cost(4 * rows * high.shape[0] * width, 8 * rows * width),
+
+    def kernel(high_ref, low_ref, *refs):
+        y = score(high_ref, low_ref, [ref[...] for ref in refs[:-1]], lax.axis_index("rep"))
+        refs[-1][...] = y.reshape(rows, width)
+
+    return pl.pallas_call(
+        kernel,
+        in_specs=[VMEM] * (2 + len(parts)),
+        out_specs=VMEM,
+        out_shape=jax.ShapeDtypeStruct((rows, width), F32),
+        cost_estimate=cost(4 * rows * high.size, 8 * rows * width),
         compiler_params=PARAMS,
         name="late_scores",
-    )(last, high, low, *others)
+    )(high, low, *parts)
 
 
 def merge(table, early, late, n_shard):
@@ -418,17 +443,19 @@
     bulk = base if extra else base + base // 2
     ids = cluster_ids.reshape(-1, LANES)
 
-    me = lax.axis_index("shard")
+    last_hops = n_shard - 1
+
+    def with_rep(x):
+        return [x] + [shift(x, "rep", n_rep, d) for d in range(1, n_rep)]
+
+    matrices = with_rep(precond[0])
+
     picked = pick_queries(query_store, block_slot, pattern, n_group)
-    pieces = [picked[:1]]
-    for d in range(1, n_shard):
-        pieces.append(shift(picked[d:d + 1], "shard", n_shard, d))
-
-    cuts = [(d, 0, bulk) for d in range(n_shard)]
-    packed = pack_rows(train, ids, columns, bulk, extra, cuts)
+    pieces = [picked[0]] + [shift(picked[d], "shard", n_shard, d) for d in range(1, n_shard)]
+
+    *packed, goal = pack_rows(train, ids, columns, bulk, extra, [(d, 0, bulk) for d in range(1, n_shard)])
+    sent = dict(zip(range(1, n_shard), packed))
     table, flag = row_table(ids, lines, bulk, extra)
-    here = {0: packed[0]}
-    last_hops = n_shard - 1
 
     def swap_far(x):
         return jnp.concatenate([x, swap(x, "shard", n_shard, 2)])
@@ -436,70 +463,54 @@
     def swap_near(x):
         return jnp.concatenate([x, swap(x, "shard", n_shard, 1)])
 
-    before_join = []
+    mine = own_rows(goal, train, bulk)
+    before_join, firsts, seconds = [mine], [], []
     if extra:
         for d in range(1, n_group):
             flag = jnp.maximum(flag, shift(flag, "groups", n_group, d))
-        second = lax.cond(
+        seconds = lax.cond(
             flag[0, 0] > 0,
-            lambda x: swap_near(swap_far(x)),
-            lambda x: jnp.zeros((n_shard * extra, columns), BF16),
+            lambda x: with_rep(swap_near(swap_far(x))),
+            lambda x: [jnp.zeros((n_shard * extra, columns), BF16)] * n_rep,
             packed[-1],
         )
         far = swap(packed[-2], "shard", n_shard, 2)
-        before_join = [far, second]
-
-    arrived = after(jnp.concatenate(pieces), packed[1], flag)
+        before_join = [far, mine, *seconds]
+        firsts = with_rep(swap_near(jnp.concatenate([packed[-2], far])))
+
+    arrived = after(jnp.concatenate(pieces), sent[1], flag)
     parts = [arrived] + [shift(arrived, "groups", n_group, d) for d in range(1, n_group)]
     chosen = join_queries(parts, block_slot, pattern, query_store.shape[0], n_feat, n_rep, *before_join)
-    here[1] = shift(after(packed[1], *before_join[:1]), "shard", n_shard, 1)
-
-    matrix = precond[0]
-
-    def weights(f, r, dtype, *addends, others=()):
-        return partial_weights(matrix, chosen, f * n_rep + r, columns, dtype, *addends, others=others)
-
-    def away(f, others=()):
-        return [
-            shift(weights(f, (rep + d) % n_rep, F32, others=others), "rep", n_rep, d) for d in range(1, n_rep)
-        ]
-
-    targets = [(feat + d) % n_feat for d in range(1, n_feat)]
-    sends = [weights(f, rep, BF16, *x) for f, x in [(f, away(f)) for f in targets]]
+    queries = [chosen[0]] + [shift(chosen[d], "rep", n_rep, d) for d in range(1, n_rep)]
+    here = {1: shift(after(sent[1], *before_join[:1]), "shard", n_shard, 1)}
+
+    def weights(f, dtype, *others):
+        return partial_weights(matrices, queries, f, n_rep * columns, dtype, *others)
+
+    sends = [weights((feat + d) % n_feat, BF16) for d in range(1, n_feat)]
     others = [shift(x, "feat", n_feat, d + 1) for d, x in enumerate(sends)]
-    own = weights(feat, rep, F32, *away(feat, [here[1], *sends]))
-
-    firsts, seconds = [], []
-    if extra:
-        first = swap_near(jnp.concatenate([packed[-2], far]))
-        firsts = [first[j * extra:(j + 1) * extra] for j in range(n_shard)]
-        seconds = [second[j * extra:(j + 1) * extra] for j in range(n_shard)]
+    own = weights(feat, F32, *sends)
+
     for d in range(2, last_hops):
-        here[d] = shift(after(packed[d], *sends), "shard", n_shard, d)
-    last = shift(after(packed[last_hops], here[last_hops - 1]), "shard", n_shard, last_hops)
-
-    ready = [here[d] for d in range(last_hops)]
-    high, low, *shares = early_scores(
-        own, others, ready, firsts, seconds, table, rows, n_rep, n_shard, bulk
+        here[d] = shift(after(sent[d], own), "shard", n_shard, d)
+    last = shift(after(sent[last_hops], here[last_hops - 1]), "shard", n_shard, last_hops)
+
+    ready = [with_rep(here[d]) for d in range(1, last_hops)]
+    high, low, early = early_scores(
+        own, others, mine, ready, firsts, seconds, table, rows, n_rep, n_shard, bulk, extra
     )
-
-    def over_rep(shares):
-        total = shares[0]
-        for d in range(1, n_rep):
-            total = total + shift(shares[d], "rep", n_rep, d)
-        return total
 
     def for_feat(total, d):
         share = total.shape[1] // n_feat
         return lax.dynamic_slice_in_dim(total, ((feat + d) % n_feat) * share, share, 1)
 
-    early = over_rep(shares)
+    def over_feat(total, sends):
+        return [for_feat(total, 0)] + [shift(x, "feat", n_feat, d + 1) for d, x in enumerate(sends)]
+
     early_sends = [for_feat(early, d).astype(BF16) for d in range(1, n_feat)]
-    late = over_rep(late_scores(last, high, low, n_rep, *early_sends))
+    late = late_scores(with_rep(after(last, *early_sends)), high, low)
     late_sends = [for_feat(late, d).astype(BF16) for d in range(1, n_feat)]
-    early_all = [for_feat(early, 0)] + [shift(x, "feat", n_feat, d + 1) for d, x in enumerate(early_sends)]
-    late_all = [for_feat(late, 0)] + [shift(x, "feat", n_feat, d + 1) for d, x in enumerate(late_sends)]
-    return merge(table, early_all, late_all, n_shard)[None]
+    return merge(table, over_feat(early, early_sends), over_feat(late, late_sends), n_shard)[None]
 
 
 def solution(mesh):

time: 129 us -> 120 us (0.930)
  waiting for transfers between devices: 60.7 us -> 51.8 us
  local copies, waits for them, and re-layouts: 8.71 us -> 11.8 us
  Pallas kernels: 37.2 us -> 35.3 us
  other arithmetic: 3.56 us -> 1.83 us
    ppermute x2, waiting for transfers between devices: 30.1 us -> 13.3 us  [swap(): return lax.ppermute(x, axis, [(i, i ^ bit) for i in range(size)])]
    ppermute x15 -> x17, waiting for transfers between devices: 30.6 us -> 38.5 us  [shift(): return lax.ppermute(x, axis, [(i, (i + by) % size) for i in range(size)])]
    pallas_call x4 -> x2, Pallas kernels: 17 us -> 12 us  [partial_weights(): pl.pallas_call(kernel, grid_spec=pltpu.PrefetchScalarGridSpec(num_scalar_...]
    unnamed x22 -> x18, local copies, waits for them, and re-layouts: 1.39 us -> 5.02 us
    slice x3 -> x0, local copies, waits for them, and re-layouts: 3.46 us -> none  [the longest x1 1.26 us: body(): seconds = [second[j * extra:(j + 1) * extra] for j in range(n_shard)]]
    add x2 -> x0, other arithmetic: 2.68 us -> none  [over_rep(): total = total + shift(shares[d], 'rep', n_rep, d)]
    pallas_call x3 -> x4, Pallas kernels: 11.5 us -> 14.1 us  [the longest x1 7.23 us: early_scores(): pl.pallas_call(kernel, in_specs=[SMEM] + [VMEM] * (2 + n_other + n_rep *...]
    concatenate x0 -> x1, local copies, waits for them, and re-layouts: none -> 1.85 us  [swap_near(): return jnp.concatenate([x, swap(x, 'shard', n_shard, 1)])]
  transfers between devices with their start and end apart: 17 -> 19, of which waited for: 9 -> 8; matrix products, arithmetic and copies ran while one was open for 8% -> 8% of each run, Pallas kernels for 11% -> 28%
where the time goes in v6:
time: 120 us
  waiting for transfers between devices  51.8 us (43%)
  Pallas kernels  35.3 us (29%)
  starting transfers between devices  18.1 us (15%)
  local copies, waits for them, and re-layouts  11.8 us (10%)
  other arithmetic  1.83 us (2%)
    ppermute x17, waiting for transfers between devices, shift(): return lax.ppermute(x, axis, [(i, (i + by) % size) for i in range(size)])  38.5 us
    ppermute x17, starting transfers between devices, shift(): return lax.ppermute(x, axis, [(i, (i + by) % size) for i in range(size)])  15.7 us
    ppermute x2, waiting for transfers between devices, swap(): return lax.ppermute(x, axis, [(i, i ^ bit) for i in range(size)])  13.3 us
    pallas_call x2, Pallas kernels, partial_weights(): pl.pallas_call(kernel, grid_spec=pltpu.PrefetchScalarGridSpec(num_scalar_...  12 us
    pallas_call x1, Pallas kernels, early_scores(): pl.pallas_call(kernel, in_specs=[SMEM] + [VMEM] * (2 + n_other + n_rep *...  7.23 us
    unnamed x18, local copies, waits for them, and re-layouts  5.02 us
    pallas_call x1, Pallas kernels, pack_rows(): pl.pallas_call(kernel, grid=(1,), in_specs=[pl.BlockSpec((lines, LANES),...  4.74 us
    pallas_call x1, Pallas kernels, own_rows(): pl.pallas_call(kernel, in_specs=[VMEM] * 2, out_specs=VMEM, out_shape=jax...  3.46 us
  transfers between devices with their start and end apart: 19, of which 8 were waited for; matrix products, arithmetic and copies ran while one was open for 8% of the time, Pallas kernels for 28%

profile of v6, /device:TPU:0, one launch (start us, length us, event | category | flops | bytes accessed | tf_op | source)
XLA Modules:
  0.0 119.7 jit_solution(6278928321232658943)
XLA Ops:
  0.0 0.5 collective-permute-start.3
  0.5 2.7 %pick_queries.1 = (bf16[1,64,1024]{2,1,0:T(8,128)(2,1)}, bf16[1,64,1024]{2,1,0:T(8,128)(2,1)}, bf16[1,64,1024]{2,1,0:T(8,128)(2,1)}, bf16[1,64,1024]{2,1,0:T(8,128)(2,1)}) custom-call(s32[4,4]{1,0:T(4,128)} %pattern_ref.3, s32[16]{0:T(128)} %slot_ref.3, bf16[4,128,1024]{2,1,0:T(8,128)(2,1)} %in_ref.1), custom_call_target="tpu_custom_call" | custom-call | flops 1 | bytes 1 | tf_op jit(solution)/shard_map/pick_queries/pallas_call | solution.py:73
  3.2 4.7 %collective-permute-start.6 = (bf16[1,64,1024]{2,1,0:T(8,128)(2,1)}, bf16[1,64,1024]{2,1,0:T(8,128)(2,1)S(1)}, u32[]{:S(2)}, u32[]{:S(2)}) collective-permute-start(bf16[1,64,1024]{2,1,0:T(8,128)(2,1)} %get-tuple-element.29), channel_id=1, source_target_pairs={{0,12},{4,0},{8,4},{12,8},{1,13},{5,1},{9,5},{13,9},{2,14},{6,2},{... | collective-permute-start | bytes 393224 | tf_op jit(solution)/shard_map/ppermute | solution.py:20
  7.8 1.0 collective-permute-start.4
  8.9 0.7 copy-done.5
  9.6 0.8 row_table.1
  10.4 0.0 copy-start.6
  10.4 0.0 copy-start.7
  10.4 1.6 %collective-permute-start.7 = (s32[8,128]{1,0:T(8,128)S(1)}, s32[8,128]{1,0:T(8,128)S(1)}, u32[]{:S(2)}, u32[]{:S(2)}) collective-permute-start(s32[8,128]{1,0:T(8,128)S(1)} %get-tuple-element.31), channel_id=1, source_target_pairs={{0,16},{16,0},{1,17},{17,1},{2,18},{18,2},{3,19},{19,3},{4,20},{20... | collective-permute-start | bytes 12296 | tf_op jit(solution)/shard_map/ppermute | solution.py:20
  12.0 4.7 %pack_rows.1 = (bf16[256,1024]{1,0:T(8,128)(2,1)}, bf16[256,1024]{1,0:T(8,128)(2,1)S(1)}, bf16[256,1024]{1,0:T(8,128)(2,1)}, bf16[128,1024]{1,0:T(8,128)(2,1)S(1...) custom-call(s32[32,128]{1,0:T(8,128)S(1)} %bitcast.7, bf16[1024,2048]{1,0:T(8,128)(2,1)} %train_ref.3), custom_call_target="tpu_custom_call" | custom-call | flops 1 | bytes 1 | tf_op jit(solution)/shard_map/pack_rows/pallas_call | solution.py:198
  16.8 3.4 %collective-permute-done.5 = bf16[1,64,1024]{2,1,0:T(8,128)(2,1)S(1)} collective-permute-done((bf16[1,64,1024]{2,1,0:T(8,128)(2,1)}, bf16[1,64,1024]{2,1,0:T(8,128)(2,1)S(1)}, u32[]{:S(2)}, u32[]{:S(2)}) %collective-permute-start.5) | collective-permute-done | bytes 131104 | tf_op jit(solution)/shard_map/ppermute | solution.py:20
  20.2 1.0 pad_maximum_fusion.1.refs_0_
  21.2 1.6 %collective-permute-start.8 = (bf16[4,64,1024]{2,1,0:T(8,128)(2,1)S(1)}, bf16[4,64,1024]{2,1,0:T(8,128)(2,1)S(1)}, u32[]{:S(2)}, u32[]{:S(2)}) collective-permute-start(bf16[4,64,1024]{2,1,0:T(8,128)(2,1)S(1)} %after.5.refs_0_), channel_id=1, source_target_pairs={{0,16},{16,0},{1,17},{17,1},{2,18},{18,2},{3,19},{19,3},{4,20},{20... | collective-permute-start | bytes 1572872 | tf_op jit(solution)/shard_map/ppermute | solution.py:20
  22.8 2.4 %collective-permute-start.9 = (bf16[128,1024]{1,0:T(8,128)(2,1)S(1)}, bf16[128,1024]{1,0:T(8,128)(2,1)S(1)}, u32[]{:S(2)}, u32[]{:S(2)}) collective-permute-start(bf16[128,1024]{1,0:T(8,128)(2,1)S(1)} %get-tuple-element.32), channel_id=1, source_target_pairs={{0,8},{4,12},{8,0},{12,4},{1,9},{5,13},{9,1},{13,5},{2,10},{6,14},... | collective-permute-start | bytes 786440 | tf_op jit(solution)/shard_map/ppermute | solution.py:24
  25.2 11.5 %collective-permute-done.9.refs_2_.refs_1_ = bf16[128,1024]{1,0:T(8,128)(2,1)S(1)} collective-permute-done((bf16[128,1024]{1,0:T(8,128)(2,1)S(1)}, bf16[128,1024]{1,0:T(8,128)(2,1)S(1)}, u32[]{:S(2)}, u32[]{:S(2)}) %collective-permute-start.9) | collective-permute-done | bytes 262176 | tf_op jit(solution)/shard_map/ppermute | solution.py:24
  36.7 0.8 pad_maximum_fusion.2
  37.5 3.5 %own_rows.1.refs_3_.refs_2_ = bf16[256,2048]{1,0:T(8,128)(2,1)S(1)} custom-call(s32[8,128]{1,0:T(8,128)S(1)} %get-tuple-element.33.goal_ref, bf16[1024,2048]{1,0:T(8,128)(2,1)} %train_ref.3), custom_call_target="tpu_custom_call" | custom-call | flops 1 | bytes 1 | tf_op jit(solution)/shard_map/own_rows/pallas_call | solution.py:141
  41.0 0.6 slice.3
  42.2 2.2 %conditional.1 = (bf16[512,1024]{1,0:T(8,128)(2,1)}, bf16[512,1024]{1,0:T(8,128)(2,1)}) conditional(s32[]{:T(128)} %bitcast.3, () %tuple.13, bf16[128,1024]{1,0:T(8,128)(2,1)S(1)} %get-tuple-element.34), branch_computations={%region_0.0_spmd, %region_1.0_spmd} | conditional | flops 1048576 | bytes 10485896 | solution.py:471
  42.2 1.1 broadcast.4
  43.3 1.1 broadcast.4.clone
  44.5 1.9 %join_queries.1 = (bf16[1024,256]{1,0:T(8,128)(2,1)S(1)}, bf16[1024,256]{1,0:T(8,128)(2,1)}) custom-call(s32[4,4]{1,0:T(4,128)S(1)} %copy-done.6, s32[16]{0:T(128)S(1)} %copy-done.7, bf16[4,64,1024]{2,1,0:T(8,128)(2,1)S(1)} %after.5.refs_0_, bf16[4,64,1024]{2,1,0:T(8,128)(2,1)S(1)} %collective-permute-done.8.refs_1_, ...), custom_call_target="tpu_custom_call" | custom-call | flops 1 | bytes 1 | tf_op jit(solution)/shard_map/join_queries/pallas_call | solution.py:115
  46.4 0.0 collective-permute-start.10
  46.4 0.7 constant_dynamic-update-slice_fusion.5
  47.1 2.0 %collective-permute-start.12 = (bf16[256,1024]{1,0:T(8,128)(2,1)}, bf16[256,1024]{1,0:T(8,128)(2,1)}, u32[]{:S(2)}, u32[]{:S(2)}) collective-permute-start(bf16[256,1024]{1,0:T(8,128)(2,1)} %after.6), channel_id=1, source_target_pairs={{0,4},{4,8},{8,12},{12,0},{1,5},{5,9},{9,13},{13,1},{2,6},{6,10},{... | collective-permute-start | bytes 1572872 | tf_op jit(solution)/shard_map/ppermute | solution.py:20
  49.2 0.7 constant_dynamic-update-slice_fusion.4
  49.9 1.8 %collective-permute-done.16 = bf16[256,1024]{1,0:T(8,128)(2,1)} collective-permute-done((bf16[256,1024]{1,0:T(8,128)(2,1)}, bf16[256,1024]{1,0:T(8,128)(2,1)}, u32[]{:S(2)}, u32[]{:S(2)}) %collective-permute-start.16) | collective-permute-done | bytes 524320 | tf_op jit(solution)/shard_map/ppermute | solution.py:24
  51.7 1.9 %constant_dynamic-update-slice_fusion.3.refs_7_ = bf16[512,1024]{1,0:T(8,128)(2,1)} fusion(bf16[512,1024]{1,0:T(8,128)(2,1)} %constant_dynamic-update-slice_fusion.4, bf16[256,1024]{1,0:T(8,128)(2,1)} %collective-permute-done.16), kind=kLoop, calls=%fused_computation.8 | loop fusion | bytes 1048576 | tf_op jit(solution)/shard_map/concatenate | solution.py:464
  53.6 5.4 %partial_weights.2.refs_4_ = bf16[2048,256]{1,0:T(8,128)(2,1)S(1)} custom-call(s32[1]{0:T(128)} %bitcast.4.block_ref, bf16[4096,1024]{1,0:T(8,128)(2,1)} %bitcast.9, bf16[4096,1024]{1,0:T(8,128)(2,1)} %collective-permute-done.3.refs_1_, bf16[1024,256]{1,0:T(8,128)(2,1)S(1)} %get-tuple-element.37.refs_2_, bf16[1024,256]{1,0:T(8,128)(2,1)S(1)} %collective-permute-done.10.refs_3_), custom_call_target="tpu_custom_call" | custom-call | flops 1 | bytes 1 | tf_op jit(solution)/shard_map/partial_weights/pallas_call | solution.py:225
  59.0 6.5 %partial_weights.3.refs_1_.refs_0_ = f32[2048,256]{1,0:T(8,128)} custom-call(s32[1]{0:T(128)} %bitcast.1.block_ref, bf16[4096,1024]{1,0:T(8,128)(2,1)} %bitcast.10, bf16[4096,1024]{1,0:T(8,128)(2,1)} %collective-permute-done.3.refs_1_, bf16[1024,256]{1,0:T(8,128)(2,1)S(1)} %get-tuple-element.37.refs_2_, ...), custom_call_target="tpu_custom_call" | custom-call | flops 1 | bytes 1 | tf_op jit(solution)/shard_map/partial_weights/pallas_call | solution.py:225
  65.6 1.6 %copy-done = f32[2048,256]{1,0:T(8,128)S(1)} copy-done((f32[2048,256]{1,0:T(8,128)S(1)}, f32[2048,256]{1,0:T(8,128)}, u32[]{:S(2)}) %copy-start) | copy-done | bytes 2097176
  67.1 1.5 %collective-permute-start.11 = (bf16[2048,256]{1,0:T(8,128)(2,1)S(1)}, bf16[2048,256]{1,0:T(8,128)(2,1)}, u32[]{:S(2)}, u32[]{:S(2)}) collective-permute-start(bf16[2048,256]{1,0:T(8,128)(2,1)S(1)} %partial_weights.2.refs_4_), channel_id=1, source_target_pairs={{0,2},{2,0},{1,3},{3,1},{4,6},{6,4},{5,7},{7,5},{8,10},{10,8},{9,1... | collective-permute-start | bytes 3145736 | tf_op jit(solution)/shard_map/ppermute | solution.py:20
  68.6 0.2 collective-permute-start.13
  68.9 24.5 %collective-permute-done.14.refs_5_.refs_1_ = bf16[256,1024]{1,0:T(8,128)(2,1)S(1)} collective-permute-done((bf16[256,1024]{1,0:T(8,128)(2,1)S(1)}, bf16[256,1024]{1,0:T(8,128)(2,1)S(1)}, u32[]{:S(2)}, u32[]{:S(2)}) %collective-permute-start.14) | collective-permute-done | bytes 524320 | tf_op jit(solution)/shard_map/ppermute | solution.py:20
  93.3 0.1 collective-permute-start.15
  93.4 0.2 collective-permute-start.19
  93.6 1.6 %collective-permute-done.15.refs_6_ = bf16[256,1024]{1,0:T(8,128)(2,1)S(1)} collective-permute-done((bf16[256,1024]{1,0:T(8,128)(2,1)S(1)}, bf16[256,1024]{1,0:T(8,128)(2,1)S(1)}, u32[]{:S(2)}, u32[]{:S(2)}) %collective-permute-start.15) | collective-permute-done | bytes 524320 | tf_op jit(solution)/shard_map/ppermute | solution.py:20
  95.2 7.2 %early_scores.1 = (bf16[2048,256]{1,0:T(8,128)(2,1)S(1)}, bf16[2048,256]{1,0:T(8,128)(2,1)}, f32[1024,256]{1,0:T(8,128)}) custom-call(s32[4,4]{1,0:T(4,128)S(1)} %get-tuple-element.25.table_ref, f32[2048,256]{1,0:T(8,128)} %partial_weights.3.refs_1_.refs_0_, bf16[2048,256]{1,0:T(8,128)(2,1)} %collective-permute-done.11.refs_1_, bf16[256,2048]{1,0:T(8,128)(2,1)} %copy-done.1, ...), custom_call_target="tpu_custom_call" | custom-call | flops 1 | bytes 1 | tf_op jit(solution)/shard_map/early_scores/pallas_call | solution.py:366
  102.5 1.1 dynamic-slice_convert_fusion.refs_1_
  103.6 4.3 %collective-permute-done.19.refs_0_ = bf16[256,1024]{1,0:T(8,128)(2,1)S(1)} collective-permute-done((bf16[256,1024]{1,0:T(8,128)(2,1)}, bf16[256,1024]{1,0:T(8,128)(2,1)S(1)}, u32[]{:S(2)}, u32[]{:S(2)}) %collective-permute-start.19) | collective-permute-done | bytes 524320 | tf_op jit(solution)/shard_map/ppermute | solution.py:20
  107.9 1.5 %collective-permute-start.18 = (bf16[1024,128]{1,0:T(8,128)(2,1)S(1)}, bf16[1024,128]{1,0:T(8,128)(2,1)S(1)}, u32[]{:S(2)}, u32[]{:S(2)}) collective-permute-start(bf16[1024,128]{1,0:T(8,128)(2,1)S(1)} %dynamic-slice_convert_fusion.refs_1_), channel_id=1, source_target_pairs={{0,2},{2,0},{1,3},{3,1},{4,6},{6,4},{5,7},{7,5},{8,10},{10,8},{9,1... | collective-permute-start | bytes 786440 | tf_op jit(solution)/shard_map/ppermute | solution.py:20
  109.4 1.1 constant_dynamic-slice_fusion.1.refs_0_
  110.5 1.2 %copy-done.2 = bf16[2048,256]{1,0:T(8,128)(2,1)S(1)} copy-done((bf16[2048,256]{1,0:T(8,128)(2,1)S(1)}, bf16[2048,256]{1,0:T(8,128)(2,1)}, u32[]{:S(2)}) %copy-start.2) | copy-done | bytes 1048600
  111.7 0.7 late_scores.1
  112.4 0.9 collective-permute-start.21
  113.3 3.7 %collective-permute-done.18.refs_1_ = bf16[1024,128]{1,0:T(8,128)(2,1)S(1)} collective-permute-done((bf16[1024,128]{1,0:T(8,128)(2,1)S(1)}, bf16[1024,128]{1,0:T(8,128)(2,1)S(1)}, u32[]{:S(2)}, u32[]{:S(2)}) %collective-permute-start.18) | collective-permute-done | bytes 262176 | tf_op jit(solution)/shard_map/ppermute | solution.py:20
  117.0 1.0 collective-permute-done.21.refs_3_
  118.0 1.7 %merge.1 = f32[128,1024]{1,0:T(8,128)} custom-call(s32[4,4]{1,0:T(4,128)S(1)} %get-tuple-element.25.table_ref, f32[1024,128]{1,0:T(8,128)S(1)} %constant_dynamic-slice_fusion.1.refs_0_, bf16[1024,128]{1,0:T(8,128)(2,1)S(1)} %collective-permute-done.18.refs_1_, f32[256,128]{1,0:T(8,128)S(1)} %constant_dynamic-slice_fusion.refs_2_, ...), custom_call_target="tpu_custom_call" | custom-call | flops 1 | bytes 1 | tf_op jit(solution)/shard_map/merge/pallas_call | solution.py:422
  (35 shorter events, 0.1 us)
Async XLA Ops:
  0.0 53.5 %collective-permute-start.3 = (bf16[4096,1024]{1,0:T(8,128)(2,1)}, bf16[4096,1024]{1,0:T(8,128)(2,1)}, u32[]{:S(2)}, u32[]{:S(2)}) collective-permute-start(bf16[4096,1024]{1,0:T(8,128)(2,1)} %bitcast.8), channel_id=1, source_target_pairs={{0,1},{1,0},{2,3},{3,2},{4,5},{5,4},{6,7},{7,6},{8,9},{9,8},{10,11... | collective-permute-start | bytes 25165832 | tf_op jit(solution)/shard_map/ppermute | solution.py:20
  3.2 13.6 %collective-permute-start.6 = (bf16[1,64,1024]{2,1,0:T(8,128)(2,1)}, bf16[1,64,1024]{2,1,0:T(8,128)(2,1)S(1)}, u32[]{:S(2)}, u32[]{:S(2)}) collective-permute-start(bf16[1,64,1024]{2,1,0:T(8,128)(2,1)} %get-tuple-element.29), channel_id=1, source_target_pairs={{0,12},{4,0},{8,4},{12,8},{1,13},{5,1},{9,5},{13,9},{2,14},{6,2},{... | collective-permute-start | bytes 393224 | tf_op jit(solution)/shard_map/ppermute | solution.py:20
  7.8 12.4 %collective-permute-start.5 = (bf16[1,64,1024]{2,1,0:T(8,128)(2,1)}, bf16[1,64,1024]{2,1,0:T(8,128)(2,1)S(1)}, u32[]{:S(2)}, u32[]{:S(2)}) collective-permute-start(bf16[1,64,1024]{2,1,0:T(8,128)(2,1)} %get-tuple-element.28), channel_id=1, source_target_pairs={{0,8},{4,12},{8,0},{12,4},{1,9},{5,13},{9,1},{13,5},{2,10},{6,14},... | collective-permute-start | bytes 393224 | tf_op jit(solution)/shard_map/ppermute | solution.py:20
  7.8 12.4 %collective-permute-start.4 = (bf16[1,64,1024]{2,1,0:T(8,128)(2,1)}, bf16[1,64,1024]{2,1,0:T(8,128)(2,1)S(1)}, u32[]{:S(2)}, u32[]{:S(2)}) collective-permute-start(bf16[1,64,1024]{2,1,0:T(8,128)(2,1)} %get-tuple-element.27), channel_id=1, source_target_pairs={{0,4},{4,8},{8,12},{12,0},{1,5},{5,9},{9,13},{13,1},{2,6},{6,10},{... | collective-permute-start | bytes 393224 | tf_op jit(solution)/shard_map/ppermute | solution.py:20
  8.9 0.7 copy-start.5
  10.4 34.0 %copy-start.6 = (s32[4,4]{1,0:T(4,128)S(1)}, s32[4,4]{1,0:T(4,128)}, u32[]{:S(2)}) copy-start(s32[4,4]{1,0:T(4,128)} %pattern_ref.3) | copy-start | bytes 196
  10.4 34.0 %copy-start.7 = (s32[16]{0:T(128)S(1)}, s32[16]{0:T(128)}, u32[]{:S(2)}) copy-start(s32[16]{0:T(128)} %slot_ref.3) | copy-start | bytes 196
  10.4 6.3 %collective-permute-start.7 = (s32[8,128]{1,0:T(8,128)S(1)}, s32[8,128]{1,0:T(8,128)S(1)}, u32[]{:S(2)}, u32[]{:S(2)}) collective-permute-start(s32[8,128]{1,0:T(8,128)S(1)} %get-tuple-element.31), channel_id=1, source_target_pairs={{0,16},{16,0},{1,17},{17,1},{2,18},{18,2},{3,19},{19,3},{4,20},{20... | collective-permute-start | bytes 12296 | tf_op jit(solution)/shard_map/ppermute | solution.py:20
  16.8 4.4 %copy-start.3 = (bf16[256,1024]{1,0:T(8,128)(2,1)}, bf16[256,1024]{1,0:T(8,128)(2,1)S(1)}, u32[]{:S(2)}) copy-start(bf16[256,1024]{1,0:T(8,128)(2,1)S(1)} %get-tuple-element.39.refs_0_) | copy-start | bytes 1572868
  21.2 23.2 %collective-permute-start.8 = (bf16[4,64,1024]{2,1,0:T(8,128)(2,1)S(1)}, bf16[4,64,1024]{2,1,0:T(8,128)(2,1)S(1)}, u32[]{:S(2)}, u32[]{:S(2)}) collective-permute-start(bf16[4,64,1024]{2,1,0:T(8,128)(2,1)S(1)} %after.5.refs_0_), channel_id=1, source_target_pairs={{0,16},{16,0},{1,17},{17,1},{2,18},{18,2},{3,19},{19,3},{4,20},{20... | collective-permute-start | bytes 1572872 | tf_op jit(solution)/shard_map/ppermute | solution.py:20
  22.8 13.9 %collective-permute-start.9 = (bf16[128,1024]{1,0:T(8,128)(2,1)S(1)}, bf16[128,1024]{1,0:T(8,128)(2,1)S(1)}, u32[]{:S(2)}, u32[]{:S(2)}) collective-permute-start(bf16[128,1024]{1,0:T(8,128)(2,1)S(1)} %get-tuple-element.32), channel_id=1, source_target_pairs={{0,8},{4,12},{8,0},{12,4},{1,9},{5,13},{9,1},{13,5},{2,10},{6,14},... | collective-permute-start | bytes 786440 | tf_op jit(solution)/shard_map/ppermute | solution.py:24
  37.5 14.2 %collective-permute-start.16 = (bf16[256,1024]{1,0:T(8,128)(2,1)}, bf16[256,1024]{1,0:T(8,128)(2,1)}, u32[]{:S(2)}, u32[]{:S(2)}) collective-permute-start(bf16[256,1024]{1,0:T(8,128)(2,1)} %pad_maximum_fusion.2), channel_id=1, source_target_pairs={{0,4},{4,0},{8,12},{12,8},{1,5},{5,1},{9,13},{13,9},{2,6},{6,2},{1... | collective-permute-start | bytes 1572872 | tf_op jit(solution)/shard_map/ppermute | solution.py:24
  41.0 18.0 %copy-start.1 = (bf16[256,2048]{1,0:T(8,128)(2,1)}, bf16[256,2048]{1,0:T(8,128)(2,1)S(1)}, u32[]{:S(2)}) copy-start(bf16[256,2048]{1,0:T(8,128)(2,1)S(1)} %own_rows.1.refs_3_.refs_2_) | copy-start | bytes 3145732
  46.4 7.2 %collective-permute-start.10 = (bf16[1024,256]{1,0:T(8,128)(2,1)}, bf16[1024,256]{1,0:T(8,128)(2,1)S(1)}, u32[]{:S(2)}, u32[]{:S(2)}) collective-permute-start(bf16[1024,256]{1,0:T(8,128)(2,1)} %get-tuple-element.38), channel_id=1, source_target_pairs={{0,1},{1,0},{2,3},{3,2},{4,5},{5,4},{6,7},{7,6},{8,9},{9,8},{10,11... | collective-permute-start | bytes 1572872 | tf_op jit(solution)/shard_map/ppermute | solution.py:20
  47.1 21.5 %collective-permute-start.12 = (bf16[256,1024]{1,0:T(8,128)(2,1)}, bf16[256,1024]{1,0:T(8,128)(2,1)}, u32[]{:S(2)}, u32[]{:S(2)}) collective-permute-start(bf16[256,1024]{1,0:T(8,128)(2,1)} %after.6), channel_id=1, source_target_pairs={{0,4},{4,8},{8,12},{12,0},{1,5},{5,9},{9,13},{13,1},{2,6},{6,10},{... | collective-permute-start | bytes 1572872 | tf_op jit(solution)/shard_map/ppermute | solution.py:20
  53.5 40.1 %collective-permute-start.17 = (bf16[512,1024]{1,0:T(8,128)(2,1)}, bf16[512,1024]{1,0:T(8,128)(2,1)}, u32[]{:S(2)}, u32[]{:S(2)}) collective-permute-start(bf16[512,1024]{1,0:T(8,128)(2,1)} %constant_dynamic-update-slice_fusion.3.refs_7_), channel_id=1, source_target_pairs={{0,1},{1,0},{2,3},{3,2},{4,5},{5,4},{6,7},{7,6},{8,9},{9,8},{10,11... | collective-permute-start | bytes 3145736 | tf_op jit(solution)/shard_map/ppermute | solution.py:20
  59.0 6.5 %copy-start.4 = (bf16[256,1024]{1,0:T(8,128)(2,1)S(1)}, bf16[256,1024]{1,0:T(8,128)(2,1)}, u32[]{:S(2)}) copy-start(bf16[256,1024]{1,0:T(8,128)(2,1)} %copy-done.3) | copy-start | bytes 1572868
  65.6 1.6 %copy-start = (f32[2048,256]{1,0:T(8,128)S(1)}, f32[2048,256]{1,0:T(8,128)}, u32[]{:S(2)}) copy-start(f32[2048,256]{1,0:T(8,128)} %partial_weights.3.refs_1_.refs_0_) | copy-start | bytes 6291460
  67.1 26.2 %collective-permute-start.14 = (bf16[256,1024]{1,0:T(8,128)(2,1)S(1)}, bf16[256,1024]{1,0:T(8,128)(2,1)S(1)}, u32[]{:S(2)}, u32[]{:S(2)}) collective-permute-start(bf16[256,1024]{1,0:T(8,128)(2,1)S(1)} %after.7), channel_id=1, source_target_pairs={{0,8},{4,12},{8,0},{12,4},{1,9},{5,13},{9,1},{13,5},{2,10},{6,14},... | collective-permute-start | bytes 1572872 | tf_op jit(solution)/shard_map/ppermute | solution.py:20
  67.1 26.5 %collective-permute-start.11 = (bf16[2048,256]{1,0:T(8,128)(2,1)S(1)}, bf16[2048,256]{1,0:T(8,128)(2,1)}, u32[]{:S(2)}, u32[]{:S(2)}) collective-permute-start(bf16[2048,256]{1,0:T(8,128)(2,1)S(1)} %partial_weights.2.refs_4_), channel_id=1, source_target_pairs={{0,2},{2,0},{1,3},{3,1},{4,6},{6,4},{5,7},{7,5},{8,10},{10,8},{9,1... | collective-permute-start | bytes 3145736 | tf_op jit(solution)/shard_map/ppermute | solution.py:20
  68.6 25.0 %collective-permute-start.13 = (bf16[256,1024]{1,0:T(8,128)(2,1)}, bf16[256,1024]{1,0:T(8,128)(2,1)S(1)}, u32[]{:S(2)}, u32[]{:S(2)}) collective-permute-start(bf16[256,1024]{1,0:T(8,128)(2,1)} %collective-permute-done.12.refs_3_), channel_id=1, source_target_pairs={{0,1},{1,0},{2,3},{3,2},{4,5},{5,4},{6,7},{7,6},{8,9},{9,8},{10,11... | collective-permute-start | bytes 1572872 | tf_op jit(solution)/shard_map/ppermute | solution.py:20
  93.3 1.9 %collective-permute-start.15 = (bf16[256,1024]{1,0:T(8,128)(2,1)S(1)}, bf16[256,1024]{1,0:T(8,128)(2,1)S(1)}, u32[]{:S(2)}, u32[]{:S(2)}) collective-permute-start(bf16[256,1024]{1,0:T(8,128)(2,1)S(1)} %collective-permute-done.14.refs_5_.refs_1_), channel_id=1, source_target_pairs={{0,1},{1,0},{2,3},{3,2},{4,5},{5,4},{6,7},{7,6},{8,9},{9,8},{10,11... | collective-permute-start | bytes 1572872 | tf_op jit(solution)/shard_map/ppermute | solution.py:20
  93.4 14.5 %collective-permute-start.19 = (bf16[256,1024]{1,0:T(8,128)(2,1)}, bf16[256,1024]{1,0:T(8,128)(2,1)S(1)}, u32[]{:S(2)}, u32[]{:S(2)}) collective-permute-start(bf16[256,1024]{1,0:T(8,128)(2,1)} %after.8), channel_id=1, source_target_pairs={{0,12},{4,0},{8,4},{12,8},{1,13},{5,1},{9,5},{13,9},{2,14},{6,2},{... | collective-permute-start | bytes 1572872 | tf_op jit(solution)/shard_map/ppermute | solution.py:20
  107.9 2.6 %collective-permute-start.20 = (bf16[256,1024]{1,0:T(8,128)(2,1)S(1)}, bf16[256,1024]{1,0:T(8,128)(2,1)S(1)}, u32[]{:S(2)}, u32[]{:S(2)}) collective-permute-start(bf16[256,1024]{1,0:T(8,128)(2,1)S(1)} %after.9.refs_0_), channel_id=1, source_target_pairs={{0,1},{1,0},{2,3},{3,2},{4,5},{5,4},{6,7},{7,6},{8,9},{9,8},{10,11... | collective-permute-start | bytes 1572872 | tf_op jit(solution)/shard_map/ppermute | solution.py:20
  107.9 9.1 %collective-permute-start.18 = (bf16[1024,128]{1,0:T(8,128)(2,1)S(1)}, bf16[1024,128]{1,0:T(8,128)(2,1)S(1)}, u32[]{:S(2)}, u32[]{:S(2)}) collective-permute-start(bf16[1024,128]{1,0:T(8,128)(2,1)S(1)} %dynamic-slice_convert_fusion.refs_1_), channel_id=1, source_target_pairs={{0,2},{2,0},{1,3},{3,1},{4,6},{6,4},{5,7},{7,5},{8,10},{10,8},{9,1... | collective-permute-start | bytes 786440 | tf_op jit(solution)/shard_map/ppermute | solution.py:20
  110.5 1.2 %copy-start.2 = (bf16[2048,256]{1,0:T(8,128)(2,1)S(1)}, bf16[2048,256]{1,0:T(8,128)(2,1)}, u32[]{:S(2)}) copy-start(bf16[2048,256]{1,0:T(8,128)(2,1)} %get-tuple-element.42.low_ref) | copy-start | bytes 3145732
  112.4 5.6 %collective-permute-start.21 = (bf16[256,128]{1,0:T(8,128)(2,1)S(1)}, bf16[256,128]{1,0:T(8,128)(2,1)S(1)}, u32[]{:S(2)}, u32[]{:S(2)}) collective-permute-start(bf16[256,128]{1,0:T(8,128)(2,1)S(1)} %dynamic-slice_convert_fusion.1), channel_id=1, source_target_pairs={{0,2},{2,0},{1,3},{3,1},{4,6},{6,4},{5,7},{7,5},{8,10},{10,8},{9,1... | collective-permute-start | bytes 196616 | tf_op jit(solution)/shard_map/ppermute | solution.py:20

commit v7 on v6

--- a/solution.py
+++ b/solution.py
@@ -11,7 +11,7 @@
 VMEM = pl.BlockSpec(memory_space=pltpu.VMEM)
 ANY = pl.BlockSpec(memory_space=pl.ANY)
 SMEM = pl.BlockSpec(memory_space=pltpu.SMEM)
-PARAMS = pltpu.CompilerParams(vmem_limit_bytes=50 * 2**20)
+PARAMS = pltpu.CompilerParams(vmem_limit_bytes=24 * 2**20)
 FIRST = pltpu.CompilerParams(vmem_limit_bytes=60 * 2**20)
 LANES = 128
 
@@ -46,6 +46,32 @@
         compiler_params=PARAMS,
         name="after",
     )(x, *others)
+
+
+def stack(parts, *others):
+    size, width = parts[0].shape
+    n = len(parts)
+
+    def kernel(*refs):
+        out, sem = refs[-2:]
+        copies = [
+            pltpu.make_async_copy(refs[j], out.at[j * size:(j + 1) * size], sem.at[j]) for j in range(n)
+        ]
+        for copy in copies:
+            copy.start()
+        for copy in copies:
+            copy.wait()
+
+    return pl.pallas_call(
+        kernel,
+        in_specs=[ANY] * (n + len(others)),
+        out_specs=ANY,
+        out_shape=jax.ShapeDtypeStruct((n * size, width), parts[0].dtype),
+        scratch_shapes=[pltpu.SemaphoreType.DMA((n,))],
+        cost_estimate=cost(0, 0),
+        compiler_params=PARAMS,
+        name="stack",
+    )(*parts, *others)
 
 
 def pick_queries(query_store, block_slot, pattern, n_group):
@@ -83,12 +109,13 @@
 
 
 def join_queries(parts, block_slot, pattern, local_blocks, n_feat, n_rep, *others):
-    n_group = len(parts)
-    n_cluster, part, width = parts[0].shape
+    n_group, n_cluster = len(parts), len(parts[0])
+    _, part, width = parts[0][0].shape
     n_list = pattern.shape[1]
     total = n_list * n_group * part
     share = total // (n_feat * n_rep)
     unit = min(share, part)
+    half = total // n_rep
 
     def kernel(pattern_ref, slot_ref, *refs):
         outs, rows_ref = refs[-1 - n_rep:-1], refs[-1]
@@ -98,13 +125,15 @@
             hops = lax.rem(me + (n_cluster - owner), jnp.int32(n_cluster))
             for d in range(n_group):
                 origin = lax.rem(group + (n_group - d), jnp.int32(n_group))
-                for u in range(part // unit):
-                    first = (k * n_group + origin) * part + u * unit
-                    chunk = lax.div(first, jnp.int32(share))
-                    goal = lax.rem(chunk, jnp.int32(n_rep)) * n_feat + lax.div(chunk, jnp.int32(n_rep))
-                    goal = goal * share + lax.rem(first, jnp.int32(share))
-                    rows_ref[pl.ds(pl.multiple_of(goal, unit), unit), :] = refs[d][hops, u * unit:(u + 1) * unit, :]
-        half = total // n_rep
+                for h in range(n_cluster):
+                    @pl.when(hops == h)
+                    def _():
+                        for u in range(part // unit):
+                            first = (k * n_group + origin) * part + u * unit
+                            chunk = lax.div(first, jnp.int32(share))
+                            goal = lax.rem(chunk, jnp.int32(n_rep)) * n_feat + lax.div(chunk, jnp.int32(n_rep))
+                            goal = pl.multiple_of(goal * share + lax.rem(first, jnp.int32(share)), unit)
+                            rows_ref[pl.ds(goal, unit), :] = refs[d * n_cluster + h][0, u * unit:(u + 1) * unit, :]
         for r in range(n_rep):
             @pl.when(lax.axis_index("rep") == r)
             def _():
@@ -114,14 +143,14 @@
 
     return pl.pallas_call(
         kernel,
-        in_specs=[SMEM, SMEM] + [VMEM] * n_group + [ANY] * len(others),
+        in_specs=[SMEM, SMEM] + [VMEM] * (n_group * n_cluster) + [ANY] * len(others),
         out_specs=[VMEM] * n_rep,
-        out_shape=[jax.ShapeDtypeStruct((width, total // n_rep), BF16)] * n_rep,
+        out_shape=[jax.ShapeDtypeStruct((width, half), BF16)] * n_rep,
         scratch_shapes=[pltpu.VMEM((total, width), BF16)],
         cost_estimate=cost(0, 4 * total * width),
         compiler_params=PARAMS,
         name="join_queries",
-    )(pattern, block_slot, *parts, *others)
+    )(pattern, block_slot, *[x for line in parts for x in line], *others)
 
 
 def select(goal_ref, train_ref, base, size):
@@ -308,10 +337,27 @@
     return total.reshape(total.shape[0] // 8, 8, total.shape[1])
 
 
-def early_scores(own, others, mine, pieces, firsts, seconds, table, rows, n_rep, n_shard, bulk, extra):
+def for_feats(value, outs):
+    n = len(outs)
+    share = outs[0].shape[1]
+    for f in range(n):
+        @pl.when(lax.axis_index("feat") == f)
+        def _():
+            for d, out in enumerate(outs):
+                at = ((f + d) % n) * share
+                out[...] = value(slice(at, at + share)).astype(out.dtype)
+
+
+def feat_shapes(rows, width, n_feat):
+    share = (rows, width // n_feat)
+    return [jax.ShapeDtypeStruct(share, F32)] + [jax.ShapeDtypeStruct(share, BF16)] * (n_feat - 1)
+
+
+def early_scores(own, others, mine, pieces, cuts, firsts, seconds, table, rows, n_feat, n_rep, n_shard, bulk, extra):
     depth, width = own.shape
     columns = depth // n_rep
     n_other, n_piece = len(others), len(pieces)
+    n_first = len(firsts) * n_rep
     last_hops = n_shard - 1
 
     def kernel(table_ref, *refs):
@@ -320,8 +366,8 @@
         mine_ref, refs = refs[0], refs[1:]
         piece_refs = [refs[j * n_rep:(j + 1) * n_rep] for j in range(n_piece)]
         refs = refs[n_piece * n_rep:]
-        first_refs, second_refs = refs[:len(firsts)], refs[len(firsts):len(firsts) + len(seconds)]
-        high_ref, low_ref, out_ref, scored, held, acc, sem = refs[len(firsts) + len(seconds):]
+        first_refs, second_refs, refs = refs[:n_first], refs[n_first:2 * n_first], refs[2 * n_first:]
+        high_ref, low_ref, outs, (scored, held, acc, sem) = refs[0], refs[1], refs[2:-4], refs[-4:]
         me, rep = lax.axis_index("shard"), lax.axis_index("rep")
         weight = own_ref[...]
         for ref in other_refs:
@@ -331,9 +377,9 @@
         low_ref[...] = (weight - high.astype(F32)).astype(BF16)
 
         scored[me] = score(high_ref, low_ref, [mine_ref[...]], jnp.int32(0))
-        for j, parts in enumerate(piece_refs):
-            source = lax.rem(me + (n_shard - 1 - j), jnp.int32(n_shard))
-            scored[source] = score(high_ref, low_ref, [p[...] for p in parts], rep)
+        for parts, (hops, first, size) in zip(piece_refs, cuts):
+            source = lax.rem(me + (n_shard - hops), jnp.int32(n_shard))
+            scored[source, first // 8:(first + size) // 8] = score(high_ref, low_ref, [p[...] for p in parts], rep)
         last = lax.rem(me + (n_shard - last_hops), jnp.int32(n_shard))
         for s in range(n_shard):
             start = table_ref[s, 0]
@@ -346,28 +392,32 @@
                 @pl.when(table_ref[s, 3] > 0)
                 def _():
                     apart = jnp.bitwise_xor(me, s)
-                    index = jnp.bitwise_and(apart, 1) * 2 + lax.div(apart, jnp.int32(2))
-                    rows_in = pl.ds(pl.multiple_of(index * extra, extra), extra)
-                    copies = []
-                    for j, ref in enumerate([*first_refs, *second_refs]):
-                        r, d = j // n_rep, j % n_rep
-                        goal = held.at[d, r * extra:(r + 1) * extra]
-                        copies.append(pltpu.make_async_copy(ref.at[rows_in], goal, sem.at[j]))
-                    for copy in copies:
-                        copy.start()
-                    for copy in copies:
-                        copy.wait()
+                    rows_in = pl.ds(pl.multiple_of(lax.div(apart, jnp.int32(2)) * extra, extra), extra)
+                    for odd in range(2):
+                        @pl.when(jnp.bitwise_and(apart, 1) == odd)
+                        def _():
+                            copies = []
+                            for j, refs in enumerate([first_refs, second_refs]):
+                                for d in range(n_rep):
+                                    goal = held.at[d, j * extra:(j + 1) * extra]
+                                    which = refs[odd * n_rep + d].at[rows_in]
+                                    copies.append(pltpu.make_async_copy(which, goal, sem.at[j * n_rep + d]))
+                            for copy in copies:
+                                copy.start()
+                            for copy in copies:
+                                copy.wait()
                     some = pl.ds(pl.multiple_of(table_ref[s, 2] * 16, 16), extra)
                     x = [held[d, some, :] for d in range(n_rep)]
                     put(acc, score(high_ref, low_ref, x, rep), start + table_ref[s, 1])
-        out_ref[...] = acc[:rows // 8].reshape(rows, width)
+        for_feats(lambda at: acc[:rows // 8, :, at].reshape(rows, width // n_feat), outs)
 
     count = n_shard * bulk
-    return pl.pallas_call(
-        kernel,
-        in_specs=[SMEM] + [VMEM] * (2 + n_other + n_rep * n_piece) + [ANY] * (len(firsts) + len(seconds)),
-        out_specs=[VMEM] * 3,
-        out_shape=[jax.ShapeDtypeStruct((depth, width), BF16)] * 2 + [jax.ShapeDtypeStruct((rows, width), F32)],
+    surplus = [x for parts in [*firsts, *seconds] for x in parts]
+    return pl.pallas_call(
+        kernel,
+        in_specs=[SMEM] + [VMEM] * (2 + n_other + n_rep * n_piece) + [ANY] * len(surplus),
+        out_specs=[VMEM] * (2 + n_feat),
+        out_shape=[jax.ShapeDtypeStruct((depth, width), BF16)] * 2 + feat_shapes(rows, width, n_feat),
         scratch_shapes=[
             pltpu.VMEM((n_shard, bulk // 8, 8, width), F32),
             pltpu.VMEM((n_rep, 3 * extra + 16, columns), BF16),
@@ -377,22 +427,25 @@
         cost_estimate=cost(4 * count * depth * width, 10 * depth * width + count * (2 * depth + 4 * width)),
         compiler_params=PARAMS,
         name="early_scores",
-    )(table, own, *others, mine, *[p for parts in pieces for p in parts], *firsts, *seconds)
-
-
-def late_scores(parts, high, low):
+    )(table, own, *others, mine, *[p for parts in pieces for p in parts], *surplus)
+
+
+def late_scores(parts, high, low, n_feat):
     rows = parts[0].shape[0]
     width = high.shape[1]
 
     def kernel(high_ref, low_ref, *refs):
-        y = score(high_ref, low_ref, [ref[...] for ref in refs[:-1]], lax.axis_index("rep"))
-        refs[-1][...] = y.reshape(rows, width)
+        part_refs, outs, acc = refs[:len(parts)], refs[len(parts):-1], refs[-1]
+        y = score(high_ref, low_ref, [ref[...] for ref in part_refs], lax.axis_index("rep"))
+        acc[...] = y.reshape(rows, width)
+        for_feats(lambda at: acc[:, at], outs)
 
     return pl.pallas_call(
         kernel,
         in_specs=[VMEM] * (2 + len(parts)),
-        out_specs=VMEM,
-        out_shape=jax.ShapeDtypeStruct((rows, width), F32),
+        out_specs=[VMEM] * n_feat,
+        out_shape=feat_shapes(rows, width, n_feat),
+        scratch_shapes=[pltpu.VMEM((rows, width), F32)],
         cost_estimate=cost(4 * rows * high.size, 8 * rows * width),
         compiler_params=PARAMS,
         name="late_scores",
@@ -453,36 +506,34 @@
     picked = pick_queries(query_store, block_slot, pattern, n_group)
     pieces = [picked[0]] + [shift(picked[d], "shard", n_shard, d) for d in range(1, n_shard)]
 
-    *packed, goal = pack_rows(train, ids, columns, bulk, extra, [(d, 0, bulk) for d in range(1, n_shard)])
-    sent = dict(zip(range(1, n_shard), packed))
+    middle = [(d, 0, bulk) for d in range(1, last_hops)]
+    if extra:
+        middle = middle[:-1] + [(last_hops - 1, j * bulk // 2, bulk // 2) for j in range(2)]
+    *packed, goal = pack_rows(train, ids, columns, bulk, extra, middle + [(last_hops, 0, bulk)])
     table, flag = row_table(ids, lines, bulk, extra)
-
-    def swap_far(x):
-        return jnp.concatenate([x, swap(x, "shard", n_shard, 2)])
-
-    def swap_near(x):
-        return jnp.concatenate([x, swap(x, "shard", n_shard, 1)])
-
     mine = own_rows(goal, train, bulk)
     before_join, firsts, seconds = [mine], [], []
     if extra:
         for d in range(1, n_group):
             flag = jnp.maximum(flag, shift(flag, "groups", n_group, d))
-        seconds = lax.cond(
-            flag[0, 0] > 0,
-            lambda x: with_rep(swap_near(swap_far(x))),
-            lambda x: [jnp.zeros((n_shard * extra, columns), BF16)] * n_rep,
-            packed[-1],
-        )
+
+        def second_round(x):
+            pair = jnp.concatenate([x, swap(x, "shard", n_shard, 2)])
+            return [with_rep(pair), with_rep(swap(pair, "shard", n_shard, 1))]
+
+        def no_round(x):
+            return [[jnp.zeros((2 * extra, columns), BF16)] * n_rep] * 2
+
+        seconds = lax.cond(flag[0, 0] > 0, second_round, no_round, packed[-1])
         far = swap(packed[-2], "shard", n_shard, 2)
-        before_join = [far, mine, *seconds]
-        firsts = with_rep(swap_near(jnp.concatenate([packed[-2], far])))
-
-    arrived = after(jnp.concatenate(pieces), sent[1], flag)
-    parts = [arrived] + [shift(arrived, "groups", n_group, d) for d in range(1, n_group)]
+        before_join += [far] + [x for parts in seconds for x in parts]
+
+    final = after(pieces[n_shard // 2], packed[0], flag, *[x for d, x in enumerate(pieces) if d != n_shard // 2])
+    pieces = [final if d == n_shard // 2 else x for d, x in enumerate(pieces)]
+    parts = [pieces] + [[shift(x, "groups", n_group, d) for x in pieces] for d in range(1, n_group)]
     chosen = join_queries(parts, block_slot, pattern, query_store.shape[0], n_feat, n_rep, *before_join)
     queries = [chosen[0]] + [shift(chosen[d], "rep", n_rep, d) for d in range(1, n_rep)]
-    here = {1: shift(after(sent[1], *before_join[:1]), "shard", n_shard, 1)}
+    here = [shift(after(packed[0], *before_join[1:2]), "shard", n_shard, 1)]
 
     def weights(f, dtype, *others):
         return partial_weights(matrices, queries, f, n_rep * columns, dtype, *others)
@@ -491,26 +542,23 @@
     others = [shift(x, "feat", n_feat, d + 1) for d, x in enumerate(sends)]
     own = weights(feat, F32, *sends)
 
-    for d in range(2, last_hops):
-        here[d] = shift(after(sent[d], own), "shard", n_shard, d)
-    last = shift(after(sent[last_hops], here[last_hops - 1]), "shard", n_shard, last_hops)
-
-    ready = [with_rep(here[d]) for d in range(1, last_hops)]
-    high, low, early = early_scores(
-        own, others, mine, ready, firsts, seconds, table, rows, n_rep, n_shard, bulk, extra
+    for (hops, _, _), x in zip(middle[1:], packed[1:]):
+        here.append(shift(after(x, own), "shard", n_shard, hops))
+    last = shift(after(packed[len(middle)], *here[1:]), "shard", n_shard, last_hops)
+    if extra:
+        pair = stack([packed[-2], far], chosen[0])
+        firsts = [with_rep(pair), with_rep(swap(pair, "shard", n_shard, 1))]
+
+    ready = [with_rep(after(x, own)) for x in here[:1]] + [with_rep(x) for x in here[1:]]
+    high, low, *early = early_scores(
+        own, others, mine, ready, middle, firsts, seconds, table, rows, n_feat, n_rep, n_shard, bulk, extra
     )
 
-    def for_feat(total, d):
-        share = total.shape[1] // n_feat
-        return lax.dynamic_slice_in_dim(total, ((feat + d) % n_feat) * share, share, 1)
-
-    def over_feat(total, sends):
-        return [for_feat(total, 0)] + [shift(x, "feat", n_feat, d + 1) for d, x in enumerate(sends)]
-
-    early_sends = [for_feat(early, d).astype(BF16) for d in range(1, n_feat)]
-    late = late_scores(with_rep(after(last, *early_sends)), high, low)
-    late_sends = [for_feat(late, d).astype(BF16) for d in range(1, n_feat)]
-    return merge(table, over_feat(early, early_sends), over_feat(late, late_sends), n_shard)[None]
+    def over_feat(shares):
+        return [shares[0]] + [shift(shares[d], "feat", n_feat, d) for d in range(1, n_feat)]
+
+    late = late_scores(with_rep(after(last, *early[1:])), high, low, n_feat)
+    return merge(table, over_feat(early), over_feat(late), n_shard)[None]
 
 
 def solution(mesh):

time: 120 us -> 119 us (level)
  Pallas kernels: 35.3 us -> 26.5 us
  local copies, waits for them, and re-layouts: 11.8 us -> 18.5 us
  starting transfers between devices: 18.1 us -> 23.9 us
  waiting for transfers between devices: 51.8 us -> 48.7 us
  other arithmetic: 1.83 us -> 0.01 us
    unnamed x18 -> x30, local copies, waits for them, and re-layouts: 5.02 us -> 14.5 us
    ppermute x2, waiting for transfers between devices: 13.3 us -> 3.85 us  [swap(): return lax.ppermute(x, axis, [(i, i ^ bit) for i in range(size)])]
    ppermute x17 -> x23, waiting for transfers between devices: 38.5 us -> 44.9 us  [shift(): return lax.ppermute(x, axis, [(i, (i + by) % size) for i in range(size)])]
    ppermute x17 -> x23, starting transfers between devices: 15.7 us -> 19.5 us  [shift(): return lax.ppermute(x, axis, [(i, (i + by) % size) for i in range(size)])]
    pallas_call x2, Pallas kernels: 12 us -> 9.45 us  [partial_weights(): pl.pallas_call(kernel, grid_spec=pltpu.PrefetchScalarGridSpec(num_scalar_...]
    pallas_call x1, Pallas kernels: 7.23 us -> 5.03 us  [early_scores(): pl.pallas_call(kernel, in_specs=[SMEM] + [VMEM] * (2 + n_other + n_rep *...]
    pallas_call x1, Pallas kernels: 3.46 us -> 1.27 us  [own_rows(): pl.pallas_call(kernel, in_specs=[VMEM] * 2, out_specs=VMEM, out_shape=jax...]
    pallas_call x1, Pallas kernels: 4.74 us -> 2.73 us  [pack_rows(): pl.pallas_call(kernel, grid=(1,), in_specs=[pl.BlockSpec((lines, LANES),...]
  transfers between devices with their start and end apart: 19 -> 25, of which waited for: 8 -> 14; matrix products, arithmetic and copies ran while one was open for 8% -> 3% of each run, Pallas kernels for 28% -> 21%
where the time goes in v7:
time: 119 us
  waiting for transfers between devices  48.7 us (41%)
  Pallas kernels  26.5 us (22%)
  starting transfers between devices  23.9 us (20%)
  local copies, waits for them, and re-layouts  18.5 us (16%)
    ppermute x23, waiting for transfers between devices, shift(): return lax.ppermute(x, axis, [(i, (i + by) % size) for i in range(size)])  44.9 us
    ppermute x23, starting transfers between devices, shift(): return lax.ppermute(x, axis, [(i, (i + by) % size) for i in range(size)])  19.5 us
    unnamed x30, local copies, waits for them, and re-layouts  14.5 us
    pallas_call x2, Pallas kernels, partial_weights(): pl.pallas_call(kernel, grid_spec=pltpu.PrefetchScalarGridSpec(num_scalar_...  9.45 us
    pallas_call x1, Pallas kernels, early_scores(): pl.pallas_call(kernel, in_specs=[SMEM] + [VMEM] * (2 + n_other + n_rep *...  5.03 us
    ppermute x2, starting transfers between devices, swap(): return lax.ppermute(x, axis, [(i, i ^ bit) for i in range(size)])  4.4 us
    ppermute x2, waiting for transfers between devices, swap(): return lax.ppermute(x, axis, [(i, i ^ bit) for i in range(size)])  3.85 us
    another operation x4, local copies, waits for them, and re-layouts  3.44 us
  transfers between devices with their start and end apart: 25, of which 14 were waited for; matrix products, arithmetic and copies ran while one was open for 3% of the time, Pallas kernels for 21%

profile of v7, /device:TPU:0, one launch (start us, length us, event | category | flops | bytes accessed | tf_op | source)
XLA Modules:
  0.0 118.5 jit_solution(6715766088833557454)
XLA Ops:
  0.5 2.7 %pick_queries.1 = (bf16[1,64,1024]{2,1,0:T(8,128)(2,1)}, bf16[1,64,1024]{2,1,0:T(8,128)(2,1)}, bf16[1,64,1024]{2,1,0:T(8,128)(2,1)}, bf16[1,64,1024]{2,1,0:T(8,128)(2,1)}) custom-call(s32[4,4]{1,0:T(4,128)} %pattern_ref.3, s32[16]{0:T(128)} %slot_ref.3, bf16[4,128,1024]{2,1,0:T(8,128)(2,1)} %in_ref.1), custom_call_target="tpu_custom_call" | custom-call | flops 1 | bytes 1 | tf_op jit(solution)/shard_map/pick_queries/pallas_call | solution.py:99
  3.2 2.8 %collective-permute-start.5 = (bf16[1,64,1024]{2,1,0:T(8,128)(2,1)}, bf16[1,64,1024]{2,1,0:T(8,128)(2,1)S(1)}, u32[]{:S(2)}, u32[]{:S(2)}) collective-permute-start(bf16[1,64,1024]{2,1,0:T(8,128)(2,1)} %get-tuple-element.33), channel_id=1, source_target_pairs={{0,4},{4,8},{8,12},{12,0},{1,5},{5,9},{9,13},{13,1},{2,6},{6,10},{... | collective-permute-start | bytes 393224 | tf_op jit(solution)/shard_map/ppermute | solution.py:20
  5.9 0.7 copy-done.12
  6.7 0.8 row_table.1
  7.5 1.6 %collective-permute-start.7 = (s32[8,128]{1,0:T(8,128)S(1)}, s32[8,128]{1,0:T(8,128)S(1)}, u32[]{:S(2)}, u32[]{:S(2)}) collective-permute-start(s32[8,128]{1,0:T(8,128)S(1)} %get-tuple-element.36), channel_id=1, source_target_pairs={{0,16},{16,0},{1,17},{17,1},{2,18},{18,2},{3,19},{19,3},{4,20},{20... | collective-permute-start | bytes 12296 | tf_op jit(solution)/shard_map/ppermute | solution.py:20
  9.1 2.6 %collective-permute-start.6 = (bf16[1,64,1024]{2,1,0:T(8,128)(2,1)}, bf16[1,64,1024]{2,1,0:T(8,128)(2,1)S(1)}, u32[]{:S(2)}, u32[]{:S(2)}) collective-permute-start(bf16[1,64,1024]{2,1,0:T(8,128)(2,1)} %get-tuple-element.34), channel_id=1, source_target_pairs={{0,8},{4,12},{8,0},{12,4},{1,9},{5,13},{9,1},{13,5},{2,10},{6,14},... | collective-permute-start | bytes 393224 | tf_op jit(solution)/shard_map/ppermute | solution.py:20
  11.7 2.2 %copy-done.2 = bf16[1024,2048]{1,0:T(8,128)(2,1)S(1)} copy-done((bf16[1024,2048]{1,0:T(8,128)(2,1)S(1)}, bf16[1024,2048]{1,0:T(8,128)(2,1)}, u32[]{:S(2)}) %copy-start.2) | copy-done | bytes 4194328
  13.9 2.7 %pack_rows.1 = (bf16[256,1024]{1,0:T(8,128)(2,1)S(1)}, bf16[128,1024]{1,0:T(8,128)(2,1)S(1)}, bf16[128,1024]{1,0:T(8,128)(2,1)S(1)}, bf16[256,1024]{1,0:T(8,128)...) custom-call(s32[32,128]{1,0:T(8,128)S(1)} %bitcast.10, ...), custom_call_target="tpu_custom_call" | custom-call | flops 1 | bytes 1 | tf_op jit(solution)/shard_map/pack_rows/pallas_call | solution.py:227
  16.6 0.8 copy-done.4
  17.4 0.6 slice.3
  18.6 3.5 %conditional.1 = (bf16[256,1024]{1,0:T(8,128)(2,1)}, bf16[256,1024]{1,0:T(8,128)(2,1)}, bf16[256,1024]{1,0:T(8,128)(2,1)}, bf16[256,1024]{1,0:T(8,128)(2,1)}) conditional(s32[]{:T(128)} %bitcast.3, () %tuple.13, bf16[128,1024]{1,0:T(8,128)(2,1)S(1)} %get-tuple-element.40), branch_computations={%region_0.0_spmd, %region_1.0_spmd} | conditional | bytes 8388800 | solution.py:527
  18.6 0.9 broadcast.3
  19.5 0.9 broadcast.3.clone
  20.4 0.9 broadcast.3.clone.1
  21.2 0.9 broadcast.3.clone.2
  22.1 1.3 %collective-permute-start.8 = (bf16[1,64,1024]{2,1,0:T(8,128)(2,1)}, bf16[1,64,1024]{2,1,0:T(8,128)(2,1)S(1)}, u32[]{:S(2)}, u32[]{:S(2)}) collective-permute-start(bf16[1,64,1024]{2,1,0:T(8,128)(2,1)} %get-tuple-element.37), channel_id=1, source_target_pairs={{0,12},{4,0},{8,4},{12,8},{1,13},{5,1},{9,5},{13,9},{2,14},{6,2},{... | collective-permute-start | bytes 393224 | tf_op jit(solution)/shard_map/ppermute | solution.py:20
  24.1 3.6 %collective-permute-done.8.refs_5_.refs_3_ = bf16[1,64,1024]{2,1,0:T(8,128)(2,1)S(1)} collective-permute-done((bf16[1,64,1024]{2,1,0:T(8,128)(2,1)}, bf16[1,64,1024]{2,1,0:T(8,128)(2,1)S(1)}, u32[]{:S(2)}, u32[]{:S(2)}) %collective-permute-start.8) | collective-permute-done | bytes 131104 | tf_op jit(solution)/shard_map/ppermute | solution.py:20
  27.7 0.9 copy-done.6
  29.2 1.5 %collective-permute-start.10 = (bf16[1,64,1024]{2,1,0:T(8,128)(2,1)S(1)}, bf16[1,64,1024]{2,1,0:T(8,128)(2,1)S(1)}, u32[]{:S(2)}, u32[]{:S(2)}) collective-permute-start(bf16[1,64,1024]{2,1,0:T(8,128)(2,1)S(1)} %collective-permute-done.5.refs_4_.refs_1_), channel_id=1, source_target_pairs={{0,16},{16,0},{1,17},{17,1},{2,18},{18,2},{3,19},{19,3},{4,20},{20... | collective-permute-start | bytes 393224 | tf_op jit(solution)/shard_map/ppermute | solution.py:20
  30.6 0.5 collective-permute-start.12
  31.2 2.2 %copy-done.3 = bf16[1024,2048]{1,0:T(8,128)(2,1)S(1)} copy-done((bf16[1024,2048]{1,0:T(8,128)(2,1)S(1)}, bf16[1024,2048]{1,0:T(8,128)(2,1)}, u32[]{:S(2)}) %copy-start.3) | copy-done | bytes 4194328
  33.4 1.3 %own_rows.1.refs_8_.refs_2_ = bf16[256,2048]{1,0:T(8,128)(2,1)S(1)} custom-call(s32[8,128]{1,0:T(8,128)S(1)} %get-tuple-element.38.goal_ref, bf16[1024,2048]{1,0:T(8,128)(2,1)S(1)} %copy-done.3), custom_call_target="tpu_custom_call" | custom-call | flops 1 | bytes 1 | tf_op jit(solution)/shard_map/own_rows/pallas_call | solution.py:170
  34.7 1.5 %collective-permute-done.10.refs_5_ = bf16[1,64,1024]{2,1,0:T(8,128)(2,1)S(1)} collective-permute-done((bf16[1,64,1024]{2,1,0:T(8,128)(2,1)S(1)}, bf16[1,64,1024]{2,1,0:T(8,128)(2,1)S(1)}, u32[]{:S(2)}, u32[]{:S(2)}) %collective-permute-start.10) | collective-permute-done | bytes 131104 | tf_op jit(solution)/shard_map/ppermute | solution.py:20
  36.1 1.4 %collective-permute-done.12.refs_7_ = bf16[1,64,1024]{2,1,0:T(8,128)(2,1)S(1)} collective-permute-done((bf16[1,64,1024]{2,1,0:T(8,128)(2,1)S(1)}, bf16[1,64,1024]{2,1,0:T(8,128)(2,1)S(1)}, u32[]{:S(2)}, u32[]{:S(2)}) %collective-permute-start.12) | collective-permute-done | bytes 131104 | tf_op jit(solution)/shard_map/ppermute | solution.py:20
  37.5 0.6 collective-permute-done.13.refs_9_.refs_1_
  38.2 2.0 %join_queries.1 = (bf16[1024,256]{1,0:T(8,128)(2,1)S(1)}, bf16[1024,256]{1,0:T(8,128)(2,1)}) custom-call(s32[4,4]{1,0:T(4,128)S(1)} %copy-done.13, s32[16]{0:T(128)S(1)} %copy-done.14, bf16[1,64,1024]{2,1,0:T(8,128)(2,1)S(1)} %copy-done.7, bf16[1,64,1024]{2,1,0:T(8,128)(2,1)S(1)} %collective-permute-done.5.refs_4_.refs_1_, ...), custom_call_target="tpu_custom_call" | custom-call | flops 1 | bytes 1 | tf_op jit(solution)/shard_map/join_queries/pallas_call | solution.py:144
  40.2 0.9 copy-done.11
  41.2 4.3 %collective-permute-start.23 = (bf16[256,1024]{1,0:T(8,128)(2,1)S(1)}, bf16[256,1024]{1,0:T(8,128)(2,1)}, u32[]{:S(2)}, u32[]{:S(2)}) collective-permute-start(bf16[256,1024]{1,0:T(8,128)(2,1)S(1)} %stack.1.refs_9_), channel_id=1, source_target_pairs={{0,4},{4,0},{8,12},{12,8},{1,5},{5,1},{9,13},{13,9},{2,6},{6,2},{1... | collective-permute-start | bytes 1572872 | tf_op jit(solution)/shard_map/ppermute | solution.py:24
  45.6 3.4 %copy-done = bf16[1,4096,1024]{2,1,0:T(8,128)(2,1)S(1)} copy-done((bf16[1,4096,1024]{2,1,0:T(8,128)(2,1)S(1)}, bf16[1,4096,1024]{2,1,0:T(8,128)(2,1)}, u32[]{:S(2)}) %copy-start) | copy-done | bytes 8388632
  49.0 4.7 %partial_weights.2.refs_4_ = bf16[2048,256]{1,0:T(8,128)(2,1)S(1)} custom-call(s32[1]{0:T(128)} %bitcast.4.block_ref, bf16[4096,1024]{1,0:T(8,128)(2,1)S(1)} %bitcast.7, bf16[4096,1024]{1,0:T(8,128)(2,1)} %collective-permute-done.4.refs_1_, bf16[1024,256]{1,0:T(8,128)(2,1)S(1)} %get-tuple-element.45.refs_2_, ...), custom_call_target="tpu_custom_call" | custom-call | flops 1 | bytes 1 | tf_op jit(solution)/shard_map/partial_weights/pallas_call | solution.py:254
  53.7 1.6 %collective-permute-start.15 = (bf16[2048,256]{1,0:T(8,128)(2,1)S(1)}, bf16[2048,256]{1,0:T(8,128)(2,1)S(1)}, u32[]{:S(2)}, u32[]{:S(2)}) collective-permute-start(bf16[2048,256]{1,0:T(8,128)(2,1)S(1)} %partial_weights.2.refs_4_), channel_id=1, source_target_pairs={{0,2},{2,0},{1,3},{3,1},{4,6},{6,4},{5,7},{7,5},{8,10},{10,8},{9,1... | collective-permute-start | bytes 3145736 | tf_op jit(solution)/shard_map/ppermute | solution.py:20
  55.2 3.2 %collective-permute-done.23.refs_11_ = bf16[256,1024]{1,0:T(8,128)(2,1)} collective-permute-done((bf16[256,1024]{1,0:T(8,128)(2,1)S(1)}, bf16[256,1024]{1,0:T(8,128)(2,1)}, u32[]{:S(2)}, u32[]{:S(2)}) %collective-permute-start.23) | collective-permute-done | bytes 524320 | tf_op jit(solution)/shard_map/ppermute | solution.py:24
  58.5 3.4 %copy-done.1 = bf16[1,4096,1024]{2,1,0:T(8,128)(2,1)S(1)} copy-done((bf16[1,4096,1024]{2,1,0:T(8,128)(2,1)S(1)}, bf16[1,4096,1024]{2,1,0:T(8,128)(2,1)}, u32[]{:S(2)}) %copy-start.1) | copy-done | bytes 8388632
  61.9 4.7 %partial_weights.3.refs_1_.refs_0_ = f32[2048,256]{1,0:T(8,128)S(1)} custom-call(s32[1]{0:T(128)} %bitcast.1.block_ref, bf16[4096,1024]{1,0:T(8,128)(2,1)S(1)} %bitcast.8, bf16[4096,1024]{1,0:T(8,128)(2,1)} %collective-permute-done.4.refs_1_, bf16[1024,256]{1,0:T(8,128)(2,1)S(1)} %get-tuple-element.45.refs_2_, ...), custom_call_target="tpu_custom_call" | custom-call | flops 1 | bytes 1 | tf_op jit(solution)/shard_map/partial_weights/pallas_call | solution.py:254
  66.6 0.9 collective-permute-start.18
  67.5 2.0 %collective-permute-done.16.refs_0_ = bf16[256,1024]{1,0:T(8,128)(2,1)} collective-permute-done((bf16[256,1024]{1,0:T(8,128)(2,1)S(1)}, bf16[256,1024]{1,0:T(8,128)(2,1)}, u32[]{:S(2)}, u32[]{:S(2)}) %collective-permute-start.16) | collective-permute-done | bytes 524320 | tf_op jit(solution)/shard_map/ppermute | solution.py:20
  69.6 18.3 %collective-permute-done.18.refs_5_.refs_1_ = bf16[128,1024]{1,0:T(8,128)(2,1)S(1)} collective-permute-done((bf16[128,1024]{1,0:T(8,128)(2,1)S(1)}, bf16[128,1024]{1,0:T(8,128)(2,1)S(1)}, u32[]{:S(2)}, u32[]{:S(2)}) %collective-permute-start.18) | collective-permute-done | bytes 262176 | tf_op jit(solution)/shard_map/ppermute | solution.py:20
  87.9 5.2 %collective-permute-done.20.refs_7_.refs_2_ = bf16[128,1024]{1,0:T(8,128)(2,1)S(1)} collective-permute-done((bf16[128,1024]{1,0:T(8,128)(2,1)S(1)}, bf16[128,1024]{1,0:T(8,128)(2,1)S(1)}, u32[]{:S(2)}, u32[]{:S(2)}) %collective-permute-start.20) | collective-permute-done | bytes 262176 | tf_op jit(solution)/shard_map/ppermute | solution.py:20
  93.2 1.6 %collective-permute-start.26 = (bf16[256,1024]{1,0:T(8,128)(2,1)S(1)}, bf16[256,1024]{1,0:T(8,128)(2,1)S(1)}, u32[]{:S(2)}, u32[]{:S(2)}) collective-permute-start(bf16[256,1024]{1,0:T(8,128)(2,1)S(1)} %after.12), channel_id=1, source_target_pairs={{0,12},{4,0},{8,4},{12,8},{1,13},{5,1},{9,5},{13,9},{2,14},{6,2},{... | collective-permute-start | bytes 1572872 | tf_op jit(solution)/shard_map/ppermute | solution.py:20
  95.3 1.0 collective-permute-done.19.refs_6_
  96.7 5.0 %early_scores.1 = (bf16[2048,256]{1,0:T(8,128)(2,1)S(1)}, bf16[2048,256]{1,0:T(8,128)(2,1)S(1)}, f32[1024,128]{1,0:T(8,128)S(1)}, bf16[1024,128]{1,0:T(8,128)(2,1)S(1)}) custom-call(s32[4,4]{1,0:T(4,128)S(1)} %get-tuple-element.31.table_ref, f32[2048,256]{1,0:T(8,128)S(1)} %partial_weights.3.refs_1_.refs_0_, ...), custom_call_target="tpu_custom_call" | custom-call | flops 1 | bytes 1 | tf_op jit(solution)/shard_map/early_scores/pallas_call | solution.py:416
  101.7 5.0 %collective-permute-done.26.refs_0_ = bf16[256,1024]{1,0:T(8,128)(2,1)S(1)} collective-permute-done((bf16[256,1024]{1,0:T(8,128)(2,1)S(1)}, bf16[256,1024]{1,0:T(8,128)(2,1)S(1)}, u32[]{:S(2)}, u32[]{:S(2)}) %collective-permute-start.26) | collective-permute-done | bytes 524320 | tf_op jit(solution)/shard_map/ppermute | solution.py:20
  106.7 1.5 %collective-permute-start.25 = (bf16[1024,128]{1,0:T(8,128)(2,1)S(1)}, bf16[1024,128]{1,0:T(8,128)(2,1)S(1)}, u32[]{:S(2)}, u32[]{:S(2)}) collective-permute-start(bf16[1024,128]{1,0:T(8,128)(2,1)S(1)} %get-tuple-element.50.refs_1_), channel_id=1, source_target_pairs={{0,2},{2,0},{1,3},{3,1},{4,6},{6,4},{5,7},{7,5},{8,10},{10,8},{9,1... | collective-permute-start | bytes 786440 | tf_op jit(solution)/shard_map/ppermute | solution.py:20
  108.6 0.7 late_scores.1
  109.4 1.6 %collective-permute-start.28 = (bf16[256,128]{1,0:T(8,128)(2,1)S(1)}, bf16[256,128]{1,0:T(8,128)(2,1)S(1)}, u32[]{:S(2)}, u32[]{:S(2)}) collective-permute-start(bf16[256,128]{1,0:T(8,128)(2,1)S(1)} %get-tuple-element.55), channel_id=1, source_target_pairs={{0,2},{2,0},{1,3},{3,1},{4,6},{6,4},{5,7},{7,5},{8,10},{10,8},{9,1... | collective-permute-start | bytes 196616 | tf_op jit(solution)/shard_map/ppermute | solution.py:20
  111.0 4.9 %collective-permute-done.25.refs_1_ = bf16[1024,128]{1,0:T(8,128)(2,1)S(1)} collective-permute-done((bf16[1024,128]{1,0:T(8,128)(2,1)S(1)}, bf16[1024,128]{1,0:T(8,128)(2,1)S(1)}, u32[]{:S(2)}, u32[]{:S(2)}) %collective-permute-start.25) | collective-permute-done | bytes 262176 | tf_op jit(solution)/shard_map/ppermute | solution.py:20
  115.8 1.0 collective-permute-done.28.refs_3_
  116.9 1.7 %merge.1 = f32[128,1024]{1,0:T(8,128)} custom-call(s32[4,4]{1,0:T(4,128)S(1)} %get-tuple-element.31.table_ref, f32[1024,128]{1,0:T(8,128)S(1)} %get-tuple-element.49.refs_0_, bf16[1024,128]{1,0:T(8,128)(2,1)S(1)} %collective-permute-done.25.refs_1_, f32[256,128]{1,0:T(8,128)S(1)} %get-tuple-element.54.refs_2_, ...), custom_call_target="tpu_custom_call" | custom-call | flops 1 | bytes 1 | tf_op jit(solution)/shard_map/merge/pallas_call | solution.py:475
  (57 shorter events, 3.2 us)
Async XLA Ops:
  0.0 38.2 %copy-start.13 = (s32[4,4]{1,0:T(4,128)S(1)}, s32[4,4]{1,0:T(4,128)}, u32[]{:S(2)}) copy-start(s32[4,4]{1,0:T(4,128)} %pattern_ref.3) | copy-start | bytes 196
  0.0 38.2 %copy-start.14 = (s32[16]{0:T(128)S(1)}, s32[16]{0:T(128)}, u32[]{:S(2)}) copy-start(s32[16]{0:T(128)} %slot_ref.3) | copy-start | bytes 196
  0.0 45.6 %collective-permute-start.4 = (bf16[4096,1024]{1,0:T(8,128)(2,1)}, bf16[4096,1024]{1,0:T(8,128)(2,1)}, u32[]{:S(2)}, u32[]{:S(2)}) collective-permute-start(bf16[4096,1024]{1,0:T(8,128)(2,1)} %bitcast.6), channel_id=1, source_target_pairs={{0,1},{1,0},{2,3},{3,2},{4,5},{5,4},{6,7},{7,6},{8,9},{9,8},{10,11... | collective-permute-start | bytes 25165832 | tf_op jit(solution)/shard_map/ppermute | solution.py:20
  3.2 20.8 %collective-permute-start.5 = (bf16[1,64,1024]{2,1,0:T(8,128)(2,1)}, bf16[1,64,1024]{2,1,0:T(8,128)(2,1)S(1)}, u32[]{:S(2)}, u32[]{:S(2)}) collective-permute-start(bf16[1,64,1024]{2,1,0:T(8,128)(2,1)} %get-tuple-element.33), channel_id=1, source_target_pairs={{0,4},{4,8},{8,12},{12,0},{1,5},{5,9},{9,13},{13,1},{2,6},{6,10},{... | collective-permute-start | bytes 393224 | tf_op jit(solution)/shard_map/ppermute | solution.py:20
  5.9 0.7 copy-start.12
  7.5 9.9 %collective-permute-start.7 = (s32[8,128]{1,0:T(8,128)S(1)}, s32[8,128]{1,0:T(8,128)S(1)}, u32[]{:S(2)}, u32[]{:S(2)}) collective-permute-start(s32[8,128]{1,0:T(8,128)S(1)} %get-tuple-element.36), channel_id=1, source_target_pairs={{0,16},{16,0},{1,17},{17,1},{2,18},{18,2},{3,19},{19,3},{4,20},{20... | collective-permute-start | bytes 12296 | tf_op jit(solution)/shard_map/ppermute | solution.py:20
  9.1 15.0 %collective-permute-start.6 = (bf16[1,64,1024]{2,1,0:T(8,128)(2,1)}, bf16[1,64,1024]{2,1,0:T(8,128)(2,1)S(1)}, u32[]{:S(2)}, u32[]{:S(2)}) collective-permute-start(bf16[1,64,1024]{2,1,0:T(8,128)(2,1)} %get-tuple-element.34), channel_id=1, source_target_pairs={{0,8},{4,12},{8,0},{12,4},{1,9},{5,13},{9,1},{13,5},{2,10},{6,14},... | collective-permute-start | bytes 393224 | tf_op jit(solution)/shard_map/ppermute | solution.py:20
  11.7 2.2 %copy-start.2 = (bf16[1024,2048]{1,0:T(8,128)(2,1)S(1)}, bf16[1024,2048]{1,0:T(8,128)(2,1)}, u32[]{:S(2)}) copy-start(bf16[1024,2048]{1,0:T(8,128)(2,1)} %train_ref.3) | copy-start | bytes 12582916
  13.9 24.3 %copy-start.7 = (bf16[1,64,1024]{2,1,0:T(8,128)(2,1)S(1)}, bf16[1,64,1024]{2,1,0:T(8,128)(2,1)}, u32[]{:S(2)}) copy-start(bf16[1,64,1024]{2,1,0:T(8,128)(2,1)} %get-tuple-element.32.refs_3_.refs_0_) | copy-start | bytes 393220
  16.6 0.8 copy-start.4
  17.4 4.7 %copy-start.8 = (bf16[128,1024]{1,0:T(8,128)(2,1)}, bf16[128,1024]{1,0:T(8,128)(2,1)S(1)}, u32[]{:S(2)}) copy-start(bf16[128,1024]{1,0:T(8,128)(2,1)S(1)} %get-tuple-element.47.refs_0_) | copy-start | bytes 786436
  17.4 22.8 %copy-start.10 = (bf16[128,1024]{1,0:T(8,128)(2,1)}, bf16[128,1024]{1,0:T(8,128)(2,1)S(1)}, u32[]{:S(2)}) copy-start(bf16[128,1024]{1,0:T(8,128)(2,1)S(1)} %get-tuple-element.39.refs_0_) | copy-start | bytes 786436
  22.1 5.6 %collective-permute-start.8 = (bf16[1,64,1024]{2,1,0:T(8,128)(2,1)}, bf16[1,64,1024]{2,1,0:T(8,128)(2,1)S(1)}, u32[]{:S(2)}, u32[]{:S(2)}) collective-permute-start(bf16[1,64,1024]{2,1,0:T(8,128)(2,1)} %get-tuple-element.37), channel_id=1, source_target_pairs={{0,12},{4,0},{8,4},{12,8},{1,13},{5,1},{9,5},{13,9},{2,14},{6,2},{... | collective-permute-start | bytes 393224 | tf_op jit(solution)/shard_map/ppermute | solution.py:20
  23.4 7.2 %collective-permute-start.9 = (bf16[1,64,1024]{2,1,0:T(8,128)(2,1)}, bf16[1,64,1024]{2,1,0:T(8,128)(2,1)S(1)}, u32[]{:S(2)}, u32[]{:S(2)}) collective-permute-start(bf16[1,64,1024]{2,1,0:T(8,128)(2,1)} %get-tuple-element.32.refs_3_.refs_0_), channel_id=1, source_target_pairs={{0,16},{16,0},{1,17},{17,1},{2,18},{18,2},{3,19},{19,3},{4,20},{20... | collective-permute-start | bytes 393224 | tf_op jit(solution)/shard_map/ppermute | solution.py:20
  23.9 14.2 %collective-permute-start.13 = (bf16[128,1024]{1,0:T(8,128)(2,1)S(1)}, bf16[128,1024]{1,0:T(8,128)(2,1)S(1)}, u32[]{:S(2)}, u32[]{:S(2)}) collective-permute-start(bf16[128,1024]{1,0:T(8,128)(2,1)S(1)} %get-tuple-element.39.refs_0_), channel_id=1, source_target_pairs={{0,8},{4,12},{8,0},{12,4},{1,9},{5,13},{9,1},{13,5},{2,10},{6,14},... | collective-permute-start | bytes 786440 | tf_op jit(solution)/shard_map/ppermute | solution.py:24
  27.7 0.9 copy-start.6
  28.6 7.5 %collective-permute-start.11 = (bf16[1,64,1024]{2,1,0:T(8,128)(2,1)S(1)}, bf16[1,64,1024]{2,1,0:T(8,128)(2,1)S(1)}, u32[]{:S(2)}, u32[]{:S(2)}) collective-permute-start(bf16[1,64,1024]{2,1,0:T(8,128)(2,1)S(1)} %after.7.refs_2_), channel_id=1, source_target_pairs={{0,16},{16,0},{1,17},{17,1},{2,18},{18,2},{3,19},{19,3},{4,20},{20... | collective-permute-start | bytes 393224 | tf_op jit(solution)/shard_map/ppermute | solution.py:20
  29.2 7.0 %collective-permute-start.10 = (bf16[1,64,1024]{2,1,0:T(8,128)(2,1)S(1)}, bf16[1,64,1024]{2,1,0:T(8,128)(2,1)S(1)}, u32[]{:S(2)}, u32[]{:S(2)}) collective-permute-start(bf16[1,64,1024]{2,1,0:T(8,128)(2,1)S(1)} %collective-permute-done.5.refs_4_.refs_1_), channel_id=1, source_target_pairs={{0,16},{16,0},{1,17},{17,1},{2,18},{18,2},{3,19},{19,3},{4,20},{20... | collective-permute-start | bytes 393224 | tf_op jit(solution)/shard_map/ppermute | solution.py:20
  30.6 6.9 %collective-permute-start.12 = (bf16[1,64,1024]{2,1,0:T(8,128)(2,1)S(1)}, bf16[1,64,1024]{2,1,0:T(8,128)(2,1)S(1)}, u32[]{:S(2)}, u32[]{:S(2)}) collective-permute-start(bf16[1,64,1024]{2,1,0:T(8,128)(2,1)S(1)} %collective-permute-done.8.refs_5_.refs_3_), channel_id=1, source_target_pairs={{0,16},{16,0},{1,17},{17,1},{2,18},{18,2},{3,19},{19,3},{4,20},{20... | collective-permute-start | bytes 393224 | tf_op jit(solution)/shard_map/ppermute | solution.py:20
  31.2 2.2 %copy-start.3 = (bf16[1024,2048]{1,0:T(8,128)(2,1)S(1)}, bf16[1024,2048]{1,0:T(8,128)(2,1)}, u32[]{:S(2)}) copy-start(bf16[1024,2048]{1,0:T(8,128)(2,1)} %train_ref.3) | copy-start | bytes 12582916
  40.2 5.4 %collective-permute-start.14 = (bf16[1024,256]{1,0:T(8,128)(2,1)}, bf16[1024,256]{1,0:T(8,128)(2,1)S(1)}, u32[]{:S(2)}, u32[]{:S(2)}) collective-permute-start(bf16[1024,256]{1,0:T(8,128)(2,1)} %get-tuple-element.46), channel_id=1, source_target_pairs={{0,1},{1,0},{2,3},{3,2},{4,5},{5,4},{6,7},{7,6},{8,9},{9,8},{10,11... | collective-permute-start | bytes 1572872 | tf_op jit(solution)/shard_map/ppermute | solution.py:20
  40.2 1.0 copy-start.11
  41.2 17.2 %collective-permute-start.23 = (bf16[256,1024]{1,0:T(8,128)(2,1)S(1)}, bf16[256,1024]{1,0:T(8,128)(2,1)}, u32[]{:S(2)}, u32[]{:S(2)}) collective-permute-start(bf16[256,1024]{1,0:T(8,128)(2,1)S(1)} %stack.1.refs_9_), channel_id=1, source_target_pairs={{0,4},{4,0},{8,12},{12,8},{1,5},{5,1},{9,13},{13,9},{2,6},{6,2},{1... | collective-permute-start | bytes 1572872 | tf_op jit(solution)/shard_map/ppermute | solution.py:24
  45.5 24.1 %collective-permute-start.16 = (bf16[256,1024]{1,0:T(8,128)(2,1)S(1)}, bf16[256,1024]{1,0:T(8,128)(2,1)}, u32[]{:S(2)}, u32[]{:S(2)}) collective-permute-start(bf16[256,1024]{1,0:T(8,128)(2,1)S(1)} %after.8), channel_id=1, source_target_pairs={{0,4},{4,8},{8,12},{12,0},{1,5},{5,9},{9,13},{13,1},{2,6},{6,10},{... | collective-permute-start | bytes 1572872 | tf_op jit(solution)/shard_map/ppermute | solution.py:20
  45.6 3.4 %copy-start = (bf16[1,4096,1024]{2,1,0:T(8,128)(2,1)S(1)}, bf16[1,4096,1024]{2,1,0:T(8,128)(2,1)}, u32[]{:S(2)}) copy-start(bf16[1,4096,1024]{2,1,0:T(8,128)(2,1)} %param.10) | copy-start | bytes 25165828
  53.7 43.0 %collective-permute-start.15 = (bf16[2048,256]{1,0:T(8,128)(2,1)S(1)}, bf16[2048,256]{1,0:T(8,128)(2,1)S(1)}, u32[]{:S(2)}, u32[]{:S(2)}) collective-permute-start(bf16[2048,256]{1,0:T(8,128)(2,1)S(1)} %partial_weights.2.refs_4_), channel_id=1, source_target_pairs={{0,2},{2,0},{1,3},{3,1},{4,6},{6,4},{5,7},{7,5},{8,10},{10,8},{9,1... | collective-permute-start | bytes 3145736 | tf_op jit(solution)/shard_map/ppermute | solution.py:20
  55.2 39.5 %collective-permute-start.22 = (bf16[256,1024]{1,0:T(8,128)(2,1)S(1)}, bf16[256,1024]{1,0:T(8,128)(2,1)S(1)}, u32[]{:S(2)}, u32[]{:S(2)}) collective-permute-start(bf16[256,1024]{1,0:T(8,128)(2,1)S(1)} %stack.1.refs_9_), channel_id=1, source_target_pairs={{0,1},{1,0},{2,3},{3,2},{4,5},{5,4},{6,7},{7,6},{8,9},{9,8},{10,11... | collective-permute-start | bytes 1572872 | tf_op jit(solution)/shard_map/ppermute | solution.py:20
  58.5 36.3 %collective-permute-start.24 = (bf16[256,1024]{1,0:T(8,128)(2,1)}, bf16[256,1024]{1,0:T(8,128)(2,1)S(1)}, u32[]{:S(2)}, u32[]{:S(2)}) collective-permute-start(bf16[256,1024]{1,0:T(8,128)(2,1)} %collective-permute-done.23.refs_11_), channel_id=1, source_target_pairs={{0,1},{1,0},{2,3},{3,2},{4,5},{5,4},{6,7},{7,6},{8,9},{9,8},{10,11... | collective-permute-start | bytes 1572872 | tf_op jit(solution)/shard_map/ppermute | solution.py:20
  58.5 3.4 %copy-start.1 = (bf16[1,4096,1024]{2,1,0:T(8,128)(2,1)S(1)}, bf16[1,4096,1024]{2,1,0:T(8,128)(2,1)}, u32[]{:S(2)}) copy-start(bf16[1,4096,1024]{2,1,0:T(8,128)(2,1)} %param.10) | copy-start | bytes 25165828
  61.9 4.8 %copy-start.9 = (bf16[128,1024]{1,0:T(8,128)(2,1)S(1)}, bf16[128,1024]{1,0:T(8,128)(2,1)}, u32[]{:S(2)}) copy-start(bf16[128,1024]{1,0:T(8,128)(2,1)} %copy-done.8) | copy-start | bytes 786436
  66.6 26.6 %copy-start.5 = (bf16[256,1024]{1,0:T(8,128)(2,1)S(1)}, bf16[256,1024]{1,0:T(8,128)(2,1)}, u32[]{:S(2)}) copy-start(bf16[256,1024]{1,0:T(8,128)(2,1)} %copy-done.4) | copy-start | bytes 1572868
  66.6 21.3 %collective-permute-start.18 = (bf16[128,1024]{1,0:T(8,128)(2,1)S(1)}, bf16[128,1024]{1,0:T(8,128)(2,1)S(1)}, u32[]{:S(2)}, u32[]{:S(2)}) collective-permute-start(bf16[128,1024]{1,0:T(8,128)(2,1)S(1)} %after.10), channel_id=1, source_target_pairs={{0,8},{4,12},{8,0},{12,4},{1,9},{5,13},{9,1},{13,5},{2,10},{6,14},... | collective-permute-start | bytes 786440 | tf_op jit(solution)/shard_map/ppermute | solution.py:20
  69.6 23.6 %collective-permute-start.20 = (bf16[128,1024]{1,0:T(8,128)(2,1)S(1)}, bf16[128,1024]{1,0:T(8,128)(2,1)S(1)}, u32[]{:S(2)}, u32[]{:S(2)}) collective-permute-start(bf16[128,1024]{1,0:T(8,128)(2,1)S(1)} %after.11), channel_id=1, source_target_pairs={{0,8},{4,12},{8,0},{12,4},{1,9},{5,13},{9,1},{13,5},{2,10},{6,14},... | collective-permute-start | bytes 786440 | tf_op jit(solution)/shard_map/ppermute | solution.py:20
  87.9 7.3 %collective-permute-start.17 = (bf16[256,1024]{1,0:T(8,128)(2,1)}, bf16[256,1024]{1,0:T(8,128)(2,1)S(1)}, u32[]{:S(2)}, u32[]{:S(2)}) collective-permute-start(bf16[256,1024]{1,0:T(8,128)(2,1)} %after.9.refs_3_), channel_id=1, source_target_pairs={{0,1},{1,0},{2,3},{3,2},{4,5},{5,4},{6,7},{7,6},{8,9},{9,8},{10,11... | collective-permute-start | bytes 1572872 | tf_op jit(solution)/shard_map/ppermute | solution.py:20
  93.2 13.6 %collective-permute-start.26 = (bf16[256,1024]{1,0:T(8,128)(2,1)S(1)}, bf16[256,1024]{1,0:T(8,128)(2,1)S(1)}, u32[]{:S(2)}, u32[]{:S(2)}) collective-permute-start(bf16[256,1024]{1,0:T(8,128)(2,1)S(1)} %after.12), channel_id=1, source_target_pairs={{0,12},{4,0},{8,4},{12,8},{1,13},{5,1},{9,5},{13,9},{2,14},{6,2},{... | collective-permute-start | bytes 1572872 | tf_op jit(solution)/shard_map/ppermute | solution.py:20
  94.8 1.5 %collective-permute-start.19 = (bf16[128,1024]{1,0:T(8,128)(2,1)S(1)}, bf16[128,1024]{1,0:T(8,128)(2,1)S(1)}, u32[]{:S(2)}, u32[]{:S(2)}) collective-permute-start(bf16[128,1024]{1,0:T(8,128)(2,1)S(1)} %collective-permute-done.18.refs_5_.refs_1_), channel_id=1, source_target_pairs={{0,1},{1,0},{2,3},{3,2},{4,5},{5,4},{6,7},{7,6},{8,9},{9,8},{10,11... | collective-permute-start | bytes 786440 | tf_op jit(solution)/shard_map/ppermute | solution.py:20
  94.8 1.9 %collective-permute-start.21 = (bf16[128,1024]{1,0:T(8,128)(2,1)S(1)}, bf16[128,1024]{1,0:T(8,128)(2,1)S(1)}, u32[]{:S(2)}, u32[]{:S(2)}) collective-permute-start(bf16[128,1024]{1,0:T(8,128)(2,1)S(1)} %collective-permute-done.20.refs_7_.refs_2_), channel_id=1, source_target_pairs={{0,1},{1,0},{2,3},{3,2},{4,5},{5,4},{6,7},{7,6},{8,9},{9,8},{10,11... | collective-permute-start | bytes 786440 | tf_op jit(solution)/shard_map/ppermute | solution.py:20
  106.7 1.9 %collective-permute-start.27 = (bf16[256,1024]{1,0:T(8,128)(2,1)S(1)}, bf16[256,1024]{1,0:T(8,128)(2,1)S(1)}, u32[]{:S(2)}, u32[]{:S(2)}) collective-permute-start(bf16[256,1024]{1,0:T(8,128)(2,1)S(1)} %after.13.refs_0_), channel_id=1, source_target_pairs={{0,1},{1,0},{2,3},{3,2},{4,5},{5,4},{6,7},{7,6},{8,9},{9,8},{10,11... | collective-permute-start | bytes 1572872 | tf_op jit(solution)/shard_map/ppermute | solution.py:20
  106.7 9.1 %collective-permute-start.25 = (bf16[1024,128]{1,0:T(8,128)(2,1)S(1)}, bf16[1024,128]{1,0:T(8,128)(2,1)S(1)}, u32[]{:S(2)}, u32[]{:S(2)}) collective-permute-start(bf16[1024,128]{1,0:T(8,128)(2,1)S(1)} %get-tuple-element.50.refs_1_), channel_id=1, source_target_pairs={{0,2},{2,0},{1,3},{3,1},{4,6},{6,4},{5,7},{7,5},{8,10},{10,8},{9,1... | collective-permute-start | bytes 786440 | tf_op jit(solution)/shard_map/ppermute | solution.py:20
  109.4 7.5 %collective-permute-start.28 = (bf16[256,128]{1,0:T(8,128)(2,1)S(1)}, bf16[256,128]{1,0:T(8,128)(2,1)S(1)}, u32[]{:S(2)}, u32[]{:S(2)}) collective-permute-start(bf16[256,128]{1,0:T(8,128)(2,1)S(1)} %get-tuple-element.55), channel_id=1, source_target_pairs={{0,2},{2,0},{1,3},{3,1},{4,6},{6,4},{5,7},{7,5},{8,10},{10,8},{9,1... | collective-permute-start | bytes 196616 | tf_op jit(solution)/shard_map/ppermute | solution.py:20

commit v8 on v7

--- a/solution.py
+++ b/solution.py
@@ -53,21 +53,14 @@
     n = len(parts)
 
     def kernel(*refs):
-        out, sem = refs[-2:]
-        copies = [
-            pltpu.make_async_copy(refs[j], out.at[j * size:(j + 1) * size], sem.at[j]) for j in range(n)
-        ]
-        for copy in copies:
-            copy.start()
-        for copy in copies:
-            copy.wait()
-
-    return pl.pallas_call(
-        kernel,
-        in_specs=[ANY] * (n + len(others)),
-        out_specs=ANY,
+        for j in range(n):
+            refs[-1][j * size:(j + 1) * size, :] = refs[j][...]
+
+    return pl.pallas_call(
+        kernel,
+        in_specs=[VMEM] * n + [ANY] * len(others),
+        out_specs=VMEM,
         out_shape=jax.ShapeDtypeStruct((n * size, width), parts[0].dtype),
-        scratch_shapes=[pltpu.SemaphoreType.DMA((n,))],
         cost_estimate=cost(0, 0),
         compiler_params=PARAMS,
         name="stack",
@@ -173,7 +166,7 @@
         out_specs=VMEM,
         out_shape=jax.ShapeDtypeStruct((bulk, train.shape[1]), BF16),
         cost_estimate=cost(2 * bulk * train.size, 2 * train.size),
-        compiler_params=PARAMS,
+        compiler_params=FIRST,
         name="own_rows",
     )(goal, train)
 
@@ -234,7 +227,7 @@
         out_specs=[VMEM] * len(shapes),
         out_shape=shapes,
         cost_estimate=cost(2 * packed * rows * columns, 2 * (rows + packed) * columns),
-        compiler_params=PARAMS,
+        compiler_params=FIRST,
         name="pack_rows",
     )(ids, train)
 
@@ -263,7 +256,7 @@
         ),
         out_shape=jax.ShapeDtypeStruct((depth, total), dtype),
         cost_estimate=cost(2 * n * depth * width * total, 2 * n * depth * width + 4 * depth * total),
-        compiler_params=PARAMS,
+        compiler_params=FIRST,
         name="partial_weights",
     )(jnp.reshape(block, (1,)).astype(I32), *matrices, *queries, *others)
 
@@ -303,7 +296,7 @@
         out_specs=[SMEM, VMEM],
         out_shape=[jax.ShapeDtypeStruct((n_shard, 4), I32), jax.ShapeDtypeStruct((8, LANES), I32)],
         cost_estimate=cost(0, 4 * ids.size),
-        compiler_params=PARAMS,
+        compiler_params=FIRST,
         name="row_table",
     )(ids)
 
@@ -430,26 +423,29 @@
     )(table, own, *others, mine, *[p for parts in pieces for p in parts], *surplus)
 
 
-def late_scores(parts, high, low, n_feat):
-    rows = parts[0].shape[0]
+def late_scores(pieces, high, low, n_feat):
+    n, n_rep = len(pieces), len(pieces[0])
+    size = pieces[0][0].shape[0]
+    rows = n * size
     width = high.shape[1]
 
     def kernel(high_ref, low_ref, *refs):
-        part_refs, outs, acc = refs[:len(parts)], refs[len(parts):-1], refs[-1]
-        y = score(high_ref, low_ref, [ref[...] for ref in part_refs], lax.axis_index("rep"))
+        part_refs, outs, acc = refs[:n * n_rep], refs[n * n_rep:-1], refs[-1]
+        parts = [jnp.concatenate([part_refs[j * n_rep + d][...] for j in range(n)]) for d in range(n_rep)]
+        y = score(high_ref, low_ref, parts, lax.axis_index("rep"))
         acc[...] = y.reshape(rows, width)
         for_feats(lambda at: acc[:, at], outs)
 
     return pl.pallas_call(
         kernel,
-        in_specs=[VMEM] * (2 + len(parts)),
+        in_specs=[VMEM] * (2 + n * n_rep),
         out_specs=[VMEM] * n_feat,
         out_shape=feat_shapes(rows, width, n_feat),
         scratch_shapes=[pltpu.VMEM((rows, width), F32)],
         cost_estimate=cost(4 * rows * high.size, 8 * rows * width),
         compiler_params=PARAMS,
         name="late_scores",
-    )(high, low, *parts)
+    )(high, low, *[p for parts in pieces for p in parts])
 
 
 def merge(table, early, late, n_shard):
@@ -507,9 +503,9 @@
     pieces = [picked[0]] + [shift(picked[d], "shard", n_shard, d) for d in range(1, n_shard)]
 
     middle = [(d, 0, bulk) for d in range(1, last_hops)]
-    if extra:
-        middle = middle[:-1] + [(last_hops - 1, j * bulk // 2, bulk // 2) for j in range(2)]
-    *packed, goal = pack_rows(train, ids, columns, bulk, extra, middle + [(last_hops, 0, bulk)])
+    part = 64 if bulk % 64 == 0 else bulk
+    final = [(last_hops, at, part) for at in range(0, bulk, part)]
+    *packed, goal = pack_rows(train, ids, columns, bulk, extra, middle + final)
     table, flag = row_table(ids, lines, bulk, extra)
     mine = own_rows(goal, train, bulk)
     before_join, firsts, seconds = [mine], [], []
@@ -524,12 +520,10 @@
         def no_round(x):
             return [[jnp.zeros((2 * extra, columns), BF16)] * n_rep] * 2
 
-        seconds = lax.cond(flag[0, 0] > 0, second_round, no_round, packed[-1])
-        far = swap(packed[-2], "shard", n_shard, 2)
+        seconds = lax.cond(flag[0, 0] > 0, second_round, no_round, after(packed[-1], *pieces[1:]))
+        far = swap(after(packed[-2], *pieces[1:]), "shard", n_shard, 2)
         before_join += [far] + [x for parts in seconds for x in parts]
 
-    final = after(pieces[n_shard // 2], packed[0], flag, *[x for d, x in enumerate(pieces) if d != n_shard // 2])
-    pieces = [final if d == n_shard // 2 else x for d, x in enumerate(pieces)]
     parts = [pieces] + [[shift(x, "groups", n_group, d) for x in pieces] for d in range(1, n_group)]
     chosen = join_queries(parts, block_slot, pattern, query_store.shape[0], n_feat, n_rep, *before_join)
     queries = [chosen[0]] + [shift(chosen[d], "rep", n_rep, d) for d in range(1, n_rep)]
@@ -543,13 +537,16 @@
     own = weights(feat, F32, *sends)
 
     for (hops, _, _), x in zip(middle[1:], packed[1:]):
-        here.append(shift(after(x, own), "shard", n_shard, hops))
-    last = shift(after(packed[len(middle)], *here[1:]), "shard", n_shard, last_hops)
+        here.append(shift(after(x, here[-1], *sends), "shard", n_shard, hops))
+    last = [
+        shift(after(packed[len(middle) + j], here[-1], own), "shard", n_shard, last_hops) for j in range(len(final))
+    ]
     if extra:
-        pair = stack([packed[-2], far], chosen[0])
+        pair = stack([packed[-2], far], *sends)
         firsts = [with_rep(pair), with_rep(swap(pair, "shard", n_shard, 1))]
 
-    ready = [with_rep(after(x, own)) for x in here[:1]] + [with_rep(x) for x in here[1:]]
+    mark = shift(after(jnp.zeros((8, LANES), I32), own), "rep", n_rep, 1)
+    ready = [with_rep(after(x, mark)) for x in here]
     high, low, *early = early_scores(
         own, others, mine, ready, middle, firsts, seconds, table, rows, n_feat, n_rep, n_shard, bulk, extra
     )
@@ -557,7 +554,7 @@
     def over_feat(shares):
         return [shares[0]] + [shift(shares[d], "feat", n_feat, d) for d in range(1, n_feat)]
 
-    late = late_scores(with_rep(after(last, *early[1:])), high, low, n_feat)
+    late = late_scores([with_rep(after(x, *early[1:])) for x in last], high, low, n_feat)
     return merge(table, over_feat(early), over_feat(late), n_shard)[None]
 
 

time: 119 us -> 111 us (0.933)
  waiting for transfers between devices: 48.7 us -> 30.7 us
  Pallas kernels: 26.5 us -> 35.8 us
  local copies, waits for them, and re-layouts: 18.5 us -> 11.1 us
  starting transfers between devices: 23.9 us -> 30.9 us
    ppermute x23 -> x28, waiting for transfers between devices: 44.9 us -> 30.7 us  [shift(): return lax.ppermute(x, axis, [(i, (i + by) % size) for i in range(size)])]
    unnamed x30 -> x37, local copies, waits for them, and re-layouts: 14.5 us -> 7.03 us
    ppermute x23 -> x28, starting transfers between devices: 19.5 us -> 27 us  [shift(): return lax.ppermute(x, axis, [(i, (i + by) % size) for i in range(size)])]
    pallas_call x2, Pallas kernels: 9.45 us -> 13.5 us  [partial_weights(): pl.pallas_call(kernel, grid_spec=pltpu.PrefetchScalarGridSpec(num_scalar_...]
    ppermute x2, waiting for transfers between devices: 3.85 us -> 0.01 us  [swap(): return lax.ppermute(x, axis, [(i, i ^ bit) for i in range(size)])]
    pallas_call x1, Pallas kernels: 1.27 us -> 4.43 us  [own_rows(): pl.pallas_call(kernel, in_specs=[VMEM] * 2, out_specs=VMEM, out_shape=jax...]
    pallas_call x1, Pallas kernels: 2.73 us -> 5.7 us  [pack_rows(): pl.pallas_call(kernel, grid=(1,), in_specs=[pl.BlockSpec((lines, LANES),...]
  transfers between devices with their start and end apart: 25 -> 30, of which waited for: 14 -> 10; matrix products, arithmetic and copies ran while one was open for 3% -> 5% of each run, Pallas kernels for 21% -> 31%
where the time goes in v8:
time: 111 us; the launch traced here: 110 us
  Pallas kernels  35.8 us (32%)
  starting transfers between devices  30.9 us (28%)
  waiting for transfers between devices  30.7 us (28%)
  local copies, waits for them, and re-layouts  11.1 us (10%)
    ppermute x28, waiting for transfers between devices, shift(): return lax.ppermute(x, axis, [(i, (i + by) % size) for i in range(size)])  30.7 us
    ppermute x28, starting transfers between devices, shift(): return lax.ppermute(x, axis, [(i, (i + by) % size) for i in range(size)])  27 us
    pallas_call x2, Pallas kernels, partial_weights(): pl.pallas_call(kernel, grid_spec=pltpu.PrefetchScalarGridSpec(num_scalar_...  13.5 us
    unnamed x37, local copies, waits for them, and re-layouts  7.03 us
    pallas_call x1, Pallas kernels, pack_rows(): pl.pallas_call(kernel, grid=(1,), in_specs=[pl.BlockSpec((lines, LANES),...  5.7 us
    pallas_call x1, Pallas kernels, own_rows(): pl.pallas_call(kernel, in_specs=[VMEM] * 2, out_specs=VMEM, out_shape=jax...  4.43 us
    pallas_call x1, Pallas kernels, early_scores(): pl.pallas_call(kernel, in_specs=[SMEM] + [VMEM] * (2 + n_other + n_rep *...  4.35 us
    ppermute x2, starting transfers between devices, swap(): return lax.ppermute(x, axis, [(i, i ^ bit) for i in range(size)])  3.94 us
  transfers between devices with their start and end apart: 30, of which 10 were waited for; matrix products, arithmetic and copies ran while one was open for 5% of the time, Pallas kernels for 31%

profile of v8, /device:TPU:0, one launch (start us, length us, event | category | flops | bytes accessed | tf_op | source)
XLA Modules:
  0.0 110.2 jit_solution(1815609404877882839)
XLA Ops:
  0.5 2.7 %pick_queries.1 = (bf16[1,64,1024]{2,1,0:T(8,128)(2,1)}, bf16[1,64,1024]{2,1,0:T(8,128)(2,1)}, bf16[1,64,1024]{2,1,0:T(8,128)(2,1)}, bf16[1,64,1024]{2,1,0:T(8,128)(2,1)}) custom-call(s32[4,4]{1,0:T(4,128)} %pattern_ref.3, s32[16]{0:T(128)} %slot_ref.3, bf16[4,128,1024]{2,1,0:T(8,128)(2,1)} %in_ref.1), custom_call_target="tpu_custom_call" | custom-call | flops 1 | bytes 1 | tf_op jit(solution)/shard_map/pick_queries/pallas_call | solution.py:92
  3.2 2.8 %collective-permute-start.5 = (bf16[1,64,1024]{2,1,0:T(8,128)(2,1)}, bf16[1,64,1024]{2,1,0:T(8,128)(2,1)S(1)}, u32[]{:S(2)}, u32[]{:S(2)}) collective-permute-start(bf16[1,64,1024]{2,1,0:T(8,128)(2,1)} %get-tuple-element.35), channel_id=1, source_target_pairs={{0,4},{4,8},{8,12},{12,0},{1,5},{5,9},{9,13},{13,1},{2,6},{6,10},{... | collective-permute-start | bytes 393224 | tf_op jit(solution)/shard_map/ppermute | solution.py:20
  5.9 2.6 %collective-permute-start.6 = (bf16[1,64,1024]{2,1,0:T(8,128)(2,1)}, bf16[1,64,1024]{2,1,0:T(8,128)(2,1)S(1)}, u32[]{:S(2)}, u32[]{:S(2)}) collective-permute-start(bf16[1,64,1024]{2,1,0:T(8,128)(2,1)} %get-tuple-element.36), channel_id=1, source_target_pairs={{0,8},{4,12},{8,0},{12,4},{1,9},{5,13},{9,1},{13,5},{2,10},{6,14},... | collective-permute-start | bytes 393224 | tf_op jit(solution)/shard_map/ppermute | solution.py:20
  8.5 1.3 %collective-permute-start.7 = (bf16[1,64,1024]{2,1,0:T(8,128)(2,1)}, bf16[1,64,1024]{2,1,0:T(8,128)(2,1)S(1)}, u32[]{:S(2)}, u32[]{:S(2)}) collective-permute-start(bf16[1,64,1024]{2,1,0:T(8,128)(2,1)} %get-tuple-element.37), channel_id=1, source_target_pairs={{0,12},{4,0},{8,4},{12,8},{1,13},{5,1},{9,5},{13,9},{2,14},{6,2},{... | collective-permute-start | bytes 393224 | tf_op jit(solution)/shard_map/ppermute | solution.py:20
  9.9 1.5 %collective-permute-start.8 = (bf16[1,64,1024]{2,1,0:T(8,128)(2,1)}, bf16[1,64,1024]{2,1,0:T(8,128)(2,1)S(1)}, u32[]{:S(2)}, u32[]{:S(2)}) collective-permute-start(bf16[1,64,1024]{2,1,0:T(8,128)(2,1)} %get-tuple-element.34.refs_0_), channel_id=1, source_target_pairs={{0,16},{16,0},{1,17},{17,1},{2,18},{18,2},{3,19},{19,3},{4,20},{20... | collective-permute-start | bytes 393224 | tf_op jit(solution)/shard_map/ppermute | solution.py:20
  11.4 5.7 %pack_rows.1 = (bf16[256,1024]{1,0:T(8,128)(2,1)}, bf16[256,1024]{1,0:T(8,128)(2,1)}, bf16[64,1024]{1,0:T(8,128)(2,1)}, bf16[64,1024]{1,0:T(8,128)(2,1)}, bf16[6...) custom-call(s32[32,128]{1,0:T(8,128)} %bitcast.9, ...), custom_call_target="tpu_custom_call" | custom-call | flops 1 | bytes 1 | tf_op jit(solution)/shard_map/pack_rows/pallas_call | solution.py:220
  17.1 1.0 copy.23.refs_0_
  18.1 2.1 %collective-permute-start.12 = (bf16[128,1024]{1,0:T(8,128)(2,1)S(1)}, bf16[128,1024]{1,0:T(8,128)(2,1)S(1)}, u32[]{:S(2)}, u32[]{:S(2)}) collective-permute-start(bf16[128,1024]{1,0:T(8,128)(2,1)S(1)} %after.15), channel_id=1, source_target_pairs={{0,8},{4,12},{8,0},{12,4},{1,9},{5,13},{9,1},{13,5},{2,10},{6,14},... | collective-permute-start | bytes 786440 | tf_op jit(solution)/shard_map/ppermute | solution.py:24
  20.3 1.5 %row_table.1 = (s32[4,4]{1,0:T(4,128)}, s32[8,128]{1,0:T(8,128)}) custom-call(s32[32,128]{1,0:T(8,128)} %bitcast.10), custom_call_target="tpu_custom_call" | custom-call | flops 1 | bytes 1 | tf_op jit(solution)/shard_map/row_table/pallas_call | solution.py:293
  21.8 1.6 %collective-permute-start.13 = (s32[8,128]{1,0:T(8,128)}, s32[8,128]{1,0:T(8,128)S(1)}, u32[]{:S(2)}, u32[]{:S(2)}) collective-permute-start(s32[8,128]{1,0:T(8,128)} %get-tuple-element.40), channel_id=1, source_target_pairs={{0,16},{16,0},{1,17},{17,1},{2,18},{18,2},{3,19},{19,3},{4,20},{20... | collective-permute-start | bytes 12296 | tf_op jit(solution)/shard_map/ppermute | solution.py:20
  23.4 2.3 %collective-permute-done.13 = s32[8,128]{1,0:T(8,128)S(1)} collective-permute-done((s32[8,128]{1,0:T(8,128)}, s32[8,128]{1,0:T(8,128)S(1)}, u32[]{:S(2)}, u32[]{:S(2)}) %collective-permute-start.13) | collective-permute-done | bytes 4128 | tf_op jit(solution)/shard_map/ppermute | solution.py:20
  25.7 0.7 max.3
  26.4 0.6 slice.3
  27.7 3.5 %conditional.1 = (bf16[256,1024]{1,0:T(8,128)(2,1)}, bf16[256,1024]{1,0:T(8,128)(2,1)}, bf16[256,1024]{1,0:T(8,128)(2,1)}, bf16[256,1024]{1,0:T(8,128)(2,1)}) conditional(s32[]{:T(128)} %bitcast.3, () %tuple.13, bf16[128,1024]{1,0:T(8,128)(2,1)S(1)} %after.16), branch_computations={%region_0.0_spmd, %region_1.0_spmd} | conditional | bytes 8388800 | solution.py:523
  27.7 0.9 broadcast.3
  28.6 0.9 broadcast.3.clone
  29.4 0.9 broadcast.3.clone.1
  30.3 0.9 broadcast.3.clone.2
  31.2 1.5 %collective-permute-start.9 = (bf16[1,64,1024]{2,1,0:T(8,128)(2,1)S(1)}, bf16[1,64,1024]{2,1,0:T(8,128)(2,1)S(1)}, u32[]{:S(2)}, u32[]{:S(2)}) collective-permute-start(bf16[1,64,1024]{2,1,0:T(8,128)(2,1)S(1)} %collective-permute-done.5.refs_1_), channel_id=1, source_target_pairs={{0,16},{16,0},{1,17},{17,1},{2,18},{18,2},{3,19},{19,3},{4,20},{20... | collective-permute-start | bytes 393224 | tf_op jit(solution)/shard_map/ppermute | solution.py:20
  33.2 1.5 %collective-permute-start.11 = (bf16[1,64,1024]{2,1,0:T(8,128)(2,1)S(1)}, bf16[1,64,1024]{2,1,0:T(8,128)(2,1)S(1)}, u32[]{:S(2)}, u32[]{:S(2)}) collective-permute-start(bf16[1,64,1024]{2,1,0:T(8,128)(2,1)S(1)} %collective-permute-done.7.refs_3_), channel_id=1, source_target_pairs={{0,16},{16,0},{1,17},{17,1},{2,18},{18,2},{3,19},{19,3},{4,20},{20... | collective-permute-start | bytes 393224 | tf_op jit(solution)/shard_map/ppermute | solution.py:20
  34.7 4.4 %own_rows.1.refs_8_.refs_2_ = bf16[256,2048]{1,0:T(8,128)(2,1)} custom-call(s32[8,128]{1,0:T(8,128)} %get-tuple-element.38.goal_ref, bf16[1024,2048]{1,0:T(8,128)(2,1)} %train_ref.3), custom_call_target="tpu_custom_call" | custom-call | flops 1 | bytes 1 | tf_op jit(solution)/shard_map/own_rows/pallas_call | solution.py:163
  39.2 0.5 collective-permute-done.10.refs_6_
  39.7 1.4 %collective-permute-done.11.refs_7_ = bf16[1,64,1024]{2,1,0:T(8,128)(2,1)S(1)} collective-permute-done((bf16[1,64,1024]{2,1,0:T(8,128)(2,1)S(1)}, bf16[1,64,1024]{2,1,0:T(8,128)(2,1)S(1)}, u32[]{:S(2)}, u32[]{:S(2)}) %collective-permute-start.11) | collective-permute-done | bytes 131104 | tf_op jit(solution)/shard_map/ppermute | solution.py:20
  41.1 1.2 %copy-done.3 = bf16[256,2048]{1,0:T(8,128)(2,1)S(1)} copy-done((bf16[256,2048]{1,0:T(8,128)(2,1)S(1)}, bf16[256,2048]{1,0:T(8,128)(2,1)}, u32[]{:S(2)}) %copy-start.3) | copy-done | bytes 1048600
  42.3 1.2 %join_queries.1 = (bf16[1024,256]{1,0:T(8,128)(2,1)S(1)}, bf16[1024,256]{1,0:T(8,128)(2,1)S(1)}) custom-call(s32[4,4]{1,0:T(4,128)S(1)} %copy-done.14, s32[16]{0:T(128)S(1)} %copy-done.16, bf16[1,64,1024]{2,1,0:T(8,128)(2,1)S(1)} %copy-done.13, bf16[1,64,1024]{2,1,0:T(8,128)(2,1)S(1)} %collective-permute-done.5.refs_1_, ...), custom_call_target="tpu_custom_call" | custom-call | flops 1 | bytes 1 | tf_op jit(solution)/shard_map/join_queries/pallas_call | solution.py:137
  43.6 0.8 copy-done.5
  44.4 2.1 %collective-permute-start.16 = (bf16[256,1024]{1,0:T(8,128)(2,1)S(1)}, bf16[256,1024]{1,0:T(8,128)(2,1)S(1)}, u32[]{:S(2)}, u32[]{:S(2)}) collective-permute-start(bf16[256,1024]{1,0:T(8,128)(2,1)S(1)} %after.17), channel_id=1, source_target_pairs={{0,4},{4,8},{8,12},{12,0},{1,5},{5,9},{9,13},{13,1},{2,6},{6,10},{... | collective-permute-start | bytes 1572872 | tf_op jit(solution)/shard_map/ppermute | solution.py:20
  46.4 0.8 copy-done.17
  47.2 6.6 %partial_weights.2.refs_4_.refs_2_ = bf16[2048,256]{1,0:T(8,128)(2,1)} custom-call(s32[1]{0:T(128)} %bitcast.4.block_ref, bf16[4096,1024]{1,0:T(8,128)(2,1)} %bitcast.7, bf16[4096,1024]{1,0:T(8,128)(2,1)} %collective-permute-done.4.refs_1_, bf16[1024,256]{1,0:T(8,128)(2,1)} %copy-done.5, bf16[1024,256]{1,0:T(8,128)(2,1)} %copy-done.17), custom_call_target="tpu_custom_call" | custom-call | flops 1 | bytes 1 | tf_op jit(solution)/shard_map/partial_weights/pallas_call | solution.py:247
  53.8 6.6 %collective-permute-done.16.refs_0_.refs_1_ = bf16[256,1024]{1,0:T(8,128)(2,1)S(1)} collective-permute-done((bf16[256,1024]{1,0:T(8,128)(2,1)S(1)}, bf16[256,1024]{1,0:T(8,128)(2,1)S(1)}, u32[]{:S(2)}, u32[]{:S(2)}) %collective-permute-start.16) | collective-permute-done | bytes 524320 | tf_op jit(solution)/shard_map/ppermute | solution.py:20
  60.5 1.5 %collective-permute-start.15 = (bf16[2048,256]{1,0:T(8,128)(2,1)}, bf16[2048,256]{1,0:T(8,128)(2,1)S(1)}, u32[]{:S(2)}, u32[]{:S(2)}) collective-permute-start(bf16[2048,256]{1,0:T(8,128)(2,1)} %partial_weights.2.refs_4_.refs_2_), channel_id=1, source_target_pairs={{0,2},{2,0},{1,3},{3,1},{4,6},{6,4},{5,7},{7,5},{8,10},{10,8},{9,1... | collective-permute-start | bytes 3145736 | tf_op jit(solution)/shard_map/ppermute | solution.py:20
  62.0 1.8 %collective-permute-start.22 = (bf16[256,1024]{1,0:T(8,128)(2,1)S(1)}, bf16[256,1024]{1,0:T(8,128)(2,1)}, u32[]{:S(2)}, u32[]{:S(2)}) collective-permute-start(bf16[256,1024]{1,0:T(8,128)(2,1)S(1)} %stack.1.refs_7_), channel_id=1, source_target_pairs={{0,4},{4,0},{8,12},{12,8},{1,5},{5,1},{9,13},{13,9},{2,6},{6,2},{1... | collective-permute-start | bytes 1572872 | tf_op jit(solution)/shard_map/ppermute | solution.py:24
  63.8 6.8 %partial_weights.3.refs_1_.refs_0_.refs_2_ = f32[2048,256]{1,0:T(8,128)} custom-call(s32[1]{0:T(128)} %bitcast.1.block_ref, bf16[4096,1024]{1,0:T(8,128)(2,1)} %bitcast.8, bf16[4096,1024]{1,0:T(8,128)(2,1)} %collective-permute-done.4.refs_1_, bf16[1024,256]{1,0:T(8,128)(2,1)} %copy-done.5, bf16[1024,256]{1,0:T(8,128)(2,1)} %copy-done.17, ...), custom_call_target="tpu_custom_call" | custom-call | flops 1 | bytes 1 | tf_op jit(solution)/shard_map/partial_weights/pallas_call | solution.py:247
  70.7 1.6 %copy-done = f32[2048,256]{1,0:T(8,128)S(1)} copy-done((f32[2048,256]{1,0:T(8,128)S(1)}, f32[2048,256]{1,0:T(8,128)}, u32[]{:S(2)}) %copy-start) | copy-done | bytes 2097176
  72.8 0.7 collective-permute-done.17.refs_1_
  73.6 12.4 %collective-permute-done.19.refs_0_.refs_1_ = bf16[256,1024]{1,0:T(8,128)(2,1)S(1)} collective-permute-done((bf16[256,1024]{1,0:T(8,128)(2,1)S(1)}, bf16[256,1024]{1,0:T(8,128)(2,1)S(1)}, u32[]{:S(2)}, u32[]{:S(2)}) %collective-permute-start.19) | collective-permute-done | bytes 524320 | tf_op jit(solution)/shard_map/ppermute | solution.py:20
  86.0 1.6 %copy-done.1 = f32[2048,256]{1,0:T(8,128)S(1)} copy-done((f32[2048,256]{1,0:T(8,128)S(1)}, f32[2048,256]{1,0:T(8,128)}, u32[]{:S(2)}) %copy-start.1) | copy-done | bytes 2097176
  88.2 1.5 %collective-permute-start.25 = (bf16[64,1024]{1,0:T(8,128)(2,1)S(1)}, bf16[64,1024]{1,0:T(8,128)(2,1)S(1)}, u32[]{:S(2)}, u32[]{:S(2)}) collective-permute-start(bf16[64,1024]{1,0:T(8,128)(2,1)S(1)} %after.22), channel_id=1, source_target_pairs={{0,12},{4,0},{8,4},{12,8},{1,13},{5,1},{9,5},{13,9},{2,14},{6,2},{... | collective-permute-start | bytes 393224 | tf_op jit(solution)/shard_map/ppermute | solution.py:20
  89.8 3.3 %collective-permute-start.31 = (bf16[64,1024]{1,0:T(8,128)(2,1)S(1)}, bf16[64,1024]{1,0:T(8,128)(2,1)S(1)}, u32[]{:S(2)}, u32[]{:S(2)}) collective-permute-start(bf16[64,1024]{1,0:T(8,128)(2,1)S(1)} %after.28), channel_id=1, source_target_pairs={{0,12},{4,0},{8,4},{12,8},{1,13},{5,1},{9,5},{13,9},{2,14},{6,2},{... | collective-permute-start | bytes 393224 | tf_op jit(solution)/shard_map/ppermute | solution.py:20
  93.2 4.3 %early_scores.1 = (bf16[2048,256]{1,0:T(8,128)(2,1)S(1)}, bf16[2048,256]{1,0:T(8,128)(2,1)S(1)}, f32[1024,128]{1,0:T(8,128)S(1)}, bf16[1024,128]{1,0:T(8,128)(2,1)S(1)}) custom-call(s32[4,4]{1,0:T(4,128)S(1)} %copy-done.15, f32[2048,256]{1,0:T(8,128)S(1)} %copy-done.2, bf16[2048,256]{1,0:T(8,128)(2,1)S(1)} %collective-permute-done.15.refs_1_, ...), custom_call_target="tpu_custom_call" | custom-call | flops 1 | bytes 1 | tf_op jit(solution)/shard_map/early_scores/pallas_call | solution.py:409
  97.6 1.4 %collective-permute-start.24 = (bf16[1024,128]{1,0:T(8,128)(2,1)S(1)}, bf16[1024,128]{1,0:T(8,128)(2,1)S(1)}, u32[]{:S(2)}, u32[]{:S(2)}) collective-permute-start(bf16[1024,128]{1,0:T(8,128)(2,1)S(1)} %get-tuple-element.51.refs_1_), channel_id=1, source_target_pairs={{0,2},{2,0},{1,3},{3,1},{4,6},{6,4},{5,7},{7,5},{8,10},{10,8},{9,1... | collective-permute-start | bytes 786440 | tf_op jit(solution)/shard_map/ppermute | solution.py:20
  99.5 0.7 collective-permute-done.29.refs_0_
  100.2 1.9 %collective-permute-done.31.refs_0_ = bf16[64,1024]{1,0:T(8,128)(2,1)S(1)} collective-permute-done((bf16[64,1024]{1,0:T(8,128)(2,1)S(1)}, bf16[64,1024]{1,0:T(8,128)(2,1)S(1)}, u32[]{:S(2)}, u32[]{:S(2)}) %collective-permute-start.31) | collective-permute-done | bytes 131104 | tf_op jit(solution)/shard_map/ppermute | solution.py:20
  102.2 1.3 %collective-permute-done.32.refs_7_ = bf16[64,1024]{1,0:T(8,128)(2,1)S(1)} collective-permute-done((bf16[64,1024]{1,0:T(8,128)(2,1)S(1)}, bf16[64,1024]{1,0:T(8,128)(2,1)S(1)}, u32[]{:S(2)}, u32[]{:S(2)}) %collective-permute-start.32) | collective-permute-done | bytes 131104 | tf_op jit(solution)/shard_map/ppermute | solution.py:20
  103.5 0.7 late_scores.1
  104.2 1.5 %collective-permute-start.33 = (bf16[256,128]{1,0:T(8,128)(2,1)S(1)}, bf16[256,128]{1,0:T(8,128)(2,1)S(1)}, u32[]{:S(2)}, u32[]{:S(2)}) collective-permute-start(bf16[256,128]{1,0:T(8,128)(2,1)S(1)} %get-tuple-element.59), channel_id=1, source_target_pairs={{0,2},{2,0},{1,3},{3,1},{4,6},{6,4},{5,7},{7,5},{8,10},{10,8},{9,1... | collective-permute-start | bytes 196616 | tf_op jit(solution)/shard_map/ppermute | solution.py:20
  105.7 2.9 %collective-permute-done.33.refs_3_ = bf16[256,128]{1,0:T(8,128)(2,1)S(1)} collective-permute-done((bf16[256,128]{1,0:T(8,128)(2,1)S(1)}, bf16[256,128]{1,0:T(8,128)(2,1)S(1)}, u32[]{:S(2)}, u32[]{:S(2)}) %collective-permute-start.33) | collective-permute-done | bytes 65568 | tf_op jit(solution)/shard_map/ppermute | solution.py:20
  108.6 1.7 %merge.1 = f32[128,1024]{1,0:T(8,128)} custom-call(s32[4,4]{1,0:T(4,128)S(1)} %copy-done.15, f32[1024,128]{1,0:T(8,128)S(1)} %get-tuple-element.50.refs_0_, bf16[1024,128]{1,0:T(8,128)(2,1)S(1)} %collective-permute-done.24.refs_1_, f32[256,128]{1,0:T(8,128)S(1)} %get-tuple-element.58.refs_2_, bf16[256,128]{1,0:T(8,128)(2,1)S(1)} %collective-permute-done.33.refs_3_), custom_call_target="tpu_custom_call" | custom-call | flops 1 | bytes 1 | tf_op jit(solution)/shard_map/merge/pallas_call | solution.py:471
  (83 shorter events, 3.0 us)
Async XLA Ops:
  0.0 41.1 %copy-start.14 = (s32[4,4]{1,0:T(4,128)S(1)}, s32[4,4]{1,0:T(4,128)}, u32[]{:S(2)}) copy-start(s32[4,4]{1,0:T(4,128)} %pattern_ref.3) | copy-start | bytes 196
  0.0 41.1 %copy-start.16 = (s32[16]{0:T(128)S(1)}, s32[16]{0:T(128)}, u32[]{:S(2)}) copy-start(s32[16]{0:T(128)} %slot_ref.3) | copy-start | bytes 196
  0.0 46.4 %collective-permute-start.4 = (bf16[4096,1024]{1,0:T(8,128)(2,1)}, bf16[4096,1024]{1,0:T(8,128)(2,1)}, u32[]{:S(2)}, u32[]{:S(2)}) collective-permute-start(bf16[4096,1024]{1,0:T(8,128)(2,1)} %bitcast.6), channel_id=1, source_target_pairs={{0,1},{1,0},{2,3},{3,2},{4,5},{5,4},{6,7},{7,6},{8,9},{9,8},{10,11... | collective-permute-start | bytes 25165832 | tf_op jit(solution)/shard_map/ppermute | solution.py:20
  3.2 37.9 %copy-start.13 = (bf16[1,64,1024]{2,1,0:T(8,128)(2,1)S(1)}, bf16[1,64,1024]{2,1,0:T(8,128)(2,1)}, u32[]{:S(2)}) copy-start(bf16[1,64,1024]{2,1,0:T(8,128)(2,1)} %get-tuple-element.34.refs_0_) | copy-start | bytes 393220
  3.2 15.0 %collective-permute-start.5 = (bf16[1,64,1024]{2,1,0:T(8,128)(2,1)}, bf16[1,64,1024]{2,1,0:T(8,128)(2,1)S(1)}, u32[]{:S(2)}, u32[]{:S(2)}) collective-permute-start(bf16[1,64,1024]{2,1,0:T(8,128)(2,1)} %get-tuple-element.35), channel_id=1, source_target_pairs={{0,4},{4,8},{8,12},{12,0},{1,5},{5,9},{9,13},{13,1},{2,6},{6,10},{... | collective-permute-start | bytes 393224 | tf_op jit(solution)/shard_map/ppermute | solution.py:20
  5.9 12.2 %collective-permute-start.6 = (bf16[1,64,1024]{2,1,0:T(8,128)(2,1)}, bf16[1,64,1024]{2,1,0:T(8,128)(2,1)S(1)}, u32[]{:S(2)}, u32[]{:S(2)}) collective-permute-start(bf16[1,64,1024]{2,1,0:T(8,128)(2,1)} %get-tuple-element.36), channel_id=1, source_target_pairs={{0,8},{4,12},{8,0},{12,4},{1,9},{5,13},{9,1},{13,5},{2,10},{6,14},... | collective-permute-start | bytes 393224 | tf_op jit(solution)/shard_map/ppermute | solution.py:20
  8.5 9.6 %collective-permute-start.7 = (bf16[1,64,1024]{2,1,0:T(8,128)(2,1)}, bf16[1,64,1024]{2,1,0:T(8,128)(2,1)S(1)}, u32[]{:S(2)}, u32[]{:S(2)}) collective-permute-start(bf16[1,64,1024]{2,1,0:T(8,128)(2,1)} %get-tuple-element.37), channel_id=1, source_target_pairs={{0,12},{4,0},{8,4},{12,8},{1,13},{5,1},{9,5},{13,9},{2,14},{6,2},{... | collective-permute-start | bytes 393224 | tf_op jit(solution)/shard_map/ppermute | solution.py:20
  9.9 23.3 %collective-permute-start.8 = (bf16[1,64,1024]{2,1,0:T(8,128)(2,1)}, bf16[1,64,1024]{2,1,0:T(8,128)(2,1)S(1)}, u32[]{:S(2)}, u32[]{:S(2)}) collective-permute-start(bf16[1,64,1024]{2,1,0:T(8,128)(2,1)} %get-tuple-element.34.refs_0_), channel_id=1, source_target_pairs={{0,16},{16,0},{1,17},{17,1},{2,18},{18,2},{3,19},{19,3},{4,20},{20... | collective-permute-start | bytes 393224 | tf_op jit(solution)/shard_map/ppermute | solution.py:20
  17.1 27.2 %copy-start.8 = (bf16[256,1024]{1,0:T(8,128)(2,1)S(1)}, bf16[256,1024]{1,0:T(8,128)(2,1)}, u32[]{:S(2)}) copy-start(bf16[256,1024]{1,0:T(8,128)(2,1)} %get-tuple-element.48.refs_0_) | copy-start | bytes 1572868
  18.1 22.9 %collective-permute-start.12 = (bf16[128,1024]{1,0:T(8,128)(2,1)S(1)}, bf16[128,1024]{1,0:T(8,128)(2,1)S(1)}, u32[]{:S(2)}, u32[]{:S(2)}) collective-permute-start(bf16[128,1024]{1,0:T(8,128)(2,1)S(1)} %after.15), channel_id=1, source_target_pairs={{0,8},{4,12},{8,0},{12,4},{1,9},{5,13},{9,1},{13,5},{2,10},{6,14},... | collective-permute-start | bytes 786440 | tf_op jit(solution)/shard_map/ppermute | solution.py:24
  21.8 3.9 %collective-permute-start.13 = (s32[8,128]{1,0:T(8,128)}, s32[8,128]{1,0:T(8,128)S(1)}, u32[]{:S(2)}, u32[]{:S(2)}) collective-permute-start(s32[8,128]{1,0:T(8,128)} %get-tuple-element.40), channel_id=1, source_target_pairs={{0,16},{16,0},{1,17},{17,1},{2,18},{18,2},{3,19},{19,3},{4,20},{20... | collective-permute-start | bytes 12296 | tf_op jit(solution)/shard_map/ppermute | solution.py:20
  31.2 8.0 %collective-permute-start.9 = (bf16[1,64,1024]{2,1,0:T(8,128)(2,1)S(1)}, bf16[1,64,1024]{2,1,0:T(8,128)(2,1)S(1)}, u32[]{:S(2)}, u32[]{:S(2)}) collective-permute-start(bf16[1,64,1024]{2,1,0:T(8,128)(2,1)S(1)} %collective-permute-done.5.refs_1_), channel_id=1, source_target_pairs={{0,16},{16,0},{1,17},{17,1},{2,18},{18,2},{3,19},{19,3},{4,20},{20... | collective-permute-start | bytes 393224 | tf_op jit(solution)/shard_map/ppermute | solution.py:20
  32.7 7.0 %collective-permute-start.10 = (bf16[1,64,1024]{2,1,0:T(8,128)(2,1)S(1)}, bf16[1,64,1024]{2,1,0:T(8,128)(2,1)S(1)}, u32[]{:S(2)}, u32[]{:S(2)}) collective-permute-start(bf16[1,64,1024]{2,1,0:T(8,128)(2,1)S(1)} %collective-permute-done.6.refs_2_), channel_id=1, source_target_pairs={{0,16},{16,0},{1,17},{17,1},{2,18},{18,2},{3,19},{19,3},{4,20},{20... | collective-permute-start | bytes 393224 | tf_op jit(solution)/shard_map/ppermute | solution.py:20
  33.2 7.9 %collective-permute-start.11 = (bf16[1,64,1024]{2,1,0:T(8,128)(2,1)S(1)}, bf16[1,64,1024]{2,1,0:T(8,128)(2,1)S(1)}, u32[]{:S(2)}, u32[]{:S(2)}) collective-permute-start(bf16[1,64,1024]{2,1,0:T(8,128)(2,1)S(1)} %collective-permute-done.7.refs_3_), channel_id=1, source_target_pairs={{0,16},{16,0},{1,17},{17,1},{2,18},{18,2},{3,19},{19,3},{4,20},{20... | collective-permute-start | bytes 393224 | tf_op jit(solution)/shard_map/ppermute | solution.py:20
  41.1 1.2 %copy-start.3 = (bf16[256,2048]{1,0:T(8,128)(2,1)S(1)}, bf16[256,2048]{1,0:T(8,128)(2,1)}, u32[]{:S(2)}) copy-start(bf16[256,2048]{1,0:T(8,128)(2,1)} %own_rows.1.refs_8_.refs_2_) | copy-start | bytes 3145732
  43.5 0.8 copy-start.5
  44.3 2.1 %collective-permute-start.14 = (bf16[1024,256]{1,0:T(8,128)(2,1)S(1)}, bf16[1024,256]{1,0:T(8,128)(2,1)S(1)}, u32[]{:S(2)}, u32[]{:S(2)}) collective-permute-start(bf16[1024,256]{1,0:T(8,128)(2,1)S(1)} %get-tuple-element.47), channel_id=1, source_target_pairs={{0,1},{1,0},{2,3},{3,2},{4,5},{5,4},{6,7},{7,6},{8,9},{9,8},{10,11... | collective-permute-start | bytes 1572872 | tf_op jit(solution)/shard_map/ppermute | solution.py:20
  44.4 16.1 %collective-permute-start.16 = (bf16[256,1024]{1,0:T(8,128)(2,1)S(1)}, bf16[256,1024]{1,0:T(8,128)(2,1)S(1)}, u32[]{:S(2)}, u32[]{:S(2)}) collective-permute-start(bf16[256,1024]{1,0:T(8,128)(2,1)S(1)} %after.17), channel_id=1, source_target_pairs={{0,4},{4,8},{8,12},{12,0},{1,5},{5,9},{9,13},{13,1},{2,6},{6,10},{... | collective-permute-start | bytes 1572872 | tf_op jit(solution)/shard_map/ppermute | solution.py:20
  46.4 0.8 copy-start.17
  47.2 13.3 %copy-start.7 = (bf16[256,1024]{1,0:T(8,128)(2,1)S(1)}, bf16[256,1024]{1,0:T(8,128)(2,1)}, u32[]{:S(2)}) copy-start(bf16[256,1024]{1,0:T(8,128)(2,1)} %get-tuple-element.49.refs_0_) | copy-start | bytes 1572868
  47.2 14.8 %copy-start.6 = (bf16[128,1024]{1,0:T(8,128)(2,1)S(1)}, bf16[128,1024]{1,0:T(8,128)(2,1)}, u32[]{:S(2)}) copy-start(bf16[128,1024]{1,0:T(8,128)(2,1)} %get-tuple-element.39.refs_0_) | copy-start | bytes 786436
  60.5 25.5 %collective-permute-start.19 = (bf16[256,1024]{1,0:T(8,128)(2,1)S(1)}, bf16[256,1024]{1,0:T(8,128)(2,1)S(1)}, u32[]{:S(2)}, u32[]{:S(2)}) collective-permute-start(bf16[256,1024]{1,0:T(8,128)(2,1)S(1)} %after.20), channel_id=1, source_target_pairs={{0,8},{4,12},{8,0},{12,4},{1,9},{5,13},{9,1},{13,5},{2,10},{6,14},... | collective-permute-start | bytes 1572872 | tf_op jit(solution)/shard_map/ppermute | solution.py:20
  60.5 29.3 %collective-permute-start.15 = (bf16[2048,256]{1,0:T(8,128)(2,1)}, bf16[2048,256]{1,0:T(8,128)(2,1)S(1)}, u32[]{:S(2)}, u32[]{:S(2)}) collective-permute-start(bf16[2048,256]{1,0:T(8,128)(2,1)} %partial_weights.2.refs_4_.refs_2_), channel_id=1, source_target_pairs={{0,2},{2,0},{1,3},{3,1},{4,6},{6,4},{5,7},{7,5},{8,10},{10,8},{9,1... | collective-permute-start | bytes 3145736 | tf_op jit(solution)/shard_map/ppermute | solution.py:20
  62.0 25.7 %collective-permute-start.22 = (bf16[256,1024]{1,0:T(8,128)(2,1)S(1)}, bf16[256,1024]{1,0:T(8,128)(2,1)}, u32[]{:S(2)}, u32[]{:S(2)}) collective-permute-start(bf16[256,1024]{1,0:T(8,128)(2,1)S(1)} %stack.1.refs_7_), channel_id=1, source_target_pairs={{0,4},{4,0},{8,12},{12,8},{1,5},{5,1},{9,13},{13,9},{2,6},{6,2},{1... | collective-permute-start | bytes 1572872 | tf_op jit(solution)/shard_map/ppermute | solution.py:24
  63.8 22.2 %copy-start.12 = (bf16[64,1024]{1,0:T(8,128)(2,1)S(1)}, bf16[64,1024]{1,0:T(8,128)(2,1)}, u32[]{:S(2)}) copy-start(bf16[64,1024]{1,0:T(8,128)(2,1)} %get-tuple-element.57.refs_0_) | copy-start | bytes 393220
  63.8 23.8 %copy-start.11 = (bf16[64,1024]{1,0:T(8,128)(2,1)S(1)}, bf16[64,1024]{1,0:T(8,128)(2,1)}, u32[]{:S(2)}) copy-start(bf16[64,1024]{1,0:T(8,128)(2,1)} %get-tuple-element.56.refs_0_) | copy-start | bytes 393220
  63.8 23.8 %copy-start.10 = (bf16[64,1024]{1,0:T(8,128)(2,1)S(1)}, bf16[64,1024]{1,0:T(8,128)(2,1)}, u32[]{:S(2)}) copy-start(bf16[64,1024]{1,0:T(8,128)(2,1)} %get-tuple-element.55.refs_0_) | copy-start | bytes 393220
  63.8 23.8 %copy-start.9 = (bf16[64,1024]{1,0:T(8,128)(2,1)S(1)}, bf16[64,1024]{1,0:T(8,128)(2,1)}, u32[]{:S(2)}) copy-start(bf16[64,1024]{1,0:T(8,128)(2,1)} %get-tuple-element.54.refs_0_) | copy-start | bytes 393220
  70.7 22.5 %copy-start.15 = (s32[4,4]{1,0:T(4,128)S(1)}, s32[4,4]{1,0:T(4,128)}, u32[]{:S(2)}) copy-start(s32[4,4]{1,0:T(4,128)} %get-tuple-element.33.table_ref) | copy-start | bytes 196
  70.7 1.6 %copy-start = (f32[2048,256]{1,0:T(8,128)S(1)}, f32[2048,256]{1,0:T(8,128)}, u32[]{:S(2)}) copy-start(f32[2048,256]{1,0:T(8,128)} %partial_weights.3.refs_1_.refs_0_.refs_2_) | copy-start | bytes 6291460
  72.3 20.9 %copy-start.2 = (f32[2048,256]{1,0:T(8,128)S(1)}, f32[2048,256]{1,0:T(8,128)}, u32[]{:S(2)}) copy-start(f32[2048,256]{1,0:T(8,128)} %partial_weights.3.refs_1_.refs_0_.refs_2_) | copy-start | bytes 6291460
  72.3 20.9 %copy-start.4 = (bf16[256,2048]{1,0:T(8,128)(2,1)S(1)}, bf16[256,2048]{1,0:T(8,128)(2,1)}, u32[]{:S(2)}) copy-start(bf16[256,2048]{1,0:T(8,128)(2,1)} %own_rows.1.refs_8_.refs_2_) | copy-start | bytes 3145732
  72.3 1.2 %collective-permute-start.17 = (s32[8,128]{1,0:T(8,128)S(1)}, s32[8,128]{1,0:T(8,128)S(1)}, u32[]{:S(2)}, u32[]{:S(2)}) collective-permute-start(s32[8,128]{1,0:T(8,128)S(1)} %after.18), channel_id=1, source_target_pairs={{0,1},{1,0},{2,3},{3,2},{4,5},{5,4},{6,7},{7,6},{8,9},{9,8},{10,11... | collective-permute-start | bytes 12296 | tf_op jit(solution)/shard_map/ppermute | solution.py:20
  72.3 15.9 %collective-permute-start.21 = (bf16[256,1024]{1,0:T(8,128)(2,1)S(1)}, bf16[256,1024]{1,0:T(8,128)(2,1)S(1)}, u32[]{:S(2)}, u32[]{:S(2)}) collective-permute-start(bf16[256,1024]{1,0:T(8,128)(2,1)S(1)} %stack.1.refs_7_), channel_id=1, source_target_pairs={{0,1},{1,0},{2,3},{3,2},{4,5},{5,4},{6,7},{7,6},{8,9},{9,8},{10,11... | collective-permute-start | bytes 1572872 | tf_op jit(solution)/shard_map/ppermute | solution.py:20
  73.5 16.2 %collective-permute-start.18 = (bf16[256,1024]{1,0:T(8,128)(2,1)S(1)}, bf16[256,1024]{1,0:T(8,128)(2,1)S(1)}, u32[]{:S(2)}, u32[]{:S(2)}) collective-permute-start(bf16[256,1024]{1,0:T(8,128)(2,1)S(1)} %after.19.refs_3_), channel_id=1, source_target_pairs={{0,1},{1,0},{2,3},{3,2},{4,5},{5,4},{6,7},{7,6},{8,9},{9,8},{10,11... | collective-permute-start | bytes 1572872 | tf_op jit(solution)/shard_map/ppermute | solution.py:20
  86.0 1.6 %copy-start.1 = (f32[2048,256]{1,0:T(8,128)S(1)}, f32[2048,256]{1,0:T(8,128)}, u32[]{:S(2)}) copy-start(f32[2048,256]{1,0:T(8,128)} %partial_weights.3.refs_1_.refs_0_.refs_2_) | copy-start | bytes 6291460
  87.6 2.2 %collective-permute-start.20 = (bf16[256,1024]{1,0:T(8,128)(2,1)S(1)}, bf16[256,1024]{1,0:T(8,128)(2,1)S(1)}, u32[]{:S(2)}, u32[]{:S(2)}) collective-permute-start(bf16[256,1024]{1,0:T(8,128)(2,1)S(1)} %after.21.refs_5_), channel_id=1, source_target_pairs={{0,1},{1,0},{2,3},{3,2},{4,5},{5,4},{6,7},{7,6},{8,9},{9,8},{10,11... | collective-permute-start | bytes 1572872 | tf_op jit(solution)/shard_map/ppermute | solution.py:20
  87.7 5.5 %collective-permute-start.23 = (bf16[256,1024]{1,0:T(8,128)(2,1)}, bf16[256,1024]{1,0:T(8,128)(2,1)S(1)}, u32[]{:S(2)}, u32[]{:S(2)}) collective-permute-start(bf16[256,1024]{1,0:T(8,128)(2,1)} %collective-permute-done.22.refs_9_), channel_id=1, source_target_pairs={{0,1},{1,0},{2,3},{3,2},{4,5},{5,4},{6,7},{7,6},{8,9},{9,8},{10,11... | collective-permute-start | bytes 1572872 | tf_op jit(solution)/shard_map/ppermute | solution.py:20
  88.2 10.8 %collective-permute-start.25 = (bf16[64,1024]{1,0:T(8,128)(2,1)S(1)}, bf16[64,1024]{1,0:T(8,128)(2,1)S(1)}, u32[]{:S(2)}, u32[]{:S(2)}) collective-permute-start(bf16[64,1024]{1,0:T(8,128)(2,1)S(1)} %after.22), channel_id=1, source_target_pairs={{0,12},{4,0},{8,4},{12,8},{1,13},{5,1},{9,5},{13,9},{2,14},{6,2},{... | collective-permute-start | bytes 393224 | tf_op jit(solution)/shard_map/ppermute | solution.py:20
  89.7 9.3 %collective-permute-start.27 = (bf16[64,1024]{1,0:T(8,128)(2,1)S(1)}, bf16[64,1024]{1,0:T(8,128)(2,1)S(1)}, u32[]{:S(2)}, u32[]{:S(2)}) collective-permute-start(bf16[64,1024]{1,0:T(8,128)(2,1)S(1)} %after.24), channel_id=1, source_target_pairs={{0,12},{4,0},{8,4},{12,8},{1,13},{5,1},{9,5},{13,9},{2,14},{6,2},{... | collective-permute-start | bytes 393224 | tf_op jit(solution)/shard_map/ppermute | solution.py:20
  89.8 10.4 %collective-permute-start.29 = (bf16[64,1024]{1,0:T(8,128)(2,1)S(1)}, bf16[64,1024]{1,0:T(8,128)(2,1)S(1)}, u32[]{:S(2)}, u32[]{:S(2)}) collective-permute-start(bf16[64,1024]{1,0:T(8,128)(2,1)S(1)} %after.26), channel_id=1, source_target_pairs={{0,12},{4,0},{8,4},{12,8},{1,13},{5,1},{9,5},{13,9},{2,14},{6,2},{... | collective-permute-start | bytes 393224 | tf_op jit(solution)/shard_map/ppermute | solution.py:20
  89.8 12.3 %collective-permute-start.31 = (bf16[64,1024]{1,0:T(8,128)(2,1)S(1)}, bf16[64,1024]{1,0:T(8,128)(2,1)S(1)}, u32[]{:S(2)}, u32[]{:S(2)}) collective-permute-start(bf16[64,1024]{1,0:T(8,128)(2,1)S(1)} %after.28), channel_id=1, source_target_pairs={{0,12},{4,0},{8,4},{12,8},{1,13},{5,1},{9,5},{13,9},{2,14},{6,2},{... | collective-permute-start | bytes 393224 | tf_op jit(solution)/shard_map/ppermute | solution.py:20
  97.6 11.0 %collective-permute-start.24 = (bf16[1024,128]{1,0:T(8,128)(2,1)S(1)}, bf16[1024,128]{1,0:T(8,128)(2,1)S(1)}, u32[]{:S(2)}, u32[]{:S(2)}) collective-permute-start(bf16[1024,128]{1,0:T(8,128)(2,1)S(1)} %get-tuple-element.51.refs_1_), channel_id=1, source_target_pairs={{0,2},{2,0},{1,3},{3,1},{4,6},{6,4},{5,7},{7,5},{8,10},{10,8},{9,1... | collective-permute-start | bytes 786440 | tf_op jit(solution)/shard_map/ppermute | solution.py:20
  99.0 3.1 %collective-permute-start.26 = (bf16[64,1024]{1,0:T(8,128)(2,1)S(1)}, bf16[64,1024]{1,0:T(8,128)(2,1)S(1)}, u32[]{:S(2)}, u32[]{:S(2)}) collective-permute-start(bf16[64,1024]{1,0:T(8,128)(2,1)S(1)} %after.23.refs_0_), channel_id=1, source_target_pairs={{0,1},{1,0},{2,3},{3,2},{4,5},{5,4},{6,7},{7,6},{8,9},{9,8},{10,11... | collective-permute-start | bytes 393224 | tf_op jit(solution)/shard_map/ppermute | solution.py:20
  99.0 3.1 %collective-permute-start.28 = (bf16[64,1024]{1,0:T(8,128)(2,1)S(1)}, bf16[64,1024]{1,0:T(8,128)(2,1)S(1)}, u32[]{:S(2)}, u32[]{:S(2)}) collective-permute-start(bf16[64,1024]{1,0:T(8,128)(2,1)S(1)} %after.25.refs_2_), channel_id=1, source_target_pairs={{0,1},{1,0},{2,3},{3,2},{4,5},{5,4},{6,7},{7,6},{8,9},{9,8},{10,11... | collective-permute-start | bytes 393224 | tf_op jit(solution)/shard_map/ppermute | solution.py:20
  100.2 2.0 %collective-permute-start.30 = (bf16[64,1024]{1,0:T(8,128)(2,1)S(1)}, bf16[64,1024]{1,0:T(8,128)(2,1)S(1)}, u32[]{:S(2)}, u32[]{:S(2)}) collective-permute-start(bf16[64,1024]{1,0:T(8,128)(2,1)S(1)} %after.27.refs_4_), channel_id=1, source_target_pairs={{0,1},{1,0},{2,3},{3,2},{4,5},{5,4},{6,7},{7,6},{8,9},{9,8},{10,11... | collective-permute-start | bytes 393224 | tf_op jit(solution)/shard_map/ppermute | solution.py:20
  102.1 1.3 %collective-permute-start.32 = (bf16[64,1024]{1,0:T(8,128)(2,1)S(1)}, bf16[64,1024]{1,0:T(8,128)(2,1)S(1)}, u32[]{:S(2)}, u32[]{:S(2)}) collective-permute-start(bf16[64,1024]{1,0:T(8,128)(2,1)S(1)} %after.29.refs_6_), channel_id=1, source_target_pairs={{0,1},{1,0},{2,3},{3,2},{4,5},{5,4},{6,7},{7,6},{8,9},{9,8},{10,11... | collective-permute-start | bytes 393224 | tf_op jit(solution)/shard_map/ppermute | solution.py:20
  104.2 4.3 %collective-permute-start.33 = (bf16[256,128]{1,0:T(8,128)(2,1)S(1)}, bf16[256,128]{1,0:T(8,128)(2,1)S(1)}, u32[]{:S(2)}, u32[]{:S(2)}) collective-permute-start(bf16[256,128]{1,0:T(8,128)(2,1)S(1)} %get-tuple-element.59), channel_id=1, source_target_pairs={{0,2},{2,0},{1,3},{3,1},{4,6},{6,4},{5,7},{7,5},{8,10},{10,8},{9,1... | collective-permute-start | bytes 196616 | tf_op jit(solution)/shard_map/ppermute | solution.py:20

commit v9 on v8

--- a/solution.py
+++ b/solution.py
@@ -156,19 +156,19 @@
     return jnp.concatenate(found)
 
 
-def own_rows(goal, train, bulk):
-    def kernel(goal_ref, train_ref, out_ref):
-        out_ref[...] = select(goal_ref, train_ref, lax.axis_index("shard") * bulk, bulk)
-
-    return pl.pallas_call(
-        kernel,
-        in_specs=[VMEM] * 2,
+def own_rows(goal, train, bulk, *others):
+    def kernel(goal_ref, train_ref, *rest):
+        rest[-1][...] = select(goal_ref, train_ref, lax.axis_index("shard") * bulk, bulk)
+
+    return pl.pallas_call(
+        kernel,
+        in_specs=[VMEM] * 2 + [ANY] * len(others),
         out_specs=VMEM,
         out_shape=jax.ShapeDtypeStruct((bulk, train.shape[1]), BF16),
         cost_estimate=cost(2 * bulk * train.size, 2 * train.size),
         compiler_params=FIRST,
         name="own_rows",
-    )(goal, train)
+    )(goal, train, *others)
 
 
 def pack_rows(train, ids, columns, bulk, extra, cuts):
@@ -211,10 +211,10 @@
         for out, (hops, first, _) in zip(outs, cuts):
             fill(out, lax.rem(me + hops, jnp.int32(n_shard)) * bulk + first)
         for j, out in enumerate(outs[len(cuts):]):
-            fill(out, n_shard * bulk + j * extra)
+            fill(out, n_shard * bulk + max(j - 1, 0) * extra)
 
     shapes = [jax.ShapeDtypeStruct((n, columns), BF16) for _, _, n in cuts]
-    shapes += [jax.ShapeDtypeStruct((extra, columns), BF16)] * (2 if extra else 0)
+    shapes += [jax.ShapeDtypeStruct((extra, columns), BF16)] * (3 if extra else 0)
     shapes += [jax.ShapeDtypeStruct((lines, LANES), I32)]
     packed = n_shard * bulk + 2 * extra
     return pl.pallas_call(
@@ -261,10 +261,68 @@
     )(jnp.reshape(block, (1,)).astype(I32), *matrices, *queries, *others)
 
 
-def row_table(ids, lines, bulk, extra):
+def fetch(matrices, block, depth, *others):
+    width = matrices[0].shape[1]
+    n = len(matrices)
+    cuts = 4
+
+    def kernel(block_ref, *refs):
+        outs, sem = refs[-1 - n:-1], refs[-1]
+        first = pl.multiple_of(block_ref[0] * depth, depth)
+        copies = []
+        for j in range(n):
+            for c in range(cuts):
+                size = depth // cuts
+                source = refs[j].at[pl.ds(first + c * size, size)]
+                copies.append(
+                    pltpu.make_async_copy(source, outs[j].at[c * size:(c + 1) * size], sem.at[j * cuts + c])
+                )
+        for copy in copies:
+            copy.start()
+        for copy in copies:
+            copy.wait()
+
+    return pl.pallas_call(
+        kernel,
+        in_specs=[SMEM] + [ANY] * (n + len(others)),
+        out_specs=[VMEM] * n,
+        out_shape=[jax.ShapeDtypeStruct((depth, width), BF16)] * n,
+        scratch_shapes=[pltpu.SemaphoreType.DMA((n * cuts,))],
+        cost_estimate=cost(0, 2 * n * depth * width),
+        compiler_params=PARAMS,
+        name="fetch",
+    )(jnp.reshape(block, (1,)).astype(I32), *matrices, *others)
+
+
+def fetched_weights(matrices, queries, dtype):
+    depth = matrices[0].shape[0]
+    total = queries[0].shape[1]
+    tile = 512 if depth % 512 == 0 else depth
+    n = len(matrices)
+
+    def kernel(*refs):
+        for at in range(0, depth, tile):
+            value = dot(refs[0][at:at + tile, :], refs[n][...])
+            for j in range(1, n):
+                value = value + dot(refs[j][at:at + tile, :], refs[n + j][...])
+            refs[-1][at:at + tile, :] = value.astype(dtype)
+
+    return pl.pallas_call(
+        kernel,
+        in_specs=[VMEM] * (2 * n),
+        out_specs=VMEM,
+        out_shape=jax.ShapeDtypeStruct((depth, total), dtype),
+        cost_estimate=cost(2 * n * matrices[0].size * total, 2 * n * matrices[0].size),
+        compiler_params=PARAMS,
+        name="fetched_weights",
+    )(*matrices, *queries)
+
+
+def row_table(ids, lines, bulk, extra, *others):
     n_shard = ids.shape[0] // lines
 
-    def kernel(ids_ref, table_ref, flag_ref):
+    def kernel(ids_ref, *rest):
+        table_ref, flag_ref = rest[-2:]
         me = lax.axis_index("shard")
         start = jnp.int32(0)
         most = jnp.int32(0)
@@ -292,13 +350,13 @@
 
     return pl.pallas_call(
         kernel,
-        in_specs=[VMEM],
+        in_specs=[VMEM] + [ANY] * len(others),
         out_specs=[SMEM, VMEM],
         out_shape=[jax.ShapeDtypeStruct((n_shard, 4), I32), jax.ShapeDtypeStruct((8, LANES), I32)],
         cost_estimate=cost(0, 4 * ids.size),
         compiler_params=FIRST,
         name="row_table",
-    )(ids)
+    )(ids, *others)
 
 
 def put(acc, x, start, count=None):
@@ -506,46 +564,53 @@
     part = 64 if bulk % 64 == 0 else bulk
     final = [(last_hops, at, part) for at in range(0, bulk, part)]
     *packed, goal = pack_rows(train, ids, columns, bulk, extra, middle + final)
-    table, flag = row_table(ids, lines, bulk, extra)
-    mine = own_rows(goal, train, bulk)
-    before_join, firsts, seconds = [mine], [], []
+    before_join, firsts, seconds = [], [], []
     if extra:
-        for d in range(1, n_group):
-            flag = jnp.maximum(flag, shift(flag, "groups", n_group, d))
-
-        def second_round(x):
-            pair = jnp.concatenate([x, swap(x, "shard", n_shard, 2)])
-            return [with_rep(pair), with_rep(swap(pair, "shard", n_shard, 1))]
-
-        def no_round(x):
-            return [[jnp.zeros((2 * extra, columns), BF16)] * n_rep] * 2
-
-        seconds = lax.cond(flag[0, 0] > 0, second_round, no_round, after(packed[-1], *pieces[1:]))
         far = swap(after(packed[-2], *pieces[1:]), "shard", n_shard, 2)
-        before_join += [far] + [x for parts in seconds for x in parts]
+        before_join = [far]
+    depth = n_rep * columns
+    targets = [(feat + d) % n_feat for d in range(1, n_feat)]
+    near_chip = fetch(matrices, targets[0], depth, *pieces[1:])
 
     parts = [pieces] + [[shift(x, "groups", n_group, d) for x in pieces] for d in range(1, n_group)]
-    chosen = join_queries(parts, block_slot, pattern, query_store.shape[0], n_feat, n_rep, *before_join)
+    chosen = join_queries(
+        parts, block_slot, pattern, query_store.shape[0], n_feat, n_rep, *before_join, *near_chip
+    )
     queries = [chosen[0]] + [shift(chosen[d], "rep", n_rep, d) for d in range(1, n_rep)]
-    here = [shift(after(packed[0], *before_join[1:2]), "shard", n_shard, 1)]
-
-    def weights(f, dtype, *others):
-        return partial_weights(matrices, queries, f, n_rep * columns, dtype, *others)
-
-    sends = [weights((feat + d) % n_feat, BF16) for d in range(1, n_feat)]
+    here = [shift(after(packed[0], *before_join), "shard", n_shard, 1)]
+
+    sends = [fetched_weights(near_chip, queries, BF16)]
+    sends += [partial_weights(matrices, queries, f, depth, BF16) for f in targets[1:]]
     others = [shift(x, "feat", n_feat, d + 1) for d, x in enumerate(sends)]
-    own = weights(feat, F32, *sends)
+    own = partial_weights(matrices, queries, feat, depth, F32, *sends)
 
     for (hops, _, _), x in zip(middle[1:], packed[1:]):
         here.append(shift(after(x, here[-1], *sends), "shard", n_shard, hops))
     last = [
         shift(after(packed[len(middle) + j], here[-1], own), "shard", n_shard, last_hops) for j in range(len(final))
     ]
+
+    mine = own_rows(goal, train, bulk, own)
+    table, flag = row_table(ids, lines, bulk, extra, own)
+    marks = [own, mine]
     if extra:
-        pair = stack([packed[-2], far], *sends)
-        firsts = [with_rep(pair), with_rep(swap(pair, "shard", n_shard, 1))]
-
-    mark = shift(after(jnp.zeros((8, LANES), I32), own), "rep", n_rep, 1)
+        for d in range(1, n_group):
+            flag = jnp.maximum(flag, shift(flag, "groups", n_group, d))
+
+        def second_round(x):
+            pair = jnp.concatenate([x, swap(x, "shard", n_shard, 2)])
+            return [with_rep(pair), with_rep(swap(pair, "shard", n_shard, 1))]
+
+        def no_round(x):
+            return [[jnp.zeros((2 * extra, columns), BF16)] * n_rep] * 2
+
+        seconds = lax.cond(flag[0, 0] > 0, second_round, no_round, packed[-1])
+        pair = stack([packed[-3], far], *sends)
+        near = swap(pair, "shard", n_shard, 1)
+        firsts = [with_rep(pair), with_rep(near)]
+        marks += [seconds[0][0], near]
+
+    mark = shift(after(jnp.zeros((8, LANES), I32), *marks), "rep", n_rep, 1)
     ready = [with_rep(after(x, mark)) for x in here]
     high, low, *early = early_scores(
         own, others, mine, ready, middle, firsts, seconds, table, rows, n_feat, n_rep, n_shard, bulk, extra

time: 111 us -> 101 us (0.910)
  waiting for transfers between devices: 30.7 us -> 22.8 us
  local copies, waits for them, and re-layouts: 11.1 us -> 9.45 us
  Pallas kernels: 35.8 us -> 37.1 us
    ppermute x28, waiting for transfers between devices: 30.7 us -> 22.8 us  [shift(): return lax.ppermute(x, axis, [(i, (i + by) % size) for i in range(size)])]
    pallas_call x2 -> x1, Pallas kernels: 13.5 us -> 6.75 us  [partial_weights(): pl.pallas_call(kernel, grid_spec=pltpu.PrefetchScalarGridSpec(num_scalar_...]
    pallas_call x2 -> x4, Pallas kernels: 5.96 us -> 12 us  [the longest x1 4.64 us: own_rows(): pl.pallas_call(kernel, in_specs=[VMEM] * 2 + [ANY] * len(others), out_spe...]
    unnamed x37 -> x36, local copies, waits for them, and re-layouts: 7.03 us -> 5.51 us
  transfers between devices with their start and end apart: 30 -> 30, of which waited for: 10 -> 8; matrix products, arithmetic and copies ran while one was open for 5% -> 4% of each run, Pallas kernels for 31% -> 34%
where the time goes in v9:
time: 101 us
  Pallas kernels  37.1 us (37%)
  starting transfers between devices  30.4 us (30%)
  waiting for transfers between devices  22.8 us (23%)
  local copies, waits for them, and re-layouts  9.45 us (9%)
    ppermute x28, starting transfers between devices, shift(): return lax.ppermute(x, axis, [(i, (i + by) % size) for i in range(size)])  26.2 us
    ppermute x28, waiting for transfers between devices, shift(): return lax.ppermute(x, axis, [(i, (i + by) % size) for i in range(size)])  22.8 us
    pallas_call x1, Pallas kernels, partial_weights(): pl.pallas_call(kernel, grid_spec=pltpu.PrefetchScalarGridSpec(num_scalar_...  6.75 us
    pallas_call x1, Pallas kernels, pack_rows(): pl.pallas_call(kernel, grid=(1,), in_specs=[pl.BlockSpec((lines, LANES),...  6.21 us
    unnamed x36, local copies, waits for them, and re-layouts  5.51 us
    pallas_call x1, Pallas kernels, early_scores(): pl.pallas_call(kernel, in_specs=[SMEM] + [VMEM] * (2 + n_other + n_rep *...  4.94 us
    pallas_call x1, Pallas kernels, own_rows(): pl.pallas_call(kernel, in_specs=[VMEM] * 2 + [ANY] * len(others), out_spe...  4.64 us
    ppermute x2, starting transfers between devices, swap(): return lax.ppermute(x, axis, [(i, i ^ bit) for i in range(size)])  4.21 us
  transfers between devices with their start and end apart: 30, of which 8 were waited for; matrix products, arithmetic and copies ran while one was open for 4% of the time, Pallas kernels for 34%

profile of v9, /device:TPU:0, one launch (start us, length us, event | category | flops | bytes accessed | tf_op | source)
XLA Modules:
  0.0 100.7 jit_solution(12595177438974706476)
XLA Ops:
  0.5 2.7 %pick_queries.1 = (bf16[1,64,1024]{2,1,0:T(8,128)(2,1)}, bf16[1,64,1024]{2,1,0:T(8,128)(2,1)}, bf16[1,64,1024]{2,1,0:T(8,128)(2,1)}, bf16[1,64,1024]{2,1,0:T(8,128)(2,1)}) custom-call(s32[4,4]{1,0:T(4,128)} %pattern_ref.3, s32[16]{0:T(128)} %slot_ref.3, bf16[4,128,1024]{2,1,0:T(8,128)(2,1)} %in_ref.1), custom_call_target="tpu_custom_call" | custom-call | flops 1 | bytes 1 | tf_op jit(solution)/shard_map/pick_queries/pallas_call | solution.py:92
  3.1 2.6 %collective-permute-start.5 = (bf16[1,64,1024]{2,1,0:T(8,128)(2,1)}, bf16[1,64,1024]{2,1,0:T(8,128)(2,1)S(1)}, u32[]{:S(2)}, u32[]{:S(2)}) collective-permute-start(bf16[1,64,1024]{2,1,0:T(8,128)(2,1)} %get-tuple-element.37), channel_id=1, source_target_pairs={{0,4},{4,8},{8,12},{12,0},{1,5},{5,9},{9,13},{13,1},{2,6},{6,10},{... | collective-permute-start | bytes 393224 | tf_op jit(solution)/shard_map/ppermute | solution.py:20
  5.8 2.6 %collective-permute-start.6 = (bf16[1,64,1024]{2,1,0:T(8,128)(2,1)}, bf16[1,64,1024]{2,1,0:T(8,128)(2,1)S(1)}, u32[]{:S(2)}, u32[]{:S(2)}) collective-permute-start(bf16[1,64,1024]{2,1,0:T(8,128)(2,1)} %get-tuple-element.38), channel_id=1, source_target_pairs={{0,8},{4,12},{8,0},{12,4},{1,9},{5,13},{9,1},{13,5},{2,10},{6,14},... | collective-permute-start | bytes 393224 | tf_op jit(solution)/shard_map/ppermute | solution.py:20
  8.4 1.3 %collective-permute-start.7 = (bf16[1,64,1024]{2,1,0:T(8,128)(2,1)}, bf16[1,64,1024]{2,1,0:T(8,128)(2,1)S(1)}, u32[]{:S(2)}, u32[]{:S(2)}) collective-permute-start(bf16[1,64,1024]{2,1,0:T(8,128)(2,1)} %get-tuple-element.39), channel_id=1, source_target_pairs={{0,12},{4,0},{8,4},{12,8},{1,13},{5,1},{9,5},{13,9},{2,14},{6,2},{... | collective-permute-start | bytes 393224 | tf_op jit(solution)/shard_map/ppermute | solution.py:20
  9.7 6.2 %pack_rows.1 = (bf16[256,1024]{1,0:T(8,128)(2,1)}, bf16[256,1024]{1,0:T(8,128)(2,1)}, bf16[64,1024]{1,0:T(8,128)(2,1)}, bf16[64,1024]{1,0:T(8,128)(2,1)}, bf16[6...) custom-call(s32[32,128]{1,0:T(8,128)} %bitcast.9, ...), custom_call_target="tpu_custom_call" | custom-call | flops 1 | bytes 1 | tf_op jit(solution)/shard_map/pack_rows/pallas_call | solution.py:220
  15.9 1.9 %collective-permute-done.6.refs_2_.refs_3_ = bf16[1,64,1024]{2,1,0:T(8,128)(2,1)S(1)} collective-permute-done((bf16[1,64,1024]{2,1,0:T(8,128)(2,1)}, bf16[1,64,1024]{2,1,0:T(8,128)(2,1)S(1)}, u32[]{:S(2)}, u32[]{:S(2)}) %collective-permute-start.6) | collective-permute-done | bytes 131104 | tf_op jit(solution)/shard_map/ppermute | solution.py:20
  17.9 2.4 %collective-permute-start.12 = (bf16[128,1024]{1,0:T(8,128)(2,1)}, bf16[128,1024]{1,0:T(8,128)(2,1)S(1)}, u32[]{:S(2)}, u32[]{:S(2)}) collective-permute-start(bf16[128,1024]{1,0:T(8,128)(2,1)} %after.14), channel_id=1, source_target_pairs={{0,8},{4,12},{8,0},{12,4},{1,9},{5,13},{9,1},{13,5},{2,10},{6,14},... | collective-permute-start | bytes 786440 | tf_op jit(solution)/shard_map/ppermute | solution.py:24
  20.3 1.5 %collective-permute-start.8 = (bf16[1,64,1024]{2,1,0:T(8,128)(2,1)S(1)}, bf16[1,64,1024]{2,1,0:T(8,128)(2,1)S(1)}, u32[]{:S(2)}, u32[]{:S(2)}) collective-permute-start(bf16[1,64,1024]{2,1,0:T(8,128)(2,1)S(1)} %copy-done.8), channel_id=1, source_target_pairs={{0,16},{16,0},{1,17},{17,1},{2,18},{18,2},{3,19},{19,3},{4,20},{20... | collective-permute-start | bytes 393224 | tf_op jit(solution)/shard_map/ppermute | solution.py:20
  21.8 0.5 collective-permute-start.10
  22.3 1.5 %collective-permute-start.11 = (bf16[1,64,1024]{2,1,0:T(8,128)(2,1)S(1)}, bf16[1,64,1024]{2,1,0:T(8,128)(2,1)S(1)}, u32[]{:S(2)}, u32[]{:S(2)}) collective-permute-start(bf16[1,64,1024]{2,1,0:T(8,128)(2,1)S(1)} %collective-permute-done.7.refs_3_.refs_4_), channel_id=1, source_target_pairs={{0,16},{16,0},{1,17},{17,1},{2,18},{18,2},{3,19},{19,3},{4,20},{20... | collective-permute-start | bytes 393224 | tf_op jit(solution)/shard_map/ppermute | solution.py:20
  23.8 0.5 collective-permute-start.9
  24.3 3.4 %copy-done.1 = bf16[1,4096,1024]{2,1,0:T(8,128)(2,1)S(1)} copy-done((bf16[1,4096,1024]{2,1,0:T(8,128)(2,1)S(1)}, bf16[1,4096,1024]{2,1,0:T(8,128)(2,1)}, u32[]{:S(2)}) %copy-start.1) | copy-done | bytes 8388632
  27.7 2.5 %fetch.1 = (bf16[2048,1024]{1,0:T(8,128)(2,1)S(1)}, bf16[2048,1024]{1,0:T(8,128)(2,1)S(1)}) custom-call(s32[1]{0:T(128)} %bitcast.3.block_ref, bf16[4096,1024]{1,0:T(8,128)(2,1)S(1)} %bitcast.8, bf16[4096,1024]{1,0:T(8,128)(2,1)} %collective-permute-done.4.refs_1_, bf16[1,64,1024]{2,1,0:T(8,128)(2,1)S(1)} %collective-permute-done.5.refs_1_.refs_2_, ...), custom_call_target="tpu_custom_call" | custom-call | flops 1 | bytes 1 | tf_op jit(solution)/shard_map/fetch/pallas_call | solution.py:285
  30.2 2.0 %collective-permute-done.11.refs_7_ = bf16[1,64,1024]{2,1,0:T(8,128)(2,1)S(1)} collective-permute-done((bf16[1,64,1024]{2,1,0:T(8,128)(2,1)S(1)}, bf16[1,64,1024]{2,1,0:T(8,128)(2,1)S(1)}, u32[]{:S(2)}, u32[]{:S(2)}) %collective-permute-start.11) | collective-permute-done | bytes 131104 | tf_op jit(solution)/shard_map/ppermute | solution.py:20
  32.3 1.6 %collective-permute-done.9.refs_5_ = bf16[1,64,1024]{2,1,0:T(8,128)(2,1)S(1)} collective-permute-done((bf16[1,64,1024]{2,1,0:T(8,128)(2,1)S(1)}, bf16[1,64,1024]{2,1,0:T(8,128)(2,1)S(1)}, u32[]{:S(2)}, u32[]{:S(2)}) %collective-permute-start.9) | collective-permute-done | bytes 131104 | tf_op jit(solution)/shard_map/ppermute | solution.py:20
  33.9 1.2 %join_queries.1 = (bf16[1024,256]{1,0:T(8,128)(2,1)S(1)}, bf16[1024,256]{1,0:T(8,128)(2,1)S(1)}) custom-call(s32[4,4]{1,0:T(4,128)S(1)} %copy-done.13, s32[16]{0:T(128)S(1)} %copy-done.15, bf16[1,64,1024]{2,1,0:T(8,128)(2,1)S(1)} %copy-done.8, bf16[1,64,1024]{2,1,0:T(8,128)(2,1)S(1)} %collective-permute-done.5.refs_1_.refs_2_, ...), custom_call_target="tpu_custom_call" | custom-call | flops 1 | bytes 1 | tf_op jit(solution)/shard_map/join_queries/pallas_call | solution.py:137
  35.2 2.3 %collective-permute-start.15 = (bf16[256,1024]{1,0:T(8,128)(2,1)S(1)}, bf16[256,1024]{1,0:T(8,128)(2,1)S(1)}, u32[]{:S(2)}, u32[]{:S(2)}) collective-permute-start(bf16[256,1024]{1,0:T(8,128)(2,1)S(1)} %after.15), channel_id=1, source_target_pairs={{0,4},{4,8},{8,12},{12,0},{1,5},{5,9},{9,13},{13,1},{2,6},{6,10},{... | collective-permute-start | bytes 1572872 | tf_op jit(solution)/shard_map/ppermute | solution.py:20
  37.5 3.3 %fetched_weights.1.refs_4_.refs_2_ = bf16[2048,256]{1,0:T(8,128)(2,1)} custom-call(bf16[2048,1024]{1,0:T(8,128)(2,1)S(1)} %get-tuple-element.41.refs_9_.refs_0_, bf16[2048,1024]{1,0:T(8,128)(2,1)S(1)} %get-tuple-element.42.refs_10_.refs_1_, bf16[1024,256]{1,0:T(8,128)(2,1)S(1)} %get-tuple-element.43.refs_2_, ...), custom_call_target="tpu_custom_call" | custom-call | flops 1 | bytes 1 | tf_op jit(solution)/shard_map/fetched_weights/pallas_call | solution.py:310
  40.8 0.8 stack.1.refs_7_
  41.6 1.8 %collective-permute-start.17 = (bf16[256,1024]{1,0:T(8,128)(2,1)}, bf16[256,1024]{1,0:T(8,128)(2,1)}, u32[]{:S(2)}, u32[]{:S(2)}) collective-permute-start(bf16[256,1024]{1,0:T(8,128)(2,1)} %stack.1.refs_7_), channel_id=1, source_target_pairs={{0,4},{4,0},{8,12},{12,8},{1,5},{5,1},{9,13},{13,9},{2,6},{6,2},{1... | collective-permute-start | bytes 1572872 | tf_op jit(solution)/shard_map/ppermute | solution.py:24
  43.5 8.3 %collective-permute-done.15.refs_0_.refs_1_ = bf16[256,1024]{1,0:T(8,128)(2,1)S(1)} collective-permute-done((bf16[256,1024]{1,0:T(8,128)(2,1)S(1)}, bf16[256,1024]{1,0:T(8,128)(2,1)S(1)}, u32[]{:S(2)}, u32[]{:S(2)}) %collective-permute-start.15) | collective-permute-done | bytes 524320 | tf_op jit(solution)/shard_map/ppermute | solution.py:20
  51.8 1.5 %collective-permute-start.14 = (bf16[2048,256]{1,0:T(8,128)(2,1)}, bf16[2048,256]{1,0:T(8,128)(2,1)}, u32[]{:S(2)}, u32[]{:S(2)}) collective-permute-start(bf16[2048,256]{1,0:T(8,128)(2,1)} %fetched_weights.1.refs_4_.refs_2_), channel_id=1, source_target_pairs={{0,2},{2,0},{1,3},{3,1},{4,6},{6,4},{5,7},{7,5},{8,10},{10,8},{9,1... | collective-permute-start | bytes 3145736 | tf_op jit(solution)/shard_map/ppermute | solution.py:20
  53.3 6.7 %partial_weights.1.rest_0_.refs_1_.refs_0_.refs_2_ = f32[2048,256]{1,0:T(8,128)} custom-call(s32[1]{0:T(128)} %bitcast.1.block_ref, bf16[4096,1024]{1,0:T(8,128)(2,1)} %bitcast.7, bf16[4096,1024]{1,0:T(8,128)(2,1)} %collective-permute-done.4.refs_1_, bf16[1024,256]{1,0:T(8,128)(2,1)} %copy-done.4, bf16[1024,256]{1,0:T(8,128)(2,1)} %copy-done.5, ...), custom_call_target="tpu_custom_call" | custom-call | flops 1 | bytes 1 | tf_op jit(solution)/shard_map/partial_weights/pallas_call | solution.py:247
  60.0 1.5 %row_table.1 = (s32[4,4]{1,0:T(4,128)}, s32[8,128]{1,0:T(8,128)}) custom-call(s32[32,128]{1,0:T(8,128)} %bitcast.10, f32[2048,256]{1,0:T(8,128)} %partial_weights.1.rest_0_.refs_1_.refs_0_.refs_2_), custom_call_target="tpu_custom_call" | custom-call | flops 1 | bytes 1 | tf_op jit(solution)/shard_map/row_table/pallas_call | solution.py:351
  61.6 1.6 %collective-permute-start.16 = (s32[8,128]{1,0:T(8,128)}, s32[8,128]{1,0:T(8,128)S(1)}, u32[]{:S(2)}, u32[]{:S(2)}) collective-permute-start(s32[8,128]{1,0:T(8,128)} %get-tuple-element.48), channel_id=1, source_target_pairs={{0,16},{16,0},{1,17},{17,1},{2,18},{18,2},{3,19},{19,3},{4,20},{20... | collective-permute-start | bytes 12296 | tf_op jit(solution)/shard_map/ppermute | solution.py:20
  63.2 4.6 %own_rows.1.refs_2_ = bf16[256,2048]{1,0:T(8,128)(2,1)} custom-call(s32[8,128]{1,0:T(8,128)} %get-tuple-element.46.goal_ref, bf16[1024,2048]{1,0:T(8,128)(2,1)} %train_ref.3, f32[2048,256]{1,0:T(8,128)} %partial_weights.1.rest_0_.refs_1_.refs_0_.refs_2_), custom_call_target="tpu_custom_call" | custom-call | flops 1 | bytes 1 | tf_op jit(solution)/shard_map/own_rows/pallas_call | solution.py:163
  67.8 0.5 slice.3
  69.0 3.4 %conditional.1 = (bf16[256,1024]{1,0:T(8,128)(2,1)}, bf16[256,1024]{1,0:T(8,128)(2,1)}, bf16[256,1024]{1,0:T(8,128)(2,1)}, bf16[256,1024]{1,0:T(8,128)(2,1)}) conditional(s32[]{:T(128)} %bitcast.4, () %tuple.13, bf16[128,1024]{1,0:T(8,128)(2,1)S(1)} %copy-done.16), branch_computations={%region_0.1_spmd, %region_1.2_spmd} | conditional | bytes 8388800 | solution.py:607
  69.0 0.9 broadcast.3
  69.9 0.8 broadcast.3.clone
  70.7 0.9 broadcast.3.clone.1
  71.6 0.9 broadcast.3.clone.2
  72.5 1.2 %copy-done.2 = bf16[256,2048]{1,0:T(8,128)(2,1)S(1)} copy-done((bf16[256,2048]{1,0:T(8,128)(2,1)S(1)}, bf16[256,2048]{1,0:T(8,128)(2,1)}, u32[]{:S(2)}) %copy-start.2) | copy-done | bytes 1048600
  73.7 0.5 collective-permute-start.22
  74.2 3.0 %collective-permute-done.20.refs_0_.refs_1_ = bf16[256,1024]{1,0:T(8,128)(2,1)S(1)} collective-permute-done((bf16[256,1024]{1,0:T(8,128)(2,1)}, bf16[256,1024]{1,0:T(8,128)(2,1)S(1)}, u32[]{:S(2)}, u32[]{:S(2)}) %collective-permute-start.20) | collective-permute-done | bytes 524320 | tf_op jit(solution)/shard_map/ppermute | solution.py:20
  77.3 0.8 copy-done.9
  78.6 1.5 %collective-permute-start.31 = (bf16[64,1024]{1,0:T(8,128)(2,1)S(1)}, bf16[64,1024]{1,0:T(8,128)(2,1)S(1)}, u32[]{:S(2)}, u32[]{:S(2)}) collective-permute-start(bf16[64,1024]{1,0:T(8,128)(2,1)S(1)} %after.26), channel_id=1, source_target_pairs={{0,12},{4,0},{8,4},{12,8},{1,13},{5,1},{9,5},{13,9},{2,14},{6,2},{... | collective-permute-start | bytes 393224 | tf_op jit(solution)/shard_map/ppermute | solution.py:20
  80.4 0.6 collective-permute-start.27
  81.0 2.6 %collective-permute-start.25 = (bf16[64,1024]{1,0:T(8,128)(2,1)S(1)}, bf16[64,1024]{1,0:T(8,128)(2,1)S(1)}, u32[]{:S(2)}, u32[]{:S(2)}) collective-permute-start(bf16[64,1024]{1,0:T(8,128)(2,1)S(1)} %after.20), channel_id=1, source_target_pairs={{0,12},{4,0},{8,4},{12,8},{1,13},{5,1},{9,5},{13,9},{2,14},{6,2},{... | collective-permute-start | bytes 393224 | tf_op jit(solution)/shard_map/ppermute | solution.py:20
  83.6 4.9 %early_scores.1 = (bf16[2048,256]{1,0:T(8,128)(2,1)S(1)}, bf16[2048,256]{1,0:T(8,128)(2,1)S(1)}, f32[1024,128]{1,0:T(8,128)S(1)}, bf16[1024,128]{1,0:T(8,128)(2,1)S(1)}) custom-call(s32[4,4]{1,0:T(4,128)S(1)} %copy-done.14, f32[2048,256]{1,0:T(8,128)S(1)} %copy-done, bf16[2048,256]{1,0:T(8,128)(2,1)} %collective-permute-done.14.refs_1_, ...), custom_call_target="tpu_custom_call" | custom-call | flops 1 | bytes 1 | tf_op jit(solution)/shard_map/early_scores/pallas_call | solution.py:467
  88.5 1.6 %collective-permute-start.24 = (bf16[1024,128]{1,0:T(8,128)(2,1)S(1)}, bf16[1024,128]{1,0:T(8,128)(2,1)S(1)}, u32[]{:S(2)}, u32[]{:S(2)}) collective-permute-start(bf16[1024,128]{1,0:T(8,128)(2,1)S(1)} %get-tuple-element.57.refs_1_), channel_id=1, source_target_pairs={{0,2},{2,0},{1,3},{3,1},{4,6},{6,4},{5,7},{7,5},{8,10},{10,8},{9,1... | collective-permute-start | bytes 786440 | tf_op jit(solution)/shard_map/ppermute | solution.py:20
  90.1 0.5 collective-permute-start.30
  90.7 1.8 %collective-permute-done.25.refs_0_ = bf16[64,1024]{1,0:T(8,128)(2,1)S(1)} collective-permute-done((bf16[64,1024]{1,0:T(8,128)(2,1)S(1)}, bf16[64,1024]{1,0:T(8,128)(2,1)S(1)}, u32[]{:S(2)}, u32[]{:S(2)}) %collective-permute-start.25) | collective-permute-done | bytes 131104 | tf_op jit(solution)/shard_map/ppermute | solution.py:20
  92.6 1.3 %collective-permute-done.26.refs_1_ = bf16[64,1024]{1,0:T(8,128)(2,1)S(1)} collective-permute-done((bf16[64,1024]{1,0:T(8,128)(2,1)S(1)}, bf16[64,1024]{1,0:T(8,128)(2,1)S(1)}, u32[]{:S(2)}, u32[]{:S(2)}) %collective-permute-start.26) | collective-permute-done | bytes 131104 | tf_op jit(solution)/shard_map/ppermute | solution.py:20
  93.9 0.7 late_scores.1
  94.6 1.6 %collective-permute-start.33 = (bf16[256,128]{1,0:T(8,128)(2,1)S(1)}, bf16[256,128]{1,0:T(8,128)(2,1)S(1)}, u32[]{:S(2)}, u32[]{:S(2)}) collective-permute-start(bf16[256,128]{1,0:T(8,128)(2,1)S(1)} %get-tuple-element.65), channel_id=1, source_target_pairs={{0,2},{2,0},{1,3},{3,1},{4,6},{6,4},{5,7},{7,5},{8,10},{10,8},{9,1... | collective-permute-start | bytes 196616 | tf_op jit(solution)/shard_map/ppermute | solution.py:20
  96.2 2.8 %collective-permute-done.33.refs_3_ = bf16[256,128]{1,0:T(8,128)(2,1)S(1)} collective-permute-done((bf16[256,128]{1,0:T(8,128)(2,1)S(1)}, bf16[256,128]{1,0:T(8,128)(2,1)S(1)}, u32[]{:S(2)}, u32[]{:S(2)}) %collective-permute-start.33) | collective-permute-done | bytes 65568 | tf_op jit(solution)/shard_map/ppermute | solution.py:20
  99.0 1.7 %merge.1 = f32[128,1024]{1,0:T(8,128)} custom-call(s32[4,4]{1,0:T(4,128)S(1)} %copy-done.14, f32[1024,128]{1,0:T(8,128)S(1)} %get-tuple-element.56.refs_0_, bf16[1024,128]{1,0:T(8,128)(2,1)S(1)} %collective-permute-done.24.refs_1_, f32[256,128]{1,0:T(8,128)S(1)} %get-tuple-element.64.refs_2_, bf16[256,128]{1,0:T(8,128)(2,1)S(1)} %collective-permute-done.33.refs_3_), custom_call_target="tpu_custom_call" | custom-call | flops 1 | bytes 1 | tf_op jit(solution)/shard_map/merge/pallas_call | solution.py:529
  (82 shorter events, 1.5 us)
Async XLA Ops:
  0.0 23.8 %collective-permute-start.4 = (bf16[4096,1024]{1,0:T(8,128)(2,1)}, bf16[4096,1024]{1,0:T(8,128)(2,1)}, u32[]{:S(2)}, u32[]{:S(2)}) collective-permute-start(bf16[4096,1024]{1,0:T(8,128)(2,1)} %bitcast.6), channel_id=1, source_target_pairs={{0,1},{1,0},{2,3},{3,2},{4,5},{5,4},{6,7},{7,6},{8,9},{9,8},{10,11... | collective-permute-start | bytes 25165832 | tf_op jit(solution)/shard_map/ppermute | solution.py:20
  3.1 17.1 %copy-start.8 = (bf16[1,64,1024]{2,1,0:T(8,128)(2,1)S(1)}, bf16[1,64,1024]{2,1,0:T(8,128)(2,1)}, u32[]{:S(2)}) copy-start(bf16[1,64,1024]{2,1,0:T(8,128)(2,1)} %get-tuple-element.36.refs_0_) | copy-start | bytes 393220
  3.1 12.8 %collective-permute-start.5 = (bf16[1,64,1024]{2,1,0:T(8,128)(2,1)}, bf16[1,64,1024]{2,1,0:T(8,128)(2,1)S(1)}, u32[]{:S(2)}, u32[]{:S(2)}) collective-permute-start(bf16[1,64,1024]{2,1,0:T(8,128)(2,1)} %get-tuple-element.37), channel_id=1, source_target_pairs={{0,4},{4,8},{8,12},{12,0},{1,5},{5,9},{9,13},{13,1},{2,6},{6,10},{... | collective-permute-start | bytes 393224 | tf_op jit(solution)/shard_map/ppermute | solution.py:20
  5.8 12.1 %collective-permute-start.6 = (bf16[1,64,1024]{2,1,0:T(8,128)(2,1)}, bf16[1,64,1024]{2,1,0:T(8,128)(2,1)S(1)}, u32[]{:S(2)}, u32[]{:S(2)}) collective-permute-start(bf16[1,64,1024]{2,1,0:T(8,128)(2,1)} %get-tuple-element.38), channel_id=1, source_target_pairs={{0,8},{4,12},{8,0},{12,4},{1,9},{5,13},{9,1},{13,5},{2,10},{6,14},... | collective-permute-start | bytes 393224 | tf_op jit(solution)/shard_map/ppermute | solution.py:20
  8.4 9.5 %collective-permute-start.7 = (bf16[1,64,1024]{2,1,0:T(8,128)(2,1)}, bf16[1,64,1024]{2,1,0:T(8,128)(2,1)S(1)}, u32[]{:S(2)}, u32[]{:S(2)}) collective-permute-start(bf16[1,64,1024]{2,1,0:T(8,128)(2,1)} %get-tuple-element.39), channel_id=1, source_target_pairs={{0,12},{4,0},{8,4},{12,8},{1,13},{5,1},{9,5},{13,9},{2,14},{6,2},{... | collective-permute-start | bytes 393224 | tf_op jit(solution)/shard_map/ppermute | solution.py:20
  17.9 16.0 %collective-permute-start.12 = (bf16[128,1024]{1,0:T(8,128)(2,1)}, bf16[128,1024]{1,0:T(8,128)(2,1)S(1)}, u32[]{:S(2)}, u32[]{:S(2)}) collective-permute-start(bf16[128,1024]{1,0:T(8,128)(2,1)} %after.14), channel_id=1, source_target_pairs={{0,8},{4,12},{8,0},{12,4},{1,9},{5,13},{9,1},{13,5},{2,10},{6,14},... | collective-permute-start | bytes 786440 | tf_op jit(solution)/shard_map/ppermute | solution.py:24
  20.3 10.0 %collective-permute-start.8 = (bf16[1,64,1024]{2,1,0:T(8,128)(2,1)S(1)}, bf16[1,64,1024]{2,1,0:T(8,128)(2,1)S(1)}, u32[]{:S(2)}, u32[]{:S(2)}) collective-permute-start(bf16[1,64,1024]{2,1,0:T(8,128)(2,1)S(1)} %copy-done.8), channel_id=1, source_target_pairs={{0,16},{16,0},{1,17},{17,1},{2,18},{18,2},{3,19},{19,3},{4,20},{20... | collective-permute-start | bytes 393224 | tf_op jit(solution)/shard_map/ppermute | solution.py:20
  21.8 8.5 %collective-permute-start.10 = (bf16[1,64,1024]{2,1,0:T(8,128)(2,1)S(1)}, bf16[1,64,1024]{2,1,0:T(8,128)(2,1)S(1)}, u32[]{:S(2)}, u32[]{:S(2)}) collective-permute-start(bf16[1,64,1024]{2,1,0:T(8,128)(2,1)S(1)} %collective-permute-done.6.refs_2_.refs_3_), channel_id=1, source_target_pairs={{0,16},{16,0},{1,17},{17,1},{2,18},{18,2},{3,19},{19,3},{4,20},{20... | collective-permute-start | bytes 393224 | tf_op jit(solution)/shard_map/ppermute | solution.py:20
  22.3 10.0 %collective-permute-start.11 = (bf16[1,64,1024]{2,1,0:T(8,128)(2,1)S(1)}, bf16[1,64,1024]{2,1,0:T(8,128)(2,1)S(1)}, u32[]{:S(2)}, u32[]{:S(2)}) collective-permute-start(bf16[1,64,1024]{2,1,0:T(8,128)(2,1)S(1)} %collective-permute-done.7.refs_3_.refs_4_), channel_id=1, source_target_pairs={{0,16},{16,0},{1,17},{17,1},{2,18},{18,2},{3,19},{19,3},{4,20},{20... | collective-permute-start | bytes 393224 | tf_op jit(solution)/shard_map/ppermute | solution.py:20
  23.8 10.0 %collective-permute-start.9 = (bf16[1,64,1024]{2,1,0:T(8,128)(2,1)S(1)}, bf16[1,64,1024]{2,1,0:T(8,128)(2,1)S(1)}, u32[]{:S(2)}, u32[]{:S(2)}) collective-permute-start(bf16[1,64,1024]{2,1,0:T(8,128)(2,1)S(1)} %collective-permute-done.5.refs_1_.refs_2_), channel_id=1, source_target_pairs={{0,16},{16,0},{1,17},{17,1},{2,18},{18,2},{3,19},{19,3},{4,20},{20... | collective-permute-start | bytes 393224 | tf_op jit(solution)/shard_map/ppermute | solution.py:20
  24.3 3.4 %copy-start.1 = (bf16[1,4096,1024]{2,1,0:T(8,128)(2,1)S(1)}, bf16[1,4096,1024]{2,1,0:T(8,128)(2,1)}, u32[]{:S(2)}) copy-start(bf16[1,4096,1024]{2,1,0:T(8,128)(2,1)} %param.10) | copy-start | bytes 25165828
  27.7 6.2 %copy-start.13 = (s32[4,4]{1,0:T(4,128)S(1)}, s32[4,4]{1,0:T(4,128)}, u32[]{:S(2)}) copy-start(s32[4,4]{1,0:T(4,128)} %pattern_ref.3) | copy-start | bytes 196
  27.7 6.2 %copy-start.15 = (s32[16]{0:T(128)S(1)}, s32[16]{0:T(128)}, u32[]{:S(2)}) copy-start(s32[16]{0:T(128)} %slot_ref.3) | copy-start | bytes 196
  33.9 1.3 %copy-start.6 = (bf16[256,1024]{1,0:T(8,128)(2,1)S(1)}, bf16[256,1024]{1,0:T(8,128)(2,1)}, u32[]{:S(2)}) copy-start(bf16[256,1024]{1,0:T(8,128)(2,1)} %get-tuple-element.47.refs_0_) | copy-start | bytes 1572868
  35.1 5.7 %copy-start.4 = (bf16[1024,256]{1,0:T(8,128)(2,1)}, bf16[1024,256]{1,0:T(8,128)(2,1)S(1)}, u32[]{:S(2)}) copy-start(bf16[1024,256]{1,0:T(8,128)(2,1)S(1)} %get-tuple-element.43.refs_2_) | copy-start | bytes 1572868
  35.1 2.4 %collective-permute-start.13 = (bf16[1024,256]{1,0:T(8,128)(2,1)S(1)}, bf16[1024,256]{1,0:T(8,128)(2,1)S(1)}, u32[]{:S(2)}, u32[]{:S(2)}) collective-permute-start(bf16[1024,256]{1,0:T(8,128)(2,1)S(1)} %get-tuple-element.44), channel_id=1, source_target_pairs={{0,1},{1,0},{2,3},{3,2},{4,5},{5,4},{6,7},{7,6},{8,9},{9,8},{10,11... | collective-permute-start | bytes 1572872 | tf_op jit(solution)/shard_map/ppermute | solution.py:20
  35.2 16.6 %collective-permute-start.15 = (bf16[256,1024]{1,0:T(8,128)(2,1)S(1)}, bf16[256,1024]{1,0:T(8,128)(2,1)S(1)}, u32[]{:S(2)}, u32[]{:S(2)}) collective-permute-start(bf16[256,1024]{1,0:T(8,128)(2,1)S(1)} %after.15), channel_id=1, source_target_pairs={{0,4},{4,8},{8,12},{12,0},{1,5},{5,9},{9,13},{13,1},{2,6},{6,10},{... | collective-permute-start | bytes 1572872 | tf_op jit(solution)/shard_map/ppermute | solution.py:20
  37.5 3.3 %copy-start.5 = (bf16[1024,256]{1,0:T(8,128)(2,1)}, bf16[1024,256]{1,0:T(8,128)(2,1)S(1)}, u32[]{:S(2)}) copy-start(bf16[1024,256]{1,0:T(8,128)(2,1)S(1)} %collective-permute-done.13.refs_3_) | copy-start | bytes 1572868
  37.5 3.3 %copy-start.7 = (bf16[128,1024]{1,0:T(8,128)(2,1)S(1)}, bf16[128,1024]{1,0:T(8,128)(2,1)}, u32[]{:S(2)}) copy-start(bf16[128,1024]{1,0:T(8,128)(2,1)} %get-tuple-element.51.refs_0_) | copy-start | bytes 786436
  41.6 30.8 %collective-permute-start.17 = (bf16[256,1024]{1,0:T(8,128)(2,1)}, bf16[256,1024]{1,0:T(8,128)(2,1)}, u32[]{:S(2)}, u32[]{:S(2)}) collective-permute-start(bf16[256,1024]{1,0:T(8,128)(2,1)} %stack.1.refs_7_), channel_id=1, source_target_pairs={{0,4},{4,0},{8,12},{12,8},{1,5},{5,1},{9,13},{13,9},{2,6},{6,2},{1... | collective-permute-start | bytes 1572872 | tf_op jit(solution)/shard_map/ppermute | solution.py:24
  51.8 25.4 %collective-permute-start.20 = (bf16[256,1024]{1,0:T(8,128)(2,1)}, bf16[256,1024]{1,0:T(8,128)(2,1)S(1)}, u32[]{:S(2)}, u32[]{:S(2)}) collective-permute-start(bf16[256,1024]{1,0:T(8,128)(2,1)} %after.18), channel_id=1, source_target_pairs={{0,8},{4,12},{8,0},{12,4},{1,9},{5,13},{9,1},{13,5},{2,10},{6,14},... | collective-permute-start | bytes 1572872 | tf_op jit(solution)/shard_map/ppermute | solution.py:20
  51.8 28.3 %collective-permute-start.14 = (bf16[2048,256]{1,0:T(8,128)(2,1)}, bf16[2048,256]{1,0:T(8,128)(2,1)}, u32[]{:S(2)}, u32[]{:S(2)}) collective-permute-start(bf16[2048,256]{1,0:T(8,128)(2,1)} %fetched_weights.1.refs_4_.refs_2_), channel_id=1, source_target_pairs={{0,2},{2,0},{1,3},{3,1},{4,6},{6,4},{5,7},{7,5},{8,10},{10,8},{9,1... | collective-permute-start | bytes 3145736 | tf_op jit(solution)/shard_map/ppermute | solution.py:20
  61.6 6.3 %copy-start.17 = (s32[8,128]{1,0:T(8,128)S(1)}, s32[8,128]{1,0:T(8,128)}, u32[]{:S(2)}) copy-start(s32[8,128]{1,0:T(8,128)} %get-tuple-element.48) | copy-start | bytes 12292
  61.6 7.4 %copy-start.16 = (bf16[128,1024]{1,0:T(8,128)(2,1)S(1)}, bf16[128,1024]{1,0:T(8,128)(2,1)}, u32[]{:S(2)}) copy-start(bf16[128,1024]{1,0:T(8,128)(2,1)} %get-tuple-element.49) | copy-start | bytes 786436
  61.6 6.2 %collective-permute-start.16 = (s32[8,128]{1,0:T(8,128)}, s32[8,128]{1,0:T(8,128)S(1)}, u32[]{:S(2)}, u32[]{:S(2)}) collective-permute-start(s32[8,128]{1,0:T(8,128)} %get-tuple-element.48), channel_id=1, source_target_pairs={{0,16},{16,0},{1,17},{17,1},{2,18},{18,2},{3,19},{19,3},{4,20},{20... | collective-permute-start | bytes 12296 | tf_op jit(solution)/shard_map/ppermute | solution.py:20
  63.2 9.3 %copy-start = (f32[2048,256]{1,0:T(8,128)S(1)}, f32[2048,256]{1,0:T(8,128)}, u32[]{:S(2)}) copy-start(f32[2048,256]{1,0:T(8,128)} %partial_weights.1.rest_0_.refs_1_.refs_0_.refs_2_) | copy-start | bytes 6291460
  67.8 9.4 %copy-start.12 = (bf16[64,1024]{1,0:T(8,128)(2,1)S(1)}, bf16[64,1024]{1,0:T(8,128)(2,1)}, u32[]{:S(2)}) copy-start(bf16[64,1024]{1,0:T(8,128)(2,1)} %get-tuple-element.60.refs_0_) | copy-start | bytes 393220
  69.0 8.2 %copy-start.11 = (bf16[64,1024]{1,0:T(8,128)(2,1)S(1)}, bf16[64,1024]{1,0:T(8,128)(2,1)}, u32[]{:S(2)}) copy-start(bf16[64,1024]{1,0:T(8,128)(2,1)} %get-tuple-element.61.refs_0_) | copy-start | bytes 393220
  72.5 1.2 %copy-start.2 = (bf16[256,2048]{1,0:T(8,128)(2,1)S(1)}, bf16[256,2048]{1,0:T(8,128)(2,1)}, u32[]{:S(2)}) copy-start(bf16[256,2048]{1,0:T(8,128)(2,1)} %own_rows.1.refs_2_) | copy-start | bytes 3145732
  73.7 3.5 %copy-start.10 = (bf16[64,1024]{1,0:T(8,128)(2,1)S(1)}, bf16[64,1024]{1,0:T(8,128)(2,1)}, u32[]{:S(2)}) copy-start(bf16[64,1024]{1,0:T(8,128)(2,1)} %get-tuple-element.62.refs_0_) | copy-start | bytes 393220
  73.7 4.4 %collective-permute-start.18 = (s32[8,128]{1,0:T(8,128)S(1)}, s32[8,128]{1,0:T(8,128)S(1)}, u32[]{:S(2)}, u32[]{:S(2)}) collective-permute-start(s32[8,128]{1,0:T(8,128)S(1)} %after.16), channel_id=1, source_target_pairs={{0,1},{1,0},{2,3},{3,2},{4,5},{5,4},{6,7},{7,6},{8,9},{9,8},{10,11... | collective-permute-start | bytes 12296 | tf_op jit(solution)/shard_map/ppermute | solution.py:20
  73.7 4.9 %collective-permute-start.22 = (bf16[256,1024]{1,0:T(8,128)(2,1)}, bf16[256,1024]{1,0:T(8,128)(2,1)S(1)}, u32[]{:S(2)}, u32[]{:S(2)}) collective-permute-start(bf16[256,1024]{1,0:T(8,128)(2,1)} %stack.1.refs_7_), channel_id=1, source_target_pairs={{0,1},{1,0},{2,3},{3,2},{4,5},{5,4},{6,7},{7,6},{8,9},{9,8},{10,11... | collective-permute-start | bytes 1572872 | tf_op jit(solution)/shard_map/ppermute | solution.py:20
  74.2 6.2 %collective-permute-start.23 = (bf16[256,1024]{1,0:T(8,128)(2,1)}, bf16[256,1024]{1,0:T(8,128)(2,1)S(1)}, u32[]{:S(2)}, u32[]{:S(2)}) collective-permute-start(bf16[256,1024]{1,0:T(8,128)(2,1)} %collective-permute-done.17.refs_4_.refs_9_), channel_id=1, source_target_pairs={{0,1},{1,0},{2,3},{3,2},{4,5},{5,4},{6,7},{7,6},{8,9},{9,8},{10,11... | collective-permute-start | bytes 1572872 | tf_op jit(solution)/shard_map/ppermute | solution.py:20
  77.2 0.9 copy-start.9
  77.2 6.4 %copy-start.3 = (bf16[256,2048]{1,0:T(8,128)(2,1)S(1)}, bf16[256,2048]{1,0:T(8,128)(2,1)}, u32[]{:S(2)}) copy-start(bf16[256,2048]{1,0:T(8,128)(2,1)} %own_rows.1.refs_2_) | copy-start | bytes 3145732
  77.2 6.4 %copy-start.14 = (s32[4,4]{1,0:T(4,128)S(1)}, s32[4,4]{1,0:T(4,128)}, u32[]{:S(2)}) copy-start(s32[4,4]{1,0:T(4,128)} %get-tuple-element.45.table_ref) | copy-start | bytes 196
  78.1 2.8 %collective-permute-start.21 = (bf16[256,1024]{1,0:T(8,128)(2,1)S(1)}, bf16[256,1024]{1,0:T(8,128)(2,1)S(1)}, u32[]{:S(2)}, u32[]{:S(2)}) collective-permute-start(bf16[256,1024]{1,0:T(8,128)(2,1)S(1)} %after.19.refs_5_), channel_id=1, source_target_pairs={{0,1},{1,0},{2,3},{3,2},{4,5},{5,4},{6,7},{7,6},{8,9},{9,8},{10,11... | collective-permute-start | bytes 1572872 | tf_op jit(solution)/shard_map/ppermute | solution.py:20
  78.1 5.5 %collective-permute-start.19 = (bf16[256,1024]{1,0:T(8,128)(2,1)S(1)}, bf16[256,1024]{1,0:T(8,128)(2,1)S(1)}, u32[]{:S(2)}, u32[]{:S(2)}) collective-permute-start(bf16[256,1024]{1,0:T(8,128)(2,1)S(1)} %after.17.refs_3_), channel_id=1, source_target_pairs={{0,1},{1,0},{2,3},{3,2},{4,5},{5,4},{6,7},{7,6},{8,9},{9,8},{10,11... | collective-permute-start | bytes 1572872 | tf_op jit(solution)/shard_map/ppermute | solution.py:20
  78.6 11.5 %collective-permute-start.31 = (bf16[64,1024]{1,0:T(8,128)(2,1)S(1)}, bf16[64,1024]{1,0:T(8,128)(2,1)S(1)}, u32[]{:S(2)}, u32[]{:S(2)}) collective-permute-start(bf16[64,1024]{1,0:T(8,128)(2,1)S(1)} %after.26), channel_id=1, source_target_pairs={{0,12},{4,0},{8,4},{12,8},{1,13},{5,1},{9,5},{13,9},{2,14},{6,2},{... | collective-permute-start | bytes 393224 | tf_op jit(solution)/shard_map/ppermute | solution.py:20
  80.1 10.0 %collective-permute-start.29 = (bf16[64,1024]{1,0:T(8,128)(2,1)S(1)}, bf16[64,1024]{1,0:T(8,128)(2,1)S(1)}, u32[]{:S(2)}, u32[]{:S(2)}) collective-permute-start(bf16[64,1024]{1,0:T(8,128)(2,1)S(1)} %after.24), channel_id=1, source_target_pairs={{0,12},{4,0},{8,4},{12,8},{1,13},{5,1},{9,5},{13,9},{2,14},{6,2},{... | collective-permute-start | bytes 393224 | tf_op jit(solution)/shard_map/ppermute | solution.py:20
  80.4 10.2 %collective-permute-start.27 = (bf16[64,1024]{1,0:T(8,128)(2,1)S(1)}, bf16[64,1024]{1,0:T(8,128)(2,1)S(1)}, u32[]{:S(2)}, u32[]{:S(2)}) collective-permute-start(bf16[64,1024]{1,0:T(8,128)(2,1)S(1)} %after.22), channel_id=1, source_target_pairs={{0,12},{4,0},{8,4},{12,8},{1,13},{5,1},{9,5},{13,9},{2,14},{6,2},{... | collective-permute-start | bytes 393224 | tf_op jit(solution)/shard_map/ppermute | solution.py:20
  81.0 11.6 %collective-permute-start.25 = (bf16[64,1024]{1,0:T(8,128)(2,1)S(1)}, bf16[64,1024]{1,0:T(8,128)(2,1)S(1)}, u32[]{:S(2)}, u32[]{:S(2)}) collective-permute-start(bf16[64,1024]{1,0:T(8,128)(2,1)S(1)} %after.20), channel_id=1, source_target_pairs={{0,12},{4,0},{8,4},{12,8},{1,13},{5,1},{9,5},{13,9},{2,14},{6,2},{... | collective-permute-start | bytes 393224 | tf_op jit(solution)/shard_map/ppermute | solution.py:20
  88.5 10.4 %collective-permute-start.24 = (bf16[1024,128]{1,0:T(8,128)(2,1)S(1)}, bf16[1024,128]{1,0:T(8,128)(2,1)S(1)}, u32[]{:S(2)}, u32[]{:S(2)}) collective-permute-start(bf16[1024,128]{1,0:T(8,128)(2,1)S(1)} %get-tuple-element.57.refs_1_), channel_id=1, source_target_pairs={{0,2},{2,0},{1,3},{3,1},{4,6},{6,4},{5,7},{7,5},{8,10},{10,8},{9,1... | collective-permute-start | bytes 786440 | tf_op jit(solution)/shard_map/ppermute | solution.py:20
  90.1 2.4 %collective-permute-start.32 = (bf16[64,1024]{1,0:T(8,128)(2,1)S(1)}, bf16[64,1024]{1,0:T(8,128)(2,1)S(1)}, u32[]{:S(2)}, u32[]{:S(2)}) collective-permute-start(bf16[64,1024]{1,0:T(8,128)(2,1)S(1)} %after.27.refs_6_), channel_id=1, source_target_pairs={{0,1},{1,0},{2,3},{3,2},{4,5},{5,4},{6,7},{7,6},{8,9},{9,8},{10,11... | collective-permute-start | bytes 393224 | tf_op jit(solution)/shard_map/ppermute | solution.py:20
  90.1 2.4 %collective-permute-start.30 = (bf16[64,1024]{1,0:T(8,128)(2,1)S(1)}, bf16[64,1024]{1,0:T(8,128)(2,1)S(1)}, u32[]{:S(2)}, u32[]{:S(2)}) collective-permute-start(bf16[64,1024]{1,0:T(8,128)(2,1)S(1)} %after.25.refs_4_), channel_id=1, source_target_pairs={{0,1},{1,0},{2,3},{3,2},{4,5},{5,4},{6,7},{7,6},{8,9},{9,8},{10,11... | collective-permute-start | bytes 393224 | tf_op jit(solution)/shard_map/ppermute | solution.py:20
  90.6 1.9 %collective-permute-start.28 = (bf16[64,1024]{1,0:T(8,128)(2,1)S(1)}, bf16[64,1024]{1,0:T(8,128)(2,1)S(1)}, u32[]{:S(2)}, u32[]{:S(2)}) collective-permute-start(bf16[64,1024]{1,0:T(8,128)(2,1)S(1)} %after.23.refs_2_), channel_id=1, source_target_pairs={{0,1},{1,0},{2,3},{3,2},{4,5},{5,4},{6,7},{7,6},{8,9},{9,8},{10,11... | collective-permute-start | bytes 393224 | tf_op jit(solution)/shard_map/ppermute | solution.py:20
  92.5 1.3 %collective-permute-start.26 = (bf16[64,1024]{1,0:T(8,128)(2,1)S(1)}, bf16[64,1024]{1,0:T(8,128)(2,1)S(1)}, u32[]{:S(2)}, u32[]{:S(2)}) collective-permute-start(bf16[64,1024]{1,0:T(8,128)(2,1)S(1)} %after.21.refs_0_), channel_id=1, source_target_pairs={{0,1},{1,0},{2,3},{3,2},{4,5},{5,4},{6,7},{7,6},{8,9},{9,8},{10,11... | collective-permute-start | bytes 393224 | tf_op jit(solution)/shard_map/ppermute | solution.py:20
  94.6 4.3 %collective-permute-start.33 = (bf16[256,128]{1,0:T(8,128)(2,1)S(1)}, bf16[256,128]{1,0:T(8,128)(2,1)S(1)}, u32[]{:S(2)}, u32[]{:S(2)}) collective-permute-start(bf16[256,128]{1,0:T(8,128)(2,1)S(1)} %get-tuple-element.65), channel_id=1, source_target_pairs={{0,2},{2,0},{1,3},{3,1},{4,6},{6,4},{5,7},{7,5},{8,10},{10,8},{9,1... | collective-permute-start | bytes 196616 | tf_op jit(solution)/shard_map/ppermute | solution.py:20

commit v10 on v9

--- a/solution.py
+++ b/solution.py
@@ -12,6 +12,7 @@
 ANY = pl.BlockSpec(memory_space=pl.ANY)
 SMEM = pl.BlockSpec(memory_space=pltpu.SMEM)
 PARAMS = pltpu.CompilerParams(vmem_limit_bytes=24 * 2**20)
+MIDDLE = pltpu.CompilerParams(vmem_limit_bytes=48 * 2**20)
 FIRST = pltpu.CompilerParams(vmem_limit_bytes=60 * 2**20)
 LANES = 128
 
@@ -289,7 +290,7 @@
         out_shape=[jax.ShapeDtypeStruct((depth, width), BF16)] * n,
         scratch_shapes=[pltpu.SemaphoreType.DMA((n * cuts,))],
         cost_estimate=cost(0, 2 * n * depth * width),
-        compiler_params=PARAMS,
+        compiler_params=MIDDLE,
         name="fetch",
     )(jnp.reshape(block, (1,)).astype(I32), *matrices, *others)
 
@@ -564,20 +565,19 @@
     part = 64 if bulk % 64 == 0 else bulk
     final = [(last_hops, at, part) for at in range(0, bulk, part)]
     *packed, goal = pack_rows(train, ids, columns, bulk, extra, middle + final)
-    before_join, firsts, seconds = [], [], []
+    firsts, seconds = [], []
+    parts = [pieces] + [[shift(x, "groups", n_group, d) for x in pieces] for d in range(1, n_group)]
+    first_cut = packed[0]
     if extra:
-        far = swap(after(packed[-2], *pieces[1:]), "shard", n_shard, 2)
-        before_join = [far]
+        far = swap(after(packed[-2], *pieces[1:], *[x[0] for x in parts[1:]]), "shard", n_shard, 2)
+        first_cut = after(first_cut, far)
     depth = n_rep * columns
     targets = [(feat + d) % n_feat for d in range(1, n_feat)]
     near_chip = fetch(matrices, targets[0], depth, *pieces[1:])
 
-    parts = [pieces] + [[shift(x, "groups", n_group, d) for x in pieces] for d in range(1, n_group)]
-    chosen = join_queries(
-        parts, block_slot, pattern, query_store.shape[0], n_feat, n_rep, *before_join, *near_chip
-    )
+    chosen = join_queries(parts, block_slot, pattern, query_store.shape[0], n_feat, n_rep, *near_chip)
     queries = [chosen[0]] + [shift(chosen[d], "rep", n_rep, d) for d in range(1, n_rep)]
-    here = [shift(after(packed[0], *before_join), "shard", n_shard, 1)]
+    here = [shift(first_cut, "shard", n_shard, 1)]
 
     sends = [fetched_weights(near_chip, queries, BF16)]
     sends += [partial_weights(matrices, queries, f, depth, BF16) for f in targets[1:]]
@@ -605,7 +605,7 @@
             return [[jnp.zeros((2 * extra, columns), BF16)] * n_rep] * 2
 
         seconds = lax.cond(flag[0, 0] > 0, second_round, no_round, packed[-1])
-        pair = stack([packed[-3], far], *sends)
+        pair = stack([packed[-3], far], here[0], *sends)
         near = swap(pair, "shard", n_shard, 1)
         firsts = [with_rep(pair), with_rep(near)]
         marks += [seconds[0][0], near]

time: 101 us -> 102 us (level)
  Pallas kernels: 37.1 us -> 40 us
  waiting for transfers between devices: 22.8 us -> 20.3 us
  starting transfers between devices: 30.4 us -> 31.7 us
  local copies, waits for them, and re-layouts: 9.45 us -> 8.28 us
    ppermute x28, waiting for transfers between devices: 22.8 us -> 19.2 us  [shift(): return lax.ppermute(x, axis, [(i, (i + by) % size) for i in range(size)])]
    pallas_call x1, Pallas kernels: 2.52 us -> 5.57 us  [fetch(): pl.pallas_call(kernel, in_specs=[SMEM] + [ANY] * (n + len(others)), out_s...]
    ppermute x28, starting transfers between devices: 26.2 us -> 28.8 us  [shift(): return lax.ppermute(x, axis, [(i, (i + by) % size) for i in range(size)])]
    ppermute x2, starting transfers between devices: 4.21 us -> 2.88 us  [swap(): return lax.ppermute(x, axis, [(i, i ^ bit) for i in range(size)])]
    unnamed x36 -> x38, local copies, waits for them, and re-layouts: 5.51 us -> 4.32 us
    ppermute x2, waiting for transfers between devices: 0.01 us -> 1.07 us  [swap(): return lax.ppermute(x, axis, [(i, i ^ bit) for i in range(size)])]
  transfers between devices with their start and end apart: 30 -> 30, of which waited for: 8 -> 9; matrix products, arithmetic and copies ran while one was open for 4% -> 4% of each run, Pallas kernels for 34% -> 37%
where the time goes in v10:
time: 102 us; the launch traced here: 101 us
  Pallas kernels  40 us (39%)
  starting transfers between devices  31.7 us (31%)
  waiting for transfers between devices  20.3 us (20%)
  local copies, waits for them, and re-layouts  8.28 us (8%)
    ppermute x28, starting transfers between devices, shift(): return lax.ppermute(x, axis, [(i, (i + by) % size) for i in range(size)])  28.8 us
    ppermute x28, waiting for transfers between devices, shift(): return lax.ppermute(x, axis, [(i, (i + by) % size) for i in range(size)])  19.2 us
    pallas_call x1, Pallas kernels, partial_weights(): pl.pallas_call(kernel, grid_spec=pltpu.PrefetchScalarGridSpec(num_scalar_...  6.75 us
    pallas_call x1, Pallas kernels, pack_rows(): pl.pallas_call(kernel, grid=(1,), in_specs=[pl.BlockSpec((lines, LANES),...  6.24 us
    pallas_call x1, Pallas kernels, fetch(): pl.pallas_call(kernel, in_specs=[SMEM] + [ANY] * (n + len(others)), out_s...  5.57 us
    pallas_call x1, Pallas kernels, early_scores(): pl.pallas_call(kernel, in_specs=[SMEM] + [VMEM] * (2 + n_other + n_rep *...  4.87 us
    pallas_call x1, Pallas kernels, own_rows(): pl.pallas_call(kernel, in_specs=[VMEM] * 2 + [ANY] * len(others), out_spe...  4.63 us
    unnamed x38, local copies, waits for them, and re-layouts  4.32 us
  transfers between devices with their start and end apart: 30, of which 9 were waited for; matrix products, arithmetic and copies ran while one was open for 4% of the time, Pallas kernels for 37%

profile of v10, /device:TPU:0, one launch (start us, length us, event | category | flops | bytes accessed | tf_op | source)
XLA Modules:
  0.0 101.2 jit_solution(11040199504653721930)
XLA Ops:
  0.5 2.7 %pick_queries.1 = (bf16[1,64,1024]{2,1,0:T(8,128)(2,1)}, bf16[1,64,1024]{2,1,0:T(8,128)(2,1)}, bf16[1,64,1024]{2,1,0:T(8,128)(2,1)}, bf16[1,64,1024]{2,1,0:T(8,128)(2,1)}) custom-call(s32[4,4]{1,0:T(4,128)} %pattern_ref.3, s32[16]{0:T(128)} %slot_ref.3, bf16[4,128,1024]{2,1,0:T(8,128)(2,1)} %in_ref.1), custom_call_target="tpu_custom_call" | custom-call | flops 1 | bytes 1 | tf_op jit(solution)/shard_map/pick_queries/pallas_call | solution.py:93
  3.1 2.6 %collective-permute-start.5 = (bf16[1,64,1024]{2,1,0:T(8,128)(2,1)}, bf16[1,64,1024]{2,1,0:T(8,128)(2,1)S(1)}, u32[]{:S(2)}, u32[]{:S(2)}) collective-permute-start(bf16[1,64,1024]{2,1,0:T(8,128)(2,1)} %get-tuple-element.37), channel_id=1, source_target_pairs={{0,4},{4,8},{8,12},{12,0},{1,5},{5,9},{9,13},{13,1},{2,6},{6,10},{... | collective-permute-start | bytes 393224 | tf_op jit(solution)/shard_map/ppermute | solution.py:21
  5.7 2.6 %collective-permute-start.6 = (bf16[1,64,1024]{2,1,0:T(8,128)(2,1)}, bf16[1,64,1024]{2,1,0:T(8,128)(2,1)S(1)}, u32[]{:S(2)}, u32[]{:S(2)}) collective-permute-start(bf16[1,64,1024]{2,1,0:T(8,128)(2,1)} %get-tuple-element.38), channel_id=1, source_target_pairs={{0,8},{4,12},{8,0},{12,4},{1,9},{5,13},{9,1},{13,5},{2,10},{6,14},... | collective-permute-start | bytes 393224 | tf_op jit(solution)/shard_map/ppermute | solution.py:21
  8.3 1.3 %collective-permute-start.7 = (bf16[1,64,1024]{2,1,0:T(8,128)(2,1)}, bf16[1,64,1024]{2,1,0:T(8,128)(2,1)S(1)}, u32[]{:S(2)}, u32[]{:S(2)}) collective-permute-start(bf16[1,64,1024]{2,1,0:T(8,128)(2,1)} %get-tuple-element.39), channel_id=1, source_target_pairs={{0,12},{4,0},{8,4},{12,8},{1,13},{5,1},{9,5},{13,9},{2,14},{6,2},{... | collective-permute-start | bytes 393224 | tf_op jit(solution)/shard_map/ppermute | solution.py:21
  9.7 1.5 %collective-permute-start.8 = (bf16[1,64,1024]{2,1,0:T(8,128)(2,1)}, bf16[1,64,1024]{2,1,0:T(8,128)(2,1)S(1)}, u32[]{:S(2)}, u32[]{:S(2)}) collective-permute-start(bf16[1,64,1024]{2,1,0:T(8,128)(2,1)} %get-tuple-element.36.refs_0_), channel_id=1, source_target_pairs={{0,16},{16,0},{1,17},{17,1},{2,18},{18,2},{3,19},{19,3},{4,20},{20... | collective-permute-start | bytes 393224 | tf_op jit(solution)/shard_map/ppermute | solution.py:21
  11.2 6.2 %pack_rows.1 = (bf16[256,1024]{1,0:T(8,128)(2,1)}, bf16[256,1024]{1,0:T(8,128)(2,1)}, bf16[64,1024]{1,0:T(8,128)(2,1)}, bf16[64,1024]{1,0:T(8,128)(2,1)}, bf16[6...) custom-call(s32[32,128]{1,0:T(8,128)} %bitcast.9, ...), custom_call_target="tpu_custom_call" | custom-call | flops 1 | bytes 1 | tf_op jit(solution)/shard_map/pack_rows/pallas_call | solution.py:221
  17.8 2.4 %collective-permute-start.14 = (bf16[128,1024]{1,0:T(8,128)(2,1)}, bf16[128,1024]{1,0:T(8,128)(2,1)S(1)}, u32[]{:S(2)}, u32[]{:S(2)}) collective-permute-start(bf16[128,1024]{1,0:T(8,128)(2,1)} %after.14), channel_id=1, source_target_pairs={{0,8},{4,12},{8,0},{12,4},{1,9},{5,13},{9,1},{13,5},{2,10},{6,14},... | collective-permute-start | bytes 786440 | tf_op jit(solution)/shard_map/ppermute | solution.py:25
  20.2 1.5 %collective-permute-start.10 = (bf16[1,64,1024]{2,1,0:T(8,128)(2,1)S(1)}, bf16[1,64,1024]{2,1,0:T(8,128)(2,1)S(1)}, u32[]{:S(2)}, u32[]{:S(2)}) collective-permute-start(bf16[1,64,1024]{2,1,0:T(8,128)(2,1)S(1)} %collective-permute-done.6.refs_3_.refs_2_), channel_id=1, source_target_pairs={{0,16},{16,0},{1,17},{17,1},{2,18},{18,2},{3,19},{19,3},{4,20},{20... | collective-permute-start | bytes 393224 | tf_op jit(solution)/shard_map/ppermute | solution.py:21
  21.8 0.5 collective-permute-start.11
  22.3 1.5 %collective-permute-start.9 = (bf16[1,64,1024]{2,1,0:T(8,128)(2,1)S(1)}, bf16[1,64,1024]{2,1,0:T(8,128)(2,1)S(1)}, u32[]{:S(2)}, u32[]{:S(2)}) collective-permute-start(bf16[1,64,1024]{2,1,0:T(8,128)(2,1)S(1)} %collective-permute-done.5.refs_2_.refs_1_), channel_id=1, source_target_pairs={{0,16},{16,0},{1,17},{17,1},{2,18},{18,2},{3,19},{19,3},{4,20},{20... | collective-permute-start | bytes 393224 | tf_op jit(solution)/shard_map/ppermute | solution.py:21
  23.8 5.6 %fetch.1 = (bf16[2048,1024]{1,0:T(8,128)(2,1)S(1)}, bf16[2048,1024]{1,0:T(8,128)(2,1)}) custom-call(s32[1]{0:T(128)} %bitcast.3.block_ref, bf16[4096,1024]{1,0:T(8,128)(2,1)} %bitcast.7, bf16[4096,1024]{1,0:T(8,128)(2,1)} %collective-permute-done.4.refs_1_, bf16[1,64,1024]{2,1,0:T(8,128)(2,1)S(1)} %collective-permute-done.5.refs_2_.refs_1_, ...), custom_call_target="tpu_custom_call" | custom-call | flops 1 | bytes 1 | tf_op jit(solution)/shard_map/fetch/pallas_call | solution.py:286
  29.4 1.6 %collective-permute-done.9.refs_5_ = bf16[1,64,1024]{2,1,0:T(8,128)(2,1)S(1)} collective-permute-done((bf16[1,64,1024]{2,1,0:T(8,128)(2,1)S(1)}, bf16[1,64,1024]{2,1,0:T(8,128)(2,1)S(1)}, u32[]{:S(2)}, u32[]{:S(2)}) %collective-permute-start.9) | collective-permute-done | bytes 131104 | tf_op jit(solution)/shard_map/ppermute | solution.py:21
  31.0 2.2 %copy-done.1 = bf16[2048,1024]{1,0:T(8,128)(2,1)S(1)} copy-done((bf16[2048,1024]{1,0:T(8,128)(2,1)S(1)}, bf16[2048,1024]{1,0:T(8,128)(2,1)}, u32[]{:S(2)}) %copy-start.1) | copy-done | bytes 4194328
  33.2 1.2 %join_queries.1 = (bf16[1024,256]{1,0:T(8,128)(2,1)S(1)}, bf16[1024,256]{1,0:T(8,128)(2,1)S(1)}) custom-call(s32[4,4]{1,0:T(4,128)S(1)} %copy-done.14, s32[16]{0:T(128)S(1)} %copy-done.16, bf16[1,64,1024]{2,1,0:T(8,128)(2,1)S(1)} %copy-done.9, bf16[1,64,1024]{2,1,0:T(8,128)(2,1)S(1)} %collective-permute-done.5.refs_2_.refs_1_, ...), custom_call_target="tpu_custom_call" | custom-call | flops 1 | bytes 1 | tf_op jit(solution)/shard_map/join_queries/pallas_call | solution.py:138
  34.6 2.3 %collective-permute-start.15 = (bf16[256,1024]{1,0:T(8,128)(2,1)S(1)}, bf16[256,1024]{1,0:T(8,128)(2,1)S(1)}, u32[]{:S(2)}, u32[]{:S(2)}) collective-permute-start(bf16[256,1024]{1,0:T(8,128)(2,1)S(1)} %after.15), channel_id=1, source_target_pairs={{0,4},{4,8},{8,12},{12,0},{1,5},{5,9},{9,13},{13,1},{2,6},{6,10},{... | collective-permute-start | bytes 1572872 | tf_op jit(solution)/shard_map/ppermute | solution.py:21
  36.9 3.3 %fetched_weights.1.refs_4_.refs_3_.refs_2_ = bf16[2048,256]{1,0:T(8,128)(2,1)} custom-call(bf16[2048,1024]{1,0:T(8,128)(2,1)S(1)} %get-tuple-element.40.refs_8_.refs_0_, bf16[2048,1024]{1,0:T(8,128)(2,1)S(1)} %copy-done.2, bf16[1024,256]{1,0:T(8,128)(2,1)S(1)} %get-tuple-element.42.refs_2_, bf16[1024,256]{1,0:T(8,128)(2,1)S(1)} %collective-permute-done.12.refs_3_), custom_call_target="tpu_custom_call" | custom-call | flops 1 | bytes 1 | tf_op jit(solution)/shard_map/fetched_weights/pallas_call | solution.py:311
  40.2 10.5 %collective-permute-done.15.refs_2_.refs_0_.refs_1_ = bf16[256,1024]{1,0:T(8,128)(2,1)S(1)} collective-permute-done((bf16[256,1024]{1,0:T(8,128)(2,1)S(1)}, bf16[256,1024]{1,0:T(8,128)(2,1)S(1)}, u32[]{:S(2)}, u32[]{:S(2)}) %collective-permute-start.15) | collective-permute-done | bytes 524320 | tf_op jit(solution)/shard_map/ppermute | solution.py:21
  50.7 0.8 stack.1.refs_7_
  52.0 1.6 %collective-permute-start.20 = (bf16[256,1024]{1,0:T(8,128)(2,1)}, bf16[256,1024]{1,0:T(8,128)(2,1)S(1)}, u32[]{:S(2)}, u32[]{:S(2)}) collective-permute-start(bf16[256,1024]{1,0:T(8,128)(2,1)} %after.18), channel_id=1, source_target_pairs={{0,8},{4,12},{8,0},{12,4},{1,9},{5,13},{9,1},{13,5},{2,10},{6,14},... | collective-permute-start | bytes 1572872 | tf_op jit(solution)/shard_map/ppermute | solution.py:21
  53.6 1.5 %collective-permute-start.13 = (bf16[2048,256]{1,0:T(8,128)(2,1)}, bf16[2048,256]{1,0:T(8,128)(2,1)}, u32[]{:S(2)}, u32[]{:S(2)}) collective-permute-start(bf16[2048,256]{1,0:T(8,128)(2,1)} %fetched_weights.1.refs_4_.refs_3_.refs_2_), channel_id=1, source_target_pairs={{0,2},{2,0},{1,3},{3,1},{4,6},{6,4},{5,7},{7,5},{8,10},{10,8},{9,1... | collective-permute-start | bytes 3145736 | tf_op jit(solution)/shard_map/ppermute | solution.py:21
  55.1 6.7 %partial_weights.1.rest_0_.refs_1_.refs_0_.refs_2_ = f32[2048,256]{1,0:T(8,128)} custom-call(s32[1]{0:T(128)} %bitcast.1.block_ref, bf16[4096,1024]{1,0:T(8,128)(2,1)} %bitcast.8, bf16[4096,1024]{1,0:T(8,128)(2,1)} %collective-permute-done.4.refs_1_, bf16[1024,256]{1,0:T(8,128)(2,1)} %copy-done.5, bf16[1024,256]{1,0:T(8,128)(2,1)} %copy-done.6, ...), custom_call_target="tpu_custom_call" | custom-call | flops 1 | bytes 1 | tf_op jit(solution)/shard_map/partial_weights/pallas_call | solution.py:248
  61.8 1.5 %row_table.1 = (s32[4,4]{1,0:T(4,128)}, s32[8,128]{1,0:T(8,128)}) custom-call(s32[32,128]{1,0:T(8,128)} %bitcast.10, f32[2048,256]{1,0:T(8,128)} %partial_weights.1.rest_0_.refs_1_.refs_0_.refs_2_), custom_call_target="tpu_custom_call" | custom-call | flops 1 | bytes 1 | tf_op jit(solution)/shard_map/row_table/pallas_call | solution.py:352
  63.4 1.6 %collective-permute-start.16 = (s32[8,128]{1,0:T(8,128)}, s32[8,128]{1,0:T(8,128)S(1)}, u32[]{:S(2)}, u32[]{:S(2)}) collective-permute-start(s32[8,128]{1,0:T(8,128)} %get-tuple-element.48), channel_id=1, source_target_pairs={{0,16},{16,0},{1,17},{17,1},{2,18},{18,2},{3,19},{19,3},{4,20},{20... | collective-permute-start | bytes 12296 | tf_op jit(solution)/shard_map/ppermute | solution.py:21
  65.0 4.6 %own_rows.1.refs_2_ = bf16[256,2048]{1,0:T(8,128)(2,1)} custom-call(s32[8,128]{1,0:T(8,128)} %get-tuple-element.45.goal_ref, bf16[1024,2048]{1,0:T(8,128)(2,1)} %train_ref.3, f32[2048,256]{1,0:T(8,128)} %partial_weights.1.rest_0_.refs_1_.refs_0_.refs_2_), custom_call_target="tpu_custom_call" | custom-call | flops 1 | bytes 1 | tf_op jit(solution)/shard_map/own_rows/pallas_call | solution.py:164
  69.6 0.5 slice.3
  70.8 3.5 %conditional.1 = (bf16[256,1024]{1,0:T(8,128)(2,1)}, bf16[256,1024]{1,0:T(8,128)(2,1)}, bf16[256,1024]{1,0:T(8,128)(2,1)}, bf16[256,1024]{1,0:T(8,128)(2,1)}) conditional(s32[]{:T(128)} %bitcast.4, () %tuple.13, bf16[128,1024]{1,0:T(8,128)(2,1)S(1)} %copy-done.17), branch_computations={%region_0.1_spmd, %region_1.2_spmd} | conditional | bytes 8388800 | solution.py:607
  70.8 0.9 broadcast.3
  71.7 0.8 broadcast.3.clone
  72.5 0.9 broadcast.3.clone.1
  73.4 0.9 broadcast.3.clone.2
  74.2 1.1 %collective-permute-done.17.refs_4_.refs_9_ = bf16[256,1024]{1,0:T(8,128)(2,1)} collective-permute-done((bf16[256,1024]{1,0:T(8,128)(2,1)}, bf16[256,1024]{1,0:T(8,128)(2,1)}, u32[]{:S(2)}, u32[]{:S(2)}) %collective-permute-start.17) | collective-permute-done | bytes 524320 | tf_op jit(solution)/shard_map/ppermute | solution.py:25
  75.3 1.2 %copy-done.3 = bf16[256,2048]{1,0:T(8,128)(2,1)S(1)} copy-done((bf16[256,2048]{1,0:T(8,128)(2,1)S(1)}, bf16[256,2048]{1,0:T(8,128)(2,1)}, u32[]{:S(2)}) %copy-start.3) | copy-done | bytes 1048600
  76.5 0.5 collective-permute-start.22
  77.1 0.5 collective-permute-done.20.refs_0_.refs_1_
  77.7 0.8 copy-done.10
  78.5 0.5 collective-permute-start.19
  79.0 2.4 %collective-permute-start.31 = (bf16[64,1024]{1,0:T(8,128)(2,1)S(1)}, bf16[64,1024]{1,0:T(8,128)(2,1)S(1)}, u32[]{:S(2)}, u32[]{:S(2)}) collective-permute-start(bf16[64,1024]{1,0:T(8,128)(2,1)S(1)} %after.26), channel_id=1, source_target_pairs={{0,12},{4,0},{8,4},{12,8},{1,13},{5,1},{9,5},{13,9},{2,14},{6,2},{... | collective-permute-start | bytes 393224 | tf_op jit(solution)/shard_map/ppermute | solution.py:21
  81.4 0.7 collective-permute-start.27
  82.1 1.8 %collective-permute-start.25 = (bf16[64,1024]{1,0:T(8,128)(2,1)S(1)}, bf16[64,1024]{1,0:T(8,128)(2,1)S(1)}, u32[]{:S(2)}, u32[]{:S(2)}) collective-permute-start(bf16[64,1024]{1,0:T(8,128)(2,1)S(1)} %after.20), channel_id=1, source_target_pairs={{0,12},{4,0},{8,4},{12,8},{1,13},{5,1},{9,5},{13,9},{2,14},{6,2},{... | collective-permute-start | bytes 393224 | tf_op jit(solution)/shard_map/ppermute | solution.py:21
  84.0 4.9 %early_scores.1 = (bf16[2048,256]{1,0:T(8,128)(2,1)S(1)}, bf16[2048,256]{1,0:T(8,128)(2,1)S(1)}, f32[1024,128]{1,0:T(8,128)S(1)}, bf16[1024,128]{1,0:T(8,128)(2,1)S(1)}) custom-call(s32[4,4]{1,0:T(4,128)S(1)} %copy-done.15, f32[2048,256]{1,0:T(8,128)S(1)} %copy-done, bf16[2048,256]{1,0:T(8,128)(2,1)} %collective-permute-done.13.refs_1_, ...), custom_call_target="tpu_custom_call" | custom-call | flops 1 | bytes 1 | tf_op jit(solution)/shard_map/early_scores/pallas_call | solution.py:468
  88.9 1.6 %collective-permute-start.24 = (bf16[1024,128]{1,0:T(8,128)(2,1)S(1)}, bf16[1024,128]{1,0:T(8,128)(2,1)S(1)}, u32[]{:S(2)}, u32[]{:S(2)}) collective-permute-start(bf16[1024,128]{1,0:T(8,128)(2,1)S(1)} %get-tuple-element.57.refs_1_), channel_id=1, source_target_pairs={{0,2},{2,0},{1,3},{3,1},{4,6},{6,4},{5,7},{7,5},{8,10},{10,8},{9,1... | collective-permute-start | bytes 786440 | tf_op jit(solution)/shard_map/ppermute | solution.py:21
  90.5 0.5 collective-permute-start.30
  91.0 2.1 %collective-permute-done.25.refs_0_ = bf16[64,1024]{1,0:T(8,128)(2,1)S(1)} collective-permute-done((bf16[64,1024]{1,0:T(8,128)(2,1)S(1)}, bf16[64,1024]{1,0:T(8,128)(2,1)S(1)}, u32[]{:S(2)}, u32[]{:S(2)}) %collective-permute-start.25) | collective-permute-done | bytes 131104 | tf_op jit(solution)/shard_map/ppermute | solution.py:21
  93.1 1.3 %collective-permute-done.26.refs_1_ = bf16[64,1024]{1,0:T(8,128)(2,1)S(1)} collective-permute-done((bf16[64,1024]{1,0:T(8,128)(2,1)S(1)}, bf16[64,1024]{1,0:T(8,128)(2,1)S(1)}, u32[]{:S(2)}, u32[]{:S(2)}) %collective-permute-start.26) | collective-permute-done | bytes 131104 | tf_op jit(solution)/shard_map/ppermute | solution.py:21
  94.5 0.7 late_scores.1
  95.2 1.6 %collective-permute-start.33 = (bf16[256,128]{1,0:T(8,128)(2,1)S(1)}, bf16[256,128]{1,0:T(8,128)(2,1)S(1)}, u32[]{:S(2)}, u32[]{:S(2)}) collective-permute-start(bf16[256,128]{1,0:T(8,128)(2,1)S(1)} %get-tuple-element.65), channel_id=1, source_target_pairs={{0,2},{2,0},{1,3},{3,1},{4,6},{6,4},{5,7},{7,5},{8,10},{10,8},{9,1... | collective-permute-start | bytes 196616 | tf_op jit(solution)/shard_map/ppermute | solution.py:21
  96.8 2.8 %collective-permute-done.33.refs_3_ = bf16[256,128]{1,0:T(8,128)(2,1)S(1)} collective-permute-done((bf16[256,128]{1,0:T(8,128)(2,1)S(1)}, bf16[256,128]{1,0:T(8,128)(2,1)S(1)}, u32[]{:S(2)}, u32[]{:S(2)}) %collective-permute-start.33) | collective-permute-done | bytes 65568 | tf_op jit(solution)/shard_map/ppermute | solution.py:21
  99.5 1.7 %merge.1 = f32[128,1024]{1,0:T(8,128)} custom-call(s32[4,4]{1,0:T(4,128)S(1)} %copy-done.15, f32[1024,128]{1,0:T(8,128)S(1)} %get-tuple-element.56.refs_0_, bf16[1024,128]{1,0:T(8,128)(2,1)S(1)} %collective-permute-done.24.refs_1_, f32[256,128]{1,0:T(8,128)S(1)} %get-tuple-element.64.refs_2_, bf16[256,128]{1,0:T(8,128)(2,1)S(1)} %collective-permute-done.33.refs_3_), custom_call_target="tpu_custom_call" | custom-call | flops 1 | bytes 1 | tf_op jit(solution)/shard_map/merge/pallas_call | solution.py:530
  (84 shorter events, 1.7 us)
Async XLA Ops:
  0.0 23.8 %collective-permute-start.4 = (bf16[4096,1024]{1,0:T(8,128)(2,1)}, bf16[4096,1024]{1,0:T(8,128)(2,1)}, u32[]{:S(2)}, u32[]{:S(2)}) collective-permute-start(bf16[4096,1024]{1,0:T(8,128)(2,1)} %bitcast.6), channel_id=1, source_target_pairs={{0,1},{1,0},{2,3},{3,2},{4,5},{5,4},{6,7},{7,6},{8,9},{9,8},{10,11... | collective-permute-start | bytes 25165832 | tf_op jit(solution)/shard_map/ppermute | solution.py:21
  3.1 14.3 %collective-permute-start.5 = (bf16[1,64,1024]{2,1,0:T(8,128)(2,1)}, bf16[1,64,1024]{2,1,0:T(8,128)(2,1)S(1)}, u32[]{:S(2)}, u32[]{:S(2)}) collective-permute-start(bf16[1,64,1024]{2,1,0:T(8,128)(2,1)} %get-tuple-element.37), channel_id=1, source_target_pairs={{0,4},{4,8},{8,12},{12,0},{1,5},{5,9},{9,13},{13,1},{2,6},{6,10},{... | collective-permute-start | bytes 393224 | tf_op jit(solution)/shard_map/ppermute | solution.py:21
  5.7 12.1 %collective-permute-start.6 = (bf16[1,64,1024]{2,1,0:T(8,128)(2,1)}, bf16[1,64,1024]{2,1,0:T(8,128)(2,1)S(1)}, u32[]{:S(2)}, u32[]{:S(2)}) collective-permute-start(bf16[1,64,1024]{2,1,0:T(8,128)(2,1)} %get-tuple-element.38), channel_id=1, source_target_pairs={{0,8},{4,12},{8,0},{12,4},{1,9},{5,13},{9,1},{13,5},{2,10},{6,14},... | collective-permute-start | bytes 393224 | tf_op jit(solution)/shard_map/ppermute | solution.py:21
  8.3 9.5 %collective-permute-start.7 = (bf16[1,64,1024]{2,1,0:T(8,128)(2,1)}, bf16[1,64,1024]{2,1,0:T(8,128)(2,1)S(1)}, u32[]{:S(2)}, u32[]{:S(2)}) collective-permute-start(bf16[1,64,1024]{2,1,0:T(8,128)(2,1)} %get-tuple-element.39), channel_id=1, source_target_pairs={{0,12},{4,0},{8,4},{12,8},{1,13},{5,1},{9,5},{13,9},{2,14},{6,2},{... | collective-permute-start | bytes 393224 | tf_op jit(solution)/shard_map/ppermute | solution.py:21
  9.7 8.2 %collective-permute-start.8 = (bf16[1,64,1024]{2,1,0:T(8,128)(2,1)}, bf16[1,64,1024]{2,1,0:T(8,128)(2,1)S(1)}, u32[]{:S(2)}, u32[]{:S(2)}) collective-permute-start(bf16[1,64,1024]{2,1,0:T(8,128)(2,1)} %get-tuple-element.36.refs_0_), channel_id=1, source_target_pairs={{0,16},{16,0},{1,17},{17,1},{2,18},{18,2},{3,19},{19,3},{4,20},{20... | collective-permute-start | bytes 393224 | tf_op jit(solution)/shard_map/ppermute | solution.py:21
  17.8 16.7 %collective-permute-start.14 = (bf16[128,1024]{1,0:T(8,128)(2,1)}, bf16[128,1024]{1,0:T(8,128)(2,1)S(1)}, u32[]{:S(2)}, u32[]{:S(2)}) collective-permute-start(bf16[128,1024]{1,0:T(8,128)(2,1)} %after.14), channel_id=1, source_target_pairs={{0,8},{4,12},{8,0},{12,4},{1,9},{5,13},{9,1},{13,5},{2,10},{6,14},... | collective-permute-start | bytes 786440 | tf_op jit(solution)/shard_map/ppermute | solution.py:25
  20.2 9.1 %collective-permute-start.10 = (bf16[1,64,1024]{2,1,0:T(8,128)(2,1)S(1)}, bf16[1,64,1024]{2,1,0:T(8,128)(2,1)S(1)}, u32[]{:S(2)}, u32[]{:S(2)}) collective-permute-start(bf16[1,64,1024]{2,1,0:T(8,128)(2,1)S(1)} %collective-permute-done.6.refs_3_.refs_2_), channel_id=1, source_target_pairs={{0,16},{16,0},{1,17},{17,1},{2,18},{18,2},{3,19},{19,3},{4,20},{20... | collective-permute-start | bytes 393224 | tf_op jit(solution)/shard_map/ppermute | solution.py:21
  21.8 7.7 %collective-permute-start.11 = (bf16[1,64,1024]{2,1,0:T(8,128)(2,1)S(1)}, bf16[1,64,1024]{2,1,0:T(8,128)(2,1)S(1)}, u32[]{:S(2)}, u32[]{:S(2)}) collective-permute-start(bf16[1,64,1024]{2,1,0:T(8,128)(2,1)S(1)} %collective-permute-done.7.refs_4_.refs_3_), channel_id=1, source_target_pairs={{0,16},{16,0},{1,17},{17,1},{2,18},{18,2},{3,19},{19,3},{4,20},{20... | collective-permute-start | bytes 393224 | tf_op jit(solution)/shard_map/ppermute | solution.py:21
  22.3 8.8 %collective-permute-start.9 = (bf16[1,64,1024]{2,1,0:T(8,128)(2,1)S(1)}, bf16[1,64,1024]{2,1,0:T(8,128)(2,1)S(1)}, u32[]{:S(2)}, u32[]{:S(2)}) collective-permute-start(bf16[1,64,1024]{2,1,0:T(8,128)(2,1)S(1)} %collective-permute-done.5.refs_2_.refs_1_), channel_id=1, source_target_pairs={{0,16},{16,0},{1,17},{17,1},{2,18},{18,2},{3,19},{19,3},{4,20},{20... | collective-permute-start | bytes 393224 | tf_op jit(solution)/shard_map/ppermute | solution.py:21
  23.8 7.2 %copy-start.9 = (bf16[1,64,1024]{2,1,0:T(8,128)(2,1)S(1)}, bf16[1,64,1024]{2,1,0:T(8,128)(2,1)}, u32[]{:S(2)}) copy-start(bf16[1,64,1024]{2,1,0:T(8,128)(2,1)} %get-tuple-element.36.refs_0_) | copy-start | bytes 393220
  23.8 7.2 %copy-start.14 = (s32[4,4]{1,0:T(4,128)S(1)}, s32[4,4]{1,0:T(4,128)}, u32[]{:S(2)}) copy-start(s32[4,4]{1,0:T(4,128)} %pattern_ref.3) | copy-start | bytes 196
  23.8 7.2 %copy-start.16 = (s32[16]{0:T(128)S(1)}, s32[16]{0:T(128)}, u32[]{:S(2)}) copy-start(s32[16]{0:T(128)} %slot_ref.3) | copy-start | bytes 196
  31.0 2.2 %copy-start.1 = (bf16[2048,1024]{1,0:T(8,128)(2,1)S(1)}, bf16[2048,1024]{1,0:T(8,128)(2,1)}, u32[]{:S(2)}) copy-start(bf16[2048,1024]{1,0:T(8,128)(2,1)} %get-tuple-element.41.refs_9_.refs_1_) | copy-start | bytes 12582916
  33.2 1.3 %copy-start.7 = (bf16[256,1024]{1,0:T(8,128)(2,1)S(1)}, bf16[256,1024]{1,0:T(8,128)(2,1)}, u32[]{:S(2)}) copy-start(bf16[256,1024]{1,0:T(8,128)(2,1)} %get-tuple-element.46.refs_0_) | copy-start | bytes 1572868
  33.2 3.7 %copy-start.2 = (bf16[2048,1024]{1,0:T(8,128)(2,1)S(1)}, bf16[2048,1024]{1,0:T(8,128)(2,1)}, u32[]{:S(2)}) copy-start(bf16[2048,1024]{1,0:T(8,128)(2,1)} %get-tuple-element.41.refs_9_.refs_1_) | copy-start | bytes 12582916
  34.4 5.8 %copy-start.5 = (bf16[1024,256]{1,0:T(8,128)(2,1)}, bf16[1024,256]{1,0:T(8,128)(2,1)S(1)}, u32[]{:S(2)}) copy-start(bf16[1024,256]{1,0:T(8,128)(2,1)S(1)} %get-tuple-element.42.refs_2_) | copy-start | bytes 1572868
  34.5 2.5 %collective-permute-start.12 = (bf16[1024,256]{1,0:T(8,128)(2,1)S(1)}, bf16[1024,256]{1,0:T(8,128)(2,1)S(1)}, u32[]{:S(2)}, u32[]{:S(2)}) collective-permute-start(bf16[1024,256]{1,0:T(8,128)(2,1)S(1)} %get-tuple-element.43), channel_id=1, source_target_pairs={{0,1},{1,0},{2,3},{3,2},{4,5},{5,4},{6,7},{7,6},{8,9},{9,8},{10,11... | collective-permute-start | bytes 1572872 | tf_op jit(solution)/shard_map/ppermute | solution.py:21
  34.6 16.1 %collective-permute-start.15 = (bf16[256,1024]{1,0:T(8,128)(2,1)S(1)}, bf16[256,1024]{1,0:T(8,128)(2,1)S(1)}, u32[]{:S(2)}, u32[]{:S(2)}) collective-permute-start(bf16[256,1024]{1,0:T(8,128)(2,1)S(1)} %after.15), channel_id=1, source_target_pairs={{0,4},{4,8},{8,12},{12,0},{1,5},{5,9},{9,13},{13,1},{2,6},{6,10},{... | collective-permute-start | bytes 1572872 | tf_op jit(solution)/shard_map/ppermute | solution.py:21
  36.9 3.3 %copy-start.6 = (bf16[1024,256]{1,0:T(8,128)(2,1)}, bf16[1024,256]{1,0:T(8,128)(2,1)S(1)}, u32[]{:S(2)}) copy-start(bf16[1024,256]{1,0:T(8,128)(2,1)S(1)} %collective-permute-done.12.refs_3_) | copy-start | bytes 1572868
  36.9 13.8 %copy-start.8 = (bf16[128,1024]{1,0:T(8,128)(2,1)S(1)}, bf16[128,1024]{1,0:T(8,128)(2,1)}, u32[]{:S(2)}) copy-start(bf16[128,1024]{1,0:T(8,128)(2,1)} %get-tuple-element.51.refs_0_) | copy-start | bytes 786436
  51.5 23.8 %collective-permute-start.17 = (bf16[256,1024]{1,0:T(8,128)(2,1)}, bf16[256,1024]{1,0:T(8,128)(2,1)}, u32[]{:S(2)}, u32[]{:S(2)}) collective-permute-start(bf16[256,1024]{1,0:T(8,128)(2,1)} %stack.1.refs_7_), channel_id=1, source_target_pairs={{0,4},{4,0},{8,12},{12,8},{1,5},{5,1},{9,13},{13,9},{2,6},{6,2},{1... | collective-permute-start | bytes 1572872 | tf_op jit(solution)/shard_map/ppermute | solution.py:25
  52.0 25.6 %collective-permute-start.20 = (bf16[256,1024]{1,0:T(8,128)(2,1)}, bf16[256,1024]{1,0:T(8,128)(2,1)S(1)}, u32[]{:S(2)}, u32[]{:S(2)}) collective-permute-start(bf16[256,1024]{1,0:T(8,128)(2,1)} %after.18), channel_id=1, source_target_pairs={{0,8},{4,12},{8,0},{12,4},{1,9},{5,13},{9,1},{13,5},{2,10},{6,14},... | collective-permute-start | bytes 1572872 | tf_op jit(solution)/shard_map/ppermute | solution.py:21
  53.6 27.9 %collective-permute-start.13 = (bf16[2048,256]{1,0:T(8,128)(2,1)}, bf16[2048,256]{1,0:T(8,128)(2,1)}, u32[]{:S(2)}, u32[]{:S(2)}) collective-permute-start(bf16[2048,256]{1,0:T(8,128)(2,1)} %fetched_weights.1.refs_4_.refs_3_.refs_2_), channel_id=1, source_target_pairs={{0,2},{2,0},{1,3},{3,1},{4,6},{6,4},{5,7},{7,5},{8,10},{10,8},{9,1... | collective-permute-start | bytes 3145736 | tf_op jit(solution)/shard_map/ppermute | solution.py:21
  63.3 6.2 %copy-start.18 = (s32[8,128]{1,0:T(8,128)S(1)}, s32[8,128]{1,0:T(8,128)}, u32[]{:S(2)}) copy-start(s32[8,128]{1,0:T(8,128)} %get-tuple-element.48) | copy-start | bytes 12292
  63.4 7.4 %copy-start.17 = (bf16[128,1024]{1,0:T(8,128)(2,1)S(1)}, bf16[128,1024]{1,0:T(8,128)(2,1)}, u32[]{:S(2)}) copy-start(bf16[128,1024]{1,0:T(8,128)(2,1)} %get-tuple-element.49) | copy-start | bytes 786436
  63.4 6.2 %collective-permute-start.16 = (s32[8,128]{1,0:T(8,128)}, s32[8,128]{1,0:T(8,128)S(1)}, u32[]{:S(2)}, u32[]{:S(2)}) collective-permute-start(s32[8,128]{1,0:T(8,128)} %get-tuple-element.48), channel_id=1, source_target_pairs={{0,16},{16,0},{1,17},{17,1},{2,18},{18,2},{3,19},{19,3},{4,20},{20... | collective-permute-start | bytes 12296 | tf_op jit(solution)/shard_map/ppermute | solution.py:21
  64.9 10.4 %copy-start = (f32[2048,256]{1,0:T(8,128)S(1)}, f32[2048,256]{1,0:T(8,128)}, u32[]{:S(2)}) copy-start(f32[2048,256]{1,0:T(8,128)} %partial_weights.1.rest_0_.refs_1_.refs_0_.refs_2_) | copy-start | bytes 6291460
  69.6 8.0 %copy-start.13 = (bf16[64,1024]{1,0:T(8,128)(2,1)S(1)}, bf16[64,1024]{1,0:T(8,128)(2,1)}, u32[]{:S(2)}) copy-start(bf16[64,1024]{1,0:T(8,128)(2,1)} %get-tuple-element.60.refs_0_) | copy-start | bytes 393220
  70.8 6.8 %copy-start.12 = (bf16[64,1024]{1,0:T(8,128)(2,1)S(1)}, bf16[64,1024]{1,0:T(8,128)(2,1)}, u32[]{:S(2)}) copy-start(bf16[64,1024]{1,0:T(8,128)(2,1)} %get-tuple-element.61.refs_0_) | copy-start | bytes 393220
  75.3 1.2 %copy-start.3 = (bf16[256,2048]{1,0:T(8,128)(2,1)S(1)}, bf16[256,2048]{1,0:T(8,128)(2,1)}, u32[]{:S(2)}) copy-start(bf16[256,2048]{1,0:T(8,128)(2,1)} %own_rows.1.refs_2_) | copy-start | bytes 3145732
  76.5 1.1 %copy-start.11 = (bf16[64,1024]{1,0:T(8,128)(2,1)S(1)}, bf16[64,1024]{1,0:T(8,128)(2,1)}, u32[]{:S(2)}) copy-start(bf16[64,1024]{1,0:T(8,128)(2,1)} %get-tuple-element.62.refs_0_) | copy-start | bytes 393220
  76.5 2.0 %collective-permute-start.18 = (s32[8,128]{1,0:T(8,128)S(1)}, s32[8,128]{1,0:T(8,128)S(1)}, u32[]{:S(2)}, u32[]{:S(2)}) collective-permute-start(s32[8,128]{1,0:T(8,128)S(1)} %after.16), channel_id=1, source_target_pairs={{0,1},{1,0},{2,3},{3,2},{4,5},{5,4},{6,7},{7,6},{8,9},{9,8},{10,11... | collective-permute-start | bytes 12296 | tf_op jit(solution)/shard_map/ppermute | solution.py:21
  76.5 2.5 %collective-permute-start.22 = (bf16[256,1024]{1,0:T(8,128)(2,1)}, bf16[256,1024]{1,0:T(8,128)(2,1)S(1)}, u32[]{:S(2)}, u32[]{:S(2)}) collective-permute-start(bf16[256,1024]{1,0:T(8,128)(2,1)} %stack.1.refs_7_), channel_id=1, source_target_pairs={{0,1},{1,0},{2,3},{3,2},{4,5},{5,4},{6,7},{7,6},{8,9},{9,8},{10,11... | collective-permute-start | bytes 1572872 | tf_op jit(solution)/shard_map/ppermute | solution.py:21
  77.1 4.4 %collective-permute-start.23 = (bf16[256,1024]{1,0:T(8,128)(2,1)}, bf16[256,1024]{1,0:T(8,128)(2,1)S(1)}, u32[]{:S(2)}, u32[]{:S(2)}) collective-permute-start(bf16[256,1024]{1,0:T(8,128)(2,1)} %collective-permute-done.17.refs_4_.refs_9_), channel_id=1, source_target_pairs={{0,1},{1,0},{2,3},{3,2},{4,5},{5,4},{6,7},{7,6},{8,9},{9,8},{10,11... | collective-permute-start | bytes 1572872 | tf_op jit(solution)/shard_map/ppermute | solution.py:21
  77.6 6.4 %copy-start.4 = (bf16[256,2048]{1,0:T(8,128)(2,1)S(1)}, bf16[256,2048]{1,0:T(8,128)(2,1)}, u32[]{:S(2)}) copy-start(bf16[256,2048]{1,0:T(8,128)(2,1)} %own_rows.1.refs_2_) | copy-start | bytes 3145732
  77.6 6.4 %copy-start.15 = (s32[4,4]{1,0:T(4,128)S(1)}, s32[4,4]{1,0:T(4,128)}, u32[]{:S(2)}) copy-start(s32[4,4]{1,0:T(4,128)} %get-tuple-element.44.table_ref) | copy-start | bytes 196
  78.5 3.6 %collective-permute-start.21 = (bf16[256,1024]{1,0:T(8,128)(2,1)S(1)}, bf16[256,1024]{1,0:T(8,128)(2,1)S(1)}, u32[]{:S(2)}, u32[]{:S(2)}) collective-permute-start(bf16[256,1024]{1,0:T(8,128)(2,1)S(1)} %after.19.refs_5_), channel_id=1, source_target_pairs={{0,1},{1,0},{2,3},{3,2},{4,5},{5,4},{6,7},{7,6},{8,9},{9,8},{10,11... | collective-permute-start | bytes 1572872 | tf_op jit(solution)/shard_map/ppermute | solution.py:21
  78.5 5.5 %collective-permute-start.19 = (bf16[256,1024]{1,0:T(8,128)(2,1)S(1)}, bf16[256,1024]{1,0:T(8,128)(2,1)S(1)}, u32[]{:S(2)}, u32[]{:S(2)}) collective-permute-start(bf16[256,1024]{1,0:T(8,128)(2,1)S(1)} %after.17.refs_3_), channel_id=1, source_target_pairs={{0,1},{1,0},{2,3},{3,2},{4,5},{5,4},{6,7},{7,6},{8,9},{9,8},{10,11... | collective-permute-start | bytes 1572872 | tf_op jit(solution)/shard_map/ppermute | solution.py:21
  79.0 11.4 %collective-permute-start.31 = (bf16[64,1024]{1,0:T(8,128)(2,1)S(1)}, bf16[64,1024]{1,0:T(8,128)(2,1)S(1)}, u32[]{:S(2)}, u32[]{:S(2)}) collective-permute-start(bf16[64,1024]{1,0:T(8,128)(2,1)S(1)} %after.26), channel_id=1, source_target_pairs={{0,12},{4,0},{8,4},{12,8},{1,13},{5,1},{9,5},{13,9},{2,14},{6,2},{... | collective-permute-start | bytes 393224 | tf_op jit(solution)/shard_map/ppermute | solution.py:21
  81.4 9.0 %collective-permute-start.29 = (bf16[64,1024]{1,0:T(8,128)(2,1)S(1)}, bf16[64,1024]{1,0:T(8,128)(2,1)S(1)}, u32[]{:S(2)}, u32[]{:S(2)}) collective-permute-start(bf16[64,1024]{1,0:T(8,128)(2,1)S(1)} %after.24), channel_id=1, source_target_pairs={{0,12},{4,0},{8,4},{12,8},{1,13},{5,1},{9,5},{13,9},{2,14},{6,2},{... | collective-permute-start | bytes 393224 | tf_op jit(solution)/shard_map/ppermute | solution.py:21
  81.4 9.5 %collective-permute-start.27 = (bf16[64,1024]{1,0:T(8,128)(2,1)S(1)}, bf16[64,1024]{1,0:T(8,128)(2,1)S(1)}, u32[]{:S(2)}, u32[]{:S(2)}) collective-permute-start(bf16[64,1024]{1,0:T(8,128)(2,1)S(1)} %after.22), channel_id=1, source_target_pairs={{0,12},{4,0},{8,4},{12,8},{1,13},{5,1},{9,5},{13,9},{2,14},{6,2},{... | collective-permute-start | bytes 393224 | tf_op jit(solution)/shard_map/ppermute | solution.py:21
  82.1 11.0 %collective-permute-start.25 = (bf16[64,1024]{1,0:T(8,128)(2,1)S(1)}, bf16[64,1024]{1,0:T(8,128)(2,1)S(1)}, u32[]{:S(2)}, u32[]{:S(2)}) collective-permute-start(bf16[64,1024]{1,0:T(8,128)(2,1)S(1)} %after.20), channel_id=1, source_target_pairs={{0,12},{4,0},{8,4},{12,8},{1,13},{5,1},{9,5},{13,9},{2,14},{6,2},{... | collective-permute-start | bytes 393224 | tf_op jit(solution)/shard_map/ppermute | solution.py:21
  88.9 10.7 %collective-permute-start.24 = (bf16[1024,128]{1,0:T(8,128)(2,1)S(1)}, bf16[1024,128]{1,0:T(8,128)(2,1)S(1)}, u32[]{:S(2)}, u32[]{:S(2)}) collective-permute-start(bf16[1024,128]{1,0:T(8,128)(2,1)S(1)} %get-tuple-element.57.refs_1_), channel_id=1, source_target_pairs={{0,2},{2,0},{1,3},{3,1},{4,6},{6,4},{5,7},{7,5},{8,10},{10,8},{9,1... | collective-permute-start | bytes 786440 | tf_op jit(solution)/shard_map/ppermute | solution.py:21
  90.4 2.7 %collective-permute-start.32 = (bf16[64,1024]{1,0:T(8,128)(2,1)S(1)}, bf16[64,1024]{1,0:T(8,128)(2,1)S(1)}, u32[]{:S(2)}, u32[]{:S(2)}) collective-permute-start(bf16[64,1024]{1,0:T(8,128)(2,1)S(1)} %after.27.refs_6_), channel_id=1, source_target_pairs={{0,1},{1,0},{2,3},{3,2},{4,5},{5,4},{6,7},{7,6},{8,9},{9,8},{10,11... | collective-permute-start | bytes 393224 | tf_op jit(solution)/shard_map/ppermute | solution.py:21
  90.5 2.7 %collective-permute-start.30 = (bf16[64,1024]{1,0:T(8,128)(2,1)S(1)}, bf16[64,1024]{1,0:T(8,128)(2,1)S(1)}, u32[]{:S(2)}, u32[]{:S(2)}) collective-permute-start(bf16[64,1024]{1,0:T(8,128)(2,1)S(1)} %after.25.refs_4_), channel_id=1, source_target_pairs={{0,1},{1,0},{2,3},{3,2},{4,5},{5,4},{6,7},{7,6},{8,9},{9,8},{10,11... | collective-permute-start | bytes 393224 | tf_op jit(solution)/shard_map/ppermute | solution.py:21
  91.0 2.2 %collective-permute-start.28 = (bf16[64,1024]{1,0:T(8,128)(2,1)S(1)}, bf16[64,1024]{1,0:T(8,128)(2,1)S(1)}, u32[]{:S(2)}, u32[]{:S(2)}) collective-permute-start(bf16[64,1024]{1,0:T(8,128)(2,1)S(1)} %after.23.refs_2_), channel_id=1, source_target_pairs={{0,1},{1,0},{2,3},{3,2},{4,5},{5,4},{6,7},{7,6},{8,9},{9,8},{10,11... | collective-permute-start | bytes 393224 | tf_op jit(solution)/shard_map/ppermute | solution.py:21
  93.1 1.3 %collective-permute-start.26 = (bf16[64,1024]{1,0:T(8,128)(2,1)S(1)}, bf16[64,1024]{1,0:T(8,128)(2,1)S(1)}, u32[]{:S(2)}, u32[]{:S(2)}) collective-permute-start(bf16[64,1024]{1,0:T(8,128)(2,1)S(1)} %after.21.refs_0_), channel_id=1, source_target_pairs={{0,1},{1,0},{2,3},{3,2},{4,5},{5,4},{6,7},{7,6},{8,9},{9,8},{10,11... | collective-permute-start | bytes 393224 | tf_op jit(solution)/shard_map/ppermute | solution.py:21
  95.2 4.3 %collective-permute-start.33 = (bf16[256,128]{1,0:T(8,128)(2,1)S(1)}, bf16[256,128]{1,0:T(8,128)(2,1)S(1)}, u32[]{:S(2)}, u32[]{:S(2)}) collective-permute-start(bf16[256,128]{1,0:T(8,128)(2,1)S(1)} %get-tuple-element.65), channel_id=1, source_target_pairs={{0,2},{2,0},{1,3},{3,1},{4,6},{6,4},{5,7},{7,5},{8,10},{10,8},{9,1... | collective-permute-start | bytes 196616 | tf_op jit(solution)/shard_map/ppermute | solution.py:21
  (1 other events, 0.9 us)

commit v11 on v10

--- a/solution.py
+++ b/solution.py
@@ -112,7 +112,7 @@
     half = total // n_rep
 
     def kernel(pattern_ref, slot_ref, *refs):
-        outs, rows_ref = refs[-1 - n_rep:-1], refs[-1]
+        outs, rows_ref = refs[-1 - 2 * n_rep:-1], refs[-1]
         me, group = lax.axis_index("shard"), lax.axis_index("groups")
         for k in range(n_list):
             owner = lax.div(slot_ref[pattern_ref[me, k]], jnp.int32(local_blocks))
@@ -131,15 +131,15 @@
         for r in range(n_rep):
             @pl.when(lax.axis_index("rep") == r)
             def _():
-                for d, out in enumerate(outs):
-                    at = ((r + d) % n_rep) * half
-                    out[...] = rows_ref[at:at + half, :].T
+                for j, out in enumerate(outs):
+                    at, first = ((r + j // 2) % n_rep) * half, (j % 2) * (width // 2)
+                    out[...] = rows_ref[at:at + half, first:first + width // 2].T
 
     return pl.pallas_call(
         kernel,
         in_specs=[SMEM, SMEM] + [VMEM] * (n_group * n_cluster) + [ANY] * len(others),
-        out_specs=[VMEM] * n_rep,
-        out_shape=[jax.ShapeDtypeStruct((width, half), BF16)] * n_rep,
+        out_specs=[VMEM] * (2 * n_rep),
+        out_shape=[jax.ShapeDtypeStruct((width // 2, half), BF16)] * (2 * n_rep),
         scratch_shapes=[pltpu.VMEM((total, width), BF16)],
         cost_estimate=cost(0, 4 * total * width),
         compiler_params=PARAMS,
@@ -234,15 +234,16 @@
 
 
 def partial_weights(matrices, queries, block, depth, dtype, *others):
-    width, total = queries[0].shape
+    width, total = matrices[0].shape[1], queries[0].shape[1]
     tile = 512 if depth % 512 == 0 else depth
     steps = depth // tile
     n = len(matrices)
 
     def kernel(block_ref, *refs):
-        value = dot(refs[0][...], refs[n][...])
-        for j in range(1, n):
-            value = value + dot(refs[j][...], refs[n + j][...])
+        value = None
+        for j in range(n):
+            part = dot(refs[j][...], jnp.concatenate([refs[n + 2 * j][...], refs[n + 2 * j + 1][...]]))
+            value = part if value is None else value + part
         refs[-1][...] = value.astype(dtype)
 
     return pl.pallas_call(
@@ -251,7 +252,7 @@
             num_scalar_prefetch=1,
             grid=(steps,),
             in_specs=[pl.BlockSpec((tile, width), lambda i, b: (b[0] * steps + i, 0))] * n
-            + [pl.BlockSpec((width, total), lambda i, b: (0, 0))] * n
+            + [pl.BlockSpec((width // 2, total), lambda i, b: (0, 0))] * (2 * n)
             + [ANY] * len(others),
             out_specs=pl.BlockSpec((tile, total), lambda i, b: (i, 0)),
         ),
@@ -302,15 +303,17 @@
     n = len(matrices)
 
     def kernel(*refs):
+        parts = [jnp.concatenate([refs[n + 2 * j][...], refs[n + 2 * j + 1][...]]) for j in range(n)]
         for at in range(0, depth, tile):
-            value = dot(refs[0][at:at + tile, :], refs[n][...])
-            for j in range(1, n):
-                value = value + dot(refs[j][at:at + tile, :], refs[n + j][...])
+            value = None
+            for j in range(n):
+                part = dot(refs[j][at:at + tile, :], parts[j])
+                value = part if value is None else value + part
             refs[-1][at:at + tile, :] = value.astype(dtype)
 
     return pl.pallas_call(
         kernel,
-        in_specs=[VMEM] * (2 * n),
+        in_specs=[VMEM] * (3 * n),
         out_specs=VMEM,
         out_shape=jax.ShapeDtypeStruct((depth, total), dtype),
         cost_estimate=cost(2 * n * matrices[0].size * total, 2 * n * matrices[0].size),
@@ -567,17 +570,18 @@
     *packed, goal = pack_rows(train, ids, columns, bulk, extra, middle + final)
     firsts, seconds = [], []
     parts = [pieces] + [[shift(x, "groups", n_group, d) for x in pieces] for d in range(1, n_group)]
-    first_cut = packed[0]
+    here = [shift(after(packed[0], *pieces[1:]), "shard", n_shard, 1)]
+    urgent = [here[0]]
     if extra:
-        far = swap(after(packed[-2], *pieces[1:], *[x[0] for x in parts[1:]]), "shard", n_shard, 2)
-        first_cut = after(first_cut, far)
+        far = swap(after(packed[-2], *pieces[1:]), "shard", n_shard, 2)
+        far_all = with_rep(far)
+        urgent += far_all[1:]
     depth = n_rep * columns
     targets = [(feat + d) % n_feat for d in range(1, n_feat)]
     near_chip = fetch(matrices, targets[0], depth, *pieces[1:])
 
     chosen = join_queries(parts, block_slot, pattern, query_store.shape[0], n_feat, n_rep, *near_chip)
-    queries = [chosen[0]] + [shift(chosen[d], "rep", n_rep, d) for d in range(1, n_rep)]
-    here = [shift(first_cut, "shard", n_shard, 1)]
+    queries = [*chosen[:2]] + [shift(chosen[j], "rep", n_rep, j // 2) for j in range(2, 2 * n_rep)]
 
     sends = [fetched_weights(near_chip, queries, BF16)]
     sends += [partial_weights(matrices, queries, f, depth, BF16) for f in targets[1:]]
@@ -585,7 +589,8 @@
     own = partial_weights(matrices, queries, feat, depth, F32, *sends)
 
     for (hops, _, _), x in zip(middle[1:], packed[1:]):
-        here.append(shift(after(x, here[-1], *sends), "shard", n_shard, hops))
+        here.append(shift(after(x, *urgent, *sends), "shard", n_shard, hops))
+        urgent = [here[-1]]
     last = [
         shift(after(packed[len(middle) + j], here[-1], own), "shard", n_shard, last_hops) for j in range(len(final))
     ]
@@ -605,10 +610,10 @@
             return [[jnp.zeros((2 * extra, columns), BF16)] * n_rep] * 2
 
         seconds = lax.cond(flag[0, 0] > 0, second_round, no_round, packed[-1])
-        pair = stack([packed[-3], far], here[0], *sends)
-        near = swap(pair, "shard", n_shard, 1)
-        firsts = [with_rep(pair), with_rep(near)]
-        marks += [seconds[0][0], near]
+        near = swap(stack([packed[-3], far], *sends), "shard", n_shard, 1)
+        pairs = [stack([x, y], own) for x, y in zip(with_rep(packed[-3]), far_all)]
+        firsts = [pairs, with_rep(after(near, own))]
+        marks += [seconds[0][0], near, *pairs]
 
     mark = shift(after(jnp.zeros((8, LANES), I32), *marks), "rep", n_rep, 1)
     ready = [with_rep(after(x, mark)) for x in here]

time: 102 us -> 100 us (0.980)
  waiting for transfers between devices: 20.3 us -> 16.8 us
  local copies, waits for them, and re-layouts: 8.28 us -> 10.7 us
  starting transfers between devices: 31.7 us -> 30 us
    ppermute x28 -> x30, waiting for transfers between devices: 19.2 us -> 8.59 us  [shift(): return lax.ppermute(x, axis, [(i, (i + by) % size) for i in range(size)])]
    ppermute x2, waiting for transfers between devices: 1.07 us -> 8.2 us  [swap(): return lax.ppermute(x, axis, [(i, i ^ bit) for i in range(size)])]
    unnamed x38 -> x56, local copies, waits for them, and re-layouts: 4.32 us -> 6.79 us
    ppermute x28 -> x30, starting transfers between devices: 28.8 us -> 27.6 us  [shift(): return lax.ppermute(x, axis, [(i, (i + by) % size) for i in range(size)])]
    pallas_call x1 -> x3, Pallas kernels: 0.84 us -> 1.86 us  [stack(): pl.pallas_call(kernel, in_specs=[VMEM] * n + [ANY] * len(others), out_spe...]
  transfers between devices with their start and end apart: 30 -> 32, of which waited for: 9 -> 8; matrix products, arithmetic and copies ran while one was open for 4% -> 4% of each run, Pallas kernels for 37% -> 40%
where the time goes in v11:
time: 100 us; the launch traced here: 99.5 us
  Pallas kernels  41 us (41%)
  starting transfers between devices  30 us (30%)
  waiting for transfers between devices  16.8 us (17%)
  local copies, waits for them, and re-layouts  10.7 us (11%)
  between operations  1 us (1%)
    ppermute x30, starting transfers between devices, shift(): return lax.ppermute(x, axis, [(i, (i + by) % size) for i in range(size)])  27.6 us
    ppermute x30, waiting for transfers between devices, shift(): return lax.ppermute(x, axis, [(i, (i + by) % size) for i in range(size)])  8.59 us
    ppermute x2, waiting for transfers between devices, swap(): return lax.ppermute(x, axis, [(i, i ^ bit) for i in range(size)])  8.2 us
    unnamed x56, local copies, waits for them, and re-layouts  6.79 us
    pallas_call x1, Pallas kernels, partial_weights(): pl.pallas_call(kernel, grid_spec=pltpu.PrefetchScalarGridSpec(num_scalar_...  6.72 us
    pallas_call x1, Pallas kernels, pack_rows(): pl.pallas_call(kernel, grid=(1,), in_specs=[pl.BlockSpec((lines, LANES),...  6.22 us
    pallas_call x1, Pallas kernels, fetch(): pl.pallas_call(kernel, in_specs=[SMEM] + [ANY] * (n + len(others)), out_s...  5.57 us
    pallas_call x1, Pallas kernels, early_scores(): pl.pallas_call(kernel, in_specs=[SMEM] + [VMEM] * (2 + n_other + n_rep *...  4.9 us
  transfers between devices with their start and end apart: 32, of which 8 were waited for; matrix products, arithmetic and copies ran while one was open for 4% of the time, Pallas kernels for 40%

profile of v11, /device:TPU:0, one launch (start us, length us, event | category | flops | bytes accessed | tf_op | source)
XLA Modules:
  0.0 99.5 jit_solution(13342405083691423221)
XLA Ops:
  0.5 2.7 %pick_queries.1 = (bf16[1,64,1024]{2,1,0:T(8,128)(2,1)}, bf16[1,64,1024]{2,1,0:T(8,128)(2,1)}, bf16[1,64,1024]{2,1,0:T(8,128)(2,1)}, bf16[1,64,1024]{2,1,0:T(8,128)(2,1)}) custom-call(s32[4,4]{1,0:T(4,128)} %pattern_ref.3, s32[16]{0:T(128)} %slot_ref.3, bf16[4,128,1024]{2,1,0:T(8,128)(2,1)} %in_ref.1), custom_call_target="tpu_custom_call" | custom-call | flops 1 | bytes 1 | tf_op jit(solution)/shard_map/pick_queries/pallas_call | solution.py:93
  3.1 2.6 %collective-permute-start.5 = (bf16[1,64,1024]{2,1,0:T(8,128)(2,1)}, bf16[1,64,1024]{2,1,0:T(8,128)(2,1)S(1)}, u32[]{:S(2)}, u32[]{:S(2)}) collective-permute-start(bf16[1,64,1024]{2,1,0:T(8,128)(2,1)} %get-tuple-element.39), channel_id=1, source_target_pairs={{0,4},{4,8},{8,12},{12,0},{1,5},{5,9},{9,13},{13,1},{2,6},{6,10},{... | collective-permute-start | bytes 393224 | tf_op jit(solution)/shard_map/ppermute | solution.py:21
  5.8 2.6 %collective-permute-start.6 = (bf16[1,64,1024]{2,1,0:T(8,128)(2,1)}, bf16[1,64,1024]{2,1,0:T(8,128)(2,1)S(1)}, u32[]{:S(2)}, u32[]{:S(2)}) collective-permute-start(bf16[1,64,1024]{2,1,0:T(8,128)(2,1)} %get-tuple-element.40), channel_id=1, source_target_pairs={{0,8},{4,12},{8,0},{12,4},{1,9},{5,13},{9,1},{13,5},{2,10},{6,14},... | collective-permute-start | bytes 393224 | tf_op jit(solution)/shard_map/ppermute | solution.py:21
  8.4 1.4 %collective-permute-start.7 = (bf16[1,64,1024]{2,1,0:T(8,128)(2,1)}, bf16[1,64,1024]{2,1,0:T(8,128)(2,1)S(1)}, u32[]{:S(2)}, u32[]{:S(2)}) collective-permute-start(bf16[1,64,1024]{2,1,0:T(8,128)(2,1)} %get-tuple-element.41), channel_id=1, source_target_pairs={{0,12},{4,0},{8,4},{12,8},{1,13},{5,1},{9,5},{13,9},{2,14},{6,2},{... | collective-permute-start | bytes 393224 | tf_op jit(solution)/shard_map/ppermute | solution.py:21
  9.7 1.5 %collective-permute-start.8 = (bf16[1,64,1024]{2,1,0:T(8,128)(2,1)}, bf16[1,64,1024]{2,1,0:T(8,128)(2,1)S(1)}, u32[]{:S(2)}, u32[]{:S(2)}) collective-permute-start(bf16[1,64,1024]{2,1,0:T(8,128)(2,1)} %get-tuple-element.38.refs_0_), channel_id=1, source_target_pairs={{0,16},{16,0},{1,17},{17,1},{2,18},{18,2},{3,19},{19,3},{4,20},{20... | collective-permute-start | bytes 393224 | tf_op jit(solution)/shard_map/ppermute | solution.py:21
  11.2 6.2 %pack_rows.1 = (bf16[256,1024]{1,0:T(8,128)(2,1)}, bf16[256,1024]{1,0:T(8,128)(2,1)}, bf16[64,1024]{1,0:T(8,128)(2,1)}, bf16[64,1024]{1,0:T(8,128)(2,1)}, bf16[6...) custom-call(s32[32,128]{1,0:T(8,128)} %bitcast.9, ...), custom_call_target="tpu_custom_call" | custom-call | flops 1 | bytes 1 | tf_op jit(solution)/shard_map/pack_rows/pallas_call | solution.py:221
  17.9 2.4 %collective-permute-start.17 = (bf16[128,1024]{1,0:T(8,128)(2,1)}, bf16[128,1024]{1,0:T(8,128)(2,1)S(1)}, u32[]{:S(2)}, u32[]{:S(2)}) collective-permute-start(bf16[128,1024]{1,0:T(8,128)(2,1)} %after.16), channel_id=1, source_target_pairs={{0,8},{4,12},{8,0},{12,4},{1,9},{5,13},{9,1},{13,5},{2,10},{6,14},... | collective-permute-start | bytes 786440 | tf_op jit(solution)/shard_map/ppermute | solution.py:25
  20.3 2.6 %collective-permute-start.15 = (bf16[256,1024]{1,0:T(8,128)(2,1)}, bf16[256,1024]{1,0:T(8,128)(2,1)S(1)}, u32[]{:S(2)}, u32[]{:S(2)}) collective-permute-start(bf16[256,1024]{1,0:T(8,128)(2,1)} %after.15), channel_id=1, source_target_pairs={{0,4},{4,8},{8,12},{12,0},{1,5},{5,9},{9,13},{13,1},{2,6},{6,10},{... | collective-permute-start | bytes 1572872 | tf_op jit(solution)/shard_map/ppermute | solution.py:21
  22.8 1.5 %collective-permute-start.10 = (bf16[1,64,1024]{2,1,0:T(8,128)(2,1)S(1)}, bf16[1,64,1024]{2,1,0:T(8,128)(2,1)S(1)}, u32[]{:S(2)}, u32[]{:S(2)}) collective-permute-start(bf16[1,64,1024]{2,1,0:T(8,128)(2,1)S(1)} %collective-permute-done.6.refs_3_.refs_2_), channel_id=1, source_target_pairs={{0,16},{16,0},{1,17},{17,1},{2,18},{18,2},{3,19},{19,3},{4,20},{20... | collective-permute-start | bytes 393224 | tf_op jit(solution)/shard_map/ppermute | solution.py:21
  24.3 0.5 collective-permute-start.11
  24.8 1.5 %collective-permute-start.9 = (bf16[1,64,1024]{2,1,0:T(8,128)(2,1)S(1)}, bf16[1,64,1024]{2,1,0:T(8,128)(2,1)S(1)}, u32[]{:S(2)}, u32[]{:S(2)}) collective-permute-start(bf16[1,64,1024]{2,1,0:T(8,128)(2,1)S(1)} %collective-permute-done.5.refs_2_.refs_1_), channel_id=1, source_target_pairs={{0,16},{16,0},{1,17},{17,1},{2,18},{18,2},{3,19},{19,3},{4,20},{20... | collective-permute-start | bytes 393224 | tf_op jit(solution)/shard_map/ppermute | solution.py:21
  26.4 5.6 %fetch.1 = (bf16[2048,1024]{1,0:T(8,128)(2,1)S(1)}, bf16[2048,1024]{1,0:T(8,128)(2,1)}) custom-call(s32[1]{0:T(128)} %bitcast.3.block_ref, bf16[4096,1024]{1,0:T(8,128)(2,1)} %bitcast.7, bf16[4096,1024]{1,0:T(8,128)(2,1)} %collective-permute-done.4.refs_1_, bf16[1,64,1024]{2,1,0:T(8,128)(2,1)S(1)} %collective-permute-done.5.refs_2_.refs_1_, ...), custom_call_target="tpu_custom_call" | custom-call | flops 1 | bytes 1 | tf_op jit(solution)/shard_map/fetch/pallas_call | solution.py:287
  32.0 1.0 %collective-permute-done.9.refs_5_ = bf16[1,64,1024]{2,1,0:T(8,128)(2,1)S(1)} collective-permute-done((bf16[1,64,1024]{2,1,0:T(8,128)(2,1)S(1)}, bf16[1,64,1024]{2,1,0:T(8,128)(2,1)S(1)}, u32[]{:S(2)}, u32[]{:S(2)}) %collective-permute-start.9) | collective-permute-done | bytes 131104 | tf_op jit(solution)/shard_map/ppermute | solution.py:21
  33.0 2.2 %copy-done.1 = bf16[2048,1024]{1,0:T(8,128)(2,1)S(1)} copy-done((bf16[2048,1024]{1,0:T(8,128)(2,1)S(1)}, bf16[2048,1024]{1,0:T(8,128)(2,1)}, u32[]{:S(2)}) %copy-start.1) | copy-done | bytes 4194328
  35.2 1.2 %join_queries.1 = (bf16[512,256]{1,0:T(8,128)(2,1)S(1)}, bf16[512,256]{1,0:T(8,128)(2,1)S(1)}, bf16[512,256]{1,0:T(8,128)(2,1)S(1)}, bf16[512,256]{1,0:T(8,128)(2,1)S(1)}) custom-call(s32[4,4]{1,0:T(4,128)S(1)} %copy-done.23, s32[16]{0:T(128)S(1)} %copy-done.25, bf16[1,64,1024]{2,1,0:T(8,128)(2,1)S(1)} %copy-done.18, ...), custom_call_target="tpu_custom_call" | custom-call | flops 1 | bytes 1 | tf_op jit(solution)/shard_map/join_queries/pallas_call | solution.py:138
  36.5 0.5 collective-permute-start.13
  37.0 7.0 %collective-permute-done.17.refs_1_ = bf16[128,1024]{1,0:T(8,128)(2,1)S(1)} collective-permute-done((bf16[128,1024]{1,0:T(8,128)(2,1)}, bf16[128,1024]{1,0:T(8,128)(2,1)S(1)}, u32[]{:S(2)}, u32[]{:S(2)}) %collective-permute-start.17) | collective-permute-done | bytes 262176 | tf_op jit(solution)/shard_map/ppermute | solution.py:25
  44.1 3.3 %fetched_weights.1.refs_6_.refs_2_.refs_3_ = bf16[2048,256]{1,0:T(8,128)(2,1)} custom-call(bf16[2048,1024]{1,0:T(8,128)(2,1)S(1)} %get-tuple-element.42.refs_8_.refs_0_, bf16[2048,1024]{1,0:T(8,128)(2,1)S(1)} %copy-done.1, bf16[512,256]{1,0:T(8,128)(2,1)S(1)} %get-tuple-element.44.refs_2_, bf16[512,256]{1,0:T(8,128)(2,1)S(1)} %get-tuple-element.45.refs_3_, ...), custom_call_target="tpu_custom_call" | custom-call | flops 1 | bytes 1 | tf_op jit(solution)/shard_map/fetched_weights/pallas_call | solution.py:314
  47.4 0.8 stack.3
  48.4 1.6 %collective-permute-start.14 = (bf16[2048,256]{1,0:T(8,128)(2,1)}, bf16[2048,256]{1,0:T(8,128)(2,1)}, u32[]{:S(2)}, u32[]{:S(2)}) collective-permute-start(bf16[2048,256]{1,0:T(8,128)(2,1)} %fetched_weights.1.refs_6_.refs_2_.refs_3_), channel_id=1, source_target_pairs={{0,2},{2,0},{1,3},{3,1},{4,6},{6,4},{5,7},{7,5},{8,10},{10,8},{9,1... | collective-permute-start | bytes 3145736 | tf_op jit(solution)/shard_map/ppermute | solution.py:21
  50.1 6.7 %partial_weights.1.rest_0_.refs_2_.refs_1_.refs_0_ = f32[2048,256]{1,0:T(8,128)} custom-call(s32[1]{0:T(128)} %bitcast.1.block_ref, bf16[4096,1024]{1,0:T(8,128)(2,1)} %bitcast.8, bf16[4096,1024]{1,0:T(8,128)(2,1)} %collective-permute-done.4.refs_1_, bf16[512,256]{1,0:T(8,128)(2,1)} %copy-done.9, bf16[512,256]{1,0:T(8,128)(2,1)} %copy-done.10, ...), custom_call_target="tpu_custom_call" | custom-call | flops 1 | bytes 1 | tf_op jit(solution)/shard_map/partial_weights/pallas_call | solution.py:249
  56.9 1.5 %row_table.1 = (s32[4,4]{1,0:T(4,128)}, s32[8,128]{1,0:T(8,128)}) custom-call(s32[32,128]{1,0:T(8,128)} %bitcast.10, f32[2048,256]{1,0:T(8,128)} %partial_weights.1.rest_0_.refs_2_.refs_1_.refs_0_), custom_call_target="tpu_custom_call" | custom-call | flops 1 | bytes 1 | tf_op jit(solution)/shard_map/row_table/pallas_call | solution.py:355
  58.4 1.6 %collective-permute-start.16 = (s32[8,128]{1,0:T(8,128)}, s32[8,128]{1,0:T(8,128)S(1)}, u32[]{:S(2)}, u32[]{:S(2)}) collective-permute-start(s32[8,128]{1,0:T(8,128)} %get-tuple-element.51), channel_id=1, source_target_pairs={{0,16},{16,0},{1,17},{17,1},{2,18},{18,2},{3,19},{19,3},{4,20},{20... | collective-permute-start | bytes 12296 | tf_op jit(solution)/shard_map/ppermute | solution.py:21
  60.0 4.5 %own_rows.1.refs_2_ = bf16[256,2048]{1,0:T(8,128)(2,1)} custom-call(s32[8,128]{1,0:T(8,128)} %get-tuple-element.49.goal_ref, bf16[1024,2048]{1,0:T(8,128)(2,1)} %train_ref.3, f32[2048,256]{1,0:T(8,128)} %partial_weights.1.rest_0_.refs_2_.refs_1_.refs_0_), custom_call_target="tpu_custom_call" | custom-call | flops 1 | bytes 1 | tf_op jit(solution)/shard_map/own_rows/pallas_call | solution.py:164
  64.6 1.0 %stack.5.refs_6_.refs_8_ = bf16[256,1024]{1,0:T(8,128)(2,1)S(1)} custom-call(bf16[128,1024]{1,0:T(8,128)(2,1)} %collective-permute-done.19.refs_0_, bf16[128,1024]{1,0:T(8,128)(2,1)S(1)} %copy-done.17, f32[2048,256]{1,0:T(8,128)S(1)} %copy-done), custom_call_target="tpu_custom_call" | custom-call | flops 1 | bytes 1 | tf_op jit(solution)/shard_map/stack/pallas_call | solution.py:60
  65.7 0.8 copy-done.4
  66.5 0.5 slice.3
  67.6 3.4 %conditional.1 = (bf16[256,1024]{1,0:T(8,128)(2,1)}, bf16[256,1024]{1,0:T(8,128)(2,1)}, bf16[256,1024]{1,0:T(8,128)(2,1)}, bf16[256,1024]{1,0:T(8,128)(2,1)}) conditional(s32[]{:T(128)} %bitcast.4, () %tuple.13, bf16[128,1024]{1,0:T(8,128)(2,1)S(1)} %copy-done.26), branch_computations={%region_0.1_spmd, %region_1.2_spmd} | conditional | bytes 8388800 | solution.py:612
  67.6 0.9 broadcast.3
  68.5 0.8 broadcast.3.clone
  69.4 0.8 broadcast.3.clone.1
  70.2 0.9 broadcast.3.clone.2
  71.1 1.2 %collective-permute-done.18.refs_4_.refs_0_ = bf16[256,1024]{1,0:T(8,128)(2,1)} collective-permute-done((bf16[256,1024]{1,0:T(8,128)(2,1)}, bf16[256,1024]{1,0:T(8,128)(2,1)}, u32[]{:S(2)}, u32[]{:S(2)}) %collective-permute-start.18) | collective-permute-done | bytes 524320 | tf_op jit(solution)/shard_map/ppermute | solution.py:25
  72.3 1.2 %copy-done.2 = bf16[256,2048]{1,0:T(8,128)(2,1)S(1)} copy-done((bf16[256,2048]{1,0:T(8,128)(2,1)S(1)}, bf16[256,2048]{1,0:T(8,128)(2,1)}, u32[]{:S(2)}) %copy-start.2) | copy-done | bytes 1048600
  73.5 1.0 %copy-done.5 = bf16[256,1024]{1,0:T(8,128)(2,1)S(1)} copy-done((bf16[256,1024]{1,0:T(8,128)(2,1)S(1)}, bf16[256,1024]{1,0:T(8,128)(2,1)}, u32[]{:S(2)}) %copy-start.5) | copy-done | bytes 524312
  75.6 0.8 copy-done.19
  76.9 2.9 %collective-permute-start.33 = (bf16[64,1024]{1,0:T(8,128)(2,1)S(1)}, bf16[64,1024]{1,0:T(8,128)(2,1)S(1)}, u32[]{:S(2)}, u32[]{:S(2)}) collective-permute-start(bf16[64,1024]{1,0:T(8,128)(2,1)S(1)} %after.28), channel_id=1, source_target_pairs={{0,12},{4,0},{8,4},{12,8},{1,13},{5,1},{9,5},{13,9},{2,14},{6,2},{... | collective-permute-start | bytes 393224 | tf_op jit(solution)/shard_map/ppermute | solution.py:21
  79.8 0.6 collective-permute-start.29
  80.5 1.4 %collective-permute-start.27 = (bf16[64,1024]{1,0:T(8,128)(2,1)S(1)}, bf16[64,1024]{1,0:T(8,128)(2,1)S(1)}, u32[]{:S(2)}, u32[]{:S(2)}) collective-permute-start(bf16[64,1024]{1,0:T(8,128)(2,1)S(1)} %after.22), channel_id=1, source_target_pairs={{0,12},{4,0},{8,4},{12,8},{1,13},{5,1},{9,5},{13,9},{2,14},{6,2},{... | collective-permute-start | bytes 393224 | tf_op jit(solution)/shard_map/ppermute | solution.py:21
  81.9 4.9 %early_scores.1 = (bf16[2048,256]{1,0:T(8,128)(2,1)S(1)}, bf16[2048,256]{1,0:T(8,128)(2,1)S(1)}, f32[1024,128]{1,0:T(8,128)S(1)}, bf16[1024,128]{1,0:T(8,128)(2,1)S(1)}) custom-call(s32[4,4]{1,0:T(4,128)S(1)} %copy-done.24, f32[2048,256]{1,0:T(8,128)S(1)} %copy-done, bf16[2048,256]{1,0:T(8,128)(2,1)} %collective-permute-done.14.refs_1_, ...), custom_call_target="tpu_custom_call" | custom-call | flops 1 | bytes 1 | tf_op jit(solution)/shard_map/early_scores/pallas_call | solution.py:471
  86.8 1.6 %collective-permute-start.26 = (bf16[1024,128]{1,0:T(8,128)(2,1)S(1)}, bf16[1024,128]{1,0:T(8,128)(2,1)S(1)}, u32[]{:S(2)}, u32[]{:S(2)}) collective-permute-start(bf16[1024,128]{1,0:T(8,128)(2,1)S(1)} %get-tuple-element.61.refs_1_), channel_id=1, source_target_pairs={{0,2},{2,0},{1,3},{3,1},{4,6},{6,4},{5,7},{7,5},{8,10},{10,8},{9,1... | collective-permute-start | bytes 786440 | tf_op jit(solution)/shard_map/ppermute | solution.py:21
  88.3 0.5 collective-permute-start.32
  89.3 2.1 %collective-permute-done.27.refs_0_ = bf16[64,1024]{1,0:T(8,128)(2,1)S(1)} collective-permute-done((bf16[64,1024]{1,0:T(8,128)(2,1)S(1)}, bf16[64,1024]{1,0:T(8,128)(2,1)S(1)}, u32[]{:S(2)}, u32[]{:S(2)}) %collective-permute-start.27) | collective-permute-done | bytes 131104 | tf_op jit(solution)/shard_map/ppermute | solution.py:21
  91.4 1.3 %collective-permute-done.28.refs_1_ = bf16[64,1024]{1,0:T(8,128)(2,1)S(1)} collective-permute-done((bf16[64,1024]{1,0:T(8,128)(2,1)S(1)}, bf16[64,1024]{1,0:T(8,128)(2,1)S(1)}, u32[]{:S(2)}, u32[]{:S(2)}) %collective-permute-start.28) | collective-permute-done | bytes 131104 | tf_op jit(solution)/shard_map/ppermute | solution.py:21
  92.7 0.7 late_scores.1
  93.5 1.1 %collective-permute-start.35 = (bf16[256,128]{1,0:T(8,128)(2,1)S(1)}, bf16[256,128]{1,0:T(8,128)(2,1)S(1)}, u32[]{:S(2)}, u32[]{:S(2)}) collective-permute-start(bf16[256,128]{1,0:T(8,128)(2,1)S(1)} %get-tuple-element.69), channel_id=1, source_target_pairs={{0,2},{2,0},{1,3},{3,1},{4,6},{6,4},{5,7},{7,5},{8,10},{10,8},{9,1... | collective-permute-start | bytes 196616 | tf_op jit(solution)/shard_map/ppermute | solution.py:21
  94.6 3.2 %collective-permute-done.35.refs_3_ = bf16[256,128]{1,0:T(8,128)(2,1)S(1)} collective-permute-done((bf16[256,128]{1,0:T(8,128)(2,1)S(1)}, bf16[256,128]{1,0:T(8,128)(2,1)S(1)}, u32[]{:S(2)}, u32[]{:S(2)}) %collective-permute-start.35) | collective-permute-done | bytes 65568 | tf_op jit(solution)/shard_map/ppermute | solution.py:21
  97.8 1.7 %merge.1 = f32[128,1024]{1,0:T(8,128)} custom-call(s32[4,4]{1,0:T(4,128)S(1)} %copy-done.24, f32[1024,128]{1,0:T(8,128)S(1)} %get-tuple-element.60.refs_0_, bf16[1024,128]{1,0:T(8,128)(2,1)S(1)} %collective-permute-done.26.refs_1_, f32[256,128]{1,0:T(8,128)S(1)} %get-tuple-element.68.refs_2_, bf16[256,128]{1,0:T(8,128)(2,1)S(1)} %collective-permute-done.35.refs_3_), custom_call_target="tpu_custom_call" | custom-call | flops 1 | bytes 1 | tf_op jit(solution)/shard_map/merge/pallas_call | solution.py:533
  (109 shorter events, 3.4 us)
Async XLA Ops:
  0.0 24.8 %collective-permute-start.4 = (bf16[4096,1024]{1,0:T(8,128)(2,1)}, bf16[4096,1024]{1,0:T(8,128)(2,1)}, u32[]{:S(2)}, u32[]{:S(2)}) collective-permute-start(bf16[4096,1024]{1,0:T(8,128)(2,1)} %bitcast.6), channel_id=1, source_target_pairs={{0,1},{1,0},{2,3},{3,2},{4,5},{5,4},{6,7},{7,6},{8,9},{9,8},{10,11... | collective-permute-start | bytes 25165832 | tf_op jit(solution)/shard_map/ppermute | solution.py:21
  3.1 14.3 %collective-permute-start.5 = (bf16[1,64,1024]{2,1,0:T(8,128)(2,1)}, bf16[1,64,1024]{2,1,0:T(8,128)(2,1)S(1)}, u32[]{:S(2)}, u32[]{:S(2)}) collective-permute-start(bf16[1,64,1024]{2,1,0:T(8,128)(2,1)} %get-tuple-element.39), channel_id=1, source_target_pairs={{0,4},{4,8},{8,12},{12,0},{1,5},{5,9},{9,13},{13,1},{2,6},{6,10},{... | collective-permute-start | bytes 393224 | tf_op jit(solution)/shard_map/ppermute | solution.py:21
  5.8 12.1 %collective-permute-start.6 = (bf16[1,64,1024]{2,1,0:T(8,128)(2,1)}, bf16[1,64,1024]{2,1,0:T(8,128)(2,1)S(1)}, u32[]{:S(2)}, u32[]{:S(2)}) collective-permute-start(bf16[1,64,1024]{2,1,0:T(8,128)(2,1)} %get-tuple-element.40), channel_id=1, source_target_pairs={{0,8},{4,12},{8,0},{12,4},{1,9},{5,13},{9,1},{13,5},{2,10},{6,14},... | collective-permute-start | bytes 393224 | tf_op jit(solution)/shard_map/ppermute | solution.py:21
  8.4 9.5 %collective-permute-start.7 = (bf16[1,64,1024]{2,1,0:T(8,128)(2,1)}, bf16[1,64,1024]{2,1,0:T(8,128)(2,1)S(1)}, u32[]{:S(2)}, u32[]{:S(2)}) collective-permute-start(bf16[1,64,1024]{2,1,0:T(8,128)(2,1)} %get-tuple-element.41), channel_id=1, source_target_pairs={{0,12},{4,0},{8,4},{12,8},{1,13},{5,1},{9,5},{13,9},{2,14},{6,2},{... | collective-permute-start | bytes 393224 | tf_op jit(solution)/shard_map/ppermute | solution.py:21
  9.7 14.6 %collective-permute-start.8 = (bf16[1,64,1024]{2,1,0:T(8,128)(2,1)}, bf16[1,64,1024]{2,1,0:T(8,128)(2,1)S(1)}, u32[]{:S(2)}, u32[]{:S(2)}) collective-permute-start(bf16[1,64,1024]{2,1,0:T(8,128)(2,1)} %get-tuple-element.38.refs_0_), channel_id=1, source_target_pairs={{0,16},{16,0},{1,17},{17,1},{2,18},{18,2},{3,19},{19,3},{4,20},{20... | collective-permute-start | bytes 393224 | tf_op jit(solution)/shard_map/ppermute | solution.py:21
  17.9 26.2 %collective-permute-start.17 = (bf16[128,1024]{1,0:T(8,128)(2,1)}, bf16[128,1024]{1,0:T(8,128)(2,1)S(1)}, u32[]{:S(2)}, u32[]{:S(2)}) collective-permute-start(bf16[128,1024]{1,0:T(8,128)(2,1)} %after.16), channel_id=1, source_target_pairs={{0,8},{4,12},{8,0},{12,4},{1,9},{5,13},{9,1},{13,5},{2,10},{6,14},... | collective-permute-start | bytes 786440 | tf_op jit(solution)/shard_map/ppermute | solution.py:25
  20.3 28.0 %collective-permute-start.15 = (bf16[256,1024]{1,0:T(8,128)(2,1)}, bf16[256,1024]{1,0:T(8,128)(2,1)S(1)}, u32[]{:S(2)}, u32[]{:S(2)}) collective-permute-start(bf16[256,1024]{1,0:T(8,128)(2,1)} %after.15), channel_id=1, source_target_pairs={{0,4},{4,8},{8,12},{12,0},{1,5},{5,9},{9,13},{13,1},{2,6},{6,10},{... | collective-permute-start | bytes 1572872 | tf_op jit(solution)/shard_map/ppermute | solution.py:21
  22.8 9.1 %collective-permute-start.10 = (bf16[1,64,1024]{2,1,0:T(8,128)(2,1)S(1)}, bf16[1,64,1024]{2,1,0:T(8,128)(2,1)S(1)}, u32[]{:S(2)}, u32[]{:S(2)}) collective-permute-start(bf16[1,64,1024]{2,1,0:T(8,128)(2,1)S(1)} %collective-permute-done.6.refs_3_.refs_2_), channel_id=1, source_target_pairs={{0,16},{16,0},{1,17},{17,1},{2,18},{18,2},{3,19},{19,3},{4,20},{20... | collective-permute-start | bytes 393224 | tf_op jit(solution)/shard_map/ppermute | solution.py:21
  24.3 7.6 %collective-permute-start.11 = (bf16[1,64,1024]{2,1,0:T(8,128)(2,1)S(1)}, bf16[1,64,1024]{2,1,0:T(8,128)(2,1)S(1)}, u32[]{:S(2)}, u32[]{:S(2)}) collective-permute-start(bf16[1,64,1024]{2,1,0:T(8,128)(2,1)S(1)} %collective-permute-done.7.refs_4_.refs_3_), channel_id=1, source_target_pairs={{0,16},{16,0},{1,17},{17,1},{2,18},{18,2},{3,19},{19,3},{4,20},{20... | collective-permute-start | bytes 393224 | tf_op jit(solution)/shard_map/ppermute | solution.py:21
  24.8 8.2 %collective-permute-start.9 = (bf16[1,64,1024]{2,1,0:T(8,128)(2,1)S(1)}, bf16[1,64,1024]{2,1,0:T(8,128)(2,1)S(1)}, u32[]{:S(2)}, u32[]{:S(2)}) collective-permute-start(bf16[1,64,1024]{2,1,0:T(8,128)(2,1)S(1)} %collective-permute-done.5.refs_2_.refs_1_), channel_id=1, source_target_pairs={{0,16},{16,0},{1,17},{17,1},{2,18},{18,2},{3,19},{19,3},{4,20},{20... | collective-permute-start | bytes 393224 | tf_op jit(solution)/shard_map/ppermute | solution.py:21
  26.4 6.6 %copy-start.18 = (bf16[1,64,1024]{2,1,0:T(8,128)(2,1)S(1)}, bf16[1,64,1024]{2,1,0:T(8,128)(2,1)}, u32[]{:S(2)}) copy-start(bf16[1,64,1024]{2,1,0:T(8,128)(2,1)} %get-tuple-element.38.refs_0_) | copy-start | bytes 393220
  26.4 6.6 %copy-start.23 = (s32[4,4]{1,0:T(4,128)S(1)}, s32[4,4]{1,0:T(4,128)}, u32[]{:S(2)}) copy-start(s32[4,4]{1,0:T(4,128)} %pattern_ref.3) | copy-start | bytes 196
  26.4 6.6 %copy-start.25 = (s32[16]{0:T(128)S(1)}, s32[16]{0:T(128)}, u32[]{:S(2)}) copy-start(s32[16]{0:T(128)} %slot_ref.3) | copy-start | bytes 196
  36.4 11.0 %copy-start.9 = (bf16[512,256]{1,0:T(8,128)(2,1)}, bf16[512,256]{1,0:T(8,128)(2,1)S(1)}, u32[]{:S(2)}) copy-start(bf16[512,256]{1,0:T(8,128)(2,1)S(1)} %get-tuple-element.44.refs_2_) | copy-start | bytes 786436
  36.4 11.0 %copy-start.10 = (bf16[512,256]{1,0:T(8,128)(2,1)}, bf16[512,256]{1,0:T(8,128)(2,1)S(1)}, u32[]{:S(2)}) copy-start(bf16[512,256]{1,0:T(8,128)(2,1)S(1)} %get-tuple-element.45.refs_3_) | copy-start | bytes 786436
  36.4 7.6 %collective-permute-start.12 = (bf16[512,256]{1,0:T(8,128)(2,1)S(1)}, bf16[512,256]{1,0:T(8,128)(2,1)S(1)}, u32[]{:S(2)}, u32[]{:S(2)}) collective-permute-start(bf16[512,256]{1,0:T(8,128)(2,1)S(1)} %get-tuple-element.46), channel_id=1, source_target_pairs={{0,1},{1,0},{2,3},{3,2},{4,5},{5,4},{6,7},{7,6},{8,9},{9,8},{10,11... | collective-permute-start | bytes 786440 | tf_op jit(solution)/shard_map/ppermute | solution.py:21
  36.5 7.5 %collective-permute-start.13 = (bf16[512,256]{1,0:T(8,128)(2,1)S(1)}, bf16[512,256]{1,0:T(8,128)(2,1)S(1)}, u32[]{:S(2)}, u32[]{:S(2)}) collective-permute-start(bf16[512,256]{1,0:T(8,128)(2,1)S(1)} %get-tuple-element.47), channel_id=1, source_target_pairs={{0,1},{1,0},{2,3},{3,2},{4,5},{5,4},{6,7},{7,6},{8,9},{9,8},{10,11... | collective-permute-start | bytes 786440 | tf_op jit(solution)/shard_map/ppermute | solution.py:21
  44.0 3.4 %copy-start.14 = (bf16[128,1024]{1,0:T(8,128)(2,1)}, bf16[128,1024]{1,0:T(8,128)(2,1)S(1)}, u32[]{:S(2)}) copy-start(bf16[128,1024]{1,0:T(8,128)(2,1)S(1)} %collective-permute-done.17.refs_1_) | copy-start | bytes 786436
  44.0 4.2 %collective-permute-start.20 = (bf16[128,1024]{1,0:T(8,128)(2,1)S(1)}, bf16[128,1024]{1,0:T(8,128)(2,1)S(1)}, u32[]{:S(2)}, u32[]{:S(2)}) collective-permute-start(bf16[128,1024]{1,0:T(8,128)(2,1)S(1)} %collective-permute-done.17.refs_1_), channel_id=1, source_target_pairs={{0,1},{1,0},{2,3},{3,2},{4,5},{5,4},{6,7},{7,6},{8,9},{9,8},{10,11... | collective-permute-start | bytes 786440 | tf_op jit(solution)/shard_map/ppermute | solution.py:21
  44.0 3.4 %copy-start.11 = (bf16[512,256]{1,0:T(8,128)(2,1)}, bf16[512,256]{1,0:T(8,128)(2,1)S(1)}, u32[]{:S(2)}) copy-start(bf16[512,256]{1,0:T(8,128)(2,1)S(1)} %collective-permute-done.12.refs_4_) | copy-start | bytes 786436
  44.1 3.4 %copy-start.13 = (bf16[128,1024]{1,0:T(8,128)(2,1)S(1)}, bf16[128,1024]{1,0:T(8,128)(2,1)}, u32[]{:S(2)}) copy-start(bf16[128,1024]{1,0:T(8,128)(2,1)} %get-tuple-element.54.refs_0_) | copy-start | bytes 786436
  48.2 24.0 %collective-permute-start.18 = (bf16[256,1024]{1,0:T(8,128)(2,1)}, bf16[256,1024]{1,0:T(8,128)(2,1)}, u32[]{:S(2)}, u32[]{:S(2)}) collective-permute-start(bf16[256,1024]{1,0:T(8,128)(2,1)} %stack.3), channel_id=1, source_target_pairs={{0,4},{4,0},{8,12},{12,8},{1,5},{5,1},{9,13},{13,9},{2,6},{6,2},{1... | collective-permute-start | bytes 1572872 | tf_op jit(solution)/shard_map/ppermute | solution.py:25
  48.3 8.6 %copy-start.16 = (bf16[128,1024]{1,0:T(8,128)(2,1)}, bf16[128,1024]{1,0:T(8,128)(2,1)S(1)}, u32[]{:S(2)}) copy-start(bf16[128,1024]{1,0:T(8,128)(2,1)S(1)} %collective-permute-done.20.refs_1_.refs_2_) | copy-start | bytes 786436
  48.3 8.6 %copy-start.7 = (bf16[256,1024]{1,0:T(8,128)(2,1)}, bf16[256,1024]{1,0:T(8,128)(2,1)S(1)}, u32[]{:S(2)}) copy-start(bf16[256,1024]{1,0:T(8,128)(2,1)S(1)} %collective-permute-done.15.refs_0_.refs_1_) | copy-start | bytes 1572868
  48.3 26.8 %collective-permute-start.23 = (bf16[256,1024]{1,0:T(8,128)(2,1)}, bf16[256,1024]{1,0:T(8,128)(2,1)S(1)}, u32[]{:S(2)}, u32[]{:S(2)}) collective-permute-start(bf16[256,1024]{1,0:T(8,128)(2,1)} %after.19), channel_id=1, source_target_pairs={{0,8},{4,12},{8,0},{12,4},{1,9},{5,13},{9,1},{13,5},{2,10},{6,14},... | collective-permute-start | bytes 1572872 | tf_op jit(solution)/shard_map/ppermute | solution.py:21
  48.4 31.4 %collective-permute-start.14 = (bf16[2048,256]{1,0:T(8,128)(2,1)}, bf16[2048,256]{1,0:T(8,128)(2,1)}, u32[]{:S(2)}, u32[]{:S(2)}) collective-permute-start(bf16[2048,256]{1,0:T(8,128)(2,1)} %fetched_weights.1.refs_6_.refs_2_.refs_3_), channel_id=1, source_target_pairs={{0,2},{2,0},{1,3},{3,1},{4,6},{6,4},{5,7},{7,5},{8,10},{10,8},{9,1... | collective-permute-start | bytes 3145736 | tf_op jit(solution)/shard_map/ppermute | solution.py:21
  49.9 14.7 %collective-permute-start.19 = (bf16[128,1024]{1,0:T(8,128)(2,1)S(1)}, bf16[128,1024]{1,0:T(8,128)(2,1)}, u32[]{:S(2)}, u32[]{:S(2)}) collective-permute-start(bf16[128,1024]{1,0:T(8,128)(2,1)S(1)} %copy-done.13), channel_id=1, source_target_pairs={{0,1},{1,0},{2,3},{3,2},{4,5},{5,4},{6,7},{7,6},{8,9},{9,8},{10,11... | collective-permute-start | bytes 786440 | tf_op jit(solution)/shard_map/ppermute | solution.py:21
  58.4 6.1 %copy-start = (f32[2048,256]{1,0:T(8,128)S(1)}, f32[2048,256]{1,0:T(8,128)}, u32[]{:S(2)}) copy-start(f32[2048,256]{1,0:T(8,128)} %partial_weights.1.rest_0_.refs_2_.refs_1_.refs_0_) | copy-start | bytes 6291460
  58.4 6.1 %copy-start.15 = (bf16[128,1024]{1,0:T(8,128)(2,1)S(1)}, bf16[128,1024]{1,0:T(8,128)(2,1)}, u32[]{:S(2)}) copy-start(bf16[128,1024]{1,0:T(8,128)(2,1)} %copy-done.14) | copy-start | bytes 786436
  58.4 8.0 %collective-permute-start.16 = (s32[8,128]{1,0:T(8,128)}, s32[8,128]{1,0:T(8,128)S(1)}, u32[]{:S(2)}, u32[]{:S(2)}) collective-permute-start(s32[8,128]{1,0:T(8,128)} %get-tuple-element.51), channel_id=1, source_target_pairs={{0,16},{16,0},{1,17},{17,1},{2,18},{18,2},{3,19},{19,3},{4,20},{20... | collective-permute-start | bytes 12296 | tf_op jit(solution)/shard_map/ppermute | solution.py:21
  60.0 4.6 %copy-start.17 = (bf16[128,1024]{1,0:T(8,128)(2,1)S(1)}, bf16[128,1024]{1,0:T(8,128)(2,1)}, u32[]{:S(2)}) copy-start(bf16[128,1024]{1,0:T(8,128)(2,1)} %copy-done.16) | copy-start | bytes 786436
  74.5 1.8 %collective-permute-start.21 = (s32[8,128]{1,0:T(8,128)S(1)}, s32[8,128]{1,0:T(8,128)S(1)}, u32[]{:S(2)}, u32[]{:S(2)}) collective-permute-start(s32[8,128]{1,0:T(8,128)S(1)} %after.17), channel_id=1, source_target_pairs={{0,1},{1,0},{2,3},{3,2},{4,5},{5,4},{6,7},{7,6},{8,9},{9,8},{10,11... | collective-permute-start | bytes 12296 | tf_op jit(solution)/shard_map/ppermute | solution.py:21
  74.5 5.3 %collective-permute-start.25 = (bf16[256,1024]{1,0:T(8,128)(2,1)}, bf16[256,1024]{1,0:T(8,128)(2,1)S(1)}, u32[]{:S(2)}, u32[]{:S(2)}) collective-permute-start(bf16[256,1024]{1,0:T(8,128)(2,1)} %after.21.refs_9_), channel_id=1, source_target_pairs={{0,1},{1,0},{2,3},{3,2},{4,5},{5,4},{6,7},{7,6},{8,9},{9,8},{10,11... | collective-permute-start | bytes 1572872 | tf_op jit(solution)/shard_map/ppermute | solution.py:21
  75.5 6.4 %copy-start.3 = (bf16[256,2048]{1,0:T(8,128)(2,1)S(1)}, bf16[256,2048]{1,0:T(8,128)(2,1)}, u32[]{:S(2)}) copy-start(bf16[256,2048]{1,0:T(8,128)(2,1)} %own_rows.1.refs_2_) | copy-start | bytes 3145732
  75.5 6.4 %copy-start.6 = (bf16[256,1024]{1,0:T(8,128)(2,1)S(1)}, bf16[256,1024]{1,0:T(8,128)(2,1)}, u32[]{:S(2)}) copy-start(bf16[256,1024]{1,0:T(8,128)(2,1)} %copy-done.4) | copy-start | bytes 1572868
  75.5 6.4 %copy-start.24 = (s32[4,4]{1,0:T(4,128)S(1)}, s32[4,4]{1,0:T(4,128)}, u32[]{:S(2)}) copy-start(s32[4,4]{1,0:T(4,128)} %get-tuple-element.48.table_ref) | copy-start | bytes 196
  76.4 4.1 %collective-permute-start.24 = (bf16[256,1024]{1,0:T(8,128)(2,1)S(1)}, bf16[256,1024]{1,0:T(8,128)(2,1)S(1)}, u32[]{:S(2)}, u32[]{:S(2)}) collective-permute-start(bf16[256,1024]{1,0:T(8,128)(2,1)S(1)} %after.20.refs_5_), channel_id=1, source_target_pairs={{0,1},{1,0},{2,3},{3,2},{4,5},{5,4},{6,7},{7,6},{8,9},{9,8},{10,11... | collective-permute-start | bytes 1572872 | tf_op jit(solution)/shard_map/ppermute | solution.py:21
  76.6 5.3 %collective-permute-start.22 = (bf16[256,1024]{1,0:T(8,128)(2,1)S(1)}, bf16[256,1024]{1,0:T(8,128)(2,1)S(1)}, u32[]{:S(2)}, u32[]{:S(2)}) collective-permute-start(bf16[256,1024]{1,0:T(8,128)(2,1)S(1)} %after.18.refs_3_), channel_id=1, source_target_pairs={{0,1},{1,0},{2,3},{3,2},{4,5},{5,4},{6,7},{7,6},{8,9},{9,8},{10,11... | collective-permute-start | bytes 1572872 | tf_op jit(solution)/shard_map/ppermute | solution.py:21
  76.9 11.4 %collective-permute-start.33 = (bf16[64,1024]{1,0:T(8,128)(2,1)S(1)}, bf16[64,1024]{1,0:T(8,128)(2,1)S(1)}, u32[]{:S(2)}, u32[]{:S(2)}) collective-permute-start(bf16[64,1024]{1,0:T(8,128)(2,1)S(1)} %after.28), channel_id=1, source_target_pairs={{0,12},{4,0},{8,4},{12,8},{1,13},{5,1},{9,5},{13,9},{2,14},{6,2},{... | collective-permute-start | bytes 393224 | tf_op jit(solution)/shard_map/ppermute | solution.py:21
  79.8 8.5 %collective-permute-start.31 = (bf16[64,1024]{1,0:T(8,128)(2,1)S(1)}, bf16[64,1024]{1,0:T(8,128)(2,1)S(1)}, u32[]{:S(2)}, u32[]{:S(2)}) collective-permute-start(bf16[64,1024]{1,0:T(8,128)(2,1)S(1)} %after.26), channel_id=1, source_target_pairs={{0,12},{4,0},{8,4},{12,8},{1,13},{5,1},{9,5},{13,9},{2,14},{6,2},{... | collective-permute-start | bytes 393224 | tf_op jit(solution)/shard_map/ppermute | solution.py:21
  79.8 9.4 %collective-permute-start.29 = (bf16[64,1024]{1,0:T(8,128)(2,1)S(1)}, bf16[64,1024]{1,0:T(8,128)(2,1)S(1)}, u32[]{:S(2)}, u32[]{:S(2)}) collective-permute-start(bf16[64,1024]{1,0:T(8,128)(2,1)S(1)} %after.24), channel_id=1, source_target_pairs={{0,12},{4,0},{8,4},{12,8},{1,13},{5,1},{9,5},{13,9},{2,14},{6,2},{... | collective-permute-start | bytes 393224 | tf_op jit(solution)/shard_map/ppermute | solution.py:21
  80.5 10.9 %collective-permute-start.27 = (bf16[64,1024]{1,0:T(8,128)(2,1)S(1)}, bf16[64,1024]{1,0:T(8,128)(2,1)S(1)}, u32[]{:S(2)}, u32[]{:S(2)}) collective-permute-start(bf16[64,1024]{1,0:T(8,128)(2,1)S(1)} %after.22), channel_id=1, source_target_pairs={{0,12},{4,0},{8,4},{12,8},{1,13},{5,1},{9,5},{13,9},{2,14},{6,2},{... | collective-permute-start | bytes 393224 | tf_op jit(solution)/shard_map/ppermute | solution.py:21
  86.8 11.0 %collective-permute-start.26 = (bf16[1024,128]{1,0:T(8,128)(2,1)S(1)}, bf16[1024,128]{1,0:T(8,128)(2,1)S(1)}, u32[]{:S(2)}, u32[]{:S(2)}) collective-permute-start(bf16[1024,128]{1,0:T(8,128)(2,1)S(1)} %get-tuple-element.61.refs_1_), channel_id=1, source_target_pairs={{0,2},{2,0},{1,3},{3,1},{4,6},{6,4},{5,7},{7,5},{8,10},{10,8},{9,1... | collective-permute-start | bytes 786440 | tf_op jit(solution)/shard_map/ppermute | solution.py:21
  88.3 3.0 %collective-permute-start.34 = (bf16[64,1024]{1,0:T(8,128)(2,1)S(1)}, bf16[64,1024]{1,0:T(8,128)(2,1)S(1)}, u32[]{:S(2)}, u32[]{:S(2)}) collective-permute-start(bf16[64,1024]{1,0:T(8,128)(2,1)S(1)} %after.29.refs_6_), channel_id=1, source_target_pairs={{0,1},{1,0},{2,3},{3,2},{4,5},{5,4},{6,7},{7,6},{8,9},{9,8},{10,11... | collective-permute-start | bytes 393224 | tf_op jit(solution)/shard_map/ppermute | solution.py:21
  88.3 3.0 %collective-permute-start.32 = (bf16[64,1024]{1,0:T(8,128)(2,1)S(1)}, bf16[64,1024]{1,0:T(8,128)(2,1)S(1)}, u32[]{:S(2)}, u32[]{:S(2)}) collective-permute-start(bf16[64,1024]{1,0:T(8,128)(2,1)S(1)} %after.27.refs_4_), channel_id=1, source_target_pairs={{0,1},{1,0},{2,3},{3,2},{4,5},{5,4},{6,7},{7,6},{8,9},{9,8},{10,11... | collective-permute-start | bytes 393224 | tf_op jit(solution)/shard_map/ppermute | solution.py:21
  89.3 2.1 %collective-permute-start.30 = (bf16[64,1024]{1,0:T(8,128)(2,1)S(1)}, bf16[64,1024]{1,0:T(8,128)(2,1)S(1)}, u32[]{:S(2)}, u32[]{:S(2)}) collective-permute-start(bf16[64,1024]{1,0:T(8,128)(2,1)S(1)} %after.25.refs_2_), channel_id=1, source_target_pairs={{0,1},{1,0},{2,3},{3,2},{4,5},{5,4},{6,7},{7,6},{8,9},{9,8},{10,11... | collective-permute-start | bytes 393224 | tf_op jit(solution)/shard_map/ppermute | solution.py:21
  91.4 1.3 %collective-permute-start.28 = (bf16[64,1024]{1,0:T(8,128)(2,1)S(1)}, bf16[64,1024]{1,0:T(8,128)(2,1)S(1)}, u32[]{:S(2)}, u32[]{:S(2)}) collective-permute-start(bf16[64,1024]{1,0:T(8,128)(2,1)S(1)} %after.23.refs_0_), channel_id=1, source_target_pairs={{0,1},{1,0},{2,3},{3,2},{4,5},{5,4},{6,7},{7,6},{8,9},{9,8},{10,11... | collective-permute-start | bytes 393224 | tf_op jit(solution)/shard_map/ppermute | solution.py:21
  93.5 4.3 %collective-permute-start.35 = (bf16[256,128]{1,0:T(8,128)(2,1)S(1)}, bf16[256,128]{1,0:T(8,128)(2,1)S(1)}, u32[]{:S(2)}, u32[]{:S(2)}) collective-permute-start(bf16[256,128]{1,0:T(8,128)(2,1)S(1)} %get-tuple-element.69), channel_id=1, source_target_pairs={{0,2},{2,0},{1,3},{3,1},{4,6},{6,4},{5,7},{7,5},{8,10},{10,8},{9,1... | collective-permute-start | bytes 196616 | tf_op jit(solution)/shard_map/ppermute | solution.py:21
  (12 other events, 18.5 us)

commit v12 on v11

--- a/solution.py
+++ b/solution.py
@@ -15,6 +15,7 @@
 MIDDLE = pltpu.CompilerParams(vmem_limit_bytes=48 * 2**20)
 FIRST = pltpu.CompilerParams(vmem_limit_bytes=60 * 2**20)
 LANES = 128
+CUTS = 8
 
 
 def shift(x, axis, size, by):
@@ -47,6 +48,20 @@
         compiler_params=PARAMS,
         name="after",
     )(x, *others)
+
+
+def unwritten(shape, n):
+    def kernel(*refs):
+        pass
+
+    return pl.pallas_call(
+        kernel,
+        out_specs=[ANY] * n,
+        out_shape=[jax.ShapeDtypeStruct(shape, BF16)] * n,
+        cost_estimate=cost(0, 0),
+        compiler_params=PARAMS,
+        name="unwritten",
+    )()
 
 
 def stack(parts, *others):
@@ -112,7 +127,7 @@
     half = total // n_rep
 
     def kernel(pattern_ref, slot_ref, *refs):
-        outs, rows_ref = refs[-1 - 2 * n_rep:-1], refs[-1]
+        outs, rows_ref = refs[-1 - CUTS * n_rep:-1], refs[-1]
         me, group = lax.axis_index("shard"), lax.axis_index("groups")
         for k in range(n_list):
             owner = lax.div(slot_ref[pattern_ref[me, k]], jnp.int32(local_blocks))
@@ -132,14 +147,14 @@
             @pl.when(lax.axis_index("rep") == r)
             def _():
                 for j, out in enumerate(outs):
-                    at, first = ((r + j // 2) % n_rep) * half, (j % 2) * (width // 2)
-                    out[...] = rows_ref[at:at + half, first:first + width // 2].T
+                    at, first = ((r + j // CUTS) % n_rep) * half, (j % CUTS) * (width // CUTS)
+                    out[...] = rows_ref[at:at + half, first:first + width // CUTS].T
 
     return pl.pallas_call(
         kernel,
         in_specs=[SMEM, SMEM] + [VMEM] * (n_group * n_cluster) + [ANY] * len(others),
-        out_specs=[VMEM] * (2 * n_rep),
-        out_shape=[jax.ShapeDtypeStruct((width // 2, half), BF16)] * (2 * n_rep),
+        out_specs=[VMEM] * (CUTS * n_rep),
+        out_shape=[jax.ShapeDtypeStruct((width // CUTS, half), BF16)] * (CUTS * n_rep),
         scratch_shapes=[pltpu.VMEM((total, width), BF16)],
         cost_estimate=cost(0, 4 * total * width),
         compiler_params=PARAMS,
@@ -242,7 +257,7 @@
     def kernel(block_ref, *refs):
         value = None
         for j in range(n):
-            part = dot(refs[j][...], jnp.concatenate([refs[n + 2 * j][...], refs[n + 2 * j + 1][...]]))
+            part = dot(refs[j][...], jnp.concatenate([r[...] for r in refs[n + CUTS * j:n + CUTS * (j + 1)]]))
             value = part if value is None else value + part
         refs[-1][...] = value.astype(dtype)
 
@@ -252,7 +267,7 @@
             num_scalar_prefetch=1,
             grid=(steps,),
             in_specs=[pl.BlockSpec((tile, width), lambda i, b: (b[0] * steps + i, 0))] * n
-            + [pl.BlockSpec((width // 2, total), lambda i, b: (0, 0))] * (2 * n)
+            + [pl.BlockSpec((width // CUTS, total), lambda i, b: (0, 0))] * (CUTS * n)
             + [ANY] * len(others),
             out_specs=pl.BlockSpec((tile, total), lambda i, b: (i, 0)),
         ),
@@ -303,7 +318,7 @@
     n = len(matrices)
 
     def kernel(*refs):
-        parts = [jnp.concatenate([refs[n + 2 * j][...], refs[n + 2 * j + 1][...]]) for j in range(n)]
+        parts = [jnp.concatenate([r[...] for r in refs[n + CUTS * j:n + CUTS * (j + 1)]]) for j in range(n)]
         for at in range(0, depth, tile):
             value = None
             for j in range(n):
@@ -313,7 +328,7 @@
 
     return pl.pallas_call(
         kernel,
-        in_specs=[VMEM] * (3 * n),
+        in_specs=[VMEM] * ((1 + CUTS) * n),
         out_specs=VMEM,
         out_shape=jax.ShapeDtypeStruct((depth, total), dtype),
         cost_estimate=cost(2 * n * matrices[0].size * total, 2 * n * matrices[0].size),
@@ -574,14 +589,17 @@
     urgent = [here[0]]
     if extra:
         far = swap(after(packed[-2], *pieces[1:]), "shard", n_shard, 2)
-        far_all = with_rep(far)
-        urgent += far_all[1:]
+        urgent.append(far)
     depth = n_rep * columns
     targets = [(feat + d) % n_feat for d in range(1, n_feat)]
     near_chip = fetch(matrices, targets[0], depth, *pieces[1:])
 
-    chosen = join_queries(parts, block_slot, pattern, query_store.shape[0], n_feat, n_rep, *near_chip)
-    queries = [*chosen[:2]] + [shift(chosen[j], "rep", n_rep, j // 2) for j in range(2, 2 * n_rep)]
+    mine = own_rows(goal, train, bulk, *pieces[1:])
+    table, flag = row_table(ids, lines, bulk, extra, *pieces[1:])
+    chosen = join_queries(
+        parts, block_slot, pattern, query_store.shape[0], n_feat, n_rep, *near_chip, mine, flag
+    )
+    queries = [*chosen[:CUTS]] + [shift(chosen[j], "rep", n_rep, j // CUTS) for j in range(CUTS, CUTS * n_rep)]
 
     sends = [fetched_weights(near_chip, queries, BF16)]
     sends += [partial_weights(matrices, queries, f, depth, BF16) for f in targets[1:]]
@@ -595,9 +613,7 @@
         shift(after(packed[len(middle) + j], here[-1], own), "shard", n_shard, last_hops) for j in range(len(final))
     ]
 
-    mine = own_rows(goal, train, bulk, own)
-    table, flag = row_table(ids, lines, bulk, extra, own)
-    marks = [own, mine]
+    marks = [own]
     if extra:
         for d in range(1, n_group):
             flag = jnp.maximum(flag, shift(flag, "groups", n_group, d))
@@ -607,11 +623,12 @@
             return [with_rep(pair), with_rep(swap(pair, "shard", n_shard, 1))]
 
         def no_round(x):
-            return [[jnp.zeros((2 * extra, columns), BF16)] * n_rep] * 2
-
-        seconds = lax.cond(flag[0, 0] > 0, second_round, no_round, packed[-1])
+            empty = unwritten((2 * extra, columns), 2 * n_rep)
+            return [[*empty[:n_rep]], [*empty[n_rep:]]]
+
+        seconds = lax.cond(flag[0, 0] > 0, second_round, no_round, after(packed[-1], own))
         near = swap(stack([packed[-3], far], *sends), "shard", n_shard, 1)
-        pairs = [stack([x, y], own) for x, y in zip(with_rep(packed[-3]), far_all)]
+        pairs = [stack([x, y], own) for x, y in zip(with_rep(packed[-3]), with_rep(after(far, own)))]
         firsts = [pairs, with_rep(after(near, own))]
         marks += [seconds[0][0], near, *pairs]
 

time: 100 us -> 105 us (1.050)
  waiting for transfers between devices: 16.8 us -> 22.5 us
  Pallas kernels: 41 us -> 39.9 us
    ppermute x30 -> x36, waiting for transfers between devices: 8.59 us -> 17.2 us  [shift(): return lax.ppermute(x, axis, [(i, (i + by) % size) for i in range(size)])]
    unnamed x56 -> x94, local copies, waits for them, and re-layouts: 6.79 us -> 10.8 us
    another operation x4 -> x0, local copies, waits for them, and re-layouts: 3.42 us -> none
    ppermute x2, waiting for transfers between devices: 8.2 us -> 5.27 us  [swap(): return lax.ppermute(x, axis, [(i, i ^ bit) for i in range(size)])]
    ppermute x30 -> x36, starting transfers between devices: 27.6 us -> 28 us  [shift(): return lax.ppermute(x, axis, [(i, (i + by) % size) for i in range(size)])]
    pallas_call x1 -> x2, Pallas kernels: 3.34 us -> 3.3 us  [the longest x1 3.3 us: fetched_weights(): pl.pallas_call(kernel, in_specs=[VMEM] * ((1 + CUTS) * n), out_specs=VMEM...]
  transfers between devices with their start and end apart: 32 -> 38, of which waited for: 8 -> 14; matrix products, arithmetic and copies ran while one was open for 4% -> 0% of each run, Pallas kernels for 40% -> 36%
where the time goes in v12:
time: 105 us
  Pallas kernels  39.9 us (38%)
  starting transfers between devices  29.7 us (28%)
  waiting for transfers between devices  22.5 us (21%)
  local copies, waits for them, and re-layouts  11.4 us (11%)
  between operations  1.29 us (1%)
    ppermute x36, starting transfers between devices, shift(): return lax.ppermute(x, axis, [(i, (i + by) % size) for i in range(size)])  28 us
    ppermute x36, waiting for transfers between devices, shift(): return lax.ppermute(x, axis, [(i, (i + by) % size) for i in range(size)])  17.2 us
    unnamed x94, local copies, waits for them, and re-layouts  10.8 us
    pallas_call x1, Pallas kernels, partial_weights(): pl.pallas_call(kernel, grid_spec=pltpu.PrefetchScalarGridSpec(num_scalar_...  6.76 us
    pallas_call x1, Pallas kernels, pack_rows(): pl.pallas_call(kernel, grid=(1,), in_specs=[pl.BlockSpec((lines, LANES),...  6.22 us
    pallas_call x1, Pallas kernels, fetch(): pl.pallas_call(kernel, in_specs=[SMEM] + [ANY] * (n + len(others)), out_s...  5.64 us
    ppermute x2, waiting for transfers between devices, swap(): return lax.ppermute(x, axis, [(i, i ^ bit) for i in range(size)])  5.27 us
    pallas_call x1, Pallas kernels, early_scores(): pl.pallas_call(kernel, in_specs=[SMEM] + [VMEM] * (2 + n_other + n_rep *...  4.71 us
  transfers between devices with their start and end apart: 38, of which 14 were waited for; matrix products, arithmetic and copies ran while one was open for 0% of the time, Pallas kernels for 36%

profile of v12, /device:TPU:0, one launch (start us, length us, event | category | flops | bytes accessed | tf_op | source)
XLA Modules:
  0.0 104.8 jit_solution(16455586569495874229)
XLA Ops:
  0.5 2.7 %pick_queries.1 = (bf16[1,64,1024]{2,1,0:T(8,128)(2,1)}, bf16[1,64,1024]{2,1,0:T(8,128)(2,1)}, bf16[1,64,1024]{2,1,0:T(8,128)(2,1)}, bf16[1,64,1024]{2,1,0:T(8,128)(2,1)}) custom-call(s32[4,4]{1,0:T(4,128)} %pattern_ref.3, s32[16]{0:T(128)} %slot_ref.3, bf16[4,128,1024]{2,1,0:T(8,128)(2,1)} %in_ref.1), custom_call_target="tpu_custom_call" | custom-call | flops 1 | bytes 1 | tf_op jit(solution)/shard_map/pick_queries/pallas_call | solution.py:108
  3.1 2.6 %collective-permute-start.4 = (bf16[1,64,1024]{2,1,0:T(8,128)(2,1)}, bf16[1,64,1024]{2,1,0:T(8,128)(2,1)S(1)}, u32[]{:S(2)}, u32[]{:S(2)}) collective-permute-start(bf16[1,64,1024]{2,1,0:T(8,128)(2,1)} %get-tuple-element.50), channel_id=1, source_target_pairs={{0,4},{4,8},{8,12},{12,0},{1,5},{5,9},{9,13},{13,1},{2,6},{6,10},{... | collective-permute-start | bytes 393224 | tf_op jit(solution)/shard_map/ppermute | solution.py:22
  5.8 2.6 %collective-permute-start.5 = (bf16[1,64,1024]{2,1,0:T(8,128)(2,1)}, bf16[1,64,1024]{2,1,0:T(8,128)(2,1)S(1)}, u32[]{:S(2)}, u32[]{:S(2)}) collective-permute-start(bf16[1,64,1024]{2,1,0:T(8,128)(2,1)} %get-tuple-element.51), channel_id=1, source_target_pairs={{0,8},{4,12},{8,0},{12,4},{1,9},{5,13},{9,1},{13,5},{2,10},{6,14},... | collective-permute-start | bytes 393224 | tf_op jit(solution)/shard_map/ppermute | solution.py:22
  8.4 1.3 %collective-permute-start.6 = (bf16[1,64,1024]{2,1,0:T(8,128)(2,1)}, bf16[1,64,1024]{2,1,0:T(8,128)(2,1)S(1)}, u32[]{:S(2)}, u32[]{:S(2)}) collective-permute-start(bf16[1,64,1024]{2,1,0:T(8,128)(2,1)} %get-tuple-element.52), channel_id=1, source_target_pairs={{0,12},{4,0},{8,4},{12,8},{1,13},{5,1},{9,5},{13,9},{2,14},{6,2},{... | collective-permute-start | bytes 393224 | tf_op jit(solution)/shard_map/ppermute | solution.py:22
  9.7 1.5 %collective-permute-start.8 = (bf16[1,64,1024]{2,1,0:T(8,128)(2,1)}, bf16[1,64,1024]{2,1,0:T(8,128)(2,1)S(1)}, u32[]{:S(2)}, u32[]{:S(2)}) collective-permute-start(bf16[1,64,1024]{2,1,0:T(8,128)(2,1)} %get-tuple-element.54.refs_0_), channel_id=1, source_target_pairs={{0,16},{16,0},{1,17},{17,1},{2,18},{18,2},{3,19},{19,3},{4,20},{20... | collective-permute-start | bytes 393224 | tf_op jit(solution)/shard_map/ppermute | solution.py:22
  11.2 6.2 %pack_rows.1 = (bf16[256,1024]{1,0:T(8,128)(2,1)}, bf16[256,1024]{1,0:T(8,128)(2,1)}, bf16[64,1024]{1,0:T(8,128)(2,1)}, bf16[64,1024]{1,0:T(8,128)(2,1)}, bf16[6...) custom-call(s32[32,128]{1,0:T(8,128)} %bitcast.9, ...), custom_call_target="tpu_custom_call" | custom-call | flops 1 | bytes 1 | tf_op jit(solution)/shard_map/pack_rows/pallas_call | solution.py:236
  17.9 1.1 %copy-done.13 = bf16[256,1024]{1,0:T(8,128)(2,1)S(1)} copy-done((bf16[256,1024]{1,0:T(8,128)(2,1)S(1)}, bf16[256,1024]{1,0:T(8,128)(2,1)}, u32[]{:S(2)}) %copy-start.13) | copy-done | bytes 524312
  19.0 0.8 copy-done.14
  19.8 3.3 %collective-permute-start.21 = (bf16[256,1024]{1,0:T(8,128)(2,1)}, bf16[256,1024]{1,0:T(8,128)(2,1)S(1)}, u32[]{:S(2)}, u32[]{:S(2)}) collective-permute-start(bf16[256,1024]{1,0:T(8,128)(2,1)} %copy-done.14), channel_id=1, source_target_pairs={{0,4},{4,8},{8,12},{12,0},{1,5},{5,9},{9,13},{13,1},{2,6},{6,10},{... | collective-permute-start | bytes 1572872 | tf_op jit(solution)/shard_map/ppermute | solution.py:22
  23.1 1.5 %collective-permute-start.9 = (bf16[1,64,1024]{2,1,0:T(8,128)(2,1)S(1)}, bf16[1,64,1024]{2,1,0:T(8,128)(2,1)S(1)}, u32[]{:S(2)}, u32[]{:S(2)}) collective-permute-start(bf16[1,64,1024]{2,1,0:T(8,128)(2,1)S(1)} %collective-permute-done.4.rest_0_.refs_2_.refs_1_), channel_id=1, source_target_pairs={{0,16},{16,0},{1,17},{17,1},{2,18},{18,2},{3,19},{19,3},{4,20},{20... | collective-permute-start | bytes 393224 | tf_op jit(solution)/shard_map/ppermute | solution.py:22
  25.1 1.5 %collective-permute-start.11 = (bf16[1,64,1024]{2,1,0:T(8,128)(2,1)S(1)}, bf16[1,64,1024]{2,1,0:T(8,128)(2,1)S(1)}, u32[]{:S(2)}, u32[]{:S(2)}) collective-permute-start(bf16[1,64,1024]{2,1,0:T(8,128)(2,1)S(1)} %collective-permute-done.6.rest_2_.refs_4_.refs_3_), channel_id=1, source_target_pairs={{0,16},{16,0},{1,17},{17,1},{2,18},{18,2},{3,19},{19,3},{4,20},{20... | collective-permute-start | bytes 393224 | tf_op jit(solution)/shard_map/ppermute | solution.py:22
  26.6 0.9 copy-done.31
  27.6 0.7 copy-done.32
  28.3 1.7 %collective-permute-start.23 = (bf16[128,1024]{1,0:T(8,128)(2,1)}, bf16[128,1024]{1,0:T(8,128)(2,1)S(1)}, u32[]{:S(2)}, u32[]{:S(2)}) collective-permute-start(bf16[128,1024]{1,0:T(8,128)(2,1)} %copy-done.32), channel_id=1, source_target_pairs={{0,8},{4,12},{8,0},{12,4},{1,9},{5,13},{9,1},{13,5},{2,10},{6,14},... | collective-permute-start | bytes 786440 | tf_op jit(solution)/shard_map/ppermute | solution.py:26
  29.9 1.5 %row_table.1 = (s32[4,4]{1,0:T(4,128)}, s32[8,128]{1,0:T(8,128)}) custom-call(s32[32,128]{1,0:T(8,128)} %bitcast.10, bf16[1,64,1024]{2,1,0:T(8,128)(2,1)} %copy-done.5, bf16[1,64,1024]{2,1,0:T(8,128)(2,1)} %copy-done.7, bf16[1,64,1024]{2,1,0:T(8,128)(2,1)} %copy-done.9), custom_call_target="tpu_custom_call" | custom-call | flops 1 | bytes 1 | tf_op jit(solution)/shard_map/row_table/pallas_call | solution.py:370
  31.5 4.5 %own_rows.1.refs_10_.refs_2_ = bf16[256,2048]{1,0:T(8,128)(2,1)} custom-call(s32[8,128]{1,0:T(8,128)} %get-tuple-element.57.goal_ref, bf16[1024,2048]{1,0:T(8,128)(2,1)} %train_ref.3, bf16[1,64,1024]{2,1,0:T(8,128)(2,1)} %copy-done.5, bf16[1,64,1024]{2,1,0:T(8,128)(2,1)} %copy-done.7, bf16[1,64,1024]{2,1,0:T(8,128)(2,1)} %copy-done.9), custom_call_target="tpu_custom_call" | custom-call | flops 1 | bytes 1 | tf_op jit(solution)/shard_map/own_rows/pallas_call | solution.py:179
  36.1 5.6 %fetch.1 = (bf16[2048,1024]{1,0:T(8,128)(2,1)S(1)}, bf16[2048,1024]{1,0:T(8,128)(2,1)}) custom-call(s32[1]{0:T(128)} %bitcast.3.block_ref, bf16[4096,1024]{1,0:T(8,128)(2,1)} %bitcast.7, bf16[4096,1024]{1,0:T(8,128)(2,1)} %collective-permute-done.7.refs_1_, bf16[1,64,1024]{2,1,0:T(8,128)(2,1)S(1)} %copy-done.6, bf16[1,64,1024]{2,1,0:T(8,128)(2,1)S(1)} %copy-done.8, ...), custom_call_target="tpu_custom_call" | custom-call | flops 1 | bytes 1 | tf_op jit(solution)/shard_map/fetch/pallas_call | solution.py:302
  41.8 2.2 %copy-done.2 = bf16[2048,1024]{1,0:T(8,128)(2,1)S(1)} copy-done((bf16[2048,1024]{1,0:T(8,128)(2,1)S(1)}, bf16[2048,1024]{1,0:T(8,128)(2,1)}, u32[]{:S(2)}) %copy-start.2) | copy-done | bytes 4194328
  44.0 1.2 %join_queries.1 = (bf16[128,256]{1,0:T(8,128)(2,1)S(1)}, bf16[128,256]{1,0:T(8,128)(2,1)S(1)}, bf16[128,256]{1,0:T(8,128)(2,1)S(1)}, bf16[128,256]{1,0:T(8,128)(...) custom-call(s32[4,4]{1,0:T(4,128)S(1)} %copy-done.39, ...), custom_call_target="tpu_custom_call" | custom-call | flops 1 | bytes 1 | tf_op jit(solution)/shard_map/join_queries/pallas_call | solution.py:153
  46.0 0.7 collective-permute-done.12.refs_10_
  47.3 0.6 collective-permute-done.15.refs_13_
  48.4 0.7 collective-permute-done.18.refs_16_
  49.3 3.3 %fetched_weights.1.refs_18_.refs_2_.refs_3_ = bf16[2048,256]{1,0:T(8,128)(2,1)} custom-call(bf16[2048,1024]{1,0:T(8,128)(2,1)S(1)} %get-tuple-element.55.refs_8_.refs_0_, bf16[2048,1024]{1,0:T(8,128)(2,1)S(1)} %copy-done.2, bf16[128,256]{1,0:T(8,128)(2,1)S(1)} %get-tuple-element.59.refs_2_, bf16[128,256]{1,0:T(8,128)(2,1)S(1)} %get-tuple-element.60.refs_3_, ...), custom_call_target="tpu_custom_call" | custom-call | flops 1 | bytes 1 | tf_op jit(solution)/shard_map/fetched_weights/pallas_call | solution.py:329
  52.8 0.8 stack.3
  53.6 1.5 %collective-permute-start.20 = (bf16[2048,256]{1,0:T(8,128)(2,1)}, bf16[2048,256]{1,0:T(8,128)(2,1)}, u32[]{:S(2)}, u32[]{:S(2)}) collective-permute-start(bf16[2048,256]{1,0:T(8,128)(2,1)} %fetched_weights.1.refs_18_.refs_2_.refs_3_), channel_id=1, source_target_pairs={{0,2},{2,0},{1,3},{3,1},{4,6},{6,4},{5,7},{7,5},{8,10},{10,8},{9,1... | collective-permute-start | bytes 3145736 | tf_op jit(solution)/shard_map/ppermute | solution.py:22
  55.1 1.3 %collective-permute-start.29 = (bf16[256,1024]{1,0:T(8,128)(2,1)}, bf16[256,1024]{1,0:T(8,128)(2,1)S(1)}, u32[]{:S(2)}, u32[]{:S(2)}) collective-permute-start(bf16[256,1024]{1,0:T(8,128)(2,1)} %after.23), channel_id=1, source_target_pairs={{0,8},{4,12},{8,0},{12,4},{1,9},{5,13},{9,1},{13,5},{2,10},{6,14},... | collective-permute-start | bytes 1572872 | tf_op jit(solution)/shard_map/ppermute | solution.py:22
  56.9 3.1 %collective-permute-done.22 = s32[8,128]{1,0:T(8,128)S(1)} collective-permute-done((s32[8,128]{1,0:T(8,128)S(1)}, s32[8,128]{1,0:T(8,128)S(1)}, u32[]{:S(2)}, u32[]{:S(2)}) %collective-permute-start.22) | collective-permute-done | bytes 4128 | tf_op jit(solution)/shard_map/ppermute | solution.py:22
  60.0 0.5 slice.3
  61.2 6.8 %partial_weights.1.refs_1_.refs_2_.refs_0_ = f32[2048,256]{1,0:T(8,128)} custom-call(s32[1]{0:T(128)} %bitcast.1.block_ref, bf16[4096,1024]{1,0:T(8,128)(2,1)} %bitcast.8, bf16[4096,1024]{1,0:T(8,128)(2,1)} %collective-permute-done.7.refs_1_, bf16[128,256]{1,0:T(8,128)(2,1)} %copy-done.15, bf16[128,256]{1,0:T(8,128)(2,1)} %copy-done.16, ...), custom_call_target="tpu_custom_call" | custom-call | flops 1 | bytes 1 | tf_op jit(solution)/shard_map/partial_weights/pallas_call | solution.py:264
  67.9 1.6 %copy-done = f32[2048,256]{1,0:T(8,128)S(1)} copy-done((f32[2048,256]{1,0:T(8,128)S(1)}, f32[2048,256]{1,0:T(8,128)}, u32[]{:S(2)}) %copy-start) | copy-done | bytes 2097176
  69.5 1.6 %copy-done.1 = f32[2048,256]{1,0:T(8,128)S(1)} copy-done((f32[2048,256]{1,0:T(8,128)S(1)}, f32[2048,256]{1,0:T(8,128)}, u32[]{:S(2)}) %copy-start.1) | copy-done | bytes 2097176
  71.1 0.9 copy-done.12
  72.1 0.5 collective-permute-done.26.refs_1_
  72.7 5.3 %collective-permute-done.24.refs_3_.refs_0_ = bf16[256,1024]{1,0:T(8,128)(2,1)} collective-permute-done((bf16[256,1024]{1,0:T(8,128)(2,1)}, bf16[256,1024]{1,0:T(8,128)(2,1)}, u32[]{:S(2)}, u32[]{:S(2)}) %collective-permute-start.24) | collective-permute-done | bytes 524320 | tf_op jit(solution)/shard_map/ppermute | solution.py:26
  78.6 0.7 collective-permute-done.27.refs_1_
  79.4 2.0 %collective-permute-done.29.refs_0_.refs_1_ = bf16[256,1024]{1,0:T(8,128)(2,1)S(1)} collective-permute-done((bf16[256,1024]{1,0:T(8,128)(2,1)}, bf16[256,1024]{1,0:T(8,128)(2,1)S(1)}, u32[]{:S(2)}, u32[]{:S(2)}) %collective-permute-start.29) | collective-permute-done | bytes 524320 | tf_op jit(solution)/shard_map/ppermute | solution.py:22
  81.5 0.8 copy-done.34
  82.3 2.4 %collective-permute-start.33 = (bf16[64,1024]{1,0:T(8,128)(2,1)S(1)}, bf16[64,1024]{1,0:T(8,128)(2,1)S(1)}, u32[]{:S(2)}, u32[]{:S(2)}) collective-permute-start(bf16[64,1024]{1,0:T(8,128)(2,1)S(1)} %after.26), channel_id=1, source_target_pairs={{0,12},{4,0},{8,4},{12,8},{1,13},{5,1},{9,5},{13,9},{2,14},{6,2},{... | collective-permute-start | bytes 393224 | tf_op jit(solution)/shard_map/ppermute | solution.py:22
  85.1 2.2 %collective-permute-start.39 = (bf16[64,1024]{1,0:T(8,128)(2,1)S(1)}, bf16[64,1024]{1,0:T(8,128)(2,1)S(1)}, u32[]{:S(2)}, u32[]{:S(2)}) collective-permute-start(bf16[64,1024]{1,0:T(8,128)(2,1)S(1)} %after.32), channel_id=1, source_target_pairs={{0,12},{4,0},{8,4},{12,8},{1,13},{5,1},{9,5},{13,9},{2,14},{6,2},{... | collective-permute-start | bytes 393224 | tf_op jit(solution)/shard_map/ppermute | solution.py:22
  87.3 4.7 %early_scores.1 = (bf16[2048,256]{1,0:T(8,128)(2,1)S(1)}, bf16[2048,256]{1,0:T(8,128)(2,1)S(1)}, f32[1024,128]{1,0:T(8,128)S(1)}, bf16[1024,128]{1,0:T(8,128)(2,1)S(1)}) custom-call(s32[4,4]{1,0:T(4,128)S(1)} %copy-done.40, f32[2048,256]{1,0:T(8,128)S(1)} %copy-done.1, bf16[2048,256]{1,0:T(8,128)(2,1)} %collective-permute-done.20.refs_1_, ...), custom_call_target="tpu_custom_call" | custom-call | flops 1 | bytes 1 | tf_op jit(solution)/shard_map/early_scores/pallas_call | solution.py:486
  92.0 0.9 collective-permute-start.32
  93.4 0.8 collective-permute-done.37.refs_0_
  94.2 2.4 %collective-permute-done.39.refs_0_ = bf16[64,1024]{1,0:T(8,128)(2,1)S(1)} collective-permute-done((bf16[64,1024]{1,0:T(8,128)(2,1)S(1)}, bf16[64,1024]{1,0:T(8,128)(2,1)S(1)}, u32[]{:S(2)}, u32[]{:S(2)}) %collective-permute-start.39) | collective-permute-done | bytes 131104 | tf_op jit(solution)/shard_map/ppermute | solution.py:22
  96.7 1.3 %collective-permute-done.40.refs_7_ = bf16[64,1024]{1,0:T(8,128)(2,1)S(1)} collective-permute-done((bf16[64,1024]{1,0:T(8,128)(2,1)S(1)}, bf16[64,1024]{1,0:T(8,128)(2,1)S(1)}, u32[]{:S(2)}, u32[]{:S(2)}) %collective-permute-start.40) | collective-permute-done | bytes 131104 | tf_op jit(solution)/shard_map/ppermute | solution.py:22
  98.0 0.7 late_scores.1
  98.7 0.6 collective-permute-start.41
  99.3 3.7 %collective-permute-done.41.refs_3_ = bf16[256,128]{1,0:T(8,128)(2,1)S(1)} collective-permute-done((bf16[256,128]{1,0:T(8,128)(2,1)S(1)}, bf16[256,128]{1,0:T(8,128)(2,1)S(1)}, u32[]{:S(2)}, u32[]{:S(2)}) %collective-permute-start.41) | collective-permute-done | bytes 65568 | tf_op jit(solution)/shard_map/ppermute | solution.py:22
  103.1 1.7 %merge.1 = f32[128,1024]{1,0:T(8,128)} custom-call(s32[4,4]{1,0:T(4,128)S(1)} %copy-done.40, f32[1024,128]{1,0:T(8,128)S(1)} %get-tuple-element.84.refs_0_, bf16[1024,128]{1,0:T(8,128)(2,1)S(1)} %collective-permute-done.32.refs_1_, f32[256,128]{1,0:T(8,128)S(1)} %get-tuple-element.92.refs_2_, bf16[256,128]{1,0:T(8,128)(2,1)S(1)} %collective-permute-done.41.refs_3_), custom_call_target="tpu_custom_call" | custom-call | flops 1 | bytes 1 | tf_op jit(solution)/shard_map/merge/pallas_call | solution.py:548
  (158 shorter events, 5.7 us)
Async XLA Ops:
  0.0 28.3 %collective-permute-start.7 = (bf16[4096,1024]{1,0:T(8,128)(2,1)}, bf16[4096,1024]{1,0:T(8,128)(2,1)}, u32[]{:S(2)}, u32[]{:S(2)}) collective-permute-start(bf16[4096,1024]{1,0:T(8,128)(2,1)} %bitcast.6), channel_id=1, source_target_pairs={{0,1},{1,0},{2,3},{3,2},{4,5},{5,4},{6,7},{7,6},{8,9},{9,8},{10,11... | collective-permute-start | bytes 25165832 | tf_op jit(solution)/shard_map/ppermute | solution.py:22
  3.1 14.3 %collective-permute-start.4 = (bf16[1,64,1024]{2,1,0:T(8,128)(2,1)}, bf16[1,64,1024]{2,1,0:T(8,128)(2,1)S(1)}, u32[]{:S(2)}, u32[]{:S(2)}) collective-permute-start(bf16[1,64,1024]{2,1,0:T(8,128)(2,1)} %get-tuple-element.50), channel_id=1, source_target_pairs={{0,4},{4,8},{8,12},{12,0},{1,5},{5,9},{9,13},{13,1},{2,6},{6,10},{... | collective-permute-start | bytes 393224 | tf_op jit(solution)/shard_map/ppermute | solution.py:22
  5.8 12.1 %collective-permute-start.5 = (bf16[1,64,1024]{2,1,0:T(8,128)(2,1)}, bf16[1,64,1024]{2,1,0:T(8,128)(2,1)S(1)}, u32[]{:S(2)}, u32[]{:S(2)}) collective-permute-start(bf16[1,64,1024]{2,1,0:T(8,128)(2,1)} %get-tuple-element.51), channel_id=1, source_target_pairs={{0,8},{4,12},{8,0},{12,4},{1,9},{5,13},{9,1},{13,5},{2,10},{6,14},... | collective-permute-start | bytes 393224 | tf_op jit(solution)/shard_map/ppermute | solution.py:22
  8.4 9.5 %collective-permute-start.6 = (bf16[1,64,1024]{2,1,0:T(8,128)(2,1)}, bf16[1,64,1024]{2,1,0:T(8,128)(2,1)S(1)}, u32[]{:S(2)}, u32[]{:S(2)}) collective-permute-start(bf16[1,64,1024]{2,1,0:T(8,128)(2,1)} %get-tuple-element.52), channel_id=1, source_target_pairs={{0,12},{4,0},{8,4},{12,8},{1,13},{5,1},{9,5},{13,9},{2,14},{6,2},{... | collective-permute-start | bytes 393224 | tf_op jit(solution)/shard_map/ppermute | solution.py:22
  9.7 15.4 %collective-permute-start.8 = (bf16[1,64,1024]{2,1,0:T(8,128)(2,1)}, bf16[1,64,1024]{2,1,0:T(8,128)(2,1)S(1)}, u32[]{:S(2)}, u32[]{:S(2)}) collective-permute-start(bf16[1,64,1024]{2,1,0:T(8,128)(2,1)} %get-tuple-element.54.refs_0_), channel_id=1, source_target_pairs={{0,16},{16,0},{1,17},{17,1},{2,18},{18,2},{3,19},{19,3},{4,20},{20... | collective-permute-start | bytes 393224 | tf_op jit(solution)/shard_map/ppermute | solution.py:22
  17.4 12.5 %copy-start.5 = (bf16[1,64,1024]{2,1,0:T(8,128)(2,1)}, bf16[1,64,1024]{2,1,0:T(8,128)(2,1)S(1)}, u32[]{:S(2)}) copy-start(bf16[1,64,1024]{2,1,0:T(8,128)(2,1)S(1)} %collective-permute-done.4.rest_0_.refs_2_.refs_1_) | copy-start | bytes 393220
  17.9 12.1 %copy-start.7 = (bf16[1,64,1024]{2,1,0:T(8,128)(2,1)}, bf16[1,64,1024]{2,1,0:T(8,128)(2,1)S(1)}, u32[]{:S(2)}) copy-start(bf16[1,64,1024]{2,1,0:T(8,128)(2,1)S(1)} %collective-permute-done.5.rest_1_.refs_3_.refs_2_) | copy-start | bytes 393220
  17.9 12.1 %copy-start.9 = (bf16[1,64,1024]{2,1,0:T(8,128)(2,1)}, bf16[1,64,1024]{2,1,0:T(8,128)(2,1)S(1)}, u32[]{:S(2)}) copy-start(bf16[1,64,1024]{2,1,0:T(8,128)(2,1)S(1)} %collective-permute-done.6.rest_2_.refs_4_.refs_3_) | copy-start | bytes 393220
  19.8 35.3 %collective-permute-start.21 = (bf16[256,1024]{1,0:T(8,128)(2,1)}, bf16[256,1024]{1,0:T(8,128)(2,1)S(1)}, u32[]{:S(2)}, u32[]{:S(2)}) collective-permute-start(bf16[256,1024]{1,0:T(8,128)(2,1)} %copy-done.14), channel_id=1, source_target_pairs={{0,4},{4,8},{8,12},{12,0},{1,5},{5,9},{9,13},{13,1},{2,6},{6,10},{... | collective-permute-start | bytes 1572872 | tf_op jit(solution)/shard_map/ppermute | solution.py:22
  23.1 18.7 %collective-permute-start.9 = (bf16[1,64,1024]{2,1,0:T(8,128)(2,1)S(1)}, bf16[1,64,1024]{2,1,0:T(8,128)(2,1)S(1)}, u32[]{:S(2)}, u32[]{:S(2)}) collective-permute-start(bf16[1,64,1024]{2,1,0:T(8,128)(2,1)S(1)} %collective-permute-done.4.rest_0_.refs_2_.refs_1_), channel_id=1, source_target_pairs={{0,16},{16,0},{1,17},{17,1},{2,18},{18,2},{3,19},{19,3},{4,20},{20... | collective-permute-start | bytes 393224 | tf_op jit(solution)/shard_map/ppermute | solution.py:22
  24.6 17.2 %collective-permute-start.10 = (bf16[1,64,1024]{2,1,0:T(8,128)(2,1)S(1)}, bf16[1,64,1024]{2,1,0:T(8,128)(2,1)S(1)}, u32[]{:S(2)}, u32[]{:S(2)}) collective-permute-start(bf16[1,64,1024]{2,1,0:T(8,128)(2,1)S(1)} %collective-permute-done.5.rest_1_.refs_3_.refs_2_), channel_id=1, source_target_pairs={{0,16},{16,0},{1,17},{17,1},{2,18},{18,2},{3,19},{19,3},{4,20},{20... | collective-permute-start | bytes 393224 | tf_op jit(solution)/shard_map/ppermute | solution.py:22
  25.1 16.7 %collective-permute-start.11 = (bf16[1,64,1024]{2,1,0:T(8,128)(2,1)S(1)}, bf16[1,64,1024]{2,1,0:T(8,128)(2,1)S(1)}, u32[]{:S(2)}, u32[]{:S(2)}) collective-permute-start(bf16[1,64,1024]{2,1,0:T(8,128)(2,1)S(1)} %collective-permute-done.6.rest_2_.refs_4_.refs_3_), channel_id=1, source_target_pairs={{0,16},{16,0},{1,17},{17,1},{2,18},{18,2},{3,19},{19,3},{4,20},{20... | collective-permute-start | bytes 393224 | tf_op jit(solution)/shard_map/ppermute | solution.py:22
  28.3 24.5 %collective-permute-start.23 = (bf16[128,1024]{1,0:T(8,128)(2,1)}, bf16[128,1024]{1,0:T(8,128)(2,1)S(1)}, u32[]{:S(2)}, u32[]{:S(2)}) collective-permute-start(bf16[128,1024]{1,0:T(8,128)(2,1)} %copy-done.32), channel_id=1, source_target_pairs={{0,8},{4,12},{8,0},{12,4},{1,9},{5,13},{9,1},{13,5},{2,10},{6,14},... | collective-permute-start | bytes 786440 | tf_op jit(solution)/shard_map/ppermute | solution.py:26
  45.2 7.4 %copy-start.15 = (bf16[128,256]{1,0:T(8,128)(2,1)}, bf16[128,256]{1,0:T(8,128)(2,1)S(1)}, u32[]{:S(2)}) copy-start(bf16[128,256]{1,0:T(8,128)(2,1)S(1)} %get-tuple-element.59.refs_2_) | copy-start | bytes 196612
  45.2 7.4 %copy-start.16 = (bf16[128,256]{1,0:T(8,128)(2,1)}, bf16[128,256]{1,0:T(8,128)(2,1)S(1)}, u32[]{:S(2)}) copy-start(bf16[128,256]{1,0:T(8,128)(2,1)S(1)} %get-tuple-element.60.refs_3_) | copy-start | bytes 196612
  45.2 7.4 %copy-start.17 = (bf16[128,256]{1,0:T(8,128)(2,1)}, bf16[128,256]{1,0:T(8,128)(2,1)S(1)}, u32[]{:S(2)}) copy-start(bf16[128,256]{1,0:T(8,128)(2,1)S(1)} %get-tuple-element.61.refs_4_) | copy-start | bytes 196612
  45.3 7.4 %copy-start.18 = (bf16[128,256]{1,0:T(8,128)(2,1)}, bf16[128,256]{1,0:T(8,128)(2,1)S(1)}, u32[]{:S(2)}) copy-start(bf16[128,256]{1,0:T(8,128)(2,1)S(1)} %get-tuple-element.62.refs_5_) | copy-start | bytes 196612
  45.3 7.4 %copy-start.19 = (bf16[128,256]{1,0:T(8,128)(2,1)}, bf16[128,256]{1,0:T(8,128)(2,1)S(1)}, u32[]{:S(2)}) copy-start(bf16[128,256]{1,0:T(8,128)(2,1)S(1)} %get-tuple-element.63.refs_6_) | copy-start | bytes 196612
  45.3 7.4 %copy-start.20 = (bf16[128,256]{1,0:T(8,128)(2,1)}, bf16[128,256]{1,0:T(8,128)(2,1)S(1)}, u32[]{:S(2)}) copy-start(bf16[128,256]{1,0:T(8,128)(2,1)S(1)} %get-tuple-element.64.refs_7_) | copy-start | bytes 196612
  45.3 1.3 %collective-permute-start.12 = (bf16[128,256]{1,0:T(8,128)(2,1)S(1)}, bf16[128,256]{1,0:T(8,128)(2,1)S(1)}, u32[]{:S(2)}, u32[]{:S(2)}) collective-permute-start(bf16[128,256]{1,0:T(8,128)(2,1)S(1)} %get-tuple-element.67), channel_id=1, source_target_pairs={{0,1},{1,0},{2,3},{3,2},{4,5},{5,4},{6,7},{7,6},{8,9},{9,8},{10,11... | collective-permute-start | bytes 196616 | tf_op jit(solution)/shard_map/ppermute | solution.py:22
  45.4 1.4 %collective-permute-start.13 = (bf16[128,256]{1,0:T(8,128)(2,1)S(1)}, bf16[128,256]{1,0:T(8,128)(2,1)S(1)}, u32[]{:S(2)}, u32[]{:S(2)}) collective-permute-start(bf16[128,256]{1,0:T(8,128)(2,1)S(1)} %get-tuple-element.68), channel_id=1, source_target_pairs={{0,1},{1,0},{2,3},{3,2},{4,5},{5,4},{6,7},{7,6},{8,9},{9,8},{10,11... | collective-permute-start | bytes 196616 | tf_op jit(solution)/shard_map/ppermute | solution.py:22
  45.9 1.3 %collective-permute-start.14 = (bf16[128,256]{1,0:T(8,128)(2,1)S(1)}, bf16[128,256]{1,0:T(8,128)(2,1)S(1)}, u32[]{:S(2)}, u32[]{:S(2)}) collective-permute-start(bf16[128,256]{1,0:T(8,128)(2,1)S(1)} %get-tuple-element.69), channel_id=1, source_target_pairs={{0,1},{1,0},{2,3},{3,2},{4,5},{5,4},{6,7},{7,6},{8,9},{9,8},{10,11... | collective-permute-start | bytes 196616 | tf_op jit(solution)/shard_map/ppermute | solution.py:22
  46.6 1.3 %collective-permute-start.15 = (bf16[128,256]{1,0:T(8,128)(2,1)S(1)}, bf16[128,256]{1,0:T(8,128)(2,1)S(1)}, u32[]{:S(2)}, u32[]{:S(2)}) collective-permute-start(bf16[128,256]{1,0:T(8,128)(2,1)S(1)} %get-tuple-element.70), channel_id=1, source_target_pairs={{0,1},{1,0},{2,3},{3,2},{4,5},{5,4},{6,7},{7,6},{8,9},{9,8},{10,11... | collective-permute-start | bytes 196616 | tf_op jit(solution)/shard_map/ppermute | solution.py:22
  46.8 1.3 %collective-permute-start.16 = (bf16[128,256]{1,0:T(8,128)(2,1)S(1)}, bf16[128,256]{1,0:T(8,128)(2,1)S(1)}, u32[]{:S(2)}, u32[]{:S(2)}) collective-permute-start(bf16[128,256]{1,0:T(8,128)(2,1)S(1)} %get-tuple-element.71), channel_id=1, source_target_pairs={{0,1},{1,0},{2,3},{3,2},{4,5},{5,4},{6,7},{7,6},{8,9},{9,8},{10,11... | collective-permute-start | bytes 196616 | tf_op jit(solution)/shard_map/ppermute | solution.py:22
  47.1 1.3 %collective-permute-start.17 = (bf16[128,256]{1,0:T(8,128)(2,1)S(1)}, bf16[128,256]{1,0:T(8,128)(2,1)S(1)}, u32[]{:S(2)}, u32[]{:S(2)}) collective-permute-start(bf16[128,256]{1,0:T(8,128)(2,1)S(1)} %get-tuple-element.72), channel_id=1, source_target_pairs={{0,1},{1,0},{2,3},{3,2},{4,5},{5,4},{6,7},{7,6},{8,9},{9,8},{10,11... | collective-permute-start | bytes 196616 | tf_op jit(solution)/shard_map/ppermute | solution.py:22
  47.9 1.3 %collective-permute-start.18 = (bf16[128,256]{1,0:T(8,128)(2,1)S(1)}, bf16[128,256]{1,0:T(8,128)(2,1)S(1)}, u32[]{:S(2)}, u32[]{:S(2)}) collective-permute-start(bf16[128,256]{1,0:T(8,128)(2,1)S(1)} %get-tuple-element.73), channel_id=1, source_target_pairs={{0,1},{1,0},{2,3},{3,2},{4,5},{5,4},{6,7},{7,6},{8,9},{9,8},{10,11... | collective-permute-start | bytes 196616 | tf_op jit(solution)/shard_map/ppermute | solution.py:22
  48.0 1.3 %collective-permute-start.19 = (bf16[128,256]{1,0:T(8,128)(2,1)S(1)}, bf16[128,256]{1,0:T(8,128)(2,1)S(1)}, u32[]{:S(2)}, u32[]{:S(2)}) collective-permute-start(bf16[128,256]{1,0:T(8,128)(2,1)S(1)} %get-tuple-element.74), channel_id=1, source_target_pairs={{0,1},{1,0},{2,3},{3,2},{4,5},{5,4},{6,7},{7,6},{8,9},{9,8},{10,11... | collective-permute-start | bytes 196616 | tf_op jit(solution)/shard_map/ppermute | solution.py:22
  53.6 24.4 %collective-permute-start.24 = (bf16[256,1024]{1,0:T(8,128)(2,1)}, bf16[256,1024]{1,0:T(8,128)(2,1)}, u32[]{:S(2)}, u32[]{:S(2)}) collective-permute-start(bf16[256,1024]{1,0:T(8,128)(2,1)} %stack.3), channel_id=1, source_target_pairs={{0,4},{4,0},{8,12},{12,8},{1,5},{5,1},{9,13},{13,9},{2,6},{6,2},{1... | collective-permute-start | bytes 1572872 | tf_op jit(solution)/shard_map/ppermute | solution.py:26
  53.6 31.1 %collective-permute-start.20 = (bf16[2048,256]{1,0:T(8,128)(2,1)}, bf16[2048,256]{1,0:T(8,128)(2,1)}, u32[]{:S(2)}, u32[]{:S(2)}) collective-permute-start(bf16[2048,256]{1,0:T(8,128)(2,1)} %fetched_weights.1.refs_18_.refs_2_.refs_3_), channel_id=1, source_target_pairs={{0,2},{2,0},{1,3},{3,1},{4,6},{6,4},{5,7},{7,5},{8,10},{10,8},{9,1... | collective-permute-start | bytes 3145736 | tf_op jit(solution)/shard_map/ppermute | solution.py:22
  55.1 26.3 %collective-permute-start.29 = (bf16[256,1024]{1,0:T(8,128)(2,1)}, bf16[256,1024]{1,0:T(8,128)(2,1)S(1)}, u32[]{:S(2)}, u32[]{:S(2)}) collective-permute-start(bf16[256,1024]{1,0:T(8,128)(2,1)} %after.23), channel_id=1, source_target_pairs={{0,8},{4,12},{8,0},{12,4},{1,9},{5,13},{9,1},{13,5},{2,10},{6,14},... | collective-permute-start | bytes 1572872 | tf_op jit(solution)/shard_map/ppermute | solution.py:22
  56.4 3.6 %collective-permute-start.22 = (s32[8,128]{1,0:T(8,128)S(1)}, s32[8,128]{1,0:T(8,128)S(1)}, u32[]{:S(2)}, u32[]{:S(2)}) collective-permute-start(s32[8,128]{1,0:T(8,128)S(1)} %copy-done.38), channel_id=1, source_target_pairs={{0,16},{16,0},{1,17},{17,1},{2,18},{18,2},{3,19},{19,3},{4,20},{20... | collective-permute-start | bytes 12296 | tf_op jit(solution)/shard_map/ppermute | solution.py:22
  69.5 8.4 %copy-start.43 = (bf16[256,1024]{1,0:T(8,128)(2,1)S(1)}, bf16[256,1024]{1,0:T(8,128)(2,1)}, u32[]{:S(2)}) copy-start(bf16[256,1024]{1,0:T(8,128)(2,1)} %get-tuple-element.77.refs_2_.refs_11_) | copy-start | bytes 1572868
  69.5 2.6 %collective-permute-start.25 = (bf16[128,1024]{1,0:T(8,128)(2,1)}, bf16[128,1024]{1,0:T(8,128)(2,1)S(1)}, u32[]{:S(2)}, u32[]{:S(2)}) collective-permute-start(bf16[128,1024]{1,0:T(8,128)(2,1)} %get-tuple-element.78.refs_0_), channel_id=1, source_target_pairs={{0,1},{1,0},{2,3},{3,2},{4,5},{5,4},{6,7},{7,6},{8,9},{9,8},{10,11... | collective-permute-start | bytes 786440 | tf_op jit(solution)/shard_map/ppermute | solution.py:22
  71.1 1.5 %collective-permute-start.26 = (bf16[128,1024]{1,0:T(8,128)(2,1)S(1)}, bf16[128,1024]{1,0:T(8,128)(2,1)S(1)}, u32[]{:S(2)}, u32[]{:S(2)}) collective-permute-start(bf16[128,1024]{1,0:T(8,128)(2,1)S(1)} %after.20.refs_1_), channel_id=1, source_target_pairs={{0,1},{1,0},{2,3},{3,2},{4,5},{5,4},{6,7},{7,6},{8,9},{9,8},{10,11... | collective-permute-start | bytes 786440 | tf_op jit(solution)/shard_map/ppermute | solution.py:22
  78.0 1.2 %collective-permute-start.27 = (s32[8,128]{1,0:T(8,128)S(1)}, s32[8,128]{1,0:T(8,128)S(1)}, u32[]{:S(2)}, u32[]{:S(2)}) collective-permute-start(s32[8,128]{1,0:T(8,128)S(1)} %after.21), channel_id=1, source_target_pairs={{0,1},{1,0},{2,3},{3,2},{4,5},{5,4},{6,7},{7,6},{8,9},{9,8},{10,11... | collective-permute-start | bytes 12296 | tf_op jit(solution)/shard_map/ppermute | solution.py:22
  78.1 6.9 %collective-permute-start.31 = (bf16[256,1024]{1,0:T(8,128)(2,1)}, bf16[256,1024]{1,0:T(8,128)(2,1)S(1)}, u32[]{:S(2)}, u32[]{:S(2)}) collective-permute-start(bf16[256,1024]{1,0:T(8,128)(2,1)} %after.25.refs_9_), channel_id=1, source_target_pairs={{0,1},{1,0},{2,3},{3,2},{4,5},{5,4},{6,7},{7,6},{8,9},{9,8},{10,11... | collective-permute-start | bytes 1572872 | tf_op jit(solution)/shard_map/ppermute | solution.py:22
  79.2 5.9 %collective-permute-start.28 = (bf16[256,1024]{1,0:T(8,128)(2,1)S(1)}, bf16[256,1024]{1,0:T(8,128)(2,1)S(1)}, u32[]{:S(2)}, u32[]{:S(2)}) collective-permute-start(bf16[256,1024]{1,0:T(8,128)(2,1)S(1)} %after.22.refs_3_), channel_id=1, source_target_pairs={{0,1},{1,0},{2,3},{3,2},{4,5},{5,4},{6,7},{7,6},{8,9},{9,8},{10,11... | collective-permute-start | bytes 1572872 | tf_op jit(solution)/shard_map/ppermute | solution.py:22
  82.3 5.0 %collective-permute-start.30 = (bf16[256,1024]{1,0:T(8,128)(2,1)S(1)}, bf16[256,1024]{1,0:T(8,128)(2,1)S(1)}, u32[]{:S(2)}, u32[]{:S(2)}) collective-permute-start(bf16[256,1024]{1,0:T(8,128)(2,1)S(1)} %after.24.refs_5_), channel_id=1, source_target_pairs={{0,1},{1,0},{2,3},{3,2},{4,5},{5,4},{6,7},{7,6},{8,9},{9,8},{10,11... | collective-permute-start | bytes 1572872 | tf_op jit(solution)/shard_map/ppermute | solution.py:22
  82.3 10.6 %collective-permute-start.33 = (bf16[64,1024]{1,0:T(8,128)(2,1)S(1)}, bf16[64,1024]{1,0:T(8,128)(2,1)S(1)}, u32[]{:S(2)}, u32[]{:S(2)}) collective-permute-start(bf16[64,1024]{1,0:T(8,128)(2,1)S(1)} %after.26), channel_id=1, source_target_pairs={{0,12},{4,0},{8,4},{12,8},{1,13},{5,1},{9,5},{13,9},{2,14},{6,2},{... | collective-permute-start | bytes 393224 | tf_op jit(solution)/shard_map/ppermute | solution.py:22
  84.8 8.2 %collective-permute-start.35 = (bf16[64,1024]{1,0:T(8,128)(2,1)S(1)}, bf16[64,1024]{1,0:T(8,128)(2,1)S(1)}, u32[]{:S(2)}, u32[]{:S(2)}) collective-permute-start(bf16[64,1024]{1,0:T(8,128)(2,1)S(1)} %after.28), channel_id=1, source_target_pairs={{0,12},{4,0},{8,4},{12,8},{1,13},{5,1},{9,5},{13,9},{2,14},{6,2},{... | collective-permute-start | bytes 393224 | tf_op jit(solution)/shard_map/ppermute | solution.py:22
  85.0 9.2 %collective-permute-start.37 = (bf16[64,1024]{1,0:T(8,128)(2,1)S(1)}, bf16[64,1024]{1,0:T(8,128)(2,1)S(1)}, u32[]{:S(2)}, u32[]{:S(2)}) collective-permute-start(bf16[64,1024]{1,0:T(8,128)(2,1)S(1)} %after.30), channel_id=1, source_target_pairs={{0,12},{4,0},{8,4},{12,8},{1,13},{5,1},{9,5},{13,9},{2,14},{6,2},{... | collective-permute-start | bytes 393224 | tf_op jit(solution)/shard_map/ppermute | solution.py:22
  85.1 11.6 %collective-permute-start.39 = (bf16[64,1024]{1,0:T(8,128)(2,1)S(1)}, bf16[64,1024]{1,0:T(8,128)(2,1)S(1)}, u32[]{:S(2)}, u32[]{:S(2)}) collective-permute-start(bf16[64,1024]{1,0:T(8,128)(2,1)S(1)} %after.32), channel_id=1, source_target_pairs={{0,12},{4,0},{8,4},{12,8},{1,13},{5,1},{9,5},{13,9},{2,14},{6,2},{... | collective-permute-start | bytes 393224 | tf_op jit(solution)/shard_map/ppermute | solution.py:22
  92.0 11.0 %collective-permute-start.32 = (bf16[1024,128]{1,0:T(8,128)(2,1)S(1)}, bf16[1024,128]{1,0:T(8,128)(2,1)S(1)}, u32[]{:S(2)}, u32[]{:S(2)}) collective-permute-start(bf16[1024,128]{1,0:T(8,128)(2,1)S(1)} %get-tuple-element.85.refs_1_), channel_id=1, source_target_pairs={{0,2},{2,0},{1,3},{3,1},{4,6},{6,4},{5,7},{7,5},{8,10},{10,8},{9,1... | collective-permute-start | bytes 786440 | tf_op jit(solution)/shard_map/ppermute | solution.py:22
  92.9 3.8 %collective-permute-start.34 = (bf16[64,1024]{1,0:T(8,128)(2,1)S(1)}, bf16[64,1024]{1,0:T(8,128)(2,1)S(1)}, u32[]{:S(2)}, u32[]{:S(2)}) collective-permute-start(bf16[64,1024]{1,0:T(8,128)(2,1)S(1)} %after.27.refs_0_), channel_id=1, source_target_pairs={{0,1},{1,0},{2,3},{3,2},{4,5},{5,4},{6,7},{7,6},{8,9},{9,8},{10,11... | collective-permute-start | bytes 393224 | tf_op jit(solution)/shard_map/ppermute | solution.py:22
  92.9 3.7 %collective-permute-start.36 = (bf16[64,1024]{1,0:T(8,128)(2,1)S(1)}, bf16[64,1024]{1,0:T(8,128)(2,1)S(1)}, u32[]{:S(2)}, u32[]{:S(2)}) collective-permute-start(bf16[64,1024]{1,0:T(8,128)(2,1)S(1)} %after.29.refs_2_), channel_id=1, source_target_pairs={{0,1},{1,0},{2,3},{3,2},{4,5},{5,4},{6,7},{7,6},{8,9},{9,8},{10,11... | collective-permute-start | bytes 393224 | tf_op jit(solution)/shard_map/ppermute | solution.py:22
  94.2 2.4 %collective-permute-start.38 = (bf16[64,1024]{1,0:T(8,128)(2,1)S(1)}, bf16[64,1024]{1,0:T(8,128)(2,1)S(1)}, u32[]{:S(2)}, u32[]{:S(2)}) collective-permute-start(bf16[64,1024]{1,0:T(8,128)(2,1)S(1)} %after.31.refs_4_), channel_id=1, source_target_pairs={{0,1},{1,0},{2,3},{3,2},{4,5},{5,4},{6,7},{7,6},{8,9},{9,8},{10,11... | collective-permute-start | bytes 393224 | tf_op jit(solution)/shard_map/ppermute | solution.py:22
  96.7 1.3 %collective-permute-start.40 = (bf16[64,1024]{1,0:T(8,128)(2,1)S(1)}, bf16[64,1024]{1,0:T(8,128)(2,1)S(1)}, u32[]{:S(2)}, u32[]{:S(2)}) collective-permute-start(bf16[64,1024]{1,0:T(8,128)(2,1)S(1)} %after.33.refs_6_), channel_id=1, source_target_pairs={{0,1},{1,0},{2,3},{3,2},{4,5},{5,4},{6,7},{7,6},{8,9},{9,8},{10,11... | collective-permute-start | bytes 393224 | tf_op jit(solution)/shard_map/ppermute | solution.py:22
  98.7 4.3 %collective-permute-start.41 = (bf16[256,128]{1,0:T(8,128)(2,1)S(1)}, bf16[256,128]{1,0:T(8,128)(2,1)S(1)}, u32[]{:S(2)}, u32[]{:S(2)}) collective-permute-start(bf16[256,128]{1,0:T(8,128)(2,1)S(1)} %get-tuple-element.93), channel_id=1, source_target_pairs={{0,2},{2,0},{1,3},{3,1},{4,6},{6,4},{5,7},{7,5},{8,10},{10,8},{9,1... | collective-permute-start | bytes 196616 | tf_op jit(solution)/shard_map/ppermute | solution.py:22
  (37 other events, 155.9 us)

commit v13 on v12

--- a/solution.py
+++ b/solution.py
@@ -10,9 +10,9 @@
 F32, BF16, I32 = jnp.float32, jnp.bfloat16, jnp.int32
 VMEM = pl.BlockSpec(memory_space=pltpu.VMEM)
 ANY = pl.BlockSpec(memory_space=pl.ANY)
+HBM = pl.BlockSpec(memory_space=pltpu.HBM)
 SMEM = pl.BlockSpec(memory_space=pltpu.SMEM)
 PARAMS = pltpu.CompilerParams(vmem_limit_bytes=24 * 2**20)
-MIDDLE = pltpu.CompilerParams(vmem_limit_bytes=48 * 2**20)
 FIRST = pltpu.CompilerParams(vmem_limit_bytes=60 * 2**20)
 LANES = 128
 CUTS = 8
@@ -162,27 +162,43 @@
     )(pattern, block_slot, *[x for line in parts for x in line], *others)
 
 
+def one_hot(goal_ref, base, size):
+    index = lax.broadcasted_iota(I32, (size, LANES), 0) + base
+    lines = range(goal_ref.shape[0])
+    return jnp.concatenate([(index == goal_ref[a:a + 1, :]).astype(F32).astype(BF16) for a in lines], axis=1)
+
+
 def select(goal_ref, train_ref, base, size):
     tile = 128 if size % 128 == 0 else size
-    found = []
-    for at in range(0, size, tile):
-        index = lax.broadcasted_iota(I32, (tile, LANES), 0) + (base + at)
-        pick = [(index == goal_ref[a:a + 1, :]).astype(F32).astype(BF16) for a in range(goal_ref.shape[0])]
-        found.append(dot(jnp.concatenate(pick, axis=1), train_ref[...]).astype(BF16))
+    found = [dot(one_hot(goal_ref, base + at, tile), train_ref[...]).astype(BF16) for at in range(0, size, tile)]
     return jnp.concatenate(found)
 
 
 def own_rows(goal, train, bulk, *others):
+    rows, width = train.shape
+    cuts = 4
+    part = width // cuts
+
     def kernel(goal_ref, train_ref, *rest):
-        rest[-1][...] = select(goal_ref, train_ref, lax.axis_index("shard") * bulk, bulk)
-
-    return pl.pallas_call(
-        kernel,
-        in_specs=[VMEM] * 2 + [ANY] * len(others),
+        out_ref, held, sem = rest[-3:]
+        copies = [
+            pltpu.make_async_copy(train_ref.at[:, c * part:(c + 1) * part], held.at[c], sem.at[c]) for c in range(cuts)
+        ]
+        for copy in copies:
+            copy.start()
+        pick = one_hot(goal_ref, lax.axis_index("shard") * bulk, bulk)
+        for c, copy in enumerate(copies):
+            copy.wait()
+            out_ref[:, c * part:(c + 1) * part] = dot(pick, held[c]).astype(BF16)
+
+    return pl.pallas_call(
+        kernel,
+        in_specs=[VMEM, HBM] + [ANY] * len(others),
         out_specs=VMEM,
-        out_shape=jax.ShapeDtypeStruct((bulk, train.shape[1]), BF16),
+        out_shape=jax.ShapeDtypeStruct((bulk, width), BF16),
+        scratch_shapes=[pltpu.VMEM((cuts, rows, part), BF16), pltpu.SemaphoreType.DMA((cuts,))],
         cost_estimate=cost(2 * bulk * train.size, 2 * train.size),
-        compiler_params=FIRST,
+        compiler_params=PARAMS,
         name="own_rows",
     )(goal, train, *others)
 
@@ -255,25 +271,32 @@
     n = len(matrices)
 
     def kernel(block_ref, *refs):
-        value = None
-        for j in range(n):
-            part = dot(refs[j][...], jnp.concatenate([r[...] for r in refs[n + CUTS * j:n + CUTS * (j + 1)]]))
-            value = part if value is None else value + part
-        refs[-1][...] = value.astype(dtype)
-
-    return pl.pallas_call(
-        kernel,
-        grid_spec=pltpu.PrefetchScalarGridSpec(
-            num_scalar_prefetch=1,
-            grid=(steps,),
-            in_specs=[pl.BlockSpec((tile, width), lambda i, b: (b[0] * steps + i, 0))] * n
-            + [pl.BlockSpec((width // CUTS, total), lambda i, b: (0, 0))] * (CUTS * n)
-            + [ANY] * len(others),
-            out_specs=pl.BlockSpec((tile, total), lambda i, b: (i, 0)),
-        ),
+        out_ref, held, sem = refs[-3:]
+        first = pl.multiple_of(block_ref[0] * depth, depth)
+        copies = []
+        for i in range(steps):
+            for j in range(n):
+                source = refs[j].at[pl.ds(first + i * tile, tile)]
+                copies.append(pltpu.make_async_copy(source, held.at[j, i], sem.at[i * n + j]))
+        for copy in copies:
+            copy.start()
+        parts = [jnp.concatenate([r[...] for r in refs[n + CUTS * j:n + CUTS * (j + 1)]]) for j in range(n)]
+        for i in range(steps):
+            value = None
+            for j in range(n):
+                copies[i * n + j].wait()
+                part = dot(held[j, i], parts[j])
+                value = part if value is None else value + part
+            out_ref[i * tile:(i + 1) * tile, :] = value.astype(dtype)
+
+    return pl.pallas_call(
+        kernel,
+        in_specs=[SMEM] + [HBM] * n + [VMEM] * (CUTS * n) + [ANY] * len(others),
+        out_specs=VMEM,
         out_shape=jax.ShapeDtypeStruct((depth, total), dtype),
+        scratch_shapes=[pltpu.VMEM((n, steps, tile, width), BF16), pltpu.SemaphoreType.DMA((steps * n,))],
         cost_estimate=cost(2 * n * depth * width * total, 2 * n * depth * width + 4 * depth * total),
-        compiler_params=FIRST,
+        compiler_params=PARAMS,
         name="partial_weights",
     )(jnp.reshape(block, (1,)).astype(I32), *matrices, *queries, *others)
 
@@ -301,12 +324,12 @@
 
     return pl.pallas_call(
         kernel,
-        in_specs=[SMEM] + [ANY] * (n + len(others)),
+        in_specs=[SMEM] + [HBM] * n + [ANY] * len(others),
         out_specs=[VMEM] * n,
         out_shape=[jax.ShapeDtypeStruct((depth, width), BF16)] * n,
         scratch_shapes=[pltpu.SemaphoreType.DMA((n * cuts,))],
         cost_estimate=cost(0, 2 * n * depth * width),
-        compiler_params=MIDDLE,
+        compiler_params=PARAMS,
         name="fetch",
     )(jnp.reshape(block, (1,)).astype(I32), *matrices, *others)
 
@@ -373,7 +396,7 @@
         out_specs=[SMEM, VMEM],
         out_shape=[jax.ShapeDtypeStruct((n_shard, 4), I32), jax.ShapeDtypeStruct((8, LANES), I32)],
         cost_estimate=cost(0, 4 * ids.size),
-        compiler_params=FIRST,
+        compiler_params=PARAMS,
         name="row_table",
     )(ids, *others)
 
@@ -594,10 +617,9 @@
     targets = [(feat + d) % n_feat for d in range(1, n_feat)]
     near_chip = fetch(matrices, targets[0], depth, *pieces[1:])
 
-    mine = own_rows(goal, train, bulk, *pieces[1:])
     table, flag = row_table(ids, lines, bulk, extra, *pieces[1:])
     chosen = join_queries(
-        parts, block_slot, pattern, query_store.shape[0], n_feat, n_rep, *near_chip, mine, flag
+        parts, block_slot, pattern, query_store.shape[0], n_feat, n_rep, *near_chip, flag
     )
     queries = [*chosen[:CUTS]] + [shift(chosen[j], "rep", n_rep, j // CUTS) for j in range(CUTS, CUTS * n_rep)]
 
@@ -613,7 +635,8 @@
         shift(after(packed[len(middle) + j], here[-1], own), "shard", n_shard, last_hops) for j in range(len(final))
     ]
 
-    marks = [own]
+    mine = own_rows(goal, train, bulk, own)
+    marks = [own, mine]
     if extra:
         for d in range(1, n_group):
             flag = jnp.maximum(flag, shift(flag, "groups", n_group, d))

time: 105 us -> 97.5 us (0.929)
  Pallas kernels: 39.9 us -> 34 us
  local copies, waits for them, and re-layouts: 11.4 us -> 6.66 us
  starting transfers between devices: 29.7 us -> 33.6 us
    pallas_call x3, Pallas kernels: 16.9 us -> 11.5 us  [the longest x1 6.6 us: partial_weights(): pl.pallas_call(kernel, in_specs=[SMEM] + [HBM] * n + [VMEM] * (CUTS * n)...]
    unnamed x94 -> x36, local copies, waits for them, and re-layouts: 10.8 us -> 6.12 us
    ppermute x36, starting transfers between devices: 28 us -> 31.8 us  [shift(): return lax.ppermute(x, axis, [(i, (i + by) % size) for i in range(size)])]
    ppermute x36, waiting for transfers between devices: 17.2 us -> 15.8 us  [shift(): return lax.ppermute(x, axis, [(i, (i + by) % size) for i in range(size)])]
  transfers between devices with their start and end apart: 38 -> 38, of which waited for: 14 -> 12; matrix products, arithmetic and copies ran while one was open for 0% -> 1% of each run, Pallas kernels for 36% -> 33%
where the time goes in v13:
time: 97.5 us; the launch traced here: 97.2 us
  Pallas kernels  34 us (35%)
  starting transfers between devices  33.6 us (34%)
  waiting for transfers between devices  21.8 us (22%)
  local copies, waits for them, and re-layouts  6.66 us (7%)
  between operations  1.03 us (1%)
    ppermute x36, starting transfers between devices, shift(): return lax.ppermute(x, axis, [(i, (i + by) % size) for i in range(size)])  31.8 us
    ppermute x36, waiting for transfers between devices, shift(): return lax.ppermute(x, axis, [(i, (i + by) % size) for i in range(size)])  15.8 us
    pallas_call x1, Pallas kernels, partial_weights(): pl.pallas_call(kernel, in_specs=[SMEM] + [HBM] * n + [VMEM] * (CUTS * n)...  6.6 us
    pallas_call x1, Pallas kernels, pack_rows(): pl.pallas_call(kernel, grid=(1,), in_specs=[pl.BlockSpec((lines, LANES),...  6.25 us
    unnamed x36, local copies, waits for them, and re-layouts  6.12 us
    ppermute x2, waiting for transfers between devices, swap(): return lax.ppermute(x, axis, [(i, i ^ bit) for i in range(size)])  5.98 us
    pallas_call x1, Pallas kernels, early_scores(): pl.pallas_call(kernel, in_specs=[SMEM] + [VMEM] * (2 + n_other + n_rep *...  4.87 us
    pallas_call x1, Pallas kernels, fetched_weights(): pl.pallas_call(kernel, in_specs=[VMEM] * ((1 + CUTS) * n), out_specs=VMEM...  3.3 us
  transfers between devices with their start and end apart: 38, of which 12 were waited for; matrix products, arithmetic and copies ran while one was open for 1% of the time, Pallas kernels for 33%

profile of v13, /device:TPU:0, one launch (start us, length us, event | category | flops | bytes accessed | tf_op | source)
XLA Modules:
  0.0 97.2 jit_solution(8557522942758421427)
XLA Ops:
  0.5 2.7 %pick_queries.1 = (bf16[1,64,1024]{2,1,0:T(8,128)(2,1)}, bf16[1,64,1024]{2,1,0:T(8,128)(2,1)}, bf16[1,64,1024]{2,1,0:T(8,128)(2,1)}, bf16[1,64,1024]{2,1,0:T(8,128)(2,1)}) custom-call(s32[4,4]{1,0:T(4,128)} %pattern_ref.3, s32[16]{0:T(128)} %slot_ref.3, bf16[4,128,1024]{2,1,0:T(8,128)(2,1)} %in_ref.1), custom_call_target="tpu_custom_call" | custom-call | flops 1 | bytes 1 | tf_op jit(solution)/shard_map/pick_queries/pallas_call | solution.py:108
  3.1 2.8 %collective-permute-start.4 = (bf16[1,64,1024]{2,1,0:T(8,128)(2,1)}, bf16[1,64,1024]{2,1,0:T(8,128)(2,1)S(1)}, u32[]{:S(2)}, u32[]{:S(2)}) collective-permute-start(bf16[1,64,1024]{2,1,0:T(8,128)(2,1)} %get-tuple-element.50), channel_id=1, source_target_pairs={{0,4},{4,8},{8,12},{12,0},{1,5},{5,9},{9,13},{13,1},{2,6},{6,10},{... | collective-permute-start | bytes 393224 | tf_op jit(solution)/shard_map/ppermute | solution.py:22
  5.9 2.6 %collective-permute-start.5 = (bf16[1,64,1024]{2,1,0:T(8,128)(2,1)}, bf16[1,64,1024]{2,1,0:T(8,128)(2,1)S(1)}, u32[]{:S(2)}, u32[]{:S(2)}) collective-permute-start(bf16[1,64,1024]{2,1,0:T(8,128)(2,1)} %get-tuple-element.51), channel_id=1, source_target_pairs={{0,8},{4,12},{8,0},{12,4},{1,9},{5,13},{9,1},{13,5},{2,10},{6,14},... | collective-permute-start | bytes 393224 | tf_op jit(solution)/shard_map/ppermute | solution.py:22
  8.5 1.3 %collective-permute-start.6 = (bf16[1,64,1024]{2,1,0:T(8,128)(2,1)}, bf16[1,64,1024]{2,1,0:T(8,128)(2,1)S(1)}, u32[]{:S(2)}, u32[]{:S(2)}) collective-permute-start(bf16[1,64,1024]{2,1,0:T(8,128)(2,1)} %get-tuple-element.52), channel_id=1, source_target_pairs={{0,12},{4,0},{8,4},{12,8},{1,13},{5,1},{9,5},{13,9},{2,14},{6,2},{... | collective-permute-start | bytes 393224 | tf_op jit(solution)/shard_map/ppermute | solution.py:22
  9.9 6.3 %pack_rows.1 = (bf16[256,1024]{1,0:T(8,128)(2,1)}, bf16[256,1024]{1,0:T(8,128)(2,1)}, bf16[64,1024]{1,0:T(8,128)(2,1)}, bf16[64,1024]{1,0:T(8,128)(2,1)}, bf16[6...) custom-call(s32[32,128]{1,0:T(8,128)} %bitcast.11, ...), custom_call_target="tpu_custom_call" | custom-call | flops 1 | bytes 1 | tf_op jit(solution)/shard_map/pack_rows/pallas_call | solution.py:252
  16.1 1.8 %collective-permute-done.5.rest_1_.refs_3_.refs_2_ = bf16[1,64,1024]{2,1,0:T(8,128)(2,1)S(1)} collective-permute-done((bf16[1,64,1024]{2,1,0:T(8,128)(2,1)}, bf16[1,64,1024]{2,1,0:T(8,128)(2,1)S(1)}, u32[]{:S(2)}, u32[]{:S(2)}) %collective-permute-start.5) | collective-permute-done | bytes 131104 | tf_op jit(solution)/shard_map/ppermute | solution.py:22
  17.9 3.3 %collective-permute-start.21 = (bf16[256,1024]{1,0:T(8,128)(2,1)}, bf16[256,1024]{1,0:T(8,128)(2,1)S(1)}, u32[]{:S(2)}, u32[]{:S(2)}) collective-permute-start(bf16[256,1024]{1,0:T(8,128)(2,1)} %after.17), channel_id=1, source_target_pairs={{0,4},{4,8},{8,12},{12,0},{1,5},{5,9},{9,13},{13,1},{2,6},{6,10},{... | collective-permute-start | bytes 1572872 | tf_op jit(solution)/shard_map/ppermute | solution.py:22
  21.2 1.5 %collective-permute-start.8 = (bf16[1,64,1024]{2,1,0:T(8,128)(2,1)S(1)}, bf16[1,64,1024]{2,1,0:T(8,128)(2,1)S(1)}, u32[]{:S(2)}, u32[]{:S(2)}) collective-permute-start(bf16[1,64,1024]{2,1,0:T(8,128)(2,1)S(1)} %copy-done.6), channel_id=1, source_target_pairs={{0,16},{16,0},{1,17},{17,1},{2,18},{18,2},{3,19},{19,3},{4,20},{20... | collective-permute-start | bytes 393224 | tf_op jit(solution)/shard_map/ppermute | solution.py:22
  22.7 0.5 collective-permute-start.10
  23.2 1.5 %collective-permute-start.11 = (bf16[1,64,1024]{2,1,0:T(8,128)(2,1)S(1)}, bf16[1,64,1024]{2,1,0:T(8,128)(2,1)S(1)}, u32[]{:S(2)}, u32[]{:S(2)}) collective-permute-start(bf16[1,64,1024]{2,1,0:T(8,128)(2,1)S(1)} %collective-permute-done.6.rest_2_.refs_4_.refs_3_), channel_id=1, source_target_pairs={{0,16},{16,0},{1,17},{17,1},{2,18},{18,2},{3,19},{19,3},{4,20},{20... | collective-permute-start | bytes 393224 | tf_op jit(solution)/shard_map/ppermute | solution.py:22
  24.7 2.8 %collective-permute-done.8.refs_4_ = bf16[1,64,1024]{2,1,0:T(8,128)(2,1)S(1)} collective-permute-done((bf16[1,64,1024]{2,1,0:T(8,128)(2,1)S(1)}, bf16[1,64,1024]{2,1,0:T(8,128)(2,1)S(1)}, u32[]{:S(2)}, u32[]{:S(2)}) %collective-permute-start.8) | collective-permute-done | bytes 131104 | tf_op jit(solution)/shard_map/ppermute | solution.py:22
  27.6 1.5 %collective-permute-start.9 = (bf16[1,64,1024]{2,1,0:T(8,128)(2,1)S(1)}, bf16[1,64,1024]{2,1,0:T(8,128)(2,1)S(1)}, u32[]{:S(2)}, u32[]{:S(2)}) collective-permute-start(bf16[1,64,1024]{2,1,0:T(8,128)(2,1)S(1)} %collective-permute-done.4.rest_0_.refs_2_.refs_1_), channel_id=1, source_target_pairs={{0,16},{16,0},{1,17},{17,1},{2,18},{18,2},{3,19},{19,3},{4,20},{20... | collective-permute-start | bytes 393224 | tf_op jit(solution)/shard_map/ppermute | solution.py:22
  29.1 1.7 %collective-permute-start.23 = (bf16[128,1024]{1,0:T(8,128)(2,1)}, bf16[128,1024]{1,0:T(8,128)(2,1)S(1)}, u32[]{:S(2)}, u32[]{:S(2)}) collective-permute-start(bf16[128,1024]{1,0:T(8,128)(2,1)} %after.19), channel_id=1, source_target_pairs={{0,8},{4,12},{8,0},{12,4},{1,9},{5,13},{9,1},{13,5},{2,10},{6,14},... | collective-permute-start | bytes 786440 | tf_op jit(solution)/shard_map/ppermute | solution.py:26
  30.8 0.8 row_table.1
  31.6 3.4 %copy-done = bf16[1,4096,1024]{2,1,0:T(8,128)(2,1)S(1)} copy-done((bf16[1,4096,1024]{2,1,0:T(8,128)(2,1)S(1)}, bf16[1,4096,1024]{2,1,0:T(8,128)(2,1)}, u32[]{:S(2)}) %copy-start) | copy-done | bytes 8388632
  35.0 2.5 %fetch.1 = (bf16[2048,1024]{1,0:T(8,128)(2,1)S(1)}, bf16[2048,1024]{1,0:T(8,128)(2,1)S(1)}) custom-call(s32[1]{0:T(128)} %bitcast.3.block_ref, bf16[4096,1024]{1,0:T(8,128)(2,1)S(1)} %bitcast.7, bf16[4096,1024]{1,0:T(8,128)(2,1)} %collective-permute-done.7.refs_1_, bf16[1,64,1024]{2,1,0:T(8,128)(2,1)S(1)} %collective-permute-done.4.rest_0_.refs_2_.refs_1_, ...), custom_call_target="tpu_custom_call" | custom-call | flops 1 | bytes 1 | tf_op jit(solution)/shard_map/fetch/pallas_call | solution.py:325
  37.6 1.2 %join_queries.1 = (bf16[128,256]{1,0:T(8,128)(2,1)S(1)}, bf16[128,256]{1,0:T(8,128)(2,1)S(1)}, bf16[128,256]{1,0:T(8,128)(2,1)S(1)}, bf16[128,256]{1,0:T(8,128)(...) custom-call(s32[4,4]{1,0:T(4,128)S(1)} %copy-done.12, ...), custom_call_target="tpu_custom_call" | custom-call | flops 1 | bytes 1 | tf_op jit(solution)/shard_map/join_queries/pallas_call | solution.py:153
  38.9 0.5 collective-permute-start.13
  39.5 0.7 collective-permute-done.12.refs_10_
  40.8 0.6 collective-permute-done.15.refs_13_
  41.9 0.7 collective-permute-done.18.refs_16_
  42.8 3.3 %fetched_weights.1.refs_18_.refs_2_.refs_3_ = bf16[2048,256]{1,0:T(8,128)(2,1)} custom-call(bf16[2048,1024]{1,0:T(8,128)(2,1)S(1)} %get-tuple-element.55.refs_8_.refs_0_, bf16[2048,1024]{1,0:T(8,128)(2,1)S(1)} %get-tuple-element.56.refs_9_.refs_1_, bf16[128,256]{1,0:T(8,128)(2,1)S(1)} %get-tuple-element.58.refs_2_, ...), custom_call_target="tpu_custom_call" | custom-call | flops 1 | bytes 1 | tf_op jit(solution)/shard_map/fetched_weights/pallas_call | solution.py:352
  46.1 0.8 stack.3
  47.0 1.5 %collective-permute-start.29 = (bf16[256,1024]{1,0:T(8,128)(2,1)}, bf16[256,1024]{1,0:T(8,128)(2,1)S(1)}, u32[]{:S(2)}, u32[]{:S(2)}) collective-permute-start(bf16[256,1024]{1,0:T(8,128)(2,1)} %after.23), channel_id=1, source_target_pairs={{0,8},{4,12},{8,0},{12,4},{1,9},{5,13},{9,1},{13,5},{2,10},{6,14},... | collective-permute-start | bytes 1572872 | tf_op jit(solution)/shard_map/ppermute | solution.py:22
  48.5 1.5 %collective-permute-start.20 = (bf16[2048,256]{1,0:T(8,128)(2,1)}, bf16[2048,256]{1,0:T(8,128)(2,1)}, u32[]{:S(2)}, u32[]{:S(2)}) collective-permute-start(bf16[2048,256]{1,0:T(8,128)(2,1)} %fetched_weights.1.refs_18_.refs_2_.refs_3_), channel_id=1, source_target_pairs={{0,2},{2,0},{1,3},{3,1},{4,6},{6,4},{5,7},{7,5},{8,10},{10,8},{9,1... | collective-permute-start | bytes 3145736 | tf_op jit(solution)/shard_map/ppermute | solution.py:22
  50.0 1.5 %collective-permute-start.22 = (s32[8,128]{1,0:T(8,128)S(1)}, s32[8,128]{1,0:T(8,128)S(1)}, u32[]{:S(2)}, u32[]{:S(2)}) collective-permute-start(s32[8,128]{1,0:T(8,128)S(1)} %get-tuple-element.57.refs_10_), channel_id=1, source_target_pairs={{0,16},{16,0},{1,17},{17,1},{2,18},{18,2},{3,19},{19,3},{4,20},{20... | collective-permute-start | bytes 12296 | tf_op jit(solution)/shard_map/ppermute | solution.py:22
  51.5 2.1 %collective-permute-done.22 = s32[8,128]{1,0:T(8,128)S(1)} collective-permute-done((s32[8,128]{1,0:T(8,128)S(1)}, s32[8,128]{1,0:T(8,128)S(1)}, u32[]{:S(2)}, u32[]{:S(2)}) %collective-permute-start.22) | collective-permute-done | bytes 4128 | tf_op jit(solution)/shard_map/ppermute | solution.py:22
  53.6 0.5 slice.3
  54.8 6.6 %partial_weights.1.rest_0_.refs_1_.refs_2_.refs_0_ = f32[2048,256]{1,0:T(8,128)S(1)} custom-call(s32[1]{0:T(128)} %bitcast.1.block_ref, bf16[4096,1024]{1,0:T(8,128)(2,1)S(1)} %bitcast.10, bf16[4096,1024]{1,0:T(8,128)(2,1)} %collective-permute-done.7.refs_1_, bf16[128,256]{1,0:T(8,128)(2,1)S(1)} %get-tuple-element.58.refs_2_, ...), custom_call_target="tpu_custom_call" | custom-call | flops 1 | bytes 1 | tf_op jit(solution)/shard_map/partial_weights/pallas_call | solution.py:292
  61.8 0.5 collective-permute-start.26
  62.3 1.2 %copy-done.5 = bf16[128,1024]{1,0:T(8,128)(2,1)S(1)} copy-done((bf16[128,1024]{1,0:T(8,128)(2,1)S(1)}, bf16[128,1024]{1,0:T(8,128)(2,1)}, u32[]{:S(2)}) %copy-start.5) | copy-done | bytes 262168
  63.9 2.4 %own_rows.1.refs_2_ = bf16[256,2048]{1,0:T(8,128)(2,1)S(1)} custom-call(s32[8,128]{1,0:T(8,128)S(1)} %copy-done.13, bf16[1024,2048]{1,0:T(8,128)(2,1)S(1)} %copy-done.1, f32[2048,256]{1,0:T(8,128)S(1)} %partial_weights.1.rest_0_.refs_1_.refs_2_.refs_0_), custom_call_target="tpu_custom_call" | custom-call | flops 1 | bytes 1 | tf_op jit(solution)/shard_map/own_rows/pallas_call | solution.py:194
  66.4 6.0 %collective-permute-done.24.refs_4_.refs_0_ = bf16[256,1024]{1,0:T(8,128)(2,1)S(1)} collective-permute-done((bf16[256,1024]{1,0:T(8,128)(2,1)}, bf16[256,1024]{1,0:T(8,128)(2,1)S(1)}, u32[]{:S(2)}, u32[]{:S(2)}) %collective-permute-start.24) | collective-permute-done | bytes 524320 | tf_op jit(solution)/shard_map/ppermute | solution.py:26
  72.4 0.5 collective-permute-start.31
  72.9 0.7 collective-permute-done.29.refs_0_.refs_1_
  73.7 0.9 copy-done.7
  75.0 2.3 %collective-permute-start.39 = (bf16[64,1024]{1,0:T(8,128)(2,1)S(1)}, bf16[64,1024]{1,0:T(8,128)(2,1)S(1)}, u32[]{:S(2)}, u32[]{:S(2)}) collective-permute-start(bf16[64,1024]{1,0:T(8,128)(2,1)S(1)} %after.32), channel_id=1, source_target_pairs={{0,12},{4,0},{8,4},{12,8},{1,13},{5,1},{9,5},{13,9},{2,14},{6,2},{... | collective-permute-start | bytes 393224 | tf_op jit(solution)/shard_map/ppermute | solution.py:22
  77.4 0.9 collective-permute-start.35
  78.3 1.7 %collective-permute-start.33 = (bf16[64,1024]{1,0:T(8,128)(2,1)S(1)}, bf16[64,1024]{1,0:T(8,128)(2,1)S(1)}, u32[]{:S(2)}, u32[]{:S(2)}) collective-permute-start(bf16[64,1024]{1,0:T(8,128)(2,1)S(1)} %after.26), channel_id=1, source_target_pairs={{0,12},{4,0},{8,4},{12,8},{1,13},{5,1},{9,5},{13,9},{2,14},{6,2},{... | collective-permute-start | bytes 393224 | tf_op jit(solution)/shard_map/ppermute | solution.py:22
  80.0 4.9 %early_scores.1 = (bf16[2048,256]{1,0:T(8,128)(2,1)S(1)}, bf16[2048,256]{1,0:T(8,128)(2,1)S(1)}, f32[1024,128]{1,0:T(8,128)S(1)}, bf16[1024,128]{1,0:T(8,128)(2,1)S(1)}) custom-call(s32[4,4]{1,0:T(4,128)S(1)} %get-tuple-element.53.table_ref, f32[2048,256]{1,0:T(8,128)S(1)} %partial_weights.1.rest_0_.refs_1_.refs_2_.refs_0_, ...), custom_call_target="tpu_custom_call" | custom-call | flops 1 | bytes 1 | tf_op jit(solution)/shard_map/early_scores/pallas_call | solution.py:509
  84.9 1.5 %collective-permute-start.32 = (bf16[1024,128]{1,0:T(8,128)(2,1)S(1)}, bf16[1024,128]{1,0:T(8,128)(2,1)S(1)}, u32[]{:S(2)}, u32[]{:S(2)}) collective-permute-start(bf16[1024,128]{1,0:T(8,128)(2,1)S(1)} %get-tuple-element.85.refs_1_), channel_id=1, source_target_pairs={{0,2},{2,0},{1,3},{3,1},{4,6},{6,4},{5,7},{7,5},{8,10},{10,8},{9,1... | collective-permute-start | bytes 786440 | tf_op jit(solution)/shard_map/ppermute | solution.py:22
  86.5 0.5 collective-permute-start.38
  87.0 2.0 %collective-permute-done.33.refs_0_ = bf16[64,1024]{1,0:T(8,128)(2,1)S(1)} collective-permute-done((bf16[64,1024]{1,0:T(8,128)(2,1)S(1)}, bf16[64,1024]{1,0:T(8,128)(2,1)S(1)}, u32[]{:S(2)}, u32[]{:S(2)}) %collective-permute-start.33) | collective-permute-done | bytes 131104 | tf_op jit(solution)/shard_map/ppermute | solution.py:22
  89.1 1.3 %collective-permute-done.34.refs_1_ = bf16[64,1024]{1,0:T(8,128)(2,1)S(1)} collective-permute-done((bf16[64,1024]{1,0:T(8,128)(2,1)S(1)}, bf16[64,1024]{1,0:T(8,128)(2,1)S(1)}, u32[]{:S(2)}, u32[]{:S(2)}) %collective-permute-start.34) | collective-permute-done | bytes 131104 | tf_op jit(solution)/shard_map/ppermute | solution.py:22
  90.4 0.7 late_scores.1
  91.2 1.6 %collective-permute-start.41 = (bf16[256,128]{1,0:T(8,128)(2,1)S(1)}, bf16[256,128]{1,0:T(8,128)(2,1)S(1)}, u32[]{:S(2)}, u32[]{:S(2)}) collective-permute-start(bf16[256,128]{1,0:T(8,128)(2,1)S(1)} %get-tuple-element.93), channel_id=1, source_target_pairs={{0,2},{2,0},{1,3},{3,1},{4,6},{6,4},{5,7},{7,5},{8,10},{10,8},{9,1... | collective-permute-start | bytes 196616 | tf_op jit(solution)/shard_map/ppermute | solution.py:22
  92.7 2.8 %collective-permute-done.41.refs_3_ = bf16[256,128]{1,0:T(8,128)(2,1)S(1)} collective-permute-done((bf16[256,128]{1,0:T(8,128)(2,1)S(1)}, bf16[256,128]{1,0:T(8,128)(2,1)S(1)}, u32[]{:S(2)}, u32[]{:S(2)}) %collective-permute-start.41) | collective-permute-done | bytes 65568 | tf_op jit(solution)/shard_map/ppermute | solution.py:22
  95.5 1.7 %merge.1 = f32[128,1024]{1,0:T(8,128)} custom-call(s32[4,4]{1,0:T(4,128)S(1)} %get-tuple-element.53.table_ref, f32[1024,128]{1,0:T(8,128)S(1)} %get-tuple-element.84.refs_0_, bf16[1024,128]{1,0:T(8,128)(2,1)S(1)} %collective-permute-done.32.refs_1_, f32[256,128]{1,0:T(8,128)S(1)} %get-tuple-element.92.refs_2_, ...), custom_call_target="tpu_custom_call" | custom-call | flops 1 | bytes 1 | tf_op jit(solution)/shard_map/merge/pallas_call | solution.py:571
  (101 shorter events, 3.6 us)
Async XLA Ops:
  0.0 30.8 %copy-start.11 = (s32[4096]{0:T(1024)S(1)}, s32[4096]{0:T(1024)}, u32[]{:S(2)}) copy-start(s32[4096]{0:T(1024)} %param.9) | copy-start | bytes 49156
  0.0 29.1 %collective-permute-start.7 = (bf16[4096,1024]{1,0:T(8,128)(2,1)}, bf16[4096,1024]{1,0:T(8,128)(2,1)}, u32[]{:S(2)}, u32[]{:S(2)}) collective-permute-start(bf16[4096,1024]{1,0:T(8,128)(2,1)} %bitcast.6), channel_id=1, source_target_pairs={{0,1},{1,0},{2,3},{3,2},{4,5},{5,4},{6,7},{7,6},{8,9},{9,8},{10,11... | collective-permute-start | bytes 25165832 | tf_op jit(solution)/shard_map/ppermute | solution.py:22
  3.1 18.0 %copy-start.6 = (bf16[1,64,1024]{2,1,0:T(8,128)(2,1)S(1)}, bf16[1,64,1024]{2,1,0:T(8,128)(2,1)}, u32[]{:S(2)}) copy-start(bf16[1,64,1024]{2,1,0:T(8,128)(2,1)} %get-tuple-element.54.refs_0_) | copy-start | bytes 393220
  3.1 13.0 %collective-permute-start.4 = (bf16[1,64,1024]{2,1,0:T(8,128)(2,1)}, bf16[1,64,1024]{2,1,0:T(8,128)(2,1)S(1)}, u32[]{:S(2)}, u32[]{:S(2)}) collective-permute-start(bf16[1,64,1024]{2,1,0:T(8,128)(2,1)} %get-tuple-element.50), channel_id=1, source_target_pairs={{0,4},{4,8},{8,12},{12,0},{1,5},{5,9},{9,13},{13,1},{2,6},{6,10},{... | collective-permute-start | bytes 393224 | tf_op jit(solution)/shard_map/ppermute | solution.py:22
  5.9 12.0 %collective-permute-start.5 = (bf16[1,64,1024]{2,1,0:T(8,128)(2,1)}, bf16[1,64,1024]{2,1,0:T(8,128)(2,1)S(1)}, u32[]{:S(2)}, u32[]{:S(2)}) collective-permute-start(bf16[1,64,1024]{2,1,0:T(8,128)(2,1)} %get-tuple-element.51), channel_id=1, source_target_pairs={{0,8},{4,12},{8,0},{12,4},{1,9},{5,13},{9,1},{13,5},{2,10},{6,14},... | collective-permute-start | bytes 393224 | tf_op jit(solution)/shard_map/ppermute | solution.py:22
  8.5 9.4 %collective-permute-start.6 = (bf16[1,64,1024]{2,1,0:T(8,128)(2,1)}, bf16[1,64,1024]{2,1,0:T(8,128)(2,1)S(1)}, u32[]{:S(2)}, u32[]{:S(2)}) collective-permute-start(bf16[1,64,1024]{2,1,0:T(8,128)(2,1)} %get-tuple-element.52), channel_id=1, source_target_pairs={{0,12},{4,0},{8,4},{12,8},{1,13},{5,1},{9,5},{13,9},{2,14},{6,2},{... | collective-permute-start | bytes 393224 | tf_op jit(solution)/shard_map/ppermute | solution.py:22
  17.9 29.1 %collective-permute-start.21 = (bf16[256,1024]{1,0:T(8,128)(2,1)}, bf16[256,1024]{1,0:T(8,128)(2,1)S(1)}, u32[]{:S(2)}, u32[]{:S(2)}) collective-permute-start(bf16[256,1024]{1,0:T(8,128)(2,1)} %after.17), channel_id=1, source_target_pairs={{0,4},{4,8},{8,12},{12,0},{1,5},{5,9},{9,13},{13,1},{2,6},{6,10},{... | collective-permute-start | bytes 1572872 | tf_op jit(solution)/shard_map/ppermute | solution.py:22
  21.2 6.4 %collective-permute-start.8 = (bf16[1,64,1024]{2,1,0:T(8,128)(2,1)S(1)}, bf16[1,64,1024]{2,1,0:T(8,128)(2,1)S(1)}, u32[]{:S(2)}, u32[]{:S(2)}) collective-permute-start(bf16[1,64,1024]{2,1,0:T(8,128)(2,1)S(1)} %copy-done.6), channel_id=1, source_target_pairs={{0,16},{16,0},{1,17},{17,1},{2,18},{18,2},{3,19},{19,3},{4,20},{20... | collective-permute-start | bytes 393224 | tf_op jit(solution)/shard_map/ppermute | solution.py:22
  22.7 14.8 %collective-permute-start.10 = (bf16[1,64,1024]{2,1,0:T(8,128)(2,1)S(1)}, bf16[1,64,1024]{2,1,0:T(8,128)(2,1)S(1)}, u32[]{:S(2)}, u32[]{:S(2)}) collective-permute-start(bf16[1,64,1024]{2,1,0:T(8,128)(2,1)S(1)} %collective-permute-done.5.rest_1_.refs_3_.refs_2_), channel_id=1, source_target_pairs={{0,16},{16,0},{1,17},{17,1},{2,18},{18,2},{3,19},{19,3},{4,20},{20... | collective-permute-start | bytes 393224 | tf_op jit(solution)/shard_map/ppermute | solution.py:22
  23.2 14.3 %collective-permute-start.11 = (bf16[1,64,1024]{2,1,0:T(8,128)(2,1)S(1)}, bf16[1,64,1024]{2,1,0:T(8,128)(2,1)S(1)}, u32[]{:S(2)}, u32[]{:S(2)}) collective-permute-start(bf16[1,64,1024]{2,1,0:T(8,128)(2,1)S(1)} %collective-permute-done.6.rest_2_.refs_4_.refs_3_), channel_id=1, source_target_pairs={{0,16},{16,0},{1,17},{17,1},{2,18},{18,2},{3,19},{19,3},{4,20},{20... | collective-permute-start | bytes 393224 | tf_op jit(solution)/shard_map/ppermute | solution.py:22
  27.6 10.0 %collective-permute-start.9 = (bf16[1,64,1024]{2,1,0:T(8,128)(2,1)S(1)}, bf16[1,64,1024]{2,1,0:T(8,128)(2,1)S(1)}, u32[]{:S(2)}, u32[]{:S(2)}) collective-permute-start(bf16[1,64,1024]{2,1,0:T(8,128)(2,1)S(1)} %collective-permute-done.4.rest_0_.refs_2_.refs_1_), channel_id=1, source_target_pairs={{0,16},{16,0},{1,17},{17,1},{2,18},{18,2},{3,19},{19,3},{4,20},{20... | collective-permute-start | bytes 393224 | tf_op jit(solution)/shard_map/ppermute | solution.py:22
  29.1 17.0 %collective-permute-start.23 = (bf16[128,1024]{1,0:T(8,128)(2,1)}, bf16[128,1024]{1,0:T(8,128)(2,1)S(1)}, u32[]{:S(2)}, u32[]{:S(2)}) collective-permute-start(bf16[128,1024]{1,0:T(8,128)(2,1)} %after.19), channel_id=1, source_target_pairs={{0,8},{4,12},{8,0},{12,4},{1,9},{5,13},{9,1},{13,5},{2,10},{6,14},... | collective-permute-start | bytes 786440 | tf_op jit(solution)/shard_map/ppermute | solution.py:26
  31.6 3.4 %copy-start = (bf16[1,4096,1024]{2,1,0:T(8,128)(2,1)S(1)}, bf16[1,4096,1024]{2,1,0:T(8,128)(2,1)}, u32[]{:S(2)}) copy-start(bf16[1,4096,1024]{2,1,0:T(8,128)(2,1)} %param.10) | copy-start | bytes 25165828
  35.0 2.6 %copy-start.12 = (s32[4,4]{1,0:T(4,128)S(1)}, s32[4,4]{1,0:T(4,128)}, u32[]{:S(2)}) copy-start(s32[4,4]{1,0:T(4,128)} %pattern_ref.3) | copy-start | bytes 196
  35.0 2.6 %copy-start.14 = (s32[16]{0:T(128)S(1)}, s32[16]{0:T(128)}, u32[]{:S(2)}) copy-start(s32[16]{0:T(128)} %slot_ref.3) | copy-start | bytes 196
  38.8 1.3 %collective-permute-start.12 = (bf16[128,256]{1,0:T(8,128)(2,1)S(1)}, bf16[128,256]{1,0:T(8,128)(2,1)S(1)}, u32[]{:S(2)}, u32[]{:S(2)}) collective-permute-start(bf16[128,256]{1,0:T(8,128)(2,1)S(1)} %get-tuple-element.66), channel_id=1, source_target_pairs={{0,1},{1,0},{2,3},{3,2},{4,5},{5,4},{6,7},{7,6},{8,9},{9,8},{10,11... | collective-permute-start | bytes 196616 | tf_op jit(solution)/shard_map/ppermute | solution.py:22
  38.9 1.4 %collective-permute-start.13 = (bf16[128,256]{1,0:T(8,128)(2,1)S(1)}, bf16[128,256]{1,0:T(8,128)(2,1)S(1)}, u32[]{:S(2)}, u32[]{:S(2)}) collective-permute-start(bf16[128,256]{1,0:T(8,128)(2,1)S(1)} %get-tuple-element.67), channel_id=1, source_target_pairs={{0,1},{1,0},{2,3},{3,2},{4,5},{5,4},{6,7},{7,6},{8,9},{9,8},{10,11... | collective-permute-start | bytes 196616 | tf_op jit(solution)/shard_map/ppermute | solution.py:22
  39.4 1.3 %collective-permute-start.14 = (bf16[128,256]{1,0:T(8,128)(2,1)S(1)}, bf16[128,256]{1,0:T(8,128)(2,1)S(1)}, u32[]{:S(2)}, u32[]{:S(2)}) collective-permute-start(bf16[128,256]{1,0:T(8,128)(2,1)S(1)} %get-tuple-element.68), channel_id=1, source_target_pairs={{0,1},{1,0},{2,3},{3,2},{4,5},{5,4},{6,7},{7,6},{8,9},{9,8},{10,11... | collective-permute-start | bytes 196616 | tf_op jit(solution)/shard_map/ppermute | solution.py:22
  40.1 1.3 %collective-permute-start.15 = (bf16[128,256]{1,0:T(8,128)(2,1)S(1)}, bf16[128,256]{1,0:T(8,128)(2,1)S(1)}, u32[]{:S(2)}, u32[]{:S(2)}) collective-permute-start(bf16[128,256]{1,0:T(8,128)(2,1)S(1)} %get-tuple-element.69), channel_id=1, source_target_pairs={{0,1},{1,0},{2,3},{3,2},{4,5},{5,4},{6,7},{7,6},{8,9},{9,8},{10,11... | collective-permute-start | bytes 196616 | tf_op jit(solution)/shard_map/ppermute | solution.py:22
  40.3 1.3 %collective-permute-start.16 = (bf16[128,256]{1,0:T(8,128)(2,1)S(1)}, bf16[128,256]{1,0:T(8,128)(2,1)S(1)}, u32[]{:S(2)}, u32[]{:S(2)}) collective-permute-start(bf16[128,256]{1,0:T(8,128)(2,1)S(1)} %get-tuple-element.70), channel_id=1, source_target_pairs={{0,1},{1,0},{2,3},{3,2},{4,5},{5,4},{6,7},{7,6},{8,9},{9,8},{10,11... | collective-permute-start | bytes 196616 | tf_op jit(solution)/shard_map/ppermute | solution.py:22
  40.7 1.3 %collective-permute-start.17 = (bf16[128,256]{1,0:T(8,128)(2,1)S(1)}, bf16[128,256]{1,0:T(8,128)(2,1)S(1)}, u32[]{:S(2)}, u32[]{:S(2)}) collective-permute-start(bf16[128,256]{1,0:T(8,128)(2,1)S(1)} %get-tuple-element.71), channel_id=1, source_target_pairs={{0,1},{1,0},{2,3},{3,2},{4,5},{5,4},{6,7},{7,6},{8,9},{9,8},{10,11... | collective-permute-start | bytes 196616 | tf_op jit(solution)/shard_map/ppermute | solution.py:22
  41.4 1.3 %collective-permute-start.18 = (bf16[128,256]{1,0:T(8,128)(2,1)S(1)}, bf16[128,256]{1,0:T(8,128)(2,1)S(1)}, u32[]{:S(2)}, u32[]{:S(2)}) collective-permute-start(bf16[128,256]{1,0:T(8,128)(2,1)S(1)} %get-tuple-element.72), channel_id=1, source_target_pairs={{0,1},{1,0},{2,3},{3,2},{4,5},{5,4},{6,7},{7,6},{8,9},{9,8},{10,11... | collective-permute-start | bytes 196616 | tf_op jit(solution)/shard_map/ppermute | solution.py:22
  41.6 1.3 %collective-permute-start.19 = (bf16[128,256]{1,0:T(8,128)(2,1)S(1)}, bf16[128,256]{1,0:T(8,128)(2,1)S(1)}, u32[]{:S(2)}, u32[]{:S(2)}) collective-permute-start(bf16[128,256]{1,0:T(8,128)(2,1)S(1)} %get-tuple-element.73), channel_id=1, source_target_pairs={{0,1},{1,0},{2,3},{3,2},{4,5},{5,4},{6,7},{7,6},{8,9},{9,8},{10,11... | collective-permute-start | bytes 196616 | tf_op jit(solution)/shard_map/ppermute | solution.py:22
  42.8 12.0 %slice-start = ((s8[8388608]{0:T(1024)(128)(4,1)}), s8[4194304]{0:T(1024)(128)(4,1)S(1)}, s32[]{:S(2)}) async-start(s8[8388608]{0:T(1024)(128)(4,1)} %bitcast.8), calls=%async_computation | async-start | bytes 8388608
  42.8 3.3 %copy-start.4 = (bf16[128,1024]{1,0:T(8,128)(2,1)S(1)}, bf16[128,1024]{1,0:T(8,128)(2,1)}, u32[]{:S(2)}) copy-start(bf16[128,1024]{1,0:T(8,128)(2,1)} %get-tuple-element.78.refs_0_) | copy-start | bytes 786436
  42.8 12.0 %slice-start.1 = ((s8[8388608]{0:T(1024)(128)(4,1)}), s8[4194304]{0:T(1024)(128)(4,1)S(1)}, s32[]{:S(2)}) async-start(s8[8388608]{0:T(1024)(128)(4,1)} %bitcast.8), calls=%async_computation.1 | async-start | bytes 8388608
  46.9 25.4 %collective-permute-start.24 = (bf16[256,1024]{1,0:T(8,128)(2,1)}, bf16[256,1024]{1,0:T(8,128)(2,1)S(1)}, u32[]{:S(2)}, u32[]{:S(2)}) collective-permute-start(bf16[256,1024]{1,0:T(8,128)(2,1)} %stack.3), channel_id=1, source_target_pairs={{0,4},{4,0},{8,12},{12,8},{1,5},{5,1},{9,13},{13,9},{2,6},{6,2},{1... | collective-permute-start | bytes 1572872 | tf_op jit(solution)/shard_map/ppermute | solution.py:26
  47.0 7.8 %copy-start.2 = (bf16[256,1024]{1,0:T(8,128)(2,1)}, bf16[256,1024]{1,0:T(8,128)(2,1)S(1)}, u32[]{:S(2)}) copy-start(bf16[256,1024]{1,0:T(8,128)(2,1)S(1)} %collective-permute-done.21.refs_0_.refs_1_) | copy-start | bytes 1572868
  47.0 26.6 %collective-permute-start.29 = (bf16[256,1024]{1,0:T(8,128)(2,1)}, bf16[256,1024]{1,0:T(8,128)(2,1)S(1)}, u32[]{:S(2)}, u32[]{:S(2)}) collective-permute-start(bf16[256,1024]{1,0:T(8,128)(2,1)} %after.23), channel_id=1, source_target_pairs={{0,8},{4,12},{8,0},{12,4},{1,9},{5,13},{9,1},{13,5},{2,10},{6,14},... | collective-permute-start | bytes 1572872 | tf_op jit(solution)/shard_map/ppermute | solution.py:22
  48.5 28.9 %collective-permute-start.20 = (bf16[2048,256]{1,0:T(8,128)(2,1)}, bf16[2048,256]{1,0:T(8,128)(2,1)}, u32[]{:S(2)}, u32[]{:S(2)}) collective-permute-start(bf16[2048,256]{1,0:T(8,128)(2,1)} %fetched_weights.1.refs_18_.refs_2_.refs_3_), channel_id=1, source_target_pairs={{0,2},{2,0},{1,3},{3,1},{4,6},{6,4},{5,7},{7,5},{8,10},{10,8},{9,1... | collective-permute-start | bytes 3145736 | tf_op jit(solution)/shard_map/ppermute | solution.py:22
  50.0 3.6 %collective-permute-start.22 = (s32[8,128]{1,0:T(8,128)S(1)}, s32[8,128]{1,0:T(8,128)S(1)}, u32[]{:S(2)}, u32[]{:S(2)}) collective-permute-start(s32[8,128]{1,0:T(8,128)S(1)} %get-tuple-element.57.refs_10_), channel_id=1, source_target_pairs={{0,16},{16,0},{1,17},{17,1},{2,18},{18,2},{3,19},{19,3},{4,20},{20... | collective-permute-start | bytes 12296 | tf_op jit(solution)/shard_map/ppermute | solution.py:22
  54.8 6.6 %copy-start.15 = (bf16[128,1024]{1,0:T(8,128)(2,1)S(1)}, bf16[128,1024]{1,0:T(8,128)(2,1)}, u32[]{:S(2)}) copy-start(bf16[128,1024]{1,0:T(8,128)(2,1)} %get-tuple-element.76.refs_0_) | copy-start | bytes 786436
  61.7 4.6 %collective-permute-start.25 = (bf16[128,1024]{1,0:T(8,128)(2,1)}, bf16[128,1024]{1,0:T(8,128)(2,1)S(1)}, u32[]{:S(2)}, u32[]{:S(2)}) collective-permute-start(bf16[128,1024]{1,0:T(8,128)(2,1)} %get-tuple-element.78.refs_0_), channel_id=1, source_target_pairs={{0,1},{1,0},{2,3},{3,2},{4,5},{5,4},{6,7},{7,6},{8,9},{9,8},{10,11... | collective-permute-start | bytes 786440 | tf_op jit(solution)/shard_map/ppermute | solution.py:22
  61.8 4.5 %collective-permute-start.26 = (bf16[128,1024]{1,0:T(8,128)(2,1)S(1)}, bf16[128,1024]{1,0:T(8,128)(2,1)S(1)}, u32[]{:S(2)}, u32[]{:S(2)}) collective-permute-start(bf16[128,1024]{1,0:T(8,128)(2,1)S(1)} %after.20.refs_1_), channel_id=1, source_target_pairs={{0,1},{1,0},{2,3},{3,2},{4,5},{5,4},{6,7},{7,6},{8,9},{9,8},{10,11... | collective-permute-start | bytes 786440 | tf_op jit(solution)/shard_map/ppermute | solution.py:22
  72.3 2.2 %collective-permute-start.27 = (s32[8,128]{1,0:T(8,128)S(1)}, s32[8,128]{1,0:T(8,128)S(1)}, u32[]{:S(2)}, u32[]{:S(2)}) collective-permute-start(s32[8,128]{1,0:T(8,128)S(1)} %after.21), channel_id=1, source_target_pairs={{0,1},{1,0},{2,3},{3,2},{4,5},{5,4},{6,7},{7,6},{8,9},{9,8},{10,11... | collective-permute-start | bytes 12296 | tf_op jit(solution)/shard_map/ppermute | solution.py:22
  72.4 5.0 %collective-permute-start.31 = (bf16[256,1024]{1,0:T(8,128)(2,1)S(1)}, bf16[256,1024]{1,0:T(8,128)(2,1)S(1)}, u32[]{:S(2)}, u32[]{:S(2)}) collective-permute-start(bf16[256,1024]{1,0:T(8,128)(2,1)S(1)} %after.25.refs_9_), channel_id=1, source_target_pairs={{0,1},{1,0},{2,3},{3,2},{4,5},{5,4},{6,7},{7,6},{8,9},{9,8},{10,11... | collective-permute-start | bytes 1572872 | tf_op jit(solution)/shard_map/ppermute | solution.py:22
  74.5 3.8 %collective-permute-start.30 = (bf16[256,1024]{1,0:T(8,128)(2,1)S(1)}, bf16[256,1024]{1,0:T(8,128)(2,1)S(1)}, u32[]{:S(2)}, u32[]{:S(2)}) collective-permute-start(bf16[256,1024]{1,0:T(8,128)(2,1)S(1)} %after.24.refs_5_), channel_id=1, source_target_pairs={{0,1},{1,0},{2,3},{3,2},{4,5},{5,4},{6,7},{7,6},{8,9},{9,8},{10,11... | collective-permute-start | bytes 1572872 | tf_op jit(solution)/shard_map/ppermute | solution.py:22
  74.7 5.3 %collective-permute-start.28 = (bf16[256,1024]{1,0:T(8,128)(2,1)S(1)}, bf16[256,1024]{1,0:T(8,128)(2,1)S(1)}, u32[]{:S(2)}, u32[]{:S(2)}) collective-permute-start(bf16[256,1024]{1,0:T(8,128)(2,1)S(1)} %after.22.refs_3_), channel_id=1, source_target_pairs={{0,1},{1,0},{2,3},{3,2},{4,5},{5,4},{6,7},{7,6},{8,9},{9,8},{10,11... | collective-permute-start | bytes 1572872 | tf_op jit(solution)/shard_map/ppermute | solution.py:22
  75.0 11.4 %collective-permute-start.39 = (bf16[64,1024]{1,0:T(8,128)(2,1)S(1)}, bf16[64,1024]{1,0:T(8,128)(2,1)S(1)}, u32[]{:S(2)}, u32[]{:S(2)}) collective-permute-start(bf16[64,1024]{1,0:T(8,128)(2,1)S(1)} %after.32), channel_id=1, source_target_pairs={{0,12},{4,0},{8,4},{12,8},{1,13},{5,1},{9,5},{13,9},{2,14},{6,2},{... | collective-permute-start | bytes 393224 | tf_op jit(solution)/shard_map/ppermute | solution.py:22
  77.4 9.1 %collective-permute-start.37 = (bf16[64,1024]{1,0:T(8,128)(2,1)S(1)}, bf16[64,1024]{1,0:T(8,128)(2,1)S(1)}, u32[]{:S(2)}, u32[]{:S(2)}) collective-permute-start(bf16[64,1024]{1,0:T(8,128)(2,1)S(1)} %after.30), channel_id=1, source_target_pairs={{0,12},{4,0},{8,4},{12,8},{1,13},{5,1},{9,5},{13,9},{2,14},{6,2},{... | collective-permute-start | bytes 393224 | tf_op jit(solution)/shard_map/ppermute | solution.py:22
  77.4 9.6 %collective-permute-start.35 = (bf16[64,1024]{1,0:T(8,128)(2,1)S(1)}, bf16[64,1024]{1,0:T(8,128)(2,1)S(1)}, u32[]{:S(2)}, u32[]{:S(2)}) collective-permute-start(bf16[64,1024]{1,0:T(8,128)(2,1)S(1)} %after.28), channel_id=1, source_target_pairs={{0,12},{4,0},{8,4},{12,8},{1,13},{5,1},{9,5},{13,9},{2,14},{6,2},{... | collective-permute-start | bytes 393224 | tf_op jit(solution)/shard_map/ppermute | solution.py:22
  78.3 10.8 %collective-permute-start.33 = (bf16[64,1024]{1,0:T(8,128)(2,1)S(1)}, bf16[64,1024]{1,0:T(8,128)(2,1)S(1)}, u32[]{:S(2)}, u32[]{:S(2)}) collective-permute-start(bf16[64,1024]{1,0:T(8,128)(2,1)S(1)} %after.26), channel_id=1, source_target_pairs={{0,12},{4,0},{8,4},{12,8},{1,13},{5,1},{9,5},{13,9},{2,14},{6,2},{... | collective-permute-start | bytes 393224 | tf_op jit(solution)/shard_map/ppermute | solution.py:22
  84.9 10.6 %collective-permute-start.32 = (bf16[1024,128]{1,0:T(8,128)(2,1)S(1)}, bf16[1024,128]{1,0:T(8,128)(2,1)S(1)}, u32[]{:S(2)}, u32[]{:S(2)}) collective-permute-start(bf16[1024,128]{1,0:T(8,128)(2,1)S(1)} %get-tuple-element.85.refs_1_), channel_id=1, source_target_pairs={{0,2},{2,0},{1,3},{3,1},{4,6},{6,4},{5,7},{7,5},{8,10},{10,8},{9,1... | collective-permute-start | bytes 786440 | tf_op jit(solution)/shard_map/ppermute | solution.py:22
  86.4 2.6 %collective-permute-start.40 = (bf16[64,1024]{1,0:T(8,128)(2,1)S(1)}, bf16[64,1024]{1,0:T(8,128)(2,1)S(1)}, u32[]{:S(2)}, u32[]{:S(2)}) collective-permute-start(bf16[64,1024]{1,0:T(8,128)(2,1)S(1)} %after.33.refs_6_), channel_id=1, source_target_pairs={{0,1},{1,0},{2,3},{3,2},{4,5},{5,4},{6,7},{7,6},{8,9},{9,8},{10,11... | collective-permute-start | bytes 393224 | tf_op jit(solution)/shard_map/ppermute | solution.py:22
  86.5 2.6 %collective-permute-start.38 = (bf16[64,1024]{1,0:T(8,128)(2,1)S(1)}, bf16[64,1024]{1,0:T(8,128)(2,1)S(1)}, u32[]{:S(2)}, u32[]{:S(2)}) collective-permute-start(bf16[64,1024]{1,0:T(8,128)(2,1)S(1)} %after.31.refs_4_), channel_id=1, source_target_pairs={{0,1},{1,0},{2,3},{3,2},{4,5},{5,4},{6,7},{7,6},{8,9},{9,8},{10,11... | collective-permute-start | bytes 393224 | tf_op jit(solution)/shard_map/ppermute | solution.py:22
  87.0 2.1 %collective-permute-start.36 = (bf16[64,1024]{1,0:T(8,128)(2,1)S(1)}, bf16[64,1024]{1,0:T(8,128)(2,1)S(1)}, u32[]{:S(2)}, u32[]{:S(2)}) collective-permute-start(bf16[64,1024]{1,0:T(8,128)(2,1)S(1)} %after.29.refs_2_), channel_id=1, source_target_pairs={{0,1},{1,0},{2,3},{3,2},{4,5},{5,4},{6,7},{7,6},{8,9},{9,8},{10,11... | collective-permute-start | bytes 393224 | tf_op jit(solution)/shard_map/ppermute | solution.py:22
  89.1 1.3 %collective-permute-start.34 = (bf16[64,1024]{1,0:T(8,128)(2,1)S(1)}, bf16[64,1024]{1,0:T(8,128)(2,1)S(1)}, u32[]{:S(2)}, u32[]{:S(2)}) collective-permute-start(bf16[64,1024]{1,0:T(8,128)(2,1)S(1)} %after.27.refs_0_), channel_id=1, source_target_pairs={{0,1},{1,0},{2,3},{3,2},{4,5},{5,4},{6,7},{7,6},{8,9},{9,8},{10,11... | collective-permute-start | bytes 393224 | tf_op jit(solution)/shard_map/ppermute | solution.py:22
  91.2 4.3 %collective-permute-start.41 = (bf16[256,128]{1,0:T(8,128)(2,1)S(1)}, bf16[256,128]{1,0:T(8,128)(2,1)S(1)}, u32[]{:S(2)}, u32[]{:S(2)}) collective-permute-start(bf16[256,128]{1,0:T(8,128)(2,1)S(1)} %get-tuple-element.93), channel_id=1, source_target_pairs={{0,2},{2,0},{1,3},{3,1},{4,6},{6,4},{5,7},{7,5},{8,10},{10,8},{9,1... | collective-permute-start | bytes 196616 | tf_op jit(solution)/shard_map/ppermute | solution.py:22
  (8 other events, 11.5 us)

commit v14 on v13

--- a/solution.py
+++ b/solution.py
@@ -631,12 +631,10 @@
     for (hops, _, _), x in zip(middle[1:], packed[1:]):
         here.append(shift(after(x, *urgent, *sends), "shard", n_shard, hops))
         urgent = [here[-1]]
-    last = [
-        shift(after(packed[len(middle) + j], here[-1], own), "shard", n_shard, last_hops) for j in range(len(final))
-    ]
+    last = [after(x, own) for x in packed[len(middle):len(middle) + len(final)]]
 
     mine = own_rows(goal, train, bulk, own)
-    marks = [own, mine]
+    marks = [own, mine, *last]
     if extra:
         for d in range(1, n_group):
             flag = jnp.maximum(flag, shift(flag, "groups", n_group, d))
@@ -656,6 +654,7 @@
         marks += [seconds[0][0], near, *pairs]
 
     mark = shift(after(jnp.zeros((8, LANES), I32), *marks), "rep", n_rep, 1)
+    last = [shift(x, "shard", n_shard, last_hops) for x in last]
     ready = [with_rep(after(x, mark)) for x in here]
     high, low, *early = early_scores(
         own, others, mine, ready, middle, firsts, seconds, table, rows, n_feat, n_rep, n_shard, bulk, extra

time: 97.5 us -> 96.5 us (0.990)
  starting transfers between devices: 33.6 us -> 32.2 us
  waiting for transfers between devices: 21.8 us -> 23 us
    ppermute x36, starting transfers between devices: 31.8 us -> 30.6 us  [shift(): return lax.ppermute(x, axis, [(i, (i + by) % size) for i in range(size)])]
    ppermute x36, waiting for transfers between devices: 15.8 us -> 16.8 us  [shift(): return lax.ppermute(x, axis, [(i, (i + by) % size) for i in range(size)])]
  transfers between devices with their start and end apart: 38 -> 38, of which waited for: 12 -> 14; matrix products, arithmetic and copies ran while one was open for 1% -> 1% of each run, Pallas kernels for 33% -> 33%
where the time goes in v14:
time: 96.5 us; the launch traced here: 96.2 us
  Pallas kernels  33.2 us (34%)
  starting transfers between devices  32.2 us (33%)
  waiting for transfers between devices  23 us (24%)
  local copies, waits for them, and re-layouts  6.5 us (7%)
  between operations  1.03 us (1%)
    ppermute x36, starting transfers between devices, shift(): return lax.ppermute(x, axis, [(i, (i + by) % size) for i in range(size)])  30.6 us
    ppermute x36, waiting for transfers between devices, shift(): return lax.ppermute(x, axis, [(i, (i + by) % size) for i in range(size)])  16.8 us
    pallas_call x1, Pallas kernels, partial_weights(): pl.pallas_call(kernel, in_specs=[SMEM] + [HBM] * n + [VMEM] * (CUTS * n)...  6.6 us
    pallas_call x1, Pallas kernels, pack_rows(): pl.pallas_call(kernel, grid=(1,), in_specs=[pl.BlockSpec((lines, LANES),...  6.25 us
    ppermute x2, waiting for transfers between devices, swap(): return lax.ppermute(x, axis, [(i, i ^ bit) for i in range(size)])  6.22 us
    unnamed x36, local copies, waits for them, and re-layouts  5.96 us
    pallas_call x1, Pallas kernels, early_scores(): pl.pallas_call(kernel, in_specs=[SMEM] + [VMEM] * (2 + n_other + n_rep *...  5.08 us
    pallas_call x1, Pallas kernels, pick_queries(): pl.pallas_call(kernel, in_specs=[SMEM, SMEM, ANY], out_specs=[VMEM] * n_c...  2.68 us
  transfers between devices with their start and end apart: 38, of which 14 were waited for; matrix products, arithmetic and copies ran while one was open for 1% of the time, Pallas kernels for 33%

profile of v14, /device:TPU:0, one launch (start us, length us, event | category | flops | bytes accessed | tf_op | source)
XLA Modules:
  0.0 96.2 jit_solution(18126425464679318392)
XLA Ops:
  0.5 2.7 %pick_queries.1 = (bf16[1,64,1024]{2,1,0:T(8,128)(2,1)}, bf16[1,64,1024]{2,1,0:T(8,128)(2,1)}, bf16[1,64,1024]{2,1,0:T(8,128)(2,1)}, bf16[1,64,1024]{2,1,0:T(8,128)(2,1)}) custom-call(s32[4,4]{1,0:T(4,128)} %pattern_ref.3, s32[16]{0:T(128)} %slot_ref.3, bf16[4,128,1024]{2,1,0:T(8,128)(2,1)} %in_ref.1), custom_call_target="tpu_custom_call" | custom-call | flops 1 | bytes 1 | tf_op jit(solution)/shard_map/pick_queries/pallas_call | solution.py:108
  3.1 2.8 %collective-permute-start.4 = (bf16[1,64,1024]{2,1,0:T(8,128)(2,1)}, bf16[1,64,1024]{2,1,0:T(8,128)(2,1)S(1)}, u32[]{:S(2)}, u32[]{:S(2)}) collective-permute-start(bf16[1,64,1024]{2,1,0:T(8,128)(2,1)} %get-tuple-element.50), channel_id=1, source_target_pairs={{0,4},{4,8},{8,12},{12,0},{1,5},{5,9},{9,13},{13,1},{2,6},{6,10},{... | collective-permute-start | bytes 393224 | tf_op jit(solution)/shard_map/ppermute | solution.py:22
  5.9 2.6 %collective-permute-start.5 = (bf16[1,64,1024]{2,1,0:T(8,128)(2,1)}, bf16[1,64,1024]{2,1,0:T(8,128)(2,1)S(1)}, u32[]{:S(2)}, u32[]{:S(2)}) collective-permute-start(bf16[1,64,1024]{2,1,0:T(8,128)(2,1)} %get-tuple-element.51), channel_id=1, source_target_pairs={{0,8},{4,12},{8,0},{12,4},{1,9},{5,13},{9,1},{13,5},{2,10},{6,14},... | collective-permute-start | bytes 393224 | tf_op jit(solution)/shard_map/ppermute | solution.py:22
  8.5 1.3 %collective-permute-start.6 = (bf16[1,64,1024]{2,1,0:T(8,128)(2,1)}, bf16[1,64,1024]{2,1,0:T(8,128)(2,1)S(1)}, u32[]{:S(2)}, u32[]{:S(2)}) collective-permute-start(bf16[1,64,1024]{2,1,0:T(8,128)(2,1)} %get-tuple-element.52), channel_id=1, source_target_pairs={{0,12},{4,0},{8,4},{12,8},{1,13},{5,1},{9,5},{13,9},{2,14},{6,2},{... | collective-permute-start | bytes 393224 | tf_op jit(solution)/shard_map/ppermute | solution.py:22
  9.9 1.5 %collective-permute-start.8 = (bf16[1,64,1024]{2,1,0:T(8,128)(2,1)}, bf16[1,64,1024]{2,1,0:T(8,128)(2,1)S(1)}, u32[]{:S(2)}, u32[]{:S(2)}) collective-permute-start(bf16[1,64,1024]{2,1,0:T(8,128)(2,1)} %get-tuple-element.54.refs_0_), channel_id=1, source_target_pairs={{0,16},{16,0},{1,17},{17,1},{2,18},{18,2},{3,19},{19,3},{4,20},{20... | collective-permute-start | bytes 393224 | tf_op jit(solution)/shard_map/ppermute | solution.py:22
  11.4 6.3 %pack_rows.1 = (bf16[256,1024]{1,0:T(8,128)(2,1)}, bf16[256,1024]{1,0:T(8,128)(2,1)}, bf16[64,1024]{1,0:T(8,128)(2,1)}, bf16[64,1024]{1,0:T(8,128)(2,1)}, bf16[6...) custom-call(s32[32,128]{1,0:T(8,128)} %bitcast.11, ...), custom_call_target="tpu_custom_call" | custom-call | flops 1 | bytes 1 | tf_op jit(solution)/shard_map/pack_rows/pallas_call | solution.py:252
  17.9 3.3 %collective-permute-start.21 = (bf16[256,1024]{1,0:T(8,128)(2,1)}, bf16[256,1024]{1,0:T(8,128)(2,1)S(1)}, u32[]{:S(2)}, u32[]{:S(2)}) collective-permute-start(bf16[256,1024]{1,0:T(8,128)(2,1)} %after.17), channel_id=1, source_target_pairs={{0,4},{4,8},{8,12},{12,0},{1,5},{5,9},{9,13},{13,1},{2,6},{6,10},{... | collective-permute-start | bytes 1572872 | tf_op jit(solution)/shard_map/ppermute | solution.py:22
  21.2 1.5 %collective-permute-start.9 = (bf16[1,64,1024]{2,1,0:T(8,128)(2,1)S(1)}, bf16[1,64,1024]{2,1,0:T(8,128)(2,1)S(1)}, u32[]{:S(2)}, u32[]{:S(2)}) collective-permute-start(bf16[1,64,1024]{2,1,0:T(8,128)(2,1)S(1)} %collective-permute-done.4.rest_0_.refs_2_.refs_1_), channel_id=1, source_target_pairs={{0,16},{16,0},{1,17},{17,1},{2,18},{18,2},{3,19},{19,3},{4,20},{20... | collective-permute-start | bytes 393224 | tf_op jit(solution)/shard_map/ppermute | solution.py:22
  22.7 0.5 collective-permute-start.10
  23.2 1.5 %collective-permute-start.11 = (bf16[1,64,1024]{2,1,0:T(8,128)(2,1)S(1)}, bf16[1,64,1024]{2,1,0:T(8,128)(2,1)S(1)}, u32[]{:S(2)}, u32[]{:S(2)}) collective-permute-start(bf16[1,64,1024]{2,1,0:T(8,128)(2,1)S(1)} %collective-permute-done.6.rest_2_.refs_4_.refs_3_), channel_id=1, source_target_pairs={{0,16},{16,0},{1,17},{17,1},{2,18},{18,2},{3,19},{19,3},{4,20},{20... | collective-permute-start | bytes 393224 | tf_op jit(solution)/shard_map/ppermute | solution.py:22
  24.7 1.6 %collective-permute-start.23 = (bf16[128,1024]{1,0:T(8,128)(2,1)}, bf16[128,1024]{1,0:T(8,128)(2,1)S(1)}, u32[]{:S(2)}, u32[]{:S(2)}) collective-permute-start(bf16[128,1024]{1,0:T(8,128)(2,1)} %after.23), channel_id=1, source_target_pairs={{0,8},{4,12},{8,0},{12,4},{1,9},{5,13},{9,1},{13,5},{2,10},{6,14},... | collective-permute-start | bytes 786440 | tf_op jit(solution)/shard_map/ppermute | solution.py:26
  26.4 0.8 row_table.1
  27.2 3.4 %copy-done = bf16[1,4096,1024]{2,1,0:T(8,128)(2,1)S(1)} copy-done((bf16[1,4096,1024]{2,1,0:T(8,128)(2,1)S(1)}, bf16[1,4096,1024]{2,1,0:T(8,128)(2,1)}, u32[]{:S(2)}) %copy-start) | copy-done | bytes 8388632
  30.6 2.5 %fetch.1 = (bf16[2048,1024]{1,0:T(8,128)(2,1)S(1)}, bf16[2048,1024]{1,0:T(8,128)(2,1)S(1)}) custom-call(s32[1]{0:T(128)} %bitcast.3.block_ref, bf16[4096,1024]{1,0:T(8,128)(2,1)S(1)} %bitcast.7, bf16[4096,1024]{1,0:T(8,128)(2,1)} %collective-permute-done.7.refs_1_, bf16[1,64,1024]{2,1,0:T(8,128)(2,1)S(1)} %collective-permute-done.4.rest_0_.refs_2_.refs_1_, ...), custom_call_target="tpu_custom_call" | custom-call | flops 1 | bytes 1 | tf_op jit(solution)/shard_map/fetch/pallas_call | solution.py:325
  33.2 1.2 %join_queries.1 = (bf16[128,256]{1,0:T(8,128)(2,1)S(1)}, bf16[128,256]{1,0:T(8,128)(2,1)S(1)}, bf16[128,256]{1,0:T(8,128)(2,1)S(1)}, bf16[128,256]{1,0:T(8,128)(...) custom-call(s32[4,4]{1,0:T(4,128)S(1)} %copy-done.12, ...), custom_call_target="tpu_custom_call" | custom-call | flops 1 | bytes 1 | tf_op jit(solution)/shard_map/join_queries/pallas_call | solution.py:153
  34.5 0.5 collective-permute-start.13
  35.1 0.7 collective-permute-done.12.refs_10_
  36.4 0.6 collective-permute-done.15.refs_13_
  37.5 0.7 collective-permute-done.18.refs_16_
  38.4 2.3 %fetched_weights.1.refs_18_.refs_2_.refs_3_ = bf16[2048,256]{1,0:T(8,128)(2,1)S(1)} custom-call(bf16[2048,1024]{1,0:T(8,128)(2,1)S(1)} %get-tuple-element.55.refs_8_.refs_0_, bf16[2048,1024]{1,0:T(8,128)(2,1)S(1)} %get-tuple-element.56.refs_9_.refs_1_, bf16[128,256]{1,0:T(8,128)(2,1)S(1)} %get-tuple-element.58.refs_2_, ...), custom_call_target="tpu_custom_call" | custom-call | flops 1 | bytes 1 | tf_op jit(solution)/shard_map/fetched_weights/pallas_call | solution.py:352
  40.8 4.6 %collective-permute-done.23.refs_1_.refs_0_.refs_2_ = bf16[128,1024]{1,0:T(8,128)(2,1)S(1)} collective-permute-done((bf16[128,1024]{1,0:T(8,128)(2,1)}, bf16[128,1024]{1,0:T(8,128)(2,1)S(1)}, u32[]{:S(2)}, u32[]{:S(2)}) %collective-permute-start.23) | collective-permute-done | bytes 262176 | tf_op jit(solution)/shard_map/ppermute | solution.py:26
  45.3 0.8 stack.3
  46.2 1.5 %collective-permute-start.20 = (bf16[2048,256]{1,0:T(8,128)(2,1)S(1)}, bf16[2048,256]{1,0:T(8,128)(2,1)}, u32[]{:S(2)}, u32[]{:S(2)}) collective-permute-start(bf16[2048,256]{1,0:T(8,128)(2,1)S(1)} %fetched_weights.1.refs_18_.refs_2_.refs_3_), channel_id=1, source_target_pairs={{0,2},{2,0},{1,3},{3,1},{4,6},{6,4},{5,7},{7,5},{8,10},{10,8},{9,1... | collective-permute-start | bytes 3145736 | tf_op jit(solution)/shard_map/ppermute | solution.py:22
  47.7 2.3 %collective-permute-start.29 = (bf16[256,1024]{1,0:T(8,128)(2,1)}, bf16[256,1024]{1,0:T(8,128)(2,1)}, u32[]{:S(2)}, u32[]{:S(2)}) collective-permute-start(bf16[256,1024]{1,0:T(8,128)(2,1)} %after.27), channel_id=1, source_target_pairs={{0,8},{4,12},{8,0},{12,4},{1,9},{5,13},{9,1},{13,5},{2,10},{6,14},... | collective-permute-start | bytes 1572872 | tf_op jit(solution)/shard_map/ppermute | solution.py:22
  50.0 1.5 %collective-permute-start.22 = (s32[8,128]{1,0:T(8,128)S(1)}, s32[8,128]{1,0:T(8,128)S(1)}, u32[]{:S(2)}, u32[]{:S(2)}) collective-permute-start(s32[8,128]{1,0:T(8,128)S(1)} %get-tuple-element.57.refs_10_), channel_id=1, source_target_pairs={{0,16},{16,0},{1,17},{17,1},{2,18},{18,2},{3,19},{19,3},{4,20},{20... | collective-permute-start | bytes 12296 | tf_op jit(solution)/shard_map/ppermute | solution.py:22
  51.5 2.1 %collective-permute-done.22 = s32[8,128]{1,0:T(8,128)S(1)} collective-permute-done((s32[8,128]{1,0:T(8,128)S(1)}, s32[8,128]{1,0:T(8,128)S(1)}, u32[]{:S(2)}, u32[]{:S(2)}) %collective-permute-start.22) | collective-permute-done | bytes 4128 | tf_op jit(solution)/shard_map/ppermute | solution.py:22
  53.6 0.5 slice.3
  54.8 6.6 %partial_weights.1.rest_0_.refs_1_.refs_2_.refs_0_ = f32[2048,256]{1,0:T(8,128)S(1)} custom-call(s32[1]{0:T(128)} %bitcast.1.block_ref, bf16[4096,1024]{1,0:T(8,128)(2,1)S(1)} %bitcast.10, bf16[4096,1024]{1,0:T(8,128)(2,1)} %collective-permute-done.7.refs_1_, bf16[128,256]{1,0:T(8,128)(2,1)S(1)} %get-tuple-element.58.refs_2_, ...), custom_call_target="tpu_custom_call" | custom-call | flops 1 | bytes 1 | tf_op jit(solution)/shard_map/partial_weights/pallas_call | solution.py:292
  61.8 0.5 collective-permute-start.26
  62.3 1.2 %copy-done.5 = bf16[128,1024]{1,0:T(8,128)(2,1)S(1)} copy-done((bf16[128,1024]{1,0:T(8,128)(2,1)S(1)}, bf16[128,1024]{1,0:T(8,128)(2,1)}, u32[]{:S(2)}) %copy-start.5) | copy-done | bytes 262168
  63.9 2.4 %own_rows.1.refs_2_ = bf16[256,2048]{1,0:T(8,128)(2,1)S(1)} custom-call(s32[8,128]{1,0:T(8,128)S(1)} %copy-done.13, bf16[1024,2048]{1,0:T(8,128)(2,1)S(1)} %copy-done.1, f32[2048,256]{1,0:T(8,128)S(1)} %partial_weights.1.rest_0_.refs_1_.refs_2_.refs_0_), custom_call_target="tpu_custom_call" | custom-call | flops 1 | bytes 1 | tf_op jit(solution)/shard_map/own_rows/pallas_call | solution.py:194
  66.4 0.8 copy-done.7
  67.3 1.7 %collective-permute-done.24.refs_8_.refs_0_ = bf16[256,1024]{1,0:T(8,128)(2,1)} collective-permute-done((bf16[256,1024]{1,0:T(8,128)(2,1)}, bf16[256,1024]{1,0:T(8,128)(2,1)}, u32[]{:S(2)}, u32[]{:S(2)}) %collective-permute-start.24) | collective-permute-done | bytes 524320 | tf_op jit(solution)/shard_map/ppermute | solution.py:26
  69.0 0.5 collective-permute-start.31
  69.5 0.7 collective-permute-done.27.refs_1_
  70.3 3.4 %collective-permute-done.29.refs_0_ = bf16[256,1024]{1,0:T(8,128)(2,1)} collective-permute-done((bf16[256,1024]{1,0:T(8,128)(2,1)}, bf16[256,1024]{1,0:T(8,128)(2,1)}, u32[]{:S(2)}, u32[]{:S(2)}) %collective-permute-start.29) | collective-permute-done | bytes 524320 | tf_op jit(solution)/shard_map/ppermute | solution.py:22
  73.7 1.5 %collective-permute-start.33 = (bf16[64,1024]{1,0:T(8,128)(2,1)S(1)}, bf16[64,1024]{1,0:T(8,128)(2,1)S(1)}, u32[]{:S(2)}, u32[]{:S(2)}) collective-permute-start(bf16[64,1024]{1,0:T(8,128)(2,1)S(1)} %after.18.refs_3_), channel_id=1, source_target_pairs={{0,12},{4,0},{8,4},{12,8},{1,13},{5,1},{9,5},{13,9},{2,14},{6,2},{... | collective-permute-start | bytes 393224 | tf_op jit(solution)/shard_map/ppermute | solution.py:22
  75.4 3.3 %collective-permute-start.39 = (bf16[64,1024]{1,0:T(8,128)(2,1)S(1)}, bf16[64,1024]{1,0:T(8,128)(2,1)S(1)}, u32[]{:S(2)}, u32[]{:S(2)}) collective-permute-start(bf16[64,1024]{1,0:T(8,128)(2,1)S(1)} %after.21.refs_6_), channel_id=1, source_target_pairs={{0,12},{4,0},{8,4},{12,8},{1,13},{5,1},{9,5},{13,9},{2,14},{6,2},{... | collective-permute-start | bytes 393224 | tf_op jit(solution)/shard_map/ppermute | solution.py:22
  78.7 5.1 %early_scores.1 = (bf16[2048,256]{1,0:T(8,128)(2,1)S(1)}, bf16[2048,256]{1,0:T(8,128)(2,1)S(1)}, f32[1024,128]{1,0:T(8,128)S(1)}, bf16[1024,128]{1,0:T(8,128)(2,1)S(1)}) custom-call(s32[4,4]{1,0:T(4,128)S(1)} %get-tuple-element.53.table_ref, f32[2048,256]{1,0:T(8,128)S(1)} %partial_weights.1.rest_0_.refs_1_.refs_2_.refs_0_, ...), custom_call_target="tpu_custom_call" | custom-call | flops 1 | bytes 1 | tf_op jit(solution)/shard_map/early_scores/pallas_call | solution.py:509
  83.8 0.6 collective-permute-start.32
  84.4 0.5 collective-permute-start.36
  84.9 0.7 collective-permute-done.37.refs_0_
  85.6 2.4 %collective-permute-done.39.refs_0_ = bf16[64,1024]{1,0:T(8,128)(2,1)S(1)} collective-permute-done((bf16[64,1024]{1,0:T(8,128)(2,1)S(1)}, bf16[64,1024]{1,0:T(8,128)(2,1)S(1)}, u32[]{:S(2)}, u32[]{:S(2)}) %collective-permute-start.39) | collective-permute-done | bytes 131104 | tf_op jit(solution)/shard_map/ppermute | solution.py:22
  88.1 1.3 %collective-permute-done.40.refs_7_ = bf16[64,1024]{1,0:T(8,128)(2,1)S(1)} collective-permute-done((bf16[64,1024]{1,0:T(8,128)(2,1)S(1)}, bf16[64,1024]{1,0:T(8,128)(2,1)S(1)}, u32[]{:S(2)}, u32[]{:S(2)}) %collective-permute-start.40) | collective-permute-done | bytes 131104 | tf_op jit(solution)/shard_map/ppermute | solution.py:22
  89.4 0.7 late_scores.1
  90.2 0.6 collective-permute-start.41
  90.8 3.7 %collective-permute-done.41.refs_3_ = bf16[256,128]{1,0:T(8,128)(2,1)S(1)} collective-permute-done((bf16[256,128]{1,0:T(8,128)(2,1)S(1)}, bf16[256,128]{1,0:T(8,128)(2,1)S(1)}, u32[]{:S(2)}, u32[]{:S(2)}) %collective-permute-start.41) | collective-permute-done | bytes 65568 | tf_op jit(solution)/shard_map/ppermute | solution.py:22
  94.5 1.7 %merge.1 = f32[128,1024]{1,0:T(8,128)} custom-call(s32[4,4]{1,0:T(4,128)S(1)} %get-tuple-element.53.table_ref, f32[1024,128]{1,0:T(8,128)S(1)} %get-tuple-element.88.refs_0_, bf16[1024,128]{1,0:T(8,128)(2,1)S(1)} %collective-permute-done.32.refs_1_, f32[256,128]{1,0:T(8,128)S(1)} %get-tuple-element.92.refs_2_, ...), custom_call_target="tpu_custom_call" | custom-call | flops 1 | bytes 1 | tf_op jit(solution)/shard_map/merge/pallas_call | solution.py:571
  (101 shorter events, 3.5 us)
Async XLA Ops:
  0.0 26.4 %copy-start.11 = (s32[4096]{0:T(1024)S(1)}, s32[4096]{0:T(1024)}, u32[]{:S(2)}) copy-start(s32[4096]{0:T(1024)} %param.9) | copy-start | bytes 49156
  0.0 24.7 %collective-permute-start.7 = (bf16[4096,1024]{1,0:T(8,128)(2,1)}, bf16[4096,1024]{1,0:T(8,128)(2,1)}, u32[]{:S(2)}, u32[]{:S(2)}) collective-permute-start(bf16[4096,1024]{1,0:T(8,128)(2,1)} %bitcast.6), channel_id=1, source_target_pairs={{0,1},{1,0},{2,3},{3,2},{4,5},{5,4},{6,7},{7,6},{8,9},{9,8},{10,11... | collective-permute-start | bytes 25165832 | tf_op jit(solution)/shard_map/ppermute | solution.py:22
  3.1 14.5 %collective-permute-start.4 = (bf16[1,64,1024]{2,1,0:T(8,128)(2,1)}, bf16[1,64,1024]{2,1,0:T(8,128)(2,1)S(1)}, u32[]{:S(2)}, u32[]{:S(2)}) collective-permute-start(bf16[1,64,1024]{2,1,0:T(8,128)(2,1)} %get-tuple-element.50), channel_id=1, source_target_pairs={{0,4},{4,8},{8,12},{12,0},{1,5},{5,9},{9,13},{13,1},{2,6},{6,10},{... | collective-permute-start | bytes 393224 | tf_op jit(solution)/shard_map/ppermute | solution.py:22
  5.9 12.0 %collective-permute-start.5 = (bf16[1,64,1024]{2,1,0:T(8,128)(2,1)}, bf16[1,64,1024]{2,1,0:T(8,128)(2,1)S(1)}, u32[]{:S(2)}, u32[]{:S(2)}) collective-permute-start(bf16[1,64,1024]{2,1,0:T(8,128)(2,1)} %get-tuple-element.51), channel_id=1, source_target_pairs={{0,8},{4,12},{8,0},{12,4},{1,9},{5,13},{9,1},{13,5},{2,10},{6,14},... | collective-permute-start | bytes 393224 | tf_op jit(solution)/shard_map/ppermute | solution.py:22
  8.5 9.4 %collective-permute-start.6 = (bf16[1,64,1024]{2,1,0:T(8,128)(2,1)}, bf16[1,64,1024]{2,1,0:T(8,128)(2,1)S(1)}, u32[]{:S(2)}, u32[]{:S(2)}) collective-permute-start(bf16[1,64,1024]{2,1,0:T(8,128)(2,1)} %get-tuple-element.52), channel_id=1, source_target_pairs={{0,12},{4,0},{8,4},{12,8},{1,13},{5,1},{9,5},{13,9},{2,14},{6,2},{... | collective-permute-start | bytes 393224 | tf_op jit(solution)/shard_map/ppermute | solution.py:22
  9.9 13.3 %collective-permute-start.8 = (bf16[1,64,1024]{2,1,0:T(8,128)(2,1)}, bf16[1,64,1024]{2,1,0:T(8,128)(2,1)S(1)}, u32[]{:S(2)}, u32[]{:S(2)}) collective-permute-start(bf16[1,64,1024]{2,1,0:T(8,128)(2,1)} %get-tuple-element.54.refs_0_), channel_id=1, source_target_pairs={{0,16},{16,0},{1,17},{17,1},{2,18},{18,2},{3,19},{19,3},{4,20},{20... | collective-permute-start | bytes 393224 | tf_op jit(solution)/shard_map/ppermute | solution.py:22
  17.9 29.8 %collective-permute-start.21 = (bf16[256,1024]{1,0:T(8,128)(2,1)}, bf16[256,1024]{1,0:T(8,128)(2,1)S(1)}, u32[]{:S(2)}, u32[]{:S(2)}) collective-permute-start(bf16[256,1024]{1,0:T(8,128)(2,1)} %after.17), channel_id=1, source_target_pairs={{0,4},{4,8},{8,12},{12,0},{1,5},{5,9},{9,13},{13,1},{2,6},{6,10},{... | collective-permute-start | bytes 1572872 | tf_op jit(solution)/shard_map/ppermute | solution.py:22
  21.2 12.0 %collective-permute-start.9 = (bf16[1,64,1024]{2,1,0:T(8,128)(2,1)S(1)}, bf16[1,64,1024]{2,1,0:T(8,128)(2,1)S(1)}, u32[]{:S(2)}, u32[]{:S(2)}) collective-permute-start(bf16[1,64,1024]{2,1,0:T(8,128)(2,1)S(1)} %collective-permute-done.4.rest_0_.refs_2_.refs_1_), channel_id=1, source_target_pairs={{0,16},{16,0},{1,17},{17,1},{2,18},{18,2},{3,19},{19,3},{4,20},{20... | collective-permute-start | bytes 393224 | tf_op jit(solution)/shard_map/ppermute | solution.py:22
  22.7 10.4 %collective-permute-start.10 = (bf16[1,64,1024]{2,1,0:T(8,128)(2,1)S(1)}, bf16[1,64,1024]{2,1,0:T(8,128)(2,1)S(1)}, u32[]{:S(2)}, u32[]{:S(2)}) collective-permute-start(bf16[1,64,1024]{2,1,0:T(8,128)(2,1)S(1)} %collective-permute-done.5.rest_1_.refs_3_.refs_2_), channel_id=1, source_target_pairs={{0,16},{16,0},{1,17},{17,1},{2,18},{18,2},{3,19},{19,3},{4,20},{20... | collective-permute-start | bytes 393224 | tf_op jit(solution)/shard_map/ppermute | solution.py:22
  23.2 9.9 %collective-permute-start.11 = (bf16[1,64,1024]{2,1,0:T(8,128)(2,1)S(1)}, bf16[1,64,1024]{2,1,0:T(8,128)(2,1)S(1)}, u32[]{:S(2)}, u32[]{:S(2)}) collective-permute-start(bf16[1,64,1024]{2,1,0:T(8,128)(2,1)S(1)} %collective-permute-done.6.rest_2_.refs_4_.refs_3_), channel_id=1, source_target_pairs={{0,16},{16,0},{1,17},{17,1},{2,18},{18,2},{3,19},{19,3},{4,20},{20... | collective-permute-start | bytes 393224 | tf_op jit(solution)/shard_map/ppermute | solution.py:22
  24.7 20.6 %collective-permute-start.23 = (bf16[128,1024]{1,0:T(8,128)(2,1)}, bf16[128,1024]{1,0:T(8,128)(2,1)S(1)}, u32[]{:S(2)}, u32[]{:S(2)}) collective-permute-start(bf16[128,1024]{1,0:T(8,128)(2,1)} %after.23), channel_id=1, source_target_pairs={{0,8},{4,12},{8,0},{12,4},{1,9},{5,13},{9,1},{13,5},{2,10},{6,14},... | collective-permute-start | bytes 786440 | tf_op jit(solution)/shard_map/ppermute | solution.py:26
  27.2 3.4 %copy-start = (bf16[1,4096,1024]{2,1,0:T(8,128)(2,1)S(1)}, bf16[1,4096,1024]{2,1,0:T(8,128)(2,1)}, u32[]{:S(2)}) copy-start(bf16[1,4096,1024]{2,1,0:T(8,128)(2,1)} %param.10) | copy-start | bytes 25165828
  30.6 2.6 %copy-start.12 = (s32[4,4]{1,0:T(4,128)S(1)}, s32[4,4]{1,0:T(4,128)}, u32[]{:S(2)}) copy-start(s32[4,4]{1,0:T(4,128)} %pattern_ref.3) | copy-start | bytes 196
  30.6 2.6 %copy-start.14 = (s32[16]{0:T(128)S(1)}, s32[16]{0:T(128)}, u32[]{:S(2)}) copy-start(s32[16]{0:T(128)} %slot_ref.3) | copy-start | bytes 196
  34.4 1.3 %collective-permute-start.12 = (bf16[128,256]{1,0:T(8,128)(2,1)S(1)}, bf16[128,256]{1,0:T(8,128)(2,1)S(1)}, u32[]{:S(2)}, u32[]{:S(2)}) collective-permute-start(bf16[128,256]{1,0:T(8,128)(2,1)S(1)} %get-tuple-element.66), channel_id=1, source_target_pairs={{0,1},{1,0},{2,3},{3,2},{4,5},{5,4},{6,7},{7,6},{8,9},{9,8},{10,11... | collective-permute-start | bytes 196616 | tf_op jit(solution)/shard_map/ppermute | solution.py:22
  34.5 1.4 %collective-permute-start.13 = (bf16[128,256]{1,0:T(8,128)(2,1)S(1)}, bf16[128,256]{1,0:T(8,128)(2,1)S(1)}, u32[]{:S(2)}, u32[]{:S(2)}) collective-permute-start(bf16[128,256]{1,0:T(8,128)(2,1)S(1)} %get-tuple-element.67), channel_id=1, source_target_pairs={{0,1},{1,0},{2,3},{3,2},{4,5},{5,4},{6,7},{7,6},{8,9},{9,8},{10,11... | collective-permute-start | bytes 196616 | tf_op jit(solution)/shard_map/ppermute | solution.py:22
  35.0 1.3 %collective-permute-start.14 = (bf16[128,256]{1,0:T(8,128)(2,1)S(1)}, bf16[128,256]{1,0:T(8,128)(2,1)S(1)}, u32[]{:S(2)}, u32[]{:S(2)}) collective-permute-start(bf16[128,256]{1,0:T(8,128)(2,1)S(1)} %get-tuple-element.68), channel_id=1, source_target_pairs={{0,1},{1,0},{2,3},{3,2},{4,5},{5,4},{6,7},{7,6},{8,9},{9,8},{10,11... | collective-permute-start | bytes 196616 | tf_op jit(solution)/shard_map/ppermute | solution.py:22
  35.7 1.3 %collective-permute-start.15 = (bf16[128,256]{1,0:T(8,128)(2,1)S(1)}, bf16[128,256]{1,0:T(8,128)(2,1)S(1)}, u32[]{:S(2)}, u32[]{:S(2)}) collective-permute-start(bf16[128,256]{1,0:T(8,128)(2,1)S(1)} %get-tuple-element.69), channel_id=1, source_target_pairs={{0,1},{1,0},{2,3},{3,2},{4,5},{5,4},{6,7},{7,6},{8,9},{9,8},{10,11... | collective-permute-start | bytes 196616 | tf_op jit(solution)/shard_map/ppermute | solution.py:22
  35.9 1.3 %collective-permute-start.16 = (bf16[128,256]{1,0:T(8,128)(2,1)S(1)}, bf16[128,256]{1,0:T(8,128)(2,1)S(1)}, u32[]{:S(2)}, u32[]{:S(2)}) collective-permute-start(bf16[128,256]{1,0:T(8,128)(2,1)S(1)} %get-tuple-element.70), channel_id=1, source_target_pairs={{0,1},{1,0},{2,3},{3,2},{4,5},{5,4},{6,7},{7,6},{8,9},{9,8},{10,11... | collective-permute-start | bytes 196616 | tf_op jit(solution)/shard_map/ppermute | solution.py:22
  36.3 1.3 %collective-permute-start.17 = (bf16[128,256]{1,0:T(8,128)(2,1)S(1)}, bf16[128,256]{1,0:T(8,128)(2,1)S(1)}, u32[]{:S(2)}, u32[]{:S(2)}) collective-permute-start(bf16[128,256]{1,0:T(8,128)(2,1)S(1)} %get-tuple-element.71), channel_id=1, source_target_pairs={{0,1},{1,0},{2,3},{3,2},{4,5},{5,4},{6,7},{7,6},{8,9},{9,8},{10,11... | collective-permute-start | bytes 196616 | tf_op jit(solution)/shard_map/ppermute | solution.py:22
  37.0 1.3 %collective-permute-start.18 = (bf16[128,256]{1,0:T(8,128)(2,1)S(1)}, bf16[128,256]{1,0:T(8,128)(2,1)S(1)}, u32[]{:S(2)}, u32[]{:S(2)}) collective-permute-start(bf16[128,256]{1,0:T(8,128)(2,1)S(1)} %get-tuple-element.72), channel_id=1, source_target_pairs={{0,1},{1,0},{2,3},{3,2},{4,5},{5,4},{6,7},{7,6},{8,9},{9,8},{10,11... | collective-permute-start | bytes 196616 | tf_op jit(solution)/shard_map/ppermute | solution.py:22
  37.2 1.3 %collective-permute-start.19 = (bf16[128,256]{1,0:T(8,128)(2,1)S(1)}, bf16[128,256]{1,0:T(8,128)(2,1)S(1)}, u32[]{:S(2)}, u32[]{:S(2)}) collective-permute-start(bf16[128,256]{1,0:T(8,128)(2,1)S(1)} %get-tuple-element.73), channel_id=1, source_target_pairs={{0,1},{1,0},{2,3},{3,2},{4,5},{5,4},{6,7},{7,6},{8,9},{9,8},{10,11... | collective-permute-start | bytes 196616 | tf_op jit(solution)/shard_map/ppermute | solution.py:22
  38.4 16.4 %slice-start = ((s8[8388608]{0:T(1024)(128)(4,1)}), s8[4194304]{0:T(1024)(128)(4,1)S(1)}, s32[]{:S(2)}) async-start(s8[8388608]{0:T(1024)(128)(4,1)} %bitcast.8), calls=%async_computation | async-start | bytes 8388608
  38.4 6.9 %copy-start.4 = (bf16[128,1024]{1,0:T(8,128)(2,1)S(1)}, bf16[128,1024]{1,0:T(8,128)(2,1)}, u32[]{:S(2)}) copy-start(bf16[128,1024]{1,0:T(8,128)(2,1)} %get-tuple-element.82.refs_0_) | copy-start | bytes 786436
  38.4 16.4 %slice-start.1 = ((s8[8388608]{0:T(1024)(128)(4,1)}), s8[4194304]{0:T(1024)(128)(4,1)S(1)}, s32[]{:S(2)}) async-start(s8[8388608]{0:T(1024)(128)(4,1)} %bitcast.8), calls=%async_computation.1 | async-start | bytes 8388608
  46.2 22.8 %collective-permute-start.24 = (bf16[256,1024]{1,0:T(8,128)(2,1)}, bf16[256,1024]{1,0:T(8,128)(2,1)}, u32[]{:S(2)}, u32[]{:S(2)}) collective-permute-start(bf16[256,1024]{1,0:T(8,128)(2,1)} %stack.3), channel_id=1, source_target_pairs={{0,4},{4,0},{8,12},{12,8},{1,5},{5,1},{9,13},{13,9},{2,6},{6,2},{1... | collective-permute-start | bytes 1572872 | tf_op jit(solution)/shard_map/ppermute | solution.py:26
  46.2 29.0 %collective-permute-start.20 = (bf16[2048,256]{1,0:T(8,128)(2,1)S(1)}, bf16[2048,256]{1,0:T(8,128)(2,1)}, u32[]{:S(2)}, u32[]{:S(2)}) collective-permute-start(bf16[2048,256]{1,0:T(8,128)(2,1)S(1)} %fetched_weights.1.refs_18_.refs_2_.refs_3_), channel_id=1, source_target_pairs={{0,2},{2,0},{1,3},{3,1},{4,6},{6,4},{5,7},{7,5},{8,10},{10,8},{9,1... | collective-permute-start | bytes 3145736 | tf_op jit(solution)/shard_map/ppermute | solution.py:22
  47.7 7.1 %copy-start.2 = (bf16[256,1024]{1,0:T(8,128)(2,1)}, bf16[256,1024]{1,0:T(8,128)(2,1)S(1)}, u32[]{:S(2)}) copy-start(bf16[256,1024]{1,0:T(8,128)(2,1)S(1)} %collective-permute-done.21.refs_0_.refs_1_) | copy-start | bytes 1572868
  47.7 26.1 %collective-permute-start.29 = (bf16[256,1024]{1,0:T(8,128)(2,1)}, bf16[256,1024]{1,0:T(8,128)(2,1)}, u32[]{:S(2)}, u32[]{:S(2)}) collective-permute-start(bf16[256,1024]{1,0:T(8,128)(2,1)} %after.27), channel_id=1, source_target_pairs={{0,8},{4,12},{8,0},{12,4},{1,9},{5,13},{9,1},{13,5},{2,10},{6,14},... | collective-permute-start | bytes 1572872 | tf_op jit(solution)/shard_map/ppermute | solution.py:22
  50.0 3.6 %collective-permute-start.22 = (s32[8,128]{1,0:T(8,128)S(1)}, s32[8,128]{1,0:T(8,128)S(1)}, u32[]{:S(2)}, u32[]{:S(2)}) collective-permute-start(s32[8,128]{1,0:T(8,128)S(1)} %get-tuple-element.57.refs_10_), channel_id=1, source_target_pairs={{0,16},{16,0},{1,17},{17,1},{2,18},{18,2},{3,19},{19,3},{4,20},{20... | collective-permute-start | bytes 12296 | tf_op jit(solution)/shard_map/ppermute | solution.py:22
  54.8 6.6 %copy-start.15 = (bf16[128,1024]{1,0:T(8,128)(2,1)S(1)}, bf16[128,1024]{1,0:T(8,128)(2,1)}, u32[]{:S(2)}) copy-start(bf16[128,1024]{1,0:T(8,128)(2,1)} %get-tuple-element.80.refs_0_) | copy-start | bytes 786436
  61.7 5.6 %collective-permute-start.25 = (bf16[128,1024]{1,0:T(8,128)(2,1)}, bf16[128,1024]{1,0:T(8,128)(2,1)S(1)}, u32[]{:S(2)}, u32[]{:S(2)}) collective-permute-start(bf16[128,1024]{1,0:T(8,128)(2,1)} %get-tuple-element.82.refs_0_), channel_id=1, source_target_pairs={{0,1},{1,0},{2,3},{3,2},{4,5},{5,4},{6,7},{7,6},{8,9},{9,8},{10,11... | collective-permute-start | bytes 786440 | tf_op jit(solution)/shard_map/ppermute | solution.py:22
  61.8 5.5 %collective-permute-start.26 = (bf16[128,1024]{1,0:T(8,128)(2,1)S(1)}, bf16[128,1024]{1,0:T(8,128)(2,1)S(1)}, u32[]{:S(2)}, u32[]{:S(2)}) collective-permute-start(bf16[128,1024]{1,0:T(8,128)(2,1)S(1)} %after.24.refs_1_), channel_id=1, source_target_pairs={{0,1},{1,0},{2,3},{3,2},{4,5},{5,4},{6,7},{7,6},{8,9},{9,8},{10,11... | collective-permute-start | bytes 786440 | tf_op jit(solution)/shard_map/ppermute | solution.py:22
  63.5 2.8 %copy-start.9 = (bf16[64,1024]{1,0:T(8,128)(2,1)S(1)}, bf16[64,1024]{1,0:T(8,128)(2,1)}, u32[]{:S(2)}) copy-start(bf16[64,1024]{1,0:T(8,128)(2,1)} %get-tuple-element.76.refs_0_) | copy-start | bytes 393220
  69.0 1.2 %collective-permute-start.27 = (s32[8,128]{1,0:T(8,128)S(1)}, s32[8,128]{1,0:T(8,128)S(1)}, u32[]{:S(2)}, u32[]{:S(2)}) collective-permute-start(s32[8,128]{1,0:T(8,128)S(1)} %after.25), channel_id=1, source_target_pairs={{0,1},{1,0},{2,3},{3,2},{4,5},{5,4},{6,7},{7,6},{8,9},{9,8},{10,11... | collective-permute-start | bytes 12296 | tf_op jit(solution)/shard_map/ppermute | solution.py:22
  69.0 6.2 %collective-permute-start.31 = (bf16[256,1024]{1,0:T(8,128)(2,1)}, bf16[256,1024]{1,0:T(8,128)(2,1)S(1)}, u32[]{:S(2)}, u32[]{:S(2)}) collective-permute-start(bf16[256,1024]{1,0:T(8,128)(2,1)} %after.29.refs_9_), channel_id=1, source_target_pairs={{0,1},{1,0},{2,3},{3,2},{4,5},{5,4},{6,7},{7,6},{8,9},{9,8},{10,11... | collective-permute-start | bytes 1572872 | tf_op jit(solution)/shard_map/ppermute | solution.py:22
  70.2 5.2 %collective-permute-start.28 = (bf16[256,1024]{1,0:T(8,128)(2,1)S(1)}, bf16[256,1024]{1,0:T(8,128)(2,1)S(1)}, u32[]{:S(2)}, u32[]{:S(2)}) collective-permute-start(bf16[256,1024]{1,0:T(8,128)(2,1)S(1)} %after.26.refs_3_), channel_id=1, source_target_pairs={{0,1},{1,0},{2,3},{3,2},{4,5},{5,4},{6,7},{7,6},{8,9},{9,8},{10,11... | collective-permute-start | bytes 1572872 | tf_op jit(solution)/shard_map/ppermute | solution.py:22
  73.7 5.0 %collective-permute-start.30 = (bf16[256,1024]{1,0:T(8,128)(2,1)}, bf16[256,1024]{1,0:T(8,128)(2,1)S(1)}, u32[]{:S(2)}, u32[]{:S(2)}) collective-permute-start(bf16[256,1024]{1,0:T(8,128)(2,1)} %after.28.refs_5_), channel_id=1, source_target_pairs={{0,1},{1,0},{2,3},{3,2},{4,5},{5,4},{6,7},{7,6},{8,9},{9,8},{10,11... | collective-permute-start | bytes 1572872 | tf_op jit(solution)/shard_map/ppermute | solution.py:22
  73.7 10.7 %collective-permute-start.33 = (bf16[64,1024]{1,0:T(8,128)(2,1)S(1)}, bf16[64,1024]{1,0:T(8,128)(2,1)S(1)}, u32[]{:S(2)}, u32[]{:S(2)}) collective-permute-start(bf16[64,1024]{1,0:T(8,128)(2,1)S(1)} %after.18.refs_3_), channel_id=1, source_target_pairs={{0,12},{4,0},{8,4},{12,8},{1,13},{5,1},{9,5},{13,9},{2,14},{6,2},{... | collective-permute-start | bytes 393224 | tf_op jit(solution)/shard_map/ppermute | solution.py:22
  75.2 9.2 %collective-permute-start.35 = (bf16[64,1024]{1,0:T(8,128)(2,1)S(1)}, bf16[64,1024]{1,0:T(8,128)(2,1)S(1)}, u32[]{:S(2)}, u32[]{:S(2)}) collective-permute-start(bf16[64,1024]{1,0:T(8,128)(2,1)S(1)} %after.19.refs_4_), channel_id=1, source_target_pairs={{0,12},{4,0},{8,4},{12,8},{1,13},{5,1},{9,5},{13,9},{2,14},{6,2},{... | collective-permute-start | bytes 393224 | tf_op jit(solution)/shard_map/ppermute | solution.py:22
  75.3 10.4 %collective-permute-start.37 = (bf16[64,1024]{1,0:T(8,128)(2,1)S(1)}, bf16[64,1024]{1,0:T(8,128)(2,1)S(1)}, u32[]{:S(2)}, u32[]{:S(2)}) collective-permute-start(bf16[64,1024]{1,0:T(8,128)(2,1)S(1)} %after.20.refs_5_), channel_id=1, source_target_pairs={{0,12},{4,0},{8,4},{12,8},{1,13},{5,1},{9,5},{13,9},{2,14},{6,2},{... | collective-permute-start | bytes 393224 | tf_op jit(solution)/shard_map/ppermute | solution.py:22
  75.4 12.7 %collective-permute-start.39 = (bf16[64,1024]{1,0:T(8,128)(2,1)S(1)}, bf16[64,1024]{1,0:T(8,128)(2,1)S(1)}, u32[]{:S(2)}, u32[]{:S(2)}) collective-permute-start(bf16[64,1024]{1,0:T(8,128)(2,1)S(1)} %after.21.refs_6_), channel_id=1, source_target_pairs={{0,12},{4,0},{8,4},{12,8},{1,13},{5,1},{9,5},{13,9},{2,14},{6,2},{... | collective-permute-start | bytes 393224 | tf_op jit(solution)/shard_map/ppermute | solution.py:22
  83.8 10.7 %collective-permute-start.32 = (bf16[1024,128]{1,0:T(8,128)(2,1)S(1)}, bf16[1024,128]{1,0:T(8,128)(2,1)S(1)}, u32[]{:S(2)}, u32[]{:S(2)}) collective-permute-start(bf16[1024,128]{1,0:T(8,128)(2,1)S(1)} %get-tuple-element.89.refs_1_), channel_id=1, source_target_pairs={{0,2},{2,0},{1,3},{3,1},{4,6},{6,4},{5,7},{7,5},{8,10},{10,8},{9,1... | collective-permute-start | bytes 786440 | tf_op jit(solution)/shard_map/ppermute | solution.py:22
  84.4 3.7 %collective-permute-start.34 = (bf16[64,1024]{1,0:T(8,128)(2,1)S(1)}, bf16[64,1024]{1,0:T(8,128)(2,1)S(1)}, u32[]{:S(2)}, u32[]{:S(2)}) collective-permute-start(bf16[64,1024]{1,0:T(8,128)(2,1)S(1)} %after.30.refs_0_), channel_id=1, source_target_pairs={{0,1},{1,0},{2,3},{3,2},{4,5},{5,4},{6,7},{7,6},{8,9},{9,8},{10,11... | collective-permute-start | bytes 393224 | tf_op jit(solution)/shard_map/ppermute | solution.py:22
  84.4 3.7 %collective-permute-start.36 = (bf16[64,1024]{1,0:T(8,128)(2,1)S(1)}, bf16[64,1024]{1,0:T(8,128)(2,1)S(1)}, u32[]{:S(2)}, u32[]{:S(2)}) collective-permute-start(bf16[64,1024]{1,0:T(8,128)(2,1)S(1)} %after.31.refs_2_), channel_id=1, source_target_pairs={{0,1},{1,0},{2,3},{3,2},{4,5},{5,4},{6,7},{7,6},{8,9},{9,8},{10,11... | collective-permute-start | bytes 393224 | tf_op jit(solution)/shard_map/ppermute | solution.py:22
  85.6 2.4 %collective-permute-start.38 = (bf16[64,1024]{1,0:T(8,128)(2,1)S(1)}, bf16[64,1024]{1,0:T(8,128)(2,1)S(1)}, u32[]{:S(2)}, u32[]{:S(2)}) collective-permute-start(bf16[64,1024]{1,0:T(8,128)(2,1)S(1)} %after.32.refs_4_), channel_id=1, source_target_pairs={{0,1},{1,0},{2,3},{3,2},{4,5},{5,4},{6,7},{7,6},{8,9},{9,8},{10,11... | collective-permute-start | bytes 393224 | tf_op jit(solution)/shard_map/ppermute | solution.py:22
  88.1 1.3 %collective-permute-start.40 = (bf16[64,1024]{1,0:T(8,128)(2,1)S(1)}, bf16[64,1024]{1,0:T(8,128)(2,1)S(1)}, u32[]{:S(2)}, u32[]{:S(2)}) collective-permute-start(bf16[64,1024]{1,0:T(8,128)(2,1)S(1)} %after.33.refs_6_), channel_id=1, source_target_pairs={{0,1},{1,0},{2,3},{3,2},{4,5},{5,4},{6,7},{7,6},{8,9},{9,8},{10,11... | collective-permute-start | bytes 393224 | tf_op jit(solution)/shard_map/ppermute | solution.py:22
  90.2 4.3 %collective-permute-start.41 = (bf16[256,128]{1,0:T(8,128)(2,1)S(1)}, bf16[256,128]{1,0:T(8,128)(2,1)S(1)}, u32[]{:S(2)}, u32[]{:S(2)}) collective-permute-start(bf16[256,128]{1,0:T(8,128)(2,1)S(1)} %get-tuple-element.93), channel_id=1, source_target_pairs={{0,2},{2,0},{1,3},{3,1},{4,6},{6,4},{5,7},{7,5},{8,10},{10,8},{9,1... | collective-permute-start | bytes 196616 | tf_op jit(solution)/shard_map/ppermute | solution.py:22
  (8 other events, 13.6 us)

commit v15 on v14

--- a/solution.py
+++ b/solution.py
@@ -613,6 +613,9 @@
     if extra:
         far = swap(after(packed[-2], *pieces[1:]), "shard", n_shard, 2)
         urgent.append(far)
+    sent_last = packed[len(middle):len(middle) + len(final)]
+    last = [shift(after(sent_last[0], *pieces[1:]), "shard", n_shard, last_hops)]
+    urgent.append(last[0])
     depth = n_rep * columns
     targets = [(feat + d) % n_feat for d in range(1, n_feat)]
     near_chip = fetch(matrices, targets[0], depth, *pieces[1:])
@@ -631,10 +634,11 @@
     for (hops, _, _), x in zip(middle[1:], packed[1:]):
         here.append(shift(after(x, *urgent, *sends), "shard", n_shard, hops))
         urgent = [here[-1]]
-    last = [after(x, own) for x in packed[len(middle):len(middle) + len(final)]]
+    sent_last = [after(x, own) for x in sent_last[1:]]
+    last_all = [with_rep(after(last[0], own))]
 
     mine = own_rows(goal, train, bulk, own)
-    marks = [own, mine, *last]
+    marks = [own, mine, *sent_last, *last_all[0][1:]]
     if extra:
         for d in range(1, n_group):
             flag = jnp.maximum(flag, shift(flag, "groups", n_group, d))
@@ -654,7 +658,7 @@
         marks += [seconds[0][0], near, *pairs]
 
     mark = shift(after(jnp.zeros((8, LANES), I32), *marks), "rep", n_rep, 1)
-    last = [shift(x, "shard", n_shard, last_hops) for x in last]
+    last += [shift(x, "shard", n_shard, last_hops) for x in sent_last]
     ready = [with_rep(after(x, mark)) for x in here]
     high, low, *early = early_scores(
         own, others, mine, ready, middle, firsts, seconds, table, rows, n_feat, n_rep, n_shard, bulk, extra
@@ -663,7 +667,8 @@
     def over_feat(shares):
         return [shares[0]] + [shift(shares[d], "feat", n_feat, d) for d in range(1, n_feat)]
 
-    late = late_scores([with_rep(after(x, *early[1:])) for x in last], high, low, n_feat)
+    last_all += [with_rep(after(x, *early[1:])) for x in last[1:]]
+    late = late_scores(last_all, high, low, n_feat)
     return merge(table, over_feat(early), over_feat(late), n_shard)[None]
 
 

time: 96.5 us -> 95.5 us (0.990)
  local copies, waits for them, and re-layouts: 6.5 us -> 5.05 us
  starting transfers between devices: 32.2 us -> 33.4 us
    ppermute x2, starting transfers between devices: 1.63 us -> 3.35 us  [swap(): return lax.ppermute(x, axis, [(i, i ^ bit) for i in range(size)])]
    ppermute x2, waiting for transfers between devices: 6.22 us -> 4.69 us  [swap(): return lax.ppermute(x, axis, [(i, i ^ bit) for i in range(size)])]
    unnamed x36, local copies, waits for them, and re-layouts: 5.96 us -> 4.53 us
  transfers between devices with their start and end apart: 38 -> 38, of which waited for: 14 -> 13; matrix products, arithmetic and copies ran while one was open for 1% -> 1% of each run, Pallas kernels for 33% -> 33%
where the time goes in v15:
time: 95.5 us; the launch traced here: 95.2 us
  starting transfers between devices  33.4 us (35%)
  Pallas kernels  33.3 us (35%)
  waiting for transfers between devices  22.3 us (23%)
  local copies, waits for them, and re-layouts  5.05 us (5%)
  between operations  1 us (1%)
    ppermute x36, starting transfers between devices, shift(): return lax.ppermute(x, axis, [(i, (i + by) % size) for i in range(size)])  30 us
    ppermute x36, waiting for transfers between devices, shift(): return lax.ppermute(x, axis, [(i, (i + by) % size) for i in range(size)])  17.6 us
    pallas_call x1, Pallas kernels, partial_weights(): pl.pallas_call(kernel, in_specs=[SMEM] + [HBM] * n + [VMEM] * (CUTS * n)...  6.6 us
    pallas_call x1, Pallas kernels, pack_rows(): pl.pallas_call(kernel, grid=(1,), in_specs=[pl.BlockSpec((lines, LANES),...  6.25 us
    pallas_call x1, Pallas kernels, early_scores(): pl.pallas_call(kernel, in_specs=[SMEM] + [VMEM] * (2 + n_other + n_rep *...  5.09 us
    ppermute x2, waiting for transfers between devices, swap(): return lax.ppermute(x, axis, [(i, i ^ bit) for i in range(size)])  4.69 us
    unnamed x36, local copies, waits for them, and re-layouts  4.53 us
    ppermute x2, starting transfers between devices, swap(): return lax.ppermute(x, axis, [(i, i ^ bit) for i in range(size)])  3.35 us
  transfers between devices with their start and end apart: 38, of which 13 were waited for; matrix products, arithmetic and copies ran while one was open for 1% of the time, Pallas kernels for 33%

profile of v15, /device:TPU:0, one launch (start us, length us, event | category | flops | bytes accessed | tf_op | source)
XLA Modules:
  0.0 95.2 jit_solution(5972554957102772533)
XLA Ops:
  0.0 0.5 collective-permute-start.7
  0.5 2.7 %pick_queries.1 = (bf16[1,64,1024]{2,1,0:T(8,128)(2,1)}, bf16[1,64,1024]{2,1,0:T(8,128)(2,1)}, bf16[1,64,1024]{2,1,0:T(8,128)(2,1)}, bf16[1,64,1024]{2,1,0:T(8,128)(2,1)}) custom-call(s32[4,4]{1,0:T(4,128)} %pattern_ref.3, s32[16]{0:T(128)} %slot_ref.3, bf16[4,128,1024]{2,1,0:T(8,128)(2,1)} %in_ref.1), custom_call_target="tpu_custom_call" | custom-call | flops 1 | bytes 1 | tf_op jit(solution)/shard_map/pick_queries/pallas_call | solution.py:108
  3.2 2.8 %collective-permute-start.4 = (bf16[1,64,1024]{2,1,0:T(8,128)(2,1)}, bf16[1,64,1024]{2,1,0:T(8,128)(2,1)S(1)}, u32[]{:S(2)}, u32[]{:S(2)}) collective-permute-start(bf16[1,64,1024]{2,1,0:T(8,128)(2,1)} %get-tuple-element.50), channel_id=1, source_target_pairs={{0,4},{4,8},{8,12},{12,0},{1,5},{5,9},{9,13},{13,1},{2,6},{6,10},{... | collective-permute-start | bytes 393224 | tf_op jit(solution)/shard_map/ppermute | solution.py:22
  5.9 2.6 %collective-permute-start.5 = (bf16[1,64,1024]{2,1,0:T(8,128)(2,1)}, bf16[1,64,1024]{2,1,0:T(8,128)(2,1)S(1)}, u32[]{:S(2)}, u32[]{:S(2)}) collective-permute-start(bf16[1,64,1024]{2,1,0:T(8,128)(2,1)} %get-tuple-element.51), channel_id=1, source_target_pairs={{0,8},{4,12},{8,0},{12,4},{1,9},{5,13},{9,1},{13,5},{2,10},{6,14},... | collective-permute-start | bytes 393224 | tf_op jit(solution)/shard_map/ppermute | solution.py:22
  8.5 1.3 %collective-permute-start.6 = (bf16[1,64,1024]{2,1,0:T(8,128)(2,1)}, bf16[1,64,1024]{2,1,0:T(8,128)(2,1)S(1)}, u32[]{:S(2)}, u32[]{:S(2)}) collective-permute-start(bf16[1,64,1024]{2,1,0:T(8,128)(2,1)} %get-tuple-element.52), channel_id=1, source_target_pairs={{0,12},{4,0},{8,4},{12,8},{1,13},{5,1},{9,5},{13,9},{2,14},{6,2},{... | collective-permute-start | bytes 393224 | tf_op jit(solution)/shard_map/ppermute | solution.py:22
  9.9 1.5 %collective-permute-start.8 = (bf16[1,64,1024]{2,1,0:T(8,128)(2,1)}, bf16[1,64,1024]{2,1,0:T(8,128)(2,1)S(1)}, u32[]{:S(2)}, u32[]{:S(2)}) collective-permute-start(bf16[1,64,1024]{2,1,0:T(8,128)(2,1)} %get-tuple-element.54.refs_0_), channel_id=1, source_target_pairs={{0,16},{16,0},{1,17},{17,1},{2,18},{18,2},{3,19},{19,3},{4,20},{20... | collective-permute-start | bytes 393224 | tf_op jit(solution)/shard_map/ppermute | solution.py:22
  11.4 6.2 %pack_rows.1 = (bf16[256,1024]{1,0:T(8,128)(2,1)}, bf16[256,1024]{1,0:T(8,128)(2,1)}, bf16[64,1024]{1,0:T(8,128)(2,1)}, bf16[64,1024]{1,0:T(8,128)(2,1)}, bf16[6...) custom-call(s32[32,128]{1,0:T(8,128)} %bitcast.11, ...), custom_call_target="tpu_custom_call" | custom-call | flops 1 | bytes 1 | tf_op jit(solution)/shard_map/pack_rows/pallas_call | solution.py:252
  17.9 3.3 %collective-permute-start.21 = (bf16[256,1024]{1,0:T(8,128)(2,1)}, bf16[256,1024]{1,0:T(8,128)(2,1)S(1)}, u32[]{:S(2)}, u32[]{:S(2)}) collective-permute-start(bf16[256,1024]{1,0:T(8,128)(2,1)} %after.17), channel_id=1, source_target_pairs={{0,4},{4,8},{8,12},{12,0},{1,5},{5,9},{9,13},{13,1},{2,6},{6,10},{... | collective-permute-start | bytes 1572872 | tf_op jit(solution)/shard_map/ppermute | solution.py:22
  21.2 1.5 %collective-permute-start.9 = (bf16[1,64,1024]{2,1,0:T(8,128)(2,1)S(1)}, bf16[1,64,1024]{2,1,0:T(8,128)(2,1)S(1)}, u32[]{:S(2)}, u32[]{:S(2)}) collective-permute-start(bf16[1,64,1024]{2,1,0:T(8,128)(2,1)S(1)} %collective-permute-done.4.rest_0_.refs_2_.refs_1_), channel_id=1, source_target_pairs={{0,16},{16,0},{1,17},{17,1},{2,18},{18,2},{3,19},{19,3},{4,20},{20... | collective-permute-start | bytes 393224 | tf_op jit(solution)/shard_map/ppermute | solution.py:22
  22.7 0.5 collective-permute-start.10
  23.2 1.5 %collective-permute-start.11 = (bf16[1,64,1024]{2,1,0:T(8,128)(2,1)S(1)}, bf16[1,64,1024]{2,1,0:T(8,128)(2,1)S(1)}, u32[]{:S(2)}, u32[]{:S(2)}) collective-permute-start(bf16[1,64,1024]{2,1,0:T(8,128)(2,1)S(1)} %collective-permute-done.6.rest_2_.refs_4_.refs_3_), channel_id=1, source_target_pairs={{0,16},{16,0},{1,17},{17,1},{2,18},{18,2},{3,19},{19,3},{4,20},{20... | collective-permute-start | bytes 393224 | tf_op jit(solution)/shard_map/ppermute | solution.py:22
  24.7 1.6 %collective-permute-start.25 = (bf16[128,1024]{1,0:T(8,128)(2,1)}, bf16[128,1024]{1,0:T(8,128)(2,1)S(1)}, u32[]{:S(2)}, u32[]{:S(2)}) collective-permute-start(bf16[128,1024]{1,0:T(8,128)(2,1)} %after.24), channel_id=1, source_target_pairs={{0,8},{4,12},{8,0},{12,4},{1,9},{5,13},{9,1},{13,5},{2,10},{6,14},... | collective-permute-start | bytes 786440 | tf_op jit(solution)/shard_map/ppermute | solution.py:26
  26.4 0.8 row_table.1
  27.2 3.4 %copy-done = bf16[1,4096,1024]{2,1,0:T(8,128)(2,1)S(1)} copy-done((bf16[1,4096,1024]{2,1,0:T(8,128)(2,1)S(1)}, bf16[1,4096,1024]{2,1,0:T(8,128)(2,1)}, u32[]{:S(2)}) %copy-start) | copy-done | bytes 8388632
  30.6 2.5 %fetch.1 = (bf16[2048,1024]{1,0:T(8,128)(2,1)S(1)}, bf16[2048,1024]{1,0:T(8,128)(2,1)S(1)}) custom-call(s32[1]{0:T(128)} %bitcast.3.block_ref, bf16[4096,1024]{1,0:T(8,128)(2,1)S(1)} %bitcast.7, bf16[4096,1024]{1,0:T(8,128)(2,1)} %collective-permute-done.7.refs_1_, bf16[1,64,1024]{2,1,0:T(8,128)(2,1)S(1)} %collective-permute-done.4.rest_0_.refs_2_.refs_1_, ...), custom_call_target="tpu_custom_call" | custom-call | flops 1 | bytes 1 | tf_op jit(solution)/shard_map/fetch/pallas_call | solution.py:325
  33.2 1.2 %join_queries.1 = (bf16[128,256]{1,0:T(8,128)(2,1)S(1)}, bf16[128,256]{1,0:T(8,128)(2,1)S(1)}, bf16[128,256]{1,0:T(8,128)(2,1)S(1)}, bf16[128,256]{1,0:T(8,128)(...) custom-call(s32[4,4]{1,0:T(4,128)S(1)} %copy-done.12, ...), custom_call_target="tpu_custom_call" | custom-call | flops 1 | bytes 1 | tf_op jit(solution)/shard_map/join_queries/pallas_call | solution.py:153
  34.5 0.5 collective-permute-start.13
  35.1 0.7 collective-permute-done.12.refs_10_
  35.9 0.4 collective-permute-start.16
  36.5 0.6 collective-permute-done.15.refs_13_
  37.2 0.4 collective-permute-start.19
  37.6 0.7 collective-permute-start.22
  38.5 2.3 %fetched_weights.1.refs_18_.refs_2_.refs_4_ = bf16[2048,256]{1,0:T(8,128)(2,1)S(1)} custom-call(bf16[2048,1024]{1,0:T(8,128)(2,1)S(1)} %get-tuple-element.55.refs_8_.refs_0_, bf16[2048,1024]{1,0:T(8,128)(2,1)S(1)} %get-tuple-element.56.refs_9_.refs_1_, bf16[128,256]{1,0:T(8,128)(2,1)S(1)} %get-tuple-element.58.refs_2_, ...), custom_call_target="tpu_custom_call" | custom-call | flops 1 | bytes 1 | tf_op jit(solution)/shard_map/fetched_weights/pallas_call | solution.py:352
  40.8 4.7 %collective-permute-done.25.refs_1_.refs_0_.refs_2_ = bf16[128,1024]{1,0:T(8,128)(2,1)S(1)} collective-permute-done((bf16[128,1024]{1,0:T(8,128)(2,1)}, bf16[128,1024]{1,0:T(8,128)(2,1)S(1)}, u32[]{:S(2)}, u32[]{:S(2)}) %collective-permute-start.25) | collective-permute-done | bytes 262176 | tf_op jit(solution)/shard_map/ppermute | solution.py:26
  45.5 0.8 stack.3
  46.3 1.7 %collective-permute-start.26 = (bf16[256,1024]{1,0:T(8,128)(2,1)}, bf16[256,1024]{1,0:T(8,128)(2,1)}, u32[]{:S(2)}, u32[]{:S(2)}) collective-permute-start(bf16[256,1024]{1,0:T(8,128)(2,1)} %stack.3), channel_id=1, source_target_pairs={{0,4},{4,0},{8,12},{12,8},{1,5},{5,1},{9,13},{13,9},{2,6},{6,2},{1... | collective-permute-start | bytes 1572872 | tf_op jit(solution)/shard_map/ppermute | solution.py:26
  48.0 1.5 %collective-permute-start.20 = (bf16[2048,256]{1,0:T(8,128)(2,1)S(1)}, bf16[2048,256]{1,0:T(8,128)(2,1)}, u32[]{:S(2)}, u32[]{:S(2)}) collective-permute-start(bf16[2048,256]{1,0:T(8,128)(2,1)S(1)} %fetched_weights.1.refs_18_.refs_2_.refs_4_), channel_id=1, source_target_pairs={{0,2},{2,0},{1,3},{3,1},{4,6},{6,4},{5,7},{7,5},{8,10},{10,8},{9,1... | collective-permute-start | bytes 3145736 | tf_op jit(solution)/shard_map/ppermute | solution.py:22
  49.5 3.3 %collective-permute-start.31 = (bf16[256,1024]{1,0:T(8,128)(2,1)}, bf16[256,1024]{1,0:T(8,128)(2,1)}, u32[]{:S(2)}, u32[]{:S(2)}) collective-permute-start(bf16[256,1024]{1,0:T(8,128)(2,1)} %after.28), channel_id=1, source_target_pairs={{0,8},{4,12},{8,0},{12,4},{1,9},{5,13},{9,1},{13,5},{2,10},{6,14},... | collective-permute-start | bytes 1572872 | tf_op jit(solution)/shard_map/ppermute | solution.py:22
  52.9 1.5 %collective-permute-start.24 = (s32[8,128]{1,0:T(8,128)S(1)}, s32[8,128]{1,0:T(8,128)S(1)}, u32[]{:S(2)}, u32[]{:S(2)}) collective-permute-start(s32[8,128]{1,0:T(8,128)S(1)} %get-tuple-element.57.refs_10_), channel_id=1, source_target_pairs={{0,16},{16,0},{1,17},{17,1},{2,18},{18,2},{3,19},{19,3},{4,20},{20... | collective-permute-start | bytes 12296 | tf_op jit(solution)/shard_map/ppermute | solution.py:22
  54.4 2.1 %collective-permute-done.24 = s32[8,128]{1,0:T(8,128)S(1)} collective-permute-done((s32[8,128]{1,0:T(8,128)S(1)}, s32[8,128]{1,0:T(8,128)S(1)}, u32[]{:S(2)}, u32[]{:S(2)}) %collective-permute-start.24) | collective-permute-done | bytes 4128 | tf_op jit(solution)/shard_map/ppermute | solution.py:22
  56.5 0.5 slice.3
  57.6 6.6 %partial_weights.1.rest_0_.refs_1_.refs_2_.refs_0_ = f32[2048,256]{1,0:T(8,128)S(1)} custom-call(s32[1]{0:T(128)} %bitcast.1.block_ref, bf16[4096,1024]{1,0:T(8,128)(2,1)S(1)} %bitcast.10, bf16[4096,1024]{1,0:T(8,128)(2,1)} %collective-permute-done.7.refs_1_, bf16[128,256]{1,0:T(8,128)(2,1)S(1)} %get-tuple-element.58.refs_2_, ...), custom_call_target="tpu_custom_call" | custom-call | flops 1 | bytes 1 | tf_op jit(solution)/shard_map/partial_weights/pallas_call | solution.py:292
  64.6 0.5 collective-permute-start.28
  65.1 1.2 %collective-permute-done.27.refs_0_ = bf16[128,1024]{1,0:T(8,128)(2,1)S(1)} collective-permute-done((bf16[128,1024]{1,0:T(8,128)(2,1)}, bf16[128,1024]{1,0:T(8,128)(2,1)S(1)}, u32[]{:S(2)}, u32[]{:S(2)}) %collective-permute-start.27) | collective-permute-done | bytes 262176 | tf_op jit(solution)/shard_map/ppermute | solution.py:22
  66.8 2.4 %own_rows.1.refs_2_ = bf16[256,2048]{1,0:T(8,128)(2,1)S(1)} custom-call(s32[8,128]{1,0:T(8,128)S(1)} %copy-done.13, bf16[1024,2048]{1,0:T(8,128)(2,1)S(1)} %copy-done.1, f32[2048,256]{1,0:T(8,128)S(1)} %partial_weights.1.rest_0_.refs_1_.refs_2_.refs_0_), custom_call_target="tpu_custom_call" | custom-call | flops 1 | bytes 1 | tf_op jit(solution)/shard_map/own_rows/pallas_call | solution.py:194
  69.2 0.9 copy-done.6
  70.7 1.4 %collective-permute-done.29.refs_1_ = s32[8,128]{1,0:T(8,128)S(1)} collective-permute-done((s32[8,128]{1,0:T(8,128)S(1)}, s32[8,128]{1,0:T(8,128)S(1)}, u32[]{:S(2)}, u32[]{:S(2)}) %collective-permute-start.29) | collective-permute-done | bytes 4128 | tf_op jit(solution)/shard_map/ppermute | solution.py:22
  72.3 3.2 %collective-permute-done.31.refs_0_ = bf16[256,1024]{1,0:T(8,128)(2,1)} collective-permute-done((bf16[256,1024]{1,0:T(8,128)(2,1)}, bf16[256,1024]{1,0:T(8,128)(2,1)}, u32[]{:S(2)}, u32[]{:S(2)}) %collective-permute-start.31) | collective-permute-done | bytes 524320 | tf_op jit(solution)/shard_map/ppermute | solution.py:22
  75.5 2.4 %collective-permute-start.35 = (bf16[64,1024]{1,0:T(8,128)(2,1)S(1)}, bf16[64,1024]{1,0:T(8,128)(2,1)S(1)}, u32[]{:S(2)}, u32[]{:S(2)}) collective-permute-start(bf16[64,1024]{1,0:T(8,128)(2,1)S(1)} %after.18.refs_3_), channel_id=1, source_target_pairs={{0,12},{4,0},{8,4},{12,8},{1,13},{5,1},{9,5},{13,9},{2,14},{6,2},{... | collective-permute-start | bytes 393224 | tf_op jit(solution)/shard_map/ppermute | solution.py:22
  78.1 5.1 %early_scores.1 = (bf16[2048,256]{1,0:T(8,128)(2,1)S(1)}, bf16[2048,256]{1,0:T(8,128)(2,1)S(1)}, f32[1024,128]{1,0:T(8,128)S(1)}, bf16[1024,128]{1,0:T(8,128)(2,1)S(1)}) custom-call(s32[4,4]{1,0:T(4,128)S(1)} %get-tuple-element.53.table_ref, f32[2048,256]{1,0:T(8,128)S(1)} %partial_weights.1.rest_0_.refs_1_.refs_2_.refs_0_, ...), custom_call_target="tpu_custom_call" | custom-call | flops 1 | bytes 1 | tf_op jit(solution)/shard_map/early_scores/pallas_call | solution.py:509
  83.2 1.0 %collective-permute-start.34 = (bf16[1024,128]{1,0:T(8,128)(2,1)S(1)}, bf16[1024,128]{1,0:T(8,128)(2,1)S(1)}, u32[]{:S(2)}, u32[]{:S(2)}) collective-permute-start(bf16[1024,128]{1,0:T(8,128)(2,1)S(1)} %get-tuple-element.89.refs_1_), channel_id=1, source_target_pairs={{0,2},{2,0},{1,3},{3,1},{4,6},{6,4},{5,7},{7,5},{8,10},{10,8},{9,1... | collective-permute-start | bytes 786440 | tf_op jit(solution)/shard_map/ppermute | solution.py:22
  84.2 0.5 collective-permute-done.37.refs_0_
  84.7 2.4 %collective-permute-done.39.refs_0_ = bf16[64,1024]{1,0:T(8,128)(2,1)S(1)} collective-permute-done((bf16[64,1024]{1,0:T(8,128)(2,1)S(1)}, bf16[64,1024]{1,0:T(8,128)(2,1)S(1)}, u32[]{:S(2)}, u32[]{:S(2)}) %collective-permute-start.39) | collective-permute-done | bytes 131104 | tf_op jit(solution)/shard_map/ppermute | solution.py:22
  87.1 1.3 %collective-permute-done.40.refs_7_ = bf16[64,1024]{1,0:T(8,128)(2,1)S(1)} collective-permute-done((bf16[64,1024]{1,0:T(8,128)(2,1)S(1)}, bf16[64,1024]{1,0:T(8,128)(2,1)S(1)}, u32[]{:S(2)}, u32[]{:S(2)}) %collective-permute-start.40) | collective-permute-done | bytes 131104 | tf_op jit(solution)/shard_map/ppermute | solution.py:22
  88.4 0.7 late_scores.1
  89.2 0.6 collective-permute-start.41
  89.8 3.7 %collective-permute-done.41.refs_3_ = bf16[256,128]{1,0:T(8,128)(2,1)S(1)} collective-permute-done((bf16[256,128]{1,0:T(8,128)(2,1)S(1)}, bf16[256,128]{1,0:T(8,128)(2,1)S(1)}, u32[]{:S(2)}, u32[]{:S(2)}) %collective-permute-start.41) | collective-permute-done | bytes 65568 | tf_op jit(solution)/shard_map/ppermute | solution.py:22
  93.5 1.7 %merge.1 = f32[128,1024]{1,0:T(8,128)} custom-call(s32[4,4]{1,0:T(4,128)S(1)} %get-tuple-element.53.table_ref, f32[1024,128]{1,0:T(8,128)S(1)} %get-tuple-element.88.refs_0_, bf16[1024,128]{1,0:T(8,128)(2,1)S(1)} %collective-permute-done.34.refs_1_, f32[256,128]{1,0:T(8,128)S(1)} %get-tuple-element.92.refs_2_, ...), custom_call_target="tpu_custom_call" | custom-call | flops 1 | bytes 1 | tf_op jit(solution)/shard_map/merge/pallas_call | solution.py:571
  (101 shorter events, 2.9 us)
Async XLA Ops:
  0.0 26.4 %copy-start.11 = (s32[4096]{0:T(1024)S(1)}, s32[4096]{0:T(1024)}, u32[]{:S(2)}) copy-start(s32[4096]{0:T(1024)} %param.9) | copy-start | bytes 49156
  0.0 24.7 %collective-permute-start.7 = (bf16[4096,1024]{1,0:T(8,128)(2,1)}, bf16[4096,1024]{1,0:T(8,128)(2,1)}, u32[]{:S(2)}, u32[]{:S(2)}) collective-permute-start(bf16[4096,1024]{1,0:T(8,128)(2,1)} %bitcast.6), channel_id=1, source_target_pairs={{0,1},{1,0},{2,3},{3,2},{4,5},{5,4},{6,7},{7,6},{8,9},{9,8},{10,11... | collective-permute-start | bytes 25165832 | tf_op jit(solution)/shard_map/ppermute | solution.py:22
  3.2 14.5 %collective-permute-start.4 = (bf16[1,64,1024]{2,1,0:T(8,128)(2,1)}, bf16[1,64,1024]{2,1,0:T(8,128)(2,1)S(1)}, u32[]{:S(2)}, u32[]{:S(2)}) collective-permute-start(bf16[1,64,1024]{2,1,0:T(8,128)(2,1)} %get-tuple-element.50), channel_id=1, source_target_pairs={{0,4},{4,8},{8,12},{12,0},{1,5},{5,9},{9,13},{13,1},{2,6},{6,10},{... | collective-permute-start | bytes 393224 | tf_op jit(solution)/shard_map/ppermute | solution.py:22
  5.9 12.0 %collective-permute-start.5 = (bf16[1,64,1024]{2,1,0:T(8,128)(2,1)}, bf16[1,64,1024]{2,1,0:T(8,128)(2,1)S(1)}, u32[]{:S(2)}, u32[]{:S(2)}) collective-permute-start(bf16[1,64,1024]{2,1,0:T(8,128)(2,1)} %get-tuple-element.51), channel_id=1, source_target_pairs={{0,8},{4,12},{8,0},{12,4},{1,9},{5,13},{9,1},{13,5},{2,10},{6,14},... | collective-permute-start | bytes 393224 | tf_op jit(solution)/shard_map/ppermute | solution.py:22
  8.5 9.4 %collective-permute-start.6 = (bf16[1,64,1024]{2,1,0:T(8,128)(2,1)}, bf16[1,64,1024]{2,1,0:T(8,128)(2,1)S(1)}, u32[]{:S(2)}, u32[]{:S(2)}) collective-permute-start(bf16[1,64,1024]{2,1,0:T(8,128)(2,1)} %get-tuple-element.52), channel_id=1, source_target_pairs={{0,12},{4,0},{8,4},{12,8},{1,13},{5,1},{9,5},{13,9},{2,14},{6,2},{... | collective-permute-start | bytes 393224 | tf_op jit(solution)/shard_map/ppermute | solution.py:22
  9.9 13.3 %collective-permute-start.8 = (bf16[1,64,1024]{2,1,0:T(8,128)(2,1)}, bf16[1,64,1024]{2,1,0:T(8,128)(2,1)S(1)}, u32[]{:S(2)}, u32[]{:S(2)}) collective-permute-start(bf16[1,64,1024]{2,1,0:T(8,128)(2,1)} %get-tuple-element.54.refs_0_), channel_id=1, source_target_pairs={{0,16},{16,0},{1,17},{17,1},{2,18},{18,2},{3,19},{19,3},{4,20},{20... | collective-permute-start | bytes 393224 | tf_op jit(solution)/shard_map/ppermute | solution.py:22
  17.9 31.6 %collective-permute-start.21 = (bf16[256,1024]{1,0:T(8,128)(2,1)}, bf16[256,1024]{1,0:T(8,128)(2,1)S(1)}, u32[]{:S(2)}, u32[]{:S(2)}) collective-permute-start(bf16[256,1024]{1,0:T(8,128)(2,1)} %after.17), channel_id=1, source_target_pairs={{0,4},{4,8},{8,12},{12,0},{1,5},{5,9},{9,13},{13,1},{2,6},{6,10},{... | collective-permute-start | bytes 1572872 | tf_op jit(solution)/shard_map/ppermute | solution.py:22
  21.2 12.0 %collective-permute-start.9 = (bf16[1,64,1024]{2,1,0:T(8,128)(2,1)S(1)}, bf16[1,64,1024]{2,1,0:T(8,128)(2,1)S(1)}, u32[]{:S(2)}, u32[]{:S(2)}) collective-permute-start(bf16[1,64,1024]{2,1,0:T(8,128)(2,1)S(1)} %collective-permute-done.4.rest_0_.refs_2_.refs_1_), channel_id=1, source_target_pairs={{0,16},{16,0},{1,17},{17,1},{2,18},{18,2},{3,19},{19,3},{4,20},{20... | collective-permute-start | bytes 393224 | tf_op jit(solution)/shard_map/ppermute | solution.py:22
  22.7 10.4 %collective-permute-start.10 = (bf16[1,64,1024]{2,1,0:T(8,128)(2,1)S(1)}, bf16[1,64,1024]{2,1,0:T(8,128)(2,1)S(1)}, u32[]{:S(2)}, u32[]{:S(2)}) collective-permute-start(bf16[1,64,1024]{2,1,0:T(8,128)(2,1)S(1)} %collective-permute-done.5.rest_1_.refs_3_.refs_2_), channel_id=1, source_target_pairs={{0,16},{16,0},{1,17},{17,1},{2,18},{18,2},{3,19},{19,3},{4,20},{20... | collective-permute-start | bytes 393224 | tf_op jit(solution)/shard_map/ppermute | solution.py:22
  23.2 9.9 %collective-permute-start.11 = (bf16[1,64,1024]{2,1,0:T(8,128)(2,1)S(1)}, bf16[1,64,1024]{2,1,0:T(8,128)(2,1)S(1)}, u32[]{:S(2)}, u32[]{:S(2)}) collective-permute-start(bf16[1,64,1024]{2,1,0:T(8,128)(2,1)S(1)} %collective-permute-done.6.rest_2_.refs_4_.refs_3_), channel_id=1, source_target_pairs={{0,16},{16,0},{1,17},{17,1},{2,18},{18,2},{3,19},{19,3},{4,20},{20... | collective-permute-start | bytes 393224 | tf_op jit(solution)/shard_map/ppermute | solution.py:22
  24.7 20.7 %collective-permute-start.25 = (bf16[128,1024]{1,0:T(8,128)(2,1)}, bf16[128,1024]{1,0:T(8,128)(2,1)S(1)}, u32[]{:S(2)}, u32[]{:S(2)}) collective-permute-start(bf16[128,1024]{1,0:T(8,128)(2,1)} %after.24), channel_id=1, source_target_pairs={{0,8},{4,12},{8,0},{12,4},{1,9},{5,13},{9,1},{13,5},{2,10},{6,14},... | collective-permute-start | bytes 786440 | tf_op jit(solution)/shard_map/ppermute | solution.py:26
  27.2 3.4 %copy-start = (bf16[1,4096,1024]{2,1,0:T(8,128)(2,1)S(1)}, bf16[1,4096,1024]{2,1,0:T(8,128)(2,1)}, u32[]{:S(2)}) copy-start(bf16[1,4096,1024]{2,1,0:T(8,128)(2,1)} %param.10) | copy-start | bytes 25165828
  30.6 2.6 %copy-start.14 = (s32[16]{0:T(128)S(1)}, s32[16]{0:T(128)}, u32[]{:S(2)}) copy-start(s32[16]{0:T(128)} %slot_ref.3) | copy-start | bytes 196
  33.2 4.3 %copy-start.10 = (bf16[64,1024]{1,0:T(8,128)(2,1)S(1)}, bf16[64,1024]{1,0:T(8,128)(2,1)}, u32[]{:S(2)}) copy-start(bf16[64,1024]{1,0:T(8,128)(2,1)} %get-tuple-element.79.refs_0_) | copy-start | bytes 393220
  34.5 1.3 %collective-permute-start.12 = (bf16[128,256]{1,0:T(8,128)(2,1)S(1)}, bf16[128,256]{1,0:T(8,128)(2,1)S(1)}, u32[]{:S(2)}, u32[]{:S(2)}) collective-permute-start(bf16[128,256]{1,0:T(8,128)(2,1)S(1)} %get-tuple-element.66), channel_id=1, source_target_pairs={{0,1},{1,0},{2,3},{3,2},{4,5},{5,4},{6,7},{7,6},{8,9},{9,8},{10,11... | collective-permute-start | bytes 196616 | tf_op jit(solution)/shard_map/ppermute | solution.py:22
  34.5 1.4 %collective-permute-start.13 = (bf16[128,256]{1,0:T(8,128)(2,1)S(1)}, bf16[128,256]{1,0:T(8,128)(2,1)S(1)}, u32[]{:S(2)}, u32[]{:S(2)}) collective-permute-start(bf16[128,256]{1,0:T(8,128)(2,1)S(1)} %get-tuple-element.67), channel_id=1, source_target_pairs={{0,1},{1,0},{2,3},{3,2},{4,5},{5,4},{6,7},{7,6},{8,9},{9,8},{10,11... | collective-permute-start | bytes 196616 | tf_op jit(solution)/shard_map/ppermute | solution.py:22
  35.0 1.3 %collective-permute-start.14 = (bf16[128,256]{1,0:T(8,128)(2,1)S(1)}, bf16[128,256]{1,0:T(8,128)(2,1)S(1)}, u32[]{:S(2)}, u32[]{:S(2)}) collective-permute-start(bf16[128,256]{1,0:T(8,128)(2,1)S(1)} %get-tuple-element.68), channel_id=1, source_target_pairs={{0,1},{1,0},{2,3},{3,2},{4,5},{5,4},{6,7},{7,6},{8,9},{9,8},{10,11... | collective-permute-start | bytes 196616 | tf_op jit(solution)/shard_map/ppermute | solution.py:22
  35.8 1.3 %collective-permute-start.15 = (bf16[128,256]{1,0:T(8,128)(2,1)S(1)}, bf16[128,256]{1,0:T(8,128)(2,1)S(1)}, u32[]{:S(2)}, u32[]{:S(2)}) collective-permute-start(bf16[128,256]{1,0:T(8,128)(2,1)S(1)} %get-tuple-element.69), channel_id=1, source_target_pairs={{0,1},{1,0},{2,3},{3,2},{4,5},{5,4},{6,7},{7,6},{8,9},{9,8},{10,11... | collective-permute-start | bytes 196616 | tf_op jit(solution)/shard_map/ppermute | solution.py:22
  35.9 1.3 %collective-permute-start.16 = (bf16[128,256]{1,0:T(8,128)(2,1)S(1)}, bf16[128,256]{1,0:T(8,128)(2,1)S(1)}, u32[]{:S(2)}, u32[]{:S(2)}) collective-permute-start(bf16[128,256]{1,0:T(8,128)(2,1)S(1)} %get-tuple-element.70), channel_id=1, source_target_pairs={{0,1},{1,0},{2,3},{3,2},{4,5},{5,4},{6,7},{7,6},{8,9},{9,8},{10,11... | collective-permute-start | bytes 196616 | tf_op jit(solution)/shard_map/ppermute | solution.py:22
  36.3 1.3 %collective-permute-start.17 = (bf16[128,256]{1,0:T(8,128)(2,1)S(1)}, bf16[128,256]{1,0:T(8,128)(2,1)S(1)}, u32[]{:S(2)}, u32[]{:S(2)}) collective-permute-start(bf16[128,256]{1,0:T(8,128)(2,1)S(1)} %get-tuple-element.71), channel_id=1, source_target_pairs={{0,1},{1,0},{2,3},{3,2},{4,5},{5,4},{6,7},{7,6},{8,9},{9,8},{10,11... | collective-permute-start | bytes 196616 | tf_op jit(solution)/shard_map/ppermute | solution.py:22
  37.0 1.3 %collective-permute-start.18 = (bf16[128,256]{1,0:T(8,128)(2,1)S(1)}, bf16[128,256]{1,0:T(8,128)(2,1)S(1)}, u32[]{:S(2)}, u32[]{:S(2)}) collective-permute-start(bf16[128,256]{1,0:T(8,128)(2,1)S(1)} %get-tuple-element.72), channel_id=1, source_target_pairs={{0,1},{1,0},{2,3},{3,2},{4,5},{5,4},{6,7},{7,6},{8,9},{9,8},{10,11... | collective-permute-start | bytes 196616 | tf_op jit(solution)/shard_map/ppermute | solution.py:22
  37.2 1.3 %collective-permute-start.19 = (bf16[128,256]{1,0:T(8,128)(2,1)S(1)}, bf16[128,256]{1,0:T(8,128)(2,1)S(1)}, u32[]{:S(2)}, u32[]{:S(2)}) collective-permute-start(bf16[128,256]{1,0:T(8,128)(2,1)S(1)} %get-tuple-element.73), channel_id=1, source_target_pairs={{0,1},{1,0},{2,3},{3,2},{4,5},{5,4},{6,7},{7,6},{8,9},{9,8},{10,11... | collective-permute-start | bytes 196616 | tf_op jit(solution)/shard_map/ppermute | solution.py:22
  37.6 12.0 %collective-permute-start.22 = (bf16[64,1024]{1,0:T(8,128)(2,1)S(1)}, bf16[64,1024]{1,0:T(8,128)(2,1)S(1)}, u32[]{:S(2)}, u32[]{:S(2)}) collective-permute-start(bf16[64,1024]{1,0:T(8,128)(2,1)S(1)} %after.21), channel_id=1, source_target_pairs={{0,12},{4,0},{8,4},{12,8},{1,13},{5,1},{9,5},{13,9},{2,14},{6,2},{... | collective-permute-start | bytes 393224 | tf_op jit(solution)/shard_map/ppermute | solution.py:22
  38.4 19.2 %slice-start = ((s8[8388608]{0:T(1024)(128)(4,1)}), s8[4194304]{0:T(1024)(128)(4,1)S(1)}, s32[]{:S(2)}) async-start(s8[8388608]{0:T(1024)(128)(4,1)} %bitcast.8), calls=%async_computation | async-start | bytes 8388608
  38.5 7.0 %copy-start.4 = (bf16[128,1024]{1,0:T(8,128)(2,1)S(1)}, bf16[128,1024]{1,0:T(8,128)(2,1)}, u32[]{:S(2)}) copy-start(bf16[128,1024]{1,0:T(8,128)(2,1)} %get-tuple-element.82.refs_0_) | copy-start | bytes 786436
  38.5 19.2 %slice-start.1 = ((s8[8388608]{0:T(1024)(128)(4,1)}), s8[4194304]{0:T(1024)(128)(4,1)S(1)}, s32[]{:S(2)}) async-start(s8[8388608]{0:T(1024)(128)(4,1)} %bitcast.8), calls=%async_computation.1 | async-start | bytes 8388608
  46.3 23.8 %collective-permute-start.26 = (bf16[256,1024]{1,0:T(8,128)(2,1)}, bf16[256,1024]{1,0:T(8,128)(2,1)}, u32[]{:S(2)}, u32[]{:S(2)}) collective-permute-start(bf16[256,1024]{1,0:T(8,128)(2,1)} %stack.3), channel_id=1, source_target_pairs={{0,4},{4,0},{8,12},{12,8},{1,5},{5,1},{9,13},{13,9},{2,6},{6,2},{1... | collective-permute-start | bytes 1572872 | tf_op jit(solution)/shard_map/ppermute | solution.py:26
  48.0 29.8 %collective-permute-start.20 = (bf16[2048,256]{1,0:T(8,128)(2,1)S(1)}, bf16[2048,256]{1,0:T(8,128)(2,1)}, u32[]{:S(2)}, u32[]{:S(2)}) collective-permute-start(bf16[2048,256]{1,0:T(8,128)(2,1)S(1)} %fetched_weights.1.refs_18_.refs_2_.refs_4_), channel_id=1, source_target_pairs={{0,2},{2,0},{1,3},{3,1},{4,6},{6,4},{5,7},{7,5},{8,10},{10,8},{9,1... | collective-permute-start | bytes 3145736 | tf_op jit(solution)/shard_map/ppermute | solution.py:22
  49.5 8.1 %copy-start.2 = (bf16[256,1024]{1,0:T(8,128)(2,1)}, bf16[256,1024]{1,0:T(8,128)(2,1)S(1)}, u32[]{:S(2)}) copy-start(bf16[256,1024]{1,0:T(8,128)(2,1)S(1)} %collective-permute-done.21.refs_0_.refs_1_) | copy-start | bytes 1572868
  49.5 26.0 %collective-permute-start.31 = (bf16[256,1024]{1,0:T(8,128)(2,1)}, bf16[256,1024]{1,0:T(8,128)(2,1)}, u32[]{:S(2)}, u32[]{:S(2)}) collective-permute-start(bf16[256,1024]{1,0:T(8,128)(2,1)} %after.28), channel_id=1, source_target_pairs={{0,8},{4,12},{8,0},{12,4},{1,9},{5,13},{9,1},{13,5},{2,10},{6,14},... | collective-permute-start | bytes 1572872 | tf_op jit(solution)/shard_map/ppermute | solution.py:22
  52.9 3.6 %collective-permute-start.24 = (s32[8,128]{1,0:T(8,128)S(1)}, s32[8,128]{1,0:T(8,128)S(1)}, u32[]{:S(2)}, u32[]{:S(2)}) collective-permute-start(s32[8,128]{1,0:T(8,128)S(1)} %get-tuple-element.57.refs_10_), channel_id=1, source_target_pairs={{0,16},{16,0},{1,17},{17,1},{2,18},{18,2},{3,19},{19,3},{4,20},{20... | collective-permute-start | bytes 12296 | tf_op jit(solution)/shard_map/ppermute | solution.py:22
  57.6 6.6 %copy-start.15 = (bf16[128,1024]{1,0:T(8,128)(2,1)S(1)}, bf16[128,1024]{1,0:T(8,128)(2,1)}, u32[]{:S(2)}) copy-start(bf16[128,1024]{1,0:T(8,128)(2,1)} %get-tuple-element.80.refs_0_) | copy-start | bytes 786436
  64.5 1.8 %collective-permute-start.27 = (bf16[128,1024]{1,0:T(8,128)(2,1)}, bf16[128,1024]{1,0:T(8,128)(2,1)S(1)}, u32[]{:S(2)}, u32[]{:S(2)}) collective-permute-start(bf16[128,1024]{1,0:T(8,128)(2,1)} %get-tuple-element.82.refs_0_), channel_id=1, source_target_pairs={{0,1},{1,0},{2,3},{3,2},{4,5},{5,4},{6,7},{7,6},{8,9},{9,8},{10,11... | collective-permute-start | bytes 786440 | tf_op jit(solution)/shard_map/ppermute | solution.py:22
  64.6 5.4 %collective-permute-start.28 = (bf16[128,1024]{1,0:T(8,128)(2,1)S(1)}, bf16[128,1024]{1,0:T(8,128)(2,1)S(1)}, u32[]{:S(2)}, u32[]{:S(2)}) collective-permute-start(bf16[128,1024]{1,0:T(8,128)(2,1)S(1)} %after.25.refs_1_), channel_id=1, source_target_pairs={{0,1},{1,0},{2,3},{3,2},{4,5},{5,4},{6,7},{7,6},{8,9},{9,8},{10,11... | collective-permute-start | bytes 786440 | tf_op jit(solution)/shard_map/ppermute | solution.py:22
  66.3 3.7 %collective-permute-start.23 = (bf16[64,1024]{1,0:T(8,128)(2,1)S(1)}, bf16[64,1024]{1,0:T(8,128)(2,1)S(1)}, u32[]{:S(2)}, u32[]{:S(2)}) collective-permute-start(bf16[64,1024]{1,0:T(8,128)(2,1)S(1)} %after.22.refs_0_), channel_id=1, source_target_pairs={{0,1},{1,0},{2,3},{3,2},{4,5},{5,4},{6,7},{7,6},{8,9},{9,8},{10,11... | collective-permute-start | bytes 393224 | tf_op jit(solution)/shard_map/ppermute | solution.py:22
  66.5 2.6 %copy-start.8 = (bf16[64,1024]{1,0:T(8,128)(2,1)S(1)}, bf16[64,1024]{1,0:T(8,128)(2,1)}, u32[]{:S(2)}) copy-start(bf16[64,1024]{1,0:T(8,128)(2,1)} %get-tuple-element.76.refs_0_) | copy-start | bytes 393220
  70.1 7.8 %collective-permute-start.33 = (bf16[256,1024]{1,0:T(8,128)(2,1)}, bf16[256,1024]{1,0:T(8,128)(2,1)S(1)}, u32[]{:S(2)}, u32[]{:S(2)}) collective-permute-start(bf16[256,1024]{1,0:T(8,128)(2,1)} %after.30.refs_9_), channel_id=1, source_target_pairs={{0,1},{1,0},{2,3},{3,2},{4,5},{5,4},{6,7},{7,6},{8,9},{9,8},{10,11... | collective-permute-start | bytes 1572872 | tf_op jit(solution)/shard_map/ppermute | solution.py:22
  70.4 1.7 %collective-permute-start.29 = (s32[8,128]{1,0:T(8,128)S(1)}, s32[8,128]{1,0:T(8,128)S(1)}, u32[]{:S(2)}, u32[]{:S(2)}) collective-permute-start(s32[8,128]{1,0:T(8,128)S(1)} %after.26), channel_id=1, source_target_pairs={{0,1},{1,0},{2,3},{3,2},{4,5},{5,4},{6,7},{7,6},{8,9},{9,8},{10,11... | collective-permute-start | bytes 12296 | tf_op jit(solution)/shard_map/ppermute | solution.py:22
  72.1 5.9 %collective-permute-start.30 = (bf16[256,1024]{1,0:T(8,128)(2,1)S(1)}, bf16[256,1024]{1,0:T(8,128)(2,1)S(1)}, u32[]{:S(2)}, u32[]{:S(2)}) collective-permute-start(bf16[256,1024]{1,0:T(8,128)(2,1)S(1)} %after.27.refs_3_), channel_id=1, source_target_pairs={{0,1},{1,0},{2,3},{3,2},{4,5},{5,4},{6,7},{7,6},{8,9},{9,8},{10,11... | collective-permute-start | bytes 1572872 | tf_op jit(solution)/shard_map/ppermute | solution.py:22
  75.5 2.5 %collective-permute-start.32 = (bf16[256,1024]{1,0:T(8,128)(2,1)}, bf16[256,1024]{1,0:T(8,128)(2,1)S(1)}, u32[]{:S(2)}, u32[]{:S(2)}) collective-permute-start(bf16[256,1024]{1,0:T(8,128)(2,1)} %after.29.refs_5_), channel_id=1, source_target_pairs={{0,1},{1,0},{2,3},{3,2},{4,5},{5,4},{6,7},{7,6},{8,9},{9,8},{10,11... | collective-permute-start | bytes 1572872 | tf_op jit(solution)/shard_map/ppermute | solution.py:22
  75.5 8.6 %collective-permute-start.35 = (bf16[64,1024]{1,0:T(8,128)(2,1)S(1)}, bf16[64,1024]{1,0:T(8,128)(2,1)S(1)}, u32[]{:S(2)}, u32[]{:S(2)}) collective-permute-start(bf16[64,1024]{1,0:T(8,128)(2,1)S(1)} %after.18.refs_3_), channel_id=1, source_target_pairs={{0,12},{4,0},{8,4},{12,8},{1,13},{5,1},{9,5},{13,9},{2,14},{6,2},{... | collective-permute-start | bytes 393224 | tf_op jit(solution)/shard_map/ppermute | solution.py:22
  77.9 6.7 %collective-permute-start.37 = (bf16[64,1024]{1,0:T(8,128)(2,1)S(1)}, bf16[64,1024]{1,0:T(8,128)(2,1)S(1)}, u32[]{:S(2)}, u32[]{:S(2)}) collective-permute-start(bf16[64,1024]{1,0:T(8,128)(2,1)S(1)} %after.19.refs_4_), channel_id=1, source_target_pairs={{0,12},{4,0},{8,4},{12,8},{1,13},{5,1},{9,5},{13,9},{2,14},{6,2},{... | collective-permute-start | bytes 393224 | tf_op jit(solution)/shard_map/ppermute | solution.py:22
  77.9 9.1 %collective-permute-start.39 = (bf16[64,1024]{1,0:T(8,128)(2,1)S(1)}, bf16[64,1024]{1,0:T(8,128)(2,1)S(1)}, u32[]{:S(2)}, u32[]{:S(2)}) collective-permute-start(bf16[64,1024]{1,0:T(8,128)(2,1)S(1)} %after.20.refs_5_), channel_id=1, source_target_pairs={{0,12},{4,0},{8,4},{12,8},{1,13},{5,1},{9,5},{13,9},{2,14},{6,2},{... | collective-permute-start | bytes 393224 | tf_op jit(solution)/shard_map/ppermute | solution.py:22
  83.2 10.3 %collective-permute-start.34 = (bf16[1024,128]{1,0:T(8,128)(2,1)S(1)}, bf16[1024,128]{1,0:T(8,128)(2,1)S(1)}, u32[]{:S(2)}, u32[]{:S(2)}) collective-permute-start(bf16[1024,128]{1,0:T(8,128)(2,1)S(1)} %get-tuple-element.89.refs_1_), channel_id=1, source_target_pairs={{0,2},{2,0},{1,3},{3,1},{4,6},{6,4},{5,7},{7,5},{8,10},{10,8},{9,1... | collective-permute-start | bytes 786440 | tf_op jit(solution)/shard_map/ppermute | solution.py:22
  84.2 2.9 %collective-permute-start.36 = (bf16[64,1024]{1,0:T(8,128)(2,1)S(1)}, bf16[64,1024]{1,0:T(8,128)(2,1)S(1)}, u32[]{:S(2)}, u32[]{:S(2)}) collective-permute-start(bf16[64,1024]{1,0:T(8,128)(2,1)S(1)} %after.31.refs_2_), channel_id=1, source_target_pairs={{0,1},{1,0},{2,3},{3,2},{4,5},{5,4},{6,7},{7,6},{8,9},{9,8},{10,11... | collective-permute-start | bytes 393224 | tf_op jit(solution)/shard_map/ppermute | solution.py:22
  84.6 2.4 %collective-permute-start.38 = (bf16[64,1024]{1,0:T(8,128)(2,1)S(1)}, bf16[64,1024]{1,0:T(8,128)(2,1)S(1)}, u32[]{:S(2)}, u32[]{:S(2)}) collective-permute-start(bf16[64,1024]{1,0:T(8,128)(2,1)S(1)} %after.32.refs_4_), channel_id=1, source_target_pairs={{0,1},{1,0},{2,3},{3,2},{4,5},{5,4},{6,7},{7,6},{8,9},{9,8},{10,11... | collective-permute-start | bytes 393224 | tf_op jit(solution)/shard_map/ppermute | solution.py:22
  87.0 1.3 %collective-permute-start.40 = (bf16[64,1024]{1,0:T(8,128)(2,1)S(1)}, bf16[64,1024]{1,0:T(8,128)(2,1)S(1)}, u32[]{:S(2)}, u32[]{:S(2)}) collective-permute-start(bf16[64,1024]{1,0:T(8,128)(2,1)S(1)} %after.33.refs_6_), channel_id=1, source_target_pairs={{0,1},{1,0},{2,3},{3,2},{4,5},{5,4},{6,7},{7,6},{8,9},{9,8},{10,11... | collective-permute-start | bytes 393224 | tf_op jit(solution)/shard_map/ppermute | solution.py:22
  89.2 4.3 %collective-permute-start.41 = (bf16[256,128]{1,0:T(8,128)(2,1)S(1)}, bf16[256,128]{1,0:T(8,128)(2,1)S(1)}, u32[]{:S(2)}, u32[]{:S(2)}) collective-permute-start(bf16[256,128]{1,0:T(8,128)(2,1)S(1)} %get-tuple-element.93), channel_id=1, source_target_pairs={{0,2},{2,0},{1,3},{3,1},{4,6},{6,4},{5,7},{7,5},{8,10},{10,8},{9,1... | collective-permute-start | bytes 196616 | tf_op jit(solution)/shard_map/ppermute | solution.py:22
  (8 other events, 16.7 us)

commit v16 on v15

--- a/solution.py
+++ b/solution.py
@@ -420,14 +420,16 @@
     acc[pl.ds(first, tiles + 1)] = pieces
 
 
-def score(high_ref, low_ref, parts, rep):
+def score(weight_ref, parts, rep):
     total = None
     for d, x in enumerate(parts):
         depth = x.shape[1]
         block = pl.ds(pl.multiple_of(lax.rem(rep + (len(parts) - d), jnp.int32(len(parts))) * depth, depth), depth)
-        value = dot(x, high_ref[block, :]) + dot(x, low_ref[block, :])
+        value = dot(x, weight_ref[block, :])
         total = value if total is None else total + value
-    return total.reshape(total.shape[0] // 8, 8, total.shape[1])
+    width = total.shape[1] // 2
+    total = total[:, :width] + total[:, width:]
+    return total.reshape(total.shape[0] // 8, 8, width)
 
 
 def for_feats(value, outs):
@@ -460,19 +462,19 @@
         piece_refs = [refs[j * n_rep:(j + 1) * n_rep] for j in range(n_piece)]
         refs = refs[n_piece * n_rep:]
         first_refs, second_refs, refs = refs[:n_first], refs[n_first:2 * n_first], refs[2 * n_first:]
-        high_ref, low_ref, outs, (scored, held, acc, sem) = refs[0], refs[1], refs[2:-4], refs[-4:]
+        weight_ref, outs, (scored, held, acc, sem) = refs[0], refs[1:-4], refs[-4:]
         me, rep = lax.axis_index("shard"), lax.axis_index("rep")
         weight = own_ref[...]
         for ref in other_refs:
             weight = weight + ref[...].astype(F32)
         high = weight.astype(BF16)
-        high_ref[...] = high
-        low_ref[...] = (weight - high.astype(F32)).astype(BF16)
-
-        scored[me] = score(high_ref, low_ref, [mine_ref[...]], jnp.int32(0))
+        weight_ref[:, :width] = high
+        weight_ref[:, width:] = (weight - high.astype(F32)).astype(BF16)
+
+        scored[me] = score(weight_ref, [mine_ref[...]], jnp.int32(0))
         for parts, (hops, first, size) in zip(piece_refs, cuts):
             source = lax.rem(me + (n_shard - hops), jnp.int32(n_shard))
-            scored[source, first // 8:(first + size) // 8] = score(high_ref, low_ref, [p[...] for p in parts], rep)
+            scored[source, first // 8:(first + size) // 8] = score(weight_ref, [p[...] for p in parts], rep)
         last = lax.rem(me + (n_shard - last_hops), jnp.int32(n_shard))
         for s in range(n_shard):
             start = table_ref[s, 0]
@@ -501,7 +503,7 @@
                                 copy.wait()
                     some = pl.ds(pl.multiple_of(table_ref[s, 2] * 16, 16), extra)
                     x = [held[d, some, :] for d in range(n_rep)]
-                    put(acc, score(high_ref, low_ref, x, rep), start + table_ref[s, 1])
+                    put(acc, score(weight_ref, x, rep), start + table_ref[s, 1])
         for_feats(lambda at: acc[:rows // 8, :, at].reshape(rows, width // n_feat), outs)
 
     count = n_shard * bulk
@@ -509,8 +511,8 @@
     return pl.pallas_call(
         kernel,
         in_specs=[SMEM] + [VMEM] * (2 + n_other + n_rep * n_piece) + [ANY] * len(surplus),
-        out_specs=[VMEM] * (2 + n_feat),
-        out_shape=[jax.ShapeDtypeStruct((depth, width), BF16)] * 2 + feat_shapes(rows, width, n_feat),
+        out_specs=[VMEM] * (1 + n_feat),
+        out_shape=[jax.ShapeDtypeStruct((depth, 2 * width), BF16)] + feat_shapes(rows, width, n_feat),
         scratch_shapes=[
             pltpu.VMEM((n_shard, bulk // 8, 8, width), F32),
             pltpu.VMEM((n_rep, 3 * extra + 16, columns), BF16),
@@ -523,29 +525,27 @@
     )(table, own, *others, mine, *[p for parts in pieces for p in parts], *surplus)
 
 
-def late_scores(pieces, high, low, n_feat):
+def late_scores(pieces, weight, n_feat):
     n, n_rep = len(pieces), len(pieces[0])
-    size = pieces[0][0].shape[0]
-    rows = n * size
-    width = high.shape[1]
-
-    def kernel(high_ref, low_ref, *refs):
+    rows = sum(parts[0].shape[0] for parts in pieces)
+    width = weight.shape[1] // 2
+
+    def kernel(weight_ref, *refs):
         part_refs, outs, acc = refs[:n * n_rep], refs[n * n_rep:-1], refs[-1]
         parts = [jnp.concatenate([part_refs[j * n_rep + d][...] for j in range(n)]) for d in range(n_rep)]
-        y = score(high_ref, low_ref, parts, lax.axis_index("rep"))
-        acc[...] = y.reshape(rows, width)
+        acc[...] = score(weight_ref, parts, lax.axis_index("rep")).reshape(rows, width)
         for_feats(lambda at: acc[:, at], outs)
 
     return pl.pallas_call(
         kernel,
-        in_specs=[VMEM] * (2 + n * n_rep),
+        in_specs=[VMEM] * (1 + n * n_rep),
         out_specs=[VMEM] * n_feat,
         out_shape=feat_shapes(rows, width, n_feat),
         scratch_shapes=[pltpu.VMEM((rows, width), F32)],
-        cost_estimate=cost(4 * rows * high.size, 8 * rows * width),
+        cost_estimate=cost(4 * rows * weight.size, 8 * rows * width),
         compiler_params=PARAMS,
         name="late_scores",
-    )(high, low, *[p for parts in pieces for p in parts])
+    )(weight, *[p for parts in pieces for p in parts])
 
 
 def merge(table, early, late, n_shard):
@@ -603,7 +603,7 @@
     pieces = [picked[0]] + [shift(picked[d], "shard", n_shard, d) for d in range(1, n_shard)]
 
     middle = [(d, 0, bulk) for d in range(1, last_hops)]
-    part = 64 if bulk % 64 == 0 else bulk
+    part = 64 if bulk % 64 == 0 else bulk // 2
     final = [(last_hops, at, part) for at in range(0, bulk, part)]
     *packed, goal = pack_rows(train, ids, columns, bulk, extra, middle + final)
     firsts, seconds = [], []
@@ -660,7 +660,7 @@
     mark = shift(after(jnp.zeros((8, LANES), I32), *marks), "rep", n_rep, 1)
     last += [shift(x, "shard", n_shard, last_hops) for x in sent_last]
     ready = [with_rep(after(x, mark)) for x in here]
-    high, low, *early = early_scores(
+    weight, *early = early_scores(
         own, others, mine, ready, middle, firsts, seconds, table, rows, n_feat, n_rep, n_shard, bulk, extra
     )
 
@@ -668,7 +668,7 @@
         return [shares[0]] + [shift(shares[d], "feat", n_feat, d) for d in range(1, n_feat)]
 
     last_all += [with_rep(after(x, *early[1:])) for x in last[1:]]
-    late = late_scores(last_all, high, low, n_feat)
+    late = late_scores(last_all, weight, n_feat)
     return merge(table, over_feat(early), over_feat(late), n_shard)[None]
 
 

time: 95.5 us -> 95.5 us (level)
  no operation moved by 1% of the time
where the time goes in v16:
time: 95.5 us; the launch traced here: 95.2 us
  starting transfers between devices  33.4 us (35%)
  Pallas kernels  33.2 us (35%)
  waiting for transfers between devices  22.3 us (23%)
  local copies, waits for them, and re-layouts  5.05 us (5%)
  between operations  1 us (1%)
    ppermute x36, starting transfers between devices, shift(): return lax.ppermute(x, axis, [(i, (i + by) % size) for i in range(size)])  30 us
    ppermute x36, waiting for transfers between devices, shift(): return lax.ppermute(x, axis, [(i, (i + by) % size) for i in range(size)])  17.6 us
    pallas_call x1, Pallas kernels, partial_weights(): pl.pallas_call(kernel, in_specs=[SMEM] + [HBM] * n + [VMEM] * (CUTS * n)...  6.6 us
    pallas_call x1, Pallas kernels, pack_rows(): pl.pallas_call(kernel, grid=(1,), in_specs=[pl.BlockSpec((lines, LANES),...  6.25 us
    pallas_call x1, Pallas kernels, early_scores(): pl.pallas_call(kernel, in_specs=[SMEM] + [VMEM] * (2 + n_other + n_rep *...  5.07 us
    ppermute x2, waiting for transfers between devices, swap(): return lax.ppermute(x, axis, [(i, i ^ bit) for i in range(size)])  4.69 us
    unnamed x36, local copies, waits for them, and re-layouts  4.53 us
    ppermute x2, starting transfers between devices, swap(): return lax.ppermute(x, axis, [(i, i ^ bit) for i in range(size)])  3.35 us
  transfers between devices with their start and end apart: 38, of which 13 were waited for; matrix products, arithmetic and copies ran while one was open for 1% of the time, Pallas kernels for 33%

profile of v16, /device:TPU:0, one launch (start us, length us, event | category | flops | bytes accessed | tf_op | source)
XLA Modules:
  0.0 95.2 jit_solution(10751477387756190971)
XLA Ops:
  0.0 0.5 collective-permute-start.7
  0.5 2.7 %pick_queries.1 = (bf16[1,64,1024]{2,1,0:T(8,128)(2,1)}, bf16[1,64,1024]{2,1,0:T(8,128)(2,1)}, bf16[1,64,1024]{2,1,0:T(8,128)(2,1)}, bf16[1,64,1024]{2,1,0:T(8,128)(2,1)}) custom-call(s32[4,4]{1,0:T(4,128)} %pattern_ref.3, s32[16]{0:T(128)} %slot_ref.3, bf16[4,128,1024]{2,1,0:T(8,128)(2,1)} %in_ref.1), custom_call_target="tpu_custom_call" | custom-call | flops 1 | bytes 1 | tf_op jit(solution)/shard_map/pick_queries/pallas_call | solution.py:108
  3.2 2.8 %collective-permute-start.4 = (bf16[1,64,1024]{2,1,0:T(8,128)(2,1)}, bf16[1,64,1024]{2,1,0:T(8,128)(2,1)S(1)}, u32[]{:S(2)}, u32[]{:S(2)}) collective-permute-start(bf16[1,64,1024]{2,1,0:T(8,128)(2,1)} %get-tuple-element.49), channel_id=1, source_target_pairs={{0,4},{4,8},{8,12},{12,0},{1,5},{5,9},{9,13},{13,1},{2,6},{6,10},{... | collective-permute-start | bytes 393224 | tf_op jit(solution)/shard_map/ppermute | solution.py:22
  5.9 2.6 %collective-permute-start.5 = (bf16[1,64,1024]{2,1,0:T(8,128)(2,1)}, bf16[1,64,1024]{2,1,0:T(8,128)(2,1)S(1)}, u32[]{:S(2)}, u32[]{:S(2)}) collective-permute-start(bf16[1,64,1024]{2,1,0:T(8,128)(2,1)} %get-tuple-element.50), channel_id=1, source_target_pairs={{0,8},{4,12},{8,0},{12,4},{1,9},{5,13},{9,1},{13,5},{2,10},{6,14},... | collective-permute-start | bytes 393224 | tf_op jit(solution)/shard_map/ppermute | solution.py:22
  8.5 1.3 %collective-permute-start.6 = (bf16[1,64,1024]{2,1,0:T(8,128)(2,1)}, bf16[1,64,1024]{2,1,0:T(8,128)(2,1)S(1)}, u32[]{:S(2)}, u32[]{:S(2)}) collective-permute-start(bf16[1,64,1024]{2,1,0:T(8,128)(2,1)} %get-tuple-element.51), channel_id=1, source_target_pairs={{0,12},{4,0},{8,4},{12,8},{1,13},{5,1},{9,5},{13,9},{2,14},{6,2},{... | collective-permute-start | bytes 393224 | tf_op jit(solution)/shard_map/ppermute | solution.py:22
  9.9 1.5 %collective-permute-start.8 = (bf16[1,64,1024]{2,1,0:T(8,128)(2,1)}, bf16[1,64,1024]{2,1,0:T(8,128)(2,1)S(1)}, u32[]{:S(2)}, u32[]{:S(2)}) collective-permute-start(bf16[1,64,1024]{2,1,0:T(8,128)(2,1)} %get-tuple-element.53.refs_0_), channel_id=1, source_target_pairs={{0,16},{16,0},{1,17},{17,1},{2,18},{18,2},{3,19},{19,3},{4,20},{20... | collective-permute-start | bytes 393224 | tf_op jit(solution)/shard_map/ppermute | solution.py:22
  11.4 6.2 %pack_rows.1 = (bf16[256,1024]{1,0:T(8,128)(2,1)}, bf16[256,1024]{1,0:T(8,128)(2,1)}, bf16[64,1024]{1,0:T(8,128)(2,1)}, bf16[64,1024]{1,0:T(8,128)(2,1)}, bf16[6...) custom-call(s32[32,128]{1,0:T(8,128)} %bitcast.11, ...), custom_call_target="tpu_custom_call" | custom-call | flops 1 | bytes 1 | tf_op jit(solution)/shard_map/pack_rows/pallas_call | solution.py:252
  17.9 3.3 %collective-permute-start.21 = (bf16[256,1024]{1,0:T(8,128)(2,1)}, bf16[256,1024]{1,0:T(8,128)(2,1)S(1)}, u32[]{:S(2)}, u32[]{:S(2)}) collective-permute-start(bf16[256,1024]{1,0:T(8,128)(2,1)} %after.17), channel_id=1, source_target_pairs={{0,4},{4,8},{8,12},{12,0},{1,5},{5,9},{9,13},{13,1},{2,6},{6,10},{... | collective-permute-start | bytes 1572872 | tf_op jit(solution)/shard_map/ppermute | solution.py:22
  21.2 1.5 %collective-permute-start.9 = (bf16[1,64,1024]{2,1,0:T(8,128)(2,1)S(1)}, bf16[1,64,1024]{2,1,0:T(8,128)(2,1)S(1)}, u32[]{:S(2)}, u32[]{:S(2)}) collective-permute-start(bf16[1,64,1024]{2,1,0:T(8,128)(2,1)S(1)} %collective-permute-done.4.rest_0_.refs_2_.refs_1_), channel_id=1, source_target_pairs={{0,16},{16,0},{1,17},{17,1},{2,18},{18,2},{3,19},{19,3},{4,20},{20... | collective-permute-start | bytes 393224 | tf_op jit(solution)/shard_map/ppermute | solution.py:22
  22.7 0.5 collective-permute-start.10
  23.2 1.5 %collective-permute-start.11 = (bf16[1,64,1024]{2,1,0:T(8,128)(2,1)S(1)}, bf16[1,64,1024]{2,1,0:T(8,128)(2,1)S(1)}, u32[]{:S(2)}, u32[]{:S(2)}) collective-permute-start(bf16[1,64,1024]{2,1,0:T(8,128)(2,1)S(1)} %collective-permute-done.6.rest_2_.refs_4_.refs_3_), channel_id=1, source_target_pairs={{0,16},{16,0},{1,17},{17,1},{2,18},{18,2},{3,19},{19,3},{4,20},{20... | collective-permute-start | bytes 393224 | tf_op jit(solution)/shard_map/ppermute | solution.py:22
  24.7 1.6 %collective-permute-start.25 = (bf16[128,1024]{1,0:T(8,128)(2,1)}, bf16[128,1024]{1,0:T(8,128)(2,1)S(1)}, u32[]{:S(2)}, u32[]{:S(2)}) collective-permute-start(bf16[128,1024]{1,0:T(8,128)(2,1)} %after.24), channel_id=1, source_target_pairs={{0,8},{4,12},{8,0},{12,4},{1,9},{5,13},{9,1},{13,5},{2,10},{6,14},... | collective-permute-start | bytes 786440 | tf_op jit(solution)/shard_map/ppermute | solution.py:26
  26.4 0.8 row_table.1
  27.2 3.4 %copy-done = bf16[1,4096,1024]{2,1,0:T(8,128)(2,1)S(1)} copy-done((bf16[1,4096,1024]{2,1,0:T(8,128)(2,1)S(1)}, bf16[1,4096,1024]{2,1,0:T(8,128)(2,1)}, u32[]{:S(2)}) %copy-start) | copy-done | bytes 8388632
  30.6 2.5 %fetch.1 = (bf16[2048,1024]{1,0:T(8,128)(2,1)S(1)}, bf16[2048,1024]{1,0:T(8,128)(2,1)S(1)}) custom-call(s32[1]{0:T(128)} %bitcast.3.block_ref, bf16[4096,1024]{1,0:T(8,128)(2,1)S(1)} %bitcast.7, bf16[4096,1024]{1,0:T(8,128)(2,1)} %collective-permute-done.7.refs_1_, bf16[1,64,1024]{2,1,0:T(8,128)(2,1)S(1)} %collective-permute-done.4.rest_0_.refs_2_.refs_1_, ...), custom_call_target="tpu_custom_call" | custom-call | flops 1 | bytes 1 | tf_op jit(solution)/shard_map/fetch/pallas_call | solution.py:325
  33.2 1.2 %join_queries.1 = (bf16[128,256]{1,0:T(8,128)(2,1)S(1)}, bf16[128,256]{1,0:T(8,128)(2,1)S(1)}, bf16[128,256]{1,0:T(8,128)(2,1)S(1)}, bf16[128,256]{1,0:T(8,128)(...) custom-call(s32[4,4]{1,0:T(4,128)S(1)} %copy-done.12, ...), custom_call_target="tpu_custom_call" | custom-call | flops 1 | bytes 1 | tf_op jit(solution)/shard_map/join_queries/pallas_call | solution.py:153
  34.5 0.5 collective-permute-start.13
  35.1 0.7 collective-permute-done.12.refs_10_
  35.9 0.4 collective-permute-start.16
  36.5 0.6 collective-permute-done.15.refs_13_
  37.2 0.4 collective-permute-start.19
  37.6 0.7 collective-permute-start.22
  38.5 2.3 %fetched_weights.1.refs_18_.refs_2_.refs_4_ = bf16[2048,256]{1,0:T(8,128)(2,1)S(1)} custom-call(bf16[2048,1024]{1,0:T(8,128)(2,1)S(1)} %get-tuple-element.54.refs_8_.refs_0_, bf16[2048,1024]{1,0:T(8,128)(2,1)S(1)} %get-tuple-element.55.refs_9_.refs_1_, bf16[128,256]{1,0:T(8,128)(2,1)S(1)} %get-tuple-element.57.refs_2_, ...), custom_call_target="tpu_custom_call" | custom-call | flops 1 | bytes 1 | tf_op jit(solution)/shard_map/fetched_weights/pallas_call | solution.py:352
  40.8 4.7 %collective-permute-done.25.refs_1_.refs_0_.refs_2_ = bf16[128,1024]{1,0:T(8,128)(2,1)S(1)} collective-permute-done((bf16[128,1024]{1,0:T(8,128)(2,1)}, bf16[128,1024]{1,0:T(8,128)(2,1)S(1)}, u32[]{:S(2)}, u32[]{:S(2)}) %collective-permute-start.25) | collective-permute-done | bytes 262176 | tf_op jit(solution)/shard_map/ppermute | solution.py:26
  45.5 0.8 stack.3
  46.3 1.7 %collective-permute-start.26 = (bf16[256,1024]{1,0:T(8,128)(2,1)}, bf16[256,1024]{1,0:T(8,128)(2,1)}, u32[]{:S(2)}, u32[]{:S(2)}) collective-permute-start(bf16[256,1024]{1,0:T(8,128)(2,1)} %stack.3), channel_id=1, source_target_pairs={{0,4},{4,0},{8,12},{12,8},{1,5},{5,1},{9,13},{13,9},{2,6},{6,2},{1... | collective-permute-start | bytes 1572872 | tf_op jit(solution)/shard_map/ppermute | solution.py:26
  48.0 1.5 %collective-permute-start.20 = (bf16[2048,256]{1,0:T(8,128)(2,1)S(1)}, bf16[2048,256]{1,0:T(8,128)(2,1)}, u32[]{:S(2)}, u32[]{:S(2)}) collective-permute-start(bf16[2048,256]{1,0:T(8,128)(2,1)S(1)} %fetched_weights.1.refs_18_.refs_2_.refs_4_), channel_id=1, source_target_pairs={{0,2},{2,0},{1,3},{3,1},{4,6},{6,4},{5,7},{7,5},{8,10},{10,8},{9,1... | collective-permute-start | bytes 3145736 | tf_op jit(solution)/shard_map/ppermute | solution.py:22
  49.5 3.3 %collective-permute-start.31 = (bf16[256,1024]{1,0:T(8,128)(2,1)}, bf16[256,1024]{1,0:T(8,128)(2,1)}, u32[]{:S(2)}, u32[]{:S(2)}) collective-permute-start(bf16[256,1024]{1,0:T(8,128)(2,1)} %after.28), channel_id=1, source_target_pairs={{0,8},{4,12},{8,0},{12,4},{1,9},{5,13},{9,1},{13,5},{2,10},{6,14},... | collective-permute-start | bytes 1572872 | tf_op jit(solution)/shard_map/ppermute | solution.py:22
  52.9 1.5 %collective-permute-start.24 = (s32[8,128]{1,0:T(8,128)S(1)}, s32[8,128]{1,0:T(8,128)S(1)}, u32[]{:S(2)}, u32[]{:S(2)}) collective-permute-start(s32[8,128]{1,0:T(8,128)S(1)} %get-tuple-element.56.refs_10_), channel_id=1, source_target_pairs={{0,16},{16,0},{1,17},{17,1},{2,18},{18,2},{3,19},{19,3},{4,20},{20... | collective-permute-start | bytes 12296 | tf_op jit(solution)/shard_map/ppermute | solution.py:22
  54.4 2.1 %collective-permute-done.24 = s32[8,128]{1,0:T(8,128)S(1)} collective-permute-done((s32[8,128]{1,0:T(8,128)S(1)}, s32[8,128]{1,0:T(8,128)S(1)}, u32[]{:S(2)}, u32[]{:S(2)}) %collective-permute-start.24) | collective-permute-done | bytes 4128 | tf_op jit(solution)/shard_map/ppermute | solution.py:22
  56.5 0.5 slice.3
  57.6 6.6 %partial_weights.1.rest_0_.refs_1_.refs_2_.refs_0_ = f32[2048,256]{1,0:T(8,128)S(1)} custom-call(s32[1]{0:T(128)} %bitcast.1.block_ref, bf16[4096,1024]{1,0:T(8,128)(2,1)S(1)} %bitcast.10, bf16[4096,1024]{1,0:T(8,128)(2,1)} %collective-permute-done.7.refs_1_, bf16[128,256]{1,0:T(8,128)(2,1)S(1)} %get-tuple-element.57.refs_2_, ...), custom_call_target="tpu_custom_call" | custom-call | flops 1 | bytes 1 | tf_op jit(solution)/shard_map/partial_weights/pallas_call | solution.py:292
  64.6 0.5 collective-permute-start.28
  65.1 1.2 %collective-permute-done.27.refs_0_ = bf16[128,1024]{1,0:T(8,128)(2,1)S(1)} collective-permute-done((bf16[128,1024]{1,0:T(8,128)(2,1)}, bf16[128,1024]{1,0:T(8,128)(2,1)S(1)}, u32[]{:S(2)}, u32[]{:S(2)}) %collective-permute-start.27) | collective-permute-done | bytes 262176 | tf_op jit(solution)/shard_map/ppermute | solution.py:22
  66.8 2.4 %own_rows.1.refs_2_ = bf16[256,2048]{1,0:T(8,128)(2,1)S(1)} custom-call(s32[8,128]{1,0:T(8,128)S(1)} %copy-done.13, bf16[1024,2048]{1,0:T(8,128)(2,1)S(1)} %copy-done.1, f32[2048,256]{1,0:T(8,128)S(1)} %partial_weights.1.rest_0_.refs_1_.refs_2_.refs_0_), custom_call_target="tpu_custom_call" | custom-call | flops 1 | bytes 1 | tf_op jit(solution)/shard_map/own_rows/pallas_call | solution.py:194
  69.2 0.9 copy-done.6
  70.7 1.4 %collective-permute-done.29.refs_1_ = s32[8,128]{1,0:T(8,128)S(1)} collective-permute-done((s32[8,128]{1,0:T(8,128)S(1)}, s32[8,128]{1,0:T(8,128)S(1)}, u32[]{:S(2)}, u32[]{:S(2)}) %collective-permute-start.29) | collective-permute-done | bytes 4128 | tf_op jit(solution)/shard_map/ppermute | solution.py:22
  72.3 3.2 %collective-permute-done.31.refs_0_ = bf16[256,1024]{1,0:T(8,128)(2,1)} collective-permute-done((bf16[256,1024]{1,0:T(8,128)(2,1)}, bf16[256,1024]{1,0:T(8,128)(2,1)}, u32[]{:S(2)}, u32[]{:S(2)}) %collective-permute-start.31) | collective-permute-done | bytes 524320 | tf_op jit(solution)/shard_map/ppermute | solution.py:22
  75.5 2.4 %collective-permute-start.35 = (bf16[64,1024]{1,0:T(8,128)(2,1)S(1)}, bf16[64,1024]{1,0:T(8,128)(2,1)S(1)}, u32[]{:S(2)}, u32[]{:S(2)}) collective-permute-start(bf16[64,1024]{1,0:T(8,128)(2,1)S(1)} %after.18.refs_3_), channel_id=1, source_target_pairs={{0,12},{4,0},{8,4},{12,8},{1,13},{5,1},{9,5},{13,9},{2,14},{6,2},{... | collective-permute-start | bytes 393224 | tf_op jit(solution)/shard_map/ppermute | solution.py:22
  78.1 5.1 %early_scores.1 = (bf16[2048,512]{1,0:T(8,128)(2,1)S(1)}, f32[1024,128]{1,0:T(8,128)S(1)}, bf16[1024,128]{1,0:T(8,128)(2,1)S(1)}) custom-call(s32[4,4]{1,0:T(4,128)S(1)} %get-tuple-element.52.table_ref, f32[2048,256]{1,0:T(8,128)S(1)} %partial_weights.1.rest_0_.refs_1_.refs_2_.refs_0_, bf16[2048,256]{1,0:T(8,128)(2,1)} %collective-permute-done.20.refs_1_, ...), custom_call_target="tpu_custom_call" | custom-call | flops 1 | bytes 1 | tf_op jit(solution)/shard_map/early_scores/pallas_call | solution.py:511
  83.1 1.0 %collective-permute-start.34 = (bf16[1024,128]{1,0:T(8,128)(2,1)S(1)}, bf16[1024,128]{1,0:T(8,128)(2,1)S(1)}, u32[]{:S(2)}, u32[]{:S(2)}) collective-permute-start(bf16[1024,128]{1,0:T(8,128)(2,1)S(1)} %get-tuple-element.88.refs_1_), channel_id=1, source_target_pairs={{0,2},{2,0},{1,3},{3,1},{4,6},{6,4},{5,7},{7,5},{8,10},{10,8},{9,1... | collective-permute-start | bytes 786440 | tf_op jit(solution)/shard_map/ppermute | solution.py:22
  84.1 0.5 collective-permute-done.37.refs_0_
  84.6 2.4 %collective-permute-done.39.refs_0_ = bf16[64,1024]{1,0:T(8,128)(2,1)S(1)} collective-permute-done((bf16[64,1024]{1,0:T(8,128)(2,1)S(1)}, bf16[64,1024]{1,0:T(8,128)(2,1)S(1)}, u32[]{:S(2)}, u32[]{:S(2)}) %collective-permute-start.39) | collective-permute-done | bytes 131104 | tf_op jit(solution)/shard_map/ppermute | solution.py:22
  87.1 1.3 %collective-permute-done.40.refs_7_ = bf16[64,1024]{1,0:T(8,128)(2,1)S(1)} collective-permute-done((bf16[64,1024]{1,0:T(8,128)(2,1)S(1)}, bf16[64,1024]{1,0:T(8,128)(2,1)S(1)}, u32[]{:S(2)}, u32[]{:S(2)}) %collective-permute-start.40) | collective-permute-done | bytes 131104 | tf_op jit(solution)/shard_map/ppermute | solution.py:22
  88.4 0.8 late_scores.1
  89.2 0.6 collective-permute-start.41
  89.8 3.7 %collective-permute-done.41.refs_3_ = bf16[256,128]{1,0:T(8,128)(2,1)S(1)} collective-permute-done((bf16[256,128]{1,0:T(8,128)(2,1)S(1)}, bf16[256,128]{1,0:T(8,128)(2,1)S(1)}, u32[]{:S(2)}, u32[]{:S(2)}) %collective-permute-start.41) | collective-permute-done | bytes 65568 | tf_op jit(solution)/shard_map/ppermute | solution.py:22
  93.5 1.7 %merge.1 = f32[128,1024]{1,0:T(8,128)} custom-call(s32[4,4]{1,0:T(4,128)S(1)} %get-tuple-element.52.table_ref, f32[1024,128]{1,0:T(8,128)S(1)} %get-tuple-element.87.refs_0_, bf16[1024,128]{1,0:T(8,128)(2,1)S(1)} %collective-permute-done.34.refs_1_, f32[256,128]{1,0:T(8,128)S(1)} %get-tuple-element.90.refs_2_, ...), custom_call_target="tpu_custom_call" | custom-call | flops 1 | bytes 1 | tf_op jit(solution)/shard_map/merge/pallas_call | solution.py:571
  (101 shorter events, 2.8 us)
Async XLA Ops:
  0.0 26.4 %copy-start.11 = (s32[4096]{0:T(1024)S(1)}, s32[4096]{0:T(1024)}, u32[]{:S(2)}) copy-start(s32[4096]{0:T(1024)} %param.9) | copy-start | bytes 49156
  0.0 24.7 %collective-permute-start.7 = (bf16[4096,1024]{1,0:T(8,128)(2,1)}, bf16[4096,1024]{1,0:T(8,128)(2,1)}, u32[]{:S(2)}, u32[]{:S(2)}) collective-permute-start(bf16[4096,1024]{1,0:T(8,128)(2,1)} %bitcast.6), channel_id=1, source_target_pairs={{0,1},{1,0},{2,3},{3,2},{4,5},{5,4},{6,7},{7,6},{8,9},{9,8},{10,11... | collective-permute-start | bytes 25165832 | tf_op jit(solution)/shard_map/ppermute | solution.py:22
  3.2 14.5 %collective-permute-start.4 = (bf16[1,64,1024]{2,1,0:T(8,128)(2,1)}, bf16[1,64,1024]{2,1,0:T(8,128)(2,1)S(1)}, u32[]{:S(2)}, u32[]{:S(2)}) collective-permute-start(bf16[1,64,1024]{2,1,0:T(8,128)(2,1)} %get-tuple-element.49), channel_id=1, source_target_pairs={{0,4},{4,8},{8,12},{12,0},{1,5},{5,9},{9,13},{13,1},{2,6},{6,10},{... | collective-permute-start | bytes 393224 | tf_op jit(solution)/shard_map/ppermute | solution.py:22
  5.9 12.0 %collective-permute-start.5 = (bf16[1,64,1024]{2,1,0:T(8,128)(2,1)}, bf16[1,64,1024]{2,1,0:T(8,128)(2,1)S(1)}, u32[]{:S(2)}, u32[]{:S(2)}) collective-permute-start(bf16[1,64,1024]{2,1,0:T(8,128)(2,1)} %get-tuple-element.50), channel_id=1, source_target_pairs={{0,8},{4,12},{8,0},{12,4},{1,9},{5,13},{9,1},{13,5},{2,10},{6,14},... | collective-permute-start | bytes 393224 | tf_op jit(solution)/shard_map/ppermute | solution.py:22
  8.5 9.4 %collective-permute-start.6 = (bf16[1,64,1024]{2,1,0:T(8,128)(2,1)}, bf16[1,64,1024]{2,1,0:T(8,128)(2,1)S(1)}, u32[]{:S(2)}, u32[]{:S(2)}) collective-permute-start(bf16[1,64,1024]{2,1,0:T(8,128)(2,1)} %get-tuple-element.51), channel_id=1, source_target_pairs={{0,12},{4,0},{8,4},{12,8},{1,13},{5,1},{9,5},{13,9},{2,14},{6,2},{... | collective-permute-start | bytes 393224 | tf_op jit(solution)/shard_map/ppermute | solution.py:22
  9.9 13.3 %collective-permute-start.8 = (bf16[1,64,1024]{2,1,0:T(8,128)(2,1)}, bf16[1,64,1024]{2,1,0:T(8,128)(2,1)S(1)}, u32[]{:S(2)}, u32[]{:S(2)}) collective-permute-start(bf16[1,64,1024]{2,1,0:T(8,128)(2,1)} %get-tuple-element.53.refs_0_), channel_id=1, source_target_pairs={{0,16},{16,0},{1,17},{17,1},{2,18},{18,2},{3,19},{19,3},{4,20},{20... | collective-permute-start | bytes 393224 | tf_op jit(solution)/shard_map/ppermute | solution.py:22
  17.9 31.6 %collective-permute-start.21 = (bf16[256,1024]{1,0:T(8,128)(2,1)}, bf16[256,1024]{1,0:T(8,128)(2,1)S(1)}, u32[]{:S(2)}, u32[]{:S(2)}) collective-permute-start(bf16[256,1024]{1,0:T(8,128)(2,1)} %after.17), channel_id=1, source_target_pairs={{0,4},{4,8},{8,12},{12,0},{1,5},{5,9},{9,13},{13,1},{2,6},{6,10},{... | collective-permute-start | bytes 1572872 | tf_op jit(solution)/shard_map/ppermute | solution.py:22
  21.2 12.0 %collective-permute-start.9 = (bf16[1,64,1024]{2,1,0:T(8,128)(2,1)S(1)}, bf16[1,64,1024]{2,1,0:T(8,128)(2,1)S(1)}, u32[]{:S(2)}, u32[]{:S(2)}) collective-permute-start(bf16[1,64,1024]{2,1,0:T(8,128)(2,1)S(1)} %collective-permute-done.4.rest_0_.refs_2_.refs_1_), channel_id=1, source_target_pairs={{0,16},{16,0},{1,17},{17,1},{2,18},{18,2},{3,19},{19,3},{4,20},{20... | collective-permute-start | bytes 393224 | tf_op jit(solution)/shard_map/ppermute | solution.py:22
  22.7 10.4 %collective-permute-start.10 = (bf16[1,64,1024]{2,1,0:T(8,128)(2,1)S(1)}, bf16[1,64,1024]{2,1,0:T(8,128)(2,1)S(1)}, u32[]{:S(2)}, u32[]{:S(2)}) collective-permute-start(bf16[1,64,1024]{2,1,0:T(8,128)(2,1)S(1)} %collective-permute-done.5.rest_1_.refs_3_.refs_2_), channel_id=1, source_target_pairs={{0,16},{16,0},{1,17},{17,1},{2,18},{18,2},{3,19},{19,3},{4,20},{20... | collective-permute-start | bytes 393224 | tf_op jit(solution)/shard_map/ppermute | solution.py:22
  23.2 9.9 %collective-permute-start.11 = (bf16[1,64,1024]{2,1,0:T(8,128)(2,1)S(1)}, bf16[1,64,1024]{2,1,0:T(8,128)(2,1)S(1)}, u32[]{:S(2)}, u32[]{:S(2)}) collective-permute-start(bf16[1,64,1024]{2,1,0:T(8,128)(2,1)S(1)} %collective-permute-done.6.rest_2_.refs_4_.refs_3_), channel_id=1, source_target_pairs={{0,16},{16,0},{1,17},{17,1},{2,18},{18,2},{3,19},{19,3},{4,20},{20... | collective-permute-start | bytes 393224 | tf_op jit(solution)/shard_map/ppermute | solution.py:22
  24.7 20.7 %collective-permute-start.25 = (bf16[128,1024]{1,0:T(8,128)(2,1)}, bf16[128,1024]{1,0:T(8,128)(2,1)S(1)}, u32[]{:S(2)}, u32[]{:S(2)}) collective-permute-start(bf16[128,1024]{1,0:T(8,128)(2,1)} %after.24), channel_id=1, source_target_pairs={{0,8},{4,12},{8,0},{12,4},{1,9},{5,13},{9,1},{13,5},{2,10},{6,14},... | collective-permute-start | bytes 786440 | tf_op jit(solution)/shard_map/ppermute | solution.py:26
  27.2 3.4 %copy-start = (bf16[1,4096,1024]{2,1,0:T(8,128)(2,1)S(1)}, bf16[1,4096,1024]{2,1,0:T(8,128)(2,1)}, u32[]{:S(2)}) copy-start(bf16[1,4096,1024]{2,1,0:T(8,128)(2,1)} %param.10) | copy-start | bytes 25165828
  30.6 2.6 %copy-start.14 = (s32[16]{0:T(128)S(1)}, s32[16]{0:T(128)}, u32[]{:S(2)}) copy-start(s32[16]{0:T(128)} %slot_ref.3) | copy-start | bytes 196
  33.2 4.3 %copy-start.10 = (bf16[64,1024]{1,0:T(8,128)(2,1)S(1)}, bf16[64,1024]{1,0:T(8,128)(2,1)}, u32[]{:S(2)}) copy-start(bf16[64,1024]{1,0:T(8,128)(2,1)} %get-tuple-element.78.refs_0_) | copy-start | bytes 393220
  34.5 1.3 %collective-permute-start.12 = (bf16[128,256]{1,0:T(8,128)(2,1)S(1)}, bf16[128,256]{1,0:T(8,128)(2,1)S(1)}, u32[]{:S(2)}, u32[]{:S(2)}) collective-permute-start(bf16[128,256]{1,0:T(8,128)(2,1)S(1)} %get-tuple-element.65), channel_id=1, source_target_pairs={{0,1},{1,0},{2,3},{3,2},{4,5},{5,4},{6,7},{7,6},{8,9},{9,8},{10,11... | collective-permute-start | bytes 196616 | tf_op jit(solution)/shard_map/ppermute | solution.py:22
  34.5 1.4 %collective-permute-start.13 = (bf16[128,256]{1,0:T(8,128)(2,1)S(1)}, bf16[128,256]{1,0:T(8,128)(2,1)S(1)}, u32[]{:S(2)}, u32[]{:S(2)}) collective-permute-start(bf16[128,256]{1,0:T(8,128)(2,1)S(1)} %get-tuple-element.66), channel_id=1, source_target_pairs={{0,1},{1,0},{2,3},{3,2},{4,5},{5,4},{6,7},{7,6},{8,9},{9,8},{10,11... | collective-permute-start | bytes 196616 | tf_op jit(solution)/shard_map/ppermute | solution.py:22
  35.0 1.3 %collective-permute-start.14 = (bf16[128,256]{1,0:T(8,128)(2,1)S(1)}, bf16[128,256]{1,0:T(8,128)(2,1)S(1)}, u32[]{:S(2)}, u32[]{:S(2)}) collective-permute-start(bf16[128,256]{1,0:T(8,128)(2,1)S(1)} %get-tuple-element.67), channel_id=1, source_target_pairs={{0,1},{1,0},{2,3},{3,2},{4,5},{5,4},{6,7},{7,6},{8,9},{9,8},{10,11... | collective-permute-start | bytes 196616 | tf_op jit(solution)/shard_map/ppermute | solution.py:22
  35.8 1.3 %collective-permute-start.15 = (bf16[128,256]{1,0:T(8,128)(2,1)S(1)}, bf16[128,256]{1,0:T(8,128)(2,1)S(1)}, u32[]{:S(2)}, u32[]{:S(2)}) collective-permute-start(bf16[128,256]{1,0:T(8,128)(2,1)S(1)} %get-tuple-element.68), channel_id=1, source_target_pairs={{0,1},{1,0},{2,3},{3,2},{4,5},{5,4},{6,7},{7,6},{8,9},{9,8},{10,11... | collective-permute-start | bytes 196616 | tf_op jit(solution)/shard_map/ppermute | solution.py:22
  35.9 1.3 %collective-permute-start.16 = (bf16[128,256]{1,0:T(8,128)(2,1)S(1)}, bf16[128,256]{1,0:T(8,128)(2,1)S(1)}, u32[]{:S(2)}, u32[]{:S(2)}) collective-permute-start(bf16[128,256]{1,0:T(8,128)(2,1)S(1)} %get-tuple-element.69), channel_id=1, source_target_pairs={{0,1},{1,0},{2,3},{3,2},{4,5},{5,4},{6,7},{7,6},{8,9},{9,8},{10,11... | collective-permute-start | bytes 196616 | tf_op jit(solution)/shard_map/ppermute | solution.py:22
  36.3 1.3 %collective-permute-start.17 = (bf16[128,256]{1,0:T(8,128)(2,1)S(1)}, bf16[128,256]{1,0:T(8,128)(2,1)S(1)}, u32[]{:S(2)}, u32[]{:S(2)}) collective-permute-start(bf16[128,256]{1,0:T(8,128)(2,1)S(1)} %get-tuple-element.70), channel_id=1, source_target_pairs={{0,1},{1,0},{2,3},{3,2},{4,5},{5,4},{6,7},{7,6},{8,9},{9,8},{10,11... | collective-permute-start | bytes 196616 | tf_op jit(solution)/shard_map/ppermute | solution.py:22
  37.0 1.3 %collective-permute-start.18 = (bf16[128,256]{1,0:T(8,128)(2,1)S(1)}, bf16[128,256]{1,0:T(8,128)(2,1)S(1)}, u32[]{:S(2)}, u32[]{:S(2)}) collective-permute-start(bf16[128,256]{1,0:T(8,128)(2,1)S(1)} %get-tuple-element.71), channel_id=1, source_target_pairs={{0,1},{1,0},{2,3},{3,2},{4,5},{5,4},{6,7},{7,6},{8,9},{9,8},{10,11... | collective-permute-start | bytes 196616 | tf_op jit(solution)/shard_map/ppermute | solution.py:22
  37.2 1.3 %collective-permute-start.19 = (bf16[128,256]{1,0:T(8,128)(2,1)S(1)}, bf16[128,256]{1,0:T(8,128)(2,1)S(1)}, u32[]{:S(2)}, u32[]{:S(2)}) collective-permute-start(bf16[128,256]{1,0:T(8,128)(2,1)S(1)} %get-tuple-element.72), channel_id=1, source_target_pairs={{0,1},{1,0},{2,3},{3,2},{4,5},{5,4},{6,7},{7,6},{8,9},{9,8},{10,11... | collective-permute-start | bytes 196616 | tf_op jit(solution)/shard_map/ppermute | solution.py:22
  37.6 12.0 %collective-permute-start.22 = (bf16[64,1024]{1,0:T(8,128)(2,1)S(1)}, bf16[64,1024]{1,0:T(8,128)(2,1)S(1)}, u32[]{:S(2)}, u32[]{:S(2)}) collective-permute-start(bf16[64,1024]{1,0:T(8,128)(2,1)S(1)} %after.21), channel_id=1, source_target_pairs={{0,12},{4,0},{8,4},{12,8},{1,13},{5,1},{9,5},{13,9},{2,14},{6,2},{... | collective-permute-start | bytes 393224 | tf_op jit(solution)/shard_map/ppermute | solution.py:22
  38.4 19.2 %slice-start = ((s8[8388608]{0:T(1024)(128)(4,1)}), s8[4194304]{0:T(1024)(128)(4,1)S(1)}, s32[]{:S(2)}) async-start(s8[8388608]{0:T(1024)(128)(4,1)} %bitcast.8), calls=%async_computation | async-start | bytes 8388608
  38.5 7.0 %copy-start.4 = (bf16[128,1024]{1,0:T(8,128)(2,1)S(1)}, bf16[128,1024]{1,0:T(8,128)(2,1)}, u32[]{:S(2)}) copy-start(bf16[128,1024]{1,0:T(8,128)(2,1)} %get-tuple-element.81.refs_0_) | copy-start | bytes 786436
  38.5 19.2 %slice-start.1 = ((s8[8388608]{0:T(1024)(128)(4,1)}), s8[4194304]{0:T(1024)(128)(4,1)S(1)}, s32[]{:S(2)}) async-start(s8[8388608]{0:T(1024)(128)(4,1)} %bitcast.8), calls=%async_computation.1 | async-start | bytes 8388608
  46.3 23.8 %collective-permute-start.26 = (bf16[256,1024]{1,0:T(8,128)(2,1)}, bf16[256,1024]{1,0:T(8,128)(2,1)}, u32[]{:S(2)}, u32[]{:S(2)}) collective-permute-start(bf16[256,1024]{1,0:T(8,128)(2,1)} %stack.3), channel_id=1, source_target_pairs={{0,4},{4,0},{8,12},{12,8},{1,5},{5,1},{9,13},{13,9},{2,6},{6,2},{1... | collective-permute-start | bytes 1572872 | tf_op jit(solution)/shard_map/ppermute | solution.py:26
  48.0 29.8 %collective-permute-start.20 = (bf16[2048,256]{1,0:T(8,128)(2,1)S(1)}, bf16[2048,256]{1,0:T(8,128)(2,1)}, u32[]{:S(2)}, u32[]{:S(2)}) collective-permute-start(bf16[2048,256]{1,0:T(8,128)(2,1)S(1)} %fetched_weights.1.refs_18_.refs_2_.refs_4_), channel_id=1, source_target_pairs={{0,2},{2,0},{1,3},{3,1},{4,6},{6,4},{5,7},{7,5},{8,10},{10,8},{9,1... | collective-permute-start | bytes 3145736 | tf_op jit(solution)/shard_map/ppermute | solution.py:22
  49.5 8.1 %copy-start.2 = (bf16[256,1024]{1,0:T(8,128)(2,1)}, bf16[256,1024]{1,0:T(8,128)(2,1)S(1)}, u32[]{:S(2)}) copy-start(bf16[256,1024]{1,0:T(8,128)(2,1)S(1)} %collective-permute-done.21.refs_0_.refs_1_) | copy-start | bytes 1572868
  49.5 26.0 %collective-permute-start.31 = (bf16[256,1024]{1,0:T(8,128)(2,1)}, bf16[256,1024]{1,0:T(8,128)(2,1)}, u32[]{:S(2)}, u32[]{:S(2)}) collective-permute-start(bf16[256,1024]{1,0:T(8,128)(2,1)} %after.28), channel_id=1, source_target_pairs={{0,8},{4,12},{8,0},{12,4},{1,9},{5,13},{9,1},{13,5},{2,10},{6,14},... | collective-permute-start | bytes 1572872 | tf_op jit(solution)/shard_map/ppermute | solution.py:22
  52.9 3.6 %collective-permute-start.24 = (s32[8,128]{1,0:T(8,128)S(1)}, s32[8,128]{1,0:T(8,128)S(1)}, u32[]{:S(2)}, u32[]{:S(2)}) collective-permute-start(s32[8,128]{1,0:T(8,128)S(1)} %get-tuple-element.56.refs_10_), channel_id=1, source_target_pairs={{0,16},{16,0},{1,17},{17,1},{2,18},{18,2},{3,19},{19,3},{4,20},{20... | collective-permute-start | bytes 12296 | tf_op jit(solution)/shard_map/ppermute | solution.py:22
  57.6 6.6 %copy-start.15 = (bf16[128,1024]{1,0:T(8,128)(2,1)S(1)}, bf16[128,1024]{1,0:T(8,128)(2,1)}, u32[]{:S(2)}) copy-start(bf16[128,1024]{1,0:T(8,128)(2,1)} %get-tuple-element.79.refs_0_) | copy-start | bytes 786436
  64.5 1.8 %collective-permute-start.27 = (bf16[128,1024]{1,0:T(8,128)(2,1)}, bf16[128,1024]{1,0:T(8,128)(2,1)S(1)}, u32[]{:S(2)}, u32[]{:S(2)}) collective-permute-start(bf16[128,1024]{1,0:T(8,128)(2,1)} %get-tuple-element.81.refs_0_), channel_id=1, source_target_pairs={{0,1},{1,0},{2,3},{3,2},{4,5},{5,4},{6,7},{7,6},{8,9},{9,8},{10,11... | collective-permute-start | bytes 786440 | tf_op jit(solution)/shard_map/ppermute | solution.py:22
  64.6 5.4 %collective-permute-start.28 = (bf16[128,1024]{1,0:T(8,128)(2,1)S(1)}, bf16[128,1024]{1,0:T(8,128)(2,1)S(1)}, u32[]{:S(2)}, u32[]{:S(2)}) collective-permute-start(bf16[128,1024]{1,0:T(8,128)(2,1)S(1)} %after.25.refs_1_), channel_id=1, source_target_pairs={{0,1},{1,0},{2,3},{3,2},{4,5},{5,4},{6,7},{7,6},{8,9},{9,8},{10,11... | collective-permute-start | bytes 786440 | tf_op jit(solution)/shard_map/ppermute | solution.py:22
  66.3 3.7 %collective-permute-start.23 = (bf16[64,1024]{1,0:T(8,128)(2,1)S(1)}, bf16[64,1024]{1,0:T(8,128)(2,1)S(1)}, u32[]{:S(2)}, u32[]{:S(2)}) collective-permute-start(bf16[64,1024]{1,0:T(8,128)(2,1)S(1)} %after.22.refs_0_), channel_id=1, source_target_pairs={{0,1},{1,0},{2,3},{3,2},{4,5},{5,4},{6,7},{7,6},{8,9},{9,8},{10,11... | collective-permute-start | bytes 393224 | tf_op jit(solution)/shard_map/ppermute | solution.py:22
  66.5 2.6 %copy-start.8 = (bf16[64,1024]{1,0:T(8,128)(2,1)S(1)}, bf16[64,1024]{1,0:T(8,128)(2,1)}, u32[]{:S(2)}) copy-start(bf16[64,1024]{1,0:T(8,128)(2,1)} %get-tuple-element.75.refs_0_) | copy-start | bytes 393220
  70.1 7.8 %collective-permute-start.33 = (bf16[256,1024]{1,0:T(8,128)(2,1)}, bf16[256,1024]{1,0:T(8,128)(2,1)S(1)}, u32[]{:S(2)}, u32[]{:S(2)}) collective-permute-start(bf16[256,1024]{1,0:T(8,128)(2,1)} %after.30.refs_9_), channel_id=1, source_target_pairs={{0,1},{1,0},{2,3},{3,2},{4,5},{5,4},{6,7},{7,6},{8,9},{9,8},{10,11... | collective-permute-start | bytes 1572872 | tf_op jit(solution)/shard_map/ppermute | solution.py:22
  70.4 1.7 %collective-permute-start.29 = (s32[8,128]{1,0:T(8,128)S(1)}, s32[8,128]{1,0:T(8,128)S(1)}, u32[]{:S(2)}, u32[]{:S(2)}) collective-permute-start(s32[8,128]{1,0:T(8,128)S(1)} %after.26), channel_id=1, source_target_pairs={{0,1},{1,0},{2,3},{3,2},{4,5},{5,4},{6,7},{7,6},{8,9},{9,8},{10,11... | collective-permute-start | bytes 12296 | tf_op jit(solution)/shard_map/ppermute | solution.py:22
  72.1 5.9 %collective-permute-start.30 = (bf16[256,1024]{1,0:T(8,128)(2,1)S(1)}, bf16[256,1024]{1,0:T(8,128)(2,1)S(1)}, u32[]{:S(2)}, u32[]{:S(2)}) collective-permute-start(bf16[256,1024]{1,0:T(8,128)(2,1)S(1)} %after.27.refs_3_), channel_id=1, source_target_pairs={{0,1},{1,0},{2,3},{3,2},{4,5},{5,4},{6,7},{7,6},{8,9},{9,8},{10,11... | collective-permute-start | bytes 1572872 | tf_op jit(solution)/shard_map/ppermute | solution.py:22
  75.5 2.5 %collective-permute-start.32 = (bf16[256,1024]{1,0:T(8,128)(2,1)}, bf16[256,1024]{1,0:T(8,128)(2,1)S(1)}, u32[]{:S(2)}, u32[]{:S(2)}) collective-permute-start(bf16[256,1024]{1,0:T(8,128)(2,1)} %after.29.refs_5_), channel_id=1, source_target_pairs={{0,1},{1,0},{2,3},{3,2},{4,5},{5,4},{6,7},{7,6},{8,9},{9,8},{10,11... | collective-permute-start | bytes 1572872 | tf_op jit(solution)/shard_map/ppermute | solution.py:22
  75.5 8.6 %collective-permute-start.35 = (bf16[64,1024]{1,0:T(8,128)(2,1)S(1)}, bf16[64,1024]{1,0:T(8,128)(2,1)S(1)}, u32[]{:S(2)}, u32[]{:S(2)}) collective-permute-start(bf16[64,1024]{1,0:T(8,128)(2,1)S(1)} %after.18.refs_3_), channel_id=1, source_target_pairs={{0,12},{4,0},{8,4},{12,8},{1,13},{5,1},{9,5},{13,9},{2,14},{6,2},{... | collective-permute-start | bytes 393224 | tf_op jit(solution)/shard_map/ppermute | solution.py:22
  77.9 6.7 %collective-permute-start.37 = (bf16[64,1024]{1,0:T(8,128)(2,1)S(1)}, bf16[64,1024]{1,0:T(8,128)(2,1)S(1)}, u32[]{:S(2)}, u32[]{:S(2)}) collective-permute-start(bf16[64,1024]{1,0:T(8,128)(2,1)S(1)} %after.19.refs_4_), channel_id=1, source_target_pairs={{0,12},{4,0},{8,4},{12,8},{1,13},{5,1},{9,5},{13,9},{2,14},{6,2},{... | collective-permute-start | bytes 393224 | tf_op jit(solution)/shard_map/ppermute | solution.py:22
  77.9 9.1 %collective-permute-start.39 = (bf16[64,1024]{1,0:T(8,128)(2,1)S(1)}, bf16[64,1024]{1,0:T(8,128)(2,1)S(1)}, u32[]{:S(2)}, u32[]{:S(2)}) collective-permute-start(bf16[64,1024]{1,0:T(8,128)(2,1)S(1)} %after.20.refs_5_), channel_id=1, source_target_pairs={{0,12},{4,0},{8,4},{12,8},{1,13},{5,1},{9,5},{13,9},{2,14},{6,2},{... | collective-permute-start | bytes 393224 | tf_op jit(solution)/shard_map/ppermute | solution.py:22
  83.1 10.4 %collective-permute-start.34 = (bf16[1024,128]{1,0:T(8,128)(2,1)S(1)}, bf16[1024,128]{1,0:T(8,128)(2,1)S(1)}, u32[]{:S(2)}, u32[]{:S(2)}) collective-permute-start(bf16[1024,128]{1,0:T(8,128)(2,1)S(1)} %get-tuple-element.88.refs_1_), channel_id=1, source_target_pairs={{0,2},{2,0},{1,3},{3,1},{4,6},{6,4},{5,7},{7,5},{8,10},{10,8},{9,1... | collective-permute-start | bytes 786440 | tf_op jit(solution)/shard_map/ppermute | solution.py:22
  84.1 2.9 %collective-permute-start.36 = (bf16[64,1024]{1,0:T(8,128)(2,1)S(1)}, bf16[64,1024]{1,0:T(8,128)(2,1)S(1)}, u32[]{:S(2)}, u32[]{:S(2)}) collective-permute-start(bf16[64,1024]{1,0:T(8,128)(2,1)S(1)} %after.31.refs_2_), channel_id=1, source_target_pairs={{0,1},{1,0},{2,3},{3,2},{4,5},{5,4},{6,7},{7,6},{8,9},{9,8},{10,11... | collective-permute-start | bytes 393224 | tf_op jit(solution)/shard_map/ppermute | solution.py:22
  84.6 2.4 %collective-permute-start.38 = (bf16[64,1024]{1,0:T(8,128)(2,1)S(1)}, bf16[64,1024]{1,0:T(8,128)(2,1)S(1)}, u32[]{:S(2)}, u32[]{:S(2)}) collective-permute-start(bf16[64,1024]{1,0:T(8,128)(2,1)S(1)} %after.32.refs_4_), channel_id=1, source_target_pairs={{0,1},{1,0},{2,3},{3,2},{4,5},{5,4},{6,7},{7,6},{8,9},{9,8},{10,11... | collective-permute-start | bytes 393224 | tf_op jit(solution)/shard_map/ppermute | solution.py:22
  87.0 1.3 %collective-permute-start.40 = (bf16[64,1024]{1,0:T(8,128)(2,1)S(1)}, bf16[64,1024]{1,0:T(8,128)(2,1)S(1)}, u32[]{:S(2)}, u32[]{:S(2)}) collective-permute-start(bf16[64,1024]{1,0:T(8,128)(2,1)S(1)} %after.33.refs_6_), channel_id=1, source_target_pairs={{0,1},{1,0},{2,3},{3,2},{4,5},{5,4},{6,7},{7,6},{8,9},{9,8},{10,11... | collective-permute-start | bytes 393224 | tf_op jit(solution)/shard_map/ppermute | solution.py:22
  89.2 4.3 %collective-permute-start.41 = (bf16[256,128]{1,0:T(8,128)(2,1)S(1)}, bf16[256,128]{1,0:T(8,128)(2,1)S(1)}, u32[]{:S(2)}, u32[]{:S(2)}) collective-permute-start(bf16[256,128]{1,0:T(8,128)(2,1)S(1)} %get-tuple-element.91), channel_id=1, source_target_pairs={{0,2},{2,0},{1,3},{3,1},{4,6},{6,4},{5,7},{7,5},{8,10},{10,8},{9,1... | collective-permute-start | bytes 196616 | tf_op jit(solution)/shard_map/ppermute | solution.py:22
  (8 other events, 16.7 us)

commit v17 on v16

--- a/solution.py
+++ b/solution.py
@@ -13,6 +13,7 @@
 HBM = pl.BlockSpec(memory_space=pltpu.HBM)
 SMEM = pl.BlockSpec(memory_space=pltpu.SMEM)
 PARAMS = pltpu.CompilerParams(vmem_limit_bytes=24 * 2**20)
+WIDE = pltpu.CompilerParams(vmem_limit_bytes=32 * 2**20)
 FIRST = pltpu.CompilerParams(vmem_limit_bytes=60 * 2**20)
 LANES = 128
 CUTS = 8
@@ -471,10 +472,21 @@
         weight_ref[:, :width] = high
         weight_ref[:, width:] = (weight - high.astype(F32)).astype(BF16)
 
-        scored[me] = score(weight_ref, [mine_ref[...]], jnp.int32(0))
-        for parts, (hops, first, size) in zip(piece_refs, cuts):
+        total = None
+        for d in range(n_rep):
+            block = lax.rem(rep + (n_rep - d), jnp.int32(n_rep)) * columns
+            block = pl.ds(pl.multiple_of(block, columns), columns)
+            x = jnp.concatenate([mine_ref[:, block], *[parts[d][...] for parts in piece_refs]])
+            value = dot(x, weight_ref[block, :])
+            total = value if total is None else total + value
+        total = total[:, :width] + total[:, width:]
+        total = total.reshape(total.shape[0] // 8, 8, width)
+        scored[me] = total[:bulk // 8]
+        at = bulk // 8
+        for hops, first, size in cuts:
             source = lax.rem(me + (n_shard - hops), jnp.int32(n_shard))
-            scored[source, first // 8:(first + size) // 8] = score(weight_ref, [p[...] for p in parts], rep)
+            scored[source, first // 8:(first + size) // 8] = total[at:at + size // 8]
+            at += size // 8
         last = lax.rem(me + (n_shard - last_hops), jnp.int32(n_shard))
         for s in range(n_shard):
             start = table_ref[s, 0]
@@ -520,7 +532,7 @@
             pltpu.SemaphoreType.DMA((2 * n_rep,)),
         ],
         cost_estimate=cost(4 * count * depth * width, 10 * depth * width + count * (2 * depth + 4 * width)),
-        compiler_params=PARAMS,
+        compiler_params=WIDE,
         name="early_scores",
     )(table, own, *others, mine, *[p for parts in pieces for p in parts], *surplus)
 
@@ -603,8 +615,9 @@
     pieces = [picked[0]] + [shift(picked[d], "shard", n_shard, d) for d in range(1, n_shard)]
 
     middle = [(d, 0, bulk) for d in range(1, last_hops)]
-    part = 64 if bulk % 64 == 0 else bulk // 2
-    final = [(last_hops, at, part) for at in range(0, bulk, part)]
+    fillers = 2 if bulk % 128 == 0 else 1
+    sizes = [n * bulk // 8 for n in (2, 1, 2, 2, 1)] if bulk % 128 == 0 else [bulk // 2] * 2
+    final = [(last_hops, sum(sizes[:j]), n) for j, n in enumerate(sizes)]
     *packed, goal = pack_rows(train, ids, columns, bulk, extra, middle + final)
     firsts, seconds = [], []
     parts = [pieces] + [[shift(x, "groups", n_group, d) for x in pieces] for d in range(1, n_group)]
@@ -614,8 +627,8 @@
         far = swap(after(packed[-2], *pieces[1:]), "shard", n_shard, 2)
         urgent.append(far)
     sent_last = packed[len(middle):len(middle) + len(final)]
-    last = [shift(after(sent_last[0], *pieces[1:]), "shard", n_shard, last_hops)]
-    urgent.append(last[0])
+    last = [shift(after(x, *pieces[1:]), "shard", n_shard, last_hops) for x in sent_last[:fillers]]
+    urgent += last
     depth = n_rep * columns
     targets = [(feat + d) % n_feat for d in range(1, n_feat)]
     near_chip = fetch(matrices, targets[0], depth, *pieces[1:])
@@ -634,11 +647,11 @@
     for (hops, _, _), x in zip(middle[1:], packed[1:]):
         here.append(shift(after(x, *urgent, *sends), "shard", n_shard, hops))
         urgent = [here[-1]]
-    sent_last = [after(x, own) for x in sent_last[1:]]
-    last_all = [with_rep(after(last[0], own))]
+    sent_last = [after(x, own) for x in sent_last[fillers:]]
+    last_all = [with_rep(after(x, own)) for x in last]
 
     mine = own_rows(goal, train, bulk, own)
-    marks = [own, mine, *sent_last, *last_all[0][1:]]
+    marks = [own, mine, *sent_last, *[p for x in last_all for p in x[1:]]]
     if extra:
         for d in range(1, n_group):
             flag = jnp.maximum(flag, shift(flag, "groups", n_group, d))
@@ -667,7 +680,7 @@
     def over_feat(shares):
         return [shares[0]] + [shift(shares[d], "feat", n_feat, d) for d in range(1, n_feat)]
 
-    last_all += [with_rep(after(x, *early[1:])) for x in last[1:]]
+    last_all += [with_rep(after(x, *early[1:])) for x in last[fillers:]]
     late = late_scores(last_all, weight, n_feat)
     return merge(table, over_feat(early), over_feat(late), n_shard)[None]
 

time: 95.5 us -> 97.7 us (1.023)
  starting transfers between devices: 33.4 us -> 39.4 us
  waiting for transfers between devices: 22.3 us -> 18 us
    ppermute x36 -> x38, starting transfers between devices: 30 us -> 34.6 us  [shift(): return lax.ppermute(x, axis, [(i, (i + by) % size) for i in range(size)])]
    ppermute x36 -> x38, waiting for transfers between devices: 17.6 us -> 15.3 us  [shift(): return lax.ppermute(x, axis, [(i, (i + by) % size) for i in range(size)])]
    ppermute x2, waiting for transfers between devices: 4.69 us -> 2.77 us  [swap(): return lax.ppermute(x, axis, [(i, i ^ bit) for i in range(size)])]
    ppermute x2, starting transfers between devices: 3.35 us -> 4.76 us  [swap(): return lax.ppermute(x, axis, [(i, i ^ bit) for i in range(size)])]
    unnamed x36 -> x42, local copies, waits for them, and re-layouts: 4.53 us -> 4.25 us
  transfers between devices with their start and end apart: 38 -> 40, of which waited for: 13 -> 13; matrix products, arithmetic and copies ran while one was open for 1% -> 1% of each run, Pallas kernels for 33% -> 33%
where the time goes in v17:
time: 97.7 us; the launch traced here: 97.3 us
  starting transfers between devices  39.4 us (40%)
  Pallas kernels  33.7 us (34%)
  waiting for transfers between devices  18 us (18%)
  local copies, waits for them, and re-layouts  4.83 us (5%)
  between operations  1.16 us (1%)
    ppermute x38, starting transfers between devices, shift(): return lax.ppermute(x, axis, [(i, (i + by) % size) for i in range(size)])  34.6 us
    ppermute x38, waiting for transfers between devices, shift(): return lax.ppermute(x, axis, [(i, (i + by) % size) for i in range(size)])  15.3 us
    pallas_call x1, Pallas kernels, partial_weights(): pl.pallas_call(kernel, in_specs=[SMEM] + [HBM] * n + [VMEM] * (CUTS * n)...  6.6 us
    pallas_call x1, Pallas kernels, pack_rows(): pl.pallas_call(kernel, grid=(1,), in_specs=[pl.BlockSpec((lines, LANES),...  6.59 us
    pallas_call x1, Pallas kernels, early_scores(): pl.pallas_call(kernel, in_specs=[SMEM] + [VMEM] * (2 + n_other + n_rep *...  5.25 us
    ppermute x2, starting transfers between devices, swap(): return lax.ppermute(x, axis, [(i, i ^ bit) for i in range(size)])  4.76 us
    unnamed x42, local copies, waits for them, and re-layouts  4.25 us
    ppermute x2, waiting for transfers between devices, swap(): return lax.ppermute(x, axis, [(i, i ^ bit) for i in range(size)])  2.77 us
  transfers between devices with their start and end apart: 40, of which 13 were waited for; matrix products, arithmetic and copies ran while one was open for 1% of the time, Pallas kernels for 33%

profile of v17, /device:TPU:0, one launch (start us, length us, event | category | flops | bytes accessed | tf_op | source)
XLA Modules:
  0.0 97.3 jit_solution(3115378511641642635)
XLA Ops:
  0.5 2.7 %pick_queries.1 = (bf16[1,64,1024]{2,1,0:T(8,128)(2,1)}, bf16[1,64,1024]{2,1,0:T(8,128)(2,1)}, bf16[1,64,1024]{2,1,0:T(8,128)(2,1)}, bf16[1,64,1024]{2,1,0:T(8,128)(2,1)}) custom-call(s32[4,4]{1,0:T(4,128)} %pattern_ref.3, s32[16]{0:T(128)} %slot_ref.3, bf16[4,128,1024]{2,1,0:T(8,128)(2,1)} %in_ref.1), custom_call_target="tpu_custom_call" | custom-call | flops 1 | bytes 1 | tf_op jit(solution)/shard_map/pick_queries/pallas_call | solution.py:109
  3.1 2.8 %collective-permute-start.4 = (bf16[1,64,1024]{2,1,0:T(8,128)(2,1)}, bf16[1,64,1024]{2,1,0:T(8,128)(2,1)S(1)}, u32[]{:S(2)}, u32[]{:S(2)}) collective-permute-start(bf16[1,64,1024]{2,1,0:T(8,128)(2,1)} %get-tuple-element.50), channel_id=1, source_target_pairs={{0,4},{4,8},{8,12},{12,0},{1,5},{5,9},{9,13},{13,1},{2,6},{6,10},{... | collective-permute-start | bytes 393224 | tf_op jit(solution)/shard_map/ppermute | solution.py:23
  5.9 2.6 %collective-permute-start.5 = (bf16[1,64,1024]{2,1,0:T(8,128)(2,1)}, bf16[1,64,1024]{2,1,0:T(8,128)(2,1)S(1)}, u32[]{:S(2)}, u32[]{:S(2)}) collective-permute-start(bf16[1,64,1024]{2,1,0:T(8,128)(2,1)} %get-tuple-element.51), channel_id=1, source_target_pairs={{0,8},{4,12},{8,0},{12,4},{1,9},{5,13},{9,1},{13,5},{2,10},{6,14},... | collective-permute-start | bytes 393224 | tf_op jit(solution)/shard_map/ppermute | solution.py:23
  8.5 1.3 %collective-permute-start.6 = (bf16[1,64,1024]{2,1,0:T(8,128)(2,1)}, bf16[1,64,1024]{2,1,0:T(8,128)(2,1)S(1)}, u32[]{:S(2)}, u32[]{:S(2)}) collective-permute-start(bf16[1,64,1024]{2,1,0:T(8,128)(2,1)} %get-tuple-element.52), channel_id=1, source_target_pairs={{0,12},{4,0},{8,4},{12,8},{1,13},{5,1},{9,5},{13,9},{2,14},{6,2},{... | collective-permute-start | bytes 393224 | tf_op jit(solution)/shard_map/ppermute | solution.py:23
  9.9 1.5 %collective-permute-start.8 = (bf16[1,64,1024]{2,1,0:T(8,128)(2,1)}, bf16[1,64,1024]{2,1,0:T(8,128)(2,1)S(1)}, u32[]{:S(2)}, u32[]{:S(2)}) collective-permute-start(bf16[1,64,1024]{2,1,0:T(8,128)(2,1)} %get-tuple-element.54.refs_0_), channel_id=1, source_target_pairs={{0,16},{16,0},{1,17},{17,1},{2,18},{18,2},{3,19},{19,3},{4,20},{20... | collective-permute-start | bytes 393224 | tf_op jit(solution)/shard_map/ppermute | solution.py:23
  11.4 6.6 %pack_rows.1 = (bf16[256,1024]{1,0:T(8,128)(2,1)}, bf16[256,1024]{1,0:T(8,128)(2,1)}, bf16[64,1024]{1,0:T(8,128)(2,1)}, bf16[32,1024]{1,0:T(8,128)(2,1)}, bf16[6...) custom-call(s32[32,128]{1,0:T(8,128)} %bitcast.11, ...), custom_call_target="tpu_custom_call" | custom-call | flops 1 | bytes 1 | tf_op jit(solution)/shard_map/pack_rows/pallas_call | solution.py:253
  18.0 3.2 %collective-permute-start.21 = (bf16[256,1024]{1,0:T(8,128)(2,1)}, bf16[256,1024]{1,0:T(8,128)(2,1)S(1)}, u32[]{:S(2)}, u32[]{:S(2)}) collective-permute-start(bf16[256,1024]{1,0:T(8,128)(2,1)} %after.19), channel_id=1, source_target_pairs={{0,4},{4,8},{8,12},{12,0},{1,5},{5,9},{9,13},{13,1},{2,6},{6,10},{... | collective-permute-start | bytes 1572872 | tf_op jit(solution)/shard_map/ppermute | solution.py:23
  21.2 1.5 %collective-permute-start.9 = (bf16[1,64,1024]{2,1,0:T(8,128)(2,1)S(1)}, bf16[1,64,1024]{2,1,0:T(8,128)(2,1)S(1)}, u32[]{:S(2)}, u32[]{:S(2)}) collective-permute-start(bf16[1,64,1024]{2,1,0:T(8,128)(2,1)S(1)} %collective-permute-done.4.rest_0_.refs_2_.refs_1_), channel_id=1, source_target_pairs={{0,16},{16,0},{1,17},{17,1},{2,18},{18,2},{3,19},{19,3},{4,20},{20... | collective-permute-start | bytes 393224 | tf_op jit(solution)/shard_map/ppermute | solution.py:23
  22.7 0.5 collective-permute-start.10
  23.2 1.5 %collective-permute-start.11 = (bf16[1,64,1024]{2,1,0:T(8,128)(2,1)S(1)}, bf16[1,64,1024]{2,1,0:T(8,128)(2,1)S(1)}, u32[]{:S(2)}, u32[]{:S(2)}) collective-permute-start(bf16[1,64,1024]{2,1,0:T(8,128)(2,1)S(1)} %collective-permute-done.6.rest_2_.refs_4_.refs_3_), channel_id=1, source_target_pairs={{0,16},{16,0},{1,17},{17,1},{2,18},{18,2},{3,19},{19,3},{4,20},{20... | collective-permute-start | bytes 393224 | tf_op jit(solution)/shard_map/ppermute | solution.py:23
  24.7 1.6 %collective-permute-start.27 = (bf16[128,1024]{1,0:T(8,128)(2,1)}, bf16[128,1024]{1,0:T(8,128)(2,1)S(1)}, u32[]{:S(2)}, u32[]{:S(2)}) collective-permute-start(bf16[128,1024]{1,0:T(8,128)(2,1)} %after.28), channel_id=1, source_target_pairs={{0,8},{4,12},{8,0},{12,4},{1,9},{5,13},{9,1},{13,5},{2,10},{6,14},... | collective-permute-start | bytes 786440 | tf_op jit(solution)/shard_map/ppermute | solution.py:27
  26.4 0.8 row_table.1
  27.2 3.4 %copy-done = bf16[1,4096,1024]{2,1,0:T(8,128)(2,1)S(1)} copy-done((bf16[1,4096,1024]{2,1,0:T(8,128)(2,1)S(1)}, bf16[1,4096,1024]{2,1,0:T(8,128)(2,1)}, u32[]{:S(2)}) %copy-start) | copy-done | bytes 8388632
  30.6 2.5 %fetch.1 = (bf16[2048,1024]{1,0:T(8,128)(2,1)S(1)}, bf16[2048,1024]{1,0:T(8,128)(2,1)S(1)}) custom-call(s32[1]{0:T(128)} %bitcast.3.block_ref, bf16[4096,1024]{1,0:T(8,128)(2,1)S(1)} %bitcast.7, bf16[4096,1024]{1,0:T(8,128)(2,1)} %collective-permute-done.7.refs_1_, bf16[1,64,1024]{2,1,0:T(8,128)(2,1)S(1)} %collective-permute-done.4.rest_0_.refs_2_.refs_1_, ...), custom_call_target="tpu_custom_call" | custom-call | flops 1 | bytes 1 | tf_op jit(solution)/shard_map/fetch/pallas_call | solution.py:326
  33.2 1.2 %join_queries.1 = (bf16[128,256]{1,0:T(8,128)(2,1)S(1)}, bf16[128,256]{1,0:T(8,128)(2,1)S(1)}, bf16[128,256]{1,0:T(8,128)(2,1)S(1)}, bf16[128,256]{1,0:T(8,128)(...) custom-call(s32[4,4]{1,0:T(4,128)S(1)} %copy-done.15, ...), custom_call_target="tpu_custom_call" | custom-call | flops 1 | bytes 1 | tf_op jit(solution)/shard_map/join_queries/pallas_call | solution.py:154
  34.5 0.5 collective-permute-start.13
  35.1 0.7 collective-permute-done.12.refs_10_
  36.4 0.6 collective-permute-done.15.refs_13_
  37.5 0.7 collective-permute-start.22
  38.3 2.0 %collective-permute-start.24 = (bf16[32,1024]{1,0:T(8,128)(2,1)S(1)}, bf16[32,1024]{1,0:T(8,128)(2,1)S(1)}, u32[]{:S(2)}, u32[]{:S(2)}) collective-permute-start(bf16[32,1024]{1,0:T(8,128)(2,1)S(1)} %after.25), channel_id=1, source_target_pairs={{0,12},{4,0},{8,4},{12,8},{1,13},{5,1},{9,5},{13,9},{2,14},{6,2},{... | collective-permute-start | bytes 196616 | tf_op jit(solution)/shard_map/ppermute | solution.py:23
  40.3 2.3 %fetched_weights.1.refs_18_.refs_2_.refs_5_ = bf16[2048,256]{1,0:T(8,128)(2,1)S(1)} custom-call(bf16[2048,1024]{1,0:T(8,128)(2,1)S(1)} %get-tuple-element.55.refs_8_.refs_0_, bf16[2048,1024]{1,0:T(8,128)(2,1)S(1)} %get-tuple-element.56.refs_9_.refs_1_, bf16[128,256]{1,0:T(8,128)(2,1)S(1)} %get-tuple-element.58.refs_2_, ...), custom_call_target="tpu_custom_call" | custom-call | flops 1 | bytes 1 | tf_op jit(solution)/shard_map/fetched_weights/pallas_call | solution.py:353
  42.7 1.6 %collective-permute-start.20 = (bf16[2048,256]{1,0:T(8,128)(2,1)S(1)}, bf16[2048,256]{1,0:T(8,128)(2,1)}, u32[]{:S(2)}, u32[]{:S(2)}) collective-permute-start(bf16[2048,256]{1,0:T(8,128)(2,1)S(1)} %fetched_weights.1.refs_18_.refs_2_.refs_5_), channel_id=1, source_target_pairs={{0,2},{2,0},{1,3},{3,1},{4,6},{6,4},{5,7},{7,5},{8,10},{10,8},{9,1... | collective-permute-start | bytes 3145736 | tf_op jit(solution)/shard_map/ppermute | solution.py:23
  44.2 1.2 %collective-permute-done.27.refs_1_.refs_0_.refs_2_ = bf16[128,1024]{1,0:T(8,128)(2,1)S(1)} collective-permute-done((bf16[128,1024]{1,0:T(8,128)(2,1)}, bf16[128,1024]{1,0:T(8,128)(2,1)S(1)}, u32[]{:S(2)}, u32[]{:S(2)}) %collective-permute-start.27) | collective-permute-done | bytes 262176 | tf_op jit(solution)/shard_map/ppermute | solution.py:27
  45.5 0.8 stack.3
  46.3 3.1 %collective-permute-start.28 = (bf16[256,1024]{1,0:T(8,128)(2,1)}, bf16[256,1024]{1,0:T(8,128)(2,1)}, u32[]{:S(2)}, u32[]{:S(2)}) collective-permute-start(bf16[256,1024]{1,0:T(8,128)(2,1)} %stack.3), channel_id=1, source_target_pairs={{0,4},{4,0},{8,12},{12,8},{1,5},{5,1},{9,13},{13,9},{2,6},{6,2},{1... | collective-permute-start | bytes 1572872 | tf_op jit(solution)/shard_map/ppermute | solution.py:27
  49.6 3.2 %collective-permute-start.33 = (bf16[256,1024]{1,0:T(8,128)(2,1)}, bf16[256,1024]{1,0:T(8,128)(2,1)}, u32[]{:S(2)}, u32[]{:S(2)}) collective-permute-start(bf16[256,1024]{1,0:T(8,128)(2,1)} %after.32), channel_id=1, source_target_pairs={{0,8},{4,12},{8,0},{12,4},{1,9},{5,13},{9,1},{13,5},{2,10},{6,14},... | collective-permute-start | bytes 1572872 | tf_op jit(solution)/shard_map/ppermute | solution.py:23
  52.8 1.5 %collective-permute-start.26 = (s32[8,128]{1,0:T(8,128)S(1)}, s32[8,128]{1,0:T(8,128)S(1)}, u32[]{:S(2)}, u32[]{:S(2)}) collective-permute-start(s32[8,128]{1,0:T(8,128)S(1)} %get-tuple-element.57.refs_10_), channel_id=1, source_target_pairs={{0,16},{16,0},{1,17},{17,1},{2,18},{18,2},{3,19},{19,3},{4,20},{20... | collective-permute-start | bytes 12296 | tf_op jit(solution)/shard_map/ppermute | solution.py:23
  54.3 2.1 %collective-permute-done.26 = s32[8,128]{1,0:T(8,128)S(1)} collective-permute-done((s32[8,128]{1,0:T(8,128)S(1)}, s32[8,128]{1,0:T(8,128)S(1)}, u32[]{:S(2)}, u32[]{:S(2)}) %collective-permute-start.26) | collective-permute-done | bytes 4128 | tf_op jit(solution)/shard_map/ppermute | solution.py:23
  56.4 0.6 slice.3
  57.7 6.6 %partial_weights.1.rest_0_.refs_1_.refs_2_.refs_0_ = f32[2048,256]{1,0:T(8,128)S(1)} custom-call(s32[1]{0:T(128)} %bitcast.1.block_ref, bf16[4096,1024]{1,0:T(8,128)(2,1)S(1)} %bitcast.10, bf16[4096,1024]{1,0:T(8,128)(2,1)} %collective-permute-done.7.refs_1_, bf16[128,256]{1,0:T(8,128)(2,1)S(1)} %get-tuple-element.58.refs_2_, ...), custom_call_target="tpu_custom_call" | custom-call | flops 1 | bytes 1 | tf_op jit(solution)/shard_map/partial_weights/pallas_call | solution.py:293
  65.2 1.2 %collective-permute-done.29.refs_0_ = bf16[128,1024]{1,0:T(8,128)(2,1)S(1)} collective-permute-done((bf16[128,1024]{1,0:T(8,128)(2,1)}, bf16[128,1024]{1,0:T(8,128)(2,1)S(1)}, u32[]{:S(2)}, u32[]{:S(2)}) %collective-permute-start.29) | collective-permute-done | bytes 262176 | tf_op jit(solution)/shard_map/ppermute | solution.py:23
  67.0 2.4 %own_rows.1.refs_2_ = bf16[256,2048]{1,0:T(8,128)(2,1)S(1)} custom-call(s32[8,128]{1,0:T(8,128)S(1)} %copy-done.16, bf16[1024,2048]{1,0:T(8,128)(2,1)S(1)} %copy-done.1, f32[2048,256]{1,0:T(8,128)S(1)} %partial_weights.1.rest_0_.refs_1_.refs_2_.refs_0_), custom_call_target="tpu_custom_call" | custom-call | flops 1 | bytes 1 | tf_op jit(solution)/shard_map/own_rows/pallas_call | solution.py:195
  69.4 0.8 copy-done.10
  70.3 1.5 %collective-permute-done.28.refs_9_.refs_0_ = bf16[256,1024]{1,0:T(8,128)(2,1)} collective-permute-done((bf16[256,1024]{1,0:T(8,128)(2,1)}, bf16[256,1024]{1,0:T(8,128)(2,1)}, u32[]{:S(2)}, u32[]{:S(2)}) %collective-permute-start.28) | collective-permute-done | bytes 524320 | tf_op jit(solution)/shard_map/ppermute | solution.py:27
  71.8 0.5 collective-permute-start.35
  72.3 0.7 collective-permute-done.31.refs_1_
  73.1 3.0 %collective-permute-done.33.refs_0_ = bf16[256,1024]{1,0:T(8,128)(2,1)} collective-permute-done((bf16[256,1024]{1,0:T(8,128)(2,1)}, bf16[256,1024]{1,0:T(8,128)(2,1)}, u32[]{:S(2)}, u32[]{:S(2)}) %collective-permute-start.33) | collective-permute-done | bytes 524320 | tf_op jit(solution)/shard_map/ppermute | solution.py:23
  76.1 2.0 %collective-permute-start.37 = (bf16[64,1024]{1,0:T(8,128)(2,1)S(1)}, bf16[64,1024]{1,0:T(8,128)(2,1)S(1)}, u32[]{:S(2)}, u32[]{:S(2)}) collective-permute-start(bf16[64,1024]{1,0:T(8,128)(2,1)S(1)} %after.20.refs_3_), channel_id=1, source_target_pairs={{0,12},{4,0},{8,4},{12,8},{1,13},{5,1},{9,5},{13,9},{2,14},{6,2},{... | collective-permute-start | bytes 393224 | tf_op jit(solution)/shard_map/ppermute | solution.py:23
  78.2 5.2 %early_scores.1 = (bf16[2048,512]{1,0:T(8,128)(2,1)S(1)}, f32[1024,128]{1,0:T(8,128)S(1)}, bf16[1024,128]{1,0:T(8,128)(2,1)S(1)}) custom-call(s32[4,4]{1,0:T(4,128)S(1)} %get-tuple-element.53.table_ref, f32[2048,256]{1,0:T(8,128)S(1)} %partial_weights.1.rest_0_.refs_1_.refs_2_.refs_0_, bf16[2048,256]{1,0:T(8,128)(2,1)} %collective-permute-done.20.refs_1_, ...), custom_call_target="tpu_custom_call" | custom-call | flops 1 | bytes 1 | tf_op jit(solution)/shard_map/early_scores/pallas_call | solution.py:523
  83.5 1.6 %collective-permute-start.36 = (bf16[1024,128]{1,0:T(8,128)(2,1)S(1)}, bf16[1024,128]{1,0:T(8,128)(2,1)S(1)}, u32[]{:S(2)}, u32[]{:S(2)}) collective-permute-start(bf16[1024,128]{1,0:T(8,128)(2,1)S(1)} %get-tuple-element.90.refs_1_), channel_id=1, source_target_pairs={{0,2},{2,0},{1,3},{3,1},{4,6},{6,4},{5,7},{7,5},{8,10},{10,8},{9,1... | collective-permute-start | bytes 786440 | tf_op jit(solution)/shard_map/ppermute | solution.py:23
  85.0 2.0 %collective-permute-start.41 = (bf16[32,1024]{1,0:T(8,128)(2,1)S(1)}, bf16[32,1024]{1,0:T(8,128)(2,1)S(1)}, u32[]{:S(2)}, u32[]{:S(2)}) collective-permute-start(bf16[32,1024]{1,0:T(8,128)(2,1)S(1)} %after.22.refs_5_), channel_id=1, source_target_pairs={{0,12},{4,0},{8,4},{12,8},{1,13},{5,1},{9,5},{13,9},{2,14},{6,2},{... | collective-permute-start | bytes 196616 | tf_op jit(solution)/shard_map/ppermute | solution.py:23
  87.0 0.5 collective-permute-start.40
  87.5 1.8 %collective-permute-done.41.refs_0_ = bf16[32,1024]{1,0:T(8,128)(2,1)S(1)} collective-permute-done((bf16[32,1024]{1,0:T(8,128)(2,1)S(1)}, bf16[32,1024]{1,0:T(8,128)(2,1)S(1)}, u32[]{:S(2)}, u32[]{:S(2)}) %collective-permute-start.41) | collective-permute-done | bytes 65568 | tf_op jit(solution)/shard_map/ppermute | solution.py:23
  89.3 1.3 %collective-permute-done.42.refs_9_ = bf16[32,1024]{1,0:T(8,128)(2,1)S(1)} collective-permute-done((bf16[32,1024]{1,0:T(8,128)(2,1)S(1)}, bf16[32,1024]{1,0:T(8,128)(2,1)S(1)}, u32[]{:S(2)}, u32[]{:S(2)}) %collective-permute-start.42) | collective-permute-done | bytes 65568 | tf_op jit(solution)/shard_map/ppermute | solution.py:23
  90.6 0.7 late_scores.1
  91.3 0.6 collective-permute-start.43
  91.9 3.7 %collective-permute-done.43.refs_3_ = bf16[256,128]{1,0:T(8,128)(2,1)S(1)} collective-permute-done((bf16[256,128]{1,0:T(8,128)(2,1)S(1)}, bf16[256,128]{1,0:T(8,128)(2,1)S(1)}, u32[]{:S(2)}, u32[]{:S(2)}) %collective-permute-start.43) | collective-permute-done | bytes 65568 | tf_op jit(solution)/shard_map/ppermute | solution.py:23
  95.7 1.7 %merge.1 = f32[128,1024]{1,0:T(8,128)} custom-call(s32[4,4]{1,0:T(4,128)S(1)} %get-tuple-element.53.table_ref, f32[1024,128]{1,0:T(8,128)S(1)} %get-tuple-element.89.refs_0_, bf16[1024,128]{1,0:T(8,128)(2,1)S(1)} %collective-permute-done.36.refs_1_, f32[256,128]{1,0:T(8,128)S(1)} %get-tuple-element.92.refs_2_, ...), custom_call_target="tpu_custom_call" | custom-call | flops 1 | bytes 1 | tf_op jit(solution)/shard_map/merge/pallas_call | solution.py:583
  (113 shorter events, 3.8 us)
Async XLA Ops:
  0.0 26.4 %copy-start.13 = (s32[4096]{0:T(1024)S(1)}, s32[4096]{0:T(1024)}, u32[]{:S(2)}) copy-start(s32[4096]{0:T(1024)} %param.9) | copy-start | bytes 49156
  0.0 24.7 %collective-permute-start.7 = (bf16[4096,1024]{1,0:T(8,128)(2,1)}, bf16[4096,1024]{1,0:T(8,128)(2,1)}, u32[]{:S(2)}, u32[]{:S(2)}) collective-permute-start(bf16[4096,1024]{1,0:T(8,128)(2,1)} %bitcast.6), channel_id=1, source_target_pairs={{0,1},{1,0},{2,3},{3,2},{4,5},{5,4},{6,7},{7,6},{8,9},{9,8},{10,11... | collective-permute-start | bytes 25165832 | tf_op jit(solution)/shard_map/ppermute | solution.py:23
  3.1 14.8 %collective-permute-start.4 = (bf16[1,64,1024]{2,1,0:T(8,128)(2,1)}, bf16[1,64,1024]{2,1,0:T(8,128)(2,1)S(1)}, u32[]{:S(2)}, u32[]{:S(2)}) collective-permute-start(bf16[1,64,1024]{2,1,0:T(8,128)(2,1)} %get-tuple-element.50), channel_id=1, source_target_pairs={{0,4},{4,8},{8,12},{12,0},{1,5},{5,9},{9,13},{13,1},{2,6},{6,10},{... | collective-permute-start | bytes 393224 | tf_op jit(solution)/shard_map/ppermute | solution.py:23
  5.9 12.1 %collective-permute-start.5 = (bf16[1,64,1024]{2,1,0:T(8,128)(2,1)}, bf16[1,64,1024]{2,1,0:T(8,128)(2,1)S(1)}, u32[]{:S(2)}, u32[]{:S(2)}) collective-permute-start(bf16[1,64,1024]{2,1,0:T(8,128)(2,1)} %get-tuple-element.51), channel_id=1, source_target_pairs={{0,8},{4,12},{8,0},{12,4},{1,9},{5,13},{9,1},{13,5},{2,10},{6,14},... | collective-permute-start | bytes 393224 | tf_op jit(solution)/shard_map/ppermute | solution.py:23
  8.5 9.5 %collective-permute-start.6 = (bf16[1,64,1024]{2,1,0:T(8,128)(2,1)}, bf16[1,64,1024]{2,1,0:T(8,128)(2,1)S(1)}, u32[]{:S(2)}, u32[]{:S(2)}) collective-permute-start(bf16[1,64,1024]{2,1,0:T(8,128)(2,1)} %get-tuple-element.52), channel_id=1, source_target_pairs={{0,12},{4,0},{8,4},{12,8},{1,13},{5,1},{9,5},{13,9},{2,14},{6,2},{... | collective-permute-start | bytes 393224 | tf_op jit(solution)/shard_map/ppermute | solution.py:23
  9.9 13.3 %collective-permute-start.8 = (bf16[1,64,1024]{2,1,0:T(8,128)(2,1)}, bf16[1,64,1024]{2,1,0:T(8,128)(2,1)S(1)}, u32[]{:S(2)}, u32[]{:S(2)}) collective-permute-start(bf16[1,64,1024]{2,1,0:T(8,128)(2,1)} %get-tuple-element.54.refs_0_), channel_id=1, source_target_pairs={{0,16},{16,0},{1,17},{17,1},{2,18},{18,2},{3,19},{19,3},{4,20},{20... | collective-permute-start | bytes 393224 | tf_op jit(solution)/shard_map/ppermute | solution.py:23
  18.0 31.5 %collective-permute-start.21 = (bf16[256,1024]{1,0:T(8,128)(2,1)}, bf16[256,1024]{1,0:T(8,128)(2,1)S(1)}, u32[]{:S(2)}, u32[]{:S(2)}) collective-permute-start(bf16[256,1024]{1,0:T(8,128)(2,1)} %after.19), channel_id=1, source_target_pairs={{0,4},{4,8},{8,12},{12,0},{1,5},{5,9},{9,13},{13,1},{2,6},{6,10},{... | collective-permute-start | bytes 1572872 | tf_op jit(solution)/shard_map/ppermute | solution.py:23
  21.2 12.0 %collective-permute-start.9 = (bf16[1,64,1024]{2,1,0:T(8,128)(2,1)S(1)}, bf16[1,64,1024]{2,1,0:T(8,128)(2,1)S(1)}, u32[]{:S(2)}, u32[]{:S(2)}) collective-permute-start(bf16[1,64,1024]{2,1,0:T(8,128)(2,1)S(1)} %collective-permute-done.4.rest_0_.refs_2_.refs_1_), channel_id=1, source_target_pairs={{0,16},{16,0},{1,17},{17,1},{2,18},{18,2},{3,19},{19,3},{4,20},{20... | collective-permute-start | bytes 393224 | tf_op jit(solution)/shard_map/ppermute | solution.py:23
  22.7 10.4 %collective-permute-start.10 = (bf16[1,64,1024]{2,1,0:T(8,128)(2,1)S(1)}, bf16[1,64,1024]{2,1,0:T(8,128)(2,1)S(1)}, u32[]{:S(2)}, u32[]{:S(2)}) collective-permute-start(bf16[1,64,1024]{2,1,0:T(8,128)(2,1)S(1)} %collective-permute-done.5.rest_1_.refs_3_.refs_2_), channel_id=1, source_target_pairs={{0,16},{16,0},{1,17},{17,1},{2,18},{18,2},{3,19},{19,3},{4,20},{20... | collective-permute-start | bytes 393224 | tf_op jit(solution)/shard_map/ppermute | solution.py:23
  23.2 9.9 %collective-permute-start.11 = (bf16[1,64,1024]{2,1,0:T(8,128)(2,1)S(1)}, bf16[1,64,1024]{2,1,0:T(8,128)(2,1)S(1)}, u32[]{:S(2)}, u32[]{:S(2)}) collective-permute-start(bf16[1,64,1024]{2,1,0:T(8,128)(2,1)S(1)} %collective-permute-done.6.rest_2_.refs_4_.refs_3_), channel_id=1, source_target_pairs={{0,16},{16,0},{1,17},{17,1},{2,18},{18,2},{3,19},{19,3},{4,20},{20... | collective-permute-start | bytes 393224 | tf_op jit(solution)/shard_map/ppermute | solution.py:23
  24.7 20.7 %collective-permute-start.27 = (bf16[128,1024]{1,0:T(8,128)(2,1)}, bf16[128,1024]{1,0:T(8,128)(2,1)S(1)}, u32[]{:S(2)}, u32[]{:S(2)}) collective-permute-start(bf16[128,1024]{1,0:T(8,128)(2,1)} %after.28), channel_id=1, source_target_pairs={{0,8},{4,12},{8,0},{12,4},{1,9},{5,13},{9,1},{13,5},{2,10},{6,14},... | collective-permute-start | bytes 786440 | tf_op jit(solution)/shard_map/ppermute | solution.py:27
  33.2 5.1 %copy-start.14 = (bf16[32,1024]{1,0:T(8,128)(2,1)S(1)}, bf16[32,1024]{1,0:T(8,128)(2,1)}, u32[]{:S(2)}) copy-start(bf16[32,1024]{1,0:T(8,128)(2,1)} %get-tuple-element.80.refs_0_) | copy-start | bytes 196612
  34.4 1.3 %collective-permute-start.12 = (bf16[128,256]{1,0:T(8,128)(2,1)S(1)}, bf16[128,256]{1,0:T(8,128)(2,1)S(1)}, u32[]{:S(2)}, u32[]{:S(2)}) collective-permute-start(bf16[128,256]{1,0:T(8,128)(2,1)S(1)} %get-tuple-element.66), channel_id=1, source_target_pairs={{0,1},{1,0},{2,3},{3,2},{4,5},{5,4},{6,7},{7,6},{8,9},{9,8},{10,11... | collective-permute-start | bytes 196616 | tf_op jit(solution)/shard_map/ppermute | solution.py:23
  34.5 1.4 %collective-permute-start.13 = (bf16[128,256]{1,0:T(8,128)(2,1)S(1)}, bf16[128,256]{1,0:T(8,128)(2,1)S(1)}, u32[]{:S(2)}, u32[]{:S(2)}) collective-permute-start(bf16[128,256]{1,0:T(8,128)(2,1)S(1)} %get-tuple-element.67), channel_id=1, source_target_pairs={{0,1},{1,0},{2,3},{3,2},{4,5},{5,4},{6,7},{7,6},{8,9},{9,8},{10,11... | collective-permute-start | bytes 196616 | tf_op jit(solution)/shard_map/ppermute | solution.py:23
  35.0 1.3 %collective-permute-start.14 = (bf16[128,256]{1,0:T(8,128)(2,1)S(1)}, bf16[128,256]{1,0:T(8,128)(2,1)S(1)}, u32[]{:S(2)}, u32[]{:S(2)}) collective-permute-start(bf16[128,256]{1,0:T(8,128)(2,1)S(1)} %get-tuple-element.68), channel_id=1, source_target_pairs={{0,1},{1,0},{2,3},{3,2},{4,5},{5,4},{6,7},{7,6},{8,9},{9,8},{10,11... | collective-permute-start | bytes 196616 | tf_op jit(solution)/shard_map/ppermute | solution.py:23
  35.8 1.3 %collective-permute-start.15 = (bf16[128,256]{1,0:T(8,128)(2,1)S(1)}, bf16[128,256]{1,0:T(8,128)(2,1)S(1)}, u32[]{:S(2)}, u32[]{:S(2)}) collective-permute-start(bf16[128,256]{1,0:T(8,128)(2,1)S(1)} %get-tuple-element.69), channel_id=1, source_target_pairs={{0,1},{1,0},{2,3},{3,2},{4,5},{5,4},{6,7},{7,6},{8,9},{9,8},{10,11... | collective-permute-start | bytes 196616 | tf_op jit(solution)/shard_map/ppermute | solution.py:23
  35.9 1.3 %collective-permute-start.16 = (bf16[128,256]{1,0:T(8,128)(2,1)S(1)}, bf16[128,256]{1,0:T(8,128)(2,1)S(1)}, u32[]{:S(2)}, u32[]{:S(2)}) collective-permute-start(bf16[128,256]{1,0:T(8,128)(2,1)S(1)} %get-tuple-element.70), channel_id=1, source_target_pairs={{0,1},{1,0},{2,3},{3,2},{4,5},{5,4},{6,7},{7,6},{8,9},{9,8},{10,11... | collective-permute-start | bytes 196616 | tf_op jit(solution)/shard_map/ppermute | solution.py:23
  36.3 1.3 %collective-permute-start.17 = (bf16[128,256]{1,0:T(8,128)(2,1)S(1)}, bf16[128,256]{1,0:T(8,128)(2,1)S(1)}, u32[]{:S(2)}, u32[]{:S(2)}) collective-permute-start(bf16[128,256]{1,0:T(8,128)(2,1)S(1)} %get-tuple-element.71), channel_id=1, source_target_pairs={{0,1},{1,0},{2,3},{3,2},{4,5},{5,4},{6,7},{7,6},{8,9},{9,8},{10,11... | collective-permute-start | bytes 196616 | tf_op jit(solution)/shard_map/ppermute | solution.py:23
  37.0 1.3 %collective-permute-start.18 = (bf16[128,256]{1,0:T(8,128)(2,1)S(1)}, bf16[128,256]{1,0:T(8,128)(2,1)S(1)}, u32[]{:S(2)}, u32[]{:S(2)}) collective-permute-start(bf16[128,256]{1,0:T(8,128)(2,1)S(1)} %get-tuple-element.72), channel_id=1, source_target_pairs={{0,1},{1,0},{2,3},{3,2},{4,5},{5,4},{6,7},{7,6},{8,9},{9,8},{10,11... | collective-permute-start | bytes 196616 | tf_op jit(solution)/shard_map/ppermute | solution.py:23
  37.2 3.1 %collective-permute-start.19 = (bf16[128,256]{1,0:T(8,128)(2,1)S(1)}, bf16[128,256]{1,0:T(8,128)(2,1)S(1)}, u32[]{:S(2)}, u32[]{:S(2)}) collective-permute-start(bf16[128,256]{1,0:T(8,128)(2,1)S(1)} %get-tuple-element.73), channel_id=1, source_target_pairs={{0,1},{1,0},{2,3},{3,2},{4,5},{5,4},{6,7},{7,6},{8,9},{9,8},{10,11... | collective-permute-start | bytes 196616 | tf_op jit(solution)/shard_map/ppermute | solution.py:23
  37.5 12.0 %collective-permute-start.22 = (bf16[64,1024]{1,0:T(8,128)(2,1)S(1)}, bf16[64,1024]{1,0:T(8,128)(2,1)S(1)}, u32[]{:S(2)}, u32[]{:S(2)}) collective-permute-start(bf16[64,1024]{1,0:T(8,128)(2,1)S(1)} %after.23), channel_id=1, source_target_pairs={{0,12},{4,0},{8,4},{12,8},{1,13},{5,1},{9,5},{13,9},{2,14},{6,2},{... | collective-permute-start | bytes 393224 | tf_op jit(solution)/shard_map/ppermute | solution.py:23
  38.3 11.3 %collective-permute-start.24 = (bf16[32,1024]{1,0:T(8,128)(2,1)S(1)}, bf16[32,1024]{1,0:T(8,128)(2,1)S(1)}, u32[]{:S(2)}, u32[]{:S(2)}) collective-permute-start(bf16[32,1024]{1,0:T(8,128)(2,1)S(1)} %after.25), channel_id=1, source_target_pairs={{0,12},{4,0},{8,4},{12,8},{1,13},{5,1},{9,5},{13,9},{2,14},{6,2},{... | collective-permute-start | bytes 196616 | tf_op jit(solution)/shard_map/ppermute | solution.py:23
  40.3 17.4 %slice-start = ((s8[8388608]{0:T(1024)(128)(4,1)}), s8[4194304]{0:T(1024)(128)(4,1)S(1)}, s32[]{:S(2)}) async-start(s8[8388608]{0:T(1024)(128)(4,1)} %bitcast.8), calls=%async_computation | async-start | bytes 8388608
  40.3 5.2 %copy-start.4 = (bf16[128,1024]{1,0:T(8,128)(2,1)S(1)}, bf16[128,1024]{1,0:T(8,128)(2,1)}, u32[]{:S(2)}) copy-start(bf16[128,1024]{1,0:T(8,128)(2,1)} %get-tuple-element.83.refs_0_) | copy-start | bytes 786436
  40.3 17.4 %slice-start.1 = ((s8[8388608]{0:T(1024)(128)(4,1)}), s8[4194304]{0:T(1024)(128)(4,1)S(1)}, s32[]{:S(2)}) async-start(s8[8388608]{0:T(1024)(128)(4,1)} %bitcast.8), calls=%async_computation.1 | async-start | bytes 8388608
  42.7 35.4 %collective-permute-start.20 = (bf16[2048,256]{1,0:T(8,128)(2,1)S(1)}, bf16[2048,256]{1,0:T(8,128)(2,1)}, u32[]{:S(2)}, u32[]{:S(2)}) collective-permute-start(bf16[2048,256]{1,0:T(8,128)(2,1)S(1)} %fetched_weights.1.refs_18_.refs_2_.refs_5_), channel_id=1, source_target_pairs={{0,2},{2,0},{1,3},{3,1},{4,6},{6,4},{5,7},{7,5},{8,10},{10,8},{9,1... | collective-permute-start | bytes 3145736 | tf_op jit(solution)/shard_map/ppermute | solution.py:23
  46.3 25.5 %collective-permute-start.28 = (bf16[256,1024]{1,0:T(8,128)(2,1)}, bf16[256,1024]{1,0:T(8,128)(2,1)}, u32[]{:S(2)}, u32[]{:S(2)}) collective-permute-start(bf16[256,1024]{1,0:T(8,128)(2,1)} %stack.3), channel_id=1, source_target_pairs={{0,4},{4,0},{8,12},{12,8},{1,5},{5,1},{9,13},{13,9},{2,6},{6,2},{1... | collective-permute-start | bytes 1572872 | tf_op jit(solution)/shard_map/ppermute | solution.py:27
  49.5 14.8 %copy-start.6 = (bf16[32,1024]{1,0:T(8,128)(2,1)}, bf16[32,1024]{1,0:T(8,128)(2,1)S(1)}, u32[]{:S(2)}) copy-start(bf16[32,1024]{1,0:T(8,128)(2,1)S(1)} %collective-permute-done.24.refs_0_.refs_4_) | copy-start | bytes 196612
  49.5 8.1 %copy-start.2 = (bf16[256,1024]{1,0:T(8,128)(2,1)}, bf16[256,1024]{1,0:T(8,128)(2,1)S(1)}, u32[]{:S(2)}) copy-start(bf16[256,1024]{1,0:T(8,128)(2,1)S(1)} %collective-permute-done.21.refs_0_.refs_1_) | copy-start | bytes 1572868
  49.6 26.5 %collective-permute-start.33 = (bf16[256,1024]{1,0:T(8,128)(2,1)}, bf16[256,1024]{1,0:T(8,128)(2,1)}, u32[]{:S(2)}, u32[]{:S(2)}) collective-permute-start(bf16[256,1024]{1,0:T(8,128)(2,1)} %after.32), channel_id=1, source_target_pairs={{0,8},{4,12},{8,0},{12,4},{1,9},{5,13},{9,1},{13,5},{2,10},{6,14},... | collective-permute-start | bytes 1572872 | tf_op jit(solution)/shard_map/ppermute | solution.py:23
  52.8 3.6 %collective-permute-start.26 = (s32[8,128]{1,0:T(8,128)S(1)}, s32[8,128]{1,0:T(8,128)S(1)}, u32[]{:S(2)}, u32[]{:S(2)}) collective-permute-start(s32[8,128]{1,0:T(8,128)S(1)} %get-tuple-element.57.refs_10_), channel_id=1, source_target_pairs={{0,16},{16,0},{1,17},{17,1},{2,18},{18,2},{3,19},{19,3},{4,20},{20... | collective-permute-start | bytes 12296 | tf_op jit(solution)/shard_map/ppermute | solution.py:23
  57.7 6.6 %copy-start.18 = (bf16[128,1024]{1,0:T(8,128)(2,1)S(1)}, bf16[128,1024]{1,0:T(8,128)(2,1)}, u32[]{:S(2)}) copy-start(bf16[128,1024]{1,0:T(8,128)(2,1)} %get-tuple-element.81.refs_0_) | copy-start | bytes 786436
  64.6 1.8 %collective-permute-start.29 = (bf16[128,1024]{1,0:T(8,128)(2,1)}, bf16[128,1024]{1,0:T(8,128)(2,1)S(1)}, u32[]{:S(2)}, u32[]{:S(2)}) collective-permute-start(bf16[128,1024]{1,0:T(8,128)(2,1)} %get-tuple-element.83.refs_0_), channel_id=1, source_target_pairs={{0,1},{1,0},{2,3},{3,2},{4,5},{5,4},{6,7},{7,6},{8,9},{9,8},{10,11... | collective-permute-start | bytes 786440 | tf_op jit(solution)/shard_map/ppermute | solution.py:23
  64.7 1.9 %collective-permute-start.30 = (bf16[128,1024]{1,0:T(8,128)(2,1)S(1)}, bf16[128,1024]{1,0:T(8,128)(2,1)S(1)}, u32[]{:S(2)}, u32[]{:S(2)}) collective-permute-start(bf16[128,1024]{1,0:T(8,128)(2,1)S(1)} %after.29.refs_1_), channel_id=1, source_target_pairs={{0,1},{1,0},{2,3},{3,2},{4,5},{5,4},{6,7},{7,6},{8,9},{9,8},{10,11... | collective-permute-start | bytes 786440 | tf_op jit(solution)/shard_map/ppermute | solution.py:23
  66.4 3.9 %collective-permute-start.23 = (bf16[64,1024]{1,0:T(8,128)(2,1)S(1)}, bf16[64,1024]{1,0:T(8,128)(2,1)S(1)}, u32[]{:S(2)}, u32[]{:S(2)}) collective-permute-start(bf16[64,1024]{1,0:T(8,128)(2,1)S(1)} %after.24.refs_0_), channel_id=1, source_target_pairs={{0,1},{1,0},{2,3},{3,2},{4,5},{5,4},{6,7},{7,6},{8,9},{9,8},{10,11... | collective-permute-start | bytes 393224 | tf_op jit(solution)/shard_map/ppermute | solution.py:23
  66.6 3.7 %collective-permute-start.25 = (bf16[32,1024]{1,0:T(8,128)(2,1)S(1)}, bf16[32,1024]{1,0:T(8,128)(2,1)S(1)}, u32[]{:S(2)}, u32[]{:S(2)}) collective-permute-start(bf16[32,1024]{1,0:T(8,128)(2,1)S(1)} %after.26.refs_2_), channel_id=1, source_target_pairs={{0,1},{1,0},{2,3},{3,2},{4,5},{5,4},{6,7},{7,6},{8,9},{9,8},{10,11... | collective-permute-start | bytes 196616 | tf_op jit(solution)/shard_map/ppermute | solution.py:23
  71.8 1.2 %collective-permute-start.31 = (s32[8,128]{1,0:T(8,128)S(1)}, s32[8,128]{1,0:T(8,128)S(1)}, u32[]{:S(2)}, u32[]{:S(2)}) collective-permute-start(s32[8,128]{1,0:T(8,128)S(1)} %after.30), channel_id=1, source_target_pairs={{0,1},{1,0},{2,3},{3,2},{4,5},{5,4},{6,7},{7,6},{8,9},{9,8},{10,11... | collective-permute-start | bytes 12296 | tf_op jit(solution)/shard_map/ppermute | solution.py:23
  71.8 6.3 %collective-permute-start.35 = (bf16[256,1024]{1,0:T(8,128)(2,1)}, bf16[256,1024]{1,0:T(8,128)(2,1)S(1)}, u32[]{:S(2)}, u32[]{:S(2)}) collective-permute-start(bf16[256,1024]{1,0:T(8,128)(2,1)} %after.34.refs_9_), channel_id=1, source_target_pairs={{0,1},{1,0},{2,3},{3,2},{4,5},{5,4},{6,7},{7,6},{8,9},{9,8},{10,11... | collective-permute-start | bytes 1572872 | tf_op jit(solution)/shard_map/ppermute | solution.py:23
  73.0 5.2 %collective-permute-start.32 = (bf16[256,1024]{1,0:T(8,128)(2,1)S(1)}, bf16[256,1024]{1,0:T(8,128)(2,1)S(1)}, u32[]{:S(2)}, u32[]{:S(2)}) collective-permute-start(bf16[256,1024]{1,0:T(8,128)(2,1)S(1)} %after.31.refs_3_), channel_id=1, source_target_pairs={{0,1},{1,0},{2,3},{3,2},{4,5},{5,4},{6,7},{7,6},{8,9},{9,8},{10,11... | collective-permute-start | bytes 1572872 | tf_op jit(solution)/shard_map/ppermute | solution.py:23
  76.1 2.1 %collective-permute-start.34 = (bf16[256,1024]{1,0:T(8,128)(2,1)}, bf16[256,1024]{1,0:T(8,128)(2,1)S(1)}, u32[]{:S(2)}, u32[]{:S(2)}) collective-permute-start(bf16[256,1024]{1,0:T(8,128)(2,1)} %after.33.refs_5_), channel_id=1, source_target_pairs={{0,1},{1,0},{2,3},{3,2},{4,5},{5,4},{6,7},{7,6},{8,9},{9,8},{10,11... | collective-permute-start | bytes 1572872 | tf_op jit(solution)/shard_map/ppermute | solution.py:23
  76.1 10.9 %collective-permute-start.37 = (bf16[64,1024]{1,0:T(8,128)(2,1)S(1)}, bf16[64,1024]{1,0:T(8,128)(2,1)S(1)}, u32[]{:S(2)}, u32[]{:S(2)}) collective-permute-start(bf16[64,1024]{1,0:T(8,128)(2,1)S(1)} %after.20.refs_3_), channel_id=1, source_target_pairs={{0,12},{4,0},{8,4},{12,8},{1,13},{5,1},{9,5},{13,9},{2,14},{6,2},{... | collective-permute-start | bytes 393224 | tf_op jit(solution)/shard_map/ppermute | solution.py:23
  78.1 8.9 %collective-permute-start.39 = (bf16[64,1024]{1,0:T(8,128)(2,1)S(1)}, bf16[64,1024]{1,0:T(8,128)(2,1)S(1)}, u32[]{:S(2)}, u32[]{:S(2)}) collective-permute-start(bf16[64,1024]{1,0:T(8,128)(2,1)S(1)} %after.21.refs_4_), channel_id=1, source_target_pairs={{0,12},{4,0},{8,4},{12,8},{1,13},{5,1},{9,5},{13,9},{2,14},{6,2},{... | collective-permute-start | bytes 393224 | tf_op jit(solution)/shard_map/ppermute | solution.py:23
  83.5 12.2 %collective-permute-start.36 = (bf16[1024,128]{1,0:T(8,128)(2,1)S(1)}, bf16[1024,128]{1,0:T(8,128)(2,1)S(1)}, u32[]{:S(2)}, u32[]{:S(2)}) collective-permute-start(bf16[1024,128]{1,0:T(8,128)(2,1)S(1)} %get-tuple-element.90.refs_1_), channel_id=1, source_target_pairs={{0,2},{2,0},{1,3},{3,1},{4,6},{6,4},{5,7},{7,5},{8,10},{10,8},{9,1... | collective-permute-start | bytes 786440 | tf_op jit(solution)/shard_map/ppermute | solution.py:23
  85.0 4.3 %collective-permute-start.41 = (bf16[32,1024]{1,0:T(8,128)(2,1)S(1)}, bf16[32,1024]{1,0:T(8,128)(2,1)S(1)}, u32[]{:S(2)}, u32[]{:S(2)}) collective-permute-start(bf16[32,1024]{1,0:T(8,128)(2,1)S(1)} %after.22.refs_5_), channel_id=1, source_target_pairs={{0,12},{4,0},{8,4},{12,8},{1,13},{5,1},{9,5},{13,9},{2,14},{6,2},{... | collective-permute-start | bytes 196616 | tf_op jit(solution)/shard_map/ppermute | solution.py:23
  87.0 3.6 %collective-permute-start.38 = (bf16[64,1024]{1,0:T(8,128)(2,1)S(1)}, bf16[64,1024]{1,0:T(8,128)(2,1)S(1)}, u32[]{:S(2)}, u32[]{:S(2)}) collective-permute-start(bf16[64,1024]{1,0:T(8,128)(2,1)S(1)} %after.35.refs_4_), channel_id=1, source_target_pairs={{0,1},{1,0},{2,3},{3,2},{4,5},{5,4},{6,7},{7,6},{8,9},{9,8},{10,11... | collective-permute-start | bytes 393224 | tf_op jit(solution)/shard_map/ppermute | solution.py:23
  87.0 3.5 %collective-permute-start.40 = (bf16[64,1024]{1,0:T(8,128)(2,1)S(1)}, bf16[64,1024]{1,0:T(8,128)(2,1)S(1)}, u32[]{:S(2)}, u32[]{:S(2)}) collective-permute-start(bf16[64,1024]{1,0:T(8,128)(2,1)S(1)} %after.36.refs_6_), channel_id=1, source_target_pairs={{0,1},{1,0},{2,3},{3,2},{4,5},{5,4},{6,7},{7,6},{8,9},{9,8},{10,11... | collective-permute-start | bytes 393224 | tf_op jit(solution)/shard_map/ppermute | solution.py:23
  89.3 1.3 %collective-permute-start.42 = (bf16[32,1024]{1,0:T(8,128)(2,1)S(1)}, bf16[32,1024]{1,0:T(8,128)(2,1)S(1)}, u32[]{:S(2)}, u32[]{:S(2)}) collective-permute-start(bf16[32,1024]{1,0:T(8,128)(2,1)S(1)} %after.37.refs_8_), channel_id=1, source_target_pairs={{0,1},{1,0},{2,3},{3,2},{4,5},{5,4},{6,7},{7,6},{8,9},{9,8},{10,11... | collective-permute-start | bytes 196616 | tf_op jit(solution)/shard_map/ppermute | solution.py:23
  91.3 4.3 %collective-permute-start.43 = (bf16[256,128]{1,0:T(8,128)(2,1)S(1)}, bf16[256,128]{1,0:T(8,128)(2,1)S(1)}, u32[]{:S(2)}, u32[]{:S(2)}) collective-permute-start(bf16[256,128]{1,0:T(8,128)(2,1)S(1)} %get-tuple-element.93), channel_id=1, source_target_pairs={{0,2},{2,0},{1,3},{3,1},{4,6},{6,4},{5,7},{7,5},{8,10},{10,8},{9,1... | collective-permute-start | bytes 196616 | tf_op jit(solution)/shard_map/ppermute | solution.py:23
  (13 other events, 31.2 us)

commit v18 on v16

--- a/solution.py
+++ b/solution.py
@@ -13,6 +13,7 @@
 HBM = pl.BlockSpec(memory_space=pltpu.HBM)
 SMEM = pl.BlockSpec(memory_space=pltpu.SMEM)
 PARAMS = pltpu.CompilerParams(vmem_limit_bytes=24 * 2**20)
+WIDE = pltpu.CompilerParams(vmem_limit_bytes=32 * 2**20)
 FIRST = pltpu.CompilerParams(vmem_limit_bytes=60 * 2**20)
 LANES = 128
 CUTS = 8
@@ -464,6 +465,25 @@
         first_refs, second_refs, refs = refs[:n_first], refs[n_first:2 * n_first], refs[2 * n_first:]
         weight_ref, outs, (scored, held, acc, sem) = refs[0], refs[1:-4], refs[-4:]
         me, rep = lax.axis_index("shard"), lax.axis_index("rep")
+
+        def surplus_copies(s, odd):
+            apart = jnp.bitwise_xor(me, s)
+            rows_in = pl.ds(pl.multiple_of(lax.div(apart, jnp.int32(2)) * extra, extra), extra)
+            copies = []
+            for j, refs in enumerate([first_refs, second_refs]):
+                for d in range(n_rep):
+                    goal = held.at[s, d, j * extra:(j + 1) * extra]
+                    which = refs[odd * n_rep + d].at[rows_in]
+                    copies.append(pltpu.make_async_copy(which, goal, sem.at[s, j * n_rep + d]))
+            return copies
+
+        for s in range(n_shard if extra else 0):
+            for odd in range(2):
+                @pl.when((table_ref[s, 3] > 0) & (jnp.bitwise_and(jnp.bitwise_xor(me, s), 1) == odd))
+                def _():
+                    for copy in surplus_copies(s, odd):
+                        copy.start()
+
         weight = own_ref[...]
         for ref in other_refs:
             weight = weight + ref[...].astype(F32)
@@ -486,23 +506,10 @@
             if extra:
                 @pl.when(table_ref[s, 3] > 0)
                 def _():
-                    apart = jnp.bitwise_xor(me, s)
-                    rows_in = pl.ds(pl.multiple_of(lax.div(apart, jnp.int32(2)) * extra, extra), extra)
-                    for odd in range(2):
-                        @pl.when(jnp.bitwise_and(apart, 1) == odd)
-                        def _():
-                            copies = []
-                            for j, refs in enumerate([first_refs, second_refs]):
-                                for d in range(n_rep):
-                                    goal = held.at[d, j * extra:(j + 1) * extra]
-                                    which = refs[odd * n_rep + d].at[rows_in]
-                                    copies.append(pltpu.make_async_copy(which, goal, sem.at[j * n_rep + d]))
-                            for copy in copies:
-                                copy.start()
-                            for copy in copies:
-                                copy.wait()
+                    for copy in surplus_copies(s, 0):
+                        copy.wait()
                     some = pl.ds(pl.multiple_of(table_ref[s, 2] * 16, 16), extra)
-                    x = [held[d, some, :] for d in range(n_rep)]
+                    x = [held[s, d, some, :] for d in range(n_rep)]
                     put(acc, score(weight_ref, x, rep), start + table_ref[s, 1])
         for_feats(lambda at: acc[:rows // 8, :, at].reshape(rows, width // n_feat), outs)
 
@@ -515,12 +522,12 @@
         out_shape=[jax.ShapeDtypeStruct((depth, 2 * width), BF16)] + feat_shapes(rows, width, n_feat),
         scratch_shapes=[
             pltpu.VMEM((n_shard, bulk // 8, 8, width), F32),
-            pltpu.VMEM((n_rep, 3 * extra + 16, columns), BF16),
+            pltpu.VMEM((n_shard if extra else 1, n_rep, 3 * extra + 16, columns), BF16),
             pltpu.VMEM(((rows + bulk + extra) // 8 + 2, 8, width), F32),
-            pltpu.SemaphoreType.DMA((2 * n_rep,)),
+            pltpu.SemaphoreType.DMA((n_shard, 2 * n_rep)),
         ],
         cost_estimate=cost(4 * count * depth * width, 10 * depth * width + count * (2 * depth + 4 * width)),
-        compiler_params=PARAMS,
+        compiler_params=WIDE,
         name="early_scores",
     )(table, own, *others, mine, *[p for parts in pieces for p in parts], *surplus)
 
@@ -603,8 +610,9 @@
     pieces = [picked[0]] + [shift(picked[d], "shard", n_shard, d) for d in range(1, n_shard)]
 
     middle = [(d, 0, bulk) for d in range(1, last_hops)]
-    part = 64 if bulk % 64 == 0 else bulk // 2
-    final = [(last_hops, at, part) for at in range(0, bulk, part)]
+    fillers = 2 if bulk % 256 == 0 else 1
+    sizes = [n * bulk // 16 for n in ((4, 2, 4, 3, 3) if bulk % 256 == 0 else (8, 8))]
+    final = [(last_hops, sum(sizes[:j]), n) for j, n in enumerate(sizes)]
     *packed, goal = pack_rows(train, ids, columns, bulk, extra, middle + final)
     firsts, seconds = [], []
     parts = [pieces] + [[shift(x, "groups", n_group, d) for x in pieces] for d in range(1, n_group)]
@@ -614,8 +622,8 @@
         far = swap(after(packed[-2], *pieces[1:]), "shard", n_shard, 2)
         urgent.append(far)
     sent_last = packed[len(middle):len(middle) + len(final)]
-    last = [shift(after(sent_last[0], *pieces[1:]), "shard", n_shard, last_hops)]
-    urgent.append(last[0])
+    last = [shift(after(x, *pieces[1:]), "shard", n_shard, last_hops) for x in sent_last[:fillers]]
+    urgent += last
     depth = n_rep * columns
     targets = [(feat + d) % n_feat for d in range(1, n_feat)]
     near_chip = fetch(matrices, targets[0], depth, *pieces[1:])
@@ -634,11 +642,11 @@
     for (hops, _, _), x in zip(middle[1:], packed[1:]):
         here.append(shift(after(x, *urgent, *sends), "shard", n_shard, hops))
         urgent = [here[-1]]
-    sent_last = [after(x, own) for x in sent_last[1:]]
-    last_all = [with_rep(after(last[0], own))]
+    sent_last = [after(x, own) for x in sent_last[fillers:]]
+    last_all = [with_rep(after(x, own)) for x in last]
 
     mine = own_rows(goal, train, bulk, own)
-    marks = [own, mine, *sent_last, *last_all[0][1:]]
+    marks = [own, mine, *sent_last, *[p for x in last_all for p in x[1:]]]
     if extra:
         for d in range(1, n_group):
             flag = jnp.maximum(flag, shift(flag, "groups", n_group, d))
@@ -667,7 +675,7 @@
     def over_feat(shares):
         return [shares[0]] + [shift(shares[d], "feat", n_feat, d) for d in range(1, n_feat)]
 
-    last_all += [with_rep(after(x, *early[1:])) for x in last[1:]]
+    last_all += [with_rep(after(x, *early[1:])) for x in last[fillers:]]
     late = late_scores(last_all, weight, n_feat)
     return merge(table, over_feat(early), over_feat(late), n_shard)[None]
 

time: 95.5 us -> 95.4 us (level)
  starting transfers between devices: 33.4 us -> 36.7 us
  waiting for transfers between devices: 22.3 us -> 20.4 us
  local copies, waits for them, and re-layouts: 5.05 us -> 4.04 us
    ppermute x36 -> x38, starting transfers between devices: 30 us -> 31.9 us  [shift(): return lax.ppermute(x, axis, [(i, (i + by) % size) for i in range(size)])]
    ppermute x2, waiting for transfers between devices: 4.69 us -> 3.06 us  [swap(): return lax.ppermute(x, axis, [(i, i ^ bit) for i in range(size)])]
    ppermute x2, starting transfers between devices: 3.35 us -> 4.76 us  [swap(): return lax.ppermute(x, axis, [(i, i ^ bit) for i in range(size)])]
    unnamed x36 -> x42, local copies, waits for them, and re-layouts: 4.53 us -> 3.46 us
    ppermute x36 -> x38, waiting for transfers between devices: 17.6 us -> 17.3 us  [shift(): return lax.ppermute(x, axis, [(i, (i + by) % size) for i in range(size)])]
  transfers between devices with their start and end apart: 38 -> 40, of which waited for: 13 -> 12; matrix products, arithmetic and copies ran while one was open for 1% -> 1% of each run, Pallas kernels for 33% -> 33%
where the time goes in v18:
time: 95.4 us; the launch traced here: 95.1 us
  starting transfers between devices  36.7 us (38%)
  Pallas kernels  32.7 us (34%)
  waiting for transfers between devices  20.4 us (21%)
  local copies, waits for them, and re-layouts  4.04 us (4%)
  between operations  1.2 us (1%)
    ppermute x38, starting transfers between devices, shift(): return lax.ppermute(x, axis, [(i, (i + by) % size) for i in range(size)])  31.9 us
    ppermute x38, waiting for transfers between devices, shift(): return lax.ppermute(x, axis, [(i, (i + by) % size) for i in range(size)])  17.3 us
    pallas_call x1, Pallas kernels, pack_rows(): pl.pallas_call(kernel, grid=(1,), in_specs=[pl.BlockSpec((lines, LANES),...  6.6 us
    pallas_call x1, Pallas kernels, partial_weights(): pl.pallas_call(kernel, in_specs=[SMEM] + [HBM] * n + [VMEM] * (CUTS * n)...  6.6 us
    ppermute x2, starting transfers between devices, swap(): return lax.ppermute(x, axis, [(i, i ^ bit) for i in range(size)])  4.76 us
    pallas_call x1, Pallas kernels, early_scores(): pl.pallas_call(kernel, in_specs=[SMEM] + [VMEM] * (2 + n_other + n_rep *...  4.16 us
    unnamed x42, local copies, waits for them, and re-layouts  3.46 us
    ppermute x2, waiting for transfers between devices, swap(): return lax.ppermute(x, axis, [(i, i ^ bit) for i in range(size)])  3.06 us
  transfers between devices with their start and end apart: 40, of which 12 were waited for; matrix products, arithmetic and copies ran while one was open for 1% of the time, Pallas kernels for 33%

profile of v18, /device:TPU:0, one launch (start us, length us, event | category | flops | bytes accessed | tf_op | source)
XLA Modules:
  0.0 95.1 jit_solution(6819695018177531021)
XLA Ops:
  0.0 0.5 collective-permute-start.7
  0.5 2.7 %pick_queries.1 = (bf16[1,64,1024]{2,1,0:T(8,128)(2,1)}, bf16[1,64,1024]{2,1,0:T(8,128)(2,1)}, bf16[1,64,1024]{2,1,0:T(8,128)(2,1)}, bf16[1,64,1024]{2,1,0:T(8,128)(2,1)}) custom-call(s32[4,4]{1,0:T(4,128)} %pattern_ref.3, s32[16]{0:T(128)} %slot_ref.3, bf16[4,128,1024]{2,1,0:T(8,128)(2,1)} %in_ref.1), custom_call_target="tpu_custom_call" | custom-call | flops 1 | bytes 1 | tf_op jit(solution)/shard_map/pick_queries/pallas_call | solution.py:109
  3.1 2.8 %collective-permute-start.4 = (bf16[1,64,1024]{2,1,0:T(8,128)(2,1)}, bf16[1,64,1024]{2,1,0:T(8,128)(2,1)S(1)}, u32[]{:S(2)}, u32[]{:S(2)}) collective-permute-start(bf16[1,64,1024]{2,1,0:T(8,128)(2,1)} %get-tuple-element.50), channel_id=1, source_target_pairs={{0,4},{4,8},{8,12},{12,0},{1,5},{5,9},{9,13},{13,1},{2,6},{6,10},{... | collective-permute-start | bytes 393224 | tf_op jit(solution)/shard_map/ppermute | solution.py:23
  5.9 2.6 %collective-permute-start.5 = (bf16[1,64,1024]{2,1,0:T(8,128)(2,1)}, bf16[1,64,1024]{2,1,0:T(8,128)(2,1)S(1)}, u32[]{:S(2)}, u32[]{:S(2)}) collective-permute-start(bf16[1,64,1024]{2,1,0:T(8,128)(2,1)} %get-tuple-element.51), channel_id=1, source_target_pairs={{0,8},{4,12},{8,0},{12,4},{1,9},{5,13},{9,1},{13,5},{2,10},{6,14},... | collective-permute-start | bytes 393224 | tf_op jit(solution)/shard_map/ppermute | solution.py:23
  8.5 1.3 %collective-permute-start.6 = (bf16[1,64,1024]{2,1,0:T(8,128)(2,1)}, bf16[1,64,1024]{2,1,0:T(8,128)(2,1)S(1)}, u32[]{:S(2)}, u32[]{:S(2)}) collective-permute-start(bf16[1,64,1024]{2,1,0:T(8,128)(2,1)} %get-tuple-element.52), channel_id=1, source_target_pairs={{0,12},{4,0},{8,4},{12,8},{1,13},{5,1},{9,5},{13,9},{2,14},{6,2},{... | collective-permute-start | bytes 393224 | tf_op jit(solution)/shard_map/ppermute | solution.py:23
  9.9 1.5 %collective-permute-start.8 = (bf16[1,64,1024]{2,1,0:T(8,128)(2,1)}, bf16[1,64,1024]{2,1,0:T(8,128)(2,1)S(1)}, u32[]{:S(2)}, u32[]{:S(2)}) collective-permute-start(bf16[1,64,1024]{2,1,0:T(8,128)(2,1)} %get-tuple-element.54.refs_0_), channel_id=1, source_target_pairs={{0,16},{16,0},{1,17},{17,1},{2,18},{18,2},{3,19},{19,3},{4,20},{20... | collective-permute-start | bytes 393224 | tf_op jit(solution)/shard_map/ppermute | solution.py:23
  11.4 6.6 %pack_rows.1 = (bf16[256,1024]{1,0:T(8,128)(2,1)}, bf16[256,1024]{1,0:T(8,128)(2,1)}, bf16[64,1024]{1,0:T(8,128)(2,1)}, bf16[32,1024]{1,0:T(8,128)(2,1)}, bf16[6...) custom-call(s32[32,128]{1,0:T(8,128)} %bitcast.11, ...), custom_call_target="tpu_custom_call" | custom-call | flops 1 | bytes 1 | tf_op jit(solution)/shard_map/pack_rows/pallas_call | solution.py:253
  18.0 3.2 %collective-permute-start.21 = (bf16[256,1024]{1,0:T(8,128)(2,1)}, bf16[256,1024]{1,0:T(8,128)(2,1)S(1)}, u32[]{:S(2)}, u32[]{:S(2)}) collective-permute-start(bf16[256,1024]{1,0:T(8,128)(2,1)} %after.19), channel_id=1, source_target_pairs={{0,4},{4,8},{8,12},{12,0},{1,5},{5,9},{9,13},{13,1},{2,6},{6,10},{... | collective-permute-start | bytes 1572872 | tf_op jit(solution)/shard_map/ppermute | solution.py:23
  21.2 1.5 %collective-permute-start.9 = (bf16[1,64,1024]{2,1,0:T(8,128)(2,1)S(1)}, bf16[1,64,1024]{2,1,0:T(8,128)(2,1)S(1)}, u32[]{:S(2)}, u32[]{:S(2)}) collective-permute-start(bf16[1,64,1024]{2,1,0:T(8,128)(2,1)S(1)} %collective-permute-done.4.rest_0_.refs_2_.refs_1_), channel_id=1, source_target_pairs={{0,16},{16,0},{1,17},{17,1},{2,18},{18,2},{3,19},{19,3},{4,20},{20... | collective-permute-start | bytes 393224 | tf_op jit(solution)/shard_map/ppermute | solution.py:23
  22.7 0.5 collective-permute-start.10
  23.2 1.5 %collective-permute-start.11 = (bf16[1,64,1024]{2,1,0:T(8,128)(2,1)S(1)}, bf16[1,64,1024]{2,1,0:T(8,128)(2,1)S(1)}, u32[]{:S(2)}, u32[]{:S(2)}) collective-permute-start(bf16[1,64,1024]{2,1,0:T(8,128)(2,1)S(1)} %collective-permute-done.6.rest_2_.refs_4_.refs_3_), channel_id=1, source_target_pairs={{0,16},{16,0},{1,17},{17,1},{2,18},{18,2},{3,19},{19,3},{4,20},{20... | collective-permute-start | bytes 393224 | tf_op jit(solution)/shard_map/ppermute | solution.py:23
  24.7 1.6 %collective-permute-start.27 = (bf16[128,1024]{1,0:T(8,128)(2,1)}, bf16[128,1024]{1,0:T(8,128)(2,1)S(1)}, u32[]{:S(2)}, u32[]{:S(2)}) collective-permute-start(bf16[128,1024]{1,0:T(8,128)(2,1)} %after.28), channel_id=1, source_target_pairs={{0,8},{4,12},{8,0},{12,4},{1,9},{5,13},{9,1},{13,5},{2,10},{6,14},... | collective-permute-start | bytes 786440 | tf_op jit(solution)/shard_map/ppermute | solution.py:27
  26.4 0.8 row_table.1
  27.2 3.4 %copy-done = bf16[1,4096,1024]{2,1,0:T(8,128)(2,1)S(1)} copy-done((bf16[1,4096,1024]{2,1,0:T(8,128)(2,1)S(1)}, bf16[1,4096,1024]{2,1,0:T(8,128)(2,1)}, u32[]{:S(2)}) %copy-start) | copy-done | bytes 8388632
  30.6 2.5 %fetch.1 = (bf16[2048,1024]{1,0:T(8,128)(2,1)S(1)}, bf16[2048,1024]{1,0:T(8,128)(2,1)S(1)}) custom-call(s32[1]{0:T(128)} %bitcast.3.block_ref, bf16[4096,1024]{1,0:T(8,128)(2,1)S(1)} %bitcast.7, bf16[4096,1024]{1,0:T(8,128)(2,1)} %collective-permute-done.7.refs_1_, bf16[1,64,1024]{2,1,0:T(8,128)(2,1)S(1)} %collective-permute-done.4.rest_0_.refs_2_.refs_1_, ...), custom_call_target="tpu_custom_call" | custom-call | flops 1 | bytes 1 | tf_op jit(solution)/shard_map/fetch/pallas_call | solution.py:326
  33.2 1.2 %join_queries.1 = (bf16[128,256]{1,0:T(8,128)(2,1)S(1)}, bf16[128,256]{1,0:T(8,128)(2,1)S(1)}, bf16[128,256]{1,0:T(8,128)(2,1)S(1)}, bf16[128,256]{1,0:T(8,128)(...) custom-call(s32[4,4]{1,0:T(4,128)S(1)} %copy-done.15, ...), custom_call_target="tpu_custom_call" | custom-call | flops 1 | bytes 1 | tf_op jit(solution)/shard_map/join_queries/pallas_call | solution.py:154
  34.5 0.5 collective-permute-start.13
  35.1 0.7 collective-permute-done.12.refs_10_
  36.4 0.6 collective-permute-done.15.refs_13_
  37.2 0.7 collective-permute-start.22
  38.3 1.8 %collective-permute-start.24 = (bf16[32,1024]{1,0:T(8,128)(2,1)S(1)}, bf16[32,1024]{1,0:T(8,128)(2,1)S(1)}, u32[]{:S(2)}, u32[]{:S(2)}) collective-permute-start(bf16[32,1024]{1,0:T(8,128)(2,1)S(1)} %after.25), channel_id=1, source_target_pairs={{0,12},{4,0},{8,4},{12,8},{1,13},{5,1},{9,5},{13,9},{2,14},{6,2},{... | collective-permute-start | bytes 196616 | tf_op jit(solution)/shard_map/ppermute | solution.py:23
  40.1 2.3 %fetched_weights.1.refs_18_.refs_2_.refs_5_ = bf16[2048,256]{1,0:T(8,128)(2,1)S(1)} custom-call(bf16[2048,1024]{1,0:T(8,128)(2,1)S(1)} %get-tuple-element.55.refs_8_.refs_0_, bf16[2048,1024]{1,0:T(8,128)(2,1)S(1)} %get-tuple-element.56.refs_9_.refs_1_, bf16[128,256]{1,0:T(8,128)(2,1)S(1)} %get-tuple-element.58.refs_2_, ...), custom_call_target="tpu_custom_call" | custom-call | flops 1 | bytes 1 | tf_op jit(solution)/shard_map/fetched_weights/pallas_call | solution.py:353
  42.4 3.1 %collective-permute-done.27.refs_1_.refs_0_.refs_2_ = bf16[128,1024]{1,0:T(8,128)(2,1)S(1)} collective-permute-done((bf16[128,1024]{1,0:T(8,128)(2,1)}, bf16[128,1024]{1,0:T(8,128)(2,1)S(1)}, u32[]{:S(2)}, u32[]{:S(2)}) %collective-permute-start.27) | collective-permute-done | bytes 262176 | tf_op jit(solution)/shard_map/ppermute | solution.py:27
  45.5 0.8 stack.3
  46.3 3.1 %collective-permute-start.28 = (bf16[256,1024]{1,0:T(8,128)(2,1)}, bf16[256,1024]{1,0:T(8,128)(2,1)}, u32[]{:S(2)}, u32[]{:S(2)}) collective-permute-start(bf16[256,1024]{1,0:T(8,128)(2,1)} %stack.3), channel_id=1, source_target_pairs={{0,4},{4,0},{8,12},{12,8},{1,5},{5,1},{9,13},{13,9},{2,6},{6,2},{1... | collective-permute-start | bytes 1572872 | tf_op jit(solution)/shard_map/ppermute | solution.py:27
  49.4 1.5 %collective-permute-start.20 = (bf16[2048,256]{1,0:T(8,128)(2,1)S(1)}, bf16[2048,256]{1,0:T(8,128)(2,1)}, u32[]{:S(2)}, u32[]{:S(2)}) collective-permute-start(bf16[2048,256]{1,0:T(8,128)(2,1)S(1)} %fetched_weights.1.refs_18_.refs_2_.refs_5_), channel_id=1, source_target_pairs={{0,2},{2,0},{1,3},{3,1},{4,6},{6,4},{5,7},{7,5},{8,10},{10,8},{9,1... | collective-permute-start | bytes 3145736 | tf_op jit(solution)/shard_map/ppermute | solution.py:23
  50.9 3.3 %collective-permute-start.33 = (bf16[256,1024]{1,0:T(8,128)(2,1)}, bf16[256,1024]{1,0:T(8,128)(2,1)}, u32[]{:S(2)}, u32[]{:S(2)}) collective-permute-start(bf16[256,1024]{1,0:T(8,128)(2,1)} %after.32), channel_id=1, source_target_pairs={{0,8},{4,12},{8,0},{12,4},{1,9},{5,13},{9,1},{13,5},{2,10},{6,14},... | collective-permute-start | bytes 1572872 | tf_op jit(solution)/shard_map/ppermute | solution.py:23
  54.3 1.5 %collective-permute-start.26 = (s32[8,128]{1,0:T(8,128)S(1)}, s32[8,128]{1,0:T(8,128)S(1)}, u32[]{:S(2)}, u32[]{:S(2)}) collective-permute-start(s32[8,128]{1,0:T(8,128)S(1)} %get-tuple-element.57.refs_10_), channel_id=1, source_target_pairs={{0,16},{16,0},{1,17},{17,1},{2,18},{18,2},{3,19},{19,3},{4,20},{20... | collective-permute-start | bytes 12296 | tf_op jit(solution)/shard_map/ppermute | solution.py:23
  55.8 2.1 %collective-permute-done.26 = s32[8,128]{1,0:T(8,128)S(1)} collective-permute-done((s32[8,128]{1,0:T(8,128)S(1)}, s32[8,128]{1,0:T(8,128)S(1)}, u32[]{:S(2)}, u32[]{:S(2)}) %collective-permute-start.26) | collective-permute-done | bytes 4128 | tf_op jit(solution)/shard_map/ppermute | solution.py:23
  57.9 0.6 slice.3
  59.2 6.6 %partial_weights.1.rest_0_.refs_1_.refs_2_.refs_0_ = f32[2048,256]{1,0:T(8,128)S(1)} custom-call(s32[1]{0:T(128)} %bitcast.1.block_ref, bf16[4096,1024]{1,0:T(8,128)(2,1)S(1)} %bitcast.10, bf16[4096,1024]{1,0:T(8,128)(2,1)} %collective-permute-done.7.refs_1_, bf16[128,256]{1,0:T(8,128)(2,1)S(1)} %get-tuple-element.58.refs_2_, ...), custom_call_target="tpu_custom_call" | custom-call | flops 1 | bytes 1 | tf_op jit(solution)/shard_map/partial_weights/pallas_call | solution.py:293
  66.2 0.5 collective-permute-start.30
  66.7 1.2 %collective-permute-done.29.refs_0_ = bf16[128,1024]{1,0:T(8,128)(2,1)S(1)} collective-permute-done((bf16[128,1024]{1,0:T(8,128)(2,1)}, bf16[128,1024]{1,0:T(8,128)(2,1)S(1)}, u32[]{:S(2)}, u32[]{:S(2)}) %collective-permute-start.29) | collective-permute-done | bytes 262176 | tf_op jit(solution)/shard_map/ppermute | solution.py:23
  68.0 0.4 collective-permute-start.25
  68.5 2.4 %own_rows.1.refs_2_ = bf16[256,2048]{1,0:T(8,128)(2,1)S(1)} custom-call(s32[8,128]{1,0:T(8,128)S(1)} %copy-done.16, bf16[1024,2048]{1,0:T(8,128)(2,1)S(1)} %copy-done.1, f32[2048,256]{1,0:T(8,128)S(1)} %partial_weights.1.rest_0_.refs_1_.refs_2_.refs_0_), custom_call_target="tpu_custom_call" | custom-call | flops 1 | bytes 1 | tf_op jit(solution)/shard_map/own_rows/pallas_call | solution.py:195
  71.0 0.4 collective-permute-start.31
  71.6 0.7 collective-permute-done.31.refs_1_
  72.6 4.3 %collective-permute-done.33.refs_0_ = bf16[256,1024]{1,0:T(8,128)(2,1)} collective-permute-done((bf16[256,1024]{1,0:T(8,128)(2,1)}, bf16[256,1024]{1,0:T(8,128)(2,1)}, u32[]{:S(2)}, u32[]{:S(2)}) %collective-permute-start.33) | collective-permute-done | bytes 524320 | tf_op jit(solution)/shard_map/ppermute | solution.py:23
  76.9 2.4 %collective-permute-start.37 = (bf16[64,1024]{1,0:T(8,128)(2,1)S(1)}, bf16[64,1024]{1,0:T(8,128)(2,1)S(1)}, u32[]{:S(2)}, u32[]{:S(2)}) collective-permute-start(bf16[64,1024]{1,0:T(8,128)(2,1)S(1)} %after.20.refs_3_), channel_id=1, source_target_pairs={{0,12},{4,0},{8,4},{12,8},{1,13},{5,1},{9,5},{13,9},{2,14},{6,2},{... | collective-permute-start | bytes 393224 | tf_op jit(solution)/shard_map/ppermute | solution.py:23
  79.4 4.2 %early_scores.1 = (bf16[2048,512]{1,0:T(8,128)(2,1)S(1)}, f32[1024,128]{1,0:T(8,128)S(1)}, bf16[1024,128]{1,0:T(8,128)(2,1)S(1)}) custom-call(s32[4,4]{1,0:T(4,128)S(1)} %get-tuple-element.53.table_ref, f32[2048,256]{1,0:T(8,128)S(1)} %partial_weights.1.rest_0_.refs_1_.refs_2_.refs_0_, bf16[2048,256]{1,0:T(8,128)(2,1)} %collective-permute-done.20.refs_1_, ...), custom_call_target="tpu_custom_call" | custom-call | flops 1 | bytes 1 | tf_op jit(solution)/shard_map/early_scores/pallas_call | solution.py:518
  83.6 1.0 %collective-permute-start.36 = (bf16[1024,128]{1,0:T(8,128)(2,1)S(1)}, bf16[1024,128]{1,0:T(8,128)(2,1)S(1)}, u32[]{:S(2)}, u32[]{:S(2)}) collective-permute-start(bf16[1024,128]{1,0:T(8,128)(2,1)S(1)} %get-tuple-element.90.refs_1_), channel_id=1, source_target_pairs={{0,2},{2,0},{1,3},{3,1},{4,6},{6,4},{5,7},{7,5},{8,10},{10,8},{9,1... | collective-permute-start | bytes 786440 | tf_op jit(solution)/shard_map/ppermute | solution.py:23
  84.6 0.7 collective-permute-done.39.refs_0_
  85.3 1.7 %collective-permute-done.41.refs_0_ = bf16[48,1024]{1,0:T(8,128)(2,1)S(1)} collective-permute-done((bf16[48,1024]{1,0:T(8,128)(2,1)S(1)}, bf16[48,1024]{1,0:T(8,128)(2,1)S(1)}, u32[]{:S(2)}, u32[]{:S(2)}) %collective-permute-start.41) | collective-permute-done | bytes 98336 | tf_op jit(solution)/shard_map/ppermute | solution.py:23
  87.0 1.3 %collective-permute-done.42.refs_9_ = bf16[48,1024]{1,0:T(8,128)(2,1)S(1)} collective-permute-done((bf16[48,1024]{1,0:T(8,128)(2,1)S(1)}, bf16[48,1024]{1,0:T(8,128)(2,1)S(1)}, u32[]{:S(2)}, u32[]{:S(2)}) %collective-permute-start.42) | collective-permute-done | bytes 98336 | tf_op jit(solution)/shard_map/ppermute | solution.py:23
  88.3 0.7 late_scores.1
  89.1 0.7 collective-permute-start.43
  89.8 3.7 %collective-permute-done.43.refs_3_ = bf16[256,128]{1,0:T(8,128)(2,1)S(1)} collective-permute-done((bf16[256,128]{1,0:T(8,128)(2,1)S(1)}, bf16[256,128]{1,0:T(8,128)(2,1)S(1)}, u32[]{:S(2)}, u32[]{:S(2)}) %collective-permute-start.43) | collective-permute-done | bytes 65568 | tf_op jit(solution)/shard_map/ppermute | solution.py:23
  93.5 1.7 %merge.1 = f32[128,1024]{1,0:T(8,128)} custom-call(s32[4,4]{1,0:T(4,128)S(1)} %get-tuple-element.53.table_ref, f32[1024,128]{1,0:T(8,128)S(1)} %get-tuple-element.89.refs_0_, bf16[1024,128]{1,0:T(8,128)(2,1)S(1)} %collective-permute-done.36.refs_1_, f32[256,128]{1,0:T(8,128)S(1)} %get-tuple-element.92.refs_2_, ...), custom_call_target="tpu_custom_call" | custom-call | flops 1 | bytes 1 | tf_op jit(solution)/shard_map/merge/pallas_call | solution.py:578
  (113 shorter events, 2.7 us)
Async XLA Ops:
  0.0 26.4 %copy-start.13 = (s32[4096]{0:T(1024)S(1)}, s32[4096]{0:T(1024)}, u32[]{:S(2)}) copy-start(s32[4096]{0:T(1024)} %param.9) | copy-start | bytes 49156
  0.0 24.7 %collective-permute-start.7 = (bf16[4096,1024]{1,0:T(8,128)(2,1)}, bf16[4096,1024]{1,0:T(8,128)(2,1)}, u32[]{:S(2)}, u32[]{:S(2)}) collective-permute-start(bf16[4096,1024]{1,0:T(8,128)(2,1)} %bitcast.6), channel_id=1, source_target_pairs={{0,1},{1,0},{2,3},{3,2},{4,5},{5,4},{6,7},{7,6},{8,9},{9,8},{10,11... | collective-permute-start | bytes 25165832 | tf_op jit(solution)/shard_map/ppermute | solution.py:23
  3.1 14.8 %collective-permute-start.4 = (bf16[1,64,1024]{2,1,0:T(8,128)(2,1)}, bf16[1,64,1024]{2,1,0:T(8,128)(2,1)S(1)}, u32[]{:S(2)}, u32[]{:S(2)}) collective-permute-start(bf16[1,64,1024]{2,1,0:T(8,128)(2,1)} %get-tuple-element.50), channel_id=1, source_target_pairs={{0,4},{4,8},{8,12},{12,0},{1,5},{5,9},{9,13},{13,1},{2,6},{6,10},{... | collective-permute-start | bytes 393224 | tf_op jit(solution)/shard_map/ppermute | solution.py:23
  5.9 12.1 %collective-permute-start.5 = (bf16[1,64,1024]{2,1,0:T(8,128)(2,1)}, bf16[1,64,1024]{2,1,0:T(8,128)(2,1)S(1)}, u32[]{:S(2)}, u32[]{:S(2)}) collective-permute-start(bf16[1,64,1024]{2,1,0:T(8,128)(2,1)} %get-tuple-element.51), channel_id=1, source_target_pairs={{0,8},{4,12},{8,0},{12,4},{1,9},{5,13},{9,1},{13,5},{2,10},{6,14},... | collective-permute-start | bytes 393224 | tf_op jit(solution)/shard_map/ppermute | solution.py:23
  8.5 9.5 %collective-permute-start.6 = (bf16[1,64,1024]{2,1,0:T(8,128)(2,1)}, bf16[1,64,1024]{2,1,0:T(8,128)(2,1)S(1)}, u32[]{:S(2)}, u32[]{:S(2)}) collective-permute-start(bf16[1,64,1024]{2,1,0:T(8,128)(2,1)} %get-tuple-element.52), channel_id=1, source_target_pairs={{0,12},{4,0},{8,4},{12,8},{1,13},{5,1},{9,5},{13,9},{2,14},{6,2},{... | collective-permute-start | bytes 393224 | tf_op jit(solution)/shard_map/ppermute | solution.py:23
  9.9 13.3 %collective-permute-start.8 = (bf16[1,64,1024]{2,1,0:T(8,128)(2,1)}, bf16[1,64,1024]{2,1,0:T(8,128)(2,1)S(1)}, u32[]{:S(2)}, u32[]{:S(2)}) collective-permute-start(bf16[1,64,1024]{2,1,0:T(8,128)(2,1)} %get-tuple-element.54.refs_0_), channel_id=1, source_target_pairs={{0,16},{16,0},{1,17},{17,1},{2,18},{18,2},{3,19},{19,3},{4,20},{20... | collective-permute-start | bytes 393224 | tf_op jit(solution)/shard_map/ppermute | solution.py:23
  18.0 32.9 %collective-permute-start.21 = (bf16[256,1024]{1,0:T(8,128)(2,1)}, bf16[256,1024]{1,0:T(8,128)(2,1)S(1)}, u32[]{:S(2)}, u32[]{:S(2)}) collective-permute-start(bf16[256,1024]{1,0:T(8,128)(2,1)} %after.19), channel_id=1, source_target_pairs={{0,4},{4,8},{8,12},{12,0},{1,5},{5,9},{9,13},{13,1},{2,6},{6,10},{... | collective-permute-start | bytes 1572872 | tf_op jit(solution)/shard_map/ppermute | solution.py:23
  21.2 12.0 %collective-permute-start.9 = (bf16[1,64,1024]{2,1,0:T(8,128)(2,1)S(1)}, bf16[1,64,1024]{2,1,0:T(8,128)(2,1)S(1)}, u32[]{:S(2)}, u32[]{:S(2)}) collective-permute-start(bf16[1,64,1024]{2,1,0:T(8,128)(2,1)S(1)} %collective-permute-done.4.rest_0_.refs_2_.refs_1_), channel_id=1, source_target_pairs={{0,16},{16,0},{1,17},{17,1},{2,18},{18,2},{3,19},{19,3},{4,20},{20... | collective-permute-start | bytes 393224 | tf_op jit(solution)/shard_map/ppermute | solution.py:23
  22.7 10.4 %collective-permute-start.10 = (bf16[1,64,1024]{2,1,0:T(8,128)(2,1)S(1)}, bf16[1,64,1024]{2,1,0:T(8,128)(2,1)S(1)}, u32[]{:S(2)}, u32[]{:S(2)}) collective-permute-start(bf16[1,64,1024]{2,1,0:T(8,128)(2,1)S(1)} %collective-permute-done.5.rest_1_.refs_3_.refs_2_), channel_id=1, source_target_pairs={{0,16},{16,0},{1,17},{17,1},{2,18},{18,2},{3,19},{19,3},{4,20},{20... | collective-permute-start | bytes 393224 | tf_op jit(solution)/shard_map/ppermute | solution.py:23
  23.2 9.9 %collective-permute-start.11 = (bf16[1,64,1024]{2,1,0:T(8,128)(2,1)S(1)}, bf16[1,64,1024]{2,1,0:T(8,128)(2,1)S(1)}, u32[]{:S(2)}, u32[]{:S(2)}) collective-permute-start(bf16[1,64,1024]{2,1,0:T(8,128)(2,1)S(1)} %collective-permute-done.6.rest_2_.refs_4_.refs_3_), channel_id=1, source_target_pairs={{0,16},{16,0},{1,17},{17,1},{2,18},{18,2},{3,19},{19,3},{4,20},{20... | collective-permute-start | bytes 393224 | tf_op jit(solution)/shard_map/ppermute | solution.py:23
  24.7 20.7 %collective-permute-start.27 = (bf16[128,1024]{1,0:T(8,128)(2,1)}, bf16[128,1024]{1,0:T(8,128)(2,1)S(1)}, u32[]{:S(2)}, u32[]{:S(2)}) collective-permute-start(bf16[128,1024]{1,0:T(8,128)(2,1)} %after.28), channel_id=1, source_target_pairs={{0,8},{4,12},{8,0},{12,4},{1,9},{5,13},{9,1},{13,5},{2,10},{6,14},... | collective-permute-start | bytes 786440 | tf_op jit(solution)/shard_map/ppermute | solution.py:27
  33.2 4.8 %copy-start.14 = (bf16[32,1024]{1,0:T(8,128)(2,1)S(1)}, bf16[32,1024]{1,0:T(8,128)(2,1)}, u32[]{:S(2)}) copy-start(bf16[32,1024]{1,0:T(8,128)(2,1)} %get-tuple-element.80.refs_0_) | copy-start | bytes 196612
  34.4 1.3 %collective-permute-start.12 = (bf16[128,256]{1,0:T(8,128)(2,1)S(1)}, bf16[128,256]{1,0:T(8,128)(2,1)S(1)}, u32[]{:S(2)}, u32[]{:S(2)}) collective-permute-start(bf16[128,256]{1,0:T(8,128)(2,1)S(1)} %get-tuple-element.66), channel_id=1, source_target_pairs={{0,1},{1,0},{2,3},{3,2},{4,5},{5,4},{6,7},{7,6},{8,9},{9,8},{10,11... | collective-permute-start | bytes 196616 | tf_op jit(solution)/shard_map/ppermute | solution.py:23
  34.5 1.4 %collective-permute-start.13 = (bf16[128,256]{1,0:T(8,128)(2,1)S(1)}, bf16[128,256]{1,0:T(8,128)(2,1)S(1)}, u32[]{:S(2)}, u32[]{:S(2)}) collective-permute-start(bf16[128,256]{1,0:T(8,128)(2,1)S(1)} %get-tuple-element.67), channel_id=1, source_target_pairs={{0,1},{1,0},{2,3},{3,2},{4,5},{5,4},{6,7},{7,6},{8,9},{9,8},{10,11... | collective-permute-start | bytes 196616 | tf_op jit(solution)/shard_map/ppermute | solution.py:23
  35.0 1.3 %collective-permute-start.14 = (bf16[128,256]{1,0:T(8,128)(2,1)S(1)}, bf16[128,256]{1,0:T(8,128)(2,1)S(1)}, u32[]{:S(2)}, u32[]{:S(2)}) collective-permute-start(bf16[128,256]{1,0:T(8,128)(2,1)S(1)} %get-tuple-element.68), channel_id=1, source_target_pairs={{0,1},{1,0},{2,3},{3,2},{4,5},{5,4},{6,7},{7,6},{8,9},{9,8},{10,11... | collective-permute-start | bytes 196616 | tf_op jit(solution)/shard_map/ppermute | solution.py:23
  35.8 1.3 %collective-permute-start.15 = (bf16[128,256]{1,0:T(8,128)(2,1)S(1)}, bf16[128,256]{1,0:T(8,128)(2,1)S(1)}, u32[]{:S(2)}, u32[]{:S(2)}) collective-permute-start(bf16[128,256]{1,0:T(8,128)(2,1)S(1)} %get-tuple-element.69), channel_id=1, source_target_pairs={{0,1},{1,0},{2,3},{3,2},{4,5},{5,4},{6,7},{7,6},{8,9},{9,8},{10,11... | collective-permute-start | bytes 196616 | tf_op jit(solution)/shard_map/ppermute | solution.py:23
  35.9 1.3 %collective-permute-start.16 = (bf16[128,256]{1,0:T(8,128)(2,1)S(1)}, bf16[128,256]{1,0:T(8,128)(2,1)S(1)}, u32[]{:S(2)}, u32[]{:S(2)}) collective-permute-start(bf16[128,256]{1,0:T(8,128)(2,1)S(1)} %get-tuple-element.70), channel_id=1, source_target_pairs={{0,1},{1,0},{2,3},{3,2},{4,5},{5,4},{6,7},{7,6},{8,9},{9,8},{10,11... | collective-permute-start | bytes 196616 | tf_op jit(solution)/shard_map/ppermute | solution.py:23
  36.3 1.6 %collective-permute-start.17 = (bf16[128,256]{1,0:T(8,128)(2,1)S(1)}, bf16[128,256]{1,0:T(8,128)(2,1)S(1)}, u32[]{:S(2)}, u32[]{:S(2)}) collective-permute-start(bf16[128,256]{1,0:T(8,128)(2,1)S(1)} %get-tuple-element.71), channel_id=1, source_target_pairs={{0,1},{1,0},{2,3},{3,2},{4,5},{5,4},{6,7},{7,6},{8,9},{9,8},{10,11... | collective-permute-start | bytes 196616 | tf_op jit(solution)/shard_map/ppermute | solution.py:23
  37.0 1.3 %collective-permute-start.18 = (bf16[128,256]{1,0:T(8,128)(2,1)S(1)}, bf16[128,256]{1,0:T(8,128)(2,1)S(1)}, u32[]{:S(2)}, u32[]{:S(2)}) collective-permute-start(bf16[128,256]{1,0:T(8,128)(2,1)S(1)} %get-tuple-element.72), channel_id=1, source_target_pairs={{0,1},{1,0},{2,3},{3,2},{4,5},{5,4},{6,7},{7,6},{8,9},{9,8},{10,11... | collective-permute-start | bytes 196616 | tf_op jit(solution)/shard_map/ppermute | solution.py:23
  37.2 13.7 %collective-permute-start.22 = (bf16[64,1024]{1,0:T(8,128)(2,1)S(1)}, bf16[64,1024]{1,0:T(8,128)(2,1)S(1)}, u32[]{:S(2)}, u32[]{:S(2)}) collective-permute-start(bf16[64,1024]{1,0:T(8,128)(2,1)S(1)} %after.23), channel_id=1, source_target_pairs={{0,12},{4,0},{8,4},{12,8},{1,13},{5,1},{9,5},{13,9},{2,14},{6,2},{... | collective-permute-start | bytes 393224 | tf_op jit(solution)/shard_map/ppermute | solution.py:23
  37.9 2.1 %collective-permute-start.19 = (bf16[128,256]{1,0:T(8,128)(2,1)S(1)}, bf16[128,256]{1,0:T(8,128)(2,1)S(1)}, u32[]{:S(2)}, u32[]{:S(2)}) collective-permute-start(bf16[128,256]{1,0:T(8,128)(2,1)S(1)} %get-tuple-element.73), channel_id=1, source_target_pairs={{0,1},{1,0},{2,3},{3,2},{4,5},{5,4},{6,7},{7,6},{8,9},{9,8},{10,11... | collective-permute-start | bytes 196616 | tf_op jit(solution)/shard_map/ppermute | solution.py:23
  38.3 12.6 %collective-permute-start.24 = (bf16[32,1024]{1,0:T(8,128)(2,1)S(1)}, bf16[32,1024]{1,0:T(8,128)(2,1)S(1)}, u32[]{:S(2)}, u32[]{:S(2)}) collective-permute-start(bf16[32,1024]{1,0:T(8,128)(2,1)S(1)} %after.25), channel_id=1, source_target_pairs={{0,12},{4,0},{8,4},{12,8},{1,13},{5,1},{9,5},{13,9},{2,14},{6,2},{... | collective-permute-start | bytes 196616 | tf_op jit(solution)/shard_map/ppermute | solution.py:23
  40.1 19.1 %slice-start = ((s8[8388608]{0:T(1024)(128)(4,1)}), s8[4194304]{0:T(1024)(128)(4,1)S(1)}, s32[]{:S(2)}) async-start(s8[8388608]{0:T(1024)(128)(4,1)} %bitcast.8), calls=%async_computation | async-start | bytes 8388608
  40.1 5.4 %copy-start.4 = (bf16[128,1024]{1,0:T(8,128)(2,1)S(1)}, bf16[128,1024]{1,0:T(8,128)(2,1)}, u32[]{:S(2)}) copy-start(bf16[128,1024]{1,0:T(8,128)(2,1)} %get-tuple-element.83.refs_0_) | copy-start | bytes 786436
  40.1 19.1 %slice-start.1 = ((s8[8388608]{0:T(1024)(128)(4,1)}), s8[4194304]{0:T(1024)(128)(4,1)S(1)}, s32[]{:S(2)}) async-start(s8[8388608]{0:T(1024)(128)(4,1)} %bitcast.8), calls=%async_computation.1 | async-start | bytes 8388608
  46.3 24.7 %collective-permute-start.28 = (bf16[256,1024]{1,0:T(8,128)(2,1)}, bf16[256,1024]{1,0:T(8,128)(2,1)}, u32[]{:S(2)}, u32[]{:S(2)}) collective-permute-start(bf16[256,1024]{1,0:T(8,128)(2,1)} %stack.3), channel_id=1, source_target_pairs={{0,4},{4,0},{8,12},{12,8},{1,5},{5,1},{9,13},{13,9},{2,6},{6,2},{1... | collective-permute-start | bytes 1572872 | tf_op jit(solution)/shard_map/ppermute | solution.py:27
  49.4 29.9 %collective-permute-start.20 = (bf16[2048,256]{1,0:T(8,128)(2,1)S(1)}, bf16[2048,256]{1,0:T(8,128)(2,1)}, u32[]{:S(2)}, u32[]{:S(2)}) collective-permute-start(bf16[2048,256]{1,0:T(8,128)(2,1)S(1)} %fetched_weights.1.refs_18_.refs_2_.refs_5_), channel_id=1, source_target_pairs={{0,2},{2,0},{1,3},{3,1},{4,6},{6,4},{5,7},{7,5},{8,10},{10,8},{9,1... | collective-permute-start | bytes 3145736 | tf_op jit(solution)/shard_map/ppermute | solution.py:23
  50.9 14.9 %copy-start.6 = (bf16[32,1024]{1,0:T(8,128)(2,1)}, bf16[32,1024]{1,0:T(8,128)(2,1)S(1)}, u32[]{:S(2)}) copy-start(bf16[32,1024]{1,0:T(8,128)(2,1)S(1)} %collective-permute-done.24.refs_0_.refs_4_) | copy-start | bytes 196612
  50.9 8.2 %copy-start.2 = (bf16[256,1024]{1,0:T(8,128)(2,1)}, bf16[256,1024]{1,0:T(8,128)(2,1)S(1)}, u32[]{:S(2)}) copy-start(bf16[256,1024]{1,0:T(8,128)(2,1)S(1)} %collective-permute-done.21.refs_0_.refs_1_) | copy-start | bytes 1572868
  50.9 26.0 %collective-permute-start.33 = (bf16[256,1024]{1,0:T(8,128)(2,1)}, bf16[256,1024]{1,0:T(8,128)(2,1)}, u32[]{:S(2)}, u32[]{:S(2)}) collective-permute-start(bf16[256,1024]{1,0:T(8,128)(2,1)} %after.32), channel_id=1, source_target_pairs={{0,8},{4,12},{8,0},{12,4},{1,9},{5,13},{9,1},{13,5},{2,10},{6,14},... | collective-permute-start | bytes 1572872 | tf_op jit(solution)/shard_map/ppermute | solution.py:23
  54.3 3.6 %collective-permute-start.26 = (s32[8,128]{1,0:T(8,128)S(1)}, s32[8,128]{1,0:T(8,128)S(1)}, u32[]{:S(2)}, u32[]{:S(2)}) collective-permute-start(s32[8,128]{1,0:T(8,128)S(1)} %get-tuple-element.57.refs_10_), channel_id=1, source_target_pairs={{0,16},{16,0},{1,17},{17,1},{2,18},{18,2},{3,19},{19,3},{4,20},{20... | collective-permute-start | bytes 12296 | tf_op jit(solution)/shard_map/ppermute | solution.py:23
  59.2 6.6 %copy-start.18 = (bf16[128,1024]{1,0:T(8,128)(2,1)S(1)}, bf16[128,1024]{1,0:T(8,128)(2,1)}, u32[]{:S(2)}) copy-start(bf16[128,1024]{1,0:T(8,128)(2,1)} %get-tuple-element.81.refs_0_) | copy-start | bytes 786436
  66.1 1.8 %collective-permute-start.29 = (bf16[128,1024]{1,0:T(8,128)(2,1)}, bf16[128,1024]{1,0:T(8,128)(2,1)S(1)}, u32[]{:S(2)}, u32[]{:S(2)}) collective-permute-start(bf16[128,1024]{1,0:T(8,128)(2,1)} %get-tuple-element.83.refs_0_), channel_id=1, source_target_pairs={{0,1},{1,0},{2,3},{3,2},{4,5},{5,4},{6,7},{7,6},{8,9},{9,8},{10,11... | collective-permute-start | bytes 786440 | tf_op jit(solution)/shard_map/ppermute | solution.py:23
  66.2 1.9 %collective-permute-start.30 = (bf16[128,1024]{1,0:T(8,128)(2,1)S(1)}, bf16[128,1024]{1,0:T(8,128)(2,1)S(1)}, u32[]{:S(2)}, u32[]{:S(2)}) collective-permute-start(bf16[128,1024]{1,0:T(8,128)(2,1)S(1)} %after.29.refs_1_), channel_id=1, source_target_pairs={{0,1},{1,0},{2,3},{3,2},{4,5},{5,4},{6,7},{7,6},{8,9},{9,8},{10,11... | collective-permute-start | bytes 786440 | tf_op jit(solution)/shard_map/ppermute | solution.py:23
  67.9 3.1 %collective-permute-start.23 = (bf16[64,1024]{1,0:T(8,128)(2,1)S(1)}, bf16[64,1024]{1,0:T(8,128)(2,1)S(1)}, u32[]{:S(2)}, u32[]{:S(2)}) collective-permute-start(bf16[64,1024]{1,0:T(8,128)(2,1)S(1)} %after.24.refs_0_), channel_id=1, source_target_pairs={{0,1},{1,0},{2,3},{3,2},{4,5},{5,4},{6,7},{7,6},{8,9},{9,8},{10,11... | collective-permute-start | bytes 393224 | tf_op jit(solution)/shard_map/ppermute | solution.py:23
  68.0 2.9 %collective-permute-start.25 = (bf16[32,1024]{1,0:T(8,128)(2,1)S(1)}, bf16[32,1024]{1,0:T(8,128)(2,1)S(1)}, u32[]{:S(2)}, u32[]{:S(2)}) collective-permute-start(bf16[32,1024]{1,0:T(8,128)(2,1)S(1)} %after.26.refs_2_), channel_id=1, source_target_pairs={{0,1},{1,0},{2,3},{3,2},{4,5},{5,4},{6,7},{7,6},{8,9},{9,8},{10,11... | collective-permute-start | bytes 196616 | tf_op jit(solution)/shard_map/ppermute | solution.py:23
  71.0 1.2 %collective-permute-start.31 = (s32[8,128]{1,0:T(8,128)S(1)}, s32[8,128]{1,0:T(8,128)S(1)}, u32[]{:S(2)}, u32[]{:S(2)}) collective-permute-start(s32[8,128]{1,0:T(8,128)S(1)} %after.30), channel_id=1, source_target_pairs={{0,1},{1,0},{2,3},{3,2},{4,5},{5,4},{6,7},{7,6},{8,9},{9,8},{10,11... | collective-permute-start | bytes 12296 | tf_op jit(solution)/shard_map/ppermute | solution.py:23
  71.4 7.9 %collective-permute-start.35 = (bf16[256,1024]{1,0:T(8,128)(2,1)}, bf16[256,1024]{1,0:T(8,128)(2,1)S(1)}, u32[]{:S(2)}, u32[]{:S(2)}) collective-permute-start(bf16[256,1024]{1,0:T(8,128)(2,1)} %after.34.refs_9_), channel_id=1, source_target_pairs={{0,1},{1,0},{2,3},{3,2},{4,5},{5,4},{6,7},{7,6},{8,9},{9,8},{10,11... | collective-permute-start | bytes 1572872 | tf_op jit(solution)/shard_map/ppermute | solution.py:23
  72.3 7.2 %collective-permute-start.32 = (bf16[256,1024]{1,0:T(8,128)(2,1)S(1)}, bf16[256,1024]{1,0:T(8,128)(2,1)S(1)}, u32[]{:S(2)}, u32[]{:S(2)}) collective-permute-start(bf16[256,1024]{1,0:T(8,128)(2,1)S(1)} %after.31.refs_3_), channel_id=1, source_target_pairs={{0,1},{1,0},{2,3},{3,2},{4,5},{5,4},{6,7},{7,6},{8,9},{9,8},{10,11... | collective-permute-start | bytes 1572872 | tf_op jit(solution)/shard_map/ppermute | solution.py:23
  76.9 2.5 %collective-permute-start.34 = (bf16[256,1024]{1,0:T(8,128)(2,1)}, bf16[256,1024]{1,0:T(8,128)(2,1)S(1)}, u32[]{:S(2)}, u32[]{:S(2)}) collective-permute-start(bf16[256,1024]{1,0:T(8,128)(2,1)} %after.33.refs_5_), channel_id=1, source_target_pairs={{0,1},{1,0},{2,3},{3,2},{4,5},{5,4},{6,7},{7,6},{8,9},{9,8},{10,11... | collective-permute-start | bytes 1572872 | tf_op jit(solution)/shard_map/ppermute | solution.py:23
  76.9 7.7 %collective-permute-start.37 = (bf16[64,1024]{1,0:T(8,128)(2,1)S(1)}, bf16[64,1024]{1,0:T(8,128)(2,1)S(1)}, u32[]{:S(2)}, u32[]{:S(2)}) collective-permute-start(bf16[64,1024]{1,0:T(8,128)(2,1)S(1)} %after.20.refs_3_), channel_id=1, source_target_pairs={{0,12},{4,0},{8,4},{12,8},{1,13},{5,1},{9,5},{13,9},{2,14},{6,2},{... | collective-permute-start | bytes 393224 | tf_op jit(solution)/shard_map/ppermute | solution.py:23
  79.3 6.0 %collective-permute-start.39 = (bf16[48,1024]{1,0:T(8,128)(2,1)S(1)}, bf16[48,1024]{1,0:T(8,128)(2,1)S(1)}, u32[]{:S(2)}, u32[]{:S(2)}) collective-permute-start(bf16[48,1024]{1,0:T(8,128)(2,1)S(1)} %after.21.refs_4_), channel_id=1, source_target_pairs={{0,12},{4,0},{8,4},{12,8},{1,13},{5,1},{9,5},{13,9},{2,14},{6,2},{... | collective-permute-start | bytes 294920 | tf_op jit(solution)/shard_map/ppermute | solution.py:23
  79.3 7.7 %collective-permute-start.41 = (bf16[48,1024]{1,0:T(8,128)(2,1)S(1)}, bf16[48,1024]{1,0:T(8,128)(2,1)S(1)}, u32[]{:S(2)}, u32[]{:S(2)}) collective-permute-start(bf16[48,1024]{1,0:T(8,128)(2,1)S(1)} %after.22.refs_5_), channel_id=1, source_target_pairs={{0,12},{4,0},{8,4},{12,8},{1,13},{5,1},{9,5},{13,9},{2,14},{6,2},{... | collective-permute-start | bytes 294920 | tf_op jit(solution)/shard_map/ppermute | solution.py:23
  83.6 9.9 %collective-permute-start.36 = (bf16[1024,128]{1,0:T(8,128)(2,1)S(1)}, bf16[1024,128]{1,0:T(8,128)(2,1)S(1)}, u32[]{:S(2)}, u32[]{:S(2)}) collective-permute-start(bf16[1024,128]{1,0:T(8,128)(2,1)S(1)} %get-tuple-element.90.refs_1_), channel_id=1, source_target_pairs={{0,2},{2,0},{1,3},{3,1},{4,6},{6,4},{5,7},{7,5},{8,10},{10,8},{9,1... | collective-permute-start | bytes 786440 | tf_op jit(solution)/shard_map/ppermute | solution.py:23
  84.6 3.8 %collective-permute-start.38 = (bf16[64,1024]{1,0:T(8,128)(2,1)S(1)}, bf16[64,1024]{1,0:T(8,128)(2,1)S(1)}, u32[]{:S(2)}, u32[]{:S(2)}) collective-permute-start(bf16[64,1024]{1,0:T(8,128)(2,1)S(1)} %after.35.refs_4_), channel_id=1, source_target_pairs={{0,1},{1,0},{2,3},{3,2},{4,5},{5,4},{6,7},{7,6},{8,9},{9,8},{10,11... | collective-permute-start | bytes 393224 | tf_op jit(solution)/shard_map/ppermute | solution.py:23
  85.3 1.7 %collective-permute-start.40 = (bf16[48,1024]{1,0:T(8,128)(2,1)S(1)}, bf16[48,1024]{1,0:T(8,128)(2,1)S(1)}, u32[]{:S(2)}, u32[]{:S(2)}) collective-permute-start(bf16[48,1024]{1,0:T(8,128)(2,1)S(1)} %after.36.refs_6_), channel_id=1, source_target_pairs={{0,1},{1,0},{2,3},{3,2},{4,5},{5,4},{6,7},{7,6},{8,9},{9,8},{10,11... | collective-permute-start | bytes 294920 | tf_op jit(solution)/shard_map/ppermute | solution.py:23
  87.0 1.3 %collective-permute-start.42 = (bf16[48,1024]{1,0:T(8,128)(2,1)S(1)}, bf16[48,1024]{1,0:T(8,128)(2,1)S(1)}, u32[]{:S(2)}, u32[]{:S(2)}) collective-permute-start(bf16[48,1024]{1,0:T(8,128)(2,1)S(1)} %after.37.refs_8_), channel_id=1, source_target_pairs={{0,1},{1,0},{2,3},{3,2},{4,5},{5,4},{6,7},{7,6},{8,9},{9,8},{10,11... | collective-permute-start | bytes 294920 | tf_op jit(solution)/shard_map/ppermute | solution.py:23
  89.1 4.4 %collective-permute-start.43 = (bf16[256,128]{1,0:T(8,128)(2,1)S(1)}, bf16[256,128]{1,0:T(8,128)(2,1)S(1)}, u32[]{:S(2)}, u32[]{:S(2)}) collective-permute-start(bf16[256,128]{1,0:T(8,128)(2,1)S(1)} %get-tuple-element.93), channel_id=1, source_target_pairs={{0,2},{2,0},{1,3},{3,1},{4,6},{6,4},{5,7},{7,5},{8,10},{10,8},{9,1... | collective-permute-start | bytes 196616 | tf_op jit(solution)/shard_map/ppermute | solution.py:23
  (13 other events, 32.6 us)

commit v19 on v18

--- a/solution.py
+++ b/solution.py
@@ -611,7 +611,7 @@
 
     middle = [(d, 0, bulk) for d in range(1, last_hops)]
     fillers = 2 if bulk % 256 == 0 else 1
-    sizes = [n * bulk // 16 for n in ((4, 2, 4, 3, 3) if bulk % 256 == 0 else (8, 8))]
+    sizes = [n * bulk // 16 for n in ((3, 2, 4, 4, 3) if bulk % 256 == 0 else (8, 8))]
     final = [(last_hops, sum(sizes[:j]), n) for j, n in enumerate(sizes)]
     *packed, goal = pack_rows(train, ids, columns, bulk, extra, middle + final)
     firsts, seconds = [], []

time: 95.4 us -> 94.6 us (level)
  waiting for transfers between devices: 20.4 us -> 17.8 us
  starting transfers between devices: 36.7 us -> 37.9 us
    ppermute x38, waiting for transfers between devices: 17.3 us -> 14.8 us  [shift(): return lax.ppermute(x, axis, [(i, (i + by) % size) for i in range(size)])]
    ppermute x38, starting transfers between devices: 31.9 us -> 33.8 us  [shift(): return lax.ppermute(x, axis, [(i, (i + by) % size) for i in range(size)])]
  transfers between devices with their start and end apart: 40 -> 40, of which waited for: 12 -> 13; matrix products, arithmetic and copies ran while one was open for 1% -> 1% of each run, Pallas kernels for 33% -> 33%
where the time goes in v19:
time: 94.6 us; the launch traced here: 94.3 us
  starting transfers between devices  37.9 us (40%)
  Pallas kernels  32.7 us (35%)
  waiting for transfers between devices  17.8 us (19%)
  local copies, waits for them, and re-layouts  4.79 us (5%)
  between operations  1.03 us (1%)
    ppermute x38, starting transfers between devices, shift(): return lax.ppermute(x, axis, [(i, (i + by) % size) for i in range(size)])  33.8 us
    ppermute x38, waiting for transfers between devices, shift(): return lax.ppermute(x, axis, [(i, (i + by) % size) for i in range(size)])  14.8 us
    pallas_call x1, Pallas kernels, pack_rows(): pl.pallas_call(kernel, grid=(1,), in_specs=[pl.BlockSpec((lines, LANES),...  6.6 us
    pallas_call x1, Pallas kernels, partial_weights(): pl.pallas_call(kernel, in_specs=[SMEM] + [HBM] * n + [VMEM] * (CUTS * n)...  6.6 us
    unnamed x42, local copies, waits for them, and re-layouts  4.3 us
    pallas_call x1, Pallas kernels, early_scores(): pl.pallas_call(kernel, in_specs=[SMEM] + [VMEM] * (2 + n_other + n_rep *...  4.16 us
    ppermute x2, starting transfers between devices, swap(): return lax.ppermute(x, axis, [(i, i ^ bit) for i in range(size)])  4.05 us
    ppermute x2, waiting for transfers between devices, swap(): return lax.ppermute(x, axis, [(i, i ^ bit) for i in range(size)])  2.93 us
  transfers between devices with their start and end apart: 40, of which 13 were waited for; matrix products, arithmetic and copies ran while one was open for 1% of the time, Pallas kernels for 33%

profile of v19, /device:TPU:0, one launch (start us, length us, event | category | flops | bytes accessed | tf_op | source)
XLA Modules:
  0.0 94.3 jit_solution(9832843509790441765)
XLA Ops:
  0.5 2.7 %pick_queries.1 = (bf16[1,64,1024]{2,1,0:T(8,128)(2,1)}, bf16[1,64,1024]{2,1,0:T(8,128)(2,1)}, bf16[1,64,1024]{2,1,0:T(8,128)(2,1)}, bf16[1,64,1024]{2,1,0:T(8,128)(2,1)}) custom-call(s32[4,4]{1,0:T(4,128)} %pattern_ref.3, s32[16]{0:T(128)} %slot_ref.3, bf16[4,128,1024]{2,1,0:T(8,128)(2,1)} %in_ref.1), custom_call_target="tpu_custom_call" | custom-call | flops 1 | bytes 1 | tf_op jit(solution)/shard_map/pick_queries/pallas_call | solution.py:109
  3.1 2.8 %collective-permute-start.4 = (bf16[1,64,1024]{2,1,0:T(8,128)(2,1)}, bf16[1,64,1024]{2,1,0:T(8,128)(2,1)S(1)}, u32[]{:S(2)}, u32[]{:S(2)}) collective-permute-start(bf16[1,64,1024]{2,1,0:T(8,128)(2,1)} %get-tuple-element.50), channel_id=1, source_target_pairs={{0,4},{4,8},{8,12},{12,0},{1,5},{5,9},{9,13},{13,1},{2,6},{6,10},{... | collective-permute-start | bytes 393224 | tf_op jit(solution)/shard_map/ppermute | solution.py:23
  5.9 2.6 %collective-permute-start.5 = (bf16[1,64,1024]{2,1,0:T(8,128)(2,1)}, bf16[1,64,1024]{2,1,0:T(8,128)(2,1)S(1)}, u32[]{:S(2)}, u32[]{:S(2)}) collective-permute-start(bf16[1,64,1024]{2,1,0:T(8,128)(2,1)} %get-tuple-element.51), channel_id=1, source_target_pairs={{0,8},{4,12},{8,0},{12,4},{1,9},{5,13},{9,1},{13,5},{2,10},{6,14},... | collective-permute-start | bytes 393224 | tf_op jit(solution)/shard_map/ppermute | solution.py:23
  8.5 1.3 %collective-permute-start.6 = (bf16[1,64,1024]{2,1,0:T(8,128)(2,1)}, bf16[1,64,1024]{2,1,0:T(8,128)(2,1)S(1)}, u32[]{:S(2)}, u32[]{:S(2)}) collective-permute-start(bf16[1,64,1024]{2,1,0:T(8,128)(2,1)} %get-tuple-element.52), channel_id=1, source_target_pairs={{0,12},{4,0},{8,4},{12,8},{1,13},{5,1},{9,5},{13,9},{2,14},{6,2},{... | collective-permute-start | bytes 393224 | tf_op jit(solution)/shard_map/ppermute | solution.py:23
  9.8 1.5 %collective-permute-start.8 = (bf16[1,64,1024]{2,1,0:T(8,128)(2,1)}, bf16[1,64,1024]{2,1,0:T(8,128)(2,1)S(1)}, u32[]{:S(2)}, u32[]{:S(2)}) collective-permute-start(bf16[1,64,1024]{2,1,0:T(8,128)(2,1)} %get-tuple-element.54.refs_0_), channel_id=1, source_target_pairs={{0,16},{16,0},{1,17},{17,1},{2,18},{18,2},{3,19},{19,3},{4,20},{20... | collective-permute-start | bytes 393224 | tf_op jit(solution)/shard_map/ppermute | solution.py:23
  11.4 6.6 %pack_rows.1 = (bf16[256,1024]{1,0:T(8,128)(2,1)}, bf16[256,1024]{1,0:T(8,128)(2,1)}, bf16[48,1024]{1,0:T(8,128)(2,1)}, bf16[32,1024]{1,0:T(8,128)(2,1)}, bf16[6...) custom-call(s32[32,128]{1,0:T(8,128)} %bitcast.11, ...), custom_call_target="tpu_custom_call" | custom-call | flops 1 | bytes 1 | tf_op jit(solution)/shard_map/pack_rows/pallas_call | solution.py:253
  18.0 3.2 %collective-permute-start.21 = (bf16[256,1024]{1,0:T(8,128)(2,1)}, bf16[256,1024]{1,0:T(8,128)(2,1)S(1)}, u32[]{:S(2)}, u32[]{:S(2)}) collective-permute-start(bf16[256,1024]{1,0:T(8,128)(2,1)} %after.19), channel_id=1, source_target_pairs={{0,4},{4,8},{8,12},{12,0},{1,5},{5,9},{9,13},{13,1},{2,6},{6,10},{... | collective-permute-start | bytes 1572872 | tf_op jit(solution)/shard_map/ppermute | solution.py:23
  21.2 1.5 %collective-permute-start.9 = (bf16[1,64,1024]{2,1,0:T(8,128)(2,1)S(1)}, bf16[1,64,1024]{2,1,0:T(8,128)(2,1)S(1)}, u32[]{:S(2)}, u32[]{:S(2)}) collective-permute-start(bf16[1,64,1024]{2,1,0:T(8,128)(2,1)S(1)} %collective-permute-done.4.rest_0_.refs_2_.refs_1_), channel_id=1, source_target_pairs={{0,16},{16,0},{1,17},{17,1},{2,18},{18,2},{3,19},{19,3},{4,20},{20... | collective-permute-start | bytes 393224 | tf_op jit(solution)/shard_map/ppermute | solution.py:23
  22.7 0.5 collective-permute-start.10
  23.2 1.5 %collective-permute-start.11 = (bf16[1,64,1024]{2,1,0:T(8,128)(2,1)S(1)}, bf16[1,64,1024]{2,1,0:T(8,128)(2,1)S(1)}, u32[]{:S(2)}, u32[]{:S(2)}) collective-permute-start(bf16[1,64,1024]{2,1,0:T(8,128)(2,1)S(1)} %collective-permute-done.6.rest_2_.refs_4_.refs_3_), channel_id=1, source_target_pairs={{0,16},{16,0},{1,17},{17,1},{2,18},{18,2},{3,19},{19,3},{4,20},{20... | collective-permute-start | bytes 393224 | tf_op jit(solution)/shard_map/ppermute | solution.py:23
  24.7 1.6 %collective-permute-start.27 = (bf16[128,1024]{1,0:T(8,128)(2,1)}, bf16[128,1024]{1,0:T(8,128)(2,1)S(1)}, u32[]{:S(2)}, u32[]{:S(2)}) collective-permute-start(bf16[128,1024]{1,0:T(8,128)(2,1)} %after.28), channel_id=1, source_target_pairs={{0,8},{4,12},{8,0},{12,4},{1,9},{5,13},{9,1},{13,5},{2,10},{6,14},... | collective-permute-start | bytes 786440 | tf_op jit(solution)/shard_map/ppermute | solution.py:27
  26.3 0.8 row_table.1
  27.2 3.4 %copy-done = bf16[1,4096,1024]{2,1,0:T(8,128)(2,1)S(1)} copy-done((bf16[1,4096,1024]{2,1,0:T(8,128)(2,1)S(1)}, bf16[1,4096,1024]{2,1,0:T(8,128)(2,1)}, u32[]{:S(2)}) %copy-start) | copy-done | bytes 8388632
  30.6 2.5 %fetch.1 = (bf16[2048,1024]{1,0:T(8,128)(2,1)S(1)}, bf16[2048,1024]{1,0:T(8,128)(2,1)S(1)}) custom-call(s32[1]{0:T(128)} %bitcast.3.block_ref, bf16[4096,1024]{1,0:T(8,128)(2,1)S(1)} %bitcast.7, bf16[4096,1024]{1,0:T(8,128)(2,1)} %collective-permute-done.7.refs_1_, bf16[1,64,1024]{2,1,0:T(8,128)(2,1)S(1)} %collective-permute-done.4.rest_0_.refs_2_.refs_1_, ...), custom_call_target="tpu_custom_call" | custom-call | flops 1 | bytes 1 | tf_op jit(solution)/shard_map/fetch/pallas_call | solution.py:326
  33.2 1.2 %join_queries.1 = (bf16[128,256]{1,0:T(8,128)(2,1)S(1)}, bf16[128,256]{1,0:T(8,128)(2,1)S(1)}, bf16[128,256]{1,0:T(8,128)(2,1)S(1)}, bf16[128,256]{1,0:T(8,128)(...) custom-call(s32[4,4]{1,0:T(4,128)S(1)} %copy-done.15, ...), custom_call_target="tpu_custom_call" | custom-call | flops 1 | bytes 1 | tf_op jit(solution)/shard_map/join_queries/pallas_call | solution.py:154
  34.5 0.5 collective-permute-start.13
  35.1 0.7 collective-permute-done.12.refs_10_
  36.4 0.6 collective-permute-done.15.refs_13_
  37.5 0.7 collective-permute-start.22
  38.3 2.0 %collective-permute-start.24 = (bf16[32,1024]{1,0:T(8,128)(2,1)S(1)}, bf16[32,1024]{1,0:T(8,128)(2,1)S(1)}, u32[]{:S(2)}, u32[]{:S(2)}) collective-permute-start(bf16[32,1024]{1,0:T(8,128)(2,1)S(1)} %after.25), channel_id=1, source_target_pairs={{0,12},{4,0},{8,4},{12,8},{1,13},{5,1},{9,5},{13,9},{2,14},{6,2},{... | collective-permute-start | bytes 196616 | tf_op jit(solution)/shard_map/ppermute | solution.py:23
  40.3 2.3 %fetched_weights.1.refs_18_.refs_2_.refs_5_ = bf16[2048,256]{1,0:T(8,128)(2,1)S(1)} custom-call(bf16[2048,1024]{1,0:T(8,128)(2,1)S(1)} %get-tuple-element.55.refs_8_.refs_0_, bf16[2048,1024]{1,0:T(8,128)(2,1)S(1)} %get-tuple-element.56.refs_9_.refs_1_, bf16[128,256]{1,0:T(8,128)(2,1)S(1)} %get-tuple-element.58.refs_2_, ...), custom_call_target="tpu_custom_call" | custom-call | flops 1 | bytes 1 | tf_op jit(solution)/shard_map/fetched_weights/pallas_call | solution.py:353
  42.7 1.6 %collective-permute-start.20 = (bf16[2048,256]{1,0:T(8,128)(2,1)S(1)}, bf16[2048,256]{1,0:T(8,128)(2,1)}, u32[]{:S(2)}, u32[]{:S(2)}) collective-permute-start(bf16[2048,256]{1,0:T(8,128)(2,1)S(1)} %fetched_weights.1.refs_18_.refs_2_.refs_5_), channel_id=1, source_target_pairs={{0,2},{2,0},{1,3},{3,1},{4,6},{6,4},{5,7},{7,5},{8,10},{10,8},{9,1... | collective-permute-start | bytes 3145736 | tf_op jit(solution)/shard_map/ppermute | solution.py:23
  44.2 1.2 %collective-permute-done.27.refs_1_.refs_0_.refs_2_ = bf16[128,1024]{1,0:T(8,128)(2,1)S(1)} collective-permute-done((bf16[128,1024]{1,0:T(8,128)(2,1)}, bf16[128,1024]{1,0:T(8,128)(2,1)S(1)}, u32[]{:S(2)}, u32[]{:S(2)}) %collective-permute-start.27) | collective-permute-done | bytes 262176 | tf_op jit(solution)/shard_map/ppermute | solution.py:27
  45.5 0.8 stack.3
  46.3 2.4 %collective-permute-start.28 = (bf16[256,1024]{1,0:T(8,128)(2,1)}, bf16[256,1024]{1,0:T(8,128)(2,1)}, u32[]{:S(2)}, u32[]{:S(2)}) collective-permute-start(bf16[256,1024]{1,0:T(8,128)(2,1)} %stack.3), channel_id=1, source_target_pairs={{0,4},{4,0},{8,12},{12,8},{1,5},{5,1},{9,13},{13,9},{2,6},{6,2},{1... | collective-permute-start | bytes 1572872 | tf_op jit(solution)/shard_map/ppermute | solution.py:27
  48.9 3.2 %collective-permute-start.33 = (bf16[256,1024]{1,0:T(8,128)(2,1)}, bf16[256,1024]{1,0:T(8,128)(2,1)}, u32[]{:S(2)}, u32[]{:S(2)}) collective-permute-start(bf16[256,1024]{1,0:T(8,128)(2,1)} %after.32), channel_id=1, source_target_pairs={{0,8},{4,12},{8,0},{12,4},{1,9},{5,13},{9,1},{13,5},{2,10},{6,14},... | collective-permute-start | bytes 1572872 | tf_op jit(solution)/shard_map/ppermute | solution.py:23
  52.1 1.5 %collective-permute-start.26 = (s32[8,128]{1,0:T(8,128)S(1)}, s32[8,128]{1,0:T(8,128)S(1)}, u32[]{:S(2)}, u32[]{:S(2)}) collective-permute-start(s32[8,128]{1,0:T(8,128)S(1)} %get-tuple-element.57.refs_10_), channel_id=1, source_target_pairs={{0,16},{16,0},{1,17},{17,1},{2,18},{18,2},{3,19},{19,3},{4,20},{20... | collective-permute-start | bytes 12296 | tf_op jit(solution)/shard_map/ppermute | solution.py:23
  53.6 2.1 %collective-permute-done.26 = s32[8,128]{1,0:T(8,128)S(1)} collective-permute-done((s32[8,128]{1,0:T(8,128)S(1)}, s32[8,128]{1,0:T(8,128)S(1)}, u32[]{:S(2)}, u32[]{:S(2)}) %collective-permute-start.26) | collective-permute-done | bytes 4128 | tf_op jit(solution)/shard_map/ppermute | solution.py:23
  55.7 0.5 slice.3
  56.8 6.6 %partial_weights.1.rest_0_.refs_1_.refs_2_.refs_0_ = f32[2048,256]{1,0:T(8,128)S(1)} custom-call(s32[1]{0:T(128)} %bitcast.1.block_ref, bf16[4096,1024]{1,0:T(8,128)(2,1)S(1)} %bitcast.10, bf16[4096,1024]{1,0:T(8,128)(2,1)} %collective-permute-done.7.refs_1_, bf16[128,256]{1,0:T(8,128)(2,1)S(1)} %get-tuple-element.58.refs_2_, ...), custom_call_target="tpu_custom_call" | custom-call | flops 1 | bytes 1 | tf_op jit(solution)/shard_map/partial_weights/pallas_call | solution.py:293
  64.2 1.2 %collective-permute-done.29.refs_0_ = bf16[128,1024]{1,0:T(8,128)(2,1)S(1)} collective-permute-done((bf16[128,1024]{1,0:T(8,128)(2,1)}, bf16[128,1024]{1,0:T(8,128)(2,1)S(1)}, u32[]{:S(2)}, u32[]{:S(2)}) %collective-permute-start.29) | collective-permute-done | bytes 262176 | tf_op jit(solution)/shard_map/ppermute | solution.py:23
  66.1 2.4 %own_rows.1.refs_2_ = bf16[256,2048]{1,0:T(8,128)(2,1)S(1)} custom-call(s32[8,128]{1,0:T(8,128)S(1)} %copy-done.16, bf16[1024,2048]{1,0:T(8,128)(2,1)S(1)} %copy-done.1, f32[2048,256]{1,0:T(8,128)S(1)} %partial_weights.1.rest_0_.refs_1_.refs_2_.refs_0_), custom_call_target="tpu_custom_call" | custom-call | flops 1 | bytes 1 | tf_op jit(solution)/shard_map/own_rows/pallas_call | solution.py:195
  68.5 0.8 copy-done.10
  69.4 1.7 %collective-permute-done.28.refs_9_.refs_0_ = bf16[256,1024]{1,0:T(8,128)(2,1)} collective-permute-done((bf16[256,1024]{1,0:T(8,128)(2,1)}, bf16[256,1024]{1,0:T(8,128)(2,1)}, u32[]{:S(2)}, u32[]{:S(2)}) %collective-permute-start.28) | collective-permute-done | bytes 524320 | tf_op jit(solution)/shard_map/ppermute | solution.py:27
  71.1 0.5 collective-permute-start.35
  71.6 0.7 collective-permute-done.31.refs_1_
  72.4 3.0 %collective-permute-done.33.refs_0_ = bf16[256,1024]{1,0:T(8,128)(2,1)} collective-permute-done((bf16[256,1024]{1,0:T(8,128)(2,1)}, bf16[256,1024]{1,0:T(8,128)(2,1)}, u32[]{:S(2)}, u32[]{:S(2)}) %collective-permute-start.33) | collective-permute-done | bytes 524320 | tf_op jit(solution)/shard_map/ppermute | solution.py:23
  75.4 2.0 %collective-permute-start.37 = (bf16[64,1024]{1,0:T(8,128)(2,1)S(1)}, bf16[64,1024]{1,0:T(8,128)(2,1)S(1)}, u32[]{:S(2)}, u32[]{:S(2)}) collective-permute-start(bf16[64,1024]{1,0:T(8,128)(2,1)S(1)} %after.20.refs_3_), channel_id=1, source_target_pairs={{0,12},{4,0},{8,4},{12,8},{1,13},{5,1},{9,5},{13,9},{2,14},{6,2},{... | collective-permute-start | bytes 393224 | tf_op jit(solution)/shard_map/ppermute | solution.py:23
  77.4 0.7 collective-permute-start.41
  78.2 4.2 %early_scores.1 = (bf16[2048,512]{1,0:T(8,128)(2,1)S(1)}, f32[1024,128]{1,0:T(8,128)S(1)}, bf16[1024,128]{1,0:T(8,128)(2,1)S(1)}) custom-call(s32[4,4]{1,0:T(4,128)S(1)} %get-tuple-element.53.table_ref, f32[2048,256]{1,0:T(8,128)S(1)} %partial_weights.1.rest_0_.refs_1_.refs_2_.refs_0_, bf16[2048,256]{1,0:T(8,128)(2,1)} %collective-permute-done.20.refs_1_, ...), custom_call_target="tpu_custom_call" | custom-call | flops 1 | bytes 1 | tf_op jit(solution)/shard_map/early_scores/pallas_call | solution.py:518
  82.3 1.6 %collective-permute-start.36 = (bf16[1024,128]{1,0:T(8,128)(2,1)S(1)}, bf16[1024,128]{1,0:T(8,128)(2,1)S(1)}, u32[]{:S(2)}, u32[]{:S(2)}) collective-permute-start(bf16[1024,128]{1,0:T(8,128)(2,1)S(1)} %get-tuple-element.90.refs_1_), channel_id=1, source_target_pairs={{0,2},{2,0},{1,3},{3,1},{4,6},{6,4},{5,7},{7,5},{8,10},{10,8},{9,1... | collective-permute-start | bytes 786440 | tf_op jit(solution)/shard_map/ppermute | solution.py:23
  83.9 0.6 collective-permute-done.39.refs_0_
  84.5 1.7 %collective-permute-done.41.refs_0_ = bf16[48,1024]{1,0:T(8,128)(2,1)S(1)} collective-permute-done((bf16[48,1024]{1,0:T(8,128)(2,1)S(1)}, bf16[48,1024]{1,0:T(8,128)(2,1)S(1)}, u32[]{:S(2)}, u32[]{:S(2)}) %collective-permute-start.41) | collective-permute-done | bytes 98336 | tf_op jit(solution)/shard_map/ppermute | solution.py:23
  86.2 1.3 %collective-permute-done.42.refs_9_ = bf16[48,1024]{1,0:T(8,128)(2,1)S(1)} collective-permute-done((bf16[48,1024]{1,0:T(8,128)(2,1)S(1)}, bf16[48,1024]{1,0:T(8,128)(2,1)S(1)}, u32[]{:S(2)}, u32[]{:S(2)}) %collective-permute-start.42) | collective-permute-done | bytes 98336 | tf_op jit(solution)/shard_map/ppermute | solution.py:23
  87.5 0.7 late_scores.1
  88.3 1.6 %collective-permute-start.43 = (bf16[256,128]{1,0:T(8,128)(2,1)S(1)}, bf16[256,128]{1,0:T(8,128)(2,1)S(1)}, u32[]{:S(2)}, u32[]{:S(2)}) collective-permute-start(bf16[256,128]{1,0:T(8,128)(2,1)S(1)} %get-tuple-element.93), channel_id=1, source_target_pairs={{0,2},{2,0},{1,3},{3,1},{4,6},{6,4},{5,7},{7,5},{8,10},{10,8},{9,1... | collective-permute-start | bytes 196616 | tf_op jit(solution)/shard_map/ppermute | solution.py:23
  89.8 2.8 %collective-permute-done.43.refs_3_ = bf16[256,128]{1,0:T(8,128)(2,1)S(1)} collective-permute-done((bf16[256,128]{1,0:T(8,128)(2,1)S(1)}, bf16[256,128]{1,0:T(8,128)(2,1)S(1)}, u32[]{:S(2)}, u32[]{:S(2)}) %collective-permute-start.43) | collective-permute-done | bytes 65568 | tf_op jit(solution)/shard_map/ppermute | solution.py:23
  92.6 1.7 %merge.1 = f32[128,1024]{1,0:T(8,128)} custom-call(s32[4,4]{1,0:T(4,128)S(1)} %get-tuple-element.53.table_ref, f32[1024,128]{1,0:T(8,128)S(1)} %get-tuple-element.89.refs_0_, bf16[1024,128]{1,0:T(8,128)(2,1)S(1)} %collective-permute-done.36.refs_1_, f32[256,128]{1,0:T(8,128)S(1)} %get-tuple-element.92.refs_2_, ...), custom_call_target="tpu_custom_call" | custom-call | flops 1 | bytes 1 | tf_op jit(solution)/shard_map/merge/pallas_call | solution.py:578
  (113 shorter events, 3.7 us)
Async XLA Ops:
  0.0 26.3 %copy-start.13 = (s32[4096]{0:T(1024)S(1)}, s32[4096]{0:T(1024)}, u32[]{:S(2)}) copy-start(s32[4096]{0:T(1024)} %param.9) | copy-start | bytes 49156
  0.0 24.7 %collective-permute-start.7 = (bf16[4096,1024]{1,0:T(8,128)(2,1)}, bf16[4096,1024]{1,0:T(8,128)(2,1)}, u32[]{:S(2)}, u32[]{:S(2)}) collective-permute-start(bf16[4096,1024]{1,0:T(8,128)(2,1)} %bitcast.6), channel_id=1, source_target_pairs={{0,1},{1,0},{2,3},{3,2},{4,5},{5,4},{6,7},{7,6},{8,9},{9,8},{10,11... | collective-permute-start | bytes 25165832 | tf_op jit(solution)/shard_map/ppermute | solution.py:23
  3.1 14.8 %collective-permute-start.4 = (bf16[1,64,1024]{2,1,0:T(8,128)(2,1)}, bf16[1,64,1024]{2,1,0:T(8,128)(2,1)S(1)}, u32[]{:S(2)}, u32[]{:S(2)}) collective-permute-start(bf16[1,64,1024]{2,1,0:T(8,128)(2,1)} %get-tuple-element.50), channel_id=1, source_target_pairs={{0,4},{4,8},{8,12},{12,0},{1,5},{5,9},{9,13},{13,1},{2,6},{6,10},{... | collective-permute-start | bytes 393224 | tf_op jit(solution)/shard_map/ppermute | solution.py:23
  5.9 12.1 %collective-permute-start.5 = (bf16[1,64,1024]{2,1,0:T(8,128)(2,1)}, bf16[1,64,1024]{2,1,0:T(8,128)(2,1)S(1)}, u32[]{:S(2)}, u32[]{:S(2)}) collective-permute-start(bf16[1,64,1024]{2,1,0:T(8,128)(2,1)} %get-tuple-element.51), channel_id=1, source_target_pairs={{0,8},{4,12},{8,0},{12,4},{1,9},{5,13},{9,1},{13,5},{2,10},{6,14},... | collective-permute-start | bytes 393224 | tf_op jit(solution)/shard_map/ppermute | solution.py:23
  8.5 9.5 %collective-permute-start.6 = (bf16[1,64,1024]{2,1,0:T(8,128)(2,1)}, bf16[1,64,1024]{2,1,0:T(8,128)(2,1)S(1)}, u32[]{:S(2)}, u32[]{:S(2)}) collective-permute-start(bf16[1,64,1024]{2,1,0:T(8,128)(2,1)} %get-tuple-element.52), channel_id=1, source_target_pairs={{0,12},{4,0},{8,4},{12,8},{1,13},{5,1},{9,5},{13,9},{2,14},{6,2},{... | collective-permute-start | bytes 393224 | tf_op jit(solution)/shard_map/ppermute | solution.py:23
  9.8 13.3 %collective-permute-start.8 = (bf16[1,64,1024]{2,1,0:T(8,128)(2,1)}, bf16[1,64,1024]{2,1,0:T(8,128)(2,1)S(1)}, u32[]{:S(2)}, u32[]{:S(2)}) collective-permute-start(bf16[1,64,1024]{2,1,0:T(8,128)(2,1)} %get-tuple-element.54.refs_0_), channel_id=1, source_target_pairs={{0,16},{16,0},{1,17},{17,1},{2,18},{18,2},{3,19},{19,3},{4,20},{20... | collective-permute-start | bytes 393224 | tf_op jit(solution)/shard_map/ppermute | solution.py:23
  18.0 30.8 %collective-permute-start.21 = (bf16[256,1024]{1,0:T(8,128)(2,1)}, bf16[256,1024]{1,0:T(8,128)(2,1)S(1)}, u32[]{:S(2)}, u32[]{:S(2)}) collective-permute-start(bf16[256,1024]{1,0:T(8,128)(2,1)} %after.19), channel_id=1, source_target_pairs={{0,4},{4,8},{8,12},{12,0},{1,5},{5,9},{9,13},{13,1},{2,6},{6,10},{... | collective-permute-start | bytes 1572872 | tf_op jit(solution)/shard_map/ppermute | solution.py:23
  21.2 12.0 %collective-permute-start.9 = (bf16[1,64,1024]{2,1,0:T(8,128)(2,1)S(1)}, bf16[1,64,1024]{2,1,0:T(8,128)(2,1)S(1)}, u32[]{:S(2)}, u32[]{:S(2)}) collective-permute-start(bf16[1,64,1024]{2,1,0:T(8,128)(2,1)S(1)} %collective-permute-done.4.rest_0_.refs_2_.refs_1_), channel_id=1, source_target_pairs={{0,16},{16,0},{1,17},{17,1},{2,18},{18,2},{3,19},{19,3},{4,20},{20... | collective-permute-start | bytes 393224 | tf_op jit(solution)/shard_map/ppermute | solution.py:23
  22.7 10.4 %collective-permute-start.10 = (bf16[1,64,1024]{2,1,0:T(8,128)(2,1)S(1)}, bf16[1,64,1024]{2,1,0:T(8,128)(2,1)S(1)}, u32[]{:S(2)}, u32[]{:S(2)}) collective-permute-start(bf16[1,64,1024]{2,1,0:T(8,128)(2,1)S(1)} %collective-permute-done.5.rest_1_.refs_3_.refs_2_), channel_id=1, source_target_pairs={{0,16},{16,0},{1,17},{17,1},{2,18},{18,2},{3,19},{19,3},{4,20},{20... | collective-permute-start | bytes 393224 | tf_op jit(solution)/shard_map/ppermute | solution.py:23
  23.2 9.9 %collective-permute-start.11 = (bf16[1,64,1024]{2,1,0:T(8,128)(2,1)S(1)}, bf16[1,64,1024]{2,1,0:T(8,128)(2,1)S(1)}, u32[]{:S(2)}, u32[]{:S(2)}) collective-permute-start(bf16[1,64,1024]{2,1,0:T(8,128)(2,1)S(1)} %collective-permute-done.6.rest_2_.refs_4_.refs_3_), channel_id=1, source_target_pairs={{0,16},{16,0},{1,17},{17,1},{2,18},{18,2},{3,19},{19,3},{4,20},{20... | collective-permute-start | bytes 393224 | tf_op jit(solution)/shard_map/ppermute | solution.py:23
  24.7 20.7 %collective-permute-start.27 = (bf16[128,1024]{1,0:T(8,128)(2,1)}, bf16[128,1024]{1,0:T(8,128)(2,1)S(1)}, u32[]{:S(2)}, u32[]{:S(2)}) collective-permute-start(bf16[128,1024]{1,0:T(8,128)(2,1)} %after.28), channel_id=1, source_target_pairs={{0,8},{4,12},{8,0},{12,4},{1,9},{5,13},{9,1},{13,5},{2,10},{6,14},... | collective-permute-start | bytes 786440 | tf_op jit(solution)/shard_map/ppermute | solution.py:27
  33.2 5.1 %copy-start.14 = (bf16[32,1024]{1,0:T(8,128)(2,1)S(1)}, bf16[32,1024]{1,0:T(8,128)(2,1)}, u32[]{:S(2)}) copy-start(bf16[32,1024]{1,0:T(8,128)(2,1)} %get-tuple-element.80.refs_0_) | copy-start | bytes 196612
  34.4 1.3 %collective-permute-start.12 = (bf16[128,256]{1,0:T(8,128)(2,1)S(1)}, bf16[128,256]{1,0:T(8,128)(2,1)S(1)}, u32[]{:S(2)}, u32[]{:S(2)}) collective-permute-start(bf16[128,256]{1,0:T(8,128)(2,1)S(1)} %get-tuple-element.66), channel_id=1, source_target_pairs={{0,1},{1,0},{2,3},{3,2},{4,5},{5,4},{6,7},{7,6},{8,9},{9,8},{10,11... | collective-permute-start | bytes 196616 | tf_op jit(solution)/shard_map/ppermute | solution.py:23
  34.5 1.4 %collective-permute-start.13 = (bf16[128,256]{1,0:T(8,128)(2,1)S(1)}, bf16[128,256]{1,0:T(8,128)(2,1)S(1)}, u32[]{:S(2)}, u32[]{:S(2)}) collective-permute-start(bf16[128,256]{1,0:T(8,128)(2,1)S(1)} %get-tuple-element.67), channel_id=1, source_target_pairs={{0,1},{1,0},{2,3},{3,2},{4,5},{5,4},{6,7},{7,6},{8,9},{9,8},{10,11... | collective-permute-start | bytes 196616 | tf_op jit(solution)/shard_map/ppermute | solution.py:23
  35.0 1.3 %collective-permute-start.14 = (bf16[128,256]{1,0:T(8,128)(2,1)S(1)}, bf16[128,256]{1,0:T(8,128)(2,1)S(1)}, u32[]{:S(2)}, u32[]{:S(2)}) collective-permute-start(bf16[128,256]{1,0:T(8,128)(2,1)S(1)} %get-tuple-element.68), channel_id=1, source_target_pairs={{0,1},{1,0},{2,3},{3,2},{4,5},{5,4},{6,7},{7,6},{8,9},{9,8},{10,11... | collective-permute-start | bytes 196616 | tf_op jit(solution)/shard_map/ppermute | solution.py:23
  35.8 1.3 %collective-permute-start.15 = (bf16[128,256]{1,0:T(8,128)(2,1)S(1)}, bf16[128,256]{1,0:T(8,128)(2,1)S(1)}, u32[]{:S(2)}, u32[]{:S(2)}) collective-permute-start(bf16[128,256]{1,0:T(8,128)(2,1)S(1)} %get-tuple-element.69), channel_id=1, source_target_pairs={{0,1},{1,0},{2,3},{3,2},{4,5},{5,4},{6,7},{7,6},{8,9},{9,8},{10,11... | collective-permute-start | bytes 196616 | tf_op jit(solution)/shard_map/ppermute | solution.py:23
  35.9 1.3 %collective-permute-start.16 = (bf16[128,256]{1,0:T(8,128)(2,1)S(1)}, bf16[128,256]{1,0:T(8,128)(2,1)S(1)}, u32[]{:S(2)}, u32[]{:S(2)}) collective-permute-start(bf16[128,256]{1,0:T(8,128)(2,1)S(1)} %get-tuple-element.70), channel_id=1, source_target_pairs={{0,1},{1,0},{2,3},{3,2},{4,5},{5,4},{6,7},{7,6},{8,9},{9,8},{10,11... | collective-permute-start | bytes 196616 | tf_op jit(solution)/shard_map/ppermute | solution.py:23
  36.3 1.3 %collective-permute-start.17 = (bf16[128,256]{1,0:T(8,128)(2,1)S(1)}, bf16[128,256]{1,0:T(8,128)(2,1)S(1)}, u32[]{:S(2)}, u32[]{:S(2)}) collective-permute-start(bf16[128,256]{1,0:T(8,128)(2,1)S(1)} %get-tuple-element.71), channel_id=1, source_target_pairs={{0,1},{1,0},{2,3},{3,2},{4,5},{5,4},{6,7},{7,6},{8,9},{9,8},{10,11... | collective-permute-start | bytes 196616 | tf_op jit(solution)/shard_map/ppermute | solution.py:23
  37.0 1.3 %collective-permute-start.18 = (bf16[128,256]{1,0:T(8,128)(2,1)S(1)}, bf16[128,256]{1,0:T(8,128)(2,1)S(1)}, u32[]{:S(2)}, u32[]{:S(2)}) collective-permute-start(bf16[128,256]{1,0:T(8,128)(2,1)S(1)} %get-tuple-element.72), channel_id=1, source_target_pairs={{0,1},{1,0},{2,3},{3,2},{4,5},{5,4},{6,7},{7,6},{8,9},{9,8},{10,11... | collective-permute-start | bytes 196616 | tf_op jit(solution)/shard_map/ppermute | solution.py:23
  37.2 3.1 %collective-permute-start.19 = (bf16[128,256]{1,0:T(8,128)(2,1)S(1)}, bf16[128,256]{1,0:T(8,128)(2,1)S(1)}, u32[]{:S(2)}, u32[]{:S(2)}) collective-permute-start(bf16[128,256]{1,0:T(8,128)(2,1)S(1)} %get-tuple-element.73), channel_id=1, source_target_pairs={{0,1},{1,0},{2,3},{3,2},{4,5},{5,4},{6,7},{7,6},{8,9},{9,8},{10,11... | collective-permute-start | bytes 196616 | tf_op jit(solution)/shard_map/ppermute | solution.py:23
  37.5 11.3 %collective-permute-start.22 = (bf16[48,1024]{1,0:T(8,128)(2,1)S(1)}, bf16[48,1024]{1,0:T(8,128)(2,1)S(1)}, u32[]{:S(2)}, u32[]{:S(2)}) collective-permute-start(bf16[48,1024]{1,0:T(8,128)(2,1)S(1)} %after.23), channel_id=1, source_target_pairs={{0,12},{4,0},{8,4},{12,8},{1,13},{5,1},{9,5},{13,9},{2,14},{6,2},{... | collective-permute-start | bytes 294920 | tf_op jit(solution)/shard_map/ppermute | solution.py:23
  38.3 10.6 %collective-permute-start.24 = (bf16[32,1024]{1,0:T(8,128)(2,1)S(1)}, bf16[32,1024]{1,0:T(8,128)(2,1)S(1)}, u32[]{:S(2)}, u32[]{:S(2)}) collective-permute-start(bf16[32,1024]{1,0:T(8,128)(2,1)S(1)} %after.25), channel_id=1, source_target_pairs={{0,12},{4,0},{8,4},{12,8},{1,13},{5,1},{9,5},{13,9},{2,14},{6,2},{... | collective-permute-start | bytes 196616 | tf_op jit(solution)/shard_map/ppermute | solution.py:23
  40.3 16.4 %slice-start = ((s8[8388608]{0:T(1024)(128)(4,1)}), s8[4194304]{0:T(1024)(128)(4,1)S(1)}, s32[]{:S(2)}) async-start(s8[8388608]{0:T(1024)(128)(4,1)} %bitcast.8), calls=%async_computation | async-start | bytes 8388608
  40.3 5.2 %copy-start.4 = (bf16[128,1024]{1,0:T(8,128)(2,1)S(1)}, bf16[128,1024]{1,0:T(8,128)(2,1)}, u32[]{:S(2)}) copy-start(bf16[128,1024]{1,0:T(8,128)(2,1)} %get-tuple-element.83.refs_0_) | copy-start | bytes 786436
  40.3 16.4 %slice-start.1 = ((s8[8388608]{0:T(1024)(128)(4,1)}), s8[4194304]{0:T(1024)(128)(4,1)S(1)}, s32[]{:S(2)}) async-start(s8[8388608]{0:T(1024)(128)(4,1)} %bitcast.8), calls=%async_computation.1 | async-start | bytes 8388608
  42.7 34.7 %collective-permute-start.20 = (bf16[2048,256]{1,0:T(8,128)(2,1)S(1)}, bf16[2048,256]{1,0:T(8,128)(2,1)}, u32[]{:S(2)}, u32[]{:S(2)}) collective-permute-start(bf16[2048,256]{1,0:T(8,128)(2,1)S(1)} %fetched_weights.1.refs_18_.refs_2_.refs_5_), channel_id=1, source_target_pairs={{0,2},{2,0},{1,3},{3,1},{4,6},{6,4},{5,7},{7,5},{8,10},{10,8},{9,1... | collective-permute-start | bytes 3145736 | tf_op jit(solution)/shard_map/ppermute | solution.py:23
  46.3 24.8 %collective-permute-start.28 = (bf16[256,1024]{1,0:T(8,128)(2,1)}, bf16[256,1024]{1,0:T(8,128)(2,1)}, u32[]{:S(2)}, u32[]{:S(2)}) collective-permute-start(bf16[256,1024]{1,0:T(8,128)(2,1)} %stack.3), channel_id=1, source_target_pairs={{0,4},{4,0},{8,12},{12,8},{1,5},{5,1},{9,13},{13,9},{2,6},{6,2},{1... | collective-permute-start | bytes 1572872 | tf_op jit(solution)/shard_map/ppermute | solution.py:27
  48.8 14.6 %copy-start.6 = (bf16[32,1024]{1,0:T(8,128)(2,1)}, bf16[32,1024]{1,0:T(8,128)(2,1)S(1)}, u32[]{:S(2)}) copy-start(bf16[32,1024]{1,0:T(8,128)(2,1)S(1)} %collective-permute-done.24.refs_0_.refs_4_) | copy-start | bytes 196612
  48.8 7.9 %copy-start.2 = (bf16[256,1024]{1,0:T(8,128)(2,1)}, bf16[256,1024]{1,0:T(8,128)(2,1)S(1)}, u32[]{:S(2)}) copy-start(bf16[256,1024]{1,0:T(8,128)(2,1)S(1)} %collective-permute-done.21.refs_0_.refs_1_) | copy-start | bytes 1572868
  48.9 26.5 %collective-permute-start.33 = (bf16[256,1024]{1,0:T(8,128)(2,1)}, bf16[256,1024]{1,0:T(8,128)(2,1)}, u32[]{:S(2)}, u32[]{:S(2)}) collective-permute-start(bf16[256,1024]{1,0:T(8,128)(2,1)} %after.32), channel_id=1, source_target_pairs={{0,8},{4,12},{8,0},{12,4},{1,9},{5,13},{9,1},{13,5},{2,10},{6,14},... | collective-permute-start | bytes 1572872 | tf_op jit(solution)/shard_map/ppermute | solution.py:23
  52.1 3.6 %collective-permute-start.26 = (s32[8,128]{1,0:T(8,128)S(1)}, s32[8,128]{1,0:T(8,128)S(1)}, u32[]{:S(2)}, u32[]{:S(2)}) collective-permute-start(s32[8,128]{1,0:T(8,128)S(1)} %get-tuple-element.57.refs_10_), channel_id=1, source_target_pairs={{0,16},{16,0},{1,17},{17,1},{2,18},{18,2},{3,19},{19,3},{4,20},{20... | collective-permute-start | bytes 12296 | tf_op jit(solution)/shard_map/ppermute | solution.py:23
  56.8 6.6 %copy-start.18 = (bf16[128,1024]{1,0:T(8,128)(2,1)S(1)}, bf16[128,1024]{1,0:T(8,128)(2,1)}, u32[]{:S(2)}) copy-start(bf16[128,1024]{1,0:T(8,128)(2,1)} %get-tuple-element.81.refs_0_) | copy-start | bytes 786436
  63.7 1.8 %collective-permute-start.29 = (bf16[128,1024]{1,0:T(8,128)(2,1)}, bf16[128,1024]{1,0:T(8,128)(2,1)S(1)}, u32[]{:S(2)}, u32[]{:S(2)}) collective-permute-start(bf16[128,1024]{1,0:T(8,128)(2,1)} %get-tuple-element.83.refs_0_), channel_id=1, source_target_pairs={{0,1},{1,0},{2,3},{3,2},{4,5},{5,4},{6,7},{7,6},{8,9},{9,8},{10,11... | collective-permute-start | bytes 786440 | tf_op jit(solution)/shard_map/ppermute | solution.py:23
  63.8 1.9 %collective-permute-start.30 = (bf16[128,1024]{1,0:T(8,128)(2,1)S(1)}, bf16[128,1024]{1,0:T(8,128)(2,1)S(1)}, u32[]{:S(2)}, u32[]{:S(2)}) collective-permute-start(bf16[128,1024]{1,0:T(8,128)(2,1)S(1)} %after.29.refs_1_), channel_id=1, source_target_pairs={{0,1},{1,0},{2,3},{3,2},{4,5},{5,4},{6,7},{7,6},{8,9},{9,8},{10,11... | collective-permute-start | bytes 786440 | tf_op jit(solution)/shard_map/ppermute | solution.py:23
  65.5 3.9 %collective-permute-start.23 = (bf16[48,1024]{1,0:T(8,128)(2,1)S(1)}, bf16[48,1024]{1,0:T(8,128)(2,1)S(1)}, u32[]{:S(2)}, u32[]{:S(2)}) collective-permute-start(bf16[48,1024]{1,0:T(8,128)(2,1)S(1)} %after.24.refs_0_), channel_id=1, source_target_pairs={{0,1},{1,0},{2,3},{3,2},{4,5},{5,4},{6,7},{7,6},{8,9},{9,8},{10,11... | collective-permute-start | bytes 294920 | tf_op jit(solution)/shard_map/ppermute | solution.py:23
  65.6 3.7 %collective-permute-start.25 = (bf16[32,1024]{1,0:T(8,128)(2,1)S(1)}, bf16[32,1024]{1,0:T(8,128)(2,1)S(1)}, u32[]{:S(2)}, u32[]{:S(2)}) collective-permute-start(bf16[32,1024]{1,0:T(8,128)(2,1)S(1)} %after.26.refs_2_), channel_id=1, source_target_pairs={{0,1},{1,0},{2,3},{3,2},{4,5},{5,4},{6,7},{7,6},{8,9},{9,8},{10,11... | collective-permute-start | bytes 196616 | tf_op jit(solution)/shard_map/ppermute | solution.py:23
  71.1 1.2 %collective-permute-start.31 = (s32[8,128]{1,0:T(8,128)S(1)}, s32[8,128]{1,0:T(8,128)S(1)}, u32[]{:S(2)}, u32[]{:S(2)}) collective-permute-start(s32[8,128]{1,0:T(8,128)S(1)} %after.30), channel_id=1, source_target_pairs={{0,1},{1,0},{2,3},{3,2},{4,5},{5,4},{6,7},{7,6},{8,9},{9,8},{10,11... | collective-permute-start | bytes 12296 | tf_op jit(solution)/shard_map/ppermute | solution.py:23
  71.1 6.3 %collective-permute-start.35 = (bf16[256,1024]{1,0:T(8,128)(2,1)}, bf16[256,1024]{1,0:T(8,128)(2,1)S(1)}, u32[]{:S(2)}, u32[]{:S(2)}) collective-permute-start(bf16[256,1024]{1,0:T(8,128)(2,1)} %after.34.refs_9_), channel_id=1, source_target_pairs={{0,1},{1,0},{2,3},{3,2},{4,5},{5,4},{6,7},{7,6},{8,9},{9,8},{10,11... | collective-permute-start | bytes 1572872 | tf_op jit(solution)/shard_map/ppermute | solution.py:23
  72.3 5.9 %collective-permute-start.32 = (bf16[256,1024]{1,0:T(8,128)(2,1)S(1)}, bf16[256,1024]{1,0:T(8,128)(2,1)S(1)}, u32[]{:S(2)}, u32[]{:S(2)}) collective-permute-start(bf16[256,1024]{1,0:T(8,128)(2,1)S(1)} %after.31.refs_3_), channel_id=1, source_target_pairs={{0,1},{1,0},{2,3},{3,2},{4,5},{5,4},{6,7},{7,6},{8,9},{9,8},{10,11... | collective-permute-start | bytes 1572872 | tf_op jit(solution)/shard_map/ppermute | solution.py:23
  75.4 2.8 %collective-permute-start.34 = (bf16[256,1024]{1,0:T(8,128)(2,1)}, bf16[256,1024]{1,0:T(8,128)(2,1)S(1)}, u32[]{:S(2)}, u32[]{:S(2)}) collective-permute-start(bf16[256,1024]{1,0:T(8,128)(2,1)} %after.33.refs_5_), channel_id=1, source_target_pairs={{0,1},{1,0},{2,3},{3,2},{4,5},{5,4},{6,7},{7,6},{8,9},{9,8},{10,11... | collective-permute-start | bytes 1572872 | tf_op jit(solution)/shard_map/ppermute | solution.py:23
  75.4 8.5 %collective-permute-start.37 = (bf16[64,1024]{1,0:T(8,128)(2,1)S(1)}, bf16[64,1024]{1,0:T(8,128)(2,1)S(1)}, u32[]{:S(2)}, u32[]{:S(2)}) collective-permute-start(bf16[64,1024]{1,0:T(8,128)(2,1)S(1)} %after.20.refs_3_), channel_id=1, source_target_pairs={{0,12},{4,0},{8,4},{12,8},{1,13},{5,1},{9,5},{13,9},{2,14},{6,2},{... | collective-permute-start | bytes 393224 | tf_op jit(solution)/shard_map/ppermute | solution.py:23
  77.4 7.1 %collective-permute-start.39 = (bf16[64,1024]{1,0:T(8,128)(2,1)S(1)}, bf16[64,1024]{1,0:T(8,128)(2,1)S(1)}, u32[]{:S(2)}, u32[]{:S(2)}) collective-permute-start(bf16[64,1024]{1,0:T(8,128)(2,1)S(1)} %after.21.refs_4_), channel_id=1, source_target_pairs={{0,12},{4,0},{8,4},{12,8},{1,13},{5,1},{9,5},{13,9},{2,14},{6,2},{... | collective-permute-start | bytes 393224 | tf_op jit(solution)/shard_map/ppermute | solution.py:23
  77.4 8.8 %collective-permute-start.41 = (bf16[48,1024]{1,0:T(8,128)(2,1)S(1)}, bf16[48,1024]{1,0:T(8,128)(2,1)S(1)}, u32[]{:S(2)}, u32[]{:S(2)}) collective-permute-start(bf16[48,1024]{1,0:T(8,128)(2,1)S(1)} %after.22.refs_5_), channel_id=1, source_target_pairs={{0,12},{4,0},{8,4},{12,8},{1,13},{5,1},{9,5},{13,9},{2,14},{6,2},{... | collective-permute-start | bytes 294920 | tf_op jit(solution)/shard_map/ppermute | solution.py:23
  82.3 10.3 %collective-permute-start.36 = (bf16[1024,128]{1,0:T(8,128)(2,1)S(1)}, bf16[1024,128]{1,0:T(8,128)(2,1)S(1)}, u32[]{:S(2)}, u32[]{:S(2)}) collective-permute-start(bf16[1024,128]{1,0:T(8,128)(2,1)S(1)} %get-tuple-element.90.refs_1_), channel_id=1, source_target_pairs={{0,2},{2,0},{1,3},{3,1},{4,6},{6,4},{5,7},{7,5},{8,10},{10,8},{9,1... | collective-permute-start | bytes 786440 | tf_op jit(solution)/shard_map/ppermute | solution.py:23
  83.9 3.7 %collective-permute-start.38 = (bf16[64,1024]{1,0:T(8,128)(2,1)S(1)}, bf16[64,1024]{1,0:T(8,128)(2,1)S(1)}, u32[]{:S(2)}, u32[]{:S(2)}) collective-permute-start(bf16[64,1024]{1,0:T(8,128)(2,1)S(1)} %after.35.refs_4_), channel_id=1, source_target_pairs={{0,1},{1,0},{2,3},{3,2},{4,5},{5,4},{6,7},{7,6},{8,9},{9,8},{10,11... | collective-permute-start | bytes 393224 | tf_op jit(solution)/shard_map/ppermute | solution.py:23
  84.5 3.0 %collective-permute-start.40 = (bf16[64,1024]{1,0:T(8,128)(2,1)S(1)}, bf16[64,1024]{1,0:T(8,128)(2,1)S(1)}, u32[]{:S(2)}, u32[]{:S(2)}) collective-permute-start(bf16[64,1024]{1,0:T(8,128)(2,1)S(1)} %after.36.refs_6_), channel_id=1, source_target_pairs={{0,1},{1,0},{2,3},{3,2},{4,5},{5,4},{6,7},{7,6},{8,9},{9,8},{10,11... | collective-permute-start | bytes 393224 | tf_op jit(solution)/shard_map/ppermute | solution.py:23
  86.2 1.3 %collective-permute-start.42 = (bf16[48,1024]{1,0:T(8,128)(2,1)S(1)}, bf16[48,1024]{1,0:T(8,128)(2,1)S(1)}, u32[]{:S(2)}, u32[]{:S(2)}) collective-permute-start(bf16[48,1024]{1,0:T(8,128)(2,1)S(1)} %after.37.refs_8_), channel_id=1, source_target_pairs={{0,1},{1,0},{2,3},{3,2},{4,5},{5,4},{6,7},{7,6},{8,9},{9,8},{10,11... | collective-permute-start | bytes 294920 | tf_op jit(solution)/shard_map/ppermute | solution.py:23
  88.3 4.3 %collective-permute-start.43 = (bf16[256,128]{1,0:T(8,128)(2,1)S(1)}, bf16[256,128]{1,0:T(8,128)(2,1)S(1)}, u32[]{:S(2)}, u32[]{:S(2)}) collective-permute-start(bf16[256,128]{1,0:T(8,128)(2,1)S(1)} %get-tuple-element.93), channel_id=1, source_target_pairs={{0,2},{2,0},{1,3},{3,1},{4,6},{6,4},{5,7},{7,5},{8,10},{10,8},{9,1... | collective-permute-start | bytes 196616 | tf_op jit(solution)/shard_map/ppermute | solution.py:23
  (13 other events, 31.3 us)

commit v20 on v19

--- a/solution.py
+++ b/solution.py
@@ -175,13 +175,14 @@
     return jnp.concatenate(found)
 
 
-def own_rows(goal, train, bulk, *others):
+def own_rows(goal, train, n_shard, n_rep, bulk, extra, *others):
     rows, width = train.shape
-    cuts = 4
+    cuts = 2 * n_rep
     part = width // cuts
+    per = cuts // n_rep
 
     def kernel(goal_ref, train_ref, *rest):
-        out_ref, held, sem = rest[-3:]
+        outs, (held, sem) = rest[len(others):-2], rest[-2:]
         copies = [
             pltpu.make_async_copy(train_ref.at[:, c * part:(c + 1) * part], held.at[c], sem.at[c]) for c in range(cuts)
         ]
@@ -190,13 +191,22 @@
         pick = one_hot(goal_ref, lax.axis_index("shard") * bulk, bulk)
         for c, copy in enumerate(copies):
             copy.wait()
-            out_ref[:, c * part:(c + 1) * part] = dot(pick, held[c]).astype(BF16)
-
+            outs[0][:, c * part:(c + 1) * part] = dot(pick, held[c]).astype(BF16)
+        if extra:
+            second = one_hot(goal_ref, n_shard * bulk + extra, extra)
+            for r in range(n_rep):
+                @pl.when(lax.axis_index("rep") == r)
+                def _():
+                    for c in range(per):
+                        outs[1][:, c * part:(c + 1) * part] = dot(second, held[r * per + c]).astype(BF16)
+
+    shapes = [jax.ShapeDtypeStruct((bulk, width), BF16)]
+    shapes += [jax.ShapeDtypeStruct((extra, width // n_rep), BF16)] * (1 if extra else 0)
     return pl.pallas_call(
         kernel,
         in_specs=[VMEM, HBM] + [ANY] * len(others),
-        out_specs=VMEM,
-        out_shape=jax.ShapeDtypeStruct((bulk, width), BF16),
+        out_specs=[VMEM] * len(shapes),
+        out_shape=shapes,
         scratch_shapes=[pltpu.VMEM((cuts, rows, part), BF16), pltpu.SemaphoreType.DMA((cuts,))],
         cost_estimate=cost(2 * bulk * train.size, 2 * train.size),
         compiler_params=PARAMS,
@@ -243,11 +253,12 @@
 
         for out, (hops, first, _) in zip(outs, cuts):
             fill(out, lax.rem(me + hops, jnp.int32(n_shard)) * bulk + first)
-        for j, out in enumerate(outs[len(cuts):]):
-            fill(out, n_shard * bulk + max(j - 1, 0) * extra)
+        if extra:
+            fill(outs[-1], n_shard * bulk)
+            outs[-2][...] = outs[-1][...]
 
     shapes = [jax.ShapeDtypeStruct((n, columns), BF16) for _, _, n in cuts]
-    shapes += [jax.ShapeDtypeStruct((extra, columns), BF16)] * (3 if extra else 0)
+    shapes += [jax.ShapeDtypeStruct((extra, columns), BF16)] * (2 if extra else 0)
     shapes += [jax.ShapeDtypeStruct((lines, LANES), I32)]
     packed = n_shard * bulk + 2 * extra
     return pl.pallas_call(
@@ -616,10 +627,10 @@
     *packed, goal = pack_rows(train, ids, columns, bulk, extra, middle + final)
     firsts, seconds = [], []
     parts = [pieces] + [[shift(x, "groups", n_group, d) for x in pieces] for d in range(1, n_group)]
-    here = [shift(after(packed[0], *pieces[1:]), "shard", n_shard, 1)]
+    here = [shift(after(packed[0], pieces[1]), "shard", n_shard, 1)]
     urgent = [here[0]]
     if extra:
-        far = swap(after(packed[-2], *pieces[1:]), "shard", n_shard, 2)
+        far = swap(after(packed[-1], *pieces[1:]), "shard", n_shard, 2)
         urgent.append(far)
     sent_last = packed[len(middle):len(middle) + len(final)]
     last = [shift(after(x, *pieces[1:]), "shard", n_shard, last_hops) for x in sent_last[:fillers]]
@@ -645,7 +656,7 @@
     sent_last = [after(x, own) for x in sent_last[fillers:]]
     last_all = [with_rep(after(x, own)) for x in last]
 
-    mine = own_rows(goal, train, bulk, own)
+    mine, *further = own_rows(goal, train, n_shard, n_rep, bulk, extra, own)
     marks = [own, mine, *sent_last, *[p for x in last_all for p in x[1:]]]
     if extra:
         for d in range(1, n_group):
@@ -659,9 +670,9 @@
             empty = unwritten((2 * extra, columns), 2 * n_rep)
             return [[*empty[:n_rep]], [*empty[n_rep:]]]
 
-        seconds = lax.cond(flag[0, 0] > 0, second_round, no_round, after(packed[-1], own))
-        near = swap(stack([packed[-3], far], *sends), "shard", n_shard, 1)
-        pairs = [stack([x, y], own) for x, y in zip(with_rep(packed[-3]), with_rep(after(far, own)))]
+        seconds = lax.cond(flag[0, 0] > 0, second_round, no_round, further[0])
+        near = swap(stack([packed[-2], far], *sends), "shard", n_shard, 1)
+        pairs = [stack([x, y], own) for x, y in zip(with_rep(packed[-2]), with_rep(after(far, own)))]
         firsts = [pairs, with_rep(after(near, own))]
         marks += [seconds[0][0], near, *pairs]
 

time: 94.6 us -> 102 us (1.078)
  starting transfers between devices: 37.9 us -> 43.1 us
    ppermute x38, starting transfers between devices: 33.8 us -> 40.6 us  [shift(): return lax.ppermute(x, axis, [(i, (i + by) % size) for i in range(size)])]
    ppermute x38, waiting for transfers between devices: 14.8 us -> 17.2 us  [shift(): return lax.ppermute(x, axis, [(i, (i + by) % size) for i in range(size)])]
    ppermute x2, waiting for transfers between devices: 2.93 us -> 1.24 us  [swap(): return lax.ppermute(x, axis, [(i, i ^ bit) for i in range(size)])]
    ppermute x2, starting transfers between devices: 4.05 us -> 2.56 us  [swap(): return lax.ppermute(x, axis, [(i, i ^ bit) for i in range(size)])]
    pallas_call x1, Pallas kernels: 2.36 us -> 3.61 us  [own_rows(): pl.pallas_call(kernel, in_specs=[VMEM, HBM] + [ANY] * len(others), out_sp...]
    unnamed x42 -> x44, local copies, waits for them, and re-layouts: 4.3 us -> 4.81 us
  transfers between devices with their start and end apart: 40 -> 40, of which waited for: 13 -> 13; matrix products, arithmetic and copies ran while one was open for 1% -> 1% of each run, Pallas kernels for 33% -> 31%
where the time goes in v20:
time: 102 us
  starting transfers between devices  43.1 us (42%)
  Pallas kernels  33.6 us (33%)
  waiting for transfers between devices  18.5 us (18%)
  local copies, waits for them, and re-layouts  5.33 us (5%)
    ppermute x38, starting transfers between devices, shift(): return lax.ppermute(x, axis, [(i, (i + by) % size) for i in range(size)])  40.6 us
    ppermute x38, waiting for transfers between devices, shift(): return lax.ppermute(x, axis, [(i, (i + by) % size) for i in range(size)])  17.2 us
    pallas_call x1, Pallas kernels, partial_weights(): pl.pallas_call(kernel, in_specs=[SMEM] + [HBM] * n + [VMEM] * (CUTS * n)...  6.75 us
    pallas_call x1, Pallas kernels, pack_rows(): pl.pallas_call(kernel, grid=(1,), in_specs=[pl.BlockSpec((lines, LANES),...  6.15 us
    unnamed x44, local copies, waits for them, and re-layouts  4.81 us
    pallas_call x1, Pallas kernels, early_scores(): pl.pallas_call(kernel, in_specs=[SMEM] + [VMEM] * (2 + n_other + n_rep *...  4.16 us
    pallas_call x1, Pallas kernels, own_rows(): pl.pallas_call(kernel, in_specs=[VMEM, HBM] + [ANY] * len(others), out_sp...  3.61 us
    pallas_call x1, Pallas kernels, pick_queries(): pl.pallas_call(kernel, in_specs=[SMEM, SMEM, ANY], out_specs=[VMEM] * n_c...  2.68 us
  transfers between devices with their start and end apart: 40, of which 13 were waited for; matrix products, arithmetic and copies ran while one was open for 1% of the time, Pallas kernels for 31%

profile of v20, /device:TPU:0, one launch (start us, length us, event | category | flops | bytes accessed | tf_op | source)
XLA Modules:
  0.0 101.6 jit_solution(12236732752151432764)
XLA Ops:
  0.0 0.5 collective-permute-start.7
  0.5 2.7 %pick_queries.1 = (bf16[1,64,1024]{2,1,0:T(8,128)(2,1)}, bf16[1,64,1024]{2,1,0:T(8,128)(2,1)}, bf16[1,64,1024]{2,1,0:T(8,128)(2,1)}, bf16[1,64,1024]{2,1,0:T(8,128)(2,1)}) custom-call(s32[4,4]{1,0:T(4,128)} %pattern_ref.3, s32[16]{0:T(128)} %slot_ref.3, bf16[4,128,1024]{2,1,0:T(8,128)(2,1)} %in_ref.1), custom_call_target="tpu_custom_call" | custom-call | flops 1 | bytes 1 | tf_op jit(solution)/shard_map/pick_queries/pallas_call | solution.py:109
  3.1 2.8 %collective-permute-start.4 = (bf16[1,64,1024]{2,1,0:T(8,128)(2,1)}, bf16[1,64,1024]{2,1,0:T(8,128)(2,1)S(1)}, u32[]{:S(2)}, u32[]{:S(2)}) collective-permute-start(bf16[1,64,1024]{2,1,0:T(8,128)(2,1)} %get-tuple-element.51), channel_id=1, source_target_pairs={{0,4},{4,8},{8,12},{12,0},{1,5},{5,9},{9,13},{13,1},{2,6},{6,10},{... | collective-permute-start | bytes 393224 | tf_op jit(solution)/shard_map/ppermute | solution.py:23
  5.9 2.6 %collective-permute-start.5 = (bf16[1,64,1024]{2,1,0:T(8,128)(2,1)}, bf16[1,64,1024]{2,1,0:T(8,128)(2,1)S(1)}, u32[]{:S(2)}, u32[]{:S(2)}) collective-permute-start(bf16[1,64,1024]{2,1,0:T(8,128)(2,1)} %get-tuple-element.52), channel_id=1, source_target_pairs={{0,8},{4,12},{8,0},{12,4},{1,9},{5,13},{9,1},{13,5},{2,10},{6,14},... | collective-permute-start | bytes 393224 | tf_op jit(solution)/shard_map/ppermute | solution.py:23
  8.5 1.3 %collective-permute-start.6 = (bf16[1,64,1024]{2,1,0:T(8,128)(2,1)}, bf16[1,64,1024]{2,1,0:T(8,128)(2,1)S(1)}, u32[]{:S(2)}, u32[]{:S(2)}) collective-permute-start(bf16[1,64,1024]{2,1,0:T(8,128)(2,1)} %get-tuple-element.53), channel_id=1, source_target_pairs={{0,12},{4,0},{8,4},{12,8},{1,13},{5,1},{9,5},{13,9},{2,14},{6,2},{... | collective-permute-start | bytes 393224 | tf_op jit(solution)/shard_map/ppermute | solution.py:23
  9.9 1.5 %collective-permute-start.8 = (bf16[1,64,1024]{2,1,0:T(8,128)(2,1)}, bf16[1,64,1024]{2,1,0:T(8,128)(2,1)S(1)}, u32[]{:S(2)}, u32[]{:S(2)}) collective-permute-start(bf16[1,64,1024]{2,1,0:T(8,128)(2,1)} %get-tuple-element.55.refs_0_), channel_id=1, source_target_pairs={{0,16},{16,0},{1,17},{17,1},{2,18},{18,2},{3,19},{19,3},{4,20},{20... | collective-permute-start | bytes 393224 | tf_op jit(solution)/shard_map/ppermute | solution.py:23
  11.4 6.1 %pack_rows.1 = (bf16[256,1024]{1,0:T(8,128)(2,1)}, bf16[256,1024]{1,0:T(8,128)(2,1)}, bf16[48,1024]{1,0:T(8,128)(2,1)}, bf16[32,1024]{1,0:T(8,128)(2,1)}, bf16[6...) custom-call(s32[32,128]{1,0:T(8,128)} %bitcast.11, ...), custom_call_target="tpu_custom_call" | custom-call | flops 1 | bytes 1 | tf_op jit(solution)/shard_map/pack_rows/pallas_call | solution.py:264
  17.5 0.7 collective-permute-start.21
  18.3 1.1 %collective-permute-start.9 = (bf16[1,64,1024]{2,1,0:T(8,128)(2,1)S(1)}, bf16[1,64,1024]{2,1,0:T(8,128)(2,1)S(1)}, u32[]{:S(2)}, u32[]{:S(2)}) collective-permute-start(bf16[1,64,1024]{2,1,0:T(8,128)(2,1)S(1)} %collective-permute-done.4.rest_0_.refs_2_.refs_1_), channel_id=1, source_target_pairs={{0,16},{16,0},{1,17},{17,1},{2,18},{18,2},{3,19},{19,3},{4,20},{20... | collective-permute-start | bytes 393224 | tf_op jit(solution)/shard_map/ppermute | solution.py:23
  19.4 0.9 collective-permute-start.10
  20.3 1.1 %collective-permute-start.11 = (bf16[1,64,1024]{2,1,0:T(8,128)(2,1)S(1)}, bf16[1,64,1024]{2,1,0:T(8,128)(2,1)S(1)}, u32[]{:S(2)}, u32[]{:S(2)}) collective-permute-start(bf16[1,64,1024]{2,1,0:T(8,128)(2,1)S(1)} %collective-permute-done.6.rest_2_.refs_4_.refs_3_), channel_id=1, source_target_pairs={{0,16},{16,0},{1,17},{17,1},{2,18},{18,2},{3,19},{19,3},{4,20},{20... | collective-permute-start | bytes 393224 | tf_op jit(solution)/shard_map/ppermute | solution.py:23
  21.4 1.3 %collective-permute-start.27 = (bf16[128,1024]{1,0:T(8,128)(2,1)}, bf16[128,1024]{1,0:T(8,128)(2,1)S(1)}, u32[]{:S(2)}, u32[]{:S(2)}) collective-permute-start(bf16[128,1024]{1,0:T(8,128)(2,1)} %after.26), channel_id=1, source_target_pairs={{0,8},{4,12},{8,0},{12,4},{1,9},{5,13},{9,1},{13,5},{2,10},{6,14},... | collective-permute-start | bytes 786440 | tf_op jit(solution)/shard_map/ppermute | solution.py:27
  22.7 0.8 row_table.1
  23.6 3.4 %copy-done = bf16[1,4096,1024]{2,1,0:T(8,128)(2,1)S(1)} copy-done((bf16[1,4096,1024]{2,1,0:T(8,128)(2,1)S(1)}, bf16[1,4096,1024]{2,1,0:T(8,128)(2,1)}, u32[]{:S(2)}) %copy-start) | copy-done | bytes 8388632
  26.9 2.5 %fetch.1 = (bf16[2048,1024]{1,0:T(8,128)(2,1)S(1)}, bf16[2048,1024]{1,0:T(8,128)(2,1)S(1)}) custom-call(s32[1]{0:T(128)} %bitcast.3.block_ref, bf16[4096,1024]{1,0:T(8,128)(2,1)S(1)} %bitcast.7, bf16[4096,1024]{1,0:T(8,128)(2,1)} %collective-permute-done.7.refs_1_, bf16[1,64,1024]{2,1,0:T(8,128)(2,1)S(1)} %collective-permute-done.4.rest_0_.refs_2_.refs_1_, ...), custom_call_target="tpu_custom_call" | custom-call | flops 1 | bytes 1 | tf_op jit(solution)/shard_map/fetch/pallas_call | solution.py:337
  29.5 1.2 %join_queries.1 = (bf16[128,256]{1,0:T(8,128)(2,1)S(1)}, bf16[128,256]{1,0:T(8,128)(2,1)S(1)}, bf16[128,256]{1,0:T(8,128)(2,1)S(1)}, bf16[128,256]{1,0:T(8,128)(...) custom-call(s32[4,4]{1,0:T(4,128)S(1)} %copy-done.17, ...), custom_call_target="tpu_custom_call" | custom-call | flops 1 | bytes 1 | tf_op jit(solution)/shard_map/join_queries/pallas_call | solution.py:154
  30.9 0.5 collective-permute-start.13
  31.4 0.7 collective-permute-done.12.refs_10_
  32.8 0.6 collective-permute-done.15.refs_13_
  33.9 16.5 %collective-permute-start.22 = (bf16[48,1024]{1,0:T(8,128)(2,1)S(1)}, bf16[48,1024]{1,0:T(8,128)(2,1)S(1)}, u32[]{:S(2)}, u32[]{:S(2)}) collective-permute-start(bf16[48,1024]{1,0:T(8,128)(2,1)S(1)} %after.22), channel_id=1, source_target_pairs={{0,12},{4,0},{8,4},{12,8},{1,13},{5,1},{9,5},{13,9},{2,14},{6,2},{... | collective-permute-start | bytes 294920 | tf_op jit(solution)/shard_map/ppermute | solution.py:23
  50.4 0.7 collective-permute-start.24
  51.1 2.3 %fetched_weights.1.refs_18_.refs_2_.refs_5_ = bf16[2048,256]{1,0:T(8,128)(2,1)S(1)} custom-call(bf16[2048,1024]{1,0:T(8,128)(2,1)S(1)} %get-tuple-element.56.refs_8_.refs_0_, bf16[2048,1024]{1,0:T(8,128)(2,1)S(1)} %get-tuple-element.57.refs_9_.refs_1_, bf16[128,256]{1,0:T(8,128)(2,1)S(1)} %get-tuple-element.59.refs_2_, ...), custom_call_target="tpu_custom_call" | custom-call | flops 1 | bytes 1 | tf_op jit(solution)/shard_map/fetched_weights/pallas_call | solution.py:364
  53.5 1.6 %collective-permute-start.20 = (bf16[2048,256]{1,0:T(8,128)(2,1)S(1)}, bf16[2048,256]{1,0:T(8,128)(2,1)}, u32[]{:S(2)}, u32[]{:S(2)}) collective-permute-start(bf16[2048,256]{1,0:T(8,128)(2,1)S(1)} %fetched_weights.1.refs_18_.refs_2_.refs_5_), channel_id=1, source_target_pairs={{0,2},{2,0},{1,3},{3,1},{4,6},{6,4},{5,7},{7,5},{8,10},{10,8},{9,1... | collective-permute-start | bytes 3145736 | tf_op jit(solution)/shard_map/ppermute | solution.py:23
  55.0 0.8 stack.3
  55.9 1.3 %collective-permute-start.28 = (bf16[256,1024]{1,0:T(8,128)(2,1)}, bf16[256,1024]{1,0:T(8,128)(2,1)}, u32[]{:S(2)}, u32[]{:S(2)}) collective-permute-start(bf16[256,1024]{1,0:T(8,128)(2,1)} %stack.3), channel_id=1, source_target_pairs={{0,4},{4,0},{8,12},{12,8},{1,5},{5,1},{9,13},{13,9},{2,6},{6,2},{1... | collective-permute-start | bytes 1572872 | tf_op jit(solution)/shard_map/ppermute | solution.py:27
  57.3 2.0 %collective-permute-start.26 = (s32[8,128]{1,0:T(8,128)S(1)}, s32[8,128]{1,0:T(8,128)S(1)}, u32[]{:S(2)}, u32[]{:S(2)}) collective-permute-start(s32[8,128]{1,0:T(8,128)S(1)} %get-tuple-element.58.refs_10_), channel_id=1, source_target_pairs={{0,16},{16,0},{1,17},{17,1},{2,18},{18,2},{3,19},{19,3},{4,20},{20... | collective-permute-start | bytes 12296 | tf_op jit(solution)/shard_map/ppermute | solution.py:23
  59.3 1.7 %collective-permute-done.26 = s32[8,128]{1,0:T(8,128)S(1)} collective-permute-done((s32[8,128]{1,0:T(8,128)S(1)}, s32[8,128]{1,0:T(8,128)S(1)}, u32[]{:S(2)}, u32[]{:S(2)}) %collective-permute-start.26) | collective-permute-done | bytes 4128 | tf_op jit(solution)/shard_map/ppermute | solution.py:23
  61.0 0.5 slice.3
  62.2 6.7 %partial_weights.1.rest_0_.refs_1_.refs_2_.refs_0_ = f32[2048,256]{1,0:T(8,128)S(1)} custom-call(s32[1]{0:T(128)} %bitcast.1.block_ref, bf16[4096,1024]{1,0:T(8,128)(2,1)S(1)} %bitcast.10, bf16[4096,1024]{1,0:T(8,128)(2,1)} %collective-permute-done.7.refs_1_, bf16[128,256]{1,0:T(8,128)(2,1)S(1)} %get-tuple-element.59.refs_2_, ...), custom_call_target="tpu_custom_call" | custom-call | flops 1 | bytes 1 | tf_op jit(solution)/shard_map/partial_weights/pallas_call | solution.py:304
  68.9 3.6 %own_rows.1 = (bf16[256,2048]{1,0:T(8,128)(2,1)S(1)}, bf16[128,1024]{1,0:T(8,128)(2,1)}) custom-call(s32[8,128]{1,0:T(8,128)S(1)} %copy-done.18, bf16[1024,2048]{1,0:T(8,128)(2,1)S(1)} %copy-done.1, f32[2048,256]{1,0:T(8,128)S(1)} %partial_weights.1.rest_0_.refs_1_.refs_2_.refs_0_), custom_call_target="tpu_custom_call" | custom-call | flops 1 | bytes 1 | tf_op jit(solution)/shard_map/own_rows/pallas_call | solution.py:205
  72.6 1.0 copy-done.4
  73.6 0.5 collective-permute-start.30
  74.1 1.2 %collective-permute-done.29.refs_0_ = bf16[128,1024]{1,0:T(8,128)(2,1)S(1)} collective-permute-done((bf16[128,1024]{1,0:T(8,128)(2,1)}, bf16[128,1024]{1,0:T(8,128)(2,1)S(1)}, u32[]{:S(2)}, u32[]{:S(2)}) %collective-permute-start.29) | collective-permute-done | bytes 262176 | tf_op jit(solution)/shard_map/ppermute | solution.py:23
  75.5 0.4 collective-permute-start.25
  76.8 1.2 %collective-permute-done.28.refs_9_.refs_0_ = bf16[256,1024]{1,0:T(8,128)(2,1)} collective-permute-done((bf16[256,1024]{1,0:T(8,128)(2,1)}, bf16[256,1024]{1,0:T(8,128)(2,1)}, u32[]{:S(2)}, u32[]{:S(2)}) %collective-permute-start.28) | collective-permute-done | bytes 524320 | tf_op jit(solution)/shard_map/ppermute | solution.py:27
  78.1 0.5 collective-permute-start.35
  78.6 0.7 collective-permute-done.31.refs_1_
  79.5 3.2 %collective-permute-done.33.refs_0_ = bf16[256,1024]{1,0:T(8,128)(2,1)} collective-permute-done((bf16[256,1024]{1,0:T(8,128)(2,1)}, bf16[256,1024]{1,0:T(8,128)(2,1)}, u32[]{:S(2)}, u32[]{:S(2)}) %collective-permute-start.33) | collective-permute-done | bytes 524320 | tf_op jit(solution)/shard_map/ppermute | solution.py:23
  82.7 1.5 %collective-permute-start.37 = (bf16[64,1024]{1,0:T(8,128)(2,1)S(1)}, bf16[64,1024]{1,0:T(8,128)(2,1)S(1)}, u32[]{:S(2)}, u32[]{:S(2)}) collective-permute-start(bf16[64,1024]{1,0:T(8,128)(2,1)S(1)} %after.19.refs_3_), channel_id=1, source_target_pairs={{0,12},{4,0},{8,4},{12,8},{1,13},{5,1},{9,5},{13,9},{2,14},{6,2},{... | collective-permute-start | bytes 393224 | tf_op jit(solution)/shard_map/ppermute | solution.py:23
  84.8 4.2 %early_scores.1 = (bf16[2048,512]{1,0:T(8,128)(2,1)S(1)}, f32[1024,128]{1,0:T(8,128)S(1)}, bf16[1024,128]{1,0:T(8,128)(2,1)S(1)}) custom-call(s32[4,4]{1,0:T(4,128)S(1)} %get-tuple-element.54.table_ref, f32[2048,256]{1,0:T(8,128)S(1)} %partial_weights.1.rest_0_.refs_1_.refs_2_.refs_0_, bf16[2048,256]{1,0:T(8,128)(2,1)} %collective-permute-done.20.refs_1_, ...), custom_call_target="tpu_custom_call" | custom-call | flops 1 | bytes 1 | tf_op jit(solution)/shard_map/early_scores/pallas_call | solution.py:529
  88.9 1.1 %collective-permute-start.36 = (bf16[1024,128]{1,0:T(8,128)(2,1)S(1)}, bf16[1024,128]{1,0:T(8,128)(2,1)S(1)}, u32[]{:S(2)}, u32[]{:S(2)}) collective-permute-start(bf16[1024,128]{1,0:T(8,128)(2,1)S(1)} %get-tuple-element.92.refs_1_), channel_id=1, source_target_pairs={{0,2},{2,0},{1,3},{3,1},{4,6},{6,4},{5,7},{7,5},{8,10},{10,8},{9,1... | collective-permute-start | bytes 786440 | tf_op jit(solution)/shard_map/ppermute | solution.py:23
  90.1 1.7 %collective-permute-done.39.refs_0_ = bf16[64,1024]{1,0:T(8,128)(2,1)S(1)} collective-permute-done((bf16[64,1024]{1,0:T(8,128)(2,1)S(1)}, bf16[64,1024]{1,0:T(8,128)(2,1)S(1)}, u32[]{:S(2)}, u32[]{:S(2)}) %collective-permute-start.39) | collective-permute-done | bytes 131104 | tf_op jit(solution)/shard_map/ppermute | solution.py:23
  91.8 1.7 %collective-permute-done.41.refs_0_ = bf16[48,1024]{1,0:T(8,128)(2,1)S(1)} collective-permute-done((bf16[48,1024]{1,0:T(8,128)(2,1)S(1)}, bf16[48,1024]{1,0:T(8,128)(2,1)S(1)}, u32[]{:S(2)}, u32[]{:S(2)}) %collective-permute-start.41) | collective-permute-done | bytes 98336 | tf_op jit(solution)/shard_map/ppermute | solution.py:23
  93.5 1.3 %collective-permute-done.42.refs_9_ = bf16[48,1024]{1,0:T(8,128)(2,1)S(1)} collective-permute-done((bf16[48,1024]{1,0:T(8,128)(2,1)S(1)}, bf16[48,1024]{1,0:T(8,128)(2,1)S(1)}, u32[]{:S(2)}, u32[]{:S(2)}) %collective-permute-start.42) | collective-permute-done | bytes 98336 | tf_op jit(solution)/shard_map/ppermute | solution.py:23
  94.8 0.7 late_scores.1
  95.5 0.6 collective-permute-start.43
  96.2 3.7 %collective-permute-done.43.refs_3_ = bf16[256,128]{1,0:T(8,128)(2,1)S(1)} collective-permute-done((bf16[256,128]{1,0:T(8,128)(2,1)S(1)}, bf16[256,128]{1,0:T(8,128)(2,1)S(1)}, u32[]{:S(2)}, u32[]{:S(2)}) %collective-permute-start.43) | collective-permute-done | bytes 65568 | tf_op jit(solution)/shard_map/ppermute | solution.py:23
  99.9 1.7 %merge.1 = f32[128,1024]{1,0:T(8,128)} custom-call(s32[4,4]{1,0:T(4,128)S(1)} %get-tuple-element.54.table_ref, f32[1024,128]{1,0:T(8,128)S(1)} %get-tuple-element.91.refs_0_, bf16[1024,128]{1,0:T(8,128)(2,1)S(1)} %collective-permute-done.36.refs_1_, f32[256,128]{1,0:T(8,128)S(1)} %get-tuple-element.94.refs_2_, ...), custom_call_target="tpu_custom_call" | custom-call | flops 1 | bytes 1 | tf_op jit(solution)/shard_map/merge/pallas_call | solution.py:589
  (114 shorter events, 3.4 us)
Async XLA Ops:
  0.0 22.7 %copy-start.15 = (s32[4096]{0:T(1024)S(1)}, s32[4096]{0:T(1024)}, u32[]{:S(2)}) copy-start(s32[4096]{0:T(1024)} %param.9) | copy-start | bytes 49156
  0.0 21.4 %collective-permute-start.7 = (bf16[4096,1024]{1,0:T(8,128)(2,1)}, bf16[4096,1024]{1,0:T(8,128)(2,1)}, u32[]{:S(2)}, u32[]{:S(2)}) collective-permute-start(bf16[4096,1024]{1,0:T(8,128)(2,1)} %bitcast.6), channel_id=1, source_target_pairs={{0,1},{1,0},{2,3},{3,2},{4,5},{5,4},{6,7},{7,6},{8,9},{9,8},{10,11... | collective-permute-start | bytes 25165832 | tf_op jit(solution)/shard_map/ppermute | solution.py:23
  3.1 14.4 %collective-permute-start.4 = (bf16[1,64,1024]{2,1,0:T(8,128)(2,1)}, bf16[1,64,1024]{2,1,0:T(8,128)(2,1)S(1)}, u32[]{:S(2)}, u32[]{:S(2)}) collective-permute-start(bf16[1,64,1024]{2,1,0:T(8,128)(2,1)} %get-tuple-element.51), channel_id=1, source_target_pairs={{0,4},{4,8},{8,12},{12,0},{1,5},{5,9},{9,13},{13,1},{2,6},{6,10},{... | collective-permute-start | bytes 393224 | tf_op jit(solution)/shard_map/ppermute | solution.py:23
  5.9 12.4 %collective-permute-start.5 = (bf16[1,64,1024]{2,1,0:T(8,128)(2,1)}, bf16[1,64,1024]{2,1,0:T(8,128)(2,1)S(1)}, u32[]{:S(2)}, u32[]{:S(2)}) collective-permute-start(bf16[1,64,1024]{2,1,0:T(8,128)(2,1)} %get-tuple-element.52), channel_id=1, source_target_pairs={{0,8},{4,12},{8,0},{12,4},{1,9},{5,13},{9,1},{13,5},{2,10},{6,14},... | collective-permute-start | bytes 393224 | tf_op jit(solution)/shard_map/ppermute | solution.py:23
  8.5 10.9 %collective-permute-start.6 = (bf16[1,64,1024]{2,1,0:T(8,128)(2,1)}, bf16[1,64,1024]{2,1,0:T(8,128)(2,1)S(1)}, u32[]{:S(2)}, u32[]{:S(2)}) collective-permute-start(bf16[1,64,1024]{2,1,0:T(8,128)(2,1)} %get-tuple-element.53), channel_id=1, source_target_pairs={{0,12},{4,0},{8,4},{12,8},{1,13},{5,1},{9,5},{13,9},{2,14},{6,2},{... | collective-permute-start | bytes 393224 | tf_op jit(solution)/shard_map/ppermute | solution.py:23
  9.9 10.4 %collective-permute-start.8 = (bf16[1,64,1024]{2,1,0:T(8,128)(2,1)}, bf16[1,64,1024]{2,1,0:T(8,128)(2,1)S(1)}, u32[]{:S(2)}, u32[]{:S(2)}) collective-permute-start(bf16[1,64,1024]{2,1,0:T(8,128)(2,1)} %get-tuple-element.55.refs_0_), channel_id=1, source_target_pairs={{0,16},{16,0},{1,17},{17,1},{2,18},{18,2},{3,19},{19,3},{4,20},{20... | collective-permute-start | bytes 393224 | tf_op jit(solution)/shard_map/ppermute | solution.py:23
  17.5 39.7 %collective-permute-start.21 = (bf16[256,1024]{1,0:T(8,128)(2,1)}, bf16[256,1024]{1,0:T(8,128)(2,1)S(1)}, u32[]{:S(2)}, u32[]{:S(2)}) collective-permute-start(bf16[256,1024]{1,0:T(8,128)(2,1)} %after.18), channel_id=1, source_target_pairs={{0,4},{4,8},{8,12},{12,0},{1,5},{5,9},{9,13},{13,1},{2,6},{6,10},{... | collective-permute-start | bytes 1572872 | tf_op jit(solution)/shard_map/ppermute | solution.py:23
  18.3 11.2 %collective-permute-start.9 = (bf16[1,64,1024]{2,1,0:T(8,128)(2,1)S(1)}, bf16[1,64,1024]{2,1,0:T(8,128)(2,1)S(1)}, u32[]{:S(2)}, u32[]{:S(2)}) collective-permute-start(bf16[1,64,1024]{2,1,0:T(8,128)(2,1)S(1)} %collective-permute-done.4.rest_0_.refs_2_.refs_1_), channel_id=1, source_target_pairs={{0,16},{16,0},{1,17},{17,1},{2,18},{18,2},{3,19},{19,3},{4,20},{20... | collective-permute-start | bytes 393224 | tf_op jit(solution)/shard_map/ppermute | solution.py:23
  19.4 10.1 %collective-permute-start.10 = (bf16[1,64,1024]{2,1,0:T(8,128)(2,1)S(1)}, bf16[1,64,1024]{2,1,0:T(8,128)(2,1)S(1)}, u32[]{:S(2)}, u32[]{:S(2)}) collective-permute-start(bf16[1,64,1024]{2,1,0:T(8,128)(2,1)S(1)} %collective-permute-done.5.rest_1_.refs_3_.refs_2_), channel_id=1, source_target_pairs={{0,16},{16,0},{1,17},{17,1},{2,18},{18,2},{3,19},{19,3},{4,20},{20... | collective-permute-start | bytes 393224 | tf_op jit(solution)/shard_map/ppermute | solution.py:23
  20.3 9.2 %collective-permute-start.11 = (bf16[1,64,1024]{2,1,0:T(8,128)(2,1)S(1)}, bf16[1,64,1024]{2,1,0:T(8,128)(2,1)S(1)}, u32[]{:S(2)}, u32[]{:S(2)}) collective-permute-start(bf16[1,64,1024]{2,1,0:T(8,128)(2,1)S(1)} %collective-permute-done.6.rest_2_.refs_4_.refs_3_), channel_id=1, source_target_pairs={{0,16},{16,0},{1,17},{17,1},{2,18},{18,2},{3,19},{19,3},{4,20},{20... | collective-permute-start | bytes 393224 | tf_op jit(solution)/shard_map/ppermute | solution.py:23
  21.4 33.6 %collective-permute-start.27 = (bf16[128,1024]{1,0:T(8,128)(2,1)}, bf16[128,1024]{1,0:T(8,128)(2,1)S(1)}, u32[]{:S(2)}, u32[]{:S(2)}) collective-permute-start(bf16[128,1024]{1,0:T(8,128)(2,1)} %after.26), channel_id=1, source_target_pairs={{0,8},{4,12},{8,0},{12,4},{1,9},{5,13},{9,1},{13,5},{2,10},{6,14},... | collective-permute-start | bytes 786440 | tf_op jit(solution)/shard_map/ppermute | solution.py:27
  29.5 20.8 %copy-start.16 = (bf16[32,1024]{1,0:T(8,128)(2,1)S(1)}, bf16[32,1024]{1,0:T(8,128)(2,1)}, u32[]{:S(2)}) copy-start(bf16[32,1024]{1,0:T(8,128)(2,1)} %get-tuple-element.82.refs_0_) | copy-start | bytes 196612
  30.8 1.3 %collective-permute-start.12 = (bf16[128,256]{1,0:T(8,128)(2,1)S(1)}, bf16[128,256]{1,0:T(8,128)(2,1)S(1)}, u32[]{:S(2)}, u32[]{:S(2)}) collective-permute-start(bf16[128,256]{1,0:T(8,128)(2,1)S(1)} %get-tuple-element.67), channel_id=1, source_target_pairs={{0,1},{1,0},{2,3},{3,2},{4,5},{5,4},{6,7},{7,6},{8,9},{9,8},{10,11... | collective-permute-start | bytes 196616 | tf_op jit(solution)/shard_map/ppermute | solution.py:23
  30.9 1.4 %collective-permute-start.13 = (bf16[128,256]{1,0:T(8,128)(2,1)S(1)}, bf16[128,256]{1,0:T(8,128)(2,1)S(1)}, u32[]{:S(2)}, u32[]{:S(2)}) collective-permute-start(bf16[128,256]{1,0:T(8,128)(2,1)S(1)} %get-tuple-element.68), channel_id=1, source_target_pairs={{0,1},{1,0},{2,3},{3,2},{4,5},{5,4},{6,7},{7,6},{8,9},{9,8},{10,11... | collective-permute-start | bytes 196616 | tf_op jit(solution)/shard_map/ppermute | solution.py:23
  31.4 1.3 %collective-permute-start.14 = (bf16[128,256]{1,0:T(8,128)(2,1)S(1)}, bf16[128,256]{1,0:T(8,128)(2,1)S(1)}, u32[]{:S(2)}, u32[]{:S(2)}) collective-permute-start(bf16[128,256]{1,0:T(8,128)(2,1)S(1)} %get-tuple-element.69), channel_id=1, source_target_pairs={{0,1},{1,0},{2,3},{3,2},{4,5},{5,4},{6,7},{7,6},{8,9},{9,8},{10,11... | collective-permute-start | bytes 196616 | tf_op jit(solution)/shard_map/ppermute | solution.py:23
  32.1 1.3 %collective-permute-start.15 = (bf16[128,256]{1,0:T(8,128)(2,1)S(1)}, bf16[128,256]{1,0:T(8,128)(2,1)S(1)}, u32[]{:S(2)}, u32[]{:S(2)}) collective-permute-start(bf16[128,256]{1,0:T(8,128)(2,1)S(1)} %get-tuple-element.70), channel_id=1, source_target_pairs={{0,1},{1,0},{2,3},{3,2},{4,5},{5,4},{6,7},{7,6},{8,9},{9,8},{10,11... | collective-permute-start | bytes 196616 | tf_op jit(solution)/shard_map/ppermute | solution.py:23
  32.3 1.3 %collective-permute-start.16 = (bf16[128,256]{1,0:T(8,128)(2,1)S(1)}, bf16[128,256]{1,0:T(8,128)(2,1)S(1)}, u32[]{:S(2)}, u32[]{:S(2)}) collective-permute-start(bf16[128,256]{1,0:T(8,128)(2,1)S(1)} %get-tuple-element.71), channel_id=1, source_target_pairs={{0,1},{1,0},{2,3},{3,2},{4,5},{5,4},{6,7},{7,6},{8,9},{9,8},{10,11... | collective-permute-start | bytes 196616 | tf_op jit(solution)/shard_map/ppermute | solution.py:23
  32.6 1.3 %collective-permute-start.17 = (bf16[128,256]{1,0:T(8,128)(2,1)S(1)}, bf16[128,256]{1,0:T(8,128)(2,1)S(1)}, u32[]{:S(2)}, u32[]{:S(2)}) collective-permute-start(bf16[128,256]{1,0:T(8,128)(2,1)S(1)} %get-tuple-element.72), channel_id=1, source_target_pairs={{0,1},{1,0},{2,3},{3,2},{4,5},{5,4},{6,7},{7,6},{8,9},{9,8},{10,11... | collective-permute-start | bytes 196616 | tf_op jit(solution)/shard_map/ppermute | solution.py:23
  33.4 17.0 %collective-permute-start.18 = (bf16[128,256]{1,0:T(8,128)(2,1)S(1)}, bf16[128,256]{1,0:T(8,128)(2,1)S(1)}, u32[]{:S(2)}, u32[]{:S(2)}) collective-permute-start(bf16[128,256]{1,0:T(8,128)(2,1)S(1)} %get-tuple-element.73), channel_id=1, source_target_pairs={{0,1},{1,0},{2,3},{3,2},{4,5},{5,4},{6,7},{7,6},{8,9},{9,8},{10,11... | collective-permute-start | bytes 196616 | tf_op jit(solution)/shard_map/ppermute | solution.py:23
  33.5 17.6 %collective-permute-start.19 = (bf16[128,256]{1,0:T(8,128)(2,1)S(1)}, bf16[128,256]{1,0:T(8,128)(2,1)S(1)}, u32[]{:S(2)}, u32[]{:S(2)}) collective-permute-start(bf16[128,256]{1,0:T(8,128)(2,1)S(1)} %get-tuple-element.74), channel_id=1, source_target_pairs={{0,1},{1,0},{2,3},{3,2},{4,5},{5,4},{6,7},{7,6},{8,9},{9,8},{10,11... | collective-permute-start | bytes 196616 | tf_op jit(solution)/shard_map/ppermute | solution.py:23
  33.9 23.3 %collective-permute-start.22 = (bf16[48,1024]{1,0:T(8,128)(2,1)S(1)}, bf16[48,1024]{1,0:T(8,128)(2,1)S(1)}, u32[]{:S(2)}, u32[]{:S(2)}) collective-permute-start(bf16[48,1024]{1,0:T(8,128)(2,1)S(1)} %after.22), channel_id=1, source_target_pairs={{0,12},{4,0},{8,4},{12,8},{1,13},{5,1},{9,5},{13,9},{2,14},{6,2},{... | collective-permute-start | bytes 294920 | tf_op jit(solution)/shard_map/ppermute | solution.py:23
  50.4 6.8 %collective-permute-start.24 = (bf16[32,1024]{1,0:T(8,128)(2,1)S(1)}, bf16[32,1024]{1,0:T(8,128)(2,1)S(1)}, u32[]{:S(2)}, u32[]{:S(2)}) collective-permute-start(bf16[32,1024]{1,0:T(8,128)(2,1)S(1)} %after.24), channel_id=1, source_target_pairs={{0,12},{4,0},{8,4},{12,8},{1,13},{5,1},{9,5},{13,9},{2,14},{6,2},{... | collective-permute-start | bytes 196616 | tf_op jit(solution)/shard_map/ppermute | solution.py:23
  51.1 11.0 %slice-start = ((s8[8388608]{0:T(1024)(128)(4,1)}), s8[4194304]{0:T(1024)(128)(4,1)S(1)}, s32[]{:S(2)}) async-start(s8[8388608]{0:T(1024)(128)(4,1)} %bitcast.8), calls=%async_computation | async-start | bytes 8388608
  51.1 11.0 %slice-start.1 = ((s8[8388608]{0:T(1024)(128)(4,1)}), s8[4194304]{0:T(1024)(128)(4,1)S(1)}, s32[]{:S(2)}) async-start(s8[8388608]{0:T(1024)(128)(4,1)} %bitcast.8), calls=%async_computation.1 | async-start | bytes 8388608
  53.5 30.7 %collective-permute-start.20 = (bf16[2048,256]{1,0:T(8,128)(2,1)S(1)}, bf16[2048,256]{1,0:T(8,128)(2,1)}, u32[]{:S(2)}, u32[]{:S(2)}) collective-permute-start(bf16[2048,256]{1,0:T(8,128)(2,1)S(1)} %fetched_weights.1.refs_18_.refs_2_.refs_5_), channel_id=1, source_target_pairs={{0,2},{2,0},{1,3},{3,1},{4,6},{6,4},{5,7},{7,5},{8,10},{10,8},{9,1... | collective-permute-start | bytes 3145736 | tf_op jit(solution)/shard_map/ppermute | solution.py:23
  55.9 22.2 %collective-permute-start.28 = (bf16[256,1024]{1,0:T(8,128)(2,1)}, bf16[256,1024]{1,0:T(8,128)(2,1)}, u32[]{:S(2)}, u32[]{:S(2)}) collective-permute-start(bf16[256,1024]{1,0:T(8,128)(2,1)} %stack.3), channel_id=1, source_target_pairs={{0,4},{4,0},{8,12},{12,8},{1,5},{5,1},{9,13},{13,9},{2,6},{6,2},{1... | collective-permute-start | bytes 1572872 | tf_op jit(solution)/shard_map/ppermute | solution.py:27
  57.2 4.9 %copy-start.8 = (bf16[32,1024]{1,0:T(8,128)(2,1)}, bf16[32,1024]{1,0:T(8,128)(2,1)S(1)}, u32[]{:S(2)}) copy-start(bf16[32,1024]{1,0:T(8,128)(2,1)S(1)} %collective-permute-done.24.refs_0_.refs_4_) | copy-start | bytes 196612
  57.2 4.9 %copy-start.2 = (bf16[256,1024]{1,0:T(8,128)(2,1)}, bf16[256,1024]{1,0:T(8,128)(2,1)S(1)}, u32[]{:S(2)}) copy-start(bf16[256,1024]{1,0:T(8,128)(2,1)S(1)} %collective-permute-done.21.refs_0_.refs_1_) | copy-start | bytes 1572868
  57.2 25.4 %collective-permute-start.33 = (bf16[256,1024]{1,0:T(8,128)(2,1)}, bf16[256,1024]{1,0:T(8,128)(2,1)}, u32[]{:S(2)}, u32[]{:S(2)}) collective-permute-start(bf16[256,1024]{1,0:T(8,128)(2,1)} %after.30), channel_id=1, source_target_pairs={{0,8},{4,12},{8,0},{12,4},{1,9},{5,13},{9,1},{13,5},{2,10},{6,14},... | collective-permute-start | bytes 1572872 | tf_op jit(solution)/shard_map/ppermute | solution.py:23
  57.3 3.7 %collective-permute-start.26 = (s32[8,128]{1,0:T(8,128)S(1)}, s32[8,128]{1,0:T(8,128)S(1)}, u32[]{:S(2)}, u32[]{:S(2)}) collective-permute-start(s32[8,128]{1,0:T(8,128)S(1)} %get-tuple-element.58.refs_10_), channel_id=1, source_target_pairs={{0,16},{16,0},{1,17},{17,1},{2,18},{18,2},{3,19},{19,3},{4,20},{20... | collective-permute-start | bytes 12296 | tf_op jit(solution)/shard_map/ppermute | solution.py:23
  62.1 6.8 %copy-start.1 = (bf16[1024,2048]{1,0:T(8,128)(2,1)S(1)}, bf16[1024,2048]{1,0:T(8,128)(2,1)}, u32[]{:S(2)}) copy-start(bf16[1024,2048]{1,0:T(8,128)(2,1)} %train_ref.3) | copy-start | bytes 12582916
  62.1 6.8 %copy-start.18 = (s32[8,128]{1,0:T(8,128)S(1)}, s32[8,128]{1,0:T(8,128)}, u32[]{:S(2)}) copy-start(s32[8,128]{1,0:T(8,128)} %get-tuple-element.75.goal_ref) | copy-start | bytes 12292
  73.6 1.7 %collective-permute-start.29 = (bf16[128,1024]{1,0:T(8,128)(2,1)}, bf16[128,1024]{1,0:T(8,128)(2,1)S(1)}, u32[]{:S(2)}, u32[]{:S(2)}) collective-permute-start(bf16[128,1024]{1,0:T(8,128)(2,1)} %get-tuple-element.85.refs_0_), channel_id=1, source_target_pairs={{0,1},{1,0},{2,3},{3,2},{4,5},{5,4},{6,7},{7,6},{8,9},{9,8},{10,11... | collective-permute-start | bytes 786440 | tf_op jit(solution)/shard_map/ppermute | solution.py:23
  73.6 1.9 %collective-permute-start.30 = (bf16[128,1024]{1,0:T(8,128)(2,1)S(1)}, bf16[128,1024]{1,0:T(8,128)(2,1)S(1)}, u32[]{:S(2)}, u32[]{:S(2)}) collective-permute-start(bf16[128,1024]{1,0:T(8,128)(2,1)S(1)} %after.27.refs_1_), channel_id=1, source_target_pairs={{0,1},{1,0},{2,3},{3,2},{4,5},{5,4},{6,7},{7,6},{8,9},{9,8},{10,11... | collective-permute-start | bytes 786440 | tf_op jit(solution)/shard_map/ppermute | solution.py:23
  75.3 1.5 %collective-permute-start.23 = (bf16[48,1024]{1,0:T(8,128)(2,1)S(1)}, bf16[48,1024]{1,0:T(8,128)(2,1)S(1)}, u32[]{:S(2)}, u32[]{:S(2)}) collective-permute-start(bf16[48,1024]{1,0:T(8,128)(2,1)S(1)} %after.23.refs_0_), channel_id=1, source_target_pairs={{0,1},{1,0},{2,3},{3,2},{4,5},{5,4},{6,7},{7,6},{8,9},{9,8},{10,11... | collective-permute-start | bytes 294920 | tf_op jit(solution)/shard_map/ppermute | solution.py:23
  75.5 1.3 %collective-permute-start.25 = (bf16[32,1024]{1,0:T(8,128)(2,1)S(1)}, bf16[32,1024]{1,0:T(8,128)(2,1)S(1)}, u32[]{:S(2)}, u32[]{:S(2)}) collective-permute-start(bf16[32,1024]{1,0:T(8,128)(2,1)S(1)} %after.25.refs_2_), channel_id=1, source_target_pairs={{0,1},{1,0},{2,3},{3,2},{4,5},{5,4},{6,7},{7,6},{8,9},{9,8},{10,11... | collective-permute-start | bytes 196616 | tf_op jit(solution)/shard_map/ppermute | solution.py:23
  78.1 1.2 %collective-permute-start.31 = (s32[8,128]{1,0:T(8,128)S(1)}, s32[8,128]{1,0:T(8,128)S(1)}, u32[]{:S(2)}, u32[]{:S(2)}) collective-permute-start(s32[8,128]{1,0:T(8,128)S(1)} %after.28), channel_id=1, source_target_pairs={{0,1},{1,0},{2,3},{3,2},{4,5},{5,4},{6,7},{7,6},{8,9},{9,8},{10,11... | collective-permute-start | bytes 12296 | tf_op jit(solution)/shard_map/ppermute | solution.py:23
  78.1 6.2 %collective-permute-start.35 = (bf16[256,1024]{1,0:T(8,128)(2,1)}, bf16[256,1024]{1,0:T(8,128)(2,1)S(1)}, u32[]{:S(2)}, u32[]{:S(2)}) collective-permute-start(bf16[256,1024]{1,0:T(8,128)(2,1)} %after.32.refs_9_), channel_id=1, source_target_pairs={{0,1},{1,0},{2,3},{3,2},{4,5},{5,4},{6,7},{7,6},{8,9},{9,8},{10,11... | collective-permute-start | bytes 1572872 | tf_op jit(solution)/shard_map/ppermute | solution.py:23
  79.3 5.1 %collective-permute-start.32 = (bf16[256,1024]{1,0:T(8,128)(2,1)S(1)}, bf16[256,1024]{1,0:T(8,128)(2,1)S(1)}, u32[]{:S(2)}, u32[]{:S(2)}) collective-permute-start(bf16[256,1024]{1,0:T(8,128)(2,1)S(1)} %after.29.refs_3_), channel_id=1, source_target_pairs={{0,1},{1,0},{2,3},{3,2},{4,5},{5,4},{6,7},{7,6},{8,9},{9,8},{10,11... | collective-permute-start | bytes 1572872 | tf_op jit(solution)/shard_map/ppermute | solution.py:23
  82.7 2.1 %collective-permute-start.34 = (bf16[256,1024]{1,0:T(8,128)(2,1)}, bf16[256,1024]{1,0:T(8,128)(2,1)S(1)}, u32[]{:S(2)}, u32[]{:S(2)}) collective-permute-start(bf16[256,1024]{1,0:T(8,128)(2,1)} %after.31.refs_5_), channel_id=1, source_target_pairs={{0,1},{1,0},{2,3},{3,2},{4,5},{5,4},{6,7},{7,6},{8,9},{9,8},{10,11... | collective-permute-start | bytes 1572872 | tf_op jit(solution)/shard_map/ppermute | solution.py:23
  82.7 7.4 %collective-permute-start.37 = (bf16[64,1024]{1,0:T(8,128)(2,1)S(1)}, bf16[64,1024]{1,0:T(8,128)(2,1)S(1)}, u32[]{:S(2)}, u32[]{:S(2)}) collective-permute-start(bf16[64,1024]{1,0:T(8,128)(2,1)S(1)} %after.19.refs_3_), channel_id=1, source_target_pairs={{0,12},{4,0},{8,4},{12,8},{1,13},{5,1},{9,5},{13,9},{2,14},{6,2},{... | collective-permute-start | bytes 393224 | tf_op jit(solution)/shard_map/ppermute | solution.py:23
  84.2 7.6 %collective-permute-start.39 = (bf16[64,1024]{1,0:T(8,128)(2,1)S(1)}, bf16[64,1024]{1,0:T(8,128)(2,1)S(1)}, u32[]{:S(2)}, u32[]{:S(2)}) collective-permute-start(bf16[64,1024]{1,0:T(8,128)(2,1)S(1)} %after.20.refs_4_), channel_id=1, source_target_pairs={{0,12},{4,0},{8,4},{12,8},{1,13},{5,1},{9,5},{13,9},{2,14},{6,2},{... | collective-permute-start | bytes 393224 | tf_op jit(solution)/shard_map/ppermute | solution.py:23
  84.4 9.1 %collective-permute-start.41 = (bf16[48,1024]{1,0:T(8,128)(2,1)S(1)}, bf16[48,1024]{1,0:T(8,128)(2,1)S(1)}, u32[]{:S(2)}, u32[]{:S(2)}) collective-permute-start(bf16[48,1024]{1,0:T(8,128)(2,1)S(1)} %after.21.refs_5_), channel_id=1, source_target_pairs={{0,12},{4,0},{8,4},{12,8},{1,13},{5,1},{9,5},{13,9},{2,14},{6,2},{... | collective-permute-start | bytes 294920 | tf_op jit(solution)/shard_map/ppermute | solution.py:23
  88.9 10.9 %collective-permute-start.36 = (bf16[1024,128]{1,0:T(8,128)(2,1)S(1)}, bf16[1024,128]{1,0:T(8,128)(2,1)S(1)}, u32[]{:S(2)}, u32[]{:S(2)}) collective-permute-start(bf16[1024,128]{1,0:T(8,128)(2,1)S(1)} %get-tuple-element.92.refs_1_), channel_id=1, source_target_pairs={{0,2},{2,0},{1,3},{3,1},{4,6},{6,4},{5,7},{7,5},{8,10},{10,8},{9,1... | collective-permute-start | bytes 786440 | tf_op jit(solution)/shard_map/ppermute | solution.py:23
  90.1 4.7 %collective-permute-start.38 = (bf16[64,1024]{1,0:T(8,128)(2,1)S(1)}, bf16[64,1024]{1,0:T(8,128)(2,1)S(1)}, u32[]{:S(2)}, u32[]{:S(2)}) collective-permute-start(bf16[64,1024]{1,0:T(8,128)(2,1)S(1)} %after.33.refs_4_), channel_id=1, source_target_pairs={{0,1},{1,0},{2,3},{3,2},{4,5},{5,4},{6,7},{7,6},{8,9},{9,8},{10,11... | collective-permute-start | bytes 393224 | tf_op jit(solution)/shard_map/ppermute | solution.py:23
  91.8 3.0 %collective-permute-start.40 = (bf16[64,1024]{1,0:T(8,128)(2,1)S(1)}, bf16[64,1024]{1,0:T(8,128)(2,1)S(1)}, u32[]{:S(2)}, u32[]{:S(2)}) collective-permute-start(bf16[64,1024]{1,0:T(8,128)(2,1)S(1)} %after.34.refs_6_), channel_id=1, source_target_pairs={{0,1},{1,0},{2,3},{3,2},{4,5},{5,4},{6,7},{7,6},{8,9},{9,8},{10,11... | collective-permute-start | bytes 393224 | tf_op jit(solution)/shard_map/ppermute | solution.py:23
  93.5 1.3 %collective-permute-start.42 = (bf16[48,1024]{1,0:T(8,128)(2,1)S(1)}, bf16[48,1024]{1,0:T(8,128)(2,1)S(1)}, u32[]{:S(2)}, u32[]{:S(2)}) collective-permute-start(bf16[48,1024]{1,0:T(8,128)(2,1)S(1)} %after.35.refs_8_), channel_id=1, source_target_pairs={{0,1},{1,0},{2,3},{3,2},{4,5},{5,4},{6,7},{7,6},{8,9},{9,8},{10,11... | collective-permute-start | bytes 294920 | tf_op jit(solution)/shard_map/ppermute | solution.py:23
  95.5 4.3 %collective-permute-start.43 = (bf16[256,128]{1,0:T(8,128)(2,1)S(1)}, bf16[256,128]{1,0:T(8,128)(2,1)S(1)}, u32[]{:S(2)}, u32[]{:S(2)}) collective-permute-start(bf16[256,128]{1,0:T(8,128)(2,1)S(1)} %get-tuple-element.95), channel_id=1, source_target_pairs={{0,2},{2,0},{1,3},{3,1},{4,6},{6,4},{5,7},{7,5},{8,10},{10,8},{9,1... | collective-permute-start | bytes 196616 | tf_op jit(solution)/shard_map/ppermute | solution.py:23
  (14 other events, 33.1 us)

commit v21 on v19

--- a/solution.py
+++ b/solution.py
@@ -616,7 +616,7 @@
     *packed, goal = pack_rows(train, ids, columns, bulk, extra, middle + final)
     firsts, seconds = [], []
     parts = [pieces] + [[shift(x, "groups", n_group, d) for x in pieces] for d in range(1, n_group)]
-    here = [shift(after(packed[0], *pieces[1:]), "shard", n_shard, 1)]
+    here = [shift(after(packed[0], pieces[1], pieces[-1]), "shard", n_shard, 1)]
     urgent = [here[0]]
     if extra:
         far = swap(after(packed[-2], *pieces[1:]), "shard", n_shard, 2)

time: 94.6 us -> 104 us (1.099)
  starting transfers between devices: 37.9 us -> 43.7 us
  waiting for transfers between devices: 17.8 us -> 21.6 us
    ppermute x38, starting transfers between devices: 33.8 us -> 43.7 us  [shift(): return lax.ppermute(x, axis, [(i, (i + by) % size) for i in range(size)])]
    ppermute x2, starting transfers between devices: 4.05 us -> 0.05 us  [swap(): return lax.ppermute(x, axis, [(i, i ^ bit) for i in range(size)])]
    ppermute x38, waiting for transfers between devices: 14.8 us -> 16.9 us  [shift(): return lax.ppermute(x, axis, [(i, (i + by) % size) for i in range(size)])]
    ppermute x2, waiting for transfers between devices: 2.93 us -> 4.63 us  [swap(): return lax.ppermute(x, axis, [(i, i ^ bit) for i in range(size)])]
  transfers between devices with their start and end apart: 40 -> 40, of which waited for: 13 -> 13; matrix products, arithmetic and copies ran while one was open for 1% -> 0% of each run, Pallas kernels for 33% -> 30%
where the time goes in v21:
time: 104 us
  starting transfers between devices  43.7 us (42%)
  Pallas kernels  32.7 us (31%)
  waiting for transfers between devices  21.6 us (21%)
  local copies, waits for them, and re-layouts  4.79 us (5%)
  between operations  1.08 us (1%)
    ppermute x38, starting transfers between devices, shift(): return lax.ppermute(x, axis, [(i, (i + by) % size) for i in range(size)])  43.7 us
    ppermute x38, waiting for transfers between devices, shift(): return lax.ppermute(x, axis, [(i, (i + by) % size) for i in range(size)])  16.9 us
    pallas_call x1, Pallas kernels, pack_rows(): pl.pallas_call(kernel, grid=(1,), in_specs=[pl.BlockSpec((lines, LANES),...  6.6 us
    pallas_call x1, Pallas kernels, partial_weights(): pl.pallas_call(kernel, in_specs=[SMEM] + [HBM] * n + [VMEM] * (CUTS * n)...  6.6 us
    ppermute x2, waiting for transfers between devices, swap(): return lax.ppermute(x, axis, [(i, i ^ bit) for i in range(size)])  4.63 us
    unnamed x42, local copies, waits for them, and re-layouts  4.3 us
    pallas_call x1, Pallas kernels, early_scores(): pl.pallas_call(kernel, in_specs=[SMEM] + [VMEM] * (2 + n_other + n_rep *...  4.16 us
    pallas_call x1, Pallas kernels, pick_queries(): pl.pallas_call(kernel, in_specs=[SMEM, SMEM, ANY], out_specs=[VMEM] * n_c...  2.67 us
  transfers between devices with their start and end apart: 40, of which 13 were waited for; matrix products, arithmetic and copies ran while one was open for 0% of the time, Pallas kernels for 30%

profile of v21, /device:TPU:0, one launch (start us, length us, event | category | flops | bytes accessed | tf_op | source)
XLA Modules:
  0.0 104.0 jit_solution(3171890566492178945)
XLA Ops:
  0.0 0.5 collective-permute-start.7
  0.5 2.7 %pick_queries.1 = (bf16[1,64,1024]{2,1,0:T(8,128)(2,1)}, bf16[1,64,1024]{2,1,0:T(8,128)(2,1)}, bf16[1,64,1024]{2,1,0:T(8,128)(2,1)}, bf16[1,64,1024]{2,1,0:T(8,128)(2,1)}) custom-call(s32[4,4]{1,0:T(4,128)} %pattern_ref.3, s32[16]{0:T(128)} %slot_ref.3, bf16[4,128,1024]{2,1,0:T(8,128)(2,1)} %in_ref.1), custom_call_target="tpu_custom_call" | custom-call | flops 1 | bytes 1 | tf_op jit(solution)/shard_map/pick_queries/pallas_call | solution.py:109
  3.1 2.8 %collective-permute-start.4 = (bf16[1,64,1024]{2,1,0:T(8,128)(2,1)}, bf16[1,64,1024]{2,1,0:T(8,128)(2,1)S(1)}, u32[]{:S(2)}, u32[]{:S(2)}) collective-permute-start(bf16[1,64,1024]{2,1,0:T(8,128)(2,1)} %get-tuple-element.50), channel_id=1, source_target_pairs={{0,4},{4,8},{8,12},{12,0},{1,5},{5,9},{9,13},{13,1},{2,6},{6,10},{... | collective-permute-start | bytes 393224 | tf_op jit(solution)/shard_map/ppermute | solution.py:23
  5.9 2.1 %collective-permute-start.6 = (bf16[1,64,1024]{2,1,0:T(8,128)(2,1)}, bf16[1,64,1024]{2,1,0:T(8,128)(2,1)S(1)}, u32[]{:S(2)}, u32[]{:S(2)}) collective-permute-start(bf16[1,64,1024]{2,1,0:T(8,128)(2,1)} %get-tuple-element.52), channel_id=1, source_target_pairs={{0,12},{4,0},{8,4},{12,8},{1,13},{5,1},{9,5},{13,9},{2,14},{6,2},{... | collective-permute-start | bytes 393224 | tf_op jit(solution)/shard_map/ppermute | solution.py:23
  8.0 0.9 collective-permute-start.5
  8.9 1.5 %collective-permute-start.8 = (bf16[1,64,1024]{2,1,0:T(8,128)(2,1)}, bf16[1,64,1024]{2,1,0:T(8,128)(2,1)S(1)}, u32[]{:S(2)}, u32[]{:S(2)}) collective-permute-start(bf16[1,64,1024]{2,1,0:T(8,128)(2,1)} %get-tuple-element.54.refs_0_), channel_id=1, source_target_pairs={{0,16},{16,0},{1,17},{17,1},{2,18},{18,2},{3,19},{19,3},{4,20},{20... | collective-permute-start | bytes 393224 | tf_op jit(solution)/shard_map/ppermute | solution.py:23
  10.5 6.6 %pack_rows.1 = (bf16[256,1024]{1,0:T(8,128)(2,1)}, bf16[256,1024]{1,0:T(8,128)(2,1)}, bf16[48,1024]{1,0:T(8,128)(2,1)}, bf16[32,1024]{1,0:T(8,128)(2,1)}, bf16[6...) custom-call(s32[32,128]{1,0:T(8,128)} %bitcast.11, ...), custom_call_target="tpu_custom_call" | custom-call | flops 1 | bytes 1 | tf_op jit(solution)/shard_map/pack_rows/pallas_call | solution.py:253
  17.1 1.6 %collective-permute-start.21 = (bf16[256,1024]{1,0:T(8,128)(2,1)}, bf16[256,1024]{1,0:T(8,128)(2,1)S(1)}, u32[]{:S(2)}, u32[]{:S(2)}) collective-permute-start(bf16[256,1024]{1,0:T(8,128)(2,1)} %after.19), channel_id=1, source_target_pairs={{0,4},{4,8},{8,12},{12,0},{1,5},{5,9},{9,13},{13,1},{2,6},{6,10},{... | collective-permute-start | bytes 1572872 | tf_op jit(solution)/shard_map/ppermute | solution.py:23
  18.7 0.5 collective-permute-start.9
  19.2 1.4 %collective-permute-done.5.rest_1_.refs_3_.refs_2_ = bf16[1,64,1024]{2,1,0:T(8,128)(2,1)S(1)} collective-permute-done((bf16[1,64,1024]{2,1,0:T(8,128)(2,1)}, bf16[1,64,1024]{2,1,0:T(8,128)(2,1)S(1)}, u32[]{:S(2)}, u32[]{:S(2)}) %collective-permute-start.5) | collective-permute-done | bytes 131104 | tf_op jit(solution)/shard_map/ppermute | solution.py:23
  20.6 18.4 %collective-permute-start.10 = (bf16[1,64,1024]{2,1,0:T(8,128)(2,1)S(1)}, bf16[1,64,1024]{2,1,0:T(8,128)(2,1)S(1)}, u32[]{:S(2)}, u32[]{:S(2)}) collective-permute-start(bf16[1,64,1024]{2,1,0:T(8,128)(2,1)S(1)} %collective-permute-done.5.rest_1_.refs_3_.refs_2_), channel_id=1, source_target_pairs={{0,16},{16,0},{1,17},{17,1},{2,18},{18,2},{3,19},{19,3},{4,20},{20... | collective-permute-start | bytes 393224 | tf_op jit(solution)/shard_map/ppermute | solution.py:23
  39.1 0.8 row_table.1
  39.9 3.4 %copy-done = bf16[1,4096,1024]{2,1,0:T(8,128)(2,1)S(1)} copy-done((bf16[1,4096,1024]{2,1,0:T(8,128)(2,1)S(1)}, bf16[1,4096,1024]{2,1,0:T(8,128)(2,1)}, u32[]{:S(2)}) %copy-start) | copy-done | bytes 8388632
  43.3 2.5 %fetch.1 = (bf16[2048,1024]{1,0:T(8,128)(2,1)S(1)}, bf16[2048,1024]{1,0:T(8,128)(2,1)S(1)}) custom-call(s32[1]{0:T(128)} %bitcast.3.block_ref, bf16[4096,1024]{1,0:T(8,128)(2,1)S(1)} %bitcast.7, bf16[4096,1024]{1,0:T(8,128)(2,1)} %collective-permute-done.7.refs_1_, bf16[1,64,1024]{2,1,0:T(8,128)(2,1)S(1)} %collective-permute-done.4.rest_0_.refs_2_.refs_1_, ...), custom_call_target="tpu_custom_call" | custom-call | flops 1 | bytes 1 | tf_op jit(solution)/shard_map/fetch/pallas_call | solution.py:326
  45.9 1.2 %join_queries.1 = (bf16[128,256]{1,0:T(8,128)(2,1)S(1)}, bf16[128,256]{1,0:T(8,128)(2,1)S(1)}, bf16[128,256]{1,0:T(8,128)(2,1)S(1)}, bf16[128,256]{1,0:T(8,128)(...) custom-call(s32[4,4]{1,0:T(4,128)S(1)} %copy-done.15, ...), custom_call_target="tpu_custom_call" | custom-call | flops 1 | bytes 1 | tf_op jit(solution)/shard_map/join_queries/pallas_call | solution.py:154
  47.2 0.5 collective-permute-start.13
  47.8 0.7 collective-permute-done.12.refs_10_
  49.2 0.6 collective-permute-done.15.refs_13_
  50.3 0.7 collective-permute-done.18.refs_16_
  51.0 3.6 %collective-permute-start.24 = (bf16[32,1024]{1,0:T(8,128)(2,1)S(1)}, bf16[32,1024]{1,0:T(8,128)(2,1)S(1)}, u32[]{:S(2)}, u32[]{:S(2)}) collective-permute-start(bf16[32,1024]{1,0:T(8,128)(2,1)S(1)} %after.25), channel_id=1, source_target_pairs={{0,12},{4,0},{8,4},{12,8},{1,13},{5,1},{9,5},{13,9},{2,14},{6,2},{... | collective-permute-start | bytes 196616 | tf_op jit(solution)/shard_map/ppermute | solution.py:23
  54.6 2.3 %fetched_weights.1.refs_18_.refs_2_.refs_5_ = bf16[2048,256]{1,0:T(8,128)(2,1)S(1)} custom-call(bf16[2048,1024]{1,0:T(8,128)(2,1)S(1)} %get-tuple-element.55.refs_8_.refs_0_, bf16[2048,1024]{1,0:T(8,128)(2,1)S(1)} %get-tuple-element.56.refs_9_.refs_1_, bf16[128,256]{1,0:T(8,128)(2,1)S(1)} %get-tuple-element.58.refs_2_, ...), custom_call_target="tpu_custom_call" | custom-call | flops 1 | bytes 1 | tf_op jit(solution)/shard_map/fetched_weights/pallas_call | solution.py:353
  57.0 1.6 %collective-permute-start.20 = (bf16[2048,256]{1,0:T(8,128)(2,1)S(1)}, bf16[2048,256]{1,0:T(8,128)(2,1)}, u32[]{:S(2)}, u32[]{:S(2)}) collective-permute-start(bf16[2048,256]{1,0:T(8,128)(2,1)S(1)} %fetched_weights.1.refs_18_.refs_2_.refs_5_), channel_id=1, source_target_pairs={{0,2},{2,0},{1,3},{3,1},{4,6},{6,4},{5,7},{7,5},{8,10},{10,8},{9,1... | collective-permute-start | bytes 3145736 | tf_op jit(solution)/shard_map/ppermute | solution.py:23
  58.6 0.8 stack.3
  59.4 1.3 %collective-permute-start.33 = (bf16[256,1024]{1,0:T(8,128)(2,1)}, bf16[256,1024]{1,0:T(8,128)(2,1)}, u32[]{:S(2)}, u32[]{:S(2)}) collective-permute-start(bf16[256,1024]{1,0:T(8,128)(2,1)} %after.32), channel_id=1, source_target_pairs={{0,8},{4,12},{8,0},{12,4},{1,9},{5,13},{9,1},{13,5},{2,10},{6,14},... | collective-permute-start | bytes 1572872 | tf_op jit(solution)/shard_map/ppermute | solution.py:23
  60.8 2.0 %collective-permute-start.26 = (s32[8,128]{1,0:T(8,128)S(1)}, s32[8,128]{1,0:T(8,128)S(1)}, u32[]{:S(2)}, u32[]{:S(2)}) collective-permute-start(s32[8,128]{1,0:T(8,128)S(1)} %get-tuple-element.57.refs_10_), channel_id=1, source_target_pairs={{0,16},{16,0},{1,17},{17,1},{2,18},{18,2},{3,19},{19,3},{4,20},{20... | collective-permute-start | bytes 12296 | tf_op jit(solution)/shard_map/ppermute | solution.py:23
  62.7 1.7 %collective-permute-done.26 = s32[8,128]{1,0:T(8,128)S(1)} collective-permute-done((s32[8,128]{1,0:T(8,128)S(1)}, s32[8,128]{1,0:T(8,128)S(1)}, u32[]{:S(2)}, u32[]{:S(2)}) %collective-permute-start.26) | collective-permute-done | bytes 4128 | tf_op jit(solution)/shard_map/ppermute | solution.py:23
  64.4 0.5 slice.3
  65.5 6.6 %partial_weights.1.rest_0_.refs_1_.refs_2_.refs_0_ = f32[2048,256]{1,0:T(8,128)S(1)} custom-call(s32[1]{0:T(128)} %bitcast.1.block_ref, bf16[4096,1024]{1,0:T(8,128)(2,1)S(1)} %bitcast.10, bf16[4096,1024]{1,0:T(8,128)(2,1)} %collective-permute-done.7.refs_1_, bf16[128,256]{1,0:T(8,128)(2,1)S(1)} %get-tuple-element.58.refs_2_, ...), custom_call_target="tpu_custom_call" | custom-call | flops 1 | bytes 1 | tf_op jit(solution)/shard_map/partial_weights/pallas_call | solution.py:293
  72.4 0.5 collective-permute-start.30
  72.9 1.2 %collective-permute-done.29.refs_0_ = bf16[128,1024]{1,0:T(8,128)(2,1)S(1)} collective-permute-done((bf16[128,1024]{1,0:T(8,128)(2,1)}, bf16[128,1024]{1,0:T(8,128)(2,1)S(1)}, u32[]{:S(2)}, u32[]{:S(2)}) %collective-permute-start.29) | collective-permute-done | bytes 262176 | tf_op jit(solution)/shard_map/ppermute | solution.py:23
  74.3 0.4 collective-permute-start.25
  74.7 2.4 %own_rows.1.refs_2_ = bf16[256,2048]{1,0:T(8,128)(2,1)S(1)} custom-call(s32[8,128]{1,0:T(8,128)S(1)} %copy-done.16, bf16[1024,2048]{1,0:T(8,128)(2,1)S(1)} %copy-done.1, f32[2048,256]{1,0:T(8,128)S(1)} %partial_weights.1.rest_0_.refs_1_.refs_2_.refs_0_), custom_call_target="tpu_custom_call" | custom-call | flops 1 | bytes 1 | tf_op jit(solution)/shard_map/own_rows/pallas_call | solution.py:195
  77.2 0.8 copy-done.10
  78.1 4.6 %collective-permute-done.28.refs_9_.refs_0_ = bf16[256,1024]{1,0:T(8,128)(2,1)} collective-permute-done((bf16[256,1024]{1,0:T(8,128)(2,1)}, bf16[256,1024]{1,0:T(8,128)(2,1)}, u32[]{:S(2)}, u32[]{:S(2)}) %collective-permute-start.28) | collective-permute-done | bytes 524320 | tf_op jit(solution)/shard_map/ppermute | solution.py:27
  82.7 0.5 collective-permute-start.35
  83.2 0.7 collective-permute-done.31.refs_1_
  84.0 1.1 %collective-permute-done.33.refs_0_ = bf16[256,1024]{1,0:T(8,128)(2,1)} collective-permute-done((bf16[256,1024]{1,0:T(8,128)(2,1)}, bf16[256,1024]{1,0:T(8,128)(2,1)}, u32[]{:S(2)}, u32[]{:S(2)}) %collective-permute-start.33) | collective-permute-done | bytes 524320 | tf_op jit(solution)/shard_map/ppermute | solution.py:23
  85.1 1.5 %collective-permute-start.37 = (bf16[64,1024]{1,0:T(8,128)(2,1)S(1)}, bf16[64,1024]{1,0:T(8,128)(2,1)S(1)}, u32[]{:S(2)}, u32[]{:S(2)}) collective-permute-start(bf16[64,1024]{1,0:T(8,128)(2,1)S(1)} %after.20.refs_3_), channel_id=1, source_target_pairs={{0,12},{4,0},{8,4},{12,8},{1,13},{5,1},{9,5},{13,9},{2,14},{6,2},{... | collective-permute-start | bytes 393224 | tf_op jit(solution)/shard_map/ppermute | solution.py:23
  86.8 0.4 collective-permute-start.41
  87.3 4.2 %early_scores.1 = (bf16[2048,512]{1,0:T(8,128)(2,1)S(1)}, f32[1024,128]{1,0:T(8,128)S(1)}, bf16[1024,128]{1,0:T(8,128)(2,1)S(1)}) custom-call(s32[4,4]{1,0:T(4,128)S(1)} %get-tuple-element.53.table_ref, f32[2048,256]{1,0:T(8,128)S(1)} %partial_weights.1.rest_0_.refs_1_.refs_2_.refs_0_, bf16[2048,256]{1,0:T(8,128)(2,1)} %collective-permute-done.20.refs_1_, ...), custom_call_target="tpu_custom_call" | custom-call | flops 1 | bytes 1 | tf_op jit(solution)/shard_map/early_scores/pallas_call | solution.py:518
  91.4 0.6 collective-permute-start.36
  92.0 2.2 %collective-permute-done.39.refs_0_ = bf16[64,1024]{1,0:T(8,128)(2,1)S(1)} collective-permute-done((bf16[64,1024]{1,0:T(8,128)(2,1)S(1)}, bf16[64,1024]{1,0:T(8,128)(2,1)S(1)}, u32[]{:S(2)}, u32[]{:S(2)}) %collective-permute-start.39) | collective-permute-done | bytes 131104 | tf_op jit(solution)/shard_map/ppermute | solution.py:23
  94.2 1.7 %collective-permute-done.41.refs_0_ = bf16[48,1024]{1,0:T(8,128)(2,1)S(1)} collective-permute-done((bf16[48,1024]{1,0:T(8,128)(2,1)S(1)}, bf16[48,1024]{1,0:T(8,128)(2,1)S(1)}, u32[]{:S(2)}, u32[]{:S(2)}) %collective-permute-start.41) | collective-permute-done | bytes 98336 | tf_op jit(solution)/shard_map/ppermute | solution.py:23
  96.0 1.3 %collective-permute-done.42.refs_9_ = bf16[48,1024]{1,0:T(8,128)(2,1)S(1)} collective-permute-done((bf16[48,1024]{1,0:T(8,128)(2,1)S(1)}, bf16[48,1024]{1,0:T(8,128)(2,1)S(1)}, u32[]{:S(2)}, u32[]{:S(2)}) %collective-permute-start.42) | collective-permute-done | bytes 98336 | tf_op jit(solution)/shard_map/ppermute | solution.py:23
  97.3 0.7 late_scores.1
  98.0 0.6 collective-permute-start.43
  98.6 3.7 %collective-permute-done.43.refs_3_ = bf16[256,128]{1,0:T(8,128)(2,1)S(1)} collective-permute-done((bf16[256,128]{1,0:T(8,128)(2,1)S(1)}, bf16[256,128]{1,0:T(8,128)(2,1)S(1)}, u32[]{:S(2)}, u32[]{:S(2)}) %collective-permute-start.43) | collective-permute-done | bytes 65568 | tf_op jit(solution)/shard_map/ppermute | solution.py:23
  102.4 1.7 %merge.1 = f32[128,1024]{1,0:T(8,128)} custom-call(s32[4,4]{1,0:T(4,128)S(1)} %get-tuple-element.53.table_ref, f32[1024,128]{1,0:T(8,128)S(1)} %get-tuple-element.89.refs_0_, bf16[1024,128]{1,0:T(8,128)(2,1)S(1)} %collective-permute-done.36.refs_1_, f32[256,128]{1,0:T(8,128)S(1)} %get-tuple-element.92.refs_2_, ...), custom_call_target="tpu_custom_call" | custom-call | flops 1 | bytes 1 | tf_op jit(solution)/shard_map/merge/pallas_call | solution.py:578
  (113 shorter events, 2.5 us)
Async XLA Ops:
  0.0 39.1 %copy-start.13 = (s32[4096]{0:T(1024)S(1)}, s32[4096]{0:T(1024)}, u32[]{:S(2)}) copy-start(s32[4096]{0:T(1024)} %param.9) | copy-start | bytes 49156
  0.0 39.0 %collective-permute-start.7 = (bf16[4096,1024]{1,0:T(8,128)(2,1)}, bf16[4096,1024]{1,0:T(8,128)(2,1)}, u32[]{:S(2)}, u32[]{:S(2)}) collective-permute-start(bf16[4096,1024]{1,0:T(8,128)(2,1)} %bitcast.6), channel_id=1, source_target_pairs={{0,1},{1,0},{2,3},{3,2},{4,5},{5,4},{6,7},{7,6},{8,9},{9,8},{10,11... | collective-permute-start | bytes 25165832 | tf_op jit(solution)/shard_map/ppermute | solution.py:23
  3.1 13.9 %collective-permute-start.4 = (bf16[1,64,1024]{2,1,0:T(8,128)(2,1)}, bf16[1,64,1024]{2,1,0:T(8,128)(2,1)S(1)}, u32[]{:S(2)}, u32[]{:S(2)}) collective-permute-start(bf16[1,64,1024]{2,1,0:T(8,128)(2,1)} %get-tuple-element.50), channel_id=1, source_target_pairs={{0,4},{4,8},{8,12},{12,0},{1,5},{5,9},{9,13},{13,1},{2,6},{6,10},{... | collective-permute-start | bytes 393224 | tf_op jit(solution)/shard_map/ppermute | solution.py:23
  5.9 11.2 %collective-permute-start.6 = (bf16[1,64,1024]{2,1,0:T(8,128)(2,1)}, bf16[1,64,1024]{2,1,0:T(8,128)(2,1)S(1)}, u32[]{:S(2)}, u32[]{:S(2)}) collective-permute-start(bf16[1,64,1024]{2,1,0:T(8,128)(2,1)} %get-tuple-element.52), channel_id=1, source_target_pairs={{0,12},{4,0},{8,4},{12,8},{1,13},{5,1},{9,5},{13,9},{2,14},{6,2},{... | collective-permute-start | bytes 393224 | tf_op jit(solution)/shard_map/ppermute | solution.py:23
  8.0 12.6 %collective-permute-start.5 = (bf16[1,64,1024]{2,1,0:T(8,128)(2,1)}, bf16[1,64,1024]{2,1,0:T(8,128)(2,1)S(1)}, u32[]{:S(2)}, u32[]{:S(2)}) collective-permute-start(bf16[1,64,1024]{2,1,0:T(8,128)(2,1)} %get-tuple-element.51), channel_id=1, source_target_pairs={{0,8},{4,12},{8,0},{12,4},{1,9},{5,13},{9,1},{13,5},{2,10},{6,14},... | collective-permute-start | bytes 393224 | tf_op jit(solution)/shard_map/ppermute | solution.py:23
  8.9 30.0 %collective-permute-start.8 = (bf16[1,64,1024]{2,1,0:T(8,128)(2,1)}, bf16[1,64,1024]{2,1,0:T(8,128)(2,1)S(1)}, u32[]{:S(2)}, u32[]{:S(2)}) collective-permute-start(bf16[1,64,1024]{2,1,0:T(8,128)(2,1)} %get-tuple-element.54.refs_0_), channel_id=1, source_target_pairs={{0,16},{16,0},{1,17},{17,1},{2,18},{18,2},{3,19},{19,3},{4,20},{20... | collective-permute-start | bytes 393224 | tf_op jit(solution)/shard_map/ppermute | solution.py:23
  17.1 42.3 %collective-permute-start.21 = (bf16[256,1024]{1,0:T(8,128)(2,1)}, bf16[256,1024]{1,0:T(8,128)(2,1)S(1)}, u32[]{:S(2)}, u32[]{:S(2)}) collective-permute-start(bf16[256,1024]{1,0:T(8,128)(2,1)} %after.19), channel_id=1, source_target_pairs={{0,4},{4,8},{8,12},{12,0},{1,5},{5,9},{9,13},{13,1},{2,6},{6,10},{... | collective-permute-start | bytes 1572872 | tf_op jit(solution)/shard_map/ppermute | solution.py:23
  18.7 27.1 %collective-permute-start.9 = (bf16[1,64,1024]{2,1,0:T(8,128)(2,1)S(1)}, bf16[1,64,1024]{2,1,0:T(8,128)(2,1)S(1)}, u32[]{:S(2)}, u32[]{:S(2)}) collective-permute-start(bf16[1,64,1024]{2,1,0:T(8,128)(2,1)S(1)} %collective-permute-done.4.rest_0_.refs_2_.refs_1_), channel_id=1, source_target_pairs={{0,16},{16,0},{1,17},{17,1},{2,18},{18,2},{3,19},{19,3},{4,20},{20... | collective-permute-start | bytes 393224 | tf_op jit(solution)/shard_map/ppermute | solution.py:23
  20.6 25.3 %collective-permute-start.10 = (bf16[1,64,1024]{2,1,0:T(8,128)(2,1)S(1)}, bf16[1,64,1024]{2,1,0:T(8,128)(2,1)S(1)}, u32[]{:S(2)}, u32[]{:S(2)}) collective-permute-start(bf16[1,64,1024]{2,1,0:T(8,128)(2,1)S(1)} %collective-permute-done.5.rest_1_.refs_3_.refs_2_), channel_id=1, source_target_pairs={{0,16},{16,0},{1,17},{17,1},{2,18},{18,2},{3,19},{19,3},{4,20},{20... | collective-permute-start | bytes 393224 | tf_op jit(solution)/shard_map/ppermute | solution.py:23
  39.0 6.9 %collective-permute-start.11 = (bf16[1,64,1024]{2,1,0:T(8,128)(2,1)S(1)}, bf16[1,64,1024]{2,1,0:T(8,128)(2,1)S(1)}, u32[]{:S(2)}, u32[]{:S(2)}) collective-permute-start(bf16[1,64,1024]{2,1,0:T(8,128)(2,1)S(1)} %collective-permute-done.6.rest_2_.refs_4_.refs_3_.refs_2_), channel_id=1, source_target_pairs={{0,16},{16,0},{1,17},{17,1},{2,18},{18,2},{3,19},{19,3},{4,20},{20... | collective-permute-start | bytes 393224 | tf_op jit(solution)/shard_map/ppermute | solution.py:23
  39.0 19.5 %collective-permute-start.27 = (bf16[128,1024]{1,0:T(8,128)(2,1)}, bf16[128,1024]{1,0:T(8,128)(2,1)S(1)}, u32[]{:S(2)}, u32[]{:S(2)}) collective-permute-start(bf16[128,1024]{1,0:T(8,128)(2,1)} %after.28), channel_id=1, source_target_pairs={{0,8},{4,12},{8,0},{12,4},{1,9},{5,13},{9,1},{13,5},{2,10},{6,14},... | collective-permute-start | bytes 786440 | tf_op jit(solution)/shard_map/ppermute | solution.py:27
  45.9 4.4 %copy-start.12 = (bf16[48,1024]{1,0:T(8,128)(2,1)S(1)}, bf16[48,1024]{1,0:T(8,128)(2,1)}, u32[]{:S(2)}) copy-start(bf16[48,1024]{1,0:T(8,128)(2,1)} %get-tuple-element.79.refs_0_) | copy-start | bytes 294916
  45.9 4.4 %copy-start.14 = (bf16[32,1024]{1,0:T(8,128)(2,1)S(1)}, bf16[32,1024]{1,0:T(8,128)(2,1)}, u32[]{:S(2)}) copy-start(bf16[32,1024]{1,0:T(8,128)(2,1)} %get-tuple-element.80.refs_0_) | copy-start | bytes 196612
  47.2 1.3 %collective-permute-start.12 = (bf16[128,256]{1,0:T(8,128)(2,1)S(1)}, bf16[128,256]{1,0:T(8,128)(2,1)S(1)}, u32[]{:S(2)}, u32[]{:S(2)}) collective-permute-start(bf16[128,256]{1,0:T(8,128)(2,1)S(1)} %get-tuple-element.66), channel_id=1, source_target_pairs={{0,1},{1,0},{2,3},{3,2},{4,5},{5,4},{6,7},{7,6},{8,9},{9,8},{10,11... | collective-permute-start | bytes 196616 | tf_op jit(solution)/shard_map/ppermute | solution.py:23
  47.2 1.4 %collective-permute-start.13 = (bf16[128,256]{1,0:T(8,128)(2,1)S(1)}, bf16[128,256]{1,0:T(8,128)(2,1)S(1)}, u32[]{:S(2)}, u32[]{:S(2)}) collective-permute-start(bf16[128,256]{1,0:T(8,128)(2,1)S(1)} %get-tuple-element.67), channel_id=1, source_target_pairs={{0,1},{1,0},{2,3},{3,2},{4,5},{5,4},{6,7},{7,6},{8,9},{9,8},{10,11... | collective-permute-start | bytes 196616 | tf_op jit(solution)/shard_map/ppermute | solution.py:23
  47.7 1.3 %collective-permute-start.14 = (bf16[128,256]{1,0:T(8,128)(2,1)S(1)}, bf16[128,256]{1,0:T(8,128)(2,1)S(1)}, u32[]{:S(2)}, u32[]{:S(2)}) collective-permute-start(bf16[128,256]{1,0:T(8,128)(2,1)S(1)} %get-tuple-element.68), channel_id=1, source_target_pairs={{0,1},{1,0},{2,3},{3,2},{4,5},{5,4},{6,7},{7,6},{8,9},{9,8},{10,11... | collective-permute-start | bytes 196616 | tf_op jit(solution)/shard_map/ppermute | solution.py:23
  48.5 1.3 %collective-permute-start.15 = (bf16[128,256]{1,0:T(8,128)(2,1)S(1)}, bf16[128,256]{1,0:T(8,128)(2,1)S(1)}, u32[]{:S(2)}, u32[]{:S(2)}) collective-permute-start(bf16[128,256]{1,0:T(8,128)(2,1)S(1)} %get-tuple-element.69), channel_id=1, source_target_pairs={{0,1},{1,0},{2,3},{3,2},{4,5},{5,4},{6,7},{7,6},{8,9},{9,8},{10,11... | collective-permute-start | bytes 196616 | tf_op jit(solution)/shard_map/ppermute | solution.py:23
  48.7 1.3 %collective-permute-start.16 = (bf16[128,256]{1,0:T(8,128)(2,1)S(1)}, bf16[128,256]{1,0:T(8,128)(2,1)S(1)}, u32[]{:S(2)}, u32[]{:S(2)}) collective-permute-start(bf16[128,256]{1,0:T(8,128)(2,1)S(1)} %get-tuple-element.70), channel_id=1, source_target_pairs={{0,1},{1,0},{2,3},{3,2},{4,5},{5,4},{6,7},{7,6},{8,9},{9,8},{10,11... | collective-permute-start | bytes 196616 | tf_op jit(solution)/shard_map/ppermute | solution.py:23
  49.0 1.3 %collective-permute-start.17 = (bf16[128,256]{1,0:T(8,128)(2,1)S(1)}, bf16[128,256]{1,0:T(8,128)(2,1)S(1)}, u32[]{:S(2)}, u32[]{:S(2)}) collective-permute-start(bf16[128,256]{1,0:T(8,128)(2,1)S(1)} %get-tuple-element.71), channel_id=1, source_target_pairs={{0,1},{1,0},{2,3},{3,2},{4,5},{5,4},{6,7},{7,6},{8,9},{9,8},{10,11... | collective-permute-start | bytes 196616 | tf_op jit(solution)/shard_map/ppermute | solution.py:23
  49.7 1.3 %collective-permute-start.18 = (bf16[128,256]{1,0:T(8,128)(2,1)S(1)}, bf16[128,256]{1,0:T(8,128)(2,1)S(1)}, u32[]{:S(2)}, u32[]{:S(2)}) collective-permute-start(bf16[128,256]{1,0:T(8,128)(2,1)S(1)} %get-tuple-element.72), channel_id=1, source_target_pairs={{0,1},{1,0},{2,3},{3,2},{4,5},{5,4},{6,7},{7,6},{8,9},{9,8},{10,11... | collective-permute-start | bytes 196616 | tf_op jit(solution)/shard_map/ppermute | solution.py:23
  49.9 4.7 %collective-permute-start.19 = (bf16[128,256]{1,0:T(8,128)(2,1)S(1)}, bf16[128,256]{1,0:T(8,128)(2,1)S(1)}, u32[]{:S(2)}, u32[]{:S(2)}) collective-permute-start(bf16[128,256]{1,0:T(8,128)(2,1)S(1)} %get-tuple-element.73), channel_id=1, source_target_pairs={{0,1},{1,0},{2,3},{3,2},{4,5},{5,4},{6,7},{7,6},{8,9},{9,8},{10,11... | collective-permute-start | bytes 196616 | tf_op jit(solution)/shard_map/ppermute | solution.py:23
  50.3 9.1 %collective-permute-start.22 = (bf16[48,1024]{1,0:T(8,128)(2,1)S(1)}, bf16[48,1024]{1,0:T(8,128)(2,1)S(1)}, u32[]{:S(2)}, u32[]{:S(2)}) collective-permute-start(bf16[48,1024]{1,0:T(8,128)(2,1)S(1)} %after.23), channel_id=1, source_target_pairs={{0,12},{4,0},{8,4},{12,8},{1,13},{5,1},{9,5},{13,9},{2,14},{6,2},{... | collective-permute-start | bytes 294920 | tf_op jit(solution)/shard_map/ppermute | solution.py:23
  51.0 8.4 %collective-permute-start.24 = (bf16[32,1024]{1,0:T(8,128)(2,1)S(1)}, bf16[32,1024]{1,0:T(8,128)(2,1)S(1)}, u32[]{:S(2)}, u32[]{:S(2)}) collective-permute-start(bf16[32,1024]{1,0:T(8,128)(2,1)S(1)} %after.25), channel_id=1, source_target_pairs={{0,12},{4,0},{8,4},{12,8},{1,13},{5,1},{9,5},{13,9},{2,14},{6,2},{... | collective-permute-start | bytes 196616 | tf_op jit(solution)/shard_map/ppermute | solution.py:23
  54.6 10.8 %slice-start = ((s8[8388608]{0:T(1024)(128)(4,1)}), s8[4194304]{0:T(1024)(128)(4,1)S(1)}, s32[]{:S(2)}) async-start(s8[8388608]{0:T(1024)(128)(4,1)} %bitcast.8), calls=%async_computation | async-start | bytes 8388608
  54.6 10.8 %slice-start.1 = ((s8[8388608]{0:T(1024)(128)(4,1)}), s8[4194304]{0:T(1024)(128)(4,1)S(1)}, s32[]{:S(2)}) async-start(s8[8388608]{0:T(1024)(128)(4,1)} %bitcast.8), calls=%async_computation.1 | async-start | bytes 8388608
  57.0 29.6 %collective-permute-start.20 = (bf16[2048,256]{1,0:T(8,128)(2,1)S(1)}, bf16[2048,256]{1,0:T(8,128)(2,1)}, u32[]{:S(2)}, u32[]{:S(2)}) collective-permute-start(bf16[2048,256]{1,0:T(8,128)(2,1)S(1)} %fetched_weights.1.refs_18_.refs_2_.refs_5_), channel_id=1, source_target_pairs={{0,2},{2,0},{1,3},{3,1},{4,6},{6,4},{5,7},{7,5},{8,10},{10,8},{9,1... | collective-permute-start | bytes 3145736 | tf_op jit(solution)/shard_map/ppermute | solution.py:23
  59.4 23.3 %collective-permute-start.28 = (bf16[256,1024]{1,0:T(8,128)(2,1)}, bf16[256,1024]{1,0:T(8,128)(2,1)}, u32[]{:S(2)}, u32[]{:S(2)}) collective-permute-start(bf16[256,1024]{1,0:T(8,128)(2,1)} %stack.3), channel_id=1, source_target_pairs={{0,4},{4,0},{8,12},{12,8},{1,5},{5,1},{9,13},{13,9},{2,6},{6,2},{1... | collective-permute-start | bytes 1572872 | tf_op jit(solution)/shard_map/ppermute | solution.py:27
  59.4 12.7 %copy-start.6 = (bf16[32,1024]{1,0:T(8,128)(2,1)}, bf16[32,1024]{1,0:T(8,128)(2,1)S(1)}, u32[]{:S(2)}) copy-start(bf16[32,1024]{1,0:T(8,128)(2,1)S(1)} %collective-permute-done.24.refs_0_.refs_4_) | copy-start | bytes 196612
  59.4 6.0 %copy-start.2 = (bf16[256,1024]{1,0:T(8,128)(2,1)}, bf16[256,1024]{1,0:T(8,128)(2,1)S(1)}, u32[]{:S(2)}) copy-start(bf16[256,1024]{1,0:T(8,128)(2,1)S(1)} %collective-permute-done.21.refs_0_.refs_1_) | copy-start | bytes 1572868
  59.4 25.7 %collective-permute-start.33 = (bf16[256,1024]{1,0:T(8,128)(2,1)}, bf16[256,1024]{1,0:T(8,128)(2,1)}, u32[]{:S(2)}, u32[]{:S(2)}) collective-permute-start(bf16[256,1024]{1,0:T(8,128)(2,1)} %after.32), channel_id=1, source_target_pairs={{0,8},{4,12},{8,0},{12,4},{1,9},{5,13},{9,1},{13,5},{2,10},{6,14},... | collective-permute-start | bytes 1572872 | tf_op jit(solution)/shard_map/ppermute | solution.py:23
  60.8 3.6 %collective-permute-start.26 = (s32[8,128]{1,0:T(8,128)S(1)}, s32[8,128]{1,0:T(8,128)S(1)}, u32[]{:S(2)}, u32[]{:S(2)}) collective-permute-start(s32[8,128]{1,0:T(8,128)S(1)} %get-tuple-element.57.refs_10_), channel_id=1, source_target_pairs={{0,16},{16,0},{1,17},{17,1},{2,18},{18,2},{3,19},{19,3},{4,20},{20... | collective-permute-start | bytes 12296 | tf_op jit(solution)/shard_map/ppermute | solution.py:23
  65.5 6.6 %copy-start.18 = (bf16[128,1024]{1,0:T(8,128)(2,1)S(1)}, bf16[128,1024]{1,0:T(8,128)(2,1)}, u32[]{:S(2)}) copy-start(bf16[128,1024]{1,0:T(8,128)(2,1)} %get-tuple-element.81.refs_0_) | copy-start | bytes 786436
  72.3 1.8 %collective-permute-start.29 = (bf16[128,1024]{1,0:T(8,128)(2,1)}, bf16[128,1024]{1,0:T(8,128)(2,1)S(1)}, u32[]{:S(2)}, u32[]{:S(2)}) collective-permute-start(bf16[128,1024]{1,0:T(8,128)(2,1)} %get-tuple-element.83.refs_0_), channel_id=1, source_target_pairs={{0,1},{1,0},{2,3},{3,2},{4,5},{5,4},{6,7},{7,6},{8,9},{9,8},{10,11... | collective-permute-start | bytes 786440 | tf_op jit(solution)/shard_map/ppermute | solution.py:23
  72.4 1.9 %collective-permute-start.30 = (bf16[128,1024]{1,0:T(8,128)(2,1)S(1)}, bf16[128,1024]{1,0:T(8,128)(2,1)S(1)}, u32[]{:S(2)}, u32[]{:S(2)}) collective-permute-start(bf16[128,1024]{1,0:T(8,128)(2,1)S(1)} %after.29.refs_1_), channel_id=1, source_target_pairs={{0,1},{1,0},{2,3},{3,2},{4,5},{5,4},{6,7},{7,6},{8,9},{9,8},{10,11... | collective-permute-start | bytes 786440 | tf_op jit(solution)/shard_map/ppermute | solution.py:23
  74.1 3.9 %collective-permute-start.23 = (bf16[48,1024]{1,0:T(8,128)(2,1)S(1)}, bf16[48,1024]{1,0:T(8,128)(2,1)S(1)}, u32[]{:S(2)}, u32[]{:S(2)}) collective-permute-start(bf16[48,1024]{1,0:T(8,128)(2,1)S(1)} %after.24.refs_0_), channel_id=1, source_target_pairs={{0,1},{1,0},{2,3},{3,2},{4,5},{5,4},{6,7},{7,6},{8,9},{9,8},{10,11... | collective-permute-start | bytes 294920 | tf_op jit(solution)/shard_map/ppermute | solution.py:23
  74.3 3.7 %collective-permute-start.25 = (bf16[32,1024]{1,0:T(8,128)(2,1)S(1)}, bf16[32,1024]{1,0:T(8,128)(2,1)S(1)}, u32[]{:S(2)}, u32[]{:S(2)}) collective-permute-start(bf16[32,1024]{1,0:T(8,128)(2,1)S(1)} %after.26.refs_2_), channel_id=1, source_target_pairs={{0,1},{1,0},{2,3},{3,2},{4,5},{5,4},{6,7},{7,6},{8,9},{9,8},{10,11... | collective-permute-start | bytes 196616 | tf_op jit(solution)/shard_map/ppermute | solution.py:23
  82.7 1.2 %collective-permute-start.31 = (s32[8,128]{1,0:T(8,128)S(1)}, s32[8,128]{1,0:T(8,128)S(1)}, u32[]{:S(2)}, u32[]{:S(2)}) collective-permute-start(s32[8,128]{1,0:T(8,128)S(1)} %after.30), channel_id=1, source_target_pairs={{0,1},{1,0},{2,3},{3,2},{4,5},{5,4},{6,7},{7,6},{8,9},{9,8},{10,11... | collective-permute-start | bytes 12296 | tf_op jit(solution)/shard_map/ppermute | solution.py:23
  82.7 4.1 %collective-permute-start.35 = (bf16[256,1024]{1,0:T(8,128)(2,1)}, bf16[256,1024]{1,0:T(8,128)(2,1)S(1)}, u32[]{:S(2)}, u32[]{:S(2)}) collective-permute-start(bf16[256,1024]{1,0:T(8,128)(2,1)} %after.34.refs_9_), channel_id=1, source_target_pairs={{0,1},{1,0},{2,3},{3,2},{4,5},{5,4},{6,7},{7,6},{8,9},{9,8},{10,11... | collective-permute-start | bytes 1572872 | tf_op jit(solution)/shard_map/ppermute | solution.py:23
  83.9 3.4 %collective-permute-start.32 = (bf16[256,1024]{1,0:T(8,128)(2,1)S(1)}, bf16[256,1024]{1,0:T(8,128)(2,1)S(1)}, u32[]{:S(2)}, u32[]{:S(2)}) collective-permute-start(bf16[256,1024]{1,0:T(8,128)(2,1)S(1)} %after.31.refs_3_), channel_id=1, source_target_pairs={{0,1},{1,0},{2,3},{3,2},{4,5},{5,4},{6,7},{7,6},{8,9},{9,8},{10,11... | collective-permute-start | bytes 1572872 | tf_op jit(solution)/shard_map/ppermute | solution.py:23
  85.1 2.1 %collective-permute-start.34 = (bf16[256,1024]{1,0:T(8,128)(2,1)}, bf16[256,1024]{1,0:T(8,128)(2,1)S(1)}, u32[]{:S(2)}, u32[]{:S(2)}) collective-permute-start(bf16[256,1024]{1,0:T(8,128)(2,1)} %after.33.refs_5_), channel_id=1, source_target_pairs={{0,1},{1,0},{2,3},{3,2},{4,5},{5,4},{6,7},{7,6},{8,9},{9,8},{10,11... | collective-permute-start | bytes 1572872 | tf_op jit(solution)/shard_map/ppermute | solution.py:23
  85.1 6.9 %collective-permute-start.37 = (bf16[64,1024]{1,0:T(8,128)(2,1)S(1)}, bf16[64,1024]{1,0:T(8,128)(2,1)S(1)}, u32[]{:S(2)}, u32[]{:S(2)}) collective-permute-start(bf16[64,1024]{1,0:T(8,128)(2,1)S(1)} %after.20.refs_3_), channel_id=1, source_target_pairs={{0,12},{4,0},{8,4},{12,8},{1,13},{5,1},{9,5},{13,9},{2,14},{6,2},{... | collective-permute-start | bytes 393224 | tf_op jit(solution)/shard_map/ppermute | solution.py:23
  86.6 7.6 %collective-permute-start.39 = (bf16[64,1024]{1,0:T(8,128)(2,1)S(1)}, bf16[64,1024]{1,0:T(8,128)(2,1)S(1)}, u32[]{:S(2)}, u32[]{:S(2)}) collective-permute-start(bf16[64,1024]{1,0:T(8,128)(2,1)S(1)} %after.21.refs_4_), channel_id=1, source_target_pairs={{0,12},{4,0},{8,4},{12,8},{1,13},{5,1},{9,5},{13,9},{2,14},{6,2},{... | collective-permute-start | bytes 393224 | tf_op jit(solution)/shard_map/ppermute | solution.py:23
  86.8 9.1 %collective-permute-start.41 = (bf16[48,1024]{1,0:T(8,128)(2,1)S(1)}, bf16[48,1024]{1,0:T(8,128)(2,1)S(1)}, u32[]{:S(2)}, u32[]{:S(2)}) collective-permute-start(bf16[48,1024]{1,0:T(8,128)(2,1)S(1)} %after.22.refs_5_), channel_id=1, source_target_pairs={{0,12},{4,0},{8,4},{12,8},{1,13},{5,1},{9,5},{13,9},{2,14},{6,2},{... | collective-permute-start | bytes 294920 | tf_op jit(solution)/shard_map/ppermute | solution.py:23
  91.4 10.9 %collective-permute-start.36 = (bf16[1024,128]{1,0:T(8,128)(2,1)S(1)}, bf16[1024,128]{1,0:T(8,128)(2,1)S(1)}, u32[]{:S(2)}, u32[]{:S(2)}) collective-permute-start(bf16[1024,128]{1,0:T(8,128)(2,1)S(1)} %get-tuple-element.90.refs_1_), channel_id=1, source_target_pairs={{0,2},{2,0},{1,3},{3,1},{4,6},{6,4},{5,7},{7,5},{8,10},{10,8},{9,1... | collective-permute-start | bytes 786440 | tf_op jit(solution)/shard_map/ppermute | solution.py:23
  92.0 5.2 %collective-permute-start.38 = (bf16[64,1024]{1,0:T(8,128)(2,1)S(1)}, bf16[64,1024]{1,0:T(8,128)(2,1)S(1)}, u32[]{:S(2)}, u32[]{:S(2)}) collective-permute-start(bf16[64,1024]{1,0:T(8,128)(2,1)S(1)} %after.35.refs_4_), channel_id=1, source_target_pairs={{0,1},{1,0},{2,3},{3,2},{4,5},{5,4},{6,7},{7,6},{8,9},{9,8},{10,11... | collective-permute-start | bytes 393224 | tf_op jit(solution)/shard_map/ppermute | solution.py:23
  94.2 3.0 %collective-permute-start.40 = (bf16[64,1024]{1,0:T(8,128)(2,1)S(1)}, bf16[64,1024]{1,0:T(8,128)(2,1)S(1)}, u32[]{:S(2)}, u32[]{:S(2)}) collective-permute-start(bf16[64,1024]{1,0:T(8,128)(2,1)S(1)} %after.36.refs_6_), channel_id=1, source_target_pairs={{0,1},{1,0},{2,3},{3,2},{4,5},{5,4},{6,7},{7,6},{8,9},{9,8},{10,11... | collective-permute-start | bytes 393224 | tf_op jit(solution)/shard_map/ppermute | solution.py:23
  96.0 1.3 %collective-permute-start.42 = (bf16[48,1024]{1,0:T(8,128)(2,1)S(1)}, bf16[48,1024]{1,0:T(8,128)(2,1)S(1)}, u32[]{:S(2)}, u32[]{:S(2)}) collective-permute-start(bf16[48,1024]{1,0:T(8,128)(2,1)S(1)} %after.37.refs_8_), channel_id=1, source_target_pairs={{0,1},{1,0},{2,3},{3,2},{4,5},{5,4},{6,7},{7,6},{8,9},{9,8},{10,11... | collective-permute-start | bytes 294920 | tf_op jit(solution)/shard_map/ppermute | solution.py:23
  98.0 4.3 %collective-permute-start.43 = (bf16[256,128]{1,0:T(8,128)(2,1)S(1)}, bf16[256,128]{1,0:T(8,128)(2,1)S(1)}, u32[]{:S(2)}, u32[]{:S(2)}) collective-permute-start(bf16[256,128]{1,0:T(8,128)(2,1)S(1)} %get-tuple-element.93), channel_id=1, source_target_pairs={{0,2},{2,0},{1,3},{3,1},{4,6},{6,4},{5,7},{7,5},{8,10},{10,8},{9,1... | collective-permute-start | bytes 196616 | tf_op jit(solution)/shard_map/ppermute | solution.py:23
  (13 other events, 30.8 us)

commit v22 on v19

--- a/solution.py
+++ b/solution.py
@@ -89,10 +89,8 @@
     n_cluster, n_list = pattern.shape
     part = block_rows // n_group
 
-    def kernel(pattern_ref, slot_ref, in_ref, *rest):
-        outs, sem = rest[:-1], rest[-1]
-        me, group = lax.axis_index("shard"), lax.axis_index("groups")
-        copies = []
+    def kernel(pattern_ref, slot_ref, in_ref, *outs):
+        me = lax.axis_index("shard")
         for t, out in enumerate(outs):
             target = lax.rem(me + t, jnp.int32(n_cluster))
             found = jnp.int32(0)
@@ -100,18 +98,14 @@
                 slot = slot_ref[pattern_ref[target, k]]
                 hit = (lax.div(slot, jnp.int32(local_blocks)) == me).astype(I32)
                 found = found + hit * lax.rem(slot, jnp.int32(local_blocks))
-            rows = pl.ds(pl.multiple_of(group * part, part), part)
-            copies.append(pltpu.make_async_copy(in_ref.at[found, rows], out.at[0], sem.at[t]))
-            copies[-1].start()
-        for copy in copies:
-            copy.wait()
-
-    return pl.pallas_call(
-        kernel,
-        in_specs=[SMEM, SMEM, ANY],
+            out[0] = in_ref[found]
+
+    return pl.pallas_call(
+        kernel,
+        grid=(1,),
+        in_specs=[SMEM, SMEM, pl.BlockSpec((local_blocks, part, width), lambda i: (0, lax.axis_index("groups"), 0))],
         out_specs=[VMEM] * n_cluster,
         out_shape=[jax.ShapeDtypeStruct((1, part, width), BF16)] * n_cluster,
-        scratch_shapes=[pltpu.SemaphoreType.DMA((n_cluster,))],
         cost_estimate=cost(0, 4 * n_cluster * part * width),
         compiler_params=FIRST,
         name="pick_queries",

time: 94.6 us -> 93.9 us (level)
  transfers between devices with their start and end apart: 40 -> 40, of which waited for: 13 -> 13; matrix products, arithmetic and copies ran while one was open for 1% -> 1% of each run, Pallas kernels for 33% -> 32%
where the time goes in v22:
time: 93.9 us; the launch traced here: 93.7 us
  starting transfers between devices  37.4 us (40%)
  Pallas kernels  31.9 us (34%)
  waiting for transfers between devices  18.3 us (19%)
  local copies, waits for them, and re-layouts  4.79 us (5%)
  between operations  1.01 us (1%)
    ppermute x38, starting transfers between devices, shift(): return lax.ppermute(x, axis, [(i, (i + by) % size) for i in range(size)])  33.5 us
    ppermute x38, waiting for transfers between devices, shift(): return lax.ppermute(x, axis, [(i, (i + by) % size) for i in range(size)])  15.3 us
    pallas_call x1, Pallas kernels, pack_rows(): pl.pallas_call(kernel, grid=(1,), in_specs=[pl.BlockSpec((lines, LANES),...  6.6 us
    pallas_call x1, Pallas kernels, partial_weights(): pl.pallas_call(kernel, in_specs=[SMEM] + [HBM] * n + [VMEM] * (CUTS * n)...  6.6 us
    unnamed x42, local copies, waits for them, and re-layouts  4.3 us
    pallas_call x1, Pallas kernels, early_scores(): pl.pallas_call(kernel, in_specs=[SMEM] + [VMEM] * (2 + n_other + n_rep *...  4.17 us
    ppermute x2, starting transfers between devices, swap(): return lax.ppermute(x, axis, [(i, i ^ bit) for i in range(size)])  3.91 us
    ppermute x2, waiting for transfers between devices, swap(): return lax.ppermute(x, axis, [(i, i ^ bit) for i in range(size)])  2.99 us
  transfers between devices with their start and end apart: 40, of which 13 were waited for; matrix products, arithmetic and copies ran while one was open for 1% of the time, Pallas kernels for 32%

profile of v22, /device:TPU:0, one launch (start us, length us, event | category | flops | bytes accessed | tf_op | source)
XLA Modules:
  0.0 93.7 jit_solution(5395884313917079035)
XLA Ops:
  0.5 1.9 %pick_queries.1 = (bf16[1,64,1024]{2,1,0:T(8,128)(2,1)}, bf16[1,64,1024]{2,1,0:T(8,128)(2,1)}, bf16[1,64,1024]{2,1,0:T(8,128)(2,1)}, bf16[1,64,1024]{2,1,0:T(8,128)(2,1)}) custom-call(s32[4,4]{1,0:T(4,128)} %pattern_ref.3, s32[16]{0:T(128)} %slot_ref.3, bf16[4,128,1024]{2,1,0:T(8,128)(2,1)} %in_ref.1), custom_call_target="tpu_custom_call" | custom-call | flops 1 | bytes 1 | tf_op jit(solution)/shard_map/pick_queries/pallas_call | solution.py:103
  2.4 2.6 %collective-permute-start.4 = (bf16[1,64,1024]{2,1,0:T(8,128)(2,1)}, bf16[1,64,1024]{2,1,0:T(8,128)(2,1)S(1)}, u32[]{:S(2)}, u32[]{:S(2)}) collective-permute-start(bf16[1,64,1024]{2,1,0:T(8,128)(2,1)} %get-tuple-element.50), channel_id=1, source_target_pairs={{0,4},{4,8},{8,12},{12,0},{1,5},{5,9},{9,13},{13,1},{2,6},{6,10},{... | collective-permute-start | bytes 393224 | tf_op jit(solution)/shard_map/ppermute | solution.py:23
  5.0 2.6 %collective-permute-start.5 = (bf16[1,64,1024]{2,1,0:T(8,128)(2,1)}, bf16[1,64,1024]{2,1,0:T(8,128)(2,1)S(1)}, u32[]{:S(2)}, u32[]{:S(2)}) collective-permute-start(bf16[1,64,1024]{2,1,0:T(8,128)(2,1)} %get-tuple-element.51), channel_id=1, source_target_pairs={{0,8},{4,12},{8,0},{12,4},{1,9},{5,13},{9,1},{13,5},{2,10},{6,14},... | collective-permute-start | bytes 393224 | tf_op jit(solution)/shard_map/ppermute | solution.py:23
  7.6 1.3 %collective-permute-start.6 = (bf16[1,64,1024]{2,1,0:T(8,128)(2,1)}, bf16[1,64,1024]{2,1,0:T(8,128)(2,1)S(1)}, u32[]{:S(2)}, u32[]{:S(2)}) collective-permute-start(bf16[1,64,1024]{2,1,0:T(8,128)(2,1)} %get-tuple-element.52), channel_id=1, source_target_pairs={{0,12},{4,0},{8,4},{12,8},{1,13},{5,1},{9,5},{13,9},{2,14},{6,2},{... | collective-permute-start | bytes 393224 | tf_op jit(solution)/shard_map/ppermute | solution.py:23
  8.9 1.5 %collective-permute-start.8 = (bf16[1,64,1024]{2,1,0:T(8,128)(2,1)}, bf16[1,64,1024]{2,1,0:T(8,128)(2,1)S(1)}, u32[]{:S(2)}, u32[]{:S(2)}) collective-permute-start(bf16[1,64,1024]{2,1,0:T(8,128)(2,1)} %get-tuple-element.54.refs_0_), channel_id=1, source_target_pairs={{0,16},{16,0},{1,17},{17,1},{2,18},{18,2},{3,19},{19,3},{4,20},{20... | collective-permute-start | bytes 393224 | tf_op jit(solution)/shard_map/ppermute | solution.py:23
  10.4 6.6 %pack_rows.1 = (bf16[256,1024]{1,0:T(8,128)(2,1)}, bf16[256,1024]{1,0:T(8,128)(2,1)}, bf16[48,1024]{1,0:T(8,128)(2,1)}, bf16[32,1024]{1,0:T(8,128)(2,1)}, bf16[6...) custom-call(s32[32,128]{1,0:T(8,128)} %bitcast.11, ...), custom_call_target="tpu_custom_call" | custom-call | flops 1 | bytes 1 | tf_op jit(solution)/shard_map/pack_rows/pallas_call | solution.py:247
  17.1 3.3 %collective-permute-start.21 = (bf16[256,1024]{1,0:T(8,128)(2,1)}, bf16[256,1024]{1,0:T(8,128)(2,1)S(1)}, u32[]{:S(2)}, u32[]{:S(2)}) collective-permute-start(bf16[256,1024]{1,0:T(8,128)(2,1)} %after.19), channel_id=1, source_target_pairs={{0,4},{4,8},{8,12},{12,0},{1,5},{5,9},{9,13},{13,1},{2,6},{6,10},{... | collective-permute-start | bytes 1572872 | tf_op jit(solution)/shard_map/ppermute | solution.py:23
  20.4 1.5 %collective-permute-start.9 = (bf16[1,64,1024]{2,1,0:T(8,128)(2,1)S(1)}, bf16[1,64,1024]{2,1,0:T(8,128)(2,1)S(1)}, u32[]{:S(2)}, u32[]{:S(2)}) collective-permute-start(bf16[1,64,1024]{2,1,0:T(8,128)(2,1)S(1)} %collective-permute-done.4.rest_0_.refs_2_.refs_1_), channel_id=1, source_target_pairs={{0,16},{16,0},{1,17},{17,1},{2,18},{18,2},{3,19},{19,3},{4,20},{20... | collective-permute-start | bytes 393224 | tf_op jit(solution)/shard_map/ppermute | solution.py:23
  21.9 0.5 collective-permute-start.10
  22.4 1.5 %collective-permute-start.11 = (bf16[1,64,1024]{2,1,0:T(8,128)(2,1)S(1)}, bf16[1,64,1024]{2,1,0:T(8,128)(2,1)S(1)}, u32[]{:S(2)}, u32[]{:S(2)}) collective-permute-start(bf16[1,64,1024]{2,1,0:T(8,128)(2,1)S(1)} %collective-permute-done.6.rest_2_.refs_4_.refs_3_), channel_id=1, source_target_pairs={{0,16},{16,0},{1,17},{17,1},{2,18},{18,2},{3,19},{19,3},{4,20},{20... | collective-permute-start | bytes 393224 | tf_op jit(solution)/shard_map/ppermute | solution.py:23
  23.9 1.6 %collective-permute-start.27 = (bf16[128,1024]{1,0:T(8,128)(2,1)}, bf16[128,1024]{1,0:T(8,128)(2,1)S(1)}, u32[]{:S(2)}, u32[]{:S(2)}) collective-permute-start(bf16[128,1024]{1,0:T(8,128)(2,1)} %after.28), channel_id=1, source_target_pairs={{0,8},{4,12},{8,0},{12,4},{1,9},{5,13},{9,1},{13,5},{2,10},{6,14},... | collective-permute-start | bytes 786440 | tf_op jit(solution)/shard_map/ppermute | solution.py:27
  25.6 0.8 row_table.1
  26.4 3.4 %copy-done = bf16[1,4096,1024]{2,1,0:T(8,128)(2,1)S(1)} copy-done((bf16[1,4096,1024]{2,1,0:T(8,128)(2,1)S(1)}, bf16[1,4096,1024]{2,1,0:T(8,128)(2,1)}, u32[]{:S(2)}) %copy-start) | copy-done | bytes 8388632
  29.8 2.5 %fetch.1 = (bf16[2048,1024]{1,0:T(8,128)(2,1)S(1)}, bf16[2048,1024]{1,0:T(8,128)(2,1)S(1)}) custom-call(s32[1]{0:T(128)} %bitcast.3.block_ref, bf16[4096,1024]{1,0:T(8,128)(2,1)S(1)} %bitcast.7, bf16[4096,1024]{1,0:T(8,128)(2,1)} %collective-permute-done.7.refs_1_, bf16[1,64,1024]{2,1,0:T(8,128)(2,1)S(1)} %collective-permute-done.4.rest_0_.refs_2_.refs_1_, ...), custom_call_target="tpu_custom_call" | custom-call | flops 1 | bytes 1 | tf_op jit(solution)/shard_map/fetch/pallas_call | solution.py:320
  32.4 1.2 %join_queries.1 = (bf16[128,256]{1,0:T(8,128)(2,1)S(1)}, bf16[128,256]{1,0:T(8,128)(2,1)S(1)}, bf16[128,256]{1,0:T(8,128)(2,1)S(1)}, bf16[128,256]{1,0:T(8,128)(...) custom-call(s32[4,4]{1,0:T(4,128)S(1)} %copy-done.15, ...), custom_call_target="tpu_custom_call" | custom-call | flops 1 | bytes 1 | tf_op jit(solution)/shard_map/join_queries/pallas_call | solution.py:148
  33.7 0.5 collective-permute-start.13
  34.3 0.7 collective-permute-done.12.refs_10_
  35.6 0.6 collective-permute-done.15.refs_13_
  36.7 0.7 collective-permute-start.22
  37.5 2.0 %collective-permute-start.24 = (bf16[32,1024]{1,0:T(8,128)(2,1)S(1)}, bf16[32,1024]{1,0:T(8,128)(2,1)S(1)}, u32[]{:S(2)}, u32[]{:S(2)}) collective-permute-start(bf16[32,1024]{1,0:T(8,128)(2,1)S(1)} %after.25), channel_id=1, source_target_pairs={{0,12},{4,0},{8,4},{12,8},{1,13},{5,1},{9,5},{13,9},{2,14},{6,2},{... | collective-permute-start | bytes 196616 | tf_op jit(solution)/shard_map/ppermute | solution.py:23
  39.5 2.3 %fetched_weights.1.refs_18_.refs_2_.refs_5_ = bf16[2048,256]{1,0:T(8,128)(2,1)S(1)} custom-call(bf16[2048,1024]{1,0:T(8,128)(2,1)S(1)} %get-tuple-element.55.refs_8_.refs_0_, bf16[2048,1024]{1,0:T(8,128)(2,1)S(1)} %get-tuple-element.56.refs_9_.refs_1_, bf16[128,256]{1,0:T(8,128)(2,1)S(1)} %get-tuple-element.58.refs_2_, ...), custom_call_target="tpu_custom_call" | custom-call | flops 1 | bytes 1 | tf_op jit(solution)/shard_map/fetched_weights/pallas_call | solution.py:347
  41.9 1.6 %collective-permute-start.20 = (bf16[2048,256]{1,0:T(8,128)(2,1)S(1)}, bf16[2048,256]{1,0:T(8,128)(2,1)}, u32[]{:S(2)}, u32[]{:S(2)}) collective-permute-start(bf16[2048,256]{1,0:T(8,128)(2,1)S(1)} %fetched_weights.1.refs_18_.refs_2_.refs_5_), channel_id=1, source_target_pairs={{0,2},{2,0},{1,3},{3,1},{4,6},{6,4},{5,7},{7,5},{8,10},{10,8},{9,1... | collective-permute-start | bytes 3145736 | tf_op jit(solution)/shard_map/ppermute | solution.py:23
  43.4 1.4 %collective-permute-done.27.refs_1_.refs_0_.refs_2_ = bf16[128,1024]{1,0:T(8,128)(2,1)S(1)} collective-permute-done((bf16[128,1024]{1,0:T(8,128)(2,1)}, bf16[128,1024]{1,0:T(8,128)(2,1)S(1)}, u32[]{:S(2)}, u32[]{:S(2)}) %collective-permute-start.27) | collective-permute-done | bytes 262176 | tf_op jit(solution)/shard_map/ppermute | solution.py:27
  44.8 0.8 stack.3
  45.6 2.3 %collective-permute-start.28 = (bf16[256,1024]{1,0:T(8,128)(2,1)}, bf16[256,1024]{1,0:T(8,128)(2,1)}, u32[]{:S(2)}, u32[]{:S(2)}) collective-permute-start(bf16[256,1024]{1,0:T(8,128)(2,1)} %stack.3), channel_id=1, source_target_pairs={{0,4},{4,0},{8,12},{12,8},{1,5},{5,1},{9,13},{13,9},{2,6},{6,2},{1... | collective-permute-start | bytes 1572872 | tf_op jit(solution)/shard_map/ppermute | solution.py:27
  48.2 3.1 %collective-permute-start.33 = (bf16[256,1024]{1,0:T(8,128)(2,1)}, bf16[256,1024]{1,0:T(8,128)(2,1)}, u32[]{:S(2)}, u32[]{:S(2)}) collective-permute-start(bf16[256,1024]{1,0:T(8,128)(2,1)} %after.32), channel_id=1, source_target_pairs={{0,8},{4,12},{8,0},{12,4},{1,9},{5,13},{9,1},{13,5},{2,10},{6,14},... | collective-permute-start | bytes 1572872 | tf_op jit(solution)/shard_map/ppermute | solution.py:23
  51.3 1.5 %collective-permute-start.26 = (s32[8,128]{1,0:T(8,128)S(1)}, s32[8,128]{1,0:T(8,128)S(1)}, u32[]{:S(2)}, u32[]{:S(2)}) collective-permute-start(s32[8,128]{1,0:T(8,128)S(1)} %get-tuple-element.57.refs_10_), channel_id=1, source_target_pairs={{0,16},{16,0},{1,17},{17,1},{2,18},{18,2},{3,19},{19,3},{4,20},{20... | collective-permute-start | bytes 12296 | tf_op jit(solution)/shard_map/ppermute | solution.py:23
  52.8 2.1 %collective-permute-done.26 = s32[8,128]{1,0:T(8,128)S(1)} collective-permute-done((s32[8,128]{1,0:T(8,128)S(1)}, s32[8,128]{1,0:T(8,128)S(1)}, u32[]{:S(2)}, u32[]{:S(2)}) %collective-permute-start.26) | collective-permute-done | bytes 4128 | tf_op jit(solution)/shard_map/ppermute | solution.py:23
  54.9 0.5 slice.3
  56.0 6.6 %partial_weights.1.rest_0_.refs_1_.refs_2_.refs_0_ = f32[2048,256]{1,0:T(8,128)S(1)} custom-call(s32[1]{0:T(128)} %bitcast.1.block_ref, bf16[4096,1024]{1,0:T(8,128)(2,1)S(1)} %bitcast.10, bf16[4096,1024]{1,0:T(8,128)(2,1)} %collective-permute-done.7.refs_1_, bf16[128,256]{1,0:T(8,128)(2,1)S(1)} %get-tuple-element.58.refs_2_, ...), custom_call_target="tpu_custom_call" | custom-call | flops 1 | bytes 1 | tf_op jit(solution)/shard_map/partial_weights/pallas_call | solution.py:287
  63.5 1.2 %collective-permute-done.29.refs_0_ = bf16[128,1024]{1,0:T(8,128)(2,1)S(1)} collective-permute-done((bf16[128,1024]{1,0:T(8,128)(2,1)}, bf16[128,1024]{1,0:T(8,128)(2,1)S(1)}, u32[]{:S(2)}, u32[]{:S(2)}) %collective-permute-start.29) | collective-permute-done | bytes 262176 | tf_op jit(solution)/shard_map/ppermute | solution.py:23
  65.3 2.4 %own_rows.1.refs_2_ = bf16[256,2048]{1,0:T(8,128)(2,1)S(1)} custom-call(s32[8,128]{1,0:T(8,128)S(1)} %copy-done.16, bf16[1024,2048]{1,0:T(8,128)(2,1)S(1)} %copy-done.1, f32[2048,256]{1,0:T(8,128)S(1)} %partial_weights.1.rest_0_.refs_1_.refs_2_.refs_0_), custom_call_target="tpu_custom_call" | custom-call | flops 1 | bytes 1 | tf_op jit(solution)/shard_map/own_rows/pallas_call | solution.py:189
  67.7 0.8 copy-done.10
  68.6 1.6 %collective-permute-done.28.refs_9_.refs_0_ = bf16[256,1024]{1,0:T(8,128)(2,1)} collective-permute-done((bf16[256,1024]{1,0:T(8,128)(2,1)}, bf16[256,1024]{1,0:T(8,128)(2,1)}, u32[]{:S(2)}, u32[]{:S(2)}) %collective-permute-start.28) | collective-permute-done | bytes 524320 | tf_op jit(solution)/shard_map/ppermute | solution.py:27
  70.2 0.5 collective-permute-start.35
  70.7 0.7 collective-permute-done.31.refs_1_
  71.5 3.2 %collective-permute-done.33.refs_0_ = bf16[256,1024]{1,0:T(8,128)(2,1)} collective-permute-done((bf16[256,1024]{1,0:T(8,128)(2,1)}, bf16[256,1024]{1,0:T(8,128)(2,1)}, u32[]{:S(2)}, u32[]{:S(2)}) %collective-permute-start.33) | collective-permute-done | bytes 524320 | tf_op jit(solution)/shard_map/ppermute | solution.py:23
  74.8 1.8 %collective-permute-start.37 = (bf16[64,1024]{1,0:T(8,128)(2,1)S(1)}, bf16[64,1024]{1,0:T(8,128)(2,1)S(1)}, u32[]{:S(2)}, u32[]{:S(2)}) collective-permute-start(bf16[64,1024]{1,0:T(8,128)(2,1)S(1)} %after.20.refs_3_), channel_id=1, source_target_pairs={{0,12},{4,0},{8,4},{12,8},{1,13},{5,1},{9,5},{13,9},{2,14},{6,2},{... | collective-permute-start | bytes 393224 | tf_op jit(solution)/shard_map/ppermute | solution.py:23
  76.7 0.7 collective-permute-start.41
  77.4 4.2 %early_scores.1 = (bf16[2048,512]{1,0:T(8,128)(2,1)S(1)}, f32[1024,128]{1,0:T(8,128)S(1)}, bf16[1024,128]{1,0:T(8,128)(2,1)S(1)}) custom-call(s32[4,4]{1,0:T(4,128)S(1)} %get-tuple-element.53.table_ref, f32[2048,256]{1,0:T(8,128)S(1)} %partial_weights.1.rest_0_.refs_1_.refs_2_.refs_0_, bf16[2048,256]{1,0:T(8,128)(2,1)} %collective-permute-done.20.refs_1_, ...), custom_call_target="tpu_custom_call" | custom-call | flops 1 | bytes 1 | tf_op jit(solution)/shard_map/early_scores/pallas_call | solution.py:512
  81.6 1.6 %collective-permute-start.36 = (bf16[1024,128]{1,0:T(8,128)(2,1)S(1)}, bf16[1024,128]{1,0:T(8,128)(2,1)S(1)}, u32[]{:S(2)}, u32[]{:S(2)}) collective-permute-start(bf16[1024,128]{1,0:T(8,128)(2,1)S(1)} %get-tuple-element.90.refs_1_), channel_id=1, source_target_pairs={{0,2},{2,0},{1,3},{3,1},{4,6},{6,4},{5,7},{7,5},{8,10},{10,8},{9,1... | collective-permute-start | bytes 786440 | tf_op jit(solution)/shard_map/ppermute | solution.py:23
  83.1 0.7 collective-permute-done.39.refs_0_
  83.9 1.7 %collective-permute-done.41.refs_0_ = bf16[48,1024]{1,0:T(8,128)(2,1)S(1)} collective-permute-done((bf16[48,1024]{1,0:T(8,128)(2,1)S(1)}, bf16[48,1024]{1,0:T(8,128)(2,1)S(1)}, u32[]{:S(2)}, u32[]{:S(2)}) %collective-permute-start.41) | collective-permute-done | bytes 98336 | tf_op jit(solution)/shard_map/ppermute | solution.py:23
  85.6 1.3 %collective-permute-done.42.refs_9_ = bf16[48,1024]{1,0:T(8,128)(2,1)S(1)} collective-permute-done((bf16[48,1024]{1,0:T(8,128)(2,1)S(1)}, bf16[48,1024]{1,0:T(8,128)(2,1)S(1)}, u32[]{:S(2)}, u32[]{:S(2)}) %collective-permute-start.42) | collective-permute-done | bytes 98336 | tf_op jit(solution)/shard_map/ppermute | solution.py:23
  86.9 0.7 late_scores.1
  87.7 1.6 %collective-permute-start.43 = (bf16[256,128]{1,0:T(8,128)(2,1)S(1)}, bf16[256,128]{1,0:T(8,128)(2,1)S(1)}, u32[]{:S(2)}, u32[]{:S(2)}) collective-permute-start(bf16[256,128]{1,0:T(8,128)(2,1)S(1)} %get-tuple-element.93), channel_id=1, source_target_pairs={{0,2},{2,0},{1,3},{3,1},{4,6},{6,4},{5,7},{7,5},{8,10},{10,8},{9,1... | collective-permute-start | bytes 196616 | tf_op jit(solution)/shard_map/ppermute | solution.py:23
  89.2 2.8 %collective-permute-done.43.refs_3_ = bf16[256,128]{1,0:T(8,128)(2,1)S(1)} collective-permute-done((bf16[256,128]{1,0:T(8,128)(2,1)S(1)}, bf16[256,128]{1,0:T(8,128)(2,1)S(1)}, u32[]{:S(2)}, u32[]{:S(2)}) %collective-permute-start.43) | collective-permute-done | bytes 65568 | tf_op jit(solution)/shard_map/ppermute | solution.py:23
  92.0 1.7 %merge.1 = f32[128,1024]{1,0:T(8,128)} custom-call(s32[4,4]{1,0:T(4,128)S(1)} %get-tuple-element.53.table_ref, f32[1024,128]{1,0:T(8,128)S(1)} %get-tuple-element.89.refs_0_, bf16[1024,128]{1,0:T(8,128)(2,1)S(1)} %collective-permute-done.36.refs_1_, f32[256,128]{1,0:T(8,128)S(1)} %get-tuple-element.92.refs_2_, ...), custom_call_target="tpu_custom_call" | custom-call | flops 1 | bytes 1 | tf_op jit(solution)/shard_map/merge/pallas_call | solution.py:572
  (113 shorter events, 3.8 us)
Async XLA Ops:
  0.0 25.6 %copy-start.13 = (s32[4096]{0:T(1024)S(1)}, s32[4096]{0:T(1024)}, u32[]{:S(2)}) copy-start(s32[4096]{0:T(1024)} %param.9) | copy-start | bytes 49156
  0.0 23.9 %collective-permute-start.7 = (bf16[4096,1024]{1,0:T(8,128)(2,1)}, bf16[4096,1024]{1,0:T(8,128)(2,1)}, u32[]{:S(2)}, u32[]{:S(2)}) collective-permute-start(bf16[4096,1024]{1,0:T(8,128)(2,1)} %bitcast.6), channel_id=1, source_target_pairs={{0,1},{1,0},{2,3},{3,2},{4,5},{5,4},{6,7},{7,6},{8,9},{9,8},{10,11... | collective-permute-start | bytes 25165832 | tf_op jit(solution)/shard_map/ppermute | solution.py:23
  2.4 14.6 %collective-permute-start.4 = (bf16[1,64,1024]{2,1,0:T(8,128)(2,1)}, bf16[1,64,1024]{2,1,0:T(8,128)(2,1)S(1)}, u32[]{:S(2)}, u32[]{:S(2)}) collective-permute-start(bf16[1,64,1024]{2,1,0:T(8,128)(2,1)} %get-tuple-element.50), channel_id=1, source_target_pairs={{0,4},{4,8},{8,12},{12,0},{1,5},{5,9},{9,13},{13,1},{2,6},{6,10},{... | collective-permute-start | bytes 393224 | tf_op jit(solution)/shard_map/ppermute | solution.py:23
  5.0 12.1 %collective-permute-start.5 = (bf16[1,64,1024]{2,1,0:T(8,128)(2,1)}, bf16[1,64,1024]{2,1,0:T(8,128)(2,1)S(1)}, u32[]{:S(2)}, u32[]{:S(2)}) collective-permute-start(bf16[1,64,1024]{2,1,0:T(8,128)(2,1)} %get-tuple-element.51), channel_id=1, source_target_pairs={{0,8},{4,12},{8,0},{12,4},{1,9},{5,13},{9,1},{13,5},{2,10},{6,14},... | collective-permute-start | bytes 393224 | tf_op jit(solution)/shard_map/ppermute | solution.py:23
  7.6 9.5 %collective-permute-start.6 = (bf16[1,64,1024]{2,1,0:T(8,128)(2,1)}, bf16[1,64,1024]{2,1,0:T(8,128)(2,1)S(1)}, u32[]{:S(2)}, u32[]{:S(2)}) collective-permute-start(bf16[1,64,1024]{2,1,0:T(8,128)(2,1)} %get-tuple-element.52), channel_id=1, source_target_pairs={{0,12},{4,0},{8,4},{12,8},{1,13},{5,1},{9,5},{13,9},{2,14},{6,2},{... | collective-permute-start | bytes 393224 | tf_op jit(solution)/shard_map/ppermute | solution.py:23
  8.9 13.5 %collective-permute-start.8 = (bf16[1,64,1024]{2,1,0:T(8,128)(2,1)}, bf16[1,64,1024]{2,1,0:T(8,128)(2,1)S(1)}, u32[]{:S(2)}, u32[]{:S(2)}) collective-permute-start(bf16[1,64,1024]{2,1,0:T(8,128)(2,1)} %get-tuple-element.54.refs_0_), channel_id=1, source_target_pairs={{0,16},{16,0},{1,17},{17,1},{2,18},{18,2},{3,19},{19,3},{4,20},{20... | collective-permute-start | bytes 393224 | tf_op jit(solution)/shard_map/ppermute | solution.py:23
  17.1 31.1 %collective-permute-start.21 = (bf16[256,1024]{1,0:T(8,128)(2,1)}, bf16[256,1024]{1,0:T(8,128)(2,1)S(1)}, u32[]{:S(2)}, u32[]{:S(2)}) collective-permute-start(bf16[256,1024]{1,0:T(8,128)(2,1)} %after.19), channel_id=1, source_target_pairs={{0,4},{4,8},{8,12},{12,0},{1,5},{5,9},{9,13},{13,1},{2,6},{6,10},{... | collective-permute-start | bytes 1572872 | tf_op jit(solution)/shard_map/ppermute | solution.py:23
  20.4 12.0 %collective-permute-start.9 = (bf16[1,64,1024]{2,1,0:T(8,128)(2,1)S(1)}, bf16[1,64,1024]{2,1,0:T(8,128)(2,1)S(1)}, u32[]{:S(2)}, u32[]{:S(2)}) collective-permute-start(bf16[1,64,1024]{2,1,0:T(8,128)(2,1)S(1)} %collective-permute-done.4.rest_0_.refs_2_.refs_1_), channel_id=1, source_target_pairs={{0,16},{16,0},{1,17},{17,1},{2,18},{18,2},{3,19},{19,3},{4,20},{20... | collective-permute-start | bytes 393224 | tf_op jit(solution)/shard_map/ppermute | solution.py:23
  21.9 10.4 %collective-permute-start.10 = (bf16[1,64,1024]{2,1,0:T(8,128)(2,1)S(1)}, bf16[1,64,1024]{2,1,0:T(8,128)(2,1)S(1)}, u32[]{:S(2)}, u32[]{:S(2)}) collective-permute-start(bf16[1,64,1024]{2,1,0:T(8,128)(2,1)S(1)} %collective-permute-done.5.rest_1_.refs_3_.refs_2_), channel_id=1, source_target_pairs={{0,16},{16,0},{1,17},{17,1},{2,18},{18,2},{3,19},{19,3},{4,20},{20... | collective-permute-start | bytes 393224 | tf_op jit(solution)/shard_map/ppermute | solution.py:23
  22.4 9.9 %collective-permute-start.11 = (bf16[1,64,1024]{2,1,0:T(8,128)(2,1)S(1)}, bf16[1,64,1024]{2,1,0:T(8,128)(2,1)S(1)}, u32[]{:S(2)}, u32[]{:S(2)}) collective-permute-start(bf16[1,64,1024]{2,1,0:T(8,128)(2,1)S(1)} %collective-permute-done.6.rest_2_.refs_4_.refs_3_), channel_id=1, source_target_pairs={{0,16},{16,0},{1,17},{17,1},{2,18},{18,2},{3,19},{19,3},{4,20},{20... | collective-permute-start | bytes 393224 | tf_op jit(solution)/shard_map/ppermute | solution.py:23
  23.9 20.9 %collective-permute-start.27 = (bf16[128,1024]{1,0:T(8,128)(2,1)}, bf16[128,1024]{1,0:T(8,128)(2,1)S(1)}, u32[]{:S(2)}, u32[]{:S(2)}) collective-permute-start(bf16[128,1024]{1,0:T(8,128)(2,1)} %after.28), channel_id=1, source_target_pairs={{0,8},{4,12},{8,0},{12,4},{1,9},{5,13},{9,1},{13,5},{2,10},{6,14},... | collective-permute-start | bytes 786440 | tf_op jit(solution)/shard_map/ppermute | solution.py:27
  32.4 5.1 %copy-start.14 = (bf16[32,1024]{1,0:T(8,128)(2,1)S(1)}, bf16[32,1024]{1,0:T(8,128)(2,1)}, u32[]{:S(2)}) copy-start(bf16[32,1024]{1,0:T(8,128)(2,1)} %get-tuple-element.80.refs_0_) | copy-start | bytes 196612
  33.6 1.3 %collective-permute-start.12 = (bf16[128,256]{1,0:T(8,128)(2,1)S(1)}, bf16[128,256]{1,0:T(8,128)(2,1)S(1)}, u32[]{:S(2)}, u32[]{:S(2)}) collective-permute-start(bf16[128,256]{1,0:T(8,128)(2,1)S(1)} %get-tuple-element.66), channel_id=1, source_target_pairs={{0,1},{1,0},{2,3},{3,2},{4,5},{5,4},{6,7},{7,6},{8,9},{9,8},{10,11... | collective-permute-start | bytes 196616 | tf_op jit(solution)/shard_map/ppermute | solution.py:23
  33.7 1.4 %collective-permute-start.13 = (bf16[128,256]{1,0:T(8,128)(2,1)S(1)}, bf16[128,256]{1,0:T(8,128)(2,1)S(1)}, u32[]{:S(2)}, u32[]{:S(2)}) collective-permute-start(bf16[128,256]{1,0:T(8,128)(2,1)S(1)} %get-tuple-element.67), channel_id=1, source_target_pairs={{0,1},{1,0},{2,3},{3,2},{4,5},{5,4},{6,7},{7,6},{8,9},{9,8},{10,11... | collective-permute-start | bytes 196616 | tf_op jit(solution)/shard_map/ppermute | solution.py:23
  34.2 1.3 %collective-permute-start.14 = (bf16[128,256]{1,0:T(8,128)(2,1)S(1)}, bf16[128,256]{1,0:T(8,128)(2,1)S(1)}, u32[]{:S(2)}, u32[]{:S(2)}) collective-permute-start(bf16[128,256]{1,0:T(8,128)(2,1)S(1)} %get-tuple-element.68), channel_id=1, source_target_pairs={{0,1},{1,0},{2,3},{3,2},{4,5},{5,4},{6,7},{7,6},{8,9},{9,8},{10,11... | collective-permute-start | bytes 196616 | tf_op jit(solution)/shard_map/ppermute | solution.py:23
  35.0 1.3 %collective-permute-start.15 = (bf16[128,256]{1,0:T(8,128)(2,1)S(1)}, bf16[128,256]{1,0:T(8,128)(2,1)S(1)}, u32[]{:S(2)}, u32[]{:S(2)}) collective-permute-start(bf16[128,256]{1,0:T(8,128)(2,1)S(1)} %get-tuple-element.69), channel_id=1, source_target_pairs={{0,1},{1,0},{2,3},{3,2},{4,5},{5,4},{6,7},{7,6},{8,9},{9,8},{10,11... | collective-permute-start | bytes 196616 | tf_op jit(solution)/shard_map/ppermute | solution.py:23
  35.1 1.3 %collective-permute-start.16 = (bf16[128,256]{1,0:T(8,128)(2,1)S(1)}, bf16[128,256]{1,0:T(8,128)(2,1)S(1)}, u32[]{:S(2)}, u32[]{:S(2)}) collective-permute-start(bf16[128,256]{1,0:T(8,128)(2,1)S(1)} %get-tuple-element.70), channel_id=1, source_target_pairs={{0,1},{1,0},{2,3},{3,2},{4,5},{5,4},{6,7},{7,6},{8,9},{9,8},{10,11... | collective-permute-start | bytes 196616 | tf_op jit(solution)/shard_map/ppermute | solution.py:23
  35.5 1.3 %collective-permute-start.17 = (bf16[128,256]{1,0:T(8,128)(2,1)S(1)}, bf16[128,256]{1,0:T(8,128)(2,1)S(1)}, u32[]{:S(2)}, u32[]{:S(2)}) collective-permute-start(bf16[128,256]{1,0:T(8,128)(2,1)S(1)} %get-tuple-element.71), channel_id=1, source_target_pairs={{0,1},{1,0},{2,3},{3,2},{4,5},{5,4},{6,7},{7,6},{8,9},{9,8},{10,11... | collective-permute-start | bytes 196616 | tf_op jit(solution)/shard_map/ppermute | solution.py:23
  36.2 1.3 %collective-permute-start.18 = (bf16[128,256]{1,0:T(8,128)(2,1)S(1)}, bf16[128,256]{1,0:T(8,128)(2,1)S(1)}, u32[]{:S(2)}, u32[]{:S(2)}) collective-permute-start(bf16[128,256]{1,0:T(8,128)(2,1)S(1)} %get-tuple-element.72), channel_id=1, source_target_pairs={{0,1},{1,0},{2,3},{3,2},{4,5},{5,4},{6,7},{7,6},{8,9},{9,8},{10,11... | collective-permute-start | bytes 196616 | tf_op jit(solution)/shard_map/ppermute | solution.py:23
  36.4 3.1 %collective-permute-start.19 = (bf16[128,256]{1,0:T(8,128)(2,1)S(1)}, bf16[128,256]{1,0:T(8,128)(2,1)S(1)}, u32[]{:S(2)}, u32[]{:S(2)}) collective-permute-start(bf16[128,256]{1,0:T(8,128)(2,1)S(1)} %get-tuple-element.73), channel_id=1, source_target_pairs={{0,1},{1,0},{2,3},{3,2},{4,5},{5,4},{6,7},{7,6},{8,9},{9,8},{10,11... | collective-permute-start | bytes 196616 | tf_op jit(solution)/shard_map/ppermute | solution.py:23
  36.7 11.5 %collective-permute-start.22 = (bf16[48,1024]{1,0:T(8,128)(2,1)S(1)}, bf16[48,1024]{1,0:T(8,128)(2,1)S(1)}, u32[]{:S(2)}, u32[]{:S(2)}) collective-permute-start(bf16[48,1024]{1,0:T(8,128)(2,1)S(1)} %after.23), channel_id=1, source_target_pairs={{0,12},{4,0},{8,4},{12,8},{1,13},{5,1},{9,5},{13,9},{2,14},{6,2},{... | collective-permute-start | bytes 294920 | tf_op jit(solution)/shard_map/ppermute | solution.py:23
  37.5 10.7 %collective-permute-start.24 = (bf16[32,1024]{1,0:T(8,128)(2,1)S(1)}, bf16[32,1024]{1,0:T(8,128)(2,1)S(1)}, u32[]{:S(2)}, u32[]{:S(2)}) collective-permute-start(bf16[32,1024]{1,0:T(8,128)(2,1)S(1)} %after.25), channel_id=1, source_target_pairs={{0,12},{4,0},{8,4},{12,8},{1,13},{5,1},{9,5},{13,9},{2,14},{6,2},{... | collective-permute-start | bytes 196616 | tf_op jit(solution)/shard_map/ppermute | solution.py:23
  39.5 16.5 %slice-start = ((s8[8388608]{0:T(1024)(128)(4,1)}), s8[4194304]{0:T(1024)(128)(4,1)S(1)}, s32[]{:S(2)}) async-start(s8[8388608]{0:T(1024)(128)(4,1)} %bitcast.8), calls=%async_computation | async-start | bytes 8388608
  39.5 5.3 %copy-start.4 = (bf16[128,1024]{1,0:T(8,128)(2,1)S(1)}, bf16[128,1024]{1,0:T(8,128)(2,1)}, u32[]{:S(2)}) copy-start(bf16[128,1024]{1,0:T(8,128)(2,1)} %get-tuple-element.83.refs_0_) | copy-start | bytes 786436
  39.5 16.5 %slice-start.1 = ((s8[8388608]{0:T(1024)(128)(4,1)}), s8[4194304]{0:T(1024)(128)(4,1)S(1)}, s32[]{:S(2)}) async-start(s8[8388608]{0:T(1024)(128)(4,1)} %bitcast.8), calls=%async_computation.1 | async-start | bytes 8388608
  41.9 34.7 %collective-permute-start.20 = (bf16[2048,256]{1,0:T(8,128)(2,1)S(1)}, bf16[2048,256]{1,0:T(8,128)(2,1)}, u32[]{:S(2)}, u32[]{:S(2)}) collective-permute-start(bf16[2048,256]{1,0:T(8,128)(2,1)S(1)} %fetched_weights.1.refs_18_.refs_2_.refs_5_), channel_id=1, source_target_pairs={{0,2},{2,0},{1,3},{3,1},{4,6},{6,4},{5,7},{7,5},{8,10},{10,8},{9,1... | collective-permute-start | bytes 3145736 | tf_op jit(solution)/shard_map/ppermute | solution.py:23
  45.6 24.6 %collective-permute-start.28 = (bf16[256,1024]{1,0:T(8,128)(2,1)}, bf16[256,1024]{1,0:T(8,128)(2,1)}, u32[]{:S(2)}, u32[]{:S(2)}) collective-permute-start(bf16[256,1024]{1,0:T(8,128)(2,1)} %stack.3), channel_id=1, source_target_pairs={{0,4},{4,0},{8,12},{12,8},{1,5},{5,1},{9,13},{13,9},{2,6},{6,2},{1... | collective-permute-start | bytes 1572872 | tf_op jit(solution)/shard_map/ppermute | solution.py:27
  48.2 14.4 %copy-start.6 = (bf16[32,1024]{1,0:T(8,128)(2,1)}, bf16[32,1024]{1,0:T(8,128)(2,1)S(1)}, u32[]{:S(2)}) copy-start(bf16[32,1024]{1,0:T(8,128)(2,1)S(1)} %collective-permute-done.24.refs_0_.refs_4_) | copy-start | bytes 196612
  48.2 7.8 %copy-start.2 = (bf16[256,1024]{1,0:T(8,128)(2,1)}, bf16[256,1024]{1,0:T(8,128)(2,1)S(1)}, u32[]{:S(2)}) copy-start(bf16[256,1024]{1,0:T(8,128)(2,1)S(1)} %collective-permute-done.21.refs_0_.refs_1_) | copy-start | bytes 1572868
  48.2 26.5 %collective-permute-start.33 = (bf16[256,1024]{1,0:T(8,128)(2,1)}, bf16[256,1024]{1,0:T(8,128)(2,1)}, u32[]{:S(2)}, u32[]{:S(2)}) collective-permute-start(bf16[256,1024]{1,0:T(8,128)(2,1)} %after.32), channel_id=1, source_target_pairs={{0,8},{4,12},{8,0},{12,4},{1,9},{5,13},{9,1},{13,5},{2,10},{6,14},... | collective-permute-start | bytes 1572872 | tf_op jit(solution)/shard_map/ppermute | solution.py:23
  51.3 3.6 %collective-permute-start.26 = (s32[8,128]{1,0:T(8,128)S(1)}, s32[8,128]{1,0:T(8,128)S(1)}, u32[]{:S(2)}, u32[]{:S(2)}) collective-permute-start(s32[8,128]{1,0:T(8,128)S(1)} %get-tuple-element.57.refs_10_), channel_id=1, source_target_pairs={{0,16},{16,0},{1,17},{17,1},{2,18},{18,2},{3,19},{19,3},{4,20},{20... | collective-permute-start | bytes 12296 | tf_op jit(solution)/shard_map/ppermute | solution.py:23
  56.0 6.6 %copy-start.18 = (bf16[128,1024]{1,0:T(8,128)(2,1)S(1)}, bf16[128,1024]{1,0:T(8,128)(2,1)}, u32[]{:S(2)}) copy-start(bf16[128,1024]{1,0:T(8,128)(2,1)} %get-tuple-element.81.refs_0_) | copy-start | bytes 786436
  62.9 1.8 %collective-permute-start.29 = (bf16[128,1024]{1,0:T(8,128)(2,1)}, bf16[128,1024]{1,0:T(8,128)(2,1)S(1)}, u32[]{:S(2)}, u32[]{:S(2)}) collective-permute-start(bf16[128,1024]{1,0:T(8,128)(2,1)} %get-tuple-element.83.refs_0_), channel_id=1, source_target_pairs={{0,1},{1,0},{2,3},{3,2},{4,5},{5,4},{6,7},{7,6},{8,9},{9,8},{10,11... | collective-permute-start | bytes 786440 | tf_op jit(solution)/shard_map/ppermute | solution.py:23
  63.0 1.9 %collective-permute-start.30 = (bf16[128,1024]{1,0:T(8,128)(2,1)S(1)}, bf16[128,1024]{1,0:T(8,128)(2,1)S(1)}, u32[]{:S(2)}, u32[]{:S(2)}) collective-permute-start(bf16[128,1024]{1,0:T(8,128)(2,1)S(1)} %after.29.refs_1_), channel_id=1, source_target_pairs={{0,1},{1,0},{2,3},{3,2},{4,5},{5,4},{6,7},{7,6},{8,9},{9,8},{10,11... | collective-permute-start | bytes 786440 | tf_op jit(solution)/shard_map/ppermute | solution.py:23
  64.7 3.9 %collective-permute-start.23 = (bf16[48,1024]{1,0:T(8,128)(2,1)S(1)}, bf16[48,1024]{1,0:T(8,128)(2,1)S(1)}, u32[]{:S(2)}, u32[]{:S(2)}) collective-permute-start(bf16[48,1024]{1,0:T(8,128)(2,1)S(1)} %after.24.refs_0_), channel_id=1, source_target_pairs={{0,1},{1,0},{2,3},{3,2},{4,5},{5,4},{6,7},{7,6},{8,9},{9,8},{10,11... | collective-permute-start | bytes 294920 | tf_op jit(solution)/shard_map/ppermute | solution.py:23
  64.9 3.7 %collective-permute-start.25 = (bf16[32,1024]{1,0:T(8,128)(2,1)S(1)}, bf16[32,1024]{1,0:T(8,128)(2,1)S(1)}, u32[]{:S(2)}, u32[]{:S(2)}) collective-permute-start(bf16[32,1024]{1,0:T(8,128)(2,1)S(1)} %after.26.refs_2_), channel_id=1, source_target_pairs={{0,1},{1,0},{2,3},{3,2},{4,5},{5,4},{6,7},{7,6},{8,9},{9,8},{10,11... | collective-permute-start | bytes 196616 | tf_op jit(solution)/shard_map/ppermute | solution.py:23
  70.2 1.2 %collective-permute-start.31 = (s32[8,128]{1,0:T(8,128)S(1)}, s32[8,128]{1,0:T(8,128)S(1)}, u32[]{:S(2)}, u32[]{:S(2)}) collective-permute-start(s32[8,128]{1,0:T(8,128)S(1)} %after.30), channel_id=1, source_target_pairs={{0,1},{1,0},{2,3},{3,2},{4,5},{5,4},{6,7},{7,6},{8,9},{9,8},{10,11... | collective-permute-start | bytes 12296 | tf_op jit(solution)/shard_map/ppermute | solution.py:23
  70.2 6.4 %collective-permute-start.35 = (bf16[256,1024]{1,0:T(8,128)(2,1)}, bf16[256,1024]{1,0:T(8,128)(2,1)S(1)}, u32[]{:S(2)}, u32[]{:S(2)}) collective-permute-start(bf16[256,1024]{1,0:T(8,128)(2,1)} %after.34.refs_9_), channel_id=1, source_target_pairs={{0,1},{1,0},{2,3},{3,2},{4,5},{5,4},{6,7},{7,6},{8,9},{9,8},{10,11... | collective-permute-start | bytes 1572872 | tf_op jit(solution)/shard_map/ppermute | solution.py:23
  71.4 6.0 %collective-permute-start.32 = (bf16[256,1024]{1,0:T(8,128)(2,1)S(1)}, bf16[256,1024]{1,0:T(8,128)(2,1)S(1)}, u32[]{:S(2)}, u32[]{:S(2)}) collective-permute-start(bf16[256,1024]{1,0:T(8,128)(2,1)S(1)} %after.31.refs_3_), channel_id=1, source_target_pairs={{0,1},{1,0},{2,3},{3,2},{4,5},{5,4},{6,7},{7,6},{8,9},{9,8},{10,11... | collective-permute-start | bytes 1572872 | tf_op jit(solution)/shard_map/ppermute | solution.py:23
  74.8 2.6 %collective-permute-start.34 = (bf16[256,1024]{1,0:T(8,128)(2,1)}, bf16[256,1024]{1,0:T(8,128)(2,1)S(1)}, u32[]{:S(2)}, u32[]{:S(2)}) collective-permute-start(bf16[256,1024]{1,0:T(8,128)(2,1)} %after.33.refs_5_), channel_id=1, source_target_pairs={{0,1},{1,0},{2,3},{3,2},{4,5},{5,4},{6,7},{7,6},{8,9},{9,8},{10,11... | collective-permute-start | bytes 1572872 | tf_op jit(solution)/shard_map/ppermute | solution.py:23
  74.8 8.4 %collective-permute-start.37 = (bf16[64,1024]{1,0:T(8,128)(2,1)S(1)}, bf16[64,1024]{1,0:T(8,128)(2,1)S(1)}, u32[]{:S(2)}, u32[]{:S(2)}) collective-permute-start(bf16[64,1024]{1,0:T(8,128)(2,1)S(1)} %after.20.refs_3_), channel_id=1, source_target_pairs={{0,12},{4,0},{8,4},{12,8},{1,13},{5,1},{9,5},{13,9},{2,14},{6,2},{... | collective-permute-start | bytes 393224 | tf_op jit(solution)/shard_map/ppermute | solution.py:23
  76.6 7.3 %collective-permute-start.39 = (bf16[64,1024]{1,0:T(8,128)(2,1)S(1)}, bf16[64,1024]{1,0:T(8,128)(2,1)S(1)}, u32[]{:S(2)}, u32[]{:S(2)}) collective-permute-start(bf16[64,1024]{1,0:T(8,128)(2,1)S(1)} %after.21.refs_4_), channel_id=1, source_target_pairs={{0,12},{4,0},{8,4},{12,8},{1,13},{5,1},{9,5},{13,9},{2,14},{6,2},{... | collective-permute-start | bytes 393224 | tf_op jit(solution)/shard_map/ppermute | solution.py:23
  76.7 8.9 %collective-permute-start.41 = (bf16[48,1024]{1,0:T(8,128)(2,1)S(1)}, bf16[48,1024]{1,0:T(8,128)(2,1)S(1)}, u32[]{:S(2)}, u32[]{:S(2)}) collective-permute-start(bf16[48,1024]{1,0:T(8,128)(2,1)S(1)} %after.22.refs_5_), channel_id=1, source_target_pairs={{0,12},{4,0},{8,4},{12,8},{1,13},{5,1},{9,5},{13,9},{2,14},{6,2},{... | collective-permute-start | bytes 294920 | tf_op jit(solution)/shard_map/ppermute | solution.py:23
  81.6 10.4 %collective-permute-start.36 = (bf16[1024,128]{1,0:T(8,128)(2,1)S(1)}, bf16[1024,128]{1,0:T(8,128)(2,1)S(1)}, u32[]{:S(2)}, u32[]{:S(2)}) collective-permute-start(bf16[1024,128]{1,0:T(8,128)(2,1)S(1)} %get-tuple-element.90.refs_1_), channel_id=1, source_target_pairs={{0,2},{2,0},{1,3},{3,1},{4,6},{6,4},{5,7},{7,5},{8,10},{10,8},{9,1... | collective-permute-start | bytes 786440 | tf_op jit(solution)/shard_map/ppermute | solution.py:23
  83.1 3.8 %collective-permute-start.38 = (bf16[64,1024]{1,0:T(8,128)(2,1)S(1)}, bf16[64,1024]{1,0:T(8,128)(2,1)S(1)}, u32[]{:S(2)}, u32[]{:S(2)}) collective-permute-start(bf16[64,1024]{1,0:T(8,128)(2,1)S(1)} %after.35.refs_4_), channel_id=1, source_target_pairs={{0,1},{1,0},{2,3},{3,2},{4,5},{5,4},{6,7},{7,6},{8,9},{9,8},{10,11... | collective-permute-start | bytes 393224 | tf_op jit(solution)/shard_map/ppermute | solution.py:23
  83.9 3.0 %collective-permute-start.40 = (bf16[64,1024]{1,0:T(8,128)(2,1)S(1)}, bf16[64,1024]{1,0:T(8,128)(2,1)S(1)}, u32[]{:S(2)}, u32[]{:S(2)}) collective-permute-start(bf16[64,1024]{1,0:T(8,128)(2,1)S(1)} %after.36.refs_6_), channel_id=1, source_target_pairs={{0,1},{1,0},{2,3},{3,2},{4,5},{5,4},{6,7},{7,6},{8,9},{9,8},{10,11... | collective-permute-start | bytes 393224 | tf_op jit(solution)/shard_map/ppermute | solution.py:23
  85.6 1.3 %collective-permute-start.42 = (bf16[48,1024]{1,0:T(8,128)(2,1)S(1)}, bf16[48,1024]{1,0:T(8,128)(2,1)S(1)}, u32[]{:S(2)}, u32[]{:S(2)}) collective-permute-start(bf16[48,1024]{1,0:T(8,128)(2,1)S(1)} %after.37.refs_8_), channel_id=1, source_target_pairs={{0,1},{1,0},{2,3},{3,2},{4,5},{5,4},{6,7},{7,6},{8,9},{9,8},{10,11... | collective-permute-start | bytes 294920 | tf_op jit(solution)/shard_map/ppermute | solution.py:23
  87.7 4.3 %collective-permute-start.43 = (bf16[256,128]{1,0:T(8,128)(2,1)S(1)}, bf16[256,128]{1,0:T(8,128)(2,1)S(1)}, u32[]{:S(2)}, u32[]{:S(2)}) collective-permute-start(bf16[256,128]{1,0:T(8,128)(2,1)S(1)} %get-tuple-element.93), channel_id=1, source_target_pairs={{0,2},{2,0},{1,3},{3,1},{4,6},{6,4},{5,7},{7,5},{8,10},{10,8},{9,1... | collective-permute-start | bytes 196616 | tf_op jit(solution)/shard_map/ppermute | solution.py:23
  (13 other events, 31.3 us)

commit v23 on v22

--- a/solution.py
+++ b/solution.py
@@ -204,8 +204,11 @@
     n_shard = ids.shape[0] // lines
 
     def kernel(ids_ref, train_ref, *rest):
-        outs, goal_ref = rest[:-1], rest[-1]
+        outs, goal_ref, held, sem = rest[:-3], rest[-3], rest[-2], rest[-1]
         me = lax.axis_index("shard")
+        mine = pl.ds(pl.multiple_of(lax.axis_index("rep") * columns, columns), columns)
+        copy = pltpu.make_async_copy(train_ref.at[:, mine], held, sem)
+        copy.start()
         own = ids_ref[...]
         masks = [(own == c).astype(F32) for c in range(n_shard)]
         stacked = jnp.concatenate(masks, axis=0).astype(BF16)
@@ -232,8 +235,10 @@
             goal = goal + masks[c] * place
         goal_ref[...] = goal.astype(I32)
 
+        copy.wait()
+
         def fill(out, base):
-            out[...] = select(goal_ref, train_ref, base, out.shape[0])
+            out[...] = select(goal_ref, held, base, out.shape[0])
 
         for out, (hops, first, _) in zip(outs, cuts):
             fill(out, lax.rem(me + hops, jnp.int32(n_shard)) * bulk + first)
@@ -249,10 +254,11 @@
         grid=(1,),
         in_specs=[
             pl.BlockSpec((lines, LANES), lambda i: (lax.axis_index("shard"), 0)),
-            pl.BlockSpec((rows, columns), lambda i: (0, lax.axis_index("rep"))),
+            ANY,
         ],
         out_specs=[VMEM] * len(shapes),
         out_shape=shapes,
+        scratch_shapes=[pltpu.VMEM((rows, columns), BF16), pltpu.SemaphoreType.DMA],
         cost_estimate=cost(2 * packed * rows * columns, 2 * (rows + packed) * columns),
         compiler_params=FIRST,
         name="pack_rows",

time: 93.9 us -> 94 us (level)
  transfers between devices with their start and end apart: 40 -> 40, of which waited for: 13 -> 13; matrix products, arithmetic and copies ran while one was open for 1% -> 1% of each run, Pallas kernels for 32% -> 33%
where the time goes in v23:
time: 94 us; the launch traced here: 93.7 us
  starting transfers between devices  37 us (39%)
  Pallas kernels  32.3 us (34%)
  waiting for transfers between devices  18.3 us (19%)
  local copies, waits for them, and re-layouts  4.79 us (5%)
  between operations  1.04 us (1%)
    ppermute x38, starting transfers between devices, shift(): return lax.ppermute(x, axis, [(i, (i + by) % size) for i in range(size)])  33.1 us
    ppermute x38, waiting for transfers between devices, shift(): return lax.ppermute(x, axis, [(i, (i + by) % size) for i in range(size)])  15.3 us
    pallas_call x1, Pallas kernels, pack_rows(): pl.pallas_call(kernel, grid=(1,), in_specs=[pl.BlockSpec((lines, LANES),...  6.94 us
    pallas_call x1, Pallas kernels, partial_weights(): pl.pallas_call(kernel, in_specs=[SMEM] + [HBM] * n + [VMEM] * (CUTS * n)...  6.6 us
    unnamed x42, local copies, waits for them, and re-layouts  4.3 us
    pallas_call x1, Pallas kernels, early_scores(): pl.pallas_call(kernel, in_specs=[SMEM] + [VMEM] * (2 + n_other + n_rep *...  4.17 us
    ppermute x2, starting transfers between devices, swap(): return lax.ppermute(x, axis, [(i, i ^ bit) for i in range(size)])  3.91 us
    ppermute x2, waiting for transfers between devices, swap(): return lax.ppermute(x, axis, [(i, i ^ bit) for i in range(size)])  2.98 us
  transfers between devices with their start and end apart: 40, of which 13 were waited for; matrix products, arithmetic and copies ran while one was open for 1% of the time, Pallas kernels for 33%

profile of v23, /device:TPU:0, one launch (start us, length us, event | category | flops | bytes accessed | tf_op | source)
XLA Modules:
  0.0 93.7 jit_solution(16526092298182423323)
XLA Ops:
  0.5 1.9 %pick_queries.1 = (bf16[1,64,1024]{2,1,0:T(8,128)(2,1)}, bf16[1,64,1024]{2,1,0:T(8,128)(2,1)}, bf16[1,64,1024]{2,1,0:T(8,128)(2,1)}, bf16[1,64,1024]{2,1,0:T(8,128)(2,1)}) custom-call(s32[4,4]{1,0:T(4,128)} %pattern_ref.3, s32[16]{0:T(128)} %slot_ref.3, bf16[4,128,1024]{2,1,0:T(8,128)(2,1)} %in_ref.1), custom_call_target="tpu_custom_call" | custom-call | flops 1 | bytes 1 | tf_op jit(solution)/shard_map/pick_queries/pallas_call | solution.py:103
  2.4 2.6 %collective-permute-start.4 = (bf16[1,64,1024]{2,1,0:T(8,128)(2,1)}, bf16[1,64,1024]{2,1,0:T(8,128)(2,1)S(1)}, u32[]{:S(2)}, u32[]{:S(2)}) collective-permute-start(bf16[1,64,1024]{2,1,0:T(8,128)(2,1)} %get-tuple-element.50), channel_id=1, source_target_pairs={{0,4},{4,8},{8,12},{12,0},{1,5},{5,9},{9,13},{13,1},{2,6},{6,10},{... | collective-permute-start | bytes 393224 | tf_op jit(solution)/shard_map/ppermute | solution.py:23
  5.0 2.6 %collective-permute-start.5 = (bf16[1,64,1024]{2,1,0:T(8,128)(2,1)}, bf16[1,64,1024]{2,1,0:T(8,128)(2,1)S(1)}, u32[]{:S(2)}, u32[]{:S(2)}) collective-permute-start(bf16[1,64,1024]{2,1,0:T(8,128)(2,1)} %get-tuple-element.51), channel_id=1, source_target_pairs={{0,8},{4,12},{8,0},{12,4},{1,9},{5,13},{9,1},{13,5},{2,10},{6,14},... | collective-permute-start | bytes 393224 | tf_op jit(solution)/shard_map/ppermute | solution.py:23
  7.6 1.3 %collective-permute-start.6 = (bf16[1,64,1024]{2,1,0:T(8,128)(2,1)}, bf16[1,64,1024]{2,1,0:T(8,128)(2,1)S(1)}, u32[]{:S(2)}, u32[]{:S(2)}) collective-permute-start(bf16[1,64,1024]{2,1,0:T(8,128)(2,1)} %get-tuple-element.52), channel_id=1, source_target_pairs={{0,12},{4,0},{8,4},{12,8},{1,13},{5,1},{9,5},{13,9},{2,14},{6,2},{... | collective-permute-start | bytes 393224 | tf_op jit(solution)/shard_map/ppermute | solution.py:23
  8.9 1.5 %collective-permute-start.8 = (bf16[1,64,1024]{2,1,0:T(8,128)(2,1)}, bf16[1,64,1024]{2,1,0:T(8,128)(2,1)S(1)}, u32[]{:S(2)}, u32[]{:S(2)}) collective-permute-start(bf16[1,64,1024]{2,1,0:T(8,128)(2,1)} %get-tuple-element.54.refs_0_), channel_id=1, source_target_pairs={{0,16},{16,0},{1,17},{17,1},{2,18},{18,2},{3,19},{19,3},{4,20},{20... | collective-permute-start | bytes 393224 | tf_op jit(solution)/shard_map/ppermute | solution.py:23
  10.4 6.9 %pack_rows.1 = (bf16[256,1024]{1,0:T(8,128)(2,1)}, bf16[256,1024]{1,0:T(8,128)(2,1)}, bf16[48,1024]{1,0:T(8,128)(2,1)}, bf16[32,1024]{1,0:T(8,128)(2,1)}, bf16[6...) custom-call(s32[32,128]{1,0:T(8,128)} %bitcast.11, ...), custom_call_target="tpu_custom_call" | custom-call | flops 1 | bytes 1 | tf_op jit(solution)/shard_map/pack_rows/pallas_call | solution.py:252
  17.4 2.9 %collective-permute-start.21 = (bf16[256,1024]{1,0:T(8,128)(2,1)}, bf16[256,1024]{1,0:T(8,128)(2,1)S(1)}, u32[]{:S(2)}, u32[]{:S(2)}) collective-permute-start(bf16[256,1024]{1,0:T(8,128)(2,1)} %after.19), channel_id=1, source_target_pairs={{0,4},{4,8},{8,12},{12,0},{1,5},{5,9},{9,13},{13,1},{2,6},{6,10},{... | collective-permute-start | bytes 1572872 | tf_op jit(solution)/shard_map/ppermute | solution.py:23
  20.4 1.5 %collective-permute-start.9 = (bf16[1,64,1024]{2,1,0:T(8,128)(2,1)S(1)}, bf16[1,64,1024]{2,1,0:T(8,128)(2,1)S(1)}, u32[]{:S(2)}, u32[]{:S(2)}) collective-permute-start(bf16[1,64,1024]{2,1,0:T(8,128)(2,1)S(1)} %collective-permute-done.4.rest_0_.refs_2_.refs_1_), channel_id=1, source_target_pairs={{0,16},{16,0},{1,17},{17,1},{2,18},{18,2},{3,19},{19,3},{4,20},{20... | collective-permute-start | bytes 393224 | tf_op jit(solution)/shard_map/ppermute | solution.py:23
  21.9 0.5 collective-permute-start.10
  22.4 1.5 %collective-permute-start.11 = (bf16[1,64,1024]{2,1,0:T(8,128)(2,1)S(1)}, bf16[1,64,1024]{2,1,0:T(8,128)(2,1)S(1)}, u32[]{:S(2)}, u32[]{:S(2)}) collective-permute-start(bf16[1,64,1024]{2,1,0:T(8,128)(2,1)S(1)} %collective-permute-done.6.rest_2_.refs_4_.refs_3_), channel_id=1, source_target_pairs={{0,16},{16,0},{1,17},{17,1},{2,18},{18,2},{3,19},{19,3},{4,20},{20... | collective-permute-start | bytes 393224 | tf_op jit(solution)/shard_map/ppermute | solution.py:23
  23.9 1.6 %collective-permute-start.27 = (bf16[128,1024]{1,0:T(8,128)(2,1)}, bf16[128,1024]{1,0:T(8,128)(2,1)S(1)}, u32[]{:S(2)}, u32[]{:S(2)}) collective-permute-start(bf16[128,1024]{1,0:T(8,128)(2,1)} %after.28), channel_id=1, source_target_pairs={{0,8},{4,12},{8,0},{12,4},{1,9},{5,13},{9,1},{13,5},{2,10},{6,14},... | collective-permute-start | bytes 786440 | tf_op jit(solution)/shard_map/ppermute | solution.py:27
  25.6 0.8 row_table.1
  26.4 3.4 %copy-done = bf16[1,4096,1024]{2,1,0:T(8,128)(2,1)S(1)} copy-done((bf16[1,4096,1024]{2,1,0:T(8,128)(2,1)S(1)}, bf16[1,4096,1024]{2,1,0:T(8,128)(2,1)}, u32[]{:S(2)}) %copy-start) | copy-done | bytes 8388632
  29.8 2.5 %fetch.1 = (bf16[2048,1024]{1,0:T(8,128)(2,1)S(1)}, bf16[2048,1024]{1,0:T(8,128)(2,1)S(1)}) custom-call(s32[1]{0:T(128)} %bitcast.3.block_ref, bf16[4096,1024]{1,0:T(8,128)(2,1)S(1)} %bitcast.7, bf16[4096,1024]{1,0:T(8,128)(2,1)} %collective-permute-done.7.refs_1_, bf16[1,64,1024]{2,1,0:T(8,128)(2,1)S(1)} %collective-permute-done.4.rest_0_.refs_2_.refs_1_, ...), custom_call_target="tpu_custom_call" | custom-call | flops 1 | bytes 1 | tf_op jit(solution)/shard_map/fetch/pallas_call | solution.py:326
  32.4 1.2 %join_queries.1 = (bf16[128,256]{1,0:T(8,128)(2,1)S(1)}, bf16[128,256]{1,0:T(8,128)(2,1)S(1)}, bf16[128,256]{1,0:T(8,128)(2,1)S(1)}, bf16[128,256]{1,0:T(8,128)(...) custom-call(s32[4,4]{1,0:T(4,128)S(1)} %copy-done.15, ...), custom_call_target="tpu_custom_call" | custom-call | flops 1 | bytes 1 | tf_op jit(solution)/shard_map/join_queries/pallas_call | solution.py:148
  33.7 0.5 collective-permute-start.13
  34.3 0.7 collective-permute-done.12.refs_10_
  35.6 0.6 collective-permute-done.15.refs_13_
  36.7 0.7 collective-permute-start.22
  37.5 2.0 %collective-permute-start.24 = (bf16[32,1024]{1,0:T(8,128)(2,1)S(1)}, bf16[32,1024]{1,0:T(8,128)(2,1)S(1)}, u32[]{:S(2)}, u32[]{:S(2)}) collective-permute-start(bf16[32,1024]{1,0:T(8,128)(2,1)S(1)} %after.25), channel_id=1, source_target_pairs={{0,12},{4,0},{8,4},{12,8},{1,13},{5,1},{9,5},{13,9},{2,14},{6,2},{... | collective-permute-start | bytes 196616 | tf_op jit(solution)/shard_map/ppermute | solution.py:23
  39.5 2.3 %fetched_weights.1.refs_18_.refs_2_.refs_5_ = bf16[2048,256]{1,0:T(8,128)(2,1)S(1)} custom-call(bf16[2048,1024]{1,0:T(8,128)(2,1)S(1)} %get-tuple-element.55.refs_8_.refs_0_, bf16[2048,1024]{1,0:T(8,128)(2,1)S(1)} %get-tuple-element.56.refs_9_.refs_1_, bf16[128,256]{1,0:T(8,128)(2,1)S(1)} %get-tuple-element.58.refs_2_, ...), custom_call_target="tpu_custom_call" | custom-call | flops 1 | bytes 1 | tf_op jit(solution)/shard_map/fetched_weights/pallas_call | solution.py:353
  41.9 1.6 %collective-permute-start.20 = (bf16[2048,256]{1,0:T(8,128)(2,1)S(1)}, bf16[2048,256]{1,0:T(8,128)(2,1)}, u32[]{:S(2)}, u32[]{:S(2)}) collective-permute-start(bf16[2048,256]{1,0:T(8,128)(2,1)S(1)} %fetched_weights.1.refs_18_.refs_2_.refs_5_), channel_id=1, source_target_pairs={{0,2},{2,0},{1,3},{3,1},{4,6},{6,4},{5,7},{7,5},{8,10},{10,8},{9,1... | collective-permute-start | bytes 3145736 | tf_op jit(solution)/shard_map/ppermute | solution.py:23
  43.4 1.4 %collective-permute-done.27.refs_1_.refs_0_.refs_2_ = bf16[128,1024]{1,0:T(8,128)(2,1)S(1)} collective-permute-done((bf16[128,1024]{1,0:T(8,128)(2,1)}, bf16[128,1024]{1,0:T(8,128)(2,1)S(1)}, u32[]{:S(2)}, u32[]{:S(2)}) %collective-permute-start.27) | collective-permute-done | bytes 262176 | tf_op jit(solution)/shard_map/ppermute | solution.py:27
  44.8 0.8 stack.3
  45.6 2.3 %collective-permute-start.28 = (bf16[256,1024]{1,0:T(8,128)(2,1)}, bf16[256,1024]{1,0:T(8,128)(2,1)}, u32[]{:S(2)}, u32[]{:S(2)}) collective-permute-start(bf16[256,1024]{1,0:T(8,128)(2,1)} %stack.3), channel_id=1, source_target_pairs={{0,4},{4,0},{8,12},{12,8},{1,5},{5,1},{9,13},{13,9},{2,6},{6,2},{1... | collective-permute-start | bytes 1572872 | tf_op jit(solution)/shard_map/ppermute | solution.py:27
  48.2 3.1 %collective-permute-start.33 = (bf16[256,1024]{1,0:T(8,128)(2,1)}, bf16[256,1024]{1,0:T(8,128)(2,1)}, u32[]{:S(2)}, u32[]{:S(2)}) collective-permute-start(bf16[256,1024]{1,0:T(8,128)(2,1)} %after.32), channel_id=1, source_target_pairs={{0,8},{4,12},{8,0},{12,4},{1,9},{5,13},{9,1},{13,5},{2,10},{6,14},... | collective-permute-start | bytes 1572872 | tf_op jit(solution)/shard_map/ppermute | solution.py:23
  51.3 1.5 %collective-permute-start.26 = (s32[8,128]{1,0:T(8,128)S(1)}, s32[8,128]{1,0:T(8,128)S(1)}, u32[]{:S(2)}, u32[]{:S(2)}) collective-permute-start(s32[8,128]{1,0:T(8,128)S(1)} %get-tuple-element.57.refs_10_), channel_id=1, source_target_pairs={{0,16},{16,0},{1,17},{17,1},{2,18},{18,2},{3,19},{19,3},{4,20},{20... | collective-permute-start | bytes 12296 | tf_op jit(solution)/shard_map/ppermute | solution.py:23
  52.8 2.1 %collective-permute-done.26 = s32[8,128]{1,0:T(8,128)S(1)} collective-permute-done((s32[8,128]{1,0:T(8,128)S(1)}, s32[8,128]{1,0:T(8,128)S(1)}, u32[]{:S(2)}, u32[]{:S(2)}) %collective-permute-start.26) | collective-permute-done | bytes 4128 | tf_op jit(solution)/shard_map/ppermute | solution.py:23
  54.9 0.5 slice.3
  56.0 6.6 %partial_weights.1.rest_0_.refs_1_.refs_2_.refs_0_ = f32[2048,256]{1,0:T(8,128)S(1)} custom-call(s32[1]{0:T(128)} %bitcast.1.block_ref, bf16[4096,1024]{1,0:T(8,128)(2,1)S(1)} %bitcast.10, bf16[4096,1024]{1,0:T(8,128)(2,1)} %collective-permute-done.7.refs_1_, bf16[128,256]{1,0:T(8,128)(2,1)S(1)} %get-tuple-element.58.refs_2_, ...), custom_call_target="tpu_custom_call" | custom-call | flops 1 | bytes 1 | tf_op jit(solution)/shard_map/partial_weights/pallas_call | solution.py:293
  63.5 1.2 %collective-permute-done.29.refs_0_ = bf16[128,1024]{1,0:T(8,128)(2,1)S(1)} collective-permute-done((bf16[128,1024]{1,0:T(8,128)(2,1)}, bf16[128,1024]{1,0:T(8,128)(2,1)S(1)}, u32[]{:S(2)}, u32[]{:S(2)}) %collective-permute-start.29) | collective-permute-done | bytes 262176 | tf_op jit(solution)/shard_map/ppermute | solution.py:23
  65.3 2.4 %own_rows.1.refs_2_ = bf16[256,2048]{1,0:T(8,128)(2,1)S(1)} custom-call(s32[8,128]{1,0:T(8,128)S(1)} %copy-done.16, bf16[1024,2048]{1,0:T(8,128)(2,1)S(1)} %copy-done.1, f32[2048,256]{1,0:T(8,128)S(1)} %partial_weights.1.rest_0_.refs_1_.refs_2_.refs_0_), custom_call_target="tpu_custom_call" | custom-call | flops 1 | bytes 1 | tf_op jit(solution)/shard_map/own_rows/pallas_call | solution.py:189
  67.7 0.8 copy-done.10
  68.6 1.6 %collective-permute-done.28.refs_9_.refs_0_ = bf16[256,1024]{1,0:T(8,128)(2,1)} collective-permute-done((bf16[256,1024]{1,0:T(8,128)(2,1)}, bf16[256,1024]{1,0:T(8,128)(2,1)}, u32[]{:S(2)}, u32[]{:S(2)}) %collective-permute-start.28) | collective-permute-done | bytes 524320 | tf_op jit(solution)/shard_map/ppermute | solution.py:27
  70.2 0.5 collective-permute-start.35
  70.7 0.7 collective-permute-done.31.refs_1_
  71.5 3.2 %collective-permute-done.33.refs_0_ = bf16[256,1024]{1,0:T(8,128)(2,1)} collective-permute-done((bf16[256,1024]{1,0:T(8,128)(2,1)}, bf16[256,1024]{1,0:T(8,128)(2,1)}, u32[]{:S(2)}, u32[]{:S(2)}) %collective-permute-start.33) | collective-permute-done | bytes 524320 | tf_op jit(solution)/shard_map/ppermute | solution.py:23
  74.8 1.8 %collective-permute-start.37 = (bf16[64,1024]{1,0:T(8,128)(2,1)S(1)}, bf16[64,1024]{1,0:T(8,128)(2,1)S(1)}, u32[]{:S(2)}, u32[]{:S(2)}) collective-permute-start(bf16[64,1024]{1,0:T(8,128)(2,1)S(1)} %after.20.refs_3_), channel_id=1, source_target_pairs={{0,12},{4,0},{8,4},{12,8},{1,13},{5,1},{9,5},{13,9},{2,14},{6,2},{... | collective-permute-start | bytes 393224 | tf_op jit(solution)/shard_map/ppermute | solution.py:23
  76.7 0.7 collective-permute-start.41
  77.4 4.2 %early_scores.1 = (bf16[2048,512]{1,0:T(8,128)(2,1)S(1)}, f32[1024,128]{1,0:T(8,128)S(1)}, bf16[1024,128]{1,0:T(8,128)(2,1)S(1)}) custom-call(s32[4,4]{1,0:T(4,128)S(1)} %get-tuple-element.53.table_ref, f32[2048,256]{1,0:T(8,128)S(1)} %partial_weights.1.rest_0_.refs_1_.refs_2_.refs_0_, bf16[2048,256]{1,0:T(8,128)(2,1)} %collective-permute-done.20.refs_1_, ...), custom_call_target="tpu_custom_call" | custom-call | flops 1 | bytes 1 | tf_op jit(solution)/shard_map/early_scores/pallas_call | solution.py:518
  81.6 1.6 %collective-permute-start.36 = (bf16[1024,128]{1,0:T(8,128)(2,1)S(1)}, bf16[1024,128]{1,0:T(8,128)(2,1)S(1)}, u32[]{:S(2)}, u32[]{:S(2)}) collective-permute-start(bf16[1024,128]{1,0:T(8,128)(2,1)S(1)} %get-tuple-element.90.refs_1_), channel_id=1, source_target_pairs={{0,2},{2,0},{1,3},{3,1},{4,6},{6,4},{5,7},{7,5},{8,10},{10,8},{9,1... | collective-permute-start | bytes 786440 | tf_op jit(solution)/shard_map/ppermute | solution.py:23
  83.1 0.7 collective-permute-done.39.refs_0_
  83.9 1.7 %collective-permute-done.41.refs_0_ = bf16[48,1024]{1,0:T(8,128)(2,1)S(1)} collective-permute-done((bf16[48,1024]{1,0:T(8,128)(2,1)S(1)}, bf16[48,1024]{1,0:T(8,128)(2,1)S(1)}, u32[]{:S(2)}, u32[]{:S(2)}) %collective-permute-start.41) | collective-permute-done | bytes 98336 | tf_op jit(solution)/shard_map/ppermute | solution.py:23
  85.6 1.3 %collective-permute-done.42.refs_9_ = bf16[48,1024]{1,0:T(8,128)(2,1)S(1)} collective-permute-done((bf16[48,1024]{1,0:T(8,128)(2,1)S(1)}, bf16[48,1024]{1,0:T(8,128)(2,1)S(1)}, u32[]{:S(2)}, u32[]{:S(2)}) %collective-permute-start.42) | collective-permute-done | bytes 98336 | tf_op jit(solution)/shard_map/ppermute | solution.py:23
  86.9 0.7 late_scores.1
  87.7 1.6 %collective-permute-start.43 = (bf16[256,128]{1,0:T(8,128)(2,1)S(1)}, bf16[256,128]{1,0:T(8,128)(2,1)S(1)}, u32[]{:S(2)}, u32[]{:S(2)}) collective-permute-start(bf16[256,128]{1,0:T(8,128)(2,1)S(1)} %get-tuple-element.93), channel_id=1, source_target_pairs={{0,2},{2,0},{1,3},{3,1},{4,6},{6,4},{5,7},{7,5},{8,10},{10,8},{9,1... | collective-permute-start | bytes 196616 | tf_op jit(solution)/shard_map/ppermute | solution.py:23
  89.2 2.8 %collective-permute-done.43.refs_3_ = bf16[256,128]{1,0:T(8,128)(2,1)S(1)} collective-permute-done((bf16[256,128]{1,0:T(8,128)(2,1)S(1)}, bf16[256,128]{1,0:T(8,128)(2,1)S(1)}, u32[]{:S(2)}, u32[]{:S(2)}) %collective-permute-start.43) | collective-permute-done | bytes 65568 | tf_op jit(solution)/shard_map/ppermute | solution.py:23
  92.0 1.7 %merge.1 = f32[128,1024]{1,0:T(8,128)} custom-call(s32[4,4]{1,0:T(4,128)S(1)} %get-tuple-element.53.table_ref, f32[1024,128]{1,0:T(8,128)S(1)} %get-tuple-element.89.refs_0_, bf16[1024,128]{1,0:T(8,128)(2,1)S(1)} %collective-permute-done.36.refs_1_, f32[256,128]{1,0:T(8,128)S(1)} %get-tuple-element.92.refs_2_, ...), custom_call_target="tpu_custom_call" | custom-call | flops 1 | bytes 1 | tf_op jit(solution)/shard_map/merge/pallas_call | solution.py:578
  (113 shorter events, 3.8 us)
Async XLA Ops:
  0.0 25.6 %copy-start.13 = (s32[4096]{0:T(1024)S(1)}, s32[4096]{0:T(1024)}, u32[]{:S(2)}) copy-start(s32[4096]{0:T(1024)} %param.9) | copy-start | bytes 49156
  0.0 23.9 %collective-permute-start.7 = (bf16[4096,1024]{1,0:T(8,128)(2,1)}, bf16[4096,1024]{1,0:T(8,128)(2,1)}, u32[]{:S(2)}, u32[]{:S(2)}) collective-permute-start(bf16[4096,1024]{1,0:T(8,128)(2,1)} %bitcast.6), channel_id=1, source_target_pairs={{0,1},{1,0},{2,3},{3,2},{4,5},{5,4},{6,7},{7,6},{8,9},{9,8},{10,11... | collective-permute-start | bytes 25165832 | tf_op jit(solution)/shard_map/ppermute | solution.py:23
  2.4 15.0 %collective-permute-start.4 = (bf16[1,64,1024]{2,1,0:T(8,128)(2,1)}, bf16[1,64,1024]{2,1,0:T(8,128)(2,1)S(1)}, u32[]{:S(2)}, u32[]{:S(2)}) collective-permute-start(bf16[1,64,1024]{2,1,0:T(8,128)(2,1)} %get-tuple-element.50), channel_id=1, source_target_pairs={{0,4},{4,8},{8,12},{12,0},{1,5},{5,9},{9,13},{13,1},{2,6},{6,10},{... | collective-permute-start | bytes 393224 | tf_op jit(solution)/shard_map/ppermute | solution.py:23
  5.0 12.4 %collective-permute-start.5 = (bf16[1,64,1024]{2,1,0:T(8,128)(2,1)}, bf16[1,64,1024]{2,1,0:T(8,128)(2,1)S(1)}, u32[]{:S(2)}, u32[]{:S(2)}) collective-permute-start(bf16[1,64,1024]{2,1,0:T(8,128)(2,1)} %get-tuple-element.51), channel_id=1, source_target_pairs={{0,8},{4,12},{8,0},{12,4},{1,9},{5,13},{9,1},{13,5},{2,10},{6,14},... | collective-permute-start | bytes 393224 | tf_op jit(solution)/shard_map/ppermute | solution.py:23
  7.6 9.8 %collective-permute-start.6 = (bf16[1,64,1024]{2,1,0:T(8,128)(2,1)}, bf16[1,64,1024]{2,1,0:T(8,128)(2,1)S(1)}, u32[]{:S(2)}, u32[]{:S(2)}) collective-permute-start(bf16[1,64,1024]{2,1,0:T(8,128)(2,1)} %get-tuple-element.52), channel_id=1, source_target_pairs={{0,12},{4,0},{8,4},{12,8},{1,13},{5,1},{9,5},{13,9},{2,14},{6,2},{... | collective-permute-start | bytes 393224 | tf_op jit(solution)/shard_map/ppermute | solution.py:23
  8.9 13.5 %collective-permute-start.8 = (bf16[1,64,1024]{2,1,0:T(8,128)(2,1)}, bf16[1,64,1024]{2,1,0:T(8,128)(2,1)S(1)}, u32[]{:S(2)}, u32[]{:S(2)}) collective-permute-start(bf16[1,64,1024]{2,1,0:T(8,128)(2,1)} %get-tuple-element.54.refs_0_), channel_id=1, source_target_pairs={{0,16},{16,0},{1,17},{17,1},{2,18},{18,2},{3,19},{19,3},{4,20},{20... | collective-permute-start | bytes 393224 | tf_op jit(solution)/shard_map/ppermute | solution.py:23
  17.4 30.8 %collective-permute-start.21 = (bf16[256,1024]{1,0:T(8,128)(2,1)}, bf16[256,1024]{1,0:T(8,128)(2,1)S(1)}, u32[]{:S(2)}, u32[]{:S(2)}) collective-permute-start(bf16[256,1024]{1,0:T(8,128)(2,1)} %after.19), channel_id=1, source_target_pairs={{0,4},{4,8},{8,12},{12,0},{1,5},{5,9},{9,13},{13,1},{2,6},{6,10},{... | collective-permute-start | bytes 1572872 | tf_op jit(solution)/shard_map/ppermute | solution.py:23
  20.4 12.0 %collective-permute-start.9 = (bf16[1,64,1024]{2,1,0:T(8,128)(2,1)S(1)}, bf16[1,64,1024]{2,1,0:T(8,128)(2,1)S(1)}, u32[]{:S(2)}, u32[]{:S(2)}) collective-permute-start(bf16[1,64,1024]{2,1,0:T(8,128)(2,1)S(1)} %collective-permute-done.4.rest_0_.refs_2_.refs_1_), channel_id=1, source_target_pairs={{0,16},{16,0},{1,17},{17,1},{2,18},{18,2},{3,19},{19,3},{4,20},{20... | collective-permute-start | bytes 393224 | tf_op jit(solution)/shard_map/ppermute | solution.py:23
  21.9 10.4 %collective-permute-start.10 = (bf16[1,64,1024]{2,1,0:T(8,128)(2,1)S(1)}, bf16[1,64,1024]{2,1,0:T(8,128)(2,1)S(1)}, u32[]{:S(2)}, u32[]{:S(2)}) collective-permute-start(bf16[1,64,1024]{2,1,0:T(8,128)(2,1)S(1)} %collective-permute-done.5.rest_1_.refs_3_.refs_2_), channel_id=1, source_target_pairs={{0,16},{16,0},{1,17},{17,1},{2,18},{18,2},{3,19},{19,3},{4,20},{20... | collective-permute-start | bytes 393224 | tf_op jit(solution)/shard_map/ppermute | solution.py:23
  22.4 9.9 %collective-permute-start.11 = (bf16[1,64,1024]{2,1,0:T(8,128)(2,1)S(1)}, bf16[1,64,1024]{2,1,0:T(8,128)(2,1)S(1)}, u32[]{:S(2)}, u32[]{:S(2)}) collective-permute-start(bf16[1,64,1024]{2,1,0:T(8,128)(2,1)S(1)} %collective-permute-done.6.rest_2_.refs_4_.refs_3_), channel_id=1, source_target_pairs={{0,16},{16,0},{1,17},{17,1},{2,18},{18,2},{3,19},{19,3},{4,20},{20... | collective-permute-start | bytes 393224 | tf_op jit(solution)/shard_map/ppermute | solution.py:23
  23.9 20.9 %collective-permute-start.27 = (bf16[128,1024]{1,0:T(8,128)(2,1)}, bf16[128,1024]{1,0:T(8,128)(2,1)S(1)}, u32[]{:S(2)}, u32[]{:S(2)}) collective-permute-start(bf16[128,1024]{1,0:T(8,128)(2,1)} %after.28), channel_id=1, source_target_pairs={{0,8},{4,12},{8,0},{12,4},{1,9},{5,13},{9,1},{13,5},{2,10},{6,14},... | collective-permute-start | bytes 786440 | tf_op jit(solution)/shard_map/ppermute | solution.py:27
  32.4 5.1 %copy-start.14 = (bf16[32,1024]{1,0:T(8,128)(2,1)S(1)}, bf16[32,1024]{1,0:T(8,128)(2,1)}, u32[]{:S(2)}) copy-start(bf16[32,1024]{1,0:T(8,128)(2,1)} %get-tuple-element.80.refs_0_) | copy-start | bytes 196612
  33.6 1.3 %collective-permute-start.12 = (bf16[128,256]{1,0:T(8,128)(2,1)S(1)}, bf16[128,256]{1,0:T(8,128)(2,1)S(1)}, u32[]{:S(2)}, u32[]{:S(2)}) collective-permute-start(bf16[128,256]{1,0:T(8,128)(2,1)S(1)} %get-tuple-element.66), channel_id=1, source_target_pairs={{0,1},{1,0},{2,3},{3,2},{4,5},{5,4},{6,7},{7,6},{8,9},{9,8},{10,11... | collective-permute-start | bytes 196616 | tf_op jit(solution)/shard_map/ppermute | solution.py:23
  33.7 1.4 %collective-permute-start.13 = (bf16[128,256]{1,0:T(8,128)(2,1)S(1)}, bf16[128,256]{1,0:T(8,128)(2,1)S(1)}, u32[]{:S(2)}, u32[]{:S(2)}) collective-permute-start(bf16[128,256]{1,0:T(8,128)(2,1)S(1)} %get-tuple-element.67), channel_id=1, source_target_pairs={{0,1},{1,0},{2,3},{3,2},{4,5},{5,4},{6,7},{7,6},{8,9},{9,8},{10,11... | collective-permute-start | bytes 196616 | tf_op jit(solution)/shard_map/ppermute | solution.py:23
  34.2 1.3 %collective-permute-start.14 = (bf16[128,256]{1,0:T(8,128)(2,1)S(1)}, bf16[128,256]{1,0:T(8,128)(2,1)S(1)}, u32[]{:S(2)}, u32[]{:S(2)}) collective-permute-start(bf16[128,256]{1,0:T(8,128)(2,1)S(1)} %get-tuple-element.68), channel_id=1, source_target_pairs={{0,1},{1,0},{2,3},{3,2},{4,5},{5,4},{6,7},{7,6},{8,9},{9,8},{10,11... | collective-permute-start | bytes 196616 | tf_op jit(solution)/shard_map/ppermute | solution.py:23
  35.0 1.3 %collective-permute-start.15 = (bf16[128,256]{1,0:T(8,128)(2,1)S(1)}, bf16[128,256]{1,0:T(8,128)(2,1)S(1)}, u32[]{:S(2)}, u32[]{:S(2)}) collective-permute-start(bf16[128,256]{1,0:T(8,128)(2,1)S(1)} %get-tuple-element.69), channel_id=1, source_target_pairs={{0,1},{1,0},{2,3},{3,2},{4,5},{5,4},{6,7},{7,6},{8,9},{9,8},{10,11... | collective-permute-start | bytes 196616 | tf_op jit(solution)/shard_map/ppermute | solution.py:23
  35.1 1.3 %collective-permute-start.16 = (bf16[128,256]{1,0:T(8,128)(2,1)S(1)}, bf16[128,256]{1,0:T(8,128)(2,1)S(1)}, u32[]{:S(2)}, u32[]{:S(2)}) collective-permute-start(bf16[128,256]{1,0:T(8,128)(2,1)S(1)} %get-tuple-element.70), channel_id=1, source_target_pairs={{0,1},{1,0},{2,3},{3,2},{4,5},{5,4},{6,7},{7,6},{8,9},{9,8},{10,11... | collective-permute-start | bytes 196616 | tf_op jit(solution)/shard_map/ppermute | solution.py:23
  35.5 1.3 %collective-permute-start.17 = (bf16[128,256]{1,0:T(8,128)(2,1)S(1)}, bf16[128,256]{1,0:T(8,128)(2,1)S(1)}, u32[]{:S(2)}, u32[]{:S(2)}) collective-permute-start(bf16[128,256]{1,0:T(8,128)(2,1)S(1)} %get-tuple-element.71), channel_id=1, source_target_pairs={{0,1},{1,0},{2,3},{3,2},{4,5},{5,4},{6,7},{7,6},{8,9},{9,8},{10,11... | collective-permute-start | bytes 196616 | tf_op jit(solution)/shard_map/ppermute | solution.py:23
  36.2 1.3 %collective-permute-start.18 = (bf16[128,256]{1,0:T(8,128)(2,1)S(1)}, bf16[128,256]{1,0:T(8,128)(2,1)S(1)}, u32[]{:S(2)}, u32[]{:S(2)}) collective-permute-start(bf16[128,256]{1,0:T(8,128)(2,1)S(1)} %get-tuple-element.72), channel_id=1, source_target_pairs={{0,1},{1,0},{2,3},{3,2},{4,5},{5,4},{6,7},{7,6},{8,9},{9,8},{10,11... | collective-permute-start | bytes 196616 | tf_op jit(solution)/shard_map/ppermute | solution.py:23
  36.4 3.1 %collective-permute-start.19 = (bf16[128,256]{1,0:T(8,128)(2,1)S(1)}, bf16[128,256]{1,0:T(8,128)(2,1)S(1)}, u32[]{:S(2)}, u32[]{:S(2)}) collective-permute-start(bf16[128,256]{1,0:T(8,128)(2,1)S(1)} %get-tuple-element.73), channel_id=1, source_target_pairs={{0,1},{1,0},{2,3},{3,2},{4,5},{5,4},{6,7},{7,6},{8,9},{9,8},{10,11... | collective-permute-start | bytes 196616 | tf_op jit(solution)/shard_map/ppermute | solution.py:23
  36.7 11.5 %collective-permute-start.22 = (bf16[48,1024]{1,0:T(8,128)(2,1)S(1)}, bf16[48,1024]{1,0:T(8,128)(2,1)S(1)}, u32[]{:S(2)}, u32[]{:S(2)}) collective-permute-start(bf16[48,1024]{1,0:T(8,128)(2,1)S(1)} %after.23), channel_id=1, source_target_pairs={{0,12},{4,0},{8,4},{12,8},{1,13},{5,1},{9,5},{13,9},{2,14},{6,2},{... | collective-permute-start | bytes 294920 | tf_op jit(solution)/shard_map/ppermute | solution.py:23
  37.5 10.7 %collective-permute-start.24 = (bf16[32,1024]{1,0:T(8,128)(2,1)S(1)}, bf16[32,1024]{1,0:T(8,128)(2,1)S(1)}, u32[]{:S(2)}, u32[]{:S(2)}) collective-permute-start(bf16[32,1024]{1,0:T(8,128)(2,1)S(1)} %after.25), channel_id=1, source_target_pairs={{0,12},{4,0},{8,4},{12,8},{1,13},{5,1},{9,5},{13,9},{2,14},{6,2},{... | collective-permute-start | bytes 196616 | tf_op jit(solution)/shard_map/ppermute | solution.py:23
  39.5 16.5 %slice-start = ((s8[8388608]{0:T(1024)(128)(4,1)}), s8[4194304]{0:T(1024)(128)(4,1)S(1)}, s32[]{:S(2)}) async-start(s8[8388608]{0:T(1024)(128)(4,1)} %bitcast.8), calls=%async_computation | async-start | bytes 8388608
  39.5 5.3 %copy-start.4 = (bf16[128,1024]{1,0:T(8,128)(2,1)S(1)}, bf16[128,1024]{1,0:T(8,128)(2,1)}, u32[]{:S(2)}) copy-start(bf16[128,1024]{1,0:T(8,128)(2,1)} %get-tuple-element.83.refs_0_) | copy-start | bytes 786436
  39.5 16.5 %slice-start.1 = ((s8[8388608]{0:T(1024)(128)(4,1)}), s8[4194304]{0:T(1024)(128)(4,1)S(1)}, s32[]{:S(2)}) async-start(s8[8388608]{0:T(1024)(128)(4,1)} %bitcast.8), calls=%async_computation.1 | async-start | bytes 8388608
  41.9 34.7 %collective-permute-start.20 = (bf16[2048,256]{1,0:T(8,128)(2,1)S(1)}, bf16[2048,256]{1,0:T(8,128)(2,1)}, u32[]{:S(2)}, u32[]{:S(2)}) collective-permute-start(bf16[2048,256]{1,0:T(8,128)(2,1)S(1)} %fetched_weights.1.refs_18_.refs_2_.refs_5_), channel_id=1, source_target_pairs={{0,2},{2,0},{1,3},{3,1},{4,6},{6,4},{5,7},{7,5},{8,10},{10,8},{9,1... | collective-permute-start | bytes 3145736 | tf_op jit(solution)/shard_map/ppermute | solution.py:23
  45.6 24.6 %collective-permute-start.28 = (bf16[256,1024]{1,0:T(8,128)(2,1)}, bf16[256,1024]{1,0:T(8,128)(2,1)}, u32[]{:S(2)}, u32[]{:S(2)}) collective-permute-start(bf16[256,1024]{1,0:T(8,128)(2,1)} %stack.3), channel_id=1, source_target_pairs={{0,4},{4,0},{8,12},{12,8},{1,5},{5,1},{9,13},{13,9},{2,6},{6,2},{1... | collective-permute-start | bytes 1572872 | tf_op jit(solution)/shard_map/ppermute | solution.py:27
  48.2 14.4 %copy-start.6 = (bf16[32,1024]{1,0:T(8,128)(2,1)}, bf16[32,1024]{1,0:T(8,128)(2,1)S(1)}, u32[]{:S(2)}) copy-start(bf16[32,1024]{1,0:T(8,128)(2,1)S(1)} %collective-permute-done.24.refs_0_.refs_4_) | copy-start | bytes 196612
  48.2 7.8 %copy-start.2 = (bf16[256,1024]{1,0:T(8,128)(2,1)}, bf16[256,1024]{1,0:T(8,128)(2,1)S(1)}, u32[]{:S(2)}) copy-start(bf16[256,1024]{1,0:T(8,128)(2,1)S(1)} %collective-permute-done.21.refs_0_.refs_1_) | copy-start | bytes 1572868
  48.2 26.5 %collective-permute-start.33 = (bf16[256,1024]{1,0:T(8,128)(2,1)}, bf16[256,1024]{1,0:T(8,128)(2,1)}, u32[]{:S(2)}, u32[]{:S(2)}) collective-permute-start(bf16[256,1024]{1,0:T(8,128)(2,1)} %after.32), channel_id=1, source_target_pairs={{0,8},{4,12},{8,0},{12,4},{1,9},{5,13},{9,1},{13,5},{2,10},{6,14},... | collective-permute-start | bytes 1572872 | tf_op jit(solution)/shard_map/ppermute | solution.py:23
  51.3 3.6 %collective-permute-start.26 = (s32[8,128]{1,0:T(8,128)S(1)}, s32[8,128]{1,0:T(8,128)S(1)}, u32[]{:S(2)}, u32[]{:S(2)}) collective-permute-start(s32[8,128]{1,0:T(8,128)S(1)} %get-tuple-element.57.refs_10_), channel_id=1, source_target_pairs={{0,16},{16,0},{1,17},{17,1},{2,18},{18,2},{3,19},{19,3},{4,20},{20... | collective-permute-start | bytes 12296 | tf_op jit(solution)/shard_map/ppermute | solution.py:23
  56.0 6.6 %copy-start.18 = (bf16[128,1024]{1,0:T(8,128)(2,1)S(1)}, bf16[128,1024]{1,0:T(8,128)(2,1)}, u32[]{:S(2)}) copy-start(bf16[128,1024]{1,0:T(8,128)(2,1)} %get-tuple-element.81.refs_0_) | copy-start | bytes 786436
  62.9 1.8 %collective-permute-start.29 = (bf16[128,1024]{1,0:T(8,128)(2,1)}, bf16[128,1024]{1,0:T(8,128)(2,1)S(1)}, u32[]{:S(2)}, u32[]{:S(2)}) collective-permute-start(bf16[128,1024]{1,0:T(8,128)(2,1)} %get-tuple-element.83.refs_0_), channel_id=1, source_target_pairs={{0,1},{1,0},{2,3},{3,2},{4,5},{5,4},{6,7},{7,6},{8,9},{9,8},{10,11... | collective-permute-start | bytes 786440 | tf_op jit(solution)/shard_map/ppermute | solution.py:23
  63.0 1.9 %collective-permute-start.30 = (bf16[128,1024]{1,0:T(8,128)(2,1)S(1)}, bf16[128,1024]{1,0:T(8,128)(2,1)S(1)}, u32[]{:S(2)}, u32[]{:S(2)}) collective-permute-start(bf16[128,1024]{1,0:T(8,128)(2,1)S(1)} %after.29.refs_1_), channel_id=1, source_target_pairs={{0,1},{1,0},{2,3},{3,2},{4,5},{5,4},{6,7},{7,6},{8,9},{9,8},{10,11... | collective-permute-start | bytes 786440 | tf_op jit(solution)/shard_map/ppermute | solution.py:23
  64.7 3.9 %collective-permute-start.23 = (bf16[48,1024]{1,0:T(8,128)(2,1)S(1)}, bf16[48,1024]{1,0:T(8,128)(2,1)S(1)}, u32[]{:S(2)}, u32[]{:S(2)}) collective-permute-start(bf16[48,1024]{1,0:T(8,128)(2,1)S(1)} %after.24.refs_0_), channel_id=1, source_target_pairs={{0,1},{1,0},{2,3},{3,2},{4,5},{5,4},{6,7},{7,6},{8,9},{9,8},{10,11... | collective-permute-start | bytes 294920 | tf_op jit(solution)/shard_map/ppermute | solution.py:23
  64.9 3.7 %collective-permute-start.25 = (bf16[32,1024]{1,0:T(8,128)(2,1)S(1)}, bf16[32,1024]{1,0:T(8,128)(2,1)S(1)}, u32[]{:S(2)}, u32[]{:S(2)}) collective-permute-start(bf16[32,1024]{1,0:T(8,128)(2,1)S(1)} %after.26.refs_2_), channel_id=1, source_target_pairs={{0,1},{1,0},{2,3},{3,2},{4,5},{5,4},{6,7},{7,6},{8,9},{9,8},{10,11... | collective-permute-start | bytes 196616 | tf_op jit(solution)/shard_map/ppermute | solution.py:23
  70.2 1.2 %collective-permute-start.31 = (s32[8,128]{1,0:T(8,128)S(1)}, s32[8,128]{1,0:T(8,128)S(1)}, u32[]{:S(2)}, u32[]{:S(2)}) collective-permute-start(s32[8,128]{1,0:T(8,128)S(1)} %after.30), channel_id=1, source_target_pairs={{0,1},{1,0},{2,3},{3,2},{4,5},{5,4},{6,7},{7,6},{8,9},{9,8},{10,11... | collective-permute-start | bytes 12296 | tf_op jit(solution)/shard_map/ppermute | solution.py:23
  70.2 6.4 %collective-permute-start.35 = (bf16[256,1024]{1,0:T(8,128)(2,1)}, bf16[256,1024]{1,0:T(8,128)(2,1)S(1)}, u32[]{:S(2)}, u32[]{:S(2)}) collective-permute-start(bf16[256,1024]{1,0:T(8,128)(2,1)} %after.34.refs_9_), channel_id=1, source_target_pairs={{0,1},{1,0},{2,3},{3,2},{4,5},{5,4},{6,7},{7,6},{8,9},{9,8},{10,11... | collective-permute-start | bytes 1572872 | tf_op jit(solution)/shard_map/ppermute | solution.py:23
  71.4 6.0 %collective-permute-start.32 = (bf16[256,1024]{1,0:T(8,128)(2,1)S(1)}, bf16[256,1024]{1,0:T(8,128)(2,1)S(1)}, u32[]{:S(2)}, u32[]{:S(2)}) collective-permute-start(bf16[256,1024]{1,0:T(8,128)(2,1)S(1)} %after.31.refs_3_), channel_id=1, source_target_pairs={{0,1},{1,0},{2,3},{3,2},{4,5},{5,4},{6,7},{7,6},{8,9},{9,8},{10,11... | collective-permute-start | bytes 1572872 | tf_op jit(solution)/shard_map/ppermute | solution.py:23
  74.8 2.6 %collective-permute-start.34 = (bf16[256,1024]{1,0:T(8,128)(2,1)}, bf16[256,1024]{1,0:T(8,128)(2,1)S(1)}, u32[]{:S(2)}, u32[]{:S(2)}) collective-permute-start(bf16[256,1024]{1,0:T(8,128)(2,1)} %after.33.refs_5_), channel_id=1, source_target_pairs={{0,1},{1,0},{2,3},{3,2},{4,5},{5,4},{6,7},{7,6},{8,9},{9,8},{10,11... | collective-permute-start | bytes 1572872 | tf_op jit(solution)/shard_map/ppermute | solution.py:23
  74.8 8.4 %collective-permute-start.37 = (bf16[64,1024]{1,0:T(8,128)(2,1)S(1)}, bf16[64,1024]{1,0:T(8,128)(2,1)S(1)}, u32[]{:S(2)}, u32[]{:S(2)}) collective-permute-start(bf16[64,1024]{1,0:T(8,128)(2,1)S(1)} %after.20.refs_3_), channel_id=1, source_target_pairs={{0,12},{4,0},{8,4},{12,8},{1,13},{5,1},{9,5},{13,9},{2,14},{6,2},{... | collective-permute-start | bytes 393224 | tf_op jit(solution)/shard_map/ppermute | solution.py:23
  76.6 7.3 %collective-permute-start.39 = (bf16[64,1024]{1,0:T(8,128)(2,1)S(1)}, bf16[64,1024]{1,0:T(8,128)(2,1)S(1)}, u32[]{:S(2)}, u32[]{:S(2)}) collective-permute-start(bf16[64,1024]{1,0:T(8,128)(2,1)S(1)} %after.21.refs_4_), channel_id=1, source_target_pairs={{0,12},{4,0},{8,4},{12,8},{1,13},{5,1},{9,5},{13,9},{2,14},{6,2},{... | collective-permute-start | bytes 393224 | tf_op jit(solution)/shard_map/ppermute | solution.py:23
  76.7 8.9 %collective-permute-start.41 = (bf16[48,1024]{1,0:T(8,128)(2,1)S(1)}, bf16[48,1024]{1,0:T(8,128)(2,1)S(1)}, u32[]{:S(2)}, u32[]{:S(2)}) collective-permute-start(bf16[48,1024]{1,0:T(8,128)(2,1)S(1)} %after.22.refs_5_), channel_id=1, source_target_pairs={{0,12},{4,0},{8,4},{12,8},{1,13},{5,1},{9,5},{13,9},{2,14},{6,2},{... | collective-permute-start | bytes 294920 | tf_op jit(solution)/shard_map/ppermute | solution.py:23
  81.6 10.4 %collective-permute-start.36 = (bf16[1024,128]{1,0:T(8,128)(2,1)S(1)}, bf16[1024,128]{1,0:T(8,128)(2,1)S(1)}, u32[]{:S(2)}, u32[]{:S(2)}) collective-permute-start(bf16[1024,128]{1,0:T(8,128)(2,1)S(1)} %get-tuple-element.90.refs_1_), channel_id=1, source_target_pairs={{0,2},{2,0},{1,3},{3,1},{4,6},{6,4},{5,7},{7,5},{8,10},{10,8},{9,1... | collective-permute-start | bytes 786440 | tf_op jit(solution)/shard_map/ppermute | solution.py:23
  83.1 3.8 %collective-permute-start.38 = (bf16[64,1024]{1,0:T(8,128)(2,1)S(1)}, bf16[64,1024]{1,0:T(8,128)(2,1)S(1)}, u32[]{:S(2)}, u32[]{:S(2)}) collective-permute-start(bf16[64,1024]{1,0:T(8,128)(2,1)S(1)} %after.35.refs_4_), channel_id=1, source_target_pairs={{0,1},{1,0},{2,3},{3,2},{4,5},{5,4},{6,7},{7,6},{8,9},{9,8},{10,11... | collective-permute-start | bytes 393224 | tf_op jit(solution)/shard_map/ppermute | solution.py:23
  83.9 3.0 %collective-permute-start.40 = (bf16[64,1024]{1,0:T(8,128)(2,1)S(1)}, bf16[64,1024]{1,0:T(8,128)(2,1)S(1)}, u32[]{:S(2)}, u32[]{:S(2)}) collective-permute-start(bf16[64,1024]{1,0:T(8,128)(2,1)S(1)} %after.36.refs_6_), channel_id=1, source_target_pairs={{0,1},{1,0},{2,3},{3,2},{4,5},{5,4},{6,7},{7,6},{8,9},{9,8},{10,11... | collective-permute-start | bytes 393224 | tf_op jit(solution)/shard_map/ppermute | solution.py:23
  85.6 1.3 %collective-permute-start.42 = (bf16[48,1024]{1,0:T(8,128)(2,1)S(1)}, bf16[48,1024]{1,0:T(8,128)(2,1)S(1)}, u32[]{:S(2)}, u32[]{:S(2)}) collective-permute-start(bf16[48,1024]{1,0:T(8,128)(2,1)S(1)} %after.37.refs_8_), channel_id=1, source_target_pairs={{0,1},{1,0},{2,3},{3,2},{4,5},{5,4},{6,7},{7,6},{8,9},{9,8},{10,11... | collective-permute-start | bytes 294920 | tf_op jit(solution)/shard_map/ppermute | solution.py:23
  87.7 4.3 %collective-permute-start.43 = (bf16[256,128]{1,0:T(8,128)(2,1)S(1)}, bf16[256,128]{1,0:T(8,128)(2,1)S(1)}, u32[]{:S(2)}, u32[]{:S(2)}) collective-permute-start(bf16[256,128]{1,0:T(8,128)(2,1)S(1)} %get-tuple-element.93), channel_id=1, source_target_pairs={{0,2},{2,0},{1,3},{3,1},{4,6},{6,4},{5,7},{7,5},{8,10},{10,8},{9,1... | collective-permute-start | bytes 196616 | tf_op jit(solution)/shard_map/ppermute | solution.py:23
  (13 other events, 31.3 us)
